TPU v7x, 32 devices: a whole 2x2x4 slice. The times are simulated.
32 devices in a mesh: ka: 4 (over y, core), ga: 8 (over z, x).
Axes of the slice: x: 2, y: 2, z: 4, core: 2. Of those that a mesh axis runs over, the one named last changes fastest.
Arguments:
- bands: bfloat16 [8, 2, 512, 16384], P('ka', None, None, 'ga'), may hold values from -1.75 to 1.75
- nbr_slot: int32 [8], P('ka'), may hold values from 0 to 1, as said below
- gshift: int32 [8], P('ka'), may hold values from -1 to 1
Outputs:
- margin: float32 [512, 8, 2, 512], P('ga', 'ka')
Inputs may be any that keep to these rules, and one draw needn't show every extreme that they name: `nbr_slot`: for the 2 k-points of one group the entries are a permutation of 0 to 1.
All inputs are finite; a program needn't handle non-finite values.
Results may differ from a plain program's by a relative error of at most 0.0028.
Values may be sent and summed in bfloat16 or wider, within the bound.
No kernel may reach another device: no remote copies, remote signals or barrier semaphores. Data moves between devices by JAX's collectives and lax.ppermute only.
A program may use at most 128 MiB of HBM per device.

v0:
```python
import math

import jax
import jax.numpy as jnp
from jax import lax
from jax.sharding import PartitionSpec as P

NKB = 4
PLANE = 1024


def shifted(block, axis, distance):
    devices = range(lax.axis_size(axis))
    route = [((i - distance) % len(devices), i) for i in devices]
    return lax.ppermute(block, axis, route)


def phase_fields(slabs, shifts, planes, total_planes):
    turns = (1 + NKB * shifts[:, None]) * planes[None, :] % (NKB * total_planes)
    angle = 2.0 * math.pi / (NKB * total_planes) * turns.astype(jnp.float32)
    cosine = jnp.cos(angle)[:, None, :]
    sine = jnp.sin(angle)[:, None, :]
    real_part = slabs[:, 0].astype(jnp.float32)
    imag_part = slabs[:, 1].astype(jnp.float32)
    near_re = real_part * cosine + imag_part * sine
    near_im = imag_part * cosine - real_part * sine
    return jnp.stack([near_re, near_im], axis=1).astype(jnp.bfloat16)


def body(bands, nbr_slot, gshift):
    grid_index = lax.axis_index("ga")
    grid_count = lax.axis_size("ga")
    nbands = bands.shape[2]
    points = bands.shape[3]
    rows = nbands // grid_count
    total_planes = points // PLANE * grid_count
    planes = (grid_index * points + jnp.arange(points, dtype=jnp.int32)) // PLANE
    there = shifted(bands, "ka", -1)
    partner = jnp.take(there, nbr_slot, axis=0)
    near = phase_fields(partner, gshift, planes, total_planes)
    terms = jnp.einsum("pcmx,pdnx->mpcdn", bands, near, preferred_element_type=jnp.float32)
    real_part = terms[:, :, 0, 0] + terms[:, :, 1, 1]
    imag_part = terms[:, :, 0, 1] - terms[:, :, 1, 0]
    summed = lax.psum(jnp.stack([real_part, imag_part], axis=2), "ga")
    result = lax.dynamic_slice_in_dim(summed, grid_index * rows, rows, 0)
    return result


def solution(mesh):
    placed = (P("ka", None, None, "ga"), P("ka"), P("ka"))
    return jax.shard_map(
        body, mesh=mesh, in_specs=placed, out_specs=P("ga", "ka", None, None), check_vma=False
    )
```

profile of v0, /device:TPU:0, one launch (start us, length us, event | category | flops | bytes accessed | tf_op | source)
XLA Modules:
  0.0 309.9 jit_solution(3976393133425829957)
XLA Ops:
  6.5 0.0 all-reduce.2.cloned.1.call-start
  6.5 2.4 collective-permute-start
  8.9 0.7 compare_select_fusion.2
  9.6 0.7 compare_and_fusion
  10.3 0.7 multiply_add_fusion
  10.9 0.3 fusion.20
  11.3 88.9 %collective-permute-done = bf16[2,2,512,2048]{3,2,1,0:T(8,128)(2,1)} collective-permute-done((bf16[2,2,512,2048]{3,2,1,0:T(8,128)(2,1)}, bf16[2,2,512,2048]{3,2,1,0:T(8,128)(2,1)}, u32[]{:S(2)}, u32[]{:S(2)}) %collective-permute-start) | collective-permute-done | bytes 8388640 | tf_op jit(solution)/shard_map/ppermute | solution.py:15
  100.2 1.7 mini-gather-slice.5
  102.0 2.0 gather_fusion.2
  103.9 6.0 %fusion.23 = (bf16[2,2,512,768]{3,2,1,0:T(8,128)(2,1)}, bf16[2,2,512,768]{3,2,1,0:T(8,128)(2,1)}) fusion(bf16[2,2,512,2048]{3,2,1,0:T(8,128)(2,1)} %collective-permute-done), kind=kLoop, calls=%fused_computation.49 | loop fusion | bytes 12582912 | tf_op jit(solution)/shard_map/jit(_take)/gather | solution.py:39
  109.9 2.6 gather_fusion.1
  112.6 4.3 %gather_fusion = bf16[2,2,512,768]{3,2,1,0:T(8,128)(2,1)} fusion(bf16[2,2,512,768]{3,2,1,0:T(8,128)(2,1)} %get-tuple-element.7, s32[1024]{0:T(1024)S(1)} %pad_clamp_fusion), kind=kCustom, calls=%fused_computation | custom fusion | bytes 6291464 | tf_op jit(solution)/shard_map/jit(_take)/gather | solution.py:39
  116.8 4.4 %maximum_select_fusion = bf16[2,2,512,2048]{3,2,1,0:T(8,128)(2,1)S(1)} fusion(bf16[2,2,512,512]{3,2,1,0:T(8,128)(2,1)} %gather_fusion.2, bf16[2,2,512,768]{3,2,1,0:T(8,128)(2,1)S(1)} %gather_fusion.1, bf16[2,2,512,768]{3,2,1,0:T(8,128)(2,1)} %gather_fusion, pred[2]{0:T(512)(128)(4,1)S(1)} %compare_and_fusion), kind=kLoop, calls=%fused_computation.11 | loop fusion | flops 29360128 | bytes 16777218 | tf_op jit(solution)/shard_map/jit(_take)/select_n | solution.py:39
  121.2 5.1 %fusion.1 = (bf16[2,1,512,2048]{3,2,1,0:T(8,128)(2,1)}, bf16[2,1,512,2048]{3,2,1,0:T(8,128)(2,1)}) fusion(f32[2,2048]{1,0:T(2,128)S(1)} %get-tuple-element.10, f32[2,2048]{1,0:T(2,128)S(1)} %get-tuple-element.9, bf16[2,2,512,2048]{3,2,1,0:T(8,128)(2,1)S(1)} %maximum_select_fusion), kind=kLoop, calls=%fused_computation.8 | loop fusion | flops 20971520 | bytes 16809984 | tf_op jit(solution)/shard_map/convert
  126.3 12.6 %fusion.8 = f32[512,2,2,2,512]{0,4,2,3,1:T(8,128)S(1)} fusion(bf16[2,2,512,2048]{3,2,1,0:T(8,128)(2,1)} %param.3, bf16[2,1,512,2048]{3,2,1,0:T(8,128)(2,1)} %get-tuple-element.6, bf16[2,1,512,2048]{3,2,1,0:T(8,128)(2,1)} %get-tuple-element.5), kind=kOutput, calls=%fused_computation.18 | convolution fusion | flops 8606711808 | bytes 25165824 | tf_op jit(solution)/shard_map/pcmx,pdnx->mpcdn/dot_general | solution.py:41
  138.8 0.5 fusion.11
  139.3 0.5 fusion.13
  139.8 2.4 pad_maximum_fusion
  142.2 0.0 all-reduce.2.cloned.1.call-update
  142.2 158.1 %all-reduce.2.cloned.1.call-done = f32[512,2,2,512]{0,3,1,2:T(8,128)} async-done(((f32[512,2,2,512]{0,3,1,2:T(8,128)}), f32[512,2,2,512]{0,3,1,2:T(8,128)}) %all-reduce.2.cloned.1.call-update) | async-done | bytes 4194320 | tf_op jit(solution)/shard_map/psum | solution.py:44
  300.4 1.6 constant_dynamic-slice_fusion
  301.9 1.1 copy.6
  (2 shorter events, 0.0 us)
Async XLA Ops:
  6.5 293.8 %all-reduce.2.cloned.1.call-start = ((), (), s32[]{:S(2)}) async-start(), calls=%async_computation | async-start | bytes 8388608 | tf_op jit(solution)/shard_map/psum | solution.py:44
  6.5 93.7 %collective-permute-start = (bf16[2,2,512,2048]{3,2,1,0:T(8,128)(2,1)}, bf16[2,2,512,2048]{3,2,1,0:T(8,128)(2,1)}, u32[]{:S(2)}, u32[]{:S(2)}) collective-permute-start(bf16[2,2,512,2048]{3,2,1,0:T(8,128)(2,1)} %param.3), channel_id=1, source_target_pairs={{8,0},{16,8},{24,16},{0,24},{9,1},{17,9},{25,17},{1,25},{10,2},{18... | collective-permute-start | bytes 25165832 | tf_op jit(solution)/shard_map/ppermute | solution.py:15
Sparse Core Ops, SparseCore 0:
  142.4 157.9 all-reduce.1
where the time goes:
time: 310 us
  waiting for transfers between devices  247 us (80%)
  local copies, waits for them, and re-layouts  19.3 us (6%)
  other arithmetic  15.1 us (5%)
  between operations  13.4 us (4%)
  matrix products  12.6 us (4%)
    psum x1, waiting for transfers between devices, body(): summed = lax.psum(jnp.stack([real_part, imag_part], axis=2), 'ga')  158 us
    ppermute x1, waiting for transfers between devices, shifted(): return lax.ppermute(block, axis, route)  88.9 us
    gather x5, local copies, waits for them, and re-layouts, body(): partner = jnp.take(there, nbr_slot, axis=0)  16.6 us
    dot_general x1, matrix products, body(): jnp.einsum('pcmx,pdnx->mpcdn', bands, near, preferred_element_type=jnp.fl...  12.6 us
  transfers between devices with their start and end apart: 2, of which 2 were waited for; matrix products, arithmetic and copies ran while one was open for 1% of the time, Pallas kernels for 0%

commit v1 on v0

v1 whole, which is shorter than its diff:
```python
import functools
import math

import jax
import jax.numpy as jnp
from jax import lax
from jax.experimental import pallas as pl
from jax.experimental.pallas import tpu as pltpu
from jax.sharding import PartitionSpec as P

NKB = 4
PLANE = 1024
WIDTH = 128
DEPTH = 512


def shifted(block, axis, distance):
    count = lax.axis_size(axis)
    route = [((i - distance) % count, i) for i in range(count)]
    return lax.ppermute(block, axis, route)


def margin_kernel(slot, order_ref, cos_ref, sin_ref, own_ref, there_ref, out_ref, acc_ref):
    step = pl.program_id(0)
    point = order_ref[slot]
    plane = step * DEPTH // PLANE
    cosine = cos_ref[point, plane]
    sine = sin_ref[point, plane]
    real_part = there_ref[0].astype(jnp.float32)
    imag_part = there_ref[1].astype(jnp.float32)
    near_re = (real_part * cosine + imag_part * sine).astype(jnp.bfloat16)
    near_im = (imag_part * cosine - real_part * sine).astype(jnp.bfloat16)
    dims = (((1,), (1,)), ((), ()))
    with_re = jnp.concatenate([near_re, near_im], axis=0)
    with_im = jnp.concatenate([near_im, -near_re], axis=0)
    terms = lax.dot_general(own_ref[0, 0], with_re, dims, preferred_element_type=jnp.float32)
    terms += lax.dot_general(own_ref[0, 1], with_im, dims, preferred_element_type=jnp.float32)

    @pl.when(step == 0)
    def _():
        acc_ref[...] = terms

    @pl.when(step > 0)
    def _():
        acc_ref[...] += terms

    @pl.when(step == pl.num_programs(0) - 1)
    def _():
        out_ref[...] = acc_ref[...].astype(out_ref.dtype)


def margin_part(slot, order, cosine, sine, bands, there):
    _, _, nbands, points = bands.shape
    width = there.shape[1]
    flops = 2 * nbands * 2 * width * 2 * points
    return pl.pallas_call(
        functools.partial(margin_kernel, slot),
        grid_spec=pltpu.PrefetchScalarGridSpec(
            num_scalar_prefetch=3,
            grid=(points // DEPTH,),
            in_specs=[
                pl.BlockSpec((1, 2, nbands, DEPTH), lambda t, order, c, s: (order[slot], 0, 0, t)),
                pl.BlockSpec((2, width, DEPTH), lambda t, order, c, s: (0, 0, t)),
            ],
            out_specs=pl.BlockSpec((nbands, 2 * width), lambda t, order, c, s: (0, 0)),
            scratch_shapes=[pltpu.VMEM((nbands, 2 * width), jnp.float32)],
        ),
        out_shape=jax.ShapeDtypeStruct((nbands, 2 * width), jnp.bfloat16),
        compiler_params=pltpu.CompilerParams(
            dimension_semantics=("arbitrary",), vmem_limit_bytes=32 * 1024 * 1024
        ),
        cost_estimate=pl.CostEstimate(
            flops=flops, bytes_accessed=4 * nbands * points + 4 * width * points, transcendentals=0
        ),
        name="margin_part",
    )(order, cosine, sine, bands, there)


def gather_kernel(order_ref, parts_ref, *rest):
    out_ref = rest[-1]
    total = parts_ref[0].astype(jnp.float32)
    for source in range(1, parts_ref.shape[0]):
        total = total + parts_ref[source].astype(jnp.float32)
    width = out_ref.shape[3]
    out_ref[:, 0, 0, :] = total[:, :width]
    out_ref[:, 0, 1, :] = total[:, width:]


def add_part(slot, block, order, parts, result, shape):
    count, rows, wide = parts.shape
    width = wide // 2
    operands = (order, parts) if result is None else (order, parts, result)
    in_specs = [pl.BlockSpec((count, rows, wide), lambda i, order: (0, 0, 0))]
    if result is not None:
        in_specs.append(pl.BlockSpec(memory_space=pl.ANY))
    return pl.pallas_call(
        gather_kernel,
        grid_spec=pltpu.PrefetchScalarGridSpec(
            num_scalar_prefetch=1,
            grid=(1,),
            in_specs=in_specs,
            out_specs=pl.BlockSpec((rows, 1, 2, width), lambda i, order: (0, order[slot], 0, block)),
        ),
        out_shape=jax.ShapeDtypeStruct(shape, jnp.float32),
        input_output_aliases={} if result is None else {2: 0},
        cost_estimate=pl.CostEstimate(
            flops=count * rows * wide, bytes_accessed=2 * count * rows * wide, transcendentals=0
        ),
        name="add_part",
    )(*operands)


def body(bands, nbr_slot, gshift):
    grid_index = lax.axis_index("ga")
    grid_count = lax.axis_size("ga")
    k_dev, _, nbands, points = bands.shape
    rows = nbands // grid_count
    own_planes = points // PLANE
    total_planes = own_planes * grid_count
    planes = grid_index * own_planes + jnp.arange(own_planes, dtype=jnp.int32)
    turns = (1 + NKB * gshift[:, None]) * planes[None, :] % (NKB * total_planes)
    angle = 2.0 * math.pi / (NKB * total_planes) * turns.astype(jnp.float32)
    cosine = jnp.cos(angle)
    sine = jnp.sin(angle)
    slots = jnp.arange(k_dev, dtype=jnp.int32)
    order = jnp.sum(jnp.where(nbr_slot[None, :] == slots[:, None], slots[None, :], 0), axis=1)
    result = None
    for slot in range(k_dev):
        for block in range(nbands // WIDTH):
            piece = bands[slot, :, block * WIDTH : (block + 1) * WIDTH, :]
            there = shifted(piece, "ka", -1)
            part = margin_part(slot, order, cosine, sine, bands, there)
            part = part.reshape(grid_count, rows, 2 * WIDTH)
            parts = lax.all_to_all(part, "ga", 0, 0)
            result = add_part(slot, block, order, parts, result, (rows, k_dev, 2, nbands))
    return result


def solution(mesh):
    placed = (P("ka", None, None, "ga"), P("ka"), P("ka"))
    return jax.shard_map(
        body, mesh=mesh, in_specs=placed, out_specs=P("ga", "ka", None, None), check_vma=False
    )
```

time: 310 us -> 151 us (0.49)
  waiting for transfers between devices: 247 us -> 21.4 us
  Pallas kernels: 0 us -> 50 us
  starting transfers between devices: 2.41 us -> 43.6 us
  local copies, waits for them, and re-layouts: 19.3 us -> 34.6 us
  other arithmetic: 15.1 us -> 0.24 us
  between operations: 13.4 us -> 0.13 us
  matrix products: 12.6 us -> 0 us
    psum x1 -> x0, waiting for transfers between devices: 158 us -> none  [body(): summed = lax.psum(jnp.stack([real_part, imag_part], axis=2), 'ga')]
    ppermute x1 -> x8, waiting for transfers between devices: 88.9 us -> 11.7 us  [shifted(): return lax.ppermute(block, axis, route)]
    pallas_call x0 -> x16, Pallas kernels: none -> 50 us  [the longest x8 31.5 us: margin_part(): pl.pallas_call(functools.partial(margin_kernel, slot), grid_spec=pltpu.Pr...]
    all_to_all x0 -> x8, starting transfers between devices: none -> 37.3 us  [body(): parts = lax.all_to_all(part, 'ga', 0, 0)]
    unnamed x0 -> x34, local copies, waits for them, and re-layouts: none -> 28.5 us
    gather x5 -> x0, local copies, waits for them, and re-layouts: 16.6 us -> none  [body(): partner = jnp.take(there, nbr_slot, axis=0)]
    dot_general x1 -> x0, matrix products: 12.6 us -> none  [body(): jnp.einsum('pcmx,pdnx->mpcdn', bands, near, preferred_element_type=jnp.fl...]
    all_to_all x0 -> x8, waiting for transfers between devices: none -> 9.73 us  [body(): parts = lax.all_to_all(part, 'ga', 0, 0)]
  transfers between devices with their start and end apart: 2 -> 16, of which waited for: 2 -> 8; matrix products, arithmetic and copies ran while one was open for 1% -> 0% of each run, Pallas kernels for 0% -> 32%
where the time goes in v1:
time: 151 us; the launch traced here: 150 us
  Pallas kernels  50 us (33%)
  starting transfers between devices  43.6 us (29%)
  local copies, waits for them, and re-layouts  34.6 us (23%)
  waiting for transfers between devices  21.4 us (14%)
    all_to_all x8, starting transfers between devices, body(): parts = lax.all_to_all(part, 'ga', 0, 0)  37.3 us
    pallas_call x8, Pallas kernels, margin_part(): pl.pallas_call(functools.partial(margin_kernel, slot), grid_spec=pltpu.Pr...  31.5 us
    unnamed x34, local copies, waits for them, and re-layouts  28.5 us
    pallas_call x8, Pallas kernels, add_part(): pl.pallas_call(gather_kernel, grid_spec=pltpu.PrefetchScalarGridSpec(num_...  18.5 us
    ppermute x8, waiting for transfers between devices, shifted(): return lax.ppermute(block, axis, route)  11.7 us
    all_to_all x8, waiting for transfers between devices, body(): parts = lax.all_to_all(part, 'ga', 0, 0)  9.73 us
    ppermute x8, starting transfers between devices, shifted(): return lax.ppermute(block, axis, route)  6.25 us
    squeeze x1, local copies, waits for them, and re-layouts, body(): piece = bands[slot, :, block * WIDTH:(block + 1) * WIDTH, :]  6.13 us
  transfers between devices with their start and end apart: 16, of which 8 were waited for; matrix products, arithmetic and copies ran while one was open for 0% of the time, Pallas kernels for 32%

profile of v1, /device:TPU:0, one launch (start us, length us, event | category | flops | bytes accessed | tf_op | source)
XLA Modules:
  0.0 149.9 jit_solution(13841701076408745222)
XLA Ops:
  0.0 6.1 %slice_bitcast_fusion = (bf16[2,128,2048]{2,1,0:T(8,128)(2,1)}, bf16[2,128,2048]{2,1,0:T(8,128)(2,1)}, bf16[2,128,2048]{2,1,0:T(8,128)(2,1)}, bf16[2,128,2048]{2...) fusion(bf16[2,2,512,2048]{3,2,1,0:T(8,128)(2,1)} %own_ref.15), kind=kLoop, calls=%fused_computation | loop fusion | bytes 16777216 | tf_op jit(solution)/shard_map/squeeze | solution.py:130
  6.1 2.5 %collective-permute-start.7 = (bf16[2,128,2048]{2,1,0:T(8,128)(2,1)}, bf16[2,128,2048]{2,1,0:T(8,128)(2,1)S(1)}, u32[]{:S(2)}, u32[]{:S(2)}) collective-permute-start(bf16[2,128,2048]{2,1,0:T(8,128)(2,1)} %get-tuple-element.5), channel_id=1, source_target_pairs={{8,0},{16,8},{24,16},{0,24},{9,1},{17,9},{25,17},{1,25},{10,2},{18... | collective-permute-start | bytes 3145736 | tf_op jit(solution)/shard_map/ppermute | solution.py:20
  8.6 0.7 collective-permute-start.6
  9.6 11.6 %collective-permute-done.7.there_ref = bf16[2,128,2048]{2,1,0:T(8,128)(2,1)S(1)} collective-permute-done((bf16[2,128,2048]{2,1,0:T(8,128)(2,1)}, bf16[2,128,2048]{2,1,0:T(8,128)(2,1)S(1)}, u32[]{:S(2)}, u32[]{:S(2)}) %collective-permute-start.7) | collective-permute-done | bytes 1048608 | tf_op jit(solution)/shard_map/ppermute | solution.py:20
  21.2 3.4 %copy-done = bf16[2,2,512,2048]{3,2,1,0:T(8,128)(2,1)S(1)} copy-done((bf16[2,2,512,2048]{3,2,1,0:T(8,128)(2,1)S(1)}, bf16[2,2,512,2048]{3,2,1,0:T(8,128)(2,1)}, u32[]{:S(2)}) %copy-start) | copy-done | bytes 8388632
  24.6 3.9 %margin_part.15 = bf16[512,256]{1,0:T(8,128)(2,1)} custom-call(s32[2]{0:T(128)S(1)} %fusion.3.order_ref, f32[2,2]{1,0:T(2,128)S(1)} %get-tuple-element.14.cos_ref, f32[2,2]{1,0:T(2,128)S(1)} %get-tuple-element.13.sin_ref, bf16[2,2,512,2048]{3,2,1,0:T(8,128)(2,1)S(1)} %copy-done, bf16[2,128,2048]{2,1,0:T(8,128)(2,1)S(1)} %collective-permute-done.7.there_ref), custom_call_target="tpu_custom_call" | custom-call | flops 1073741824 | bytes 5242880 | tf_op jit(solution)/shard_map/margin_part/pallas_call | solution.py:56
  28.5 5.8 %all-to-all-start.7 = ((bf16[8,64,256]{2,1,0:T(8,128)(2,1)}), bf16[8,64,256]{2,1,0:T(8,128)(2,1)S(1)}, u32[]{:S(2)}, u32[]{:S(2)}) async-start(bf16[8,64,256]{2,1,0:T(8,128)(2,1)} %bitcast.15), calls=%async_computation.7 | async-start | bytes 524288 | tf_op jit(solution)/shard_map/all_to_all | solution.py:134
  34.4 1.5 %collective-permute-start.4 = (bf16[2,128,2048]{2,1,0:T(8,128)(2,1)}, bf16[2,128,2048]{2,1,0:T(8,128)(2,1)S(1)}, u32[]{:S(2)}, u32[]{:S(2)}) collective-permute-start(bf16[2,128,2048]{2,1,0:T(8,128)(2,1)} %get-tuple-element.8), channel_id=1, source_target_pairs={{8,0},{16,8},{24,16},{0,24},{9,1},{17,9},{25,17},{1,25},{10,2},{18... | collective-permute-start | bytes 3145736 | tf_op jit(solution)/shard_map/ppermute | solution.py:20
  35.9 3.4 %copy-done.1 = bf16[2,2,512,2048]{3,2,1,0:T(8,128)(2,1)S(1)} copy-done((bf16[2,2,512,2048]{3,2,1,0:T(8,128)(2,1)S(1)}, bf16[2,2,512,2048]{3,2,1,0:T(8,128)(2,1)}, u32[]{:S(2)}) %copy-start.1) | copy-done | bytes 8388632
  39.3 4.0 %margin_part.14 = bf16[512,256]{1,0:T(8,128)(2,1)} custom-call(s32[2]{0:T(128)S(1)} %fusion.3.order_ref, f32[2,2]{1,0:T(2,128)S(1)} %get-tuple-element.14.cos_ref, f32[2,2]{1,0:T(2,128)S(1)} %get-tuple-element.13.sin_ref, bf16[2,2,512,2048]{3,2,1,0:T(8,128)(2,1)S(1)} %copy-done.1, bf16[2,128,2048]{2,1,0:T(8,128)(2,1)S(1)} %collective-permute-done.6.there_ref), custom_call_target="tpu_custom_call" | custom-call | flops 1073741824 | bytes 5242880 | tf_op jit(solution)/shard_map/margin_part/pallas_call | solution.py:56
  43.2 1.0 all-to-all-done.7.parts_ref
  44.2 0.7 copy-done.14
  44.9 4.8 %all-to-all-start.6 = ((bf16[8,64,256]{2,1,0:T(8,128)(2,1)}), bf16[8,64,256]{2,1,0:T(8,128)(2,1)S(1)}, u32[]{:S(2)}, u32[]{:S(2)}) async-start(bf16[8,64,256]{2,1,0:T(8,128)(2,1)} %bitcast.13), calls=%async_computation.6 | async-start | bytes 524288 | tf_op jit(solution)/shard_map/all_to_all | solution.py:134
  49.7 3.4 %copy-done.2 = bf16[2,2,512,2048]{3,2,1,0:T(8,128)(2,1)S(1)} copy-done((bf16[2,2,512,2048]{3,2,1,0:T(8,128)(2,1)S(1)}, bf16[2,2,512,2048]{3,2,1,0:T(8,128)(2,1)}, u32[]{:S(2)}) %copy-start.2) | copy-done | bytes 8388632
  53.0 3.9 %margin_part.13 = bf16[512,256]{1,0:T(8,128)(2,1)} custom-call(s32[2]{0:T(128)S(1)} %fusion.3.order_ref, f32[2,2]{1,0:T(2,128)S(1)} %get-tuple-element.14.cos_ref, f32[2,2]{1,0:T(2,128)S(1)} %get-tuple-element.13.sin_ref, bf16[2,2,512,2048]{3,2,1,0:T(8,128)(2,1)S(1)} %copy-done.2, bf16[2,128,2048]{2,1,0:T(8,128)(2,1)S(1)} %collective-permute-done.5.there_ref), custom_call_target="tpu_custom_call" | custom-call | flops 1073741824 | bytes 5242880 | tf_op jit(solution)/shard_map/margin_part/pallas_call | solution.py:56
  57.0 1.2 all-to-all-done.6.parts_ref
  58.1 4.8 %all-to-all-start.5 = ((bf16[8,64,256]{2,1,0:T(8,128)(2,1)}), bf16[8,64,256]{2,1,0:T(8,128)(2,1)}, u32[]{:S(2)}, u32[]{:S(2)}) async-start(bf16[8,64,256]{2,1,0:T(8,128)(2,1)} %bitcast.11), calls=%async_computation.5 | async-start | bytes 524288 | tf_op jit(solution)/shard_map/all_to_all | solution.py:134
  63.0 0.4 collective-permute-start.2
  63.4 3.4 %copy-done.3 = bf16[2,2,512,2048]{3,2,1,0:T(8,128)(2,1)S(1)} copy-done((bf16[2,2,512,2048]{3,2,1,0:T(8,128)(2,1)S(1)}, bf16[2,2,512,2048]{3,2,1,0:T(8,128)(2,1)}, u32[]{:S(2)}) %copy-start.3) | copy-done | bytes 8388632
  66.7 3.9 %margin_part.12 = bf16[512,256]{1,0:T(8,128)(2,1)} custom-call(s32[2]{0:T(128)S(1)} %fusion.3.order_ref, f32[2,2]{1,0:T(2,128)S(1)} %get-tuple-element.14.cos_ref, f32[2,2]{1,0:T(2,128)S(1)} %get-tuple-element.13.sin_ref, bf16[2,2,512,2048]{3,2,1,0:T(8,128)(2,1)S(1)} %copy-done.3, bf16[2,128,2048]{2,1,0:T(8,128)(2,1)S(1)} %collective-permute-done.4.there_ref), custom_call_target="tpu_custom_call" | custom-call | flops 1073741824 | bytes 5242880 | tf_op jit(solution)/shard_map/margin_part/pallas_call | solution.py:56
  70.7 2.0 %all-to-all-done.5.parts_ref = bf16[8,64,256]{2,1,0:T(8,128)(2,1)} async-done(((bf16[8,64,256]{2,1,0:T(8,128)(2,1)}), bf16[8,64,256]{2,1,0:T(8,128)(2,1)}, u32[]{:S(2)}, u32[]{:S(2)}) %all-to-all-start.5) | async-done | bytes 262176 | tf_op jit(solution)/shard_map/all_to_all | solution.py:134
  72.7 4.0 %all-to-all-start.4 = ((bf16[8,64,256]{2,1,0:T(8,128)(2,1)}), bf16[8,64,256]{2,1,0:T(8,128)(2,1)}, u32[]{:S(2)}, u32[]{:S(2)}) async-start(bf16[8,64,256]{2,1,0:T(8,128)(2,1)} %bitcast.9), calls=%async_computation.4 | async-start | bytes 524288 | tf_op jit(solution)/shard_map/all_to_all | solution.py:134
  76.8 3.4 %copy-done.4 = bf16[2,2,512,2048]{3,2,1,0:T(8,128)(2,1)S(1)} copy-done((bf16[2,2,512,2048]{3,2,1,0:T(8,128)(2,1)S(1)}, bf16[2,2,512,2048]{3,2,1,0:T(8,128)(2,1)}, u32[]{:S(2)}) %copy-start.4) | copy-done | bytes 8388632
  80.2 3.9 %margin_part.11 = bf16[512,256]{1,0:T(8,128)(2,1)} custom-call(s32[2]{0:T(128)S(1)} %fusion.3.order_ref, f32[2,2]{1,0:T(2,128)S(1)} %get-tuple-element.14.cos_ref, f32[2,2]{1,0:T(2,128)S(1)} %get-tuple-element.13.sin_ref, bf16[2,2,512,2048]{3,2,1,0:T(8,128)(2,1)S(1)} %copy-done.4, bf16[2,128,2048]{2,1,0:T(8,128)(2,1)S(1)} %collective-permute-done.3.there_ref), custom_call_target="tpu_custom_call" | custom-call | flops 1073741824 | bytes 5242880 | tf_op jit(solution)/shard_map/margin_part/pallas_call | solution.py:56
  84.1 1.9 %all-to-all-done.4.parts_ref = bf16[8,64,256]{2,1,0:T(8,128)(2,1)} async-done(((bf16[8,64,256]{2,1,0:T(8,128)(2,1)}), bf16[8,64,256]{2,1,0:T(8,128)(2,1)}, u32[]{:S(2)}, u32[]{:S(2)}) %all-to-all-start.4) | async-done | bytes 262176 | tf_op jit(solution)/shard_map/all_to_all | solution.py:134
  86.0 3.9 %all-to-all-start.3 = ((bf16[8,64,256]{2,1,0:T(8,128)(2,1)}), bf16[8,64,256]{2,1,0:T(8,128)(2,1)S(1)}, u32[]{:S(2)}, u32[]{:S(2)}) async-start(bf16[8,64,256]{2,1,0:T(8,128)(2,1)} %bitcast.7), calls=%async_computation.3 | async-start | bytes 524288 | tf_op jit(solution)/shard_map/all_to_all | solution.py:134
  89.9 1.1 collective-permute-start
  91.0 3.4 %copy-done.5 = bf16[2,2,512,2048]{3,2,1,0:T(8,128)(2,1)S(1)} copy-done((bf16[2,2,512,2048]{3,2,1,0:T(8,128)(2,1)S(1)}, bf16[2,2,512,2048]{3,2,1,0:T(8,128)(2,1)}, u32[]{:S(2)}) %copy-start.5) | copy-done | bytes 8388632
  94.4 3.9 %margin_part.10 = bf16[512,256]{1,0:T(8,128)(2,1)} custom-call(s32[2]{0:T(128)S(1)} %fusion.3.order_ref, f32[2,2]{1,0:T(2,128)S(1)} %get-tuple-element.14.cos_ref, f32[2,2]{1,0:T(2,128)S(1)} %get-tuple-element.13.sin_ref, bf16[2,2,512,2048]{3,2,1,0:T(8,128)(2,1)S(1)} %copy-done.5, bf16[2,128,2048]{2,1,0:T(8,128)(2,1)S(1)} %collective-permute-done.2.there_ref), custom_call_target="tpu_custom_call" | custom-call | flops 1073741824 | bytes 5242880 | tf_op jit(solution)/shard_map/margin_part/pallas_call | solution.py:56
  98.4 1.2 all-to-all-done.3.parts_ref
  99.5 4.5 %all-to-all-start.2 = ((bf16[8,64,256]{2,1,0:T(8,128)(2,1)}), bf16[8,64,256]{2,1,0:T(8,128)(2,1)S(1)}, u32[]{:S(2)}, u32[]{:S(2)}) async-start(bf16[8,64,256]{2,1,0:T(8,128)(2,1)} %bitcast.5), calls=%async_computation.2 | async-start | bytes 524288 | tf_op jit(solution)/shard_map/all_to_all | solution.py:134
  104.1 3.4 %copy-done.6 = bf16[2,2,512,2048]{3,2,1,0:T(8,128)(2,1)S(1)} copy-done((bf16[2,2,512,2048]{3,2,1,0:T(8,128)(2,1)S(1)}, bf16[2,2,512,2048]{3,2,1,0:T(8,128)(2,1)}, u32[]{:S(2)}) %copy-start.6) | copy-done | bytes 8388632
  107.5 3.9 %margin_part.9 = bf16[512,256]{1,0:T(8,128)(2,1)} custom-call(s32[2]{0:T(128)S(1)} %fusion.3.order_ref, f32[2,2]{1,0:T(2,128)S(1)} %get-tuple-element.14.cos_ref, f32[2,2]{1,0:T(2,128)S(1)} %get-tuple-element.13.sin_ref, bf16[2,2,512,2048]{3,2,1,0:T(8,128)(2,1)S(1)} %copy-done.6, bf16[2,128,2048]{2,1,0:T(8,128)(2,1)S(1)} %collective-permute-done.1.there_ref), custom_call_target="tpu_custom_call" | custom-call | flops 1073741824 | bytes 5242880 | tf_op jit(solution)/shard_map/margin_part/pallas_call | solution.py:56
  111.4 1.5 all-to-all-done.2.parts_ref
  112.9 4.5 %all-to-all-start.1 = ((bf16[8,64,256]{2,1,0:T(8,128)(2,1)}), bf16[8,64,256]{2,1,0:T(8,128)(2,1)S(1)}, u32[]{:S(2)}, u32[]{:S(2)}) async-start(bf16[8,64,256]{2,1,0:T(8,128)(2,1)} %bitcast.3), calls=%async_computation.1 | async-start | bytes 524288 | tf_op jit(solution)/shard_map/all_to_all | solution.py:134
  117.4 3.4 %copy-done.7 = bf16[2,2,512,2048]{3,2,1,0:T(8,128)(2,1)S(1)} copy-done((bf16[2,2,512,2048]{3,2,1,0:T(8,128)(2,1)S(1)}, bf16[2,2,512,2048]{3,2,1,0:T(8,128)(2,1)}, u32[]{:S(2)}) %copy-start.7) | copy-done | bytes 8388632
  120.8 3.9 %margin_part.8 = bf16[512,256]{1,0:T(8,128)(2,1)} custom-call(s32[2]{0:T(128)S(1)} %fusion.3.order_ref, f32[2,2]{1,0:T(2,128)S(1)} %get-tuple-element.14.cos_ref, f32[2,2]{1,0:T(2,128)S(1)} %get-tuple-element.13.sin_ref, bf16[2,2,512,2048]{3,2,1,0:T(8,128)(2,1)S(1)} %copy-done.7, bf16[2,128,2048]{2,1,0:T(8,128)(2,1)S(1)} %collective-permute-done.there_ref), custom_call_target="tpu_custom_call" | custom-call | flops 1073741824 | bytes 5242880 | tf_op jit(solution)/shard_map/margin_part/pallas_call | solution.py:56
  124.7 1.0 all-to-all-done.1.parts_ref
  125.8 5.0 %all-to-all-start = ((bf16[8,64,256]{2,1,0:T(8,128)(2,1)}), bf16[8,64,256]{2,1,0:T(8,128)(2,1)S(1)}, u32[]{:S(2)}, u32[]{:S(2)}) async-start(bf16[8,64,256]{2,1,0:T(8,128)(2,1)} %bitcast.1), calls=%async_computation | async-start | bytes 524288 | tf_op jit(solution)/shard_map/all_to_all | solution.py:134
  130.7 2.3 %add_part.8.rest_0_ = f32[64,2,2,512]{3,2,1,0:T(2,128)} custom-call(s32[2]{0:T(128)} %copy-done.8, bf16[8,64,256]{2,1,0:T(8,128)(2,1)} %copy-done.14), custom_call_target="tpu_custom_call" | custom-call | flops 131072 | bytes 262144 | tf_op jit(solution)/shard_map/add_part/pallas_call | solution.py:96
  133.0 2.3 %add_part.9.rest_0_ = f32[64,2,2,512]{3,2,1,0:T(2,128)} custom-call(s32[2]{0:T(128)} %copy-done.8, bf16[8,64,256]{2,1,0:T(8,128)(2,1)} %copy-done.9, f32[64,2,2,512]{3,2,1,0:T(2,128)} %add_part.8.rest_0_), custom_call_target="tpu_custom_call", output_to_operand_aliasing={{}: (2, {})} | custom-call | flops 131072 | bytes 262144 | tf_op jit(solution)/shard_map/add_part/pallas_call | solution.py:96
  135.3 2.3 %add_part.10.rest_0_ = f32[64,2,2,512]{3,2,1,0:T(2,128)} custom-call(s32[2]{0:T(128)} %copy-done.8, bf16[8,64,256]{2,1,0:T(8,128)(2,1)} %all-to-all-done.5.parts_ref, f32[64,2,2,512]{3,2,1,0:T(2,128)} %add_part.9.rest_0_), custom_call_target="tpu_custom_call", output_to_operand_aliasing={{}: (2, {})} | custom-call | flops 131072 | bytes 262144 | tf_op jit(solution)/shard_map/add_part/pallas_call | solution.py:96
  137.7 2.3 %add_part.11.rest_0_ = f32[64,2,2,512]{3,2,1,0:T(2,128)} custom-call(s32[2]{0:T(128)} %copy-done.8, bf16[8,64,256]{2,1,0:T(8,128)(2,1)} %all-to-all-done.4.parts_ref, f32[64,2,2,512]{3,2,1,0:T(2,128)} %add_part.10.rest_0_), custom_call_target="tpu_custom_call", output_to_operand_aliasing={{}: (2, {})} | custom-call | flops 131072 | bytes 262144 | tf_op jit(solution)/shard_map/add_part/pallas_call | solution.py:96
  140.0 2.3 %add_part.12.rest_0_ = f32[64,2,2,512]{3,2,1,0:T(2,128)} custom-call(s32[2]{0:T(128)} %copy-done.8, bf16[8,64,256]{2,1,0:T(8,128)(2,1)} %copy-done.10, f32[64,2,2,512]{3,2,1,0:T(2,128)} %add_part.11.rest_0_), custom_call_target="tpu_custom_call", output_to_operand_aliasing={{}: (2, {})} | custom-call | flops 131072 | bytes 262144 | tf_op jit(solution)/shard_map/add_part/pallas_call | solution.py:96
  142.3 2.3 %add_part.13.rest_0_ = f32[64,2,2,512]{3,2,1,0:T(2,128)} custom-call(s32[2]{0:T(128)} %copy-done.8, bf16[8,64,256]{2,1,0:T(8,128)(2,1)} %copy-done.11, f32[64,2,2,512]{3,2,1,0:T(2,128)} %add_part.12.rest_0_), custom_call_target="tpu_custom_call", output_to_operand_aliasing={{}: (2, {})} | custom-call | flops 131072 | bytes 262144 | tf_op jit(solution)/shard_map/add_part/pallas_call | solution.py:96
  144.6 2.3 %add_part.14.rest_0_ = f32[64,2,2,512]{3,2,1,0:T(2,128)} custom-call(s32[2]{0:T(128)} %copy-done.8, bf16[8,64,256]{2,1,0:T(8,128)(2,1)} %copy-done.12, f32[64,2,2,512]{3,2,1,0:T(2,128)} %add_part.13.rest_0_), custom_call_target="tpu_custom_call", output_to_operand_aliasing={{}: (2, {})} | custom-call | flops 131072 | bytes 262144 | tf_op jit(solution)/shard_map/add_part/pallas_call | solution.py:96
  146.9 0.7 copy-done.13
  147.6 2.3 %add_part.15 = f32[64,2,2,512]{3,2,1,0:T(2,128)} custom-call(s32[2]{0:T(128)} %copy-done.8, bf16[8,64,256]{2,1,0:T(8,128)(2,1)} %copy-done.13, f32[64,2,2,512]{3,2,1,0:T(2,128)} %add_part.14.rest_0_), custom_call_target="tpu_custom_call", output_to_operand_aliasing={{}: (2, {})} | custom-call | flops 131072 | bytes 262144 | tf_op jit(solution)/shard_map/add_part/pallas_call | solution.py:96
  (38 shorter events, 0.4 us)
Async XLA Ops:
  0.0 9.3 %copy-start.15 = (s32[2]{0:T(128)S(1)}, s32[2]{0:T(128)}, u32[]{:S(2)}) copy-start(s32[2]{0:T(128)} %param.5) | copy-start | bytes 28
  0.0 9.5 %copy-start.16 = (s32[2]{0:T(128)S(1)}, s32[2]{0:T(128)}, u32[]{:S(2)}) copy-start(s32[2]{0:T(128)} %param.4) | copy-start | bytes 28
  6.1 15.1 %collective-permute-start.7 = (bf16[2,128,2048]{2,1,0:T(8,128)(2,1)}, bf16[2,128,2048]{2,1,0:T(8,128)(2,1)S(1)}, u32[]{:S(2)}, u32[]{:S(2)}) collective-permute-start(bf16[2,128,2048]{2,1,0:T(8,128)(2,1)} %get-tuple-element.5), channel_id=1, source_target_pairs={{8,0},{16,8},{24,16},{0,24},{9,1},{17,9},{25,17},{1,25},{10,2},{18... | collective-permute-start | bytes 3145736 | tf_op jit(solution)/shard_map/ppermute | solution.py:20
  8.6 27.3 %collective-permute-start.6 = (bf16[2,128,2048]{2,1,0:T(8,128)(2,1)}, bf16[2,128,2048]{2,1,0:T(8,128)(2,1)S(1)}, u32[]{:S(2)}, u32[]{:S(2)}) collective-permute-start(bf16[2,128,2048]{2,1,0:T(8,128)(2,1)} %get-tuple-element.6), channel_id=1, source_target_pairs={{8,0},{16,8},{24,16},{0,24},{9,1},{17,9},{25,17},{1,25},{10,2},{18... | collective-permute-start | bytes 3145736 | tf_op jit(solution)/shard_map/ppermute | solution.py:20
  9.3 40.4 %collective-permute-start.5 = (bf16[2,128,2048]{2,1,0:T(8,128)(2,1)}, bf16[2,128,2048]{2,1,0:T(8,128)(2,1)S(1)}, u32[]{:S(2)}, u32[]{:S(2)}) collective-permute-start(bf16[2,128,2048]{2,1,0:T(8,128)(2,1)} %get-tuple-element.7), channel_id=1, source_target_pairs={{8,0},{16,8},{24,16},{0,24},{9,1},{17,9},{25,17},{1,25},{10,2},{18... | collective-permute-start | bytes 3145736 | tf_op jit(solution)/shard_map/ppermute | solution.py:20
  9.6 107.8 %copy-start.8 = (s32[2]{0:T(128)}, s32[2]{0:T(128)S(1)}, u32[]{:S(2)}) copy-start(s32[2]{0:T(128)S(1)} %fusion.3.order_ref) | copy-start | bytes 28
  21.2 3.4 %copy-start = (bf16[2,2,512,2048]{3,2,1,0:T(8,128)(2,1)S(1)}, bf16[2,2,512,2048]{3,2,1,0:T(8,128)(2,1)}, u32[]{:S(2)}) copy-start(bf16[2,2,512,2048]{3,2,1,0:T(8,128)(2,1)} %own_ref.15) | copy-start | bytes 25165828
  28.5 15.6 %all-to-all-start.7 = ((bf16[8,64,256]{2,1,0:T(8,128)(2,1)}), bf16[8,64,256]{2,1,0:T(8,128)(2,1)S(1)}, u32[]{:S(2)}, u32[]{:S(2)}) async-start(bf16[8,64,256]{2,1,0:T(8,128)(2,1)} %bitcast.15), calls=%async_computation.7 | async-start | bytes 524288 | tf_op jit(solution)/shard_map/all_to_all | solution.py:134
  34.4 29.0 %collective-permute-start.4 = (bf16[2,128,2048]{2,1,0:T(8,128)(2,1)}, bf16[2,128,2048]{2,1,0:T(8,128)(2,1)S(1)}, u32[]{:S(2)}, u32[]{:S(2)}) collective-permute-start(bf16[2,128,2048]{2,1,0:T(8,128)(2,1)} %get-tuple-element.8), channel_id=1, source_target_pairs={{8,0},{16,8},{24,16},{0,24},{9,1},{17,9},{25,17},{1,25},{10,2},{18... | collective-permute-start | bytes 3145736 | tf_op jit(solution)/shard_map/ppermute | solution.py:20
  35.9 3.4 %copy-start.1 = (bf16[2,2,512,2048]{3,2,1,0:T(8,128)(2,1)S(1)}, bf16[2,2,512,2048]{3,2,1,0:T(8,128)(2,1)}, u32[]{:S(2)}) copy-start(bf16[2,2,512,2048]{3,2,1,0:T(8,128)(2,1)} %own_ref.15) | copy-start | bytes 25165828
  44.2 0.7 copy-start.14
  44.9 13.3 %all-to-all-start.6 = ((bf16[8,64,256]{2,1,0:T(8,128)(2,1)}), bf16[8,64,256]{2,1,0:T(8,128)(2,1)S(1)}, u32[]{:S(2)}, u32[]{:S(2)}) async-start(bf16[8,64,256]{2,1,0:T(8,128)(2,1)} %bitcast.13), calls=%async_computation.6 | async-start | bytes 524288 | tf_op jit(solution)/shard_map/all_to_all | solution.py:134
  49.6 27.1 %collective-permute-start.3 = (bf16[2,128,2048]{2,1,0:T(8,128)(2,1)}, bf16[2,128,2048]{2,1,0:T(8,128)(2,1)S(1)}, u32[]{:S(2)}, u32[]{:S(2)}) collective-permute-start(bf16[2,128,2048]{2,1,0:T(8,128)(2,1)} %get-tuple-element.9), channel_id=1, source_target_pairs={{8,0},{16,8},{24,16},{0,24},{9,1},{17,9},{25,17},{1,25},{10,2},{18... | collective-permute-start | bytes 3145736 | tf_op jit(solution)/shard_map/ppermute | solution.py:20
  49.7 3.4 %copy-start.2 = (bf16[2,2,512,2048]{3,2,1,0:T(8,128)(2,1)S(1)}, bf16[2,2,512,2048]{3,2,1,0:T(8,128)(2,1)}, u32[]{:S(2)}) copy-start(bf16[2,2,512,2048]{3,2,1,0:T(8,128)(2,1)} %own_ref.15) | copy-start | bytes 25165828
  58.1 26.0 %copy-start.9 = (bf16[8,64,256]{2,1,0:T(8,128)(2,1)}, bf16[8,64,256]{2,1,0:T(8,128)(2,1)S(1)}, u32[]{:S(2)}) copy-start(bf16[8,64,256]{2,1,0:T(8,128)(2,1)S(1)} %all-to-all-done.6.parts_ref) | copy-start | bytes 786436
  58.1 14.5 %all-to-all-start.5 = ((bf16[8,64,256]{2,1,0:T(8,128)(2,1)}), bf16[8,64,256]{2,1,0:T(8,128)(2,1)}, u32[]{:S(2)}, u32[]{:S(2)}) async-start(bf16[8,64,256]{2,1,0:T(8,128)(2,1)} %bitcast.11), calls=%async_computation.5 | async-start | bytes 524288 | tf_op jit(solution)/shard_map/all_to_all | solution.py:134
  63.0 28.1 %collective-permute-start.2 = (bf16[2,128,2048]{2,1,0:T(8,128)(2,1)}, bf16[2,128,2048]{2,1,0:T(8,128)(2,1)S(1)}, u32[]{:S(2)}, u32[]{:S(2)}) collective-permute-start(bf16[2,128,2048]{2,1,0:T(8,128)(2,1)} %get-tuple-element.10), channel_id=1, source_target_pairs={{8,0},{16,8},{24,16},{0,24},{9,1},{17,9},{25,17},{1,25},{10,2},{18... | collective-permute-start | bytes 3145736 | tf_op jit(solution)/shard_map/ppermute | solution.py:20
  63.4 3.4 %copy-start.3 = (bf16[2,2,512,2048]{3,2,1,0:T(8,128)(2,1)S(1)}, bf16[2,2,512,2048]{3,2,1,0:T(8,128)(2,1)}, u32[]{:S(2)}) copy-start(bf16[2,2,512,2048]{3,2,1,0:T(8,128)(2,1)} %own_ref.15) | copy-start | bytes 25165828
  72.7 13.4 %all-to-all-start.4 = ((bf16[8,64,256]{2,1,0:T(8,128)(2,1)}), bf16[8,64,256]{2,1,0:T(8,128)(2,1)}, u32[]{:S(2)}, u32[]{:S(2)}) async-start(bf16[8,64,256]{2,1,0:T(8,128)(2,1)} %bitcast.9), calls=%async_computation.4 | async-start | bytes 524288 | tf_op jit(solution)/shard_map/all_to_all | solution.py:134
  76.7 27.4 %collective-permute-start.1 = (bf16[2,128,2048]{2,1,0:T(8,128)(2,1)}, bf16[2,128,2048]{2,1,0:T(8,128)(2,1)S(1)}, u32[]{:S(2)}, u32[]{:S(2)}) collective-permute-start(bf16[2,128,2048]{2,1,0:T(8,128)(2,1)} %get-tuple-element.11), channel_id=1, source_target_pairs={{8,0},{16,8},{24,16},{0,24},{9,1},{17,9},{25,17},{1,25},{10,2},{18... | collective-permute-start | bytes 3145736 | tf_op jit(solution)/shard_map/ppermute | solution.py:20
  76.8 3.4 %copy-start.4 = (bf16[2,2,512,2048]{3,2,1,0:T(8,128)(2,1)S(1)}, bf16[2,2,512,2048]{3,2,1,0:T(8,128)(2,1)}, u32[]{:S(2)}) copy-start(bf16[2,2,512,2048]{3,2,1,0:T(8,128)(2,1)} %own_ref.15) | copy-start | bytes 25165828
  86.0 13.5 %all-to-all-start.3 = ((bf16[8,64,256]{2,1,0:T(8,128)(2,1)}), bf16[8,64,256]{2,1,0:T(8,128)(2,1)S(1)}, u32[]{:S(2)}, u32[]{:S(2)}) async-start(bf16[8,64,256]{2,1,0:T(8,128)(2,1)} %bitcast.7), calls=%async_computation.3 | async-start | bytes 524288 | tf_op jit(solution)/shard_map/all_to_all | solution.py:134
  89.9 27.4 %collective-permute-start = (bf16[2,128,2048]{2,1,0:T(8,128)(2,1)}, bf16[2,128,2048]{2,1,0:T(8,128)(2,1)S(1)}, u32[]{:S(2)}, u32[]{:S(2)}) collective-permute-start(bf16[2,128,2048]{2,1,0:T(8,128)(2,1)} %get-tuple-element.12), channel_id=1, source_target_pairs={{8,0},{16,8},{24,16},{0,24},{9,1},{17,9},{25,17},{1,25},{10,2},{18... | collective-permute-start | bytes 3145736 | tf_op jit(solution)/shard_map/ppermute | solution.py:20
  91.0 3.4 %copy-start.5 = (bf16[2,2,512,2048]{3,2,1,0:T(8,128)(2,1)S(1)}, bf16[2,2,512,2048]{3,2,1,0:T(8,128)(2,1)}, u32[]{:S(2)}) copy-start(bf16[2,2,512,2048]{3,2,1,0:T(8,128)(2,1)} %own_ref.15) | copy-start | bytes 25165828
  99.5 25.2 %copy-start.10 = (bf16[8,64,256]{2,1,0:T(8,128)(2,1)}, bf16[8,64,256]{2,1,0:T(8,128)(2,1)S(1)}, u32[]{:S(2)}) copy-start(bf16[8,64,256]{2,1,0:T(8,128)(2,1)S(1)} %all-to-all-done.3.parts_ref) | copy-start | bytes 786436
  99.5 13.3 %all-to-all-start.2 = ((bf16[8,64,256]{2,1,0:T(8,128)(2,1)}), bf16[8,64,256]{2,1,0:T(8,128)(2,1)S(1)}, u32[]{:S(2)}, u32[]{:S(2)}) async-start(bf16[8,64,256]{2,1,0:T(8,128)(2,1)} %bitcast.5), calls=%async_computation.2 | async-start | bytes 524288 | tf_op jit(solution)/shard_map/all_to_all | solution.py:134
  104.1 3.4 %copy-start.6 = (bf16[2,2,512,2048]{3,2,1,0:T(8,128)(2,1)S(1)}, bf16[2,2,512,2048]{3,2,1,0:T(8,128)(2,1)}, u32[]{:S(2)}) copy-start(bf16[2,2,512,2048]{3,2,1,0:T(8,128)(2,1)} %own_ref.15) | copy-start | bytes 25165828
  112.9 29.4 %copy-start.11 = (bf16[8,64,256]{2,1,0:T(8,128)(2,1)}, bf16[8,64,256]{2,1,0:T(8,128)(2,1)S(1)}, u32[]{:S(2)}) copy-start(bf16[8,64,256]{2,1,0:T(8,128)(2,1)S(1)} %all-to-all-done.2.parts_ref) | copy-start | bytes 786436
  112.9 12.9 %all-to-all-start.1 = ((bf16[8,64,256]{2,1,0:T(8,128)(2,1)}), bf16[8,64,256]{2,1,0:T(8,128)(2,1)S(1)}, u32[]{:S(2)}, u32[]{:S(2)}) async-start(bf16[8,64,256]{2,1,0:T(8,128)(2,1)} %bitcast.3), calls=%async_computation.1 | async-start | bytes 524288 | tf_op jit(solution)/shard_map/all_to_all | solution.py:134
  117.4 3.4 %copy-start.7 = (bf16[2,2,512,2048]{3,2,1,0:T(8,128)(2,1)S(1)}, bf16[2,2,512,2048]{3,2,1,0:T(8,128)(2,1)}, u32[]{:S(2)}) copy-start(bf16[2,2,512,2048]{3,2,1,0:T(8,128)(2,1)} %own_ref.15) | copy-start | bytes 25165828
  125.8 18.8 %copy-start.12 = (bf16[8,64,256]{2,1,0:T(8,128)(2,1)}, bf16[8,64,256]{2,1,0:T(8,128)(2,1)S(1)}, u32[]{:S(2)}) copy-start(bf16[8,64,256]{2,1,0:T(8,128)(2,1)S(1)} %all-to-all-done.1.parts_ref) | copy-start | bytes 786436
  125.8 21.1 %all-to-all-start = ((bf16[8,64,256]{2,1,0:T(8,128)(2,1)}), bf16[8,64,256]{2,1,0:T(8,128)(2,1)S(1)}, u32[]{:S(2)}, u32[]{:S(2)}) async-start(bf16[8,64,256]{2,1,0:T(8,128)(2,1)} %bitcast.1), calls=%async_computation | async-start | bytes 524288 | tf_op jit(solution)/shard_map/all_to_all | solution.py:134
  146.9 0.7 copy-start.13

commit v2 on v1

--- a/solution.py
+++ b/solution.py
@@ -10,8 +10,8 @@
 
 NKB = 4
 PLANE = 1024
-WIDTH = 128
 DEPTH = 512
+VMEM_BYTES = 60 * 1024 * 1024
 
 
 def shifted(block, axis, distance):
@@ -20,7 +20,8 @@
     return lax.ppermute(block, axis, route)
 
 
-def margin_kernel(slot, order_ref, cos_ref, sin_ref, own_ref, there_ref, out_ref, acc_ref):
+def margin_kernel(slot, order_ref, cos_ref, sin_ref, own_ref, there_ref, *rest):
+    out_ref, acc_ref = rest[-2:]
     step = pl.program_id(0)
     point = order_ref[slot]
     plane = step * DEPTH // PLANE
@@ -49,7 +50,7 @@
         out_ref[...] = acc_ref[...].astype(out_ref.dtype)
 
 
-def margin_part(slot, order, cosine, sine, bands, there):
+def margin_part(slot, order, cosine, sine, bands, there, after):
     _, _, nbands, points = bands.shape
     width = there.shape[1]
     flops = 2 * nbands * 2 * width * 2 * points
@@ -61,23 +62,25 @@
             in_specs=[
                 pl.BlockSpec((1, 2, nbands, DEPTH), lambda t, order, c, s: (order[slot], 0, 0, t)),
                 pl.BlockSpec((2, width, DEPTH), lambda t, order, c, s: (0, 0, t)),
-            ],
+            ]
+            + [pl.BlockSpec(memory_space=pl.ANY)] * len(after),
             out_specs=pl.BlockSpec((nbands, 2 * width), lambda t, order, c, s: (0, 0)),
             scratch_shapes=[pltpu.VMEM((nbands, 2 * width), jnp.float32)],
         ),
         out_shape=jax.ShapeDtypeStruct((nbands, 2 * width), jnp.bfloat16),
         compiler_params=pltpu.CompilerParams(
-            dimension_semantics=("arbitrary",), vmem_limit_bytes=32 * 1024 * 1024
+            dimension_semantics=("arbitrary",), vmem_limit_bytes=VMEM_BYTES
         ),
         cost_estimate=pl.CostEstimate(
             flops=flops, bytes_accessed=4 * nbands * points + 4 * width * points, transcendentals=0
         ),
         name="margin_part",
-    )(order, cosine, sine, bands, there)
+    )(order, cosine, sine, bands, there, *after)
 
 
 def gather_kernel(order_ref, parts_ref, *rest):
-    out_ref = rest[-1]
+    out_ref, done_ref = rest[-2:]
+    done_ref[...] = jnp.zeros_like(done_ref)
     total = parts_ref[0].astype(jnp.float32)
     for source in range(1, parts_ref.shape[0]):
         total = total + parts_ref[source].astype(jnp.float32)
@@ -99,15 +102,28 @@
             num_scalar_prefetch=1,
             grid=(1,),
             in_specs=in_specs,
-            out_specs=pl.BlockSpec((rows, 1, 2, width), lambda i, order: (0, order[slot], 0, block)),
+            out_specs=[
+                pl.BlockSpec((rows, 1, 2, width), lambda i, order: (0, order[slot], 0, block)),
+                pl.BlockSpec((8, 128), lambda i, order: (0, 0)),
+            ],
         ),
-        out_shape=jax.ShapeDtypeStruct(shape, jnp.float32),
+        out_shape=[
+            jax.ShapeDtypeStruct(shape, jnp.float32),
+            jax.ShapeDtypeStruct((8, 128), jnp.float32),
+        ],
         input_output_aliases={} if result is None else {2: 0},
         cost_estimate=pl.CostEstimate(
             flops=count * rows * wide, bytes_accessed=2 * count * rows * wide, transcendentals=0
         ),
         name="add_part",
     )(*operands)
+
+
+def cuts(nbands, last):
+    half, quarter = nbands // 2, nbands // 4
+    if not last:
+        return [(0, half), (half, half)]
+    return [(0, half), (half, quarter), (half + quarter, quarter)]
 
 
 def body(bands, nbr_slot, gshift):
@@ -124,15 +140,26 @@
     sine = jnp.sin(angle)
     slots = jnp.arange(k_dev, dtype=jnp.int32)
     order = jnp.sum(jnp.where(nbr_slot[None, :] == slots[:, None], slots[None, :], 0), axis=1)
+    parts = []
+    for slot in range(k_dev):
+        last = slot == k_dev - 1
+        for start, width in cuts(nbands, last):
+            parts.append((slot, start, width))
+    sources = bands
+    theres = []
+    for slot, start, width in parts:
+        piece = sources[slot, :, start : start + width, :]
+        piece, sources = lax.optimization_barrier((piece, sources))
+        theres.append(shifted(piece, "ka", -1))
     result = None
-    for slot in range(k_dev):
-        for block in range(nbands // WIDTH):
-            piece = bands[slot, :, block * WIDTH : (block + 1) * WIDTH, :]
-            there = shifted(piece, "ka", -1)
-            part = margin_part(slot, order, cosine, sine, bands, there)
-            part = part.reshape(grid_count, rows, 2 * WIDTH)
-            parts = lax.all_to_all(part, "ga", 0, 0)
-            result = add_part(slot, block, order, parts, result, (rows, k_dev, 2, nbands))
+    done = []
+    for (slot, start, width), there in zip(parts, theres):
+        part = margin_part(slot, order, cosine, sine, bands, there, done[-2:-1])
+        part = part.reshape(grid_count, rows, 2 * width)
+        arrived = lax.all_to_all(part, "ga", 0, 0)
+        shape = (rows, k_dev, 2, nbands)
+        result, token = add_part(slot, start // width, order, arrived, result, shape)
+        done.append(token)
     return result
 
 

time: 151 us -> 135 us (0.89)
  local copies, waits for them, and re-layouts: 34.6 us -> 14.5 us
  waiting for transfers between devices: 21.4 us -> 39.4 us
  starting transfers between devices: 43.6 us -> 33.6 us
  Pallas kernels: 50 us -> 44.7 us
    unnamed x34 -> x16, local copies, waits for them, and re-layouts: 28.5 us -> 1.73 us
    ppermute x8 -> x5, waiting for transfers between devices: 11.7 us -> 29.4 us  [shifted(): return lax.ppermute(block, axis, route)]
    all_to_all x8 -> x5, starting transfers between devices: 37.3 us -> 26.7 us  [body(): arrived = lax.all_to_all(part, 'ga', 0, 0)]
    squeeze x1 -> x5, local copies, waits for them, and re-layouts: 6.13 us -> 12.8 us  [body(): piece = sources[slot, :, start:start + width, :]]
    pallas_call x8 -> x5, Pallas kernels: 18.5 us -> 12 us  [add_part(): pl.pallas_call(gather_kernel, grid_spec=pltpu.PrefetchScalarGridSpec(num_...]
    pallas_call x8 -> x5, Pallas kernels: 31.5 us -> 32.7 us  [margin_part(): pl.pallas_call(functools.partial(margin_kernel, slot), grid_spec=pltpu.Pr...]
    ppermute x8 -> x5, starting transfers between devices: 6.25 us -> 6.9 us  [shifted(): return lax.ppermute(block, axis, route)]
    all_to_all x8 -> x5, waiting for transfers between devices: 9.73 us -> 10.1 us  [body(): arrived = lax.all_to_all(part, 'ga', 0, 0)]
  transfers between devices with their start and end apart: 16 -> 10, of which waited for: 8 -> 6; matrix products, arithmetic and copies ran while one was open for 0% -> 8% of each run, Pallas kernels for 32% -> 32%
where the time goes in v2:
time: 135 us; the launch traced here: 134 us
  Pallas kernels  44.7 us (33%)
  waiting for transfers between devices  39.4 us (29%)
  starting transfers between devices  33.6 us (25%)
  local copies, waits for them, and re-layouts  14.5 us (11%)
    pallas_call x5, Pallas kernels, margin_part(): pl.pallas_call(functools.partial(margin_kernel, slot), grid_spec=pltpu.Pr...  32.7 us
    ppermute x5, waiting for transfers between devices, shifted(): return lax.ppermute(block, axis, route)  29.4 us
    all_to_all x5, starting transfers between devices, body(): arrived = lax.all_to_all(part, 'ga', 0, 0)  26.7 us
    squeeze x5, local copies, waits for them, and re-layouts, body(): piece = sources[slot, :, start:start + width, :]  12.8 us
    pallas_call x5, Pallas kernels, add_part(): pl.pallas_call(gather_kernel, grid_spec=pltpu.PrefetchScalarGridSpec(num_...  12 us
    all_to_all x5, waiting for transfers between devices, body(): arrived = lax.all_to_all(part, 'ga', 0, 0)  10.1 us
    ppermute x5, starting transfers between devices, shifted(): return lax.ppermute(block, axis, route)  6.9 us
  transfers between devices with their start and end apart: 10, of which 6 were waited for; matrix products, arithmetic and copies ran while one was open for 8% of the time, Pallas kernels for 32%

profile of v2, /device:TPU:0, one launch (start us, length us, event | category | flops | bytes accessed | tf_op | source)
XLA Modules:
  0.0 133.6 jit_solution(345491454642786926)
XLA Ops:
  0.0 3.2 %slice_bitcast_fusion.2 = bf16[2,256,2048]{2,1,0:T(8,128)(2,1)} fusion(bf16[2,2,512,2048]{3,2,1,0:T(8,128)(2,1)} %own_ref.9), kind=kLoop, calls=%fused_computation.2 | loop fusion | bytes 4194304 | tf_op jit(solution)/shard_map/squeeze | solution.py:151
  3.2 2.4 %collective-permute-start.2 = (bf16[2,256,2048]{2,1,0:T(8,128)(2,1)}, bf16[2,256,2048]{2,1,0:T(8,128)(2,1)}, u32[]{:S(2)}, u32[]{:S(2)}) collective-permute-start(bf16[2,256,2048]{2,1,0:T(8,128)(2,1)} %slice_bitcast_fusion.2), channel_id=1, source_target_pairs={{8,0},{16,8},{24,16},{0,24},{9,1},{17,9},{25,17},{1,25},{10,2},{18... | collective-permute-start | bytes 6291464 | tf_op jit(solution)/shard_map/ppermute | solution.py:20
  5.6 3.2 %slice_bitcast_fusion.1 = bf16[2,256,2048]{2,1,0:T(8,128)(2,1)} fusion(bf16[2,2,512,2048]{3,2,1,0:T(8,128)(2,1)} %own_ref.9), kind=kLoop, calls=%fused_computation.1 | loop fusion | bytes 4194304 | tf_op jit(solution)/shard_map/squeeze | solution.py:151
  8.8 0.0 copy-start.6
  8.8 0.0 copy-start.7
  8.8 0.7 collective-permute-start.3
  9.5 1.7 %slice_bitcast_fusion = bf16[2,256,2048]{2,1,0:T(8,128)(2,1)S(1)} fusion(bf16[2,2,512,2048]{3,2,1,0:T(8,128)(2,1)} %own_ref.9), kind=kLoop, calls=%fused_computation | loop fusion | bytes 4194304 | tf_op jit(solution)/shard_map/squeeze | solution.py:151
  11.2 0.1 collective-permute-start.1
  11.3 0.0 copy-done.6
  11.3 0.0 copy-done.7
  11.3 0.7 fusion.3.order_ref
  12.0 0.6 fusion.4
  12.6 16.8 %collective-permute-done.2.there_ref = bf16[2,256,2048]{2,1,0:T(8,128)(2,1)} collective-permute-done((bf16[2,256,2048]{2,1,0:T(8,128)(2,1)}, bf16[2,256,2048]{2,1,0:T(8,128)(2,1)}, u32[]{:S(2)}, u32[]{:S(2)}) %collective-permute-start.2) | collective-permute-done | bytes 2097184 | tf_op jit(solution)/shard_map/ppermute | solution.py:20
  29.5 7.0 %margin_part.5 = bf16[512,512]{1,0:T(8,128)(2,1)} custom-call(s32[2]{0:T(128)} %fusion.3.order_ref, f32[2,2]{1,0:T(2,128)} %get-tuple-element.40.cos_ref, f32[2,2]{1,0:T(2,128)} %get-tuple-element.39.sin_ref, bf16[2,2,512,2048]{3,2,1,0:T(8,128)(2,1)} %own_ref.9, bf16[2,256,2048]{2,1,0:T(8,128)(2,1)} %collective-permute-done.2.there_ref), custom_call_target="tpu_custom_call" | custom-call | flops 2147483648 | bytes 6291456 | tf_op jit(solution)/shard_map/margin_part/pallas_call | solution.py:57
  36.5 5.8 %all-to-all-start = ((bf16[8,64,512]{2,1,0:T(8,128)(2,1)}), bf16[8,64,512]{2,1,0:T(8,128)(2,1)S(1)}, u32[]{:S(2)}, u32[]{:S(2)}) async-start(bf16[8,64,512]{2,1,0:T(8,128)(2,1)} %bitcast.17), calls=%async_computation | async-start | bytes 1048576 | tf_op jit(solution)/shard_map/all_to_all | solution.py:159
  42.3 9.6 %collective-permute-done.3.there_ref = bf16[2,256,2048]{2,1,0:T(8,128)(2,1)} collective-permute-done((bf16[2,256,2048]{2,1,0:T(8,128)(2,1)}, bf16[2,256,2048]{2,1,0:T(8,128)(2,1)}, u32[]{:S(2)}, u32[]{:S(2)}) %collective-permute-start.3) | collective-permute-done | bytes 2097184 | tf_op jit(solution)/shard_map/ppermute | solution.py:20
  51.9 7.1 %margin_part.7 = bf16[512,512]{1,0:T(8,128)(2,1)} custom-call(s32[2]{0:T(128)} %fusion.3.order_ref, f32[2,2]{1,0:T(2,128)} %get-tuple-element.40.cos_ref, f32[2,2]{1,0:T(2,128)} %get-tuple-element.39.sin_ref, bf16[2,2,512,2048]{3,2,1,0:T(8,128)(2,1)} %own_ref.9, bf16[2,256,2048]{2,1,0:T(8,128)(2,1)} %collective-permute-done.3.there_ref), custom_call_target="tpu_custom_call" | custom-call | flops 2147483648 | bytes 6291456 | tf_op jit(solution)/shard_map/margin_part/pallas_call | solution.py:57
  59.0 0.0 all-to-all-done.parts_ref
  59.0 0.0 copy-start.2
  59.0 5.8 %all-to-all-start.2 = ((bf16[8,64,512]{2,1,0:T(8,128)(2,1)}), bf16[8,64,512]{2,1,0:T(8,128)(2,1)S(1)}, u32[]{:S(2)}, u32[]{:S(2)}) async-start(bf16[8,64,512]{2,1,0:T(8,128)(2,1)} %bitcast.16), calls=%async_computation.2 | async-start | bytes 1048576 | tf_op jit(solution)/shard_map/all_to_all | solution.py:159
  64.8 2.3 %slice_bitcast_fusion.4 = bf16[2,128,2048]{2,1,0:T(8,128)(2,1)} fusion(bf16[2,2,512,2048]{3,2,1,0:T(8,128)(2,1)} %own_ref.9), kind=kLoop, calls=%fused_computation.4 | loop fusion | bytes 2097152 | tf_op jit(solution)/shard_map/squeeze | solution.py:151
  67.1 1.8 %collective-permute-start.4 = (bf16[2,128,2048]{2,1,0:T(8,128)(2,1)}, bf16[2,128,2048]{2,1,0:T(8,128)(2,1)}, u32[]{:S(2)}, u32[]{:S(2)}) collective-permute-start(bf16[2,128,2048]{2,1,0:T(8,128)(2,1)} %slice_bitcast_fusion.4), channel_id=1, source_target_pairs={{8,0},{16,8},{24,16},{0,24},{9,1},{17,9},{25,17},{1,25},{10,2},{18... | collective-permute-start | bytes 3145736 | tf_op jit(solution)/shard_map/ppermute | solution.py:20
  68.9 0.0 copy-done.2
  68.9 2.5 %add_part.5 = (f32[64,2,2,512]{3,2,1,0:T(2,128)}, f32[8,128]{1,0:T(8,128)}) custom-call(s32[2]{0:T(128)} %fusion.3.order_ref, bf16[8,64,512]{2,1,0:T(8,128)(2,1)} %copy-done.2), custom_call_target="tpu_custom_call" | custom-call | flops 262144 | bytes 524288 | tf_op jit(solution)/shard_map/add_part/pallas_call | solution.py:99
  71.4 2.9 %collective-permute-done.1.there_ref = bf16[2,256,2048]{2,1,0:T(8,128)(2,1)} collective-permute-done((bf16[2,256,2048]{2,1,0:T(8,128)(2,1)S(1)}, bf16[2,256,2048]{2,1,0:T(8,128)(2,1)}, u32[]{:S(2)}, u32[]{:S(2)}) %collective-permute-start.1) | collective-permute-done | bytes 2097184 | tf_op jit(solution)/shard_map/ppermute | solution.py:20
  74.3 7.1 %margin_part.6 = bf16[512,512]{1,0:T(8,128)(2,1)} custom-call(s32[2]{0:T(128)} %fusion.3.order_ref, f32[2,2]{1,0:T(2,128)} %get-tuple-element.40.cos_ref, f32[2,2]{1,0:T(2,128)} %get-tuple-element.39.sin_ref, bf16[2,2,512,2048]{3,2,1,0:T(8,128)(2,1)} %own_ref.9, bf16[2,256,2048]{2,1,0:T(8,128)(2,1)} %collective-permute-done.1.there_ref, ...), custom_call_target="tpu_custom_call" | custom-call | flops 2147483648 | bytes 6291456 | tf_op jit(solution)/shard_map/margin_part/pallas_call | solution.py:57
  81.4 0.0 all-to-all-done.2.parts_ref
  81.4 5.8 %all-to-all-start.1 = ((bf16[8,64,512]{2,1,0:T(8,128)(2,1)}), bf16[8,64,512]{2,1,0:T(8,128)(2,1)S(1)}, u32[]{:S(2)}, u32[]{:S(2)}) async-start(bf16[8,64,512]{2,1,0:T(8,128)(2,1)} %bitcast.15), calls=%async_computation.1 | async-start | bytes 1048576 | tf_op jit(solution)/shard_map/all_to_all | solution.py:159
  87.2 2.3 %slice_bitcast_fusion.3 = bf16[2,128,2048]{2,1,0:T(8,128)(2,1)} fusion(bf16[2,2,512,2048]{3,2,1,0:T(8,128)(2,1)} %own_ref.9), kind=kLoop, calls=%fused_computation.3 | loop fusion | bytes 2097152 | tf_op jit(solution)/shard_map/squeeze | solution.py:151
  89.5 1.9 %collective-permute-start = (bf16[2,128,2048]{2,1,0:T(8,128)(2,1)}, bf16[2,128,2048]{2,1,0:T(8,128)(2,1)S(1)}, u32[]{:S(2)}, u32[]{:S(2)}) collective-permute-start(bf16[2,128,2048]{2,1,0:T(8,128)(2,1)} %slice_bitcast_fusion.3), channel_id=1, source_target_pairs={{8,0},{16,8},{24,16},{0,24},{9,1},{17,9},{25,17},{1,25},{10,2},{18... | collective-permute-start | bytes 3145736 | tf_op jit(solution)/shard_map/ppermute | solution.py:20
  91.4 0.0 copy-done
  91.4 2.5 %add_part.6 = (f32[64,2,2,512]{3,2,1,0:T(2,128)}, f32[8,128]{1,0:T(8,128)}) custom-call(s32[2]{0:T(128)} %fusion.3.order_ref, bf16[8,64,512]{2,1,0:T(8,128)(2,1)} %copy-done, f32[64,2,2,512]{3,2,1,0:T(2,128)} %get-tuple-element.31.rest_0_), custom_call_target="tpu_custom_call", output_to_operand_aliasing={{0}: (2, {})} | custom-call | flops 262144 | bytes 524288 | tf_op jit(solution)/shard_map/add_part/pallas_call | solution.py:99
  93.9 0.0 collective-permute-done.4.there_ref
  93.9 5.8 %margin_part.9 = bf16[512,256]{1,0:T(8,128)(2,1)} custom-call(s32[2]{0:T(128)} %fusion.3.order_ref, f32[2,2]{1,0:T(2,128)} %get-tuple-element.40.cos_ref, f32[2,2]{1,0:T(2,128)} %get-tuple-element.39.sin_ref, bf16[2,2,512,2048]{3,2,1,0:T(8,128)(2,1)} %own_ref.9, bf16[2,128,2048]{2,1,0:T(8,128)(2,1)} %collective-permute-done.4.there_ref, ...), custom_call_target="tpu_custom_call" | custom-call | flops 1073741824 | bytes 5242880 | tf_op jit(solution)/shard_map/margin_part/pallas_call | solution.py:57
  99.7 3.6 %all-to-all-done.1.parts_ref = bf16[8,64,512]{2,1,0:T(8,128)(2,1)S(1)} async-done(((bf16[8,64,512]{2,1,0:T(8,128)(2,1)}), bf16[8,64,512]{2,1,0:T(8,128)(2,1)S(1)}, u32[]{:S(2)}, u32[]{:S(2)}) %all-to-all-start.1) | async-done | bytes 524320 | tf_op jit(solution)/shard_map/all_to_all | solution.py:159
  103.2 3.4 %all-to-all-start.4 = ((bf16[8,64,256]{2,1,0:T(8,128)(2,1)}), bf16[8,64,256]{2,1,0:T(8,128)(2,1)S(1)}, u32[]{:S(2)}, u32[]{:S(2)}) async-start(bf16[8,64,256]{2,1,0:T(8,128)(2,1)} %bitcast.18), calls=%async_computation.4 | async-start | bytes 524288 | tf_op jit(solution)/shard_map/all_to_all | solution.py:159
  106.7 0.0 copy-done.1
  106.7 2.5 %add_part.7 = (f32[64,2,2,512]{3,2,1,0:T(2,128)}, f32[8,128]{1,0:T(8,128)}) custom-call(s32[2]{0:T(128)} %fusion.3.order_ref, bf16[8,64,512]{2,1,0:T(8,128)(2,1)} %copy-done.1, f32[64,2,2,512]{3,2,1,0:T(2,128)} %get-tuple-element.32.rest_0_), custom_call_target="tpu_custom_call", output_to_operand_aliasing={{0}: (2, {})} | custom-call | flops 262144 | bytes 524288 | tf_op jit(solution)/shard_map/add_part/pallas_call | solution.py:99
  109.1 0.0 collective-permute-done.there_ref
  109.1 1.0 copy-done.3
  110.1 5.7 %margin_part.8 = bf16[512,256]{1,0:T(8,128)(2,1)} custom-call(s32[2]{0:T(128)} %fusion.3.order_ref, f32[2,2]{1,0:T(2,128)} %get-tuple-element.40.cos_ref, f32[2,2]{1,0:T(2,128)} %get-tuple-element.39.sin_ref, bf16[2,2,512,2048]{3,2,1,0:T(8,128)(2,1)} %own_ref.9, bf16[2,128,2048]{2,1,0:T(8,128)(2,1)} %copy-done.3, f32[8,128]{1,0:T(8,128)} %get-tuple-element.33.rest_0_), custom_call_target="tpu_custom_call" | custom-call | flops 1073741824 | bytes 5242880 | tf_op jit(solution)/shard_map/margin_part/pallas_call | solution.py:57
  115.9 0.1 all-to-all-done.4.parts_ref
  116.0 5.9 %all-to-all-start.3 = ((bf16[8,64,256]{2,1,0:T(8,128)(2,1)}), bf16[8,64,256]{2,1,0:T(8,128)(2,1)S(1)}, u32[]{:S(2)}, u32[]{:S(2)}) async-start(bf16[8,64,256]{2,1,0:T(8,128)(2,1)} %bitcast.19), calls=%async_computation.3 | async-start | bytes 524288 | tf_op jit(solution)/shard_map/all_to_all | solution.py:159
  121.9 0.0 copy-done.4
  121.9 2.3 %add_part.8 = (f32[64,2,2,512]{3,2,1,0:T(2,128)}, f32[8,128]{1,0:T(8,128)}) custom-call(s32[2]{0:T(128)} %fusion.3.order_ref, bf16[8,64,256]{2,1,0:T(8,128)(2,1)} %copy-done.4, f32[64,2,2,512]{3,2,1,0:T(2,128)} %get-tuple-element.36.rest_0_), custom_call_target="tpu_custom_call", output_to_operand_aliasing={{0}: (2, {})} | custom-call | flops 131072 | bytes 262144 | tf_op jit(solution)/shard_map/add_part/pallas_call | solution.py:99
  124.2 6.4 %all-to-all-done.3.parts_ref = bf16[8,64,256]{2,1,0:T(8,128)(2,1)S(1)} async-done(((bf16[8,64,256]{2,1,0:T(8,128)(2,1)}), bf16[8,64,256]{2,1,0:T(8,128)(2,1)S(1)}, u32[]{:S(2)}, u32[]{:S(2)}) %all-to-all-start.3) | async-done | bytes 262176 | tf_op jit(solution)/shard_map/all_to_all | solution.py:159
  130.6 0.7 copy-done.5
  131.3 2.3 %add_part.9 = (f32[64,2,2,512]{3,2,1,0:T(2,128)}, f32[8,128]{1,0:T(8,128)}) custom-call(s32[2]{0:T(128)} %fusion.3.order_ref, bf16[8,64,256]{2,1,0:T(8,128)(2,1)} %copy-done.5, f32[64,2,2,512]{3,2,1,0:T(2,128)} %get-tuple-element.37.rest_0_), custom_call_target="tpu_custom_call", output_to_operand_aliasing={{0}: (2, {})} | custom-call | flops 131072 | bytes 262144 | tf_op jit(solution)/shard_map/add_part/pallas_call | solution.py:99
  (6 shorter events, 0.0 us)
Async XLA Ops:
  3.2 26.3 %collective-permute-start.2 = (bf16[2,256,2048]{2,1,0:T(8,128)(2,1)}, bf16[2,256,2048]{2,1,0:T(8,128)(2,1)}, u32[]{:S(2)}, u32[]{:S(2)}) collective-permute-start(bf16[2,256,2048]{2,1,0:T(8,128)(2,1)} %slice_bitcast_fusion.2), channel_id=1, source_target_pairs={{8,0},{16,8},{24,16},{0,24},{9,1},{17,9},{25,17},{1,25},{10,2},{18... | collective-permute-start | bytes 6291464 | tf_op jit(solution)/shard_map/ppermute | solution.py:20
  8.8 2.5 %copy-start.6 = (s32[2]{0:T(128)S(1)}, s32[2]{0:T(128)}, u32[]{:S(2)}) copy-start(s32[2]{0:T(128)} %param.5) | copy-start | bytes 28
  8.8 2.5 %copy-start.7 = (s32[2]{0:T(128)S(1)}, s32[2]{0:T(128)}, u32[]{:S(2)}) copy-start(s32[2]{0:T(128)} %param.4) | copy-start | bytes 28
  8.8 43.1 %collective-permute-start.3 = (bf16[2,256,2048]{2,1,0:T(8,128)(2,1)}, bf16[2,256,2048]{2,1,0:T(8,128)(2,1)}, u32[]{:S(2)}, u32[]{:S(2)}) collective-permute-start(bf16[2,256,2048]{2,1,0:T(8,128)(2,1)} %slice_bitcast_fusion.1), channel_id=1, source_target_pairs={{8,0},{16,8},{24,16},{0,24},{9,1},{17,9},{25,17},{1,25},{10,2},{18... | collective-permute-start | bytes 6291464 | tf_op jit(solution)/shard_map/ppermute | solution.py:20
  11.2 63.1 %collective-permute-start.1 = (bf16[2,256,2048]{2,1,0:T(8,128)(2,1)S(1)}, bf16[2,256,2048]{2,1,0:T(8,128)(2,1)}, u32[]{:S(2)}, u32[]{:S(2)}) collective-permute-start(bf16[2,256,2048]{2,1,0:T(8,128)(2,1)S(1)} %slice_bitcast_fusion), channel_id=1, source_target_pairs={{8,0},{16,8},{24,16},{0,24},{9,1},{17,9},{25,17},{1,25},{10,2},{18... | collective-permute-start | bytes 6291464 | tf_op jit(solution)/shard_map/ppermute | solution.py:20
  36.5 22.5 %all-to-all-start = ((bf16[8,64,512]{2,1,0:T(8,128)(2,1)}), bf16[8,64,512]{2,1,0:T(8,128)(2,1)S(1)}, u32[]{:S(2)}, u32[]{:S(2)}) async-start(bf16[8,64,512]{2,1,0:T(8,128)(2,1)} %bitcast.17), calls=%async_computation | async-start | bytes 1048576 | tf_op jit(solution)/shard_map/all_to_all | solution.py:159
  59.0 9.9 %copy-start.2 = (bf16[8,64,512]{2,1,0:T(8,128)(2,1)}, bf16[8,64,512]{2,1,0:T(8,128)(2,1)S(1)}, u32[]{:S(2)}) copy-start(bf16[8,64,512]{2,1,0:T(8,128)(2,1)S(1)} %all-to-all-done.parts_ref) | copy-start | bytes 1572868
  59.0 22.4 %all-to-all-start.2 = ((bf16[8,64,512]{2,1,0:T(8,128)(2,1)}), bf16[8,64,512]{2,1,0:T(8,128)(2,1)S(1)}, u32[]{:S(2)}, u32[]{:S(2)}) async-start(bf16[8,64,512]{2,1,0:T(8,128)(2,1)} %bitcast.16), calls=%async_computation.2 | async-start | bytes 1048576 | tf_op jit(solution)/shard_map/all_to_all | solution.py:159
  67.1 26.8 %collective-permute-start.4 = (bf16[2,128,2048]{2,1,0:T(8,128)(2,1)}, bf16[2,128,2048]{2,1,0:T(8,128)(2,1)}, u32[]{:S(2)}, u32[]{:S(2)}) collective-permute-start(bf16[2,128,2048]{2,1,0:T(8,128)(2,1)} %slice_bitcast_fusion.4), channel_id=1, source_target_pairs={{8,0},{16,8},{24,16},{0,24},{9,1},{17,9},{25,17},{1,25},{10,2},{18... | collective-permute-start | bytes 3145736 | tf_op jit(solution)/shard_map/ppermute | solution.py:20
  81.4 10.1 %copy-start = (bf16[8,64,512]{2,1,0:T(8,128)(2,1)}, bf16[8,64,512]{2,1,0:T(8,128)(2,1)S(1)}, u32[]{:S(2)}) copy-start(bf16[8,64,512]{2,1,0:T(8,128)(2,1)S(1)} %all-to-all-done.2.parts_ref) | copy-start | bytes 1572868
  81.4 21.9 %all-to-all-start.1 = ((bf16[8,64,512]{2,1,0:T(8,128)(2,1)}), bf16[8,64,512]{2,1,0:T(8,128)(2,1)S(1)}, u32[]{:S(2)}, u32[]{:S(2)}) async-start(bf16[8,64,512]{2,1,0:T(8,128)(2,1)} %bitcast.15), calls=%async_computation.1 | async-start | bytes 1048576 | tf_op jit(solution)/shard_map/all_to_all | solution.py:159
  89.5 19.6 %collective-permute-start = (bf16[2,128,2048]{2,1,0:T(8,128)(2,1)}, bf16[2,128,2048]{2,1,0:T(8,128)(2,1)S(1)}, u32[]{:S(2)}, u32[]{:S(2)}) collective-permute-start(bf16[2,128,2048]{2,1,0:T(8,128)(2,1)} %slice_bitcast_fusion.3), channel_id=1, source_target_pairs={{8,0},{16,8},{24,16},{0,24},{9,1},{17,9},{25,17},{1,25},{10,2},{18... | collective-permute-start | bytes 3145736 | tf_op jit(solution)/shard_map/ppermute | solution.py:20
  103.2 3.4 %copy-start.1 = (bf16[8,64,512]{2,1,0:T(8,128)(2,1)}, bf16[8,64,512]{2,1,0:T(8,128)(2,1)S(1)}, u32[]{:S(2)}) copy-start(bf16[8,64,512]{2,1,0:T(8,128)(2,1)S(1)} %all-to-all-done.1.parts_ref) | copy-start | bytes 1572868
  103.2 12.7 %all-to-all-start.4 = ((bf16[8,64,256]{2,1,0:T(8,128)(2,1)}), bf16[8,64,256]{2,1,0:T(8,128)(2,1)S(1)}, u32[]{:S(2)}, u32[]{:S(2)}) async-start(bf16[8,64,256]{2,1,0:T(8,128)(2,1)} %bitcast.18), calls=%async_computation.4 | async-start | bytes 524288 | tf_op jit(solution)/shard_map/all_to_all | solution.py:159
  109.1 1.0 copy-start.3
  116.0 5.9 %copy-start.4 = (bf16[8,64,256]{2,1,0:T(8,128)(2,1)}, bf16[8,64,256]{2,1,0:T(8,128)(2,1)S(1)}, u32[]{:S(2)}) copy-start(bf16[8,64,256]{2,1,0:T(8,128)(2,1)S(1)} %all-to-all-done.4.parts_ref) | copy-start | bytes 786436
  116.0 14.7 %all-to-all-start.3 = ((bf16[8,64,256]{2,1,0:T(8,128)(2,1)}), bf16[8,64,256]{2,1,0:T(8,128)(2,1)S(1)}, u32[]{:S(2)}, u32[]{:S(2)}) async-start(bf16[8,64,256]{2,1,0:T(8,128)(2,1)} %bitcast.19), calls=%async_computation.3 | async-start | bytes 524288 | tf_op jit(solution)/shard_map/all_to_all | solution.py:159
  130.6 0.7 copy-start.5

commit v3 on v0

v3 whole, which is shorter than its diff:
```python
import functools
import math

import jax
import jax.numpy as jnp
from jax import lax
from jax.experimental import pallas as pl
from jax.experimental.pallas import tpu as pltpu
from jax.sharding import PartitionSpec as P

NKB = 4
PLANE = 1024
DEPTH = 512
AHEAD = 3
VMEM_BYTES = 60 * 1024 * 1024


def shifted(block, axis, distance):
    count = lax.axis_size(axis)
    route = [((i - distance) % count, i) for i in range(count)]
    return lax.ppermute(block, axis, route)


def piece_kernel(slot, start, bands_ref, *rest):
    out_ref, sems = rest[-2:]
    half = out_ref.shape[1] // 2
    copies = []
    for part in range(2):
        for side in range(2):
            rows = pl.ds(start + side * half, half)
            copies.append(
                pltpu.make_async_copy(
                    bands_ref.at[slot, part, rows, :],
                    out_ref.at[part, pl.ds(side * half, half), :],
                    sems.at[part, side],
                )
            )
    for copy in copies:
        copy.start()
    for copy in copies:
        copy.wait()


def piece_of(slot, start, width, bands, after):
    points = bands.shape[3]
    return pl.pallas_call(
        functools.partial(piece_kernel, slot, start),
        in_specs=[pl.BlockSpec(memory_space=pl.ANY)] * (1 + len(after)),
        out_specs=pl.BlockSpec(memory_space=pl.ANY),
        scratch_shapes=[pltpu.SemaphoreType.DMA((2, 2))],
        out_shape=jax.ShapeDtypeStruct((2, width, points), bands.dtype),
        compiler_params=pltpu.CompilerParams(vmem_limit_bytes=VMEM_BYTES),
        cost_estimate=pl.CostEstimate(
            flops=0, bytes_accessed=8 * width * points, transcendentals=0
        ),
        name="piece_of",
    )(bands, *after)


def margin_kernel(slot, k_dev, table_ref, bands_ref, there_ref, *rest):
    out_ref, own_buf, there_buf, sems = rest[-4:]
    pieces = own_buf.shape[0]
    planes = (table_ref.shape[0] // k_dev - 1) // 2
    base = slot * (1 + 2 * planes)
    point = table_ref[base].astype(jnp.int32)

    def copies(piece):
        columns = pl.ds(piece * DEPTH, DEPTH)
        own = pltpu.make_async_copy(
            bands_ref.at[point, :, :, columns], own_buf.at[piece], sems.at[0, piece]
        )
        there = pltpu.make_async_copy(
            there_ref.at[:, :, columns], there_buf.at[piece], sems.at[1, piece]
        )
        return there, own

    for piece in range(pieces):
        for copy in copies(piece):
            copy.start()
    for piece in range(pieces):
        plane = piece * DEPTH // PLANE
        cosine = table_ref[base + 1 + plane]
        sine = table_ref[base + 1 + planes + plane]
        there, own = copies(piece)
        there.wait()
        real_part = there_buf[piece, 0].astype(jnp.float32)
        imag_part = there_buf[piece, 1].astype(jnp.float32)
        near_re = (real_part * cosine + imag_part * sine).astype(jnp.bfloat16)
        near_im = (imag_part * cosine - real_part * sine).astype(jnp.bfloat16)
        with_re = jnp.concatenate([near_re, near_im], axis=0)
        with_im = jnp.concatenate([near_im, -near_re], axis=0)
        right = jnp.concatenate([with_re, with_im], axis=1)
        own.wait()
        left = jnp.concatenate([own_buf[piece, 0], own_buf[piece, 1]], axis=1)
        dims = (((1,), (1,)), ((), ()))
        terms = lax.dot_general(left, right, dims, preferred_element_type=jnp.float32)
        if piece == 0:
            out_ref[...] = terms
        else:
            out_ref[...] += terms


def margin_part(slot, table, bands, there, after):
    k_dev, _, nbands, points = bands.shape
    width = there.shape[1]
    pieces = points // DEPTH
    return pl.pallas_call(
        functools.partial(margin_kernel, slot, k_dev),
        in_specs=[
            pl.BlockSpec(memory_space=pltpu.SMEM),
            pl.BlockSpec(memory_space=pl.ANY),
            pl.BlockSpec(memory_space=pl.ANY),
        ]
        + [pl.BlockSpec(memory_space=pl.ANY)] * len(after),
        out_specs=pl.BlockSpec(memory_space=pltpu.VMEM),
        scratch_shapes=[
            pltpu.VMEM((pieces, 2, nbands, DEPTH), jnp.bfloat16),
            pltpu.VMEM((pieces, 2, width, DEPTH), jnp.bfloat16),
            pltpu.SemaphoreType.DMA((2, pieces)),
        ],
        out_shape=jax.ShapeDtypeStruct((nbands, 2 * width), jnp.float32),
        compiler_params=pltpu.CompilerParams(vmem_limit_bytes=VMEM_BYTES),
        cost_estimate=pl.CostEstimate(
            flops=8 * nbands * width * points,
            bytes_accessed=4 * (nbands + width) * points + 8 * nbands * width,
            transcendentals=0,
        ),
        name="margin_part",
    )(table, bands, there, *after)


def layout_kernel(parts, stride, table_ref, *refs):
    count = len(parts)
    totals, out_ref, bufs, sems = refs[:count], refs[count], refs[count + 1 : -1], refs[-1]
    copies = [
        pltpu.make_async_copy(totals[i], bufs[i], sems.at[i]) for i in range(count)
    ]
    for copy in copies:
        copy.start()
    for copy, (slot, start, width), buf in zip(copies, parts, bufs):
        copy.wait()
        point = table_ref[slot * stride].astype(jnp.int32)
        out_ref[:, point, 0, start : start + width] = buf[:, :width]
        out_ref[:, point, 1, start : start + width] = buf[:, width:]


def laid_out(parts, table, totals, shape):
    return pl.pallas_call(
        functools.partial(layout_kernel, parts, table.shape[0] // shape[1]),
        in_specs=[pl.BlockSpec(memory_space=pltpu.SMEM)]
        + [pl.BlockSpec(memory_space=pl.ANY)] * len(totals),
        out_specs=pl.BlockSpec(memory_space=pltpu.VMEM),
        scratch_shapes=[pltpu.VMEM(total.shape, total.dtype) for total in totals]
        + [pltpu.SemaphoreType.DMA((len(totals),))],
        out_shape=jax.ShapeDtypeStruct(shape, jnp.float32),
        compiler_params=pltpu.CompilerParams(vmem_limit_bytes=VMEM_BYTES),
        cost_estimate=pl.CostEstimate(
            flops=0, bytes_accessed=8 * math.prod(shape), transcendentals=0
        ),
        name="laid_out",
    )(table, *totals)


def cuts(nbands, first, last):
    half, quarter, eighth = nbands // 2, nbands // 4, nbands // 8
    widths = [half, quarter, quarter]
    if first:
        widths = [quarter, quarter, half]
    if last:
        widths = [half, quarter, eighth, eighth]
    starts = [sum(widths[:i]) for i in range(len(widths))]
    return list(zip(starts, widths))


def body(bands, nbr_slot, gshift):
    grid_index = lax.axis_index("ga")
    grid_count = lax.axis_size("ga")
    k_dev, _, nbands, points = bands.shape
    rows = nbands // grid_count
    own_planes = points // PLANE
    total_planes = own_planes * grid_count
    planes = grid_index * own_planes + jnp.arange(own_planes, dtype=jnp.int32)
    slots = jnp.arange(k_dev, dtype=jnp.int32)
    chosen = nbr_slot[None, :] == slots[:, None]
    order = jnp.sum(jnp.where(chosen, slots[None, :], 0), axis=1)
    shifts = jnp.sum(jnp.where(chosen, gshift[None, :], 0), axis=1)
    turns = (1 + NKB * shifts[:, None]) * planes[None, :] % (NKB * total_planes)
    angle = 2.0 * math.pi / (NKB * total_planes) * turns.astype(jnp.float32)
    columns = [order[:, None].astype(jnp.float32), jnp.cos(angle), jnp.sin(angle)]
    table = jnp.concatenate(columns, axis=1).reshape(-1)
    parts = []
    for slot in range(k_dev):
        for start, width in cuts(nbands, slot == 0, slot == k_dev - 1):
            parts.append((slot, start, width))
    theres = []
    piece = None
    for index, (slot, start, width) in enumerate(parts):
        after = [] if piece is None else [piece]
        if index >= AHEAD:
            after.append(theres[index - AHEAD])
        piece = piece_of(slot, start, width, bands, after)
        theres.append(shifted(piece, "ka", -1))
    totals = []
    part = None
    for (slot, start, width), there in zip(parts, theres):
        part = margin_part(slot, table, bands, there, [] if part is None else [part])
        totals.append(lax.psum_scatter(part, "ga", scatter_dimension=0, tiled=True))
    return laid_out(parts, table, totals, (rows, k_dev, 2, nbands))


def solution(mesh):
    placed = (P("ka", None, None, "ga"), P("ka"), P("ka"))
    return jax.shard_map(
        body, mesh=mesh, in_specs=placed, out_specs=P("ga", "ka", None, None), check_vma=False
    )
```

time: 310 us -> 675 us (2.18)
  Pallas kernels: 0 us -> 307 us
  waiting for transfers between devices: 247 us -> 342 us
  other arithmetic: 15.1 us -> 0.35 us
  local copies, waits for them, and re-layouts: 19.3 us -> 5.86 us
  matrix products: 12.6 us -> 0 us
    reduce_scatter x0 -> x7, waiting for transfers between devices: none -> 340 us  [body(): totals.append(lax.psum_scatter(part, 'ga', scatter_dimension=0, tiled=True))]
    pallas_call x0 -> x15, Pallas kernels: none -> 307 us  [the longest x7 262 us: piece_of(): pl.pallas_call(functools.partial(piece_kernel, slot, start), in_specs=[pl...]
    psum x1 -> x0, waiting for transfers between devices: 158 us -> none  [body(): summed = lax.psum(jnp.stack([real_part, imag_part], axis=2), 'ga')]
    ppermute x1 -> x7, waiting for transfers between devices: 88.9 us -> 0.02 us  [shifted(): return lax.ppermute(block, axis, route)]
    gather x5 -> x0, local copies, waits for them, and re-layouts: 16.6 us -> none  [body(): partner = jnp.take(there, nbr_slot, axis=0)]
    dot_general x1 -> x0, matrix products: 12.6 us -> none  [body(): jnp.einsum('pcmx,pdnx->mpcdn', bands, near, preferred_element_type=jnp.fl...]
    another operation x2 -> x0, other arithmetic: 7.46 us -> none
  transfers between devices with their start and end apart: 2 -> 14, of which waited for: 2 -> 6; matrix products, arithmetic and copies ran while one was open for 1% -> 0% of each run, Pallas kernels for 0% -> 40%
where the time goes in v3:
time: 675 us
  waiting for transfers between devices  342 us (51%)
  Pallas kernels  307 us (45%)
  between operations  13.8 us (2%)
    reduce_scatter x7, waiting for transfers between devices, body(): totals.append(lax.psum_scatter(part, 'ga', scatter_dimension=0, tiled=True))  340 us
    pallas_call x7, Pallas kernels, piece_of(): pl.pallas_call(functools.partial(piece_kernel, slot, start), in_specs=[pl...  262 us
    pallas_call x7, Pallas kernels, margin_part(): pl.pallas_call(functools.partial(margin_kernel, slot, k_dev), in_specs=[p...  41.8 us
  transfers between devices with their start and end apart: 14, of which 6 were waited for; matrix products, arithmetic and copies ran while one was open for 0% of the time, Pallas kernels for 40%

profile of v3, /device:TPU:0, one launch (start us, length us, event | category | flops | bytes accessed | tf_op | source)
XLA Modules:
  0.0 675.0 jit_solution(8675270625774829112)
XLA Ops:
  6.5 32.9 %piece_of.7.rest_0_ = bf16[2,128,2048]{2,1,0:T(8,128)(2,1)} custom-call(bf16[2,2,512,2048]{3,2,1,0:T(8,128)(2,1)} %bands_ref.27), custom_call_target="tpu_custom_call" | custom-call | bytes 2097152 | tf_op jit(solution)/shard_map/piece_of/pallas_call | solution.py:46
  39.4 2.5 collective-permute-start
  41.9 32.9 %piece_of.8.rest_0_ = bf16[2,128,2048]{2,1,0:T(8,128)(2,1)} custom-call(bf16[2,2,512,2048]{3,2,1,0:T(8,128)(2,1)} %bands_ref.27, bf16[2,128,2048]{2,1,0:T(8,128)(2,1)} %piece_of.7.rest_0_), custom_call_target="tpu_custom_call" | custom-call | bytes 2097152 | tf_op jit(solution)/shard_map/piece_of/pallas_call | solution.py:46
  74.8 0.7 collective-permute-start.1
  75.6 64.7 %piece_of.9.rest_0_ = bf16[2,256,2048]{2,1,0:T(8,128)(2,1)} custom-call(bf16[2,2,512,2048]{3,2,1,0:T(8,128)(2,1)} %bands_ref.27, bf16[2,128,2048]{2,1,0:T(8,128)(2,1)} %piece_of.8.rest_0_), custom_call_target="tpu_custom_call" | custom-call | bytes 4194304 | tf_op jit(solution)/shard_map/piece_of/pallas_call | solution.py:46
  140.2 0.1 collective-permute-start.2
  140.3 0.1 select_reduce_fusion.1
  140.5 0.1 copy.4
  140.6 1.0 copy-done.2
  141.6 64.7 %piece_of.10.rest_0_ = bf16[2,256,2048]{2,1,0:T(8,128)(2,1)} custom-call(bf16[2,2,512,2048]{3,2,1,0:T(8,128)(2,1)} %bands_ref.27, bf16[2,256,2048]{2,1,0:T(8,128)(2,1)} %piece_of.9.rest_0_, bf16[2,128,2048]{2,1,0:T(8,128)(2,1)} %copy-done.2), custom_call_target="tpu_custom_call" | custom-call | bytes 4194304 | tf_op jit(solution)/shard_map/piece_of/pallas_call | solution.py:46
  206.3 0.1 collective-permute-start.3
  206.3 0.1 fusion.4
  206.5 0.1 pad_maximum_fusion
  206.5 0.6 reshape.24.table_ref
  207.1 5.9 margin_part.7.rest_0_
  213.1 0.0 reduce-scatter.10.cloned.1.call-start
  213.1 1.0 copy-done.1
  214.2 32.9 %piece_of.11.rest_0_ = bf16[2,128,2048]{2,1,0:T(8,128)(2,1)} custom-call(bf16[2,2,512,2048]{3,2,1,0:T(8,128)(2,1)} %bands_ref.27, bf16[2,256,2048]{2,1,0:T(8,128)(2,1)} %piece_of.10.rest_0_, bf16[2,128,2048]{2,1,0:T(8,128)(2,1)} %copy-done.1), custom_call_target="tpu_custom_call" | custom-call | bytes 2097152 | tf_op jit(solution)/shard_map/piece_of/pallas_call | solution.py:46
  247.1 1.6 collective-permute-start.4
  248.6 5.9 margin_part.8.rest_0_
  254.6 0.0 reduce-scatter.18.cloned.1.call-start
  254.7 17.0 %piece_of.12.rest_0_ = bf16[2,64,2048]{2,1,0:T(8,128)(2,1)} custom-call(bf16[2,2,512,2048]{3,2,1,0:T(8,128)(2,1)} %bands_ref.27, bf16[2,128,2048]{2,1,0:T(8,128)(2,1)} %piece_of.11.rest_0_, bf16[2,256,2048]{2,1,0:T(8,128)(2,1)} %collective-permute-done.2.there_ref.rest_1_), custom_call_target="tpu_custom_call" | custom-call | bytes 1048576 | tf_op jit(solution)/shard_map/piece_of/pallas_call | solution.py:46
  271.7 0.7 collective-permute-start.5
  272.4 6.6 margin_part.9.rest_0_
  279.1 1.3 copy-done
  280.4 17.0 %piece_of.13 = bf16[2,64,2048]{2,1,0:T(8,128)(2,1)} custom-call(bf16[2,2,512,2048]{3,2,1,0:T(8,128)(2,1)} %bands_ref.27, bf16[2,64,2048]{2,1,0:T(8,128)(2,1)} %piece_of.12.rest_0_, bf16[2,256,2048]{2,1,0:T(8,128)(2,1)} %copy-done), custom_call_target="tpu_custom_call" | custom-call | bytes 1048576 | tf_op jit(solution)/shard_map/piece_of/pallas_call | solution.py:46
  297.4 0.1 collective-permute-start.6
  297.5 6.6 margin_part.10.rest_0_
  304.2 1.0 copy-done.3
  305.1 5.9 margin_part.11.rest_0_
  311.1 5.4 margin_part.12.rest_0_
  316.5 0.0 reduce-scatter.20.cloned.1.call-start
  316.6 0.8 copy-done.4
  317.4 5.4 margin_part.13
  322.8 0.0 reduce-scatter.12.cloned.1.call-start
  322.9 0.5 reduce-scatter.12.cloned.1.call-update
  323.4 0.0 reduce-scatter.16.cloned.1.call-start
  323.5 0.5 reduce-scatter.16.cloned.1.call-update
  324.0 0.0 reduce-scatter.14.cloned.1.call-start
  324.1 0.7 reduce-scatter.14.cloned.1.call-update
  324.8 0.0 reduce-scatter.8.cloned.1.call-done.refs_0_
  324.8 17.3 %reduce-scatter.10.cloned.1.call-done.refs_1_ = f32[64,256]{1,0:T(8,128)} async-done(((f32[512,256]{1,0:T(8,128)}), f32[64,256]{1,0:T(8,128)}) %reduce-scatter.10.cloned.1.call-update) | async-done | bytes 65552 | tf_op jit(solution)/shard_map/reduce_scatter | solution.py:207
  342.1 63.6 %reduce-scatter.18.cloned.1.call-done.refs_5_ = f32[64,128]{1,0:T(8,128)} async-done(((f32[512,128]{1,0:T(8,128)}), f32[64,128]{1,0:T(8,128)}) %reduce-scatter.18.cloned.1.call-update) | async-done | bytes 32784 | tf_op jit(solution)/shard_map/reduce_scatter | solution.py:207
  405.6 63.5 %reduce-scatter.20.cloned.1.call-done.refs_6_ = f32[64,128]{1,0:T(8,128)} async-done(((f32[512,128]{1,0:T(8,128)}), f32[64,128]{1,0:T(8,128)}) %reduce-scatter.20.cloned.1.call-update) | async-done | bytes 32784 | tf_op jit(solution)/shard_map/reduce_scatter | solution.py:207
  469.1 65.7 %reduce-scatter.12.cloned.1.call-done.refs_2_ = f32[64,512]{1,0:T(8,128)} async-done(((f32[512,512]{1,0:T(8,128)}), f32[64,512]{1,0:T(8,128)}) %reduce-scatter.12.cloned.1.call-update) | async-done | bytes 131088 | tf_op jit(solution)/shard_map/reduce_scatter | solution.py:207
  534.8 64.5 %reduce-scatter.16.cloned.1.call-done.refs_4_ = f32[64,256]{1,0:T(8,128)} async-done(((f32[512,256]{1,0:T(8,128)}), f32[64,256]{1,0:T(8,128)}) %reduce-scatter.16.cloned.1.call-update) | async-done | bytes 65552 | tf_op jit(solution)/shard_map/reduce_scatter | solution.py:207
  599.3 66.0 %reduce-scatter.14.cloned.1.call-done.refs_3_ = f32[64,512]{1,0:T(8,128)} async-done(((f32[512,512]{1,0:T(8,128)}), f32[64,512]{1,0:T(8,128)}) %reduce-scatter.14.cloned.1.call-update) | async-done | bytes 131088 | tf_op jit(solution)/shard_map/reduce_scatter | solution.py:207
  665.2 2.9 laid_out.1
  (23 shorter events, 0.1 us)
Async XLA Ops:
  6.5 318.2 %reduce-scatter.8.cloned.1.call-start = ((), (), s32[]{:S(2)}) async-start(), calls=%async_computation.7 | async-start | bytes 589824 | tf_op jit(solution)/shard_map/reduce_scatter | solution.py:207
  39.4 101.1 %collective-permute-start = (bf16[2,128,2048]{2,1,0:T(8,128)(2,1)}, bf16[2,128,2048]{2,1,0:T(8,128)(2,1)S(1)}, u32[]{:S(2)}, u32[]{:S(2)}) collective-permute-start(bf16[2,128,2048]{2,1,0:T(8,128)(2,1)} %piece_of.7.rest_0_), channel_id=1, source_target_pairs={{8,0},{16,8},{24,16},{0,24},{9,1},{17,9},{25,17},{1,25},{10,2},{18... | collective-permute-start | bytes 3145736 | tf_op jit(solution)/shard_map/ppermute | solution.py:21
  74.8 65.5 %copy-start.5 = (s32[2]{0:T(128)S(1)}, s32[2]{0:T(128)}, u32[]{:S(2)}) copy-start(s32[2]{0:T(128)} %param.4) | copy-start | bytes 28
  74.8 65.5 %copy-start.6 = (s32[2]{0:T(128)S(1)}, s32[2]{0:T(128)}, u32[]{:S(2)}) copy-start(s32[2]{0:T(128)} %param.5) | copy-start | bytes 28
  74.8 138.3 %collective-permute-start.1 = (bf16[2,128,2048]{2,1,0:T(8,128)(2,1)}, bf16[2,128,2048]{2,1,0:T(8,128)(2,1)S(1)}, u32[]{:S(2)}, u32[]{:S(2)}) collective-permute-start(bf16[2,128,2048]{2,1,0:T(8,128)(2,1)} %piece_of.8.rest_0_), channel_id=1, source_target_pairs={{8,0},{16,8},{24,16},{0,24},{9,1},{17,9},{25,17},{1,25},{10,2},{18... | collective-permute-start | bytes 3145736 | tf_op jit(solution)/shard_map/ppermute | solution.py:21
  140.2 114.4 %collective-permute-start.2 = (bf16[2,256,2048]{2,1,0:T(8,128)(2,1)}, bf16[2,256,2048]{2,1,0:T(8,128)(2,1)}, u32[]{:S(2)}, u32[]{:S(2)}) collective-permute-start(bf16[2,256,2048]{2,1,0:T(8,128)(2,1)} %piece_of.9.rest_0_), channel_id=1, source_target_pairs={{8,0},{16,8},{24,16},{0,24},{9,1},{17,9},{25,17},{1,25},{10,2},{18... | collective-permute-start | bytes 6291464 | tf_op jit(solution)/shard_map/ppermute | solution.py:21
  140.6 1.0 copy-start.2
  206.3 72.8 %collective-permute-start.3 = (bf16[2,256,2048]{2,1,0:T(8,128)(2,1)}, bf16[2,256,2048]{2,1,0:T(8,128)(2,1)S(1)}, u32[]{:S(2)}, u32[]{:S(2)}) collective-permute-start(bf16[2,256,2048]{2,1,0:T(8,128)(2,1)} %piece_of.10.rest_0_), channel_id=1, source_target_pairs={{8,0},{16,8},{24,16},{0,24},{9,1},{17,9},{25,17},{1,25},{10,2},{18... | collective-permute-start | bytes 6291464 | tf_op jit(solution)/shard_map/ppermute | solution.py:21
  213.1 129.0 %reduce-scatter.10.cloned.1.call-start = ((), (), s32[]{:S(2)}) async-start(), calls=%async_computation.8 | async-start | bytes 589824 | tf_op jit(solution)/shard_map/reduce_scatter | solution.py:207
  213.1 1.0 copy-start.1
  247.1 57.1 %collective-permute-start.4 = (bf16[2,128,2048]{2,1,0:T(8,128)(2,1)}, bf16[2,128,2048]{2,1,0:T(8,128)(2,1)S(1)}, u32[]{:S(2)}, u32[]{:S(2)}) collective-permute-start(bf16[2,128,2048]{2,1,0:T(8,128)(2,1)} %piece_of.11.rest_0_), channel_id=1, source_target_pairs={{8,0},{16,8},{24,16},{0,24},{9,1},{17,9},{25,17},{1,25},{10,2},{18... | collective-permute-start | bytes 3145736 | tf_op jit(solution)/shard_map/ppermute | solution.py:21
  254.6 151.0 %reduce-scatter.18.cloned.1.call-start = ((), (), s32[]{:S(2)}) async-start(), calls=%async_computation.12 | async-start | bytes 294912 | tf_op jit(solution)/shard_map/reduce_scatter | solution.py:207
  271.7 39.4 %collective-permute-start.5 = (bf16[2,64,2048]{2,1,0:T(8,128)(2,1)}, bf16[2,64,2048]{2,1,0:T(8,128)(2,1)}, u32[]{:S(2)}, u32[]{:S(2)}) collective-permute-start(bf16[2,64,2048]{2,1,0:T(8,128)(2,1)} %piece_of.12.rest_0_), channel_id=1, source_target_pairs={{8,0},{16,8},{24,16},{0,24},{9,1},{17,9},{25,17},{1,25},{10,2},{18... | collective-permute-start | bytes 1572872 | tf_op jit(solution)/shard_map/ppermute | solution.py:21
  279.1 1.3 copy-start
  297.4 19.2 %collective-permute-start.6 = (bf16[2,64,2048]{2,1,0:T(8,128)(2,1)}, bf16[2,64,2048]{2,1,0:T(8,128)(2,1)S(1)}, u32[]{:S(2)}, u32[]{:S(2)}) collective-permute-start(bf16[2,64,2048]{2,1,0:T(8,128)(2,1)} %piece_of.13), channel_id=1, source_target_pairs={{8,0},{16,8},{24,16},{0,24},{9,1},{17,9},{25,17},{1,25},{10,2},{18... | collective-permute-start | bytes 1572872 | tf_op jit(solution)/shard_map/ppermute | solution.py:21
  304.1 1.0 copy-start.3
  316.5 152.6 %reduce-scatter.20.cloned.1.call-start = ((), (), s32[]{:S(2)}) async-start(), calls=%async_computation.13 | async-start | bytes 294912 | tf_op jit(solution)/shard_map/reduce_scatter | solution.py:207
  316.6 0.8 copy-start.4
  322.8 212.0 %reduce-scatter.12.cloned.1.call-start = ((), (), s32[]{:S(2)}) async-start(), calls=%async_computation.9 | async-start | bytes 1179648 | tf_op jit(solution)/shard_map/reduce_scatter | solution.py:207
  323.4 275.8 %reduce-scatter.16.cloned.1.call-start = ((), (), s32[]{:S(2)}) async-start(), calls=%async_computation.11 | async-start | bytes 589824 | tf_op jit(solution)/shard_map/reduce_scatter | solution.py:207
  324.0 341.2 %reduce-scatter.14.cloned.1.call-start = ((), (), s32[]{:S(2)}) async-start(), calls=%async_computation.10 | async-start | bytes 1179648 | tf_op jit(solution)/shard_map/reduce_scatter | solution.py:207
Sparse Core Ops, SparseCore 0:
  213.2 64.0 reduce-scatter.7
  281.0 60.9 reduce-scatter.9
  345.4 60.2 reduce-scatter.17
  408.8 60.2 reduce-scatter.19
  472.4 62.3 reduce-scatter.11
  538.4 60.8 reduce-scatter.15
  602.7 62.5 reduce-scatter.13

commit v4 on v0

v4 whole, which is shorter than its diff:
```python
import functools
import math

import jax
import jax.numpy as jnp
from jax import lax
from jax.experimental import pallas as pl
from jax.experimental.pallas import tpu as pltpu
from jax.sharding import PartitionSpec as P

NKB = 4
PLANE = 1024
ROWS = 256
STRIP = 32
DEPTH = 512
LAG = 2
AHEAD = 3
VMEM_BYTES = 58 * 1024 * 1024


def shifted(block, axis, distance):
    count = lax.axis_size(axis)
    route = [((i - distance) % count, i) for i in range(count)]
    return lax.ppermute(block, axis, route)


def piece_kernel(slot, start, bands_ref, *rest):
    out_ref, piece_buf, sems = rest[-3:]
    width = piece_buf.shape[1]
    rows = pl.ds(start, width)
    loads = [
        pltpu.make_async_copy(bands_ref.at[slot, part, rows, :], piece_buf.at[part], sems.at[0, part])
        for part in range(2)
    ]
    stores = [
        pltpu.make_async_copy(piece_buf.at[part], out_ref.at[part], sems.at[1, part])
        for part in range(2)
    ]
    for load in loads:
        load.start()
    for load, store in zip(loads, stores):
        load.wait()
        store.start()
    for store in stores:
        store.wait()


def piece_of(slot, start, width, bands, after):
    points = bands.shape[3]
    return pl.pallas_call(
        functools.partial(piece_kernel, slot, start),
        in_specs=[pl.BlockSpec(memory_space=pl.ANY)] * (1 + len(after)),
        out_specs=pl.BlockSpec(memory_space=pl.ANY),
        scratch_shapes=[
            pltpu.VMEM((2, width, points), bands.dtype),
            pltpu.SemaphoreType.DMA((2, 2)),
        ],
        out_shape=jax.ShapeDtypeStruct((2, width, points), bands.dtype),
        compiler_params=pltpu.CompilerParams(vmem_limit_bytes=VMEM_BYTES),
        cost_estimate=pl.CostEstimate(
            flops=0, bytes_accessed=8 * width * points, transcendentals=0
        ),
        name="piece_of",
    )(bands, *after)


def near_into(near_buf, there_buf, table_ref, base, planes):
    width, points = there_buf.shape[1:]

    @pl.loop(0, width // STRIP)
    def _(strip):
        rows = pl.ds(strip * STRIP, STRIP)
        mirror = pl.ds(width + strip * STRIP, STRIP)
        for start in range(0, points, DEPTH):
            plane = start // PLANE
            cosine = table_ref[base + 1 + plane]
            sine = table_ref[base + 1 + planes + plane]
            columns = pl.ds(start, DEPTH)
            later = pl.ds(points + start, DEPTH)
            real_part = there_buf[0, rows, columns].astype(jnp.float32)
            imag_part = there_buf[1, rows, columns].astype(jnp.float32)
            near_re = (real_part * cosine + imag_part * sine).astype(jnp.bfloat16)
            near_im = (imag_part * cosine - real_part * sine).astype(jnp.bfloat16)
            near_buf[rows, columns] = near_re
            near_buf[rows, later] = near_im
            near_buf[mirror, columns] = near_im
            near_buf[mirror, later] = -near_re


def add_into(sum_buf, arrived_buf):
    width = arrived_buf.shape[2] // 2
    total = arrived_buf[0].astype(jnp.float32)
    for source in range(1, arrived_buf.shape[0]):
        total = total + arrived_buf[source].astype(jnp.float32)
    sum_buf[:, 0, :] = total[:, :width]
    sum_buf[:, 1, :] = total[:, width:]


def step_kernel(slot, k_dev, adding, first, later, table_ref, bands_ref, there_ref, *rest):
    stride = table_ref.shape[0] // k_dev
    planes = (stride - 1) // 2
    base = slot * stride
    point = table_ref[base].astype(jnp.int32)
    rest = list(rest)
    arrived_ref = rest.pop(0) if adding else None
    if adding and not first:
        rest.pop(0)
    out_ref = rest.pop(0)
    result_ref = rest.pop(0) if adding else None
    piece_ref = rest.pop(0) if later else None
    own_buf, there_buf, near_buf, sems = rest[:4]
    if later:
        piece_buf, piece_sems = rest[4:6]
        del rest[4:6]
        later_slot, later_start, later_width = later
        loads = [
            pltpu.make_async_copy(
                bands_ref.at[later_slot, part, pl.ds(later_start, later_width), :],
                piece_buf.at[part],
                piece_sems.at[0, part],
            )
            for part in range(2)
        ]
        stores = [
            pltpu.make_async_copy(piece_buf.at[part], piece_ref.at[part], piece_sems.at[1, part])
            for part in range(2)
        ]
    points = there_buf.shape[2]
    blocks = own_buf.shape[0]
    if adding:
        arrived_buf, sum_buf, add_sems = rest[4:]
        arrival = pltpu.make_async_copy(arrived_ref, arrived_buf, add_sems.at[0])
        arrival.start()
    there = [
        pltpu.make_async_copy(there_ref.at[part], there_buf.at[part], sems.at[0, part])
        for part in range(2)
    ]
    own = [
        pltpu.make_async_copy(
            bands_ref.at[point, part, pl.ds(block * ROWS, ROWS), :],
            own_buf.at[block, :, pl.ds(part * points, points)],
            sems.at[1 + block, part],
        )
        for block in range(blocks)
        for part in range(2)
    ]
    for copy in there + (loads if later else []) + own:
        copy.start()
    if adding:
        add_slot, start, width = adding
        add_point = table_ref[add_slot * stride].astype(jnp.int32)
        arrival.wait()
        add_into(sum_buf, arrived_buf)
        placing = pltpu.make_async_copy(
            sum_buf, result_ref.at[:, add_point, :, pl.ds(start, width)], add_sems.at[1]
        )
        placing.start()
    for copy in there:
        copy.wait()
    near_into(near_buf, there_buf, table_ref, base, planes)
    if later:
        for load, store in zip(loads, stores):
            load.wait()
            store.start()
    for block in range(blocks):
        own[2 * block].wait()
        own[2 * block + 1].wait()
        out_ref[pl.ds(block * ROWS, ROWS), :] = lax.dot_general(
            own_buf[block],
            near_buf[...],
            (((1,), (1,)), ((), ())),
            preferred_element_type=jnp.float32,
        ).astype(out_ref.dtype)
    if adding:
        placing.wait()
    if later:
        for store in stores:
            store.wait()


def step(slot, table, bands, there, adding, arrived, result, shape, later):
    k_dev, _, nbands, points = bands.shape
    width = there.shape[1]
    blocks = nbands // ROWS
    operands = [table, bands, there]
    out_shape = [jax.ShapeDtypeStruct((nbands, 2 * width), jnp.bfloat16)]
    out_specs = [pl.BlockSpec(memory_space=pltpu.VMEM)]
    scratch = [
        pltpu.VMEM((blocks, ROWS, 2 * points), jnp.bfloat16),
        pltpu.VMEM((2, width, points), jnp.bfloat16),
        pltpu.VMEM((2 * width, 2 * points), jnp.bfloat16),
        pltpu.SemaphoreType.DMA((1 + blocks, 2)),
    ]
    aliases = {}
    if later:
        scratch += [
            pltpu.VMEM((2, later[2], points), bands.dtype),
            pltpu.SemaphoreType.DMA((2, 2)),
        ]
    if adding:
        operands.append(arrived)
        if result is not None:
            aliases = {len(operands): 1}
            operands.append(result)
        out_shape.append(jax.ShapeDtypeStruct(shape, jnp.float32))
        out_specs.append(pl.BlockSpec(memory_space=pl.ANY))
        scratch += [
            pltpu.VMEM(arrived.shape, arrived.dtype),
            pltpu.VMEM((shape[0], 2, adding[2]), jnp.float32),
            pltpu.SemaphoreType.DMA((2,)),
        ]
    if later:
        out_shape.append(jax.ShapeDtypeStruct((2, later[2], points), bands.dtype))
        out_specs.append(pl.BlockSpec(memory_space=pl.ANY))
    outs = pl.pallas_call(
        functools.partial(step_kernel, slot, k_dev, adding, result is None, later),
        in_specs=[pl.BlockSpec(memory_space=pltpu.SMEM)]
        + [pl.BlockSpec(memory_space=pl.ANY)] * (len(operands) - 1),
        out_specs=out_specs,
        scratch_shapes=scratch,
        out_shape=out_shape,
        input_output_aliases=aliases,
        compiler_params=pltpu.CompilerParams(vmem_limit_bytes=VMEM_BYTES),
        cost_estimate=pl.CostEstimate(
            flops=8 * nbands * width * points,
            bytes_accessed=4 * (nbands + width) * points + 8 * nbands * width,
            transcendentals=0,
        ),
        name="step",
    )(*operands)
    return outs[0], outs[1] if adding else result, outs[-1] if later else None


def finish_kernel(parts, stride, table_ref, *refs):
    count = len(parts)
    arrived, result_ref = refs[:count], refs[count + 1]
    bufs, sums, sems = refs[count + 2 : -1 - count], refs[-1 - count : -1], refs[-1]
    copies = [pltpu.make_async_copy(arrived[i], bufs[i], sems.at[0, i]) for i in range(count)]
    for copy in copies:
        copy.start()
    placing = []
    for i, (slot, start, width) in enumerate(parts):
        point = table_ref[slot * stride].astype(jnp.int32)
        copies[i].wait()
        add_into(sums[i], bufs[i])
        columns = pl.ds(start, width)
        placing.append(
            pltpu.make_async_copy(sums[i], result_ref.at[:, point, :, columns], sems.at[1, i])
        )
        placing[-1].start()
    for copy in placing:
        copy.wait()


def finish(parts, table, arrived, result):
    rows, k_dev = result.shape[:2]
    return pl.pallas_call(
        functools.partial(finish_kernel, parts, table.shape[0] // k_dev),
        in_specs=[pl.BlockSpec(memory_space=pltpu.SMEM)]
        + [pl.BlockSpec(memory_space=pl.ANY)] * (len(parts) + 1),
        out_specs=pl.BlockSpec(memory_space=pl.ANY),
        scratch_shapes=[pltpu.VMEM(array.shape, array.dtype) for array in arrived]
        + [pltpu.VMEM((rows, 2, width), jnp.float32) for _, _, width in parts]
        + [pltpu.SemaphoreType.DMA((2, len(parts)))],
        out_shape=jax.ShapeDtypeStruct(result.shape, jnp.float32),
        input_output_aliases={1 + len(parts): 0},
        compiler_params=pltpu.CompilerParams(vmem_limit_bytes=VMEM_BYTES),
        cost_estimate=pl.CostEstimate(
            flops=0, bytes_accessed=4 * math.prod(result.shape), transcendentals=0
        ),
        name="finish",
    )(table, *arrived, result)


def cuts(nbands, first):
    half, quarter = nbands // 2, nbands // 4
    widths = [quarter, half + quarter] if first else [half, quarter, quarter]
    starts = [sum(widths[:i]) for i in range(len(widths))]
    return list(zip(starts, widths))


def body(bands, nbr_slot, gshift):
    grid_index = lax.axis_index("ga")
    grid_count = lax.axis_size("ga")
    k_dev, _, nbands, points = bands.shape
    rows = nbands // grid_count
    own_planes = points // PLANE
    total_planes = own_planes * grid_count
    planes = grid_index * own_planes + jnp.arange(own_planes, dtype=jnp.int32)
    slots = jnp.arange(k_dev, dtype=jnp.int32)
    chosen = nbr_slot[None, :] == slots[:, None]
    order = jnp.sum(jnp.where(chosen, slots[None, :], 0), axis=1)
    shifts = jnp.sum(jnp.where(chosen, gshift[None, :], 0), axis=1)
    turns = (1 + NKB * shifts[:, None]) * planes[None, :] % (NKB * total_planes)
    angle = 2.0 * math.pi / (NKB * total_planes) * turns.astype(jnp.float32)
    columns = [order[:, None].astype(jnp.float32), jnp.cos(angle), jnp.sin(angle)]
    table = jnp.concatenate(columns, axis=1).reshape(-1)
    parts = []
    for slot in range(k_dev):
        for start, width in cuts(nbands, slot == 0):
            parts.append((slot, start, width))
    theres = []
    piece = None
    for slot, start, width in parts[:AHEAD]:
        piece = piece_of(slot, start, width, bands, [] if piece is None else [piece])
        theres.append(shifted(piece, "ka", -1))
    arrived = []
    result = None
    shape = (rows, k_dev, 2, nbands)
    for index, part in enumerate(parts):
        adding = parts[index - LAG] if index >= LAG else None
        ready = arrived[index - LAG] if index >= LAG else None
        later = parts[index + AHEAD] if index + AHEAD < len(parts) else None
        terms, result, piece = step(
            part[0], table, bands, theres[index], adding, ready, result, shape, later
        )
        if later:
            theres.append(shifted(piece, "ka", -1))
        terms = terms.reshape(grid_count, rows, 2 * part[2])
        arrived.append(lax.all_to_all(terms, "ga", 0, 0))
    return finish(parts[-LAG:], table, arrived[-LAG:], result)


def solution(mesh):
    placed = (P("ka", None, None, "ga"), P("ka"), P("ka"))
    return jax.shard_map(
        body, mesh=mesh, in_specs=placed, out_specs=P("ga", "ka", None, None), check_vma=False
    )
```

time: 310 us -> 150 us (0.48)
  waiting for transfers between devices: 247 us -> 60.5 us
  Pallas kernels: 0 us -> 47.4 us
  starting transfers between devices: 2.41 us -> 24.5 us
  local copies, waits for them, and re-layouts: 19.3 us -> 3.06 us
  other arithmetic: 15.1 us -> 0.35 us
  blocking collectives: 0 us -> 13.3 us
  between operations: 13.4 us -> 0.14 us
  matrix products: 12.6 us -> 0 us
    psum x1 -> x0, waiting for transfers between devices: 158 us -> none  [body(): summed = lax.psum(jnp.stack([real_part, imag_part], axis=2), 'ga')]
    pallas_call x0 -> x9, Pallas kernels: none -> 47.4 us  [the longest x5 37 us: step(): pl.pallas_call(functools.partial(step_kernel, slot, k_dev, adding, result...]
    ppermute x1 -> x5, waiting for transfers between devices: 88.9 us -> 41.7 us  [shifted(): return lax.ppermute(block, axis, route)]
    all_to_all x0 -> x4, waiting for transfers between devices: none -> 18.8 us  [body(): arrived.append(lax.all_to_all(terms, 'ga', 0, 0))]
    all_to_all x0 -> x4, starting transfers between devices: none -> 18.6 us  [body(): arrived.append(lax.all_to_all(terms, 'ga', 0, 0))]
    gather x5 -> x0, local copies, waits for them, and re-layouts: 16.6 us -> none  [body(): partner = jnp.take(there, nbr_slot, axis=0)]
    all_to_all x0 -> x1, blocking collectives: none -> 13.3 us  [body(): arrived.append(lax.all_to_all(terms, 'ga', 0, 0))]
    dot_general x1 -> x0, matrix products: 12.6 us -> none  [body(): jnp.einsum('pcmx,pdnx->mpcdn', bands, near, preferred_element_type=jnp.fl...]
  transfers between devices with their start and end apart: 2 -> 9, of which waited for: 2 -> 5; matrix products, arithmetic and copies ran while one was open for 1% -> 1% of each run, Pallas kernels for 0% -> 27%
where the time goes in v4:
time: 150 us; the launch traced here: 149 us
  waiting for transfers between devices  60.5 us (40%)
  Pallas kernels  47.4 us (32%)
  starting transfers between devices  24.5 us (16%)
  blocking collectives  13.3 us (9%)
  local copies, waits for them, and re-layouts  3.06 us (2%)
    ppermute x5, waiting for transfers between devices, shifted(): return lax.ppermute(block, axis, route)  41.7 us
    pallas_call x5, Pallas kernels, step(): pl.pallas_call(functools.partial(step_kernel, slot, k_dev, adding, result...  37 us
    all_to_all x4, waiting for transfers between devices, body(): arrived.append(lax.all_to_all(terms, 'ga', 0, 0))  18.8 us
    all_to_all x4, starting transfers between devices, body(): arrived.append(lax.all_to_all(terms, 'ga', 0, 0))  18.6 us
    all_to_all x1, blocking collectives, body(): arrived.append(lax.all_to_all(terms, 'ga', 0, 0))  13.3 us
    pallas_call x3, Pallas kernels, piece_of(): pl.pallas_call(functools.partial(piece_kernel, slot, start), in_specs=[pl...  7.9 us
    ppermute x5, starting transfers between devices, shifted(): return lax.ppermute(block, axis, route)  5.95 us
  transfers between devices with their start and end apart: 9, of which 5 were waited for; matrix products, arithmetic and copies ran while one was open for 1% of the time, Pallas kernels for 27%

profile of v4, /device:TPU:0, one launch (start us, length us, event | category | flops | bytes accessed | tf_op | source)
XLA Modules:
  0.0 149.3 jit_solution(13180481393889887888)
XLA Ops:
  0.0 2.0 %piece_of.3.rest_0_ = bf16[2,128,2048]{2,1,0:T(8,128)(2,1)} custom-call(bf16[2,2,512,2048]{3,2,1,0:T(8,128)(2,1)} %bands_ref.15), custom_call_target="tpu_custom_call" | custom-call | bytes 2097152 | tf_op jit(solution)/shard_map/piece_of/pallas_call | solution.py:50
  2.1 0.0 copy-start
  2.1 3.2 %piece_of.4.rest_0_ = bf16[2,384,2048]{2,1,0:T(8,128)(2,1)} custom-call(bf16[2,2,512,2048]{3,2,1,0:T(8,128)(2,1)} %bands_ref.15, bf16[2,128,2048]{2,1,0:T(8,128)(2,1)} %piece_of.3.rest_0_), custom_call_target="tpu_custom_call" | custom-call | bytes 6291456 | tf_op jit(solution)/shard_map/piece_of/pallas_call | solution.py:50
  5.3 0.0 copy-start.7
  5.3 0.0 copy-start.8
  5.3 2.5 %collective-permute-start.2 = (bf16[2,384,2048]{2,1,0:T(8,128)(2,1)}, bf16[2,384,2048]{2,1,0:T(8,128)(2,1)}, u32[]{:S(2)}, u32[]{:S(2)}) collective-permute-start(bf16[2,384,2048]{2,1,0:T(8,128)(2,1)} %piece_of.4.rest_0_), channel_id=1, source_target_pairs={{8,0},{16,8},{24,16},{0,24},{9,1},{17,9},{25,17},{1,25},{10,2},{18... | collective-permute-start | bytes 9437192 | tf_op jit(solution)/shard_map/ppermute | solution.py:24
  7.8 0.0 copy-done
  7.8 0.7 collective-permute-start
  8.5 2.6 %piece_of.5 = bf16[2,256,2048]{2,1,0:T(8,128)(2,1)} custom-call(bf16[2,2,512,2048]{3,2,1,0:T(8,128)(2,1)} %bands_ref.15, bf16[2,384,2048]{2,1,0:T(8,128)(2,1)} %piece_of.4.rest_0_), custom_call_target="tpu_custom_call" | custom-call | bytes 4194304 | tf_op jit(solution)/shard_map/piece_of/pallas_call | solution.py:50
  11.1 0.1 collective-permute-start.3
  11.2 0.0 copy-done.7
  11.2 0.0 copy-done.8
  11.2 0.1 select_reduce_fusion.1
  11.4 0.1 copy.7
  11.5 0.1 fusion.4
  11.6 0.1 pad_maximum_fusion
  11.7 0.6 reshape.39.table_ref
  12.3 41.7 %collective-permute-done.there_ref = bf16[2,128,2048]{2,1,0:T(8,128)(2,1)} collective-permute-done((bf16[2,128,2048]{2,1,0:T(8,128)(2,1)S(1)}, bf16[2,128,2048]{2,1,0:T(8,128)(2,1)}, u32[]{:S(2)}, u32[]{:S(2)}) %collective-permute-start) | collective-permute-done | bytes 1048608 | tf_op jit(solution)/shard_map/ppermute | solution.py:24
  54.0 6.4 %step.5 = (bf16[512,256]{1,0:T(8,128)(2,1)}, bf16[2,128,2048]{2,1,0:T(8,128)(2,1)}) custom-call(f32[10]{0:T(128)} %reshape.39.table_ref, bf16[2,2,512,2048]{3,2,1,0:T(8,128)(2,1)} %bands_ref.15, bf16[2,128,2048]{2,1,0:T(8,128)(2,1)} %collective-permute-done.there_ref), custom_call_target="tpu_custom_call" | custom-call | flops 1073741824 | bytes 5767168 | tf_op jit(solution)/shard_map/step/pallas_call | solution.py:215
  60.5 5.8 %all-to-all-start.1 = ((bf16[8,64,256]{2,1,0:T(8,128)(2,1)}), bf16[8,64,256]{2,1,0:T(8,128)(2,1)S(1)}, u32[]{:S(2)}, u32[]{:S(2)}) async-start(bf16[8,64,256]{2,1,0:T(8,128)(2,1)} %bitcast.10), calls=%async_computation.1 | async-start | bytes 524288 | tf_op jit(solution)/shard_map/all_to_all | solution.py:320
  66.3 0.0 collective-permute-done.2.there_ref
  66.3 9.4 %step.6 = (bf16[512,768]{1,0:T(8,128)(2,1)}, bf16[2,128,2048]{2,1,0:T(8,128)(2,1)}) custom-call(f32[10]{0:T(128)} %reshape.39.table_ref, bf16[2,2,512,2048]{3,2,1,0:T(8,128)(2,1)} %bands_ref.15, bf16[2,384,2048]{2,1,0:T(8,128)(2,1)} %collective-permute-done.2.there_ref), custom_call_target="tpu_custom_call" | custom-call | flops 3221225472 | bytes 8912896 | tf_op jit(solution)/shard_map/step/pallas_call | solution.py:215
  75.7 0.6 all-to-all-done.1.rest_0_
  76.3 0.0 copy-start.4
  76.3 5.5 %all-to-all-start = ((bf16[8,64,768]{2,1,0:T(8,128)(2,1)}), bf16[8,64,768]{2,1,0:T(8,128)(2,1)S(1)}, u32[]{:S(2)}, u32[]{:S(2)}) async-start(bf16[8,64,768]{2,1,0:T(8,128)(2,1)} %bitcast.7), calls=%async_computation | async-start | bytes 1572864 | tf_op jit(solution)/shard_map/all_to_all | solution.py:320
  81.8 1.1 collective-permute-start.1
  82.9 0.0 collective-permute-done.3.there_ref
  82.9 0.0 copy-done.4
  82.9 0.0 copy-start.2
  82.9 1.3 copy-done.2
  84.3 7.5 %step.7 = (bf16[512,512]{1,0:T(8,128)(2,1)}, f32[64,2,2,512]{3,2,1,0:T(2,128)}) custom-call(f32[10]{0:T(128)} %reshape.39.table_ref, bf16[2,2,512,2048]{3,2,1,0:T(8,128)(2,1)} %bands_ref.15, bf16[2,256,2048]{2,1,0:T(8,128)(2,1)} %copy-done.2, bf16[8,64,256]{2,1,0:T(8,128)(2,1)} %copy-done.4), custom_call_target="tpu_custom_call" | custom-call | flops 2147483648 | bytes 7340032 | tf_op jit(solution)/shard_map/step/pallas_call | solution.py:215
  91.8 10.7 %all-to-all-done.rest_0_ = bf16[8,64,768]{2,1,0:T(8,128)(2,1)S(1)} async-done(((bf16[8,64,768]{2,1,0:T(8,128)(2,1)}), bf16[8,64,768]{2,1,0:T(8,128)(2,1)S(1)}, u32[]{:S(2)}, u32[]{:S(2)}) %all-to-all-start) | async-done | bytes 786464 | tf_op jit(solution)/shard_map/all_to_all | solution.py:320
  102.5 3.6 %all-to-all-start.3 = ((bf16[8,64,512]{2,1,0:T(8,128)(2,1)}), bf16[8,64,512]{2,1,0:T(8,128)(2,1)S(1)}, u32[]{:S(2)}, u32[]{:S(2)}) async-start(bf16[8,64,512]{2,1,0:T(8,128)(2,1)} %bitcast.8), calls=%async_computation.3 | async-start | bytes 1048576 | tf_op jit(solution)/shard_map/all_to_all | solution.py:320
  106.1 1.5 %collective-permute-start.4 = (bf16[2,128,2048]{2,1,0:T(8,128)(2,1)}, bf16[2,128,2048]{2,1,0:T(8,128)(2,1)S(1)}, u32[]{:S(2)}, u32[]{:S(2)}) collective-permute-start(bf16[2,128,2048]{2,1,0:T(8,128)(2,1)} %get-tuple-element.20), channel_id=1, source_target_pairs={{8,0},{16,8},{24,16},{0,24},{9,1},{17,9},{25,17},{1,25},{10,2},{18... | collective-permute-start | bytes 3145736 | tf_op jit(solution)/shard_map/ppermute | solution.py:24
  107.6 0.0 collective-permute-done.1.there_ref
  107.6 0.0 copy-done.1
  107.6 6.9 %step.8 = (bf16[512,256]{1,0:T(8,128)(2,1)}, f32[64,2,2,512]{3,2,1,0:T(2,128)}) custom-call(f32[10]{0:T(128)} %reshape.39.table_ref, bf16[2,2,512,2048]{3,2,1,0:T(8,128)(2,1)} %bands_ref.15, bf16[2,128,2048]{2,1,0:T(8,128)(2,1)} %collective-permute-done.1.there_ref, bf16[8,64,768]{2,1,0:T(8,128)(2,1)} %copy-done.1, ...), custom_call_target="tpu_custom_call", output_to_operand_aliasing={{1}: (4, {})} | custom-call | flops 1073741824 | bytes 5767168 | tf_op jit(solution)/shard_map/step/pallas_call | solution.py:215
  114.6 6.2 %all-to-all-done.3.rest_0_ = bf16[8,64,512]{2,1,0:T(8,128)(2,1)S(1)} async-done(((bf16[8,64,512]{2,1,0:T(8,128)(2,1)}), bf16[8,64,512]{2,1,0:T(8,128)(2,1)S(1)}, u32[]{:S(2)}, u32[]{:S(2)}) %all-to-all-start.3) | async-done | bytes 524320 | tf_op jit(solution)/shard_map/all_to_all | solution.py:320
  120.8 3.6 %all-to-all-start.2 = ((bf16[8,64,256]{2,1,0:T(8,128)(2,1)}), bf16[8,64,256]{2,1,0:T(8,128)(2,1)S(1)}, u32[]{:S(2)}, u32[]{:S(2)}) async-start(bf16[8,64,256]{2,1,0:T(8,128)(2,1)} %bitcast.9), calls=%async_computation.2 | async-start | bytes 524288 | tf_op jit(solution)/shard_map/all_to_all | solution.py:320
  124.4 0.0 collective-permute-done.4.there_ref
  124.4 0.0 copy-start.6
  124.4 0.0 copy-done.3
  124.4 1.0 copy-done.6
  125.4 6.8 %step.9 = (bf16[512,256]{1,0:T(8,128)(2,1)}, f32[64,2,2,512]{3,2,1,0:T(2,128)}) custom-call(f32[10]{0:T(128)} %reshape.39.table_ref, bf16[2,2,512,2048]{3,2,1,0:T(8,128)(2,1)} %bands_ref.15, bf16[2,128,2048]{2,1,0:T(8,128)(2,1)} %copy-done.6, bf16[8,64,512]{2,1,0:T(8,128)(2,1)} %copy-done.3, ...), custom_call_target="tpu_custom_call", output_to_operand_aliasing={{1}: (4, {})} | custom-call | flops 1073741824 | bytes 5767168 | tf_op jit(solution)/shard_map/step/pallas_call | solution.py:215
  132.2 1.3 all-to-all-done.2.refs_0_
  133.5 13.3 %all_to_all.25.refs_1_ = bf16[8,64,256]{2,1,0:T(8,128)(2,1)} all-to-all(bf16[8,64,256]{2,1,0:T(8,128)(2,1)} %bitcast.11), channel_id=1, replica_groups=mesh['ka'=4,'ga'=8] {'ga'}, dimensions={0} | all-to-all | bytes 524288 | tf_op jit(solution)/shard_map/all_to_all | solution.py:320
  146.8 0.0 copy-done.5
  146.8 2.4 %finish.1 = f32[64,2,2,512]{3,2,1,0:T(2,128)} custom-call(f32[10]{0:T(128)} %reshape.39.table_ref, bf16[8,64,256]{2,1,0:T(8,128)(2,1)} %copy-done.5, bf16[8,64,256]{2,1,0:T(8,128)(2,1)} %all_to_all.25.refs_1_, f32[64,2,2,512]{3,2,1,0:T(2,128)} %get-tuple-element.24.refs_2_), custom_call_target="tpu_custom_call", output_to_operand_aliasing={{}: (3, {})} | custom-call | bytes 524288 | tf_op jit(solution)/shard_map/finish/pallas_call | solution.py:257
  (5 shorter events, 0.0 us)
Async XLA Ops:
  2.1 5.7 %copy-start = (bf16[2,128,2048]{2,1,0:T(8,128)(2,1)S(1)}, bf16[2,128,2048]{2,1,0:T(8,128)(2,1)}, u32[]{:S(2)}) copy-start(bf16[2,128,2048]{2,1,0:T(8,128)(2,1)} %piece_of.3.rest_0_) | copy-start | bytes 3145732
  5.3 5.9 %copy-start.7 = (s32[2]{0:T(128)S(1)}, s32[2]{0:T(128)}, u32[]{:S(2)}) copy-start(s32[2]{0:T(128)} %param.4) | copy-start | bytes 28
  5.3 5.9 %copy-start.8 = (s32[2]{0:T(128)S(1)}, s32[2]{0:T(128)}, u32[]{:S(2)}) copy-start(s32[2]{0:T(128)} %param.5) | copy-start | bytes 28
  5.3 61.0 %collective-permute-start.2 = (bf16[2,384,2048]{2,1,0:T(8,128)(2,1)}, bf16[2,384,2048]{2,1,0:T(8,128)(2,1)}, u32[]{:S(2)}, u32[]{:S(2)}) collective-permute-start(bf16[2,384,2048]{2,1,0:T(8,128)(2,1)} %piece_of.4.rest_0_), channel_id=1, source_target_pairs={{8,0},{16,8},{24,16},{0,24},{9,1},{17,9},{25,17},{1,25},{10,2},{18... | collective-permute-start | bytes 9437192 | tf_op jit(solution)/shard_map/ppermute | solution.py:24
  7.8 46.2 %collective-permute-start = (bf16[2,128,2048]{2,1,0:T(8,128)(2,1)S(1)}, bf16[2,128,2048]{2,1,0:T(8,128)(2,1)}, u32[]{:S(2)}, u32[]{:S(2)}) collective-permute-start(bf16[2,128,2048]{2,1,0:T(8,128)(2,1)S(1)} %copy-done), channel_id=1, source_target_pairs={{8,0},{16,8},{24,16},{0,24},{9,1},{17,9},{25,17},{1,25},{10,2},{18... | collective-permute-start | bytes 3145736 | tf_op jit(solution)/shard_map/ppermute | solution.py:24
  11.1 71.8 %collective-permute-start.3 = (bf16[2,256,2048]{2,1,0:T(8,128)(2,1)}, bf16[2,256,2048]{2,1,0:T(8,128)(2,1)S(1)}, u32[]{:S(2)}, u32[]{:S(2)}) collective-permute-start(bf16[2,256,2048]{2,1,0:T(8,128)(2,1)} %piece_of.5), channel_id=1, source_target_pairs={{8,0},{16,8},{24,16},{0,24},{9,1},{17,9},{25,17},{1,25},{10,2},{18... | collective-permute-start | bytes 6291464 | tf_op jit(solution)/shard_map/ppermute | solution.py:24
  60.5 15.8 %all-to-all-start.1 = ((bf16[8,64,256]{2,1,0:T(8,128)(2,1)}), bf16[8,64,256]{2,1,0:T(8,128)(2,1)S(1)}, u32[]{:S(2)}, u32[]{:S(2)}) async-start(bf16[8,64,256]{2,1,0:T(8,128)(2,1)} %bitcast.10), calls=%async_computation.1 | async-start | bytes 524288 | tf_op jit(solution)/shard_map/all_to_all | solution.py:320
  76.3 6.7 %copy-start.4 = (bf16[8,64,256]{2,1,0:T(8,128)(2,1)}, bf16[8,64,256]{2,1,0:T(8,128)(2,1)S(1)}, u32[]{:S(2)}) copy-start(bf16[8,64,256]{2,1,0:T(8,128)(2,1)S(1)} %all-to-all-done.1.rest_0_) | copy-start | bytes 786436
  76.3 26.2 %all-to-all-start = ((bf16[8,64,768]{2,1,0:T(8,128)(2,1)}), bf16[8,64,768]{2,1,0:T(8,128)(2,1)S(1)}, u32[]{:S(2)}, u32[]{:S(2)}) async-start(bf16[8,64,768]{2,1,0:T(8,128)(2,1)} %bitcast.7), calls=%async_computation | async-start | bytes 1572864 | tf_op jit(solution)/shard_map/all_to_all | solution.py:320
  81.8 25.9 %collective-permute-start.1 = (bf16[2,128,2048]{2,1,0:T(8,128)(2,1)}, bf16[2,128,2048]{2,1,0:T(8,128)(2,1)}, u32[]{:S(2)}, u32[]{:S(2)}) collective-permute-start(bf16[2,128,2048]{2,1,0:T(8,128)(2,1)} %get-tuple-element.15), channel_id=1, source_target_pairs={{8,0},{16,8},{24,16},{0,24},{9,1},{17,9},{25,17},{1,25},{10,2},{18... | collective-permute-start | bytes 3145736 | tf_op jit(solution)/shard_map/ppermute | solution.py:24
  82.9 1.3 copy-start.2
  102.5 5.2 %copy-start.1 = (bf16[8,64,768]{2,1,0:T(8,128)(2,1)}, bf16[8,64,768]{2,1,0:T(8,128)(2,1)S(1)}, u32[]{:S(2)}) copy-start(bf16[8,64,768]{2,1,0:T(8,128)(2,1)S(1)} %all-to-all-done.rest_0_) | copy-start | bytes 2359300
  102.5 18.3 %all-to-all-start.3 = ((bf16[8,64,512]{2,1,0:T(8,128)(2,1)}), bf16[8,64,512]{2,1,0:T(8,128)(2,1)S(1)}, u32[]{:S(2)}, u32[]{:S(2)}) async-start(bf16[8,64,512]{2,1,0:T(8,128)(2,1)} %bitcast.8), calls=%async_computation.3 | async-start | bytes 1048576 | tf_op jit(solution)/shard_map/all_to_all | solution.py:320
  106.1 18.3 %collective-permute-start.4 = (bf16[2,128,2048]{2,1,0:T(8,128)(2,1)}, bf16[2,128,2048]{2,1,0:T(8,128)(2,1)S(1)}, u32[]{:S(2)}, u32[]{:S(2)}) collective-permute-start(bf16[2,128,2048]{2,1,0:T(8,128)(2,1)} %get-tuple-element.20), channel_id=1, source_target_pairs={{8,0},{16,8},{24,16},{0,24},{9,1},{17,9},{25,17},{1,25},{10,2},{18... | collective-permute-start | bytes 3145736 | tf_op jit(solution)/shard_map/ppermute | solution.py:24
  120.8 3.7 %copy-start.3 = (bf16[8,64,512]{2,1,0:T(8,128)(2,1)}, bf16[8,64,512]{2,1,0:T(8,128)(2,1)S(1)}, u32[]{:S(2)}) copy-start(bf16[8,64,512]{2,1,0:T(8,128)(2,1)S(1)} %all-to-all-done.3.rest_0_) | copy-start | bytes 1572868
  120.8 12.7 %all-to-all-start.2 = ((bf16[8,64,256]{2,1,0:T(8,128)(2,1)}), bf16[8,64,256]{2,1,0:T(8,128)(2,1)S(1)}, u32[]{:S(2)}, u32[]{:S(2)}) async-start(bf16[8,64,256]{2,1,0:T(8,128)(2,1)} %bitcast.9), calls=%async_computation.2 | async-start | bytes 524288 | tf_op jit(solution)/shard_map/all_to_all | solution.py:320
  124.4 1.0 copy-start.6
  133.5 13.3 %copy-start.5 = (bf16[8,64,256]{2,1,0:T(8,128)(2,1)}, bf16[8,64,256]{2,1,0:T(8,128)(2,1)S(1)}, u32[]{:S(2)}) copy-start(bf16[8,64,256]{2,1,0:T(8,128)(2,1)S(1)} %all-to-all-done.2.refs_0_) | copy-start | bytes 786436

commit v5 on v4

--- a/solution.py
+++ b/solution.py
@@ -10,12 +10,11 @@
 
 NKB = 4
 PLANE = 1024
-ROWS = 256
 STRIP = 32
 DEPTH = 512
 LAG = 2
-AHEAD = 3
-VMEM_BYTES = 58 * 1024 * 1024
+AHEAD = 2
+VMEM_BYTES = 56 * 1024 * 1024
 
 
 def shifted(block, axis, distance):
@@ -64,8 +63,8 @@
     )(bands, *after)
 
 
-def near_into(near_buf, there_buf, table_ref, base, planes):
-    width, points = there_buf.shape[1:]
+def near_into(near_buf, there_ref, table_ref, base, planes):
+    width, points = there_ref.shape[1:]
 
     @pl.loop(0, width // STRIP)
     def _(strip):
@@ -76,15 +75,12 @@
             cosine = table_ref[base + 1 + plane]
             sine = table_ref[base + 1 + planes + plane]
             columns = pl.ds(start, DEPTH)
-            later = pl.ds(points + start, DEPTH)
-            real_part = there_buf[0, rows, columns].astype(jnp.float32)
-            imag_part = there_buf[1, rows, columns].astype(jnp.float32)
-            near_re = (real_part * cosine + imag_part * sine).astype(jnp.bfloat16)
-            near_im = (imag_part * cosine - real_part * sine).astype(jnp.bfloat16)
-            near_buf[rows, columns] = near_re
-            near_buf[rows, later] = near_im
-            near_buf[mirror, columns] = near_im
-            near_buf[mirror, later] = -near_re
+            real_part = there_ref[0, rows, columns].astype(jnp.float32)
+            imag_part = there_ref[1, rows, columns].astype(jnp.float32)
+            near_re = real_part * cosine + imag_part * sine
+            near_im = imag_part * cosine - real_part * sine
+            near_buf[rows, columns] = near_re.astype(jnp.bfloat16)
+            near_buf[mirror, columns] = near_im.astype(jnp.bfloat16)
 
 
 def add_into(sum_buf, arrived_buf):
@@ -108,10 +104,11 @@
     out_ref = rest.pop(0)
     result_ref = rest.pop(0) if adding else None
     piece_ref = rest.pop(0) if later else None
-    own_buf, there_buf, near_buf, sems = rest[:4]
-    if later:
-        piece_buf, piece_sems = rest[4:6]
-        del rest[4:6]
+    own_buf, near_buf, own_sems = rest[:3]
+    del rest[:3]
+    if later:
+        piece_buf, piece_sems = rest[:2]
+        del rest[:2]
         later_slot, later_start, later_width = later
         loads = [
             pltpu.make_async_copy(
@@ -125,52 +122,37 @@
             pltpu.make_async_copy(piece_buf.at[part], piece_ref.at[part], piece_sems.at[1, part])
             for part in range(2)
         ]
-    points = there_buf.shape[2]
-    blocks = own_buf.shape[0]
     if adding:
-        arrived_buf, sum_buf, add_sems = rest[4:]
-        arrival = pltpu.make_async_copy(arrived_ref, arrived_buf, add_sems.at[0])
-        arrival.start()
-    there = [
-        pltpu.make_async_copy(there_ref.at[part], there_buf.at[part], sems.at[0, part])
+        sum_buf, placed_sem = rest
+    own = [
+        pltpu.make_async_copy(bands_ref.at[point, part], own_buf.at[part], own_sems.at[part])
         for part in range(2)
     ]
-    own = [
-        pltpu.make_async_copy(
-            bands_ref.at[point, part, pl.ds(block * ROWS, ROWS), :],
-            own_buf.at[block, :, pl.ds(part * points, points)],
-            sems.at[1 + block, part],
-        )
-        for block in range(blocks)
-        for part in range(2)
-    ]
-    for copy in there + (loads if later else []) + own:
+    for copy in own + (loads if later else []):
         copy.start()
     if adding:
         add_slot, start, width = adding
         add_point = table_ref[add_slot * stride].astype(jnp.int32)
-        arrival.wait()
-        add_into(sum_buf, arrived_buf)
+        add_into(sum_buf, arrived_ref)
         placing = pltpu.make_async_copy(
-            sum_buf, result_ref.at[:, add_point, :, pl.ds(start, width)], add_sems.at[1]
+            sum_buf, result_ref.at[:, add_point, :, pl.ds(start, width)], placed_sem
         )
         placing.start()
-    for copy in there:
-        copy.wait()
-    near_into(near_buf, there_buf, table_ref, base, planes)
+    near_into(near_buf, there_ref, table_ref, base, planes)
     if later:
         for load, store in zip(loads, stores):
             load.wait()
             store.start()
-    for block in range(blocks):
-        own[2 * block].wait()
-        own[2 * block + 1].wait()
-        out_ref[pl.ds(block * ROWS, ROWS), :] = lax.dot_general(
-            own_buf[block],
-            near_buf[...],
-            (((1,), (1,)), ((), ())),
-            preferred_element_type=jnp.float32,
-        ).astype(out_ref.dtype)
+    for copy in own:
+        copy.wait()
+    dims = (((1,), (1,)), ((), ()))
+    width = there_ref.shape[1]
+    of_re, of_im = [
+        lax.dot_general(own_buf[part], near_buf[...], dims, preferred_element_type=jnp.float32)
+        for part in range(2)
+    ]
+    out_ref[:, :width] = (of_re[:, :width] + of_im[:, width:]).astype(out_ref.dtype)
+    out_ref[:, width:] = (of_re[:, width:] - of_im[:, :width]).astype(out_ref.dtype)
     if adding:
         placing.wait()
     if later:
@@ -181,15 +163,14 @@
 def step(slot, table, bands, there, adding, arrived, result, shape, later):
     k_dev, _, nbands, points = bands.shape
     width = there.shape[1]
-    blocks = nbands // ROWS
     operands = [table, bands, there]
+    spaces = [pltpu.SMEM, pl.ANY, pltpu.VMEM]
     out_shape = [jax.ShapeDtypeStruct((nbands, 2 * width), jnp.bfloat16)]
     out_specs = [pl.BlockSpec(memory_space=pltpu.VMEM)]
     scratch = [
-        pltpu.VMEM((blocks, ROWS, 2 * points), jnp.bfloat16),
-        pltpu.VMEM((2, width, points), jnp.bfloat16),
-        pltpu.VMEM((2 * width, 2 * points), jnp.bfloat16),
-        pltpu.SemaphoreType.DMA((1 + blocks, 2)),
+        pltpu.VMEM((2, nbands, points), jnp.bfloat16),
+        pltpu.VMEM((2 * width, points), jnp.bfloat16),
+        pltpu.SemaphoreType.DMA((2,)),
     ]
     aliases = {}
     if later:
@@ -199,23 +180,23 @@
         ]
     if adding:
         operands.append(arrived)
+        spaces.append(pltpu.VMEM)
         if result is not None:
             aliases = {len(operands): 1}
             operands.append(result)
+            spaces.append(pl.ANY)
         out_shape.append(jax.ShapeDtypeStruct(shape, jnp.float32))
         out_specs.append(pl.BlockSpec(memory_space=pl.ANY))
         scratch += [
-            pltpu.VMEM(arrived.shape, arrived.dtype),
             pltpu.VMEM((shape[0], 2, adding[2]), jnp.float32),
-            pltpu.SemaphoreType.DMA((2,)),
+            pltpu.SemaphoreType.DMA,
         ]
     if later:
         out_shape.append(jax.ShapeDtypeStruct((2, later[2], points), bands.dtype))
         out_specs.append(pl.BlockSpec(memory_space=pl.ANY))
     outs = pl.pallas_call(
         functools.partial(step_kernel, slot, k_dev, adding, result is None, later),
-        in_specs=[pl.BlockSpec(memory_space=pltpu.SMEM)]
-        + [pl.BlockSpec(memory_space=pl.ANY)] * (len(operands) - 1),
+        in_specs=[pl.BlockSpec(memory_space=space) for space in spaces],
         out_specs=out_specs,
         scratch_shapes=scratch,
         out_shape=out_shape,
@@ -234,18 +215,14 @@
 def finish_kernel(parts, stride, table_ref, *refs):
     count = len(parts)
     arrived, result_ref = refs[:count], refs[count + 1]
-    bufs, sums, sems = refs[count + 2 : -1 - count], refs[-1 - count : -1], refs[-1]
-    copies = [pltpu.make_async_copy(arrived[i], bufs[i], sems.at[0, i]) for i in range(count)]
-    for copy in copies:
-        copy.start()
+    sums, sems = refs[count + 2 : -1], refs[-1]
     placing = []
     for i, (slot, start, width) in enumerate(parts):
         point = table_ref[slot * stride].astype(jnp.int32)
-        copies[i].wait()
-        add_into(sums[i], bufs[i])
+        add_into(sums[i], arrived[i])
         columns = pl.ds(start, width)
         placing.append(
-            pltpu.make_async_copy(sums[i], result_ref.at[:, point, :, columns], sems.at[1, i])
+            pltpu.make_async_copy(sums[i], result_ref.at[:, point, :, columns], sems.at[i])
         )
         placing[-1].start()
     for copy in placing:
@@ -257,11 +234,11 @@
     return pl.pallas_call(
         functools.partial(finish_kernel, parts, table.shape[0] // k_dev),
         in_specs=[pl.BlockSpec(memory_space=pltpu.SMEM)]
-        + [pl.BlockSpec(memory_space=pl.ANY)] * (len(parts) + 1),
+        + [pl.BlockSpec(memory_space=pltpu.VMEM)] * len(parts)
+        + [pl.BlockSpec(memory_space=pl.ANY)],
         out_specs=pl.BlockSpec(memory_space=pl.ANY),
-        scratch_shapes=[pltpu.VMEM(array.shape, array.dtype) for array in arrived]
-        + [pltpu.VMEM((rows, 2, width), jnp.float32) for _, _, width in parts]
-        + [pltpu.SemaphoreType.DMA((2, len(parts)))],
+        scratch_shapes=[pltpu.VMEM((rows, 2, width), jnp.float32) for _, _, width in parts]
+        + [pltpu.SemaphoreType.DMA((len(parts),))],
         out_shape=jax.ShapeDtypeStruct(result.shape, jnp.float32),
         input_output_aliases={1 + len(parts): 0},
         compiler_params=pltpu.CompilerParams(vmem_limit_bytes=VMEM_BYTES),
@@ -274,7 +251,7 @@
 
 def cuts(nbands, first):
     half, quarter = nbands // 2, nbands // 4
-    widths = [quarter, half + quarter] if first else [half, quarter, quarter]
+    widths = [quarter, quarter, half] if first else [half, quarter, quarter]
     starts = [sum(widths[:i]) for i in range(len(widths))]
     return list(zip(starts, widths))
 

time: 150 us -> 137 us (0.913)
  waiting for transfers between devices: 60.5 us -> 24.2 us
  blocking collectives: 13.3 us -> 37.6 us
  local copies, waits for them, and re-layouts: 3.06 us -> 5.22 us
  Pallas kernels: 47.4 us -> 45.3 us
    ppermute x5 -> x6, waiting for transfers between devices: 41.7 us -> 15.4 us  [shifted(): return lax.ppermute(block, axis, route)]
    all_to_all x1 -> x3, blocking collectives: 13.3 us -> 37.6 us  [body(): arrived.append(lax.all_to_all(terms, 'ga', 0, 0))]
    all_to_all x4 -> x3, waiting for transfers between devices: 18.8 us -> 8.8 us  [body(): arrived.append(lax.all_to_all(terms, 'ga', 0, 0))]
    all_to_all x4 -> x3, starting transfers between devices: 18.6 us -> 14.1 us  [body(): arrived.append(lax.all_to_all(terms, 'ga', 0, 0))]
    pallas_call x3 -> x2, Pallas kernels: 7.9 us -> 4.13 us  [piece_of(): pl.pallas_call(functools.partial(piece_kernel, slot, start), in_specs=[pl...]
    ppermute x5 -> x6, starting transfers between devices: 5.95 us -> 9.04 us  [shifted(): return lax.ppermute(block, axis, route)]
    pallas_call x5 -> x6, Pallas kernels: 37 us -> 39.3 us  [step(): pl.pallas_call(functools.partial(step_kernel, slot, k_dev, adding, result...]
    unnamed x18 -> x22, local copies, waits for them, and re-layouts: 2.34 us -> 4.46 us
  transfers between devices with their start and end apart: 9 -> 9, of which waited for: 5 -> 5; matrix products, arithmetic and copies ran while one was open for 1% -> 1% of each run, Pallas kernels for 27% -> 26%
where the time goes in v5:
time: 137 us; the launch traced here: 136 us
  Pallas kernels  45.3 us (33%)
  blocking collectives  37.6 us (27%)
  waiting for transfers between devices  24.2 us (18%)
  starting transfers between devices  23.1 us (17%)
  local copies, waits for them, and re-layouts  5.22 us (4%)
    pallas_call x6, Pallas kernels, step(): pl.pallas_call(functools.partial(step_kernel, slot, k_dev, adding, result...  39.3 us
    all_to_all x3, blocking collectives, body(): arrived.append(lax.all_to_all(terms, 'ga', 0, 0))  37.6 us
    ppermute x6, waiting for transfers between devices, shifted(): return lax.ppermute(block, axis, route)  15.4 us
    all_to_all x3, starting transfers between devices, body(): arrived.append(lax.all_to_all(terms, 'ga', 0, 0))  14.1 us
    ppermute x6, starting transfers between devices, shifted(): return lax.ppermute(block, axis, route)  9.04 us
    all_to_all x3, waiting for transfers between devices, body(): arrived.append(lax.all_to_all(terms, 'ga', 0, 0))  8.8 us
    unnamed x22, local copies, waits for them, and re-layouts  4.46 us
    pallas_call x2, Pallas kernels, piece_of(): pl.pallas_call(functools.partial(piece_kernel, slot, start), in_specs=[pl...  4.13 us
  transfers between devices with their start and end apart: 9, of which 5 were waited for; matrix products, arithmetic and copies ran while one was open for 1% of the time, Pallas kernels for 26%

profile of v5, /device:TPU:0, one launch (start us, length us, event | category | flops | bytes accessed | tf_op | source)
XLA Modules:
  0.0 135.9 jit_solution(11710068841194575329)
XLA Ops:
  0.0 2.0 %piece_of.2.rest_0_ = bf16[2,128,2048]{2,1,0:T(8,128)(2,1)} custom-call(bf16[2,2,512,2048]{3,2,1,0:T(8,128)(2,1)} %bands_ref.15), custom_call_target="tpu_custom_call" | custom-call | bytes 2097152 | tf_op jit(solution)/shard_map/piece_of/pallas_call | solution.py:49
  2.0 0.0 copy-start.9
  2.1 0.0 copy-start.10
  2.1 2.5 %collective-permute-start = (bf16[2,128,2048]{2,1,0:T(8,128)(2,1)}, bf16[2,128,2048]{2,1,0:T(8,128)(2,1)S(1)}, u32[]{:S(2)}, u32[]{:S(2)}) collective-permute-start(bf16[2,128,2048]{2,1,0:T(8,128)(2,1)} %piece_of.2.rest_0_), channel_id=1, source_target_pairs={{8,0},{16,8},{24,16},{0,24},{9,1},{17,9},{25,17},{1,25},{10,2},{18... | collective-permute-start | bytes 3145736 | tf_op jit(solution)/shard_map/ppermute | solution.py:23
  4.5 2.1 %piece_of.3 = bf16[2,128,2048]{2,1,0:T(8,128)(2,1)} custom-call(bf16[2,2,512,2048]{3,2,1,0:T(8,128)(2,1)} %bands_ref.15, bf16[2,128,2048]{2,1,0:T(8,128)(2,1)} %piece_of.2.rest_0_), custom_call_target="tpu_custom_call" | custom-call | bytes 2097152 | tf_op jit(solution)/shard_map/piece_of/pallas_call | solution.py:49
  6.6 0.7 collective-permute-start.3
  7.4 0.0 copy-done.9
  7.4 0.0 copy-done.10
  7.4 0.1 select_reduce_fusion.1
  7.5 0.1 copy.8
  7.6 0.1 fusion.4
  7.7 0.1 pad_maximum_fusion
  7.8 0.7 reshape.42.table_ref
  8.5 8.7 %collective-permute-done.there_ref = bf16[2,128,2048]{2,1,0:T(8,128)(2,1)S(1)} collective-permute-done((bf16[2,128,2048]{2,1,0:T(8,128)(2,1)}, bf16[2,128,2048]{2,1,0:T(8,128)(2,1)S(1)}, u32[]{:S(2)}, u32[]{:S(2)}) %collective-permute-start) | collective-permute-done | bytes 1048608 | tf_op jit(solution)/shard_map/ppermute | solution.py:23
  17.2 1.0 copy-done.4
  18.1 6.5 %step.6 = (bf16[512,256]{1,0:T(8,128)(2,1)}, bf16[2,256,2048]{2,1,0:T(8,128)(2,1)}) custom-call(f32[10]{0:T(128)} %reshape.42.table_ref, bf16[2,2,512,2048]{3,2,1,0:T(8,128)(2,1)} %bands_ref.15, bf16[2,128,2048]{2,1,0:T(8,128)(2,1)} %copy-done.4), custom_call_target="tpu_custom_call" | custom-call | flops 1073741824 | bytes 5767168 | tf_op jit(solution)/shard_map/step/pallas_call | solution.py:197
  24.6 0.0 copy-start.8
  24.6 1.9 %collective-permute-start.1 = (bf16[2,256,2048]{2,1,0:T(8,128)(2,1)}, bf16[2,256,2048]{2,1,0:T(8,128)(2,1)}, u32[]{:S(2)}, u32[]{:S(2)}) collective-permute-start(bf16[2,256,2048]{2,1,0:T(8,128)(2,1)} %get-tuple-element.19), channel_id=1, source_target_pairs={{8,0},{16,8},{24,16},{0,24},{9,1},{17,9},{25,17},{1,25},{10,2},{18... | collective-permute-start | bytes 6291464 | tf_op jit(solution)/shard_map/ppermute | solution.py:23
  26.5 1.9 %collective-permute-done.3.there_ref = bf16[2,128,2048]{2,1,0:T(8,128)(2,1)S(1)} collective-permute-done((bf16[2,128,2048]{2,1,0:T(8,128)(2,1)}, bf16[2,128,2048]{2,1,0:T(8,128)(2,1)S(1)}, u32[]{:S(2)}, u32[]{:S(2)}) %collective-permute-start.3) | collective-permute-done | bytes 1048608 | tf_op jit(solution)/shard_map/ppermute | solution.py:23
  28.4 1.0 copy-done.3
  29.4 6.5 %step.8 = (bf16[512,256]{1,0:T(8,128)(2,1)}, bf16[2,256,2048]{2,1,0:T(8,128)(2,1)}) custom-call(f32[10]{0:T(128)} %reshape.42.table_ref, bf16[2,2,512,2048]{3,2,1,0:T(8,128)(2,1)} %bands_ref.15, bf16[2,128,2048]{2,1,0:T(8,128)(2,1)} %copy-done.3), custom_call_target="tpu_custom_call" | custom-call | flops 1073741824 | bytes 5767168 | tf_op jit(solution)/shard_map/step/pallas_call | solution.py:197
  35.8 1.9 %collective-permute-start.4 = (bf16[2,256,2048]{2,1,0:T(8,128)(2,1)}, bf16[2,256,2048]{2,1,0:T(8,128)(2,1)S(1)}, u32[]{:S(2)}, u32[]{:S(2)}) collective-permute-start(bf16[2,256,2048]{2,1,0:T(8,128)(2,1)} %get-tuple-element.23), channel_id=1, source_target_pairs={{8,0},{16,8},{24,16},{0,24},{9,1},{17,9},{25,17},{1,25},{10,2},{18... | collective-permute-start | bytes 6291464 | tf_op jit(solution)/shard_map/ppermute | solution.py:23
  37.7 0.0 copy-done.8
  37.7 13.9 %all_to_all.30.rest_0_ = bf16[8,64,256]{2,1,0:T(8,128)(2,1)} all-to-all(bf16[8,64,256]{2,1,0:T(8,128)(2,1)S(1)} %bitcast.12), channel_id=1, replica_groups=mesh['ka'=4,'ga'=8] {'ga'}, dimensions={0} | all-to-all | bytes 524288 | tf_op jit(solution)/shard_map/all_to_all | solution.py:297
  51.6 3.4 %all-to-all-start.2 = ((bf16[8,64,256]{2,1,0:T(8,128)(2,1)}), bf16[8,64,256]{2,1,0:T(8,128)(2,1)S(1)}, u32[]{:S(2)}, u32[]{:S(2)}) async-start(bf16[8,64,256]{2,1,0:T(8,128)(2,1)} %bitcast.10), calls=%async_computation.2 | async-start | bytes 524288 | tf_op jit(solution)/shard_map/all_to_all | solution.py:297
  55.0 0.0 collective-permute-done.1.there_ref
  55.0 7.5 %step.7 = (bf16[512,512]{1,0:T(8,128)(2,1)}, f32[64,2,2,512]{3,2,1,0:T(2,128)}, bf16[2,128,2048]{2,1,0:T(8,128)(2,1)}) custom-call(f32[10]{0:T(128)} %reshape.42.table_ref, bf16[2,2,512,2048]{3,2,1,0:T(8,128)(2,1)} %bands_ref.15, bf16[2,256,2048]{2,1,0:T(8,128)(2,1)} %collective-permute-done.1.there_ref, bf16[8,64,256]{2,1,0:T(8,128)(2,1)} %all_to_all.30.rest_0_), custom_call_target="tpu_custom_call" | custom-call | flops 2147483648 | bytes 7340032 | tf_op jit(solution)/shard_map/step/pallas_call | solution.py:197
  62.6 0.9 all-to-all-done.2.rest_0_
  63.4 5.2 %all-to-all-start.1 = ((bf16[8,64,512]{2,1,0:T(8,128)(2,1)}), bf16[8,64,512]{2,1,0:T(8,128)(2,1)S(1)}, u32[]{:S(2)}, u32[]{:S(2)}) async-start(bf16[8,64,512]{2,1,0:T(8,128)(2,1)} %bitcast.8), calls=%async_computation.1 | async-start | bytes 1048576 | tf_op jit(solution)/shard_map/all_to_all | solution.py:297
  68.6 0.0 collective-permute-start.2
  68.6 4.8 %collective-permute-done.4.there_ref = bf16[2,256,2048]{2,1,0:T(8,128)(2,1)S(1)} collective-permute-done((bf16[2,256,2048]{2,1,0:T(8,128)(2,1)}, bf16[2,256,2048]{2,1,0:T(8,128)(2,1)S(1)}, u32[]{:S(2)}, u32[]{:S(2)}) %collective-permute-start.4) | collective-permute-done | bytes 2097184 | tf_op jit(solution)/shard_map/ppermute | solution.py:23
  73.3 0.0 copy-done.5
  73.3 1.3 copy-done
  74.7 7.5 %step.9 = (bf16[512,512]{1,0:T(8,128)(2,1)}, f32[64,2,2,512]{3,2,1,0:T(2,128)}, bf16[2,128,2048]{2,1,0:T(8,128)(2,1)}) custom-call(f32[10]{0:T(128)} %reshape.42.table_ref, bf16[2,2,512,2048]{3,2,1,0:T(8,128)(2,1)} %bands_ref.15, bf16[2,256,2048]{2,1,0:T(8,128)(2,1)} %copy-done, bf16[8,64,256]{2,1,0:T(8,128)(2,1)} %copy-done.5, ...), custom_call_target="tpu_custom_call", output_to_operand_aliasing={{1}: (4, {})} | custom-call | flops 2147483648 | bytes 7340032 | tf_op jit(solution)/shard_map/step/pallas_call | solution.py:197
  82.2 2.1 %collective-permute-start.5 = (bf16[2,128,2048]{2,1,0:T(8,128)(2,1)}, bf16[2,128,2048]{2,1,0:T(8,128)(2,1)S(1)}, u32[]{:S(2)}, u32[]{:S(2)}) collective-permute-start(bf16[2,128,2048]{2,1,0:T(8,128)(2,1)} %get-tuple-element.28), channel_id=1, source_target_pairs={{8,0},{16,8},{24,16},{0,24},{9,1},{17,9},{25,17},{1,25},{10,2},{18... | collective-permute-start | bytes 3145736 | tf_op jit(solution)/shard_map/ppermute | solution.py:23
  84.3 0.0 all-to-all-done.1.rest_0_
  84.3 5.5 %all-to-all-start.4 = ((bf16[8,64,512]{2,1,0:T(8,128)(2,1)}), bf16[8,64,512]{2,1,0:T(8,128)(2,1)S(1)}, u32[]{:S(2)}, u32[]{:S(2)}) async-start(bf16[8,64,512]{2,1,0:T(8,128)(2,1)} %bitcast.9), calls=%async_computation.4 | async-start | bytes 1048576 | tf_op jit(solution)/shard_map/all_to_all | solution.py:297
  89.9 0.0 collective-permute-done.2.there_ref
  89.9 0.0 copy-done.1
  89.9 5.7 %step.10 = (bf16[512,256]{1,0:T(8,128)(2,1)}, f32[64,2,2,512]{3,2,1,0:T(2,128)}) custom-call(f32[10]{0:T(128)} %reshape.42.table_ref, bf16[2,2,512,2048]{3,2,1,0:T(8,128)(2,1)} %bands_ref.15, bf16[2,128,2048]{2,1,0:T(8,128)(2,1)} %collective-permute-done.2.there_ref, bf16[8,64,512]{2,1,0:T(8,128)(2,1)} %copy-done.1, ...), custom_call_target="tpu_custom_call", output_to_operand_aliasing={{1}: (4, {})} | custom-call | flops 1073741824 | bytes 5767168 | tf_op jit(solution)/shard_map/step/pallas_call | solution.py:197
  95.6 7.9 %all-to-all-done.4.rest_0_ = bf16[8,64,512]{2,1,0:T(8,128)(2,1)S(1)} async-done(((bf16[8,64,512]{2,1,0:T(8,128)(2,1)}), bf16[8,64,512]{2,1,0:T(8,128)(2,1)S(1)}, u32[]{:S(2)}, u32[]{:S(2)}) %all-to-all-start.4) | async-done | bytes 524320 | tf_op jit(solution)/shard_map/all_to_all | solution.py:297
  103.5 0.0 collective-permute-done.5.there_ref
  103.5 0.8 copy-done.2
  104.4 0.4 copy-done.6
  104.7 5.7 %step.11 = (bf16[512,256]{1,0:T(8,128)(2,1)}, f32[64,2,2,512]{3,2,1,0:T(2,128)}) custom-call(f32[10]{0:T(128)} %reshape.42.table_ref, bf16[2,2,512,2048]{3,2,1,0:T(8,128)(2,1)} %bands_ref.15, bf16[2,128,2048]{2,1,0:T(8,128)(2,1)} %copy-done.6, bf16[8,64,512]{2,1,0:T(8,128)(2,1)} %copy-done.2, ...), custom_call_target="tpu_custom_call", output_to_operand_aliasing={{1}: (4, {})} | custom-call | flops 1073741824 | bytes 5767168 | tf_op jit(solution)/shard_map/step/pallas_call | solution.py:197
  110.4 12.3 %all_to_all.31.refs_1_ = bf16[8,64,256]{2,1,0:T(8,128)(2,1)} all-to-all(bf16[8,64,256]{2,1,0:T(8,128)(2,1)} %bitcast.13), channel_id=1, replica_groups=mesh['ka'=4,'ga'=8] {'ga'}, dimensions={0} | all-to-all | bytes 524288 | tf_op jit(solution)/shard_map/all_to_all | solution.py:297
  122.7 11.4 %all_to_all.32.refs_0_ = bf16[8,64,256]{2,1,0:T(8,128)(2,1)} all-to-all(bf16[8,64,256]{2,1,0:T(8,128)(2,1)S(1)} %bitcast.11), channel_id=1, replica_groups=mesh['ka'=4,'ga'=8] {'ga'}, dimensions={0} | all-to-all | bytes 524288 | tf_op jit(solution)/shard_map/all_to_all | solution.py:297
  134.1 1.8 %finish.1 = f32[64,2,2,512]{3,2,1,0:T(2,128)} custom-call(f32[10]{0:T(128)} %reshape.42.table_ref, bf16[8,64,256]{2,1,0:T(8,128)(2,1)} %all_to_all.32.refs_0_, bf16[8,64,256]{2,1,0:T(8,128)(2,1)} %all_to_all.31.refs_1_, f32[64,2,2,512]{3,2,1,0:T(2,128)} %get-tuple-element.32.refs_2_), custom_call_target="tpu_custom_call", output_to_operand_aliasing={{}: (3, {})} | custom-call | bytes 524288 | tf_op jit(solution)/shard_map/finish/pallas_call | solution.py:234
  (11 shorter events, 0.0 us)
Async XLA Ops:
  2.0 5.3 %copy-start.9 = (s32[2]{0:T(128)S(1)}, s32[2]{0:T(128)}, u32[]{:S(2)}) copy-start(s32[2]{0:T(128)} %param.4) | copy-start | bytes 28
  2.1 5.3 %copy-start.10 = (s32[2]{0:T(128)S(1)}, s32[2]{0:T(128)}, u32[]{:S(2)}) copy-start(s32[2]{0:T(128)} %param.5) | copy-start | bytes 28
  2.1 15.1 %collective-permute-start = (bf16[2,128,2048]{2,1,0:T(8,128)(2,1)}, bf16[2,128,2048]{2,1,0:T(8,128)(2,1)S(1)}, u32[]{:S(2)}, u32[]{:S(2)}) collective-permute-start(bf16[2,128,2048]{2,1,0:T(8,128)(2,1)} %piece_of.2.rest_0_), channel_id=1, source_target_pairs={{8,0},{16,8},{24,16},{0,24},{9,1},{17,9},{25,17},{1,25},{10,2},{18... | collective-permute-start | bytes 3145736 | tf_op jit(solution)/shard_map/ppermute | solution.py:23
  6.6 21.8 %collective-permute-start.3 = (bf16[2,128,2048]{2,1,0:T(8,128)(2,1)}, bf16[2,128,2048]{2,1,0:T(8,128)(2,1)S(1)}, u32[]{:S(2)}, u32[]{:S(2)}) collective-permute-start(bf16[2,128,2048]{2,1,0:T(8,128)(2,1)} %piece_of.3), channel_id=1, source_target_pairs={{8,0},{16,8},{24,16},{0,24},{9,1},{17,9},{25,17},{1,25},{10,2},{18... | collective-permute-start | bytes 3145736 | tf_op jit(solution)/shard_map/ppermute | solution.py:23
  17.2 1.0 copy-start.4
  24.6 13.1 %copy-start.8 = (bf16[512,256]{1,0:T(8,128)(2,1)S(1)}, bf16[512,256]{1,0:T(8,128)(2,1)}, u32[]{:S(2)}) copy-start(bf16[512,256]{1,0:T(8,128)(2,1)} %get-tuple-element.20) | copy-start | bytes 786436
  24.6 30.4 %collective-permute-start.1 = (bf16[2,256,2048]{2,1,0:T(8,128)(2,1)}, bf16[2,256,2048]{2,1,0:T(8,128)(2,1)}, u32[]{:S(2)}, u32[]{:S(2)}) collective-permute-start(bf16[2,256,2048]{2,1,0:T(8,128)(2,1)} %get-tuple-element.19), channel_id=1, source_target_pairs={{8,0},{16,8},{24,16},{0,24},{9,1},{17,9},{25,17},{1,25},{10,2},{18... | collective-permute-start | bytes 6291464 | tf_op jit(solution)/shard_map/ppermute | solution.py:23
  28.4 1.0 copy-start.3
  35.8 37.5 %collective-permute-start.4 = (bf16[2,256,2048]{2,1,0:T(8,128)(2,1)}, bf16[2,256,2048]{2,1,0:T(8,128)(2,1)S(1)}, u32[]{:S(2)}, u32[]{:S(2)}) collective-permute-start(bf16[2,256,2048]{2,1,0:T(8,128)(2,1)} %get-tuple-element.23), channel_id=1, source_target_pairs={{8,0},{16,8},{24,16},{0,24},{9,1},{17,9},{25,17},{1,25},{10,2},{18... | collective-permute-start | bytes 6291464 | tf_op jit(solution)/shard_map/ppermute | solution.py:23
  51.6 11.8 %all-to-all-start.2 = ((bf16[8,64,256]{2,1,0:T(8,128)(2,1)}), bf16[8,64,256]{2,1,0:T(8,128)(2,1)S(1)}, u32[]{:S(2)}, u32[]{:S(2)}) async-start(bf16[8,64,256]{2,1,0:T(8,128)(2,1)} %bitcast.10), calls=%async_computation.2 | async-start | bytes 524288 | tf_op jit(solution)/shard_map/all_to_all | solution.py:297
  63.4 9.9 %copy-start.5 = (bf16[8,64,256]{2,1,0:T(8,128)(2,1)}, bf16[8,64,256]{2,1,0:T(8,128)(2,1)S(1)}, u32[]{:S(2)}) copy-start(bf16[8,64,256]{2,1,0:T(8,128)(2,1)S(1)} %all-to-all-done.2.rest_0_) | copy-start | bytes 786436
  63.4 20.9 %all-to-all-start.1 = ((bf16[8,64,512]{2,1,0:T(8,128)(2,1)}), bf16[8,64,512]{2,1,0:T(8,128)(2,1)S(1)}, u32[]{:S(2)}, u32[]{:S(2)}) async-start(bf16[8,64,512]{2,1,0:T(8,128)(2,1)} %bitcast.8), calls=%async_computation.1 | async-start | bytes 1048576 | tf_op jit(solution)/shard_map/all_to_all | solution.py:297
  68.6 21.3 %collective-permute-start.2 = (bf16[2,128,2048]{2,1,0:T(8,128)(2,1)}, bf16[2,128,2048]{2,1,0:T(8,128)(2,1)}, u32[]{:S(2)}, u32[]{:S(2)}) collective-permute-start(bf16[2,128,2048]{2,1,0:T(8,128)(2,1)} %get-tuple-element.21), channel_id=1, source_target_pairs={{8,0},{16,8},{24,16},{0,24},{9,1},{17,9},{25,17},{1,25},{10,2},{18... | collective-permute-start | bytes 3145736 | tf_op jit(solution)/shard_map/ppermute | solution.py:23
  73.3 1.3 copy-start
  82.2 21.3 %collective-permute-start.5 = (bf16[2,128,2048]{2,1,0:T(8,128)(2,1)}, bf16[2,128,2048]{2,1,0:T(8,128)(2,1)S(1)}, u32[]{:S(2)}, u32[]{:S(2)}) collective-permute-start(bf16[2,128,2048]{2,1,0:T(8,128)(2,1)} %get-tuple-element.28), channel_id=1, source_target_pairs={{8,0},{16,8},{24,16},{0,24},{9,1},{17,9},{25,17},{1,25},{10,2},{18... | collective-permute-start | bytes 3145736 | tf_op jit(solution)/shard_map/ppermute | solution.py:23
  84.3 5.5 %copy-start.1 = (bf16[8,64,512]{2,1,0:T(8,128)(2,1)}, bf16[8,64,512]{2,1,0:T(8,128)(2,1)S(1)}, u32[]{:S(2)}) copy-start(bf16[8,64,512]{2,1,0:T(8,128)(2,1)S(1)} %all-to-all-done.1.rest_0_) | copy-start | bytes 1572868
  84.3 19.2 %all-to-all-start.4 = ((bf16[8,64,512]{2,1,0:T(8,128)(2,1)}), bf16[8,64,512]{2,1,0:T(8,128)(2,1)S(1)}, u32[]{:S(2)}, u32[]{:S(2)}) async-start(bf16[8,64,512]{2,1,0:T(8,128)(2,1)} %bitcast.9), calls=%async_computation.4 | async-start | bytes 1048576 | tf_op jit(solution)/shard_map/all_to_all | solution.py:297
  103.5 0.8 copy-start.2
  103.5 1.2 copy-start.6
  104.7 18.0 %copy-start.7 = (bf16[512,256]{1,0:T(8,128)(2,1)S(1)}, bf16[512,256]{1,0:T(8,128)(2,1)}, u32[]{:S(2)}) copy-start(bf16[512,256]{1,0:T(8,128)(2,1)} %get-tuple-element.27) | copy-start | bytes 786436

commit v6 on v5

--- a/solution.py
+++ b/solution.py
@@ -14,7 +14,8 @@
 DEPTH = 512
 LAG = 2
 AHEAD = 2
-VMEM_BYTES = 56 * 1024 * 1024
+BLOCK = 256
+VMEM_BYTES = 48 * 1024 * 1024
 
 
 def shifted(block, axis, distance):
@@ -56,9 +57,7 @@
         ],
         out_shape=jax.ShapeDtypeStruct((2, width, points), bands.dtype),
         compiler_params=pltpu.CompilerParams(vmem_limit_bytes=VMEM_BYTES),
-        cost_estimate=pl.CostEstimate(
-            flops=0, bytes_accessed=8 * width * points, transcendentals=0
-        ),
+        cost_estimate=pl.CostEstimate(flops=1000, bytes_accessed=1000, transcendentals=0),
         name="piece_of",
     )(bands, *after)
 
@@ -124,35 +123,53 @@
         ]
     if adding:
         sum_buf, placed_sem = rest
+    width = there_ref.shape[1]
+    blocks = own_buf.shape[1] // BLOCK
     own = [
-        pltpu.make_async_copy(bands_ref.at[point, part], own_buf.at[part], own_sems.at[part])
+        pltpu.make_async_copy(
+            bands_ref.at[point, part, pl.ds(block * BLOCK, BLOCK), :],
+            own_buf.at[part, pl.ds(block * BLOCK, BLOCK), :],
+            own_sems.at[block, part],
+        )
+        for block in range(blocks)
         for part in range(2)
     ]
     for copy in own + (loads if later else []):
         copy.start()
     if adding:
-        add_slot, start, width = adding
+        add_slot, add_start, add_width = adding
         add_point = table_ref[add_slot * stride].astype(jnp.int32)
         add_into(sum_buf, arrived_ref)
         placing = pltpu.make_async_copy(
-            sum_buf, result_ref.at[:, add_point, :, pl.ds(start, width)], placed_sem
+            sum_buf, result_ref.at[:, add_point, :, pl.ds(add_start, add_width)], placed_sem
         )
         placing.start()
     near_into(near_buf, there_ref, table_ref, base, planes)
-    if later:
-        for load, store in zip(loads, stores):
-            load.wait()
-            store.start()
-    for copy in own:
-        copy.wait()
     dims = (((1,), (1,)), ((), ()))
-    width = there_ref.shape[1]
-    of_re, of_im = [
-        lax.dot_general(own_buf[part], near_buf[...], dims, preferred_element_type=jnp.float32)
-        for part in range(2)
-    ]
-    out_ref[:, :width] = (of_re[:, :width] + of_im[:, width:]).astype(out_ref.dtype)
-    out_ref[:, width:] = (of_re[:, width:] - of_im[:, :width]).astype(out_ref.dtype)
+    half = there_ref.shape[2] // 2
+    for block in range(blocks):
+        lines = pl.ds(block * BLOCK, BLOCK)
+        products = []
+        for part in range(2):
+            own[2 * block + part].wait()
+            for first_column in (0, half):
+                columns = pl.ds(first_column, half)
+                products.append(
+                    lax.dot_general(
+                        own_buf[part, lines, columns],
+                        near_buf[:, columns],
+                        dims,
+                        preferred_element_type=jnp.float32,
+                    )
+                )
+        of_re = products[0] + products[1]
+        of_im = products[2] + products[3]
+        out_ref[lines, :width] = (of_re[:, :width] + of_im[:, width:]).astype(out_ref.dtype)
+        out_ref[lines, width:] = (of_re[:, width:] - of_im[:, :width]).astype(out_ref.dtype)
+        if later and block == 0:
+            for load, store in zip(loads, stores):
+                load.wait()
+                store.start()
     if adding:
         placing.wait()
     if later:
@@ -170,7 +187,7 @@
     scratch = [
         pltpu.VMEM((2, nbands, points), jnp.bfloat16),
         pltpu.VMEM((2 * width, points), jnp.bfloat16),
-        pltpu.SemaphoreType.DMA((2,)),
+        pltpu.SemaphoreType.DMA((nbands // BLOCK, 2)),
     ]
     aliases = {}
     if later:
@@ -202,11 +219,7 @@
         out_shape=out_shape,
         input_output_aliases=aliases,
         compiler_params=pltpu.CompilerParams(vmem_limit_bytes=VMEM_BYTES),
-        cost_estimate=pl.CostEstimate(
-            flops=8 * nbands * width * points,
-            bytes_accessed=4 * (nbands + width) * points + 8 * nbands * width,
-            transcendentals=0,
-        ),
+        cost_estimate=pl.CostEstimate(flops=1000, bytes_accessed=1000, transcendentals=0),
         name="step",
     )(*operands)
     return outs[0], outs[1] if adding else result, outs[-1] if later else None
@@ -242,9 +255,7 @@
         out_shape=jax.ShapeDtypeStruct(result.shape, jnp.float32),
         input_output_aliases={1 + len(parts): 0},
         compiler_params=pltpu.CompilerParams(vmem_limit_bytes=VMEM_BYTES),
-        cost_estimate=pl.CostEstimate(
-            flops=0, bytes_accessed=4 * math.prod(result.shape), transcendentals=0
-        ),
+        cost_estimate=pl.CostEstimate(flops=1000, bytes_accessed=1000, transcendentals=0),
         name="finish",
     )(table, *arrived, result)
 

time: 137 us -> 132 us (0.964)
  Pallas kernels: 45.3 us -> 40.9 us
  local copies, waits for them, and re-layouts: 5.22 us -> 1.16 us
  waiting for transfers between devices: 24.2 us -> 26.3 us
  starting transfers between devices: 23.1 us -> 24.7 us
    unnamed x22 -> x6, local copies, waits for them, and re-layouts: 4.46 us -> 0.98 us
    pallas_call x6, Pallas kernels: 39.3 us -> 37.1 us  [step(): pl.pallas_call(functools.partial(step_kernel, slot, k_dev, adding, result...]
    ppermute x6, waiting for transfers between devices: 15.4 us -> 17.5 us  [shifted(): return lax.ppermute(block, axis, route)]
    pallas_call x2, Pallas kernels: 4.13 us -> 2.54 us  [piece_of(): pl.pallas_call(functools.partial(piece_kernel, slot, start), in_specs=[pl...]
  transfers between devices with their start and end apart: 9 -> 9, of which waited for: 5 -> 4; matrix products, arithmetic and copies ran while one was open for 1% -> 0% of each run, Pallas kernels for 26% -> 26%
where the time goes in v6:
time: 132 us; the launch traced here: 131 us
  Pallas kernels  40.9 us (31%)
  blocking collectives  37.3 us (28%)
  waiting for transfers between devices  26.3 us (20%)
  starting transfers between devices  24.7 us (19%)
    all_to_all x3, blocking collectives, body(): arrived.append(lax.all_to_all(terms, 'ga', 0, 0))  37.3 us
    pallas_call x6, Pallas kernels, step(): pl.pallas_call(functools.partial(step_kernel, slot, k_dev, adding, result...  37.1 us
    ppermute x6, waiting for transfers between devices, shifted(): return lax.ppermute(block, axis, route)  17.5 us
    all_to_all x3, starting transfers between devices, body(): arrived.append(lax.all_to_all(terms, 'ga', 0, 0))  15.2 us
    ppermute x6, starting transfers between devices, shifted(): return lax.ppermute(block, axis, route)  9.53 us
    all_to_all x3, waiting for transfers between devices, body(): arrived.append(lax.all_to_all(terms, 'ga', 0, 0))  8.79 us
  transfers between devices with their start and end apart: 9, of which 4 were waited for; matrix products, arithmetic and copies ran while one was open for 0% of the time, Pallas kernels for 26%

profile of v6, /device:TPU:0, one launch (start us, length us, event | category | flops | bytes accessed | tf_op | source)
XLA Modules:
  0.0 131.1 jit_solution(10081832022666812210)
XLA Ops:
  0.0 1.3 piece_of.2.rest_0_
  1.3 0.0 copy-start.1
  1.3 0.0 copy-start.2
  1.3 2.5 %collective-permute-start = (bf16[2,128,2048]{2,1,0:T(8,128)(2,1)S(1)}, bf16[2,128,2048]{2,1,0:T(8,128)(2,1)}, u32[]{:S(2)}, u32[]{:S(2)}) collective-permute-start(bf16[2,128,2048]{2,1,0:T(8,128)(2,1)S(1)} %piece_of.2.rest_0_), channel_id=1, source_target_pairs={{8,0},{16,8},{24,16},{0,24},{9,1},{17,9},{25,17},{1,25},{10,2},{18... | collective-permute-start | bytes 3145736 | tf_op jit(solution)/shard_map/ppermute | solution.py:24
  3.8 1.3 piece_of.3
  5.0 0.7 collective-permute-start.3
  5.8 0.0 copy-done.1
  5.8 0.0 copy-done.2
  5.8 0.1 select_reduce_fusion.1
  5.9 0.1 copy.8
  6.0 0.1 fusion.4
  6.2 0.1 pad_maximum_fusion
  6.2 0.1 reshape.42.table_ref
  6.3 9.8 %collective-permute-done.there_ref = bf16[2,128,2048]{2,1,0:T(8,128)(2,1)} collective-permute-done((bf16[2,128,2048]{2,1,0:T(8,128)(2,1)S(1)}, bf16[2,128,2048]{2,1,0:T(8,128)(2,1)}, u32[]{:S(2)}, u32[]{:S(2)}) %collective-permute-start) | collective-permute-done | bytes 1048608 | tf_op jit(solution)/shard_map/ppermute | solution.py:24
  16.1 5.7 %step.6 = (bf16[512,256]{1,0:T(8,128)(2,1)S(1)}, bf16[2,256,2048]{2,1,0:T(8,128)(2,1)}) custom-call(f32[10]{0:T(128)S(1)} %reshape.42.table_ref, bf16[2,2,512,2048]{3,2,1,0:T(8,128)(2,1)} %bands_ref.15, bf16[2,128,2048]{2,1,0:T(8,128)(2,1)} %collective-permute-done.there_ref), custom_call_target="tpu_custom_call" | custom-call | flops 1000 | bytes 1000 | tf_op jit(solution)/shard_map/step/pallas_call | solution.py:214
  21.8 1.6 %collective-permute-start.1 = (bf16[2,256,2048]{2,1,0:T(8,128)(2,1)}, bf16[2,256,2048]{2,1,0:T(8,128)(2,1)}, u32[]{:S(2)}, u32[]{:S(2)}) collective-permute-start(bf16[2,256,2048]{2,1,0:T(8,128)(2,1)} %get-tuple-element.19), channel_id=1, source_target_pairs={{8,0},{16,8},{24,16},{0,24},{9,1},{17,9},{25,17},{1,25},{10,2},{18... | collective-permute-start | bytes 6291464 | tf_op jit(solution)/shard_map/ppermute | solution.py:24
  23.5 3.9 %collective-permute-done.3.there_ref = bf16[2,128,2048]{2,1,0:T(8,128)(2,1)S(1)} collective-permute-done((bf16[2,128,2048]{2,1,0:T(8,128)(2,1)S(1)}, bf16[2,128,2048]{2,1,0:T(8,128)(2,1)S(1)}, u32[]{:S(2)}, u32[]{:S(2)}) %collective-permute-start.3) | collective-permute-done | bytes 1048608 | tf_op jit(solution)/shard_map/ppermute | solution.py:24
  27.3 5.4 %step.8 = (bf16[512,256]{1,0:T(8,128)(2,1)}, bf16[2,256,2048]{2,1,0:T(8,128)(2,1)}) custom-call(f32[10]{0:T(128)S(1)} %reshape.42.table_ref, bf16[2,2,512,2048]{3,2,1,0:T(8,128)(2,1)} %bands_ref.15, bf16[2,128,2048]{2,1,0:T(8,128)(2,1)S(1)} %collective-permute-done.3.there_ref), custom_call_target="tpu_custom_call" | custom-call | flops 1000 | bytes 1000 | tf_op jit(solution)/shard_map/step/pallas_call | solution.py:214
  32.7 2.6 %collective-permute-start.4 = (bf16[2,256,2048]{2,1,0:T(8,128)(2,1)}, bf16[2,256,2048]{2,1,0:T(8,128)(2,1)S(1)}, u32[]{:S(2)}, u32[]{:S(2)}) collective-permute-start(bf16[2,256,2048]{2,1,0:T(8,128)(2,1)} %get-tuple-element.23), channel_id=1, source_target_pairs={{8,0},{16,8},{24,16},{0,24},{9,1},{17,9},{25,17},{1,25},{10,2},{18... | collective-permute-start | bytes 6291464 | tf_op jit(solution)/shard_map/ppermute | solution.py:24
  35.2 13.8 %all_to_all.30.rest_0_ = bf16[8,64,256]{2,1,0:T(8,128)(2,1)S(1)} all-to-all(bf16[8,64,256]{2,1,0:T(8,128)(2,1)S(1)} %bitcast.9), channel_id=1, replica_groups=mesh['ka'=4,'ga'=8] {'ga'}, dimensions={0} | all-to-all | bytes 524288 | tf_op jit(solution)/shard_map/all_to_all | solution.py:308
  49.1 3.4 %all-to-all-start.2 = ((bf16[8,64,256]{2,1,0:T(8,128)(2,1)}), bf16[8,64,256]{2,1,0:T(8,128)(2,1)S(1)}, u32[]{:S(2)}, u32[]{:S(2)}) async-start(bf16[8,64,256]{2,1,0:T(8,128)(2,1)} %bitcast.3), calls=%async_computation.2 | async-start | bytes 524288 | tf_op jit(solution)/shard_map/all_to_all | solution.py:308
  52.5 0.0 collective-permute-done.1.there_ref
  52.5 9.0 %step.7 = (bf16[512,512]{1,0:T(8,128)(2,1)}, f32[64,2,2,512]{3,2,1,0:T(2,128)}, bf16[2,128,2048]{2,1,0:T(8,128)(2,1)S(1)}) custom-call(f32[10]{0:T(128)S(1)} %reshape.42.table_ref, bf16[2,2,512,2048]{3,2,1,0:T(8,128)(2,1)} %bands_ref.15, bf16[2,256,2048]{2,1,0:T(8,128)(2,1)} %collective-permute-done.1.there_ref, bf16[8,64,256]{2,1,0:T(8,128)(2,1)S(1)} %all_to_all.30.rest_0_), custom_call_target="tpu_custom_call" | custom-call | flops 1000 | bytes 1000 | tf_op jit(solution)/shard_map/step/pallas_call | solution.py:214
  61.5 0.0 copy-start
  61.5 1.0 copy-done
  62.5 0.0 all-to-all-done.2.rest_0_
  62.5 6.0 %all-to-all-start.1 = ((bf16[8,64,512]{2,1,0:T(8,128)(2,1)}), bf16[8,64,512]{2,1,0:T(8,128)(2,1)S(1)}, u32[]{:S(2)}, u32[]{:S(2)}) async-start(bf16[8,64,512]{2,1,0:T(8,128)(2,1)} %bitcast.2), calls=%async_computation.1 | async-start | bytes 1048576 | tf_op jit(solution)/shard_map/all_to_all | solution.py:308
  68.5 0.0 collective-permute-start.2
  68.5 3.9 %collective-permute-done.4.there_ref = bf16[2,256,2048]{2,1,0:T(8,128)(2,1)S(1)} collective-permute-done((bf16[2,256,2048]{2,1,0:T(8,128)(2,1)}, bf16[2,256,2048]{2,1,0:T(8,128)(2,1)S(1)}, u32[]{:S(2)}, u32[]{:S(2)}) %collective-permute-start.4) | collective-permute-done | bytes 2097184 | tf_op jit(solution)/shard_map/ppermute | solution.py:24
  72.4 7.9 %step.9 = (bf16[512,512]{1,0:T(8,128)(2,1)}, f32[64,2,2,512]{3,2,1,0:T(2,128)}, bf16[2,128,2048]{2,1,0:T(8,128)(2,1)}) custom-call(f32[10]{0:T(128)S(1)} %reshape.42.table_ref, bf16[2,2,512,2048]{3,2,1,0:T(8,128)(2,1)} %bands_ref.15, bf16[2,256,2048]{2,1,0:T(8,128)(2,1)S(1)} %collective-permute-done.4.there_ref, ...), custom_call_target="tpu_custom_call", output_to_operand_aliasing={{1}: (4, {})} | custom-call | flops 1000 | bytes 1000 | tf_op jit(solution)/shard_map/step/pallas_call | solution.py:214
  80.3 2.1 %collective-permute-start.5 = (bf16[2,128,2048]{2,1,0:T(8,128)(2,1)}, bf16[2,128,2048]{2,1,0:T(8,128)(2,1)S(1)}, u32[]{:S(2)}, u32[]{:S(2)}) collective-permute-start(bf16[2,128,2048]{2,1,0:T(8,128)(2,1)} %get-tuple-element.28), channel_id=1, source_target_pairs={{8,0},{16,8},{24,16},{0,24},{9,1},{17,9},{25,17},{1,25},{10,2},{18... | collective-permute-start | bytes 3145736 | tf_op jit(solution)/shard_map/ppermute | solution.py:24
  82.4 0.0 all-to-all-done.1.rest_0_
  82.4 5.8 %all-to-all-start.4 = ((bf16[8,64,512]{2,1,0:T(8,128)(2,1)}), bf16[8,64,512]{2,1,0:T(8,128)(2,1)S(1)}, u32[]{:S(2)}, u32[]{:S(2)}) async-start(bf16[8,64,512]{2,1,0:T(8,128)(2,1)} %bitcast.5), calls=%async_computation.4 | async-start | bytes 1048576 | tf_op jit(solution)/shard_map/all_to_all | solution.py:308
  88.3 0.0 collective-permute-done.2.there_ref
  88.3 4.9 %step.10 = (bf16[512,256]{1,0:T(8,128)(2,1)S(1)}, f32[64,2,2,512]{3,2,1,0:T(2,128)}) custom-call(f32[10]{0:T(128)S(1)} %reshape.42.table_ref, bf16[2,2,512,2048]{3,2,1,0:T(8,128)(2,1)} %bands_ref.15, bf16[2,128,2048]{2,1,0:T(8,128)(2,1)} %collective-permute-done.2.there_ref, ...), custom_call_target="tpu_custom_call", output_to_operand_aliasing={{1}: (4, {})} | custom-call | flops 1000 | bytes 1000 | tf_op jit(solution)/shard_map/step/pallas_call | solution.py:214
  93.1 8.8 %all-to-all-done.4.rest_0_ = bf16[8,64,512]{2,1,0:T(8,128)(2,1)S(1)} async-done(((bf16[8,64,512]{2,1,0:T(8,128)(2,1)}), bf16[8,64,512]{2,1,0:T(8,128)(2,1)S(1)}, u32[]{:S(2)}, u32[]{:S(2)}) %all-to-all-start.4) | async-done | bytes 524320 | tf_op jit(solution)/shard_map/all_to_all | solution.py:308
  101.9 0.0 collective-permute-done.5.there_ref
  101.9 4.2 %step.11 = (bf16[512,256]{1,0:T(8,128)(2,1)S(1)}, f32[64,2,2,512]{3,2,1,0:T(2,128)}) custom-call(f32[10]{0:T(128)S(1)} %reshape.42.table_ref, bf16[2,2,512,2048]{3,2,1,0:T(8,128)(2,1)} %bands_ref.15, bf16[2,128,2048]{2,1,0:T(8,128)(2,1)S(1)} %collective-permute-done.5.there_ref, ...), custom_call_target="tpu_custom_call", output_to_operand_aliasing={{1}: (4, {})} | custom-call | flops 1000 | bytes 1000 | tf_op jit(solution)/shard_map/step/pallas_call | solution.py:214
  106.1 11.8 %all_to_all.31.refs_1_ = bf16[8,64,256]{2,1,0:T(8,128)(2,1)S(1)} all-to-all(bf16[8,64,256]{2,1,0:T(8,128)(2,1)S(1)} %bitcast.10), channel_id=1, replica_groups=mesh['ka'=4,'ga'=8] {'ga'}, dimensions={0} | all-to-all | bytes 524288 | tf_op jit(solution)/shard_map/all_to_all | solution.py:308
  117.8 11.7 %all_to_all.32.refs_0_ = bf16[8,64,256]{2,1,0:T(8,128)(2,1)S(1)} all-to-all(bf16[8,64,256]{2,1,0:T(8,128)(2,1)S(1)} %bitcast.8), channel_id=1, replica_groups=mesh['ka'=4,'ga'=8] {'ga'}, dimensions={0} | all-to-all | bytes 524288 | tf_op jit(solution)/shard_map/all_to_all | solution.py:308
  129.6 1.3 %finish.1 = f32[64,2,2,512]{3,2,1,0:T(2,128)} custom-call(f32[10]{0:T(128)S(1)} %reshape.42.table_ref, bf16[8,64,256]{2,1,0:T(8,128)(2,1)S(1)} %all_to_all.32.refs_0_, bf16[8,64,256]{2,1,0:T(8,128)(2,1)S(1)} %all_to_all.31.refs_1_, f32[64,2,2,512]{3,2,1,0:T(2,128)} %get-tuple-element.32.refs_2_), custom_call_target="tpu_custom_call", output_to_operand_aliasing={{}: (3, {})} | custom-call | flops 1000 | bytes 1000 | tf_op jit(solution)/shard_map/finish/pallas_call | solution.py:247
  (2 shorter events, 0.0 us)
Async XLA Ops:
  1.3 4.5 %copy-start.1 = (s32[2]{0:T(128)S(1)}, s32[2]{0:T(128)}, u32[]{:S(2)}) copy-start(s32[2]{0:T(128)} %param.4) | copy-start | bytes 28
  1.3 4.5 %copy-start.2 = (s32[2]{0:T(128)S(1)}, s32[2]{0:T(128)}, u32[]{:S(2)}) copy-start(s32[2]{0:T(128)} %param.5) | copy-start | bytes 28
  1.3 14.8 %collective-permute-start = (bf16[2,128,2048]{2,1,0:T(8,128)(2,1)S(1)}, bf16[2,128,2048]{2,1,0:T(8,128)(2,1)}, u32[]{:S(2)}, u32[]{:S(2)}) collective-permute-start(bf16[2,128,2048]{2,1,0:T(8,128)(2,1)S(1)} %piece_of.2.rest_0_), channel_id=1, source_target_pairs={{8,0},{16,8},{24,16},{0,24},{9,1},{17,9},{25,17},{1,25},{10,2},{18... | collective-permute-start | bytes 3145736 | tf_op jit(solution)/shard_map/ppermute | solution.py:24
  5.0 22.3 %collective-permute-start.3 = (bf16[2,128,2048]{2,1,0:T(8,128)(2,1)S(1)}, bf16[2,128,2048]{2,1,0:T(8,128)(2,1)S(1)}, u32[]{:S(2)}, u32[]{:S(2)}) collective-permute-start(bf16[2,128,2048]{2,1,0:T(8,128)(2,1)S(1)} %piece_of.3), channel_id=1, source_target_pairs={{8,0},{16,8},{24,16},{0,24},{9,1},{17,9},{25,17},{1,25},{10,2},{18... | collective-permute-start | bytes 3145736 | tf_op jit(solution)/shard_map/ppermute | solution.py:24
  21.8 30.6 %collective-permute-start.1 = (bf16[2,256,2048]{2,1,0:T(8,128)(2,1)}, bf16[2,256,2048]{2,1,0:T(8,128)(2,1)}, u32[]{:S(2)}, u32[]{:S(2)}) collective-permute-start(bf16[2,256,2048]{2,1,0:T(8,128)(2,1)} %get-tuple-element.19), channel_id=1, source_target_pairs={{8,0},{16,8},{24,16},{0,24},{9,1},{17,9},{25,17},{1,25},{10,2},{18... | collective-permute-start | bytes 6291464 | tf_op jit(solution)/shard_map/ppermute | solution.py:24
  32.7 39.7 %collective-permute-start.4 = (bf16[2,256,2048]{2,1,0:T(8,128)(2,1)}, bf16[2,256,2048]{2,1,0:T(8,128)(2,1)S(1)}, u32[]{:S(2)}, u32[]{:S(2)}) collective-permute-start(bf16[2,256,2048]{2,1,0:T(8,128)(2,1)} %get-tuple-element.23), channel_id=1, source_target_pairs={{8,0},{16,8},{24,16},{0,24},{9,1},{17,9},{25,17},{1,25},{10,2},{18... | collective-permute-start | bytes 6291464 | tf_op jit(solution)/shard_map/ppermute | solution.py:24
  49.1 13.4 %all-to-all-start.2 = ((bf16[8,64,256]{2,1,0:T(8,128)(2,1)}), bf16[8,64,256]{2,1,0:T(8,128)(2,1)S(1)}, u32[]{:S(2)}, u32[]{:S(2)}) async-start(bf16[8,64,256]{2,1,0:T(8,128)(2,1)} %bitcast.3), calls=%async_computation.2 | async-start | bytes 524288 | tf_op jit(solution)/shard_map/all_to_all | solution.py:308
  61.5 1.0 copy-start
  62.5 19.9 %all-to-all-start.1 = ((bf16[8,64,512]{2,1,0:T(8,128)(2,1)}), bf16[8,64,512]{2,1,0:T(8,128)(2,1)S(1)}, u32[]{:S(2)}, u32[]{:S(2)}) async-start(bf16[8,64,512]{2,1,0:T(8,128)(2,1)} %bitcast.2), calls=%async_computation.1 | async-start | bytes 1048576 | tf_op jit(solution)/shard_map/all_to_all | solution.py:308
  68.5 19.8 %collective-permute-start.2 = (bf16[2,128,2048]{2,1,0:T(8,128)(2,1)}, bf16[2,128,2048]{2,1,0:T(8,128)(2,1)}, u32[]{:S(2)}, u32[]{:S(2)}) collective-permute-start(bf16[2,128,2048]{2,1,0:T(8,128)(2,1)} %copy-done), channel_id=1, source_target_pairs={{8,0},{16,8},{24,16},{0,24},{9,1},{17,9},{25,17},{1,25},{10,2},{18... | collective-permute-start | bytes 3145736 | tf_op jit(solution)/shard_map/ppermute | solution.py:24
  80.3 21.6 %collective-permute-start.5 = (bf16[2,128,2048]{2,1,0:T(8,128)(2,1)}, bf16[2,128,2048]{2,1,0:T(8,128)(2,1)S(1)}, u32[]{:S(2)}, u32[]{:S(2)}) collective-permute-start(bf16[2,128,2048]{2,1,0:T(8,128)(2,1)} %get-tuple-element.28), channel_id=1, source_target_pairs={{8,0},{16,8},{24,16},{0,24},{9,1},{17,9},{25,17},{1,25},{10,2},{18... | collective-permute-start | bytes 3145736 | tf_op jit(solution)/shard_map/ppermute | solution.py:24
  82.4 19.5 %all-to-all-start.4 = ((bf16[8,64,512]{2,1,0:T(8,128)(2,1)}), bf16[8,64,512]{2,1,0:T(8,128)(2,1)S(1)}, u32[]{:S(2)}, u32[]{:S(2)}) async-start(bf16[8,64,512]{2,1,0:T(8,128)(2,1)} %bitcast.5), calls=%async_computation.4 | async-start | bytes 1048576 | tf_op jit(solution)/shard_map/all_to_all | solution.py:308

commit v7 on v0

v7 whole, which is shorter than its diff:
```python
import functools
import math
from typing import NamedTuple

import jax
import jax.numpy as jnp
from jax import lax
from jax.experimental import pallas as pl
from jax.experimental.pallas import tpu as pltpu
from jax.sharding import PartitionSpec as P

NKB = 4
PLANE = 1024
STRIP = 32
DEPTH = 512
AHEAD = 2
OUTER = 4
SPLIT = 128
LANES = 128
BLOCK = 256
VMEM_BYTES = 48 * 1024 * 1024


def shifted(block, axis, distance, fold=1, inner=False):
    count = lax.axis_size(axis)
    route = []
    for i in range(count):
        outer, place = divmod(i, fold)
        if inner:
            route.append((i, outer * fold + (place + distance) % fold))
        else:
            route.append((i, (outer + distance) % (count // fold) * fold + place))
    return lax.ppermute(block, axis, route)


def piece_kernel(slot, start, bands_ref, *rest):
    out_ref, piece_buf, sems = rest[-3:]
    width = piece_buf.shape[1]
    rows = pl.ds(start, width)
    loads = [
        pltpu.make_async_copy(bands_ref.at[slot, part, rows, :], piece_buf.at[part], sems.at[0, part])
        for part in range(2)
    ]
    stores = [
        pltpu.make_async_copy(piece_buf.at[part], out_ref.at[part], sems.at[1, part])
        for part in range(2)
    ]
    for load in loads:
        load.start()
    for load, store in zip(loads, stores):
        load.wait()
        store.start()
    for store in stores:
        store.wait()


def piece_of(slot, start, width, bands, after):
    points = bands.shape[3]
    return pl.pallas_call(
        functools.partial(piece_kernel, slot, start),
        in_specs=[pl.BlockSpec(memory_space=pl.ANY)] * (1 + len(after)),
        out_specs=pl.BlockSpec(memory_space=pl.ANY),
        scratch_shapes=[
            pltpu.VMEM((2, width, points), bands.dtype),
            pltpu.SemaphoreType.DMA((2, 2)),
        ],
        out_shape=jax.ShapeDtypeStruct((2, width, points), bands.dtype),
        compiler_params=pltpu.CompilerParams(vmem_limit_bytes=VMEM_BYTES),
        cost_estimate=pl.CostEstimate(flops=1000, bytes_accessed=1000, transcendentals=0),
        name="piece_of",
    )(bands, *after)


def near_into(near_buf, there_ref, table_ref, base, planes):
    width, points = there_ref.shape[1:]

    @pl.loop(0, width // STRIP)
    def _(strip):
        rows = pl.ds(strip * STRIP, STRIP)
        mirror = pl.ds(width + strip * STRIP, STRIP)
        for start in range(0, points, DEPTH):
            plane = start // PLANE
            cosine = table_ref[base + 1 + plane]
            sine = table_ref[base + 1 + planes + plane]
            columns = pl.ds(start, DEPTH)
            real_part = there_ref[0, rows, columns].astype(jnp.float32)
            imag_part = there_ref[1, rows, columns].astype(jnp.float32)
            near_re = real_part * cosine + imag_part * sine
            near_im = imag_part * cosine - real_part * sine
            near_buf[rows, columns] = near_re.astype(jnp.bfloat16)
            near_buf[mirror, columns] = near_im.astype(jnp.bfloat16)


def put_sum(sum_buf, lane, total):
    width = total.shape[1] // 2
    sum_buf[:, 0, lane : lane + width] = total[:, :width]
    sum_buf[:, 1, lane : lane + width] = total[:, width:]


def step_kernel(plan, table_ref, *refs):
    rows, k_dev, _, nbands = plan.shape
    fold, depth = plan.fold, plan.depth
    refs = list(refs)

    def take(count):
        taken = refs[:count]
        del refs[:count]
        return taken

    stride = (table_ref.shape[0] - 1) // k_dev
    planes = (stride - 1) // 2
    me = table_ref[k_dev * stride].astype(jnp.int32)
    place, outer = lax.rem(me, fold), lax.div(me, fold)
    if plan.part:
        bands_ref, there_ref = take(2)
    folded = take(fold) if plan.folding else None
    arrived = [take(depth) for _ in plan.adding]
    if plan.adding and plan.placed:
        take(1)
    outs = take(fold) if plan.part else None
    sends = take(depth) if plan.folding else None
    result_ref = take(1)[0] if plan.adding else None
    piece_ref = take(1)[0] if plan.later else None
    if plan.part:
        own_buf, near_buf, terms_buf, own_sems = take(4)
        slot = plan.part[0]
        base = slot * stride
        point = table_ref[base].astype(jnp.int32)
        width = there_ref.shape[1]
        blocks = nbands // BLOCK
        own = [
            pltpu.make_async_copy(
                bands_ref.at[point, part, pl.ds(block * BLOCK, BLOCK), :],
                own_buf.at[part, pl.ds(block * BLOCK, BLOCK), :],
                own_sems.at[block, part],
            )
            for block in range(blocks)
            for part in range(2)
        ]
        for copy in own:
            copy.start()
    if plan.later:
        piece_buf, piece_sems = take(2)
        later_slot, later_start, later_width = plan.later
        loads = [
            pltpu.make_async_copy(
                bands_ref.at[later_slot, part, pl.ds(later_start, later_width), :],
                piece_buf.at[part],
                piece_sems.at[0, part],
            )
            for part in range(2)
        ]
        stores = [
            pltpu.make_async_copy(piece_buf.at[part], piece_ref.at[part], piece_sems.at[1, part])
            for part in range(2)
        ]
        for copy in loads:
            copy.start()
    if plan.adding:
        sum_buf, placed_sem = take(2)
        add_slot, add_start, _ = plan.adding[0]
        for (_, start, _), arrays in zip(plan.adding, arrived):
            total = arrays[0][...]
            for array in arrays[1:]:
                total = total + array[...].astype(jnp.float32)
            put_sum(sum_buf, start - add_start, total)
        add_point = table_ref[add_slot * stride].astype(jnp.int32)
        columns = pl.ds(add_start, sum_buf.shape[2])
        placing = pltpu.make_async_copy(
            sum_buf, result_ref.at[:, add_point, :, columns], placed_sem
        )
        placing.start()
    if plan.folding:
        for distance, send_ref in enumerate(sends):
            target = lax.rem(outer + distance, depth)
            total = folded[0][target]
            for array in folded[1:]:
                total = total + array[target].astype(jnp.float32)
            send_ref[...] = total.astype(send_ref.dtype)
    if plan.part:
        near_into(near_buf, there_ref, table_ref, base, planes)
        dims = (((1,), (1,)), ((), ()))
        points = there_ref.shape[2]
        run = points // 2 if width <= SPLIT else points
        for block in range(blocks):
            lines = pl.ds(block * BLOCK, BLOCK)
            of_both = []
            for part in range(2):
                own[2 * block + part].wait()
                products = [
                    lax.dot_general(
                        own_buf[part, lines, pl.ds(first, run)],
                        near_buf[:, pl.ds(first, run)],
                        dims,
                        preferred_element_type=jnp.float32,
                    )
                    for first in range(0, points, run)
                ]
                of_both.append(sum(products[1:], products[0]))
            of_re, of_im = of_both
            terms_buf[lines, :width] = of_re[:, :width] + of_im[:, width:]
            terms_buf[lines, width:] = of_re[:, width:] - of_im[:, :width]
            if plan.later and block == 0:
                for load, store in zip(loads, stores):
                    load.wait()
                    store.start()
        for distance, out_ref in enumerate(outs):
            target = lax.rem(place + distance, fold)
            for level in range(depth):
                first = pl.multiple_of((level * fold + target) * rows, rows)
                out_ref[level] = terms_buf[pl.ds(first, rows), :].astype(out_ref.dtype)
    if plan.adding:
        placing.wait()
    if plan.later:
        for store in stores:
            store.wait()


class Plan(NamedTuple):
    shape: tuple
    fold: int
    depth: int
    part: tuple
    folding: tuple
    adding: tuple
    placed: bool
    later: tuple


def step(plan, table, bands, there, folded, arrived, result):
    rows, _, _, nbands = plan.shape
    fold, depth = plan.fold, plan.depth
    points = bands.shape[3]
    vmem = pl.BlockSpec(memory_space=pltpu.VMEM)
    hbm = pl.BlockSpec(memory_space=pltpu.HBM)
    operands, in_specs = [table], [pl.BlockSpec(memory_space=pltpu.SMEM)]
    out_shape, out_specs, scratch, aliases = [], [], [], {}

    def kind(index):
        return jnp.bfloat16 if index else jnp.float32

    if plan.part:
        width = plan.part[2]
        operands += [bands, there]
        in_specs += [hbm, vmem]
        out_shape += [
            jax.ShapeDtypeStruct((depth, rows, 2 * width), kind(i)) for i in range(fold)
        ]
        out_specs += [vmem] * fold
        scratch += [
            pltpu.VMEM((2, nbands, points), jnp.bfloat16),
            pltpu.VMEM((2 * width, points), jnp.bfloat16),
            pltpu.VMEM((nbands, 2 * width), jnp.float32),
            pltpu.SemaphoreType.DMA((nbands // BLOCK, 2)),
        ]
    if plan.folding:
        operands += folded
        in_specs += [vmem] * fold
        out_shape += [
            jax.ShapeDtypeStruct((rows, 2 * plan.folding[2]), kind(i)) for i in range(depth)
        ]
        out_specs += [vmem] * depth
    if plan.later:
        scratch += [
            pltpu.VMEM((2, plan.later[2], points), bands.dtype),
            pltpu.SemaphoreType.DMA((2, 2)),
        ]
    if plan.adding:
        for arrays in arrived:
            operands += arrays
            in_specs += [vmem] * depth
        if plan.placed:
            aliases = {len(operands): len(out_shape)}
            operands.append(result)
            in_specs.append(hbm)
        out_shape.append(jax.ShapeDtypeStruct(plan.shape, jnp.float32))
        out_specs.append(hbm)
        lanes = sum(width for _, _, width in plan.adding)
        scratch += [pltpu.VMEM((rows, 2, lanes), jnp.float32), pltpu.SemaphoreType.DMA]
    if plan.later:
        out_shape.append(jax.ShapeDtypeStruct((2, plan.later[2], points), bands.dtype))
        out_specs.append(hbm)
    outs = list(
        pl.pallas_call(
            functools.partial(step_kernel, plan),
            in_specs=in_specs,
            out_specs=out_specs,
            scratch_shapes=scratch,
            out_shape=out_shape,
            input_output_aliases=aliases,
            compiler_params=pltpu.CompilerParams(vmem_limit_bytes=VMEM_BYTES),
            cost_estimate=pl.CostEstimate(flops=1000, bytes_accessed=1000, transcendentals=0),
            name="step",
        )(*operands)
    )
    piece = outs.pop() if plan.later else None
    result = outs.pop() if plan.adding else result
    terms = outs[:fold] if plan.part else None
    sends = outs[-depth:] if plan.folding else None
    return terms, sends, result, piece


def cuts(nbands, first):
    half, quarter = nbands // 2, nbands // 4
    widths = [quarter, quarter, half] if first else [half, quarter, quarter]
    starts = [sum(widths[:i]) for i in range(len(widths))]
    return list(zip(starts, widths))


def adding_jobs(parts):
    jobs = {}
    group = ()
    for index, part in enumerate(parts):
        group += (part,)
        if sum(width for _, _, width in group) % LANES == 0:
            jobs[index] = group
            group = ()
    return jobs


def body(bands, nbr_slot, gshift):
    grid_index = lax.axis_index("ga")
    grid_count = lax.axis_size("ga")
    k_dev, _, nbands, points = bands.shape
    rows = nbands // grid_count
    own_planes = points // PLANE
    total_planes = own_planes * grid_count
    planes = grid_index * own_planes + jnp.arange(own_planes, dtype=jnp.int32)
    slots = jnp.arange(k_dev, dtype=jnp.int32)
    chosen = nbr_slot[None, :] == slots[:, None]
    order = jnp.sum(jnp.where(chosen, slots[None, :], 0), axis=1)
    shifts = jnp.sum(jnp.where(chosen, gshift[None, :], 0), axis=1)
    turns = (1 + NKB * shifts[:, None]) * planes[None, :] % (NKB * total_planes)
    angle = 2.0 * math.pi / (NKB * total_planes) * turns.astype(jnp.float32)
    columns = [order[:, None].astype(jnp.float32), jnp.cos(angle), jnp.sin(angle)]
    table = jnp.concatenate(columns, axis=1).reshape(-1)
    table = jnp.append(table, grid_index.astype(jnp.float32))
    parts = []
    for slot in range(k_dev):
        for start, width in cuts(nbands, slot == 0):
            parts.append((slot, start, width))
    theres = []
    piece = None
    for slot, start, width in parts[:AHEAD]:
        piece = piece_of(slot, start, width, bands, [] if piece is None else [piece])
        theres.append(shifted(piece, "ka", -1))
    shape = (rows, k_dev, 2, nbands)
    depth = min(OUTER, grid_count)
    fold = grid_count // depth
    jobs = adding_jobs(parts)
    folded, arrived = {}, {}
    result = None
    for index in range(len(parts) + 2):
        part = parts[index] if index < len(parts) else None
        folding = parts[index - 1] if 0 <= index - 1 < len(parts) else None
        adding = jobs.get(index - 2, ())
        later = parts[index + AHEAD] if index + AHEAD < len(parts) else None
        plan = Plan(shape, fold, depth, part, folding, adding, result is not None, later)
        terms, sends, result, piece = step(
            plan,
            table,
            bands,
            theres[index] if part else None,
            folded.pop(folding, None),
            [arrived.pop(done) for done in adding],
            result,
        )
        if later:
            theres.append(shifted(piece, "ka", -1))
        if part:
            folded[part] = [terms[0]] + [
                shifted(terms[i], "ga", i, fold, True) for i in range(1, fold)
            ]
        if folding:
            arrived[folding] = [sends[0]] + [
                shifted(sends[i], "ga", i, fold) for i in range(1, depth)
            ]
    return result


def solution(mesh):
    placed = (P("ka", None, None, "ga"), P("ka"), P("ka"))
    return jax.shard_map(
        body, mesh=mesh, in_specs=placed, out_specs=P("ga", "ka", None, None), check_vma=False
    )
```

time: 310 us -> 130 us (0.42)
  waiting for transfers between devices: 247 us -> 42.8 us
  starting transfers between devices: 2.41 us -> 47.2 us
  Pallas kernels: 0 us -> 38.6 us
  local copies, waits for them, and re-layouts: 19.3 us -> 0.19 us
  other arithmetic: 15.1 us -> 0.43 us
  between operations: 13.4 us -> 0.3 us
  matrix products: 12.6 us -> 0 us
    psum x1 -> x0, waiting for transfers between devices: 158 us -> none  [body(): summed = lax.psum(jnp.stack([real_part, imag_part], axis=2), 'ga')]
    ppermute x1 -> x30, waiting for transfers between devices: 88.9 us -> 42.8 us  [shifted(): return lax.ppermute(block, axis, route)]
    ppermute x1 -> x30, starting transfers between devices: 2.41 us -> 47.2 us  [shifted(): return lax.ppermute(block, axis, route)]
    pallas_call x0 -> x10, Pallas kernels: none -> 38.6 us  [the longest x8 36.1 us: step(): pl.pallas_call(functools.partial(step_kernel, plan), in_specs=in_specs, o...]
    gather x5 -> x0, local copies, waits for them, and re-layouts: 16.6 us -> none  [body(): partner = jnp.take(there, nbr_slot, axis=0)]
    dot_general x1 -> x0, matrix products: 12.6 us -> none  [body(): jnp.einsum('pcmx,pdnx->mpcdn', bands, near, preferred_element_type=jnp.fl...]
    another operation x2 -> x0, other arithmetic: 7.46 us -> none
    select_n x3 -> x0, other arithmetic: 5.03 us -> none  [the longest x2 5.02 us: body(): partner = jnp.take(there, nbr_slot, axis=0)]
  transfers between devices with their start and end apart: 2 -> 30, of which waited for: 2 -> 20; matrix products, arithmetic and copies ran while one was open for 1% -> 0% of each run, Pallas kernels for 0% -> 23%
where the time goes in v7:
time: 130 us
  starting transfers between devices  47.2 us (36%)
  waiting for transfers between devices  42.8 us (33%)
  Pallas kernels  38.6 us (30%)
    ppermute x30, starting transfers between devices, shifted(): return lax.ppermute(block, axis, route)  47.2 us
    ppermute x30, waiting for transfers between devices, shifted(): return lax.ppermute(block, axis, route)  42.8 us
    pallas_call x8, Pallas kernels, step(): pl.pallas_call(functools.partial(step_kernel, plan), in_specs=in_specs, o...  36.1 us
  transfers between devices with their start and end apart: 30, of which 20 were waited for; matrix products, arithmetic and copies ran while one was open for 0% of the time, Pallas kernels for 23%

profile of v7, /device:TPU:0, one launch (start us, length us, event | category | flops | bytes accessed | tf_op | source)
XLA Modules:
  0.0 129.5 jit_solution(16160249246327464757)
XLA Ops:
  0.0 1.3 piece_of.2.rest_0_
  1.3 2.5 %collective-permute-start.1 = (bf16[2,128,2048]{2,1,0:T(8,128)(2,1)S(1)}, bf16[2,128,2048]{2,1,0:T(8,128)(2,1)}, u32[]{:S(2)}, u32[]{:S(2)}) collective-permute-start(bf16[2,128,2048]{2,1,0:T(8,128)(2,1)S(1)} %piece_of.2.rest_0_), channel_id=1, source_target_pairs={{0,24},{8,0},{16,8},{24,16},{1,25},{9,1},{17,9},{25,17},{2,26},{10... | collective-permute-start | bytes 3145736 | tf_op jit(solution)/shard_map/ppermute | solution.py:33
  3.8 1.3 piece_of.3
  6.4 9.7 %collective-permute-done.1.refs_1_ = bf16[2,128,2048]{2,1,0:T(8,128)(2,1)} collective-permute-done((bf16[2,128,2048]{2,1,0:T(8,128)(2,1)S(1)}, bf16[2,128,2048]{2,1,0:T(8,128)(2,1)}, u32[]{:S(2)}, u32[]{:S(2)}) %collective-permute-start.1) | collective-permute-done | bytes 1048608 | tf_op jit(solution)/shard_map/ppermute | solution.py:33
  16.1 5.7 %step.8 = (f32[4,64,256]{2,1,0:T(8,128)S(1)}, bf16[4,64,256]{2,1,0:T(8,128)(2,1)S(1)}, bf16[2,256,2048]{2,1,0:T(8,128)(2,1)S(1)}) custom-call(f32[11]{0:T(128)S(1)} %pad_maximum_fusion.1.table_ref, bf16[2,2,512,2048]{3,2,1,0:T(8,128)(2,1)} %refs_0_.11, bf16[2,128,2048]{2,1,0:T(8,128)(2,1)} %collective-permute-done.1.refs_1_), custom_call_target="tpu_custom_call" | custom-call | flops 1000 | bytes 1000 | tf_op jit(solution)/shard_map/step/pallas_call | solution.py:284
  21.8 2.1 %collective-permute-start.4 = (bf16[2,256,2048]{2,1,0:T(8,128)(2,1)S(1)}, bf16[2,256,2048]{2,1,0:T(8,128)(2,1)S(1)}, u32[]{:S(2)}, u32[]{:S(2)}) collective-permute-start(bf16[2,256,2048]{2,1,0:T(8,128)(2,1)S(1)} %get-tuple-element.53), channel_id=1, source_target_pairs={{0,24},{8,0},{16,8},{24,16},{1,25},{9,1},{17,9},{25,17},{2,26},{10... | collective-permute-start | bytes 6291464 | tf_op jit(solution)/shard_map/ppermute | solution.py:33
  23.8 1.5 %collective-permute-start.2 = (bf16[4,64,256]{2,1,0:T(8,128)(2,1)S(1)}, bf16[4,64,256]{2,1,0:T(8,128)(2,1)S(1)}, u32[]{:S(2)}, u32[]{:S(2)}) collective-permute-start(bf16[4,64,256]{2,1,0:T(8,128)(2,1)S(1)} %get-tuple-element.51), channel_id=1, source_target_pairs={{0,1},{1,0},{2,3},{3,2},{4,5},{5,4},{6,7},{7,6},{8,9},{9,8},{10,11... | collective-permute-start | bytes 393224 | tf_op jit(solution)/shard_map/ppermute | solution.py:33
  25.3 2.0 %collective-permute-done.refs_1_ = bf16[2,128,2048]{2,1,0:T(8,128)(2,1)S(1)} collective-permute-done((bf16[2,128,2048]{2,1,0:T(8,128)(2,1)S(1)}, bf16[2,128,2048]{2,1,0:T(8,128)(2,1)S(1)}, u32[]{:S(2)}, u32[]{:S(2)}) %collective-permute-start) | collective-permute-done | bytes 1048608 | tf_op jit(solution)/shard_map/ppermute | solution.py:33
  27.3 1.5 %collective-permute-done.2.refs_3_ = bf16[4,64,256]{2,1,0:T(8,128)(2,1)S(1)} collective-permute-done((bf16[4,64,256]{2,1,0:T(8,128)(2,1)S(1)}, bf16[4,64,256]{2,1,0:T(8,128)(2,1)S(1)}, u32[]{:S(2)}, u32[]{:S(2)}) %collective-permute-start.2) | collective-permute-done | bytes 131104 | tf_op jit(solution)/shard_map/ppermute | solution.py:33
  28.8 5.9 %step.9 = (f32[4,64,256]{2,1,0:T(8,128)S(1)}, bf16[4,64,256]{2,1,0:T(8,128)(2,1)S(1)}, f32[64,256]{1,0:T(8,128)S(1)}, bf16[64,256]{1,0:T(8,128)(2,1)S(1)}, bf16[...) custom-call(f32[11]{0:T(128)S(1)} %pad_maximum_fusion.1.table_ref, ...), custom_call_target="tpu_custom_call" | custom-call | flops 1000 | bytes 1000 | tf_op jit(solution)/shard_map/step/pallas_call | solution.py:284
  35.4 1.5 %collective-permute-start.5 = (bf16[4,64,256]{2,1,0:T(8,128)(2,1)S(1)}, bf16[4,64,256]{2,1,0:T(8,128)(2,1)S(1)}, u32[]{:S(2)}, u32[]{:S(2)}) collective-permute-start(bf16[4,64,256]{2,1,0:T(8,128)(2,1)S(1)} %get-tuple-element.55), channel_id=1, source_target_pairs={{0,1},{1,0},{2,3},{3,2},{4,5},{5,4},{6,7},{7,6},{8,9},{9,8},{10,11... | collective-permute-start | bytes 393224 | tf_op jit(solution)/shard_map/ppermute | solution.py:33
  36.9 1.6 %collective-permute-start.6 = (bf16[64,256]{1,0:T(8,128)(2,1)S(1)}, bf16[64,256]{1,0:T(8,128)(2,1)S(1)}, u32[]{:S(2)}, u32[]{:S(2)}) collective-permute-start(bf16[64,256]{1,0:T(8,128)(2,1)S(1)} %get-tuple-element.57), channel_id=1, source_target_pairs={{0,2},{1,3},{2,4},{3,5},{4,6},{5,7},{6,0},{7,1},{8,10},{9,11},{10,... | collective-permute-start | bytes 98312 | tf_op jit(solution)/shard_map/ppermute | solution.py:33
  38.5 2.6 %collective-permute-start.7 = (bf16[64,256]{1,0:T(8,128)(2,1)S(1)}, bf16[64,256]{1,0:T(8,128)(2,1)S(1)}, u32[]{:S(2)}, u32[]{:S(2)}) collective-permute-start(bf16[64,256]{1,0:T(8,128)(2,1)S(1)} %get-tuple-element.58), channel_id=1, source_target_pairs={{0,4},{1,5},{2,6},{3,7},{4,0},{5,1},{6,2},{7,3},{8,12},{9,13},{10,... | collective-permute-start | bytes 98312 | tf_op jit(solution)/shard_map/ppermute | solution.py:33
  41.1 1.9 %collective-permute-done.6.refs_5_ = bf16[64,256]{1,0:T(8,128)(2,1)S(1)} collective-permute-done((bf16[64,256]{1,0:T(8,128)(2,1)S(1)}, bf16[64,256]{1,0:T(8,128)(2,1)S(1)}, u32[]{:S(2)}, u32[]{:S(2)}) %collective-permute-start.6) | collective-permute-done | bytes 32800 | tf_op jit(solution)/shard_map/ppermute | solution.py:33
  42.9 1.5 %collective-permute-start.8 = (bf16[64,256]{1,0:T(8,128)(2,1)S(1)}, bf16[64,256]{1,0:T(8,128)(2,1)S(1)}, u32[]{:S(2)}, u32[]{:S(2)}) collective-permute-start(bf16[64,256]{1,0:T(8,128)(2,1)S(1)} %get-tuple-element.59), channel_id=1, source_target_pairs={{0,6},{1,7},{2,0},{3,1},{4,2},{5,3},{6,4},{7,5},{8,14},{9,15},{10,... | collective-permute-start | bytes 98312 | tf_op jit(solution)/shard_map/ppermute | solution.py:33
  44.4 2.4 %collective-permute-done.8.refs_7_ = bf16[64,256]{1,0:T(8,128)(2,1)S(1)} collective-permute-done((bf16[64,256]{1,0:T(8,128)(2,1)S(1)}, bf16[64,256]{1,0:T(8,128)(2,1)S(1)}, u32[]{:S(2)}, u32[]{:S(2)}) %collective-permute-start.8) | collective-permute-done | bytes 32800 | tf_op jit(solution)/shard_map/ppermute | solution.py:33
  46.9 2.9 %collective-permute-done.4.refs_1_ = bf16[2,256,2048]{2,1,0:T(8,128)(2,1)S(1)} collective-permute-done((bf16[2,256,2048]{2,1,0:T(8,128)(2,1)S(1)}, bf16[2,256,2048]{2,1,0:T(8,128)(2,1)S(1)}, u32[]{:S(2)}, u32[]{:S(2)}) %collective-permute-start.4) | collective-permute-done | bytes 2097184 | tf_op jit(solution)/shard_map/ppermute | solution.py:33
  49.8 6.2 %step.10 = (f32[4,64,512]{2,1,0:T(8,128)S(1)}, bf16[4,64,512]{2,1,0:T(8,128)(2,1)S(1)}, f32[64,256]{1,0:T(8,128)S(1)}, bf16[64,256]{1,0:T(8,128)(2,1)S(1)}, bf16...) custom-call(f32[11]{0:T(128)S(1)} %pad_maximum_fusion.1.table_ref, ...), custom_call_target="tpu_custom_call" | custom-call | flops 1000 | bytes 1000 | tf_op jit(solution)/shard_map/step/pallas_call | solution.py:284
  56.0 1.6 %collective-permute-start.9 = (bf16[4,64,512]{2,1,0:T(8,128)(2,1)S(1)}, bf16[4,64,512]{2,1,0:T(8,128)(2,1)S(1)}, u32[]{:S(2)}, u32[]{:S(2)}) collective-permute-start(bf16[4,64,512]{2,1,0:T(8,128)(2,1)S(1)} %get-tuple-element.61), channel_id=1, source_target_pairs={{0,1},{1,0},{2,3},{3,2},{4,5},{5,4},{6,7},{7,6},{8,9},{9,8},{10,11... | collective-permute-start | bytes 786440 | tf_op jit(solution)/shard_map/ppermute | solution.py:33
  57.5 1.6 %collective-permute-start.14 = (bf16[2,128,2048]{2,1,0:T(8,128)(2,1)S(1)}, bf16[2,128,2048]{2,1,0:T(8,128)(2,1)S(1)}, u32[]{:S(2)}, u32[]{:S(2)}) collective-permute-start(bf16[2,128,2048]{2,1,0:T(8,128)(2,1)S(1)} %get-tuple-element.68), channel_id=1, source_target_pairs={{0,24},{8,0},{16,8},{24,16},{1,25},{9,1},{17,9},{25,17},{2,26},{10... | collective-permute-start | bytes 3145736 | tf_op jit(solution)/shard_map/ppermute | solution.py:33
  59.2 1.6 %collective-permute-start.10 = (bf16[64,256]{1,0:T(8,128)(2,1)S(1)}, bf16[64,256]{1,0:T(8,128)(2,1)S(1)}, u32[]{:S(2)}, u32[]{:S(2)}) collective-permute-start(bf16[64,256]{1,0:T(8,128)(2,1)S(1)} %get-tuple-element.63), channel_id=1, source_target_pairs={{0,2},{1,3},{2,4},{3,5},{4,6},{5,7},{6,0},{7,1},{8,10},{9,11},{10,... | collective-permute-start | bytes 98312 | tf_op jit(solution)/shard_map/ppermute | solution.py:33
  60.8 2.6 %collective-permute-start.11 = (bf16[64,256]{1,0:T(8,128)(2,1)S(1)}, bf16[64,256]{1,0:T(8,128)(2,1)S(1)}, u32[]{:S(2)}, u32[]{:S(2)}) collective-permute-start(bf16[64,256]{1,0:T(8,128)(2,1)S(1)} %get-tuple-element.64), channel_id=1, source_target_pairs={{0,4},{1,5},{2,6},{3,7},{4,0},{5,1},{6,2},{7,3},{8,12},{9,13},{10,... | collective-permute-start | bytes 98312 | tf_op jit(solution)/shard_map/ppermute | solution.py:33
  63.3 1.6 %collective-permute-done.10.refs_5_ = bf16[64,256]{1,0:T(8,128)(2,1)S(1)} collective-permute-done((bf16[64,256]{1,0:T(8,128)(2,1)S(1)}, bf16[64,256]{1,0:T(8,128)(2,1)S(1)}, u32[]{:S(2)}, u32[]{:S(2)}) %collective-permute-start.10) | collective-permute-done | bytes 32800 | tf_op jit(solution)/shard_map/ppermute | solution.py:33
  64.9 1.8 %collective-permute-start.12 = (bf16[64,256]{1,0:T(8,128)(2,1)S(1)}, bf16[64,256]{1,0:T(8,128)(2,1)S(1)}, u32[]{:S(2)}, u32[]{:S(2)}) collective-permute-start(bf16[64,256]{1,0:T(8,128)(2,1)S(1)} %get-tuple-element.65), channel_id=1, source_target_pairs={{0,6},{1,7},{2,0},{3,1},{4,2},{5,3},{6,4},{7,5},{8,14},{9,15},{10,... | collective-permute-start | bytes 98312 | tf_op jit(solution)/shard_map/ppermute | solution.py:33
  66.7 2.1 %collective-permute-done.12.refs_7_ = bf16[64,256]{1,0:T(8,128)(2,1)S(1)} collective-permute-done((bf16[64,256]{1,0:T(8,128)(2,1)S(1)}, bf16[64,256]{1,0:T(8,128)(2,1)S(1)}, u32[]{:S(2)}, u32[]{:S(2)}) %collective-permute-start.12) | collective-permute-done | bytes 32800 | tf_op jit(solution)/shard_map/ppermute | solution.py:33
  68.8 3.4 %collective-permute-done.3.refs_1_ = bf16[2,256,2048]{2,1,0:T(8,128)(2,1)S(1)} collective-permute-done((bf16[2,256,2048]{2,1,0:T(8,128)(2,1)S(1)}, bf16[2,256,2048]{2,1,0:T(8,128)(2,1)S(1)}, u32[]{:S(2)}, u32[]{:S(2)}) %collective-permute-start.3) | collective-permute-done | bytes 2097184 | tf_op jit(solution)/shard_map/ppermute | solution.py:33
  72.3 6.2 %step.11 = (f32[4,64,512]{2,1,0:T(8,128)S(1)}, bf16[4,64,512]{2,1,0:T(8,128)(2,1)S(1)}, f32[64,512]{1,0:T(8,128)S(1)}, bf16[64,512]{1,0:T(8,128)(2,1)S(1)}, bf16...) custom-call(f32[11]{0:T(128)S(1)} %pad_maximum_fusion.1.table_ref, ...), custom_call_target="tpu_custom_call", output_to_operand_aliasing={{6}: (9, {})} | custom-call | flops 1000 | bytes 1000 | tf_op jit(solution)/shard_map/step/pallas_call | solution.py:284
  78.5 2.0 %collective-permute-start.13 = (bf16[2,128,2048]{2,1,0:T(8,128)(2,1)S(1)}, bf16[2,128,2048]{2,1,0:T(8,128)(2,1)S(1)}, u32[]{:S(2)}, u32[]{:S(2)}) collective-permute-start(bf16[2,128,2048]{2,1,0:T(8,128)(2,1)S(1)} %get-tuple-element.67), channel_id=1, source_target_pairs={{0,24},{8,0},{16,8},{24,16},{1,25},{9,1},{17,9},{25,17},{2,26},{10... | collective-permute-start | bytes 3145736 | tf_op jit(solution)/shard_map/ppermute | solution.py:33
  80.4 1.5 %collective-permute-start.15 = (bf16[4,64,512]{2,1,0:T(8,128)(2,1)S(1)}, bf16[4,64,512]{2,1,0:T(8,128)(2,1)S(1)}, u32[]{:S(2)}, u32[]{:S(2)}) collective-permute-start(bf16[4,64,512]{2,1,0:T(8,128)(2,1)S(1)} %get-tuple-element.70), channel_id=1, source_target_pairs={{0,1},{1,0},{2,3},{3,2},{4,5},{5,4},{6,7},{7,6},{8,9},{9,8},{10,11... | collective-permute-start | bytes 786440 | tf_op jit(solution)/shard_map/ppermute | solution.py:33
  81.9 1.6 %collective-permute-start.16 = (bf16[64,512]{1,0:T(8,128)(2,1)S(1)}, bf16[64,512]{1,0:T(8,128)(2,1)S(1)}, u32[]{:S(2)}, u32[]{:S(2)}) collective-permute-start(bf16[64,512]{1,0:T(8,128)(2,1)S(1)} %get-tuple-element.72), channel_id=1, source_target_pairs={{0,2},{1,3},{2,4},{3,5},{4,6},{5,7},{6,0},{7,1},{8,10},{9,11},{10,... | collective-permute-start | bytes 196616 | tf_op jit(solution)/shard_map/ppermute | solution.py:33
  83.5 2.6 %collective-permute-start.17 = (bf16[64,512]{1,0:T(8,128)(2,1)S(1)}, bf16[64,512]{1,0:T(8,128)(2,1)S(1)}, u32[]{:S(2)}, u32[]{:S(2)}) collective-permute-start(bf16[64,512]{1,0:T(8,128)(2,1)S(1)} %get-tuple-element.73), channel_id=1, source_target_pairs={{0,4},{1,5},{2,6},{3,7},{4,0},{5,1},{6,2},{7,3},{8,12},{9,13},{10,... | collective-permute-start | bytes 196616 | tf_op jit(solution)/shard_map/ppermute | solution.py:33
  86.1 2.0 %collective-permute-done.16.refs_5_ = bf16[64,512]{1,0:T(8,128)(2,1)S(1)} collective-permute-done((bf16[64,512]{1,0:T(8,128)(2,1)S(1)}, bf16[64,512]{1,0:T(8,128)(2,1)S(1)}, u32[]{:S(2)}, u32[]{:S(2)}) %collective-permute-start.16) | collective-permute-done | bytes 65568 | tf_op jit(solution)/shard_map/ppermute | solution.py:33
  88.0 1.7 %collective-permute-start.18 = (bf16[64,512]{1,0:T(8,128)(2,1)S(1)}, bf16[64,512]{1,0:T(8,128)(2,1)S(1)}, u32[]{:S(2)}, u32[]{:S(2)}) collective-permute-start(bf16[64,512]{1,0:T(8,128)(2,1)S(1)} %get-tuple-element.74), channel_id=1, source_target_pairs={{0,6},{1,7},{2,0},{3,1},{4,2},{5,3},{6,4},{7,5},{8,14},{9,15},{10,... | collective-permute-start | bytes 196616 | tf_op jit(solution)/shard_map/ppermute | solution.py:33
  90.1 2.2 %collective-permute-done.18.refs_7_ = bf16[64,512]{1,0:T(8,128)(2,1)S(1)} collective-permute-done((bf16[64,512]{1,0:T(8,128)(2,1)S(1)}, bf16[64,512]{1,0:T(8,128)(2,1)S(1)}, u32[]{:S(2)}, u32[]{:S(2)}) %collective-permute-start.18) | collective-permute-done | bytes 65568 | tf_op jit(solution)/shard_map/ppermute | solution.py:33
  92.3 4.8 %step.12 = (f32[4,64,256]{2,1,0:T(8,128)S(1)}, bf16[4,64,256]{2,1,0:T(8,128)(2,1)S(1)}, f32[64,512]{1,0:T(8,128)S(1)}, bf16[64,512]{1,0:T(8,128)(2,1)S(1)}, bf16...) custom-call(f32[11]{0:T(128)S(1)} %pad_maximum_fusion.1.table_ref, ...), custom_call_target="tpu_custom_call", output_to_operand_aliasing={{6}: (9, {})} | custom-call | flops 1000 | bytes 1000 | tf_op jit(solution)/shard_map/step/pallas_call | solution.py:284
  98.1 3.8 %collective-permute-start.21 = (bf16[64,512]{1,0:T(8,128)(2,1)S(1)}, bf16[64,512]{1,0:T(8,128)(2,1)S(1)}, u32[]{:S(2)}, u32[]{:S(2)}) collective-permute-start(bf16[64,512]{1,0:T(8,128)(2,1)S(1)} %get-tuple-element.80), channel_id=1, source_target_pairs={{0,4},{1,5},{2,6},{3,7},{4,0},{5,1},{6,2},{7,3},{8,12},{9,13},{10,... | collective-permute-start | bytes 196616 | tf_op jit(solution)/shard_map/ppermute | solution.py:33
  102.0 1.8 %collective-permute-done.20.refs_5_ = bf16[64,512]{1,0:T(8,128)(2,1)S(1)} collective-permute-done((bf16[64,512]{1,0:T(8,128)(2,1)S(1)}, bf16[64,512]{1,0:T(8,128)(2,1)S(1)}, u32[]{:S(2)}, u32[]{:S(2)}) %collective-permute-start.20) | collective-permute-done | bytes 65568 | tf_op jit(solution)/shard_map/ppermute | solution.py:33
  103.8 1.4 %collective-permute-done.21.refs_6_ = bf16[64,512]{1,0:T(8,128)(2,1)S(1)} collective-permute-done((bf16[64,512]{1,0:T(8,128)(2,1)S(1)}, bf16[64,512]{1,0:T(8,128)(2,1)S(1)}, u32[]{:S(2)}, u32[]{:S(2)}) %collective-permute-start.21) | collective-permute-done | bytes 65568 | tf_op jit(solution)/shard_map/ppermute | solution.py:33
  106.1 4.8 %step.13 = (f32[4,64,256]{2,1,0:T(8,128)S(1)}, bf16[4,64,256]{2,1,0:T(8,128)(2,1)S(1)}, f32[64,256]{1,0:T(8,128)S(1)}, bf16[64,256]{1,0:T(8,128)(2,1)S(1)}, bf16...) custom-call(f32[11]{0:T(128)S(1)} %pad_maximum_fusion.1.table_ref, ...), custom_call_target="tpu_custom_call", output_to_operand_aliasing={{6}: (9, {})} | custom-call | flops 1000 | bytes 1000 | tf_op jit(solution)/shard_map/step/pallas_call | solution.py:284
  110.9 1.6 %collective-permute-start.23 = (bf16[4,64,256]{2,1,0:T(8,128)(2,1)S(1)}, bf16[4,64,256]{2,1,0:T(8,128)(2,1)S(1)}, u32[]{:S(2)}, u32[]{:S(2)}) collective-permute-start(bf16[4,64,256]{2,1,0:T(8,128)(2,1)S(1)} %get-tuple-element.84), channel_id=1, source_target_pairs={{0,1},{1,0},{2,3},{3,2},{4,5},{5,4},{6,7},{7,6},{8,9},{9,8},{10,11... | collective-permute-start | bytes 393224 | tf_op jit(solution)/shard_map/ppermute | solution.py:33
  112.8 2.7 %collective-permute-start.25 = (bf16[64,256]{1,0:T(8,128)(2,1)S(1)}, bf16[64,256]{1,0:T(8,128)(2,1)S(1)}, u32[]{:S(2)}, u32[]{:S(2)}) collective-permute-start(bf16[64,256]{1,0:T(8,128)(2,1)S(1)} %get-tuple-element.87), channel_id=1, source_target_pairs={{0,4},{1,5},{2,6},{3,7},{4,0},{5,1},{6,2},{7,3},{8,12},{9,13},{10,... | collective-permute-start | bytes 98312 | tf_op jit(solution)/shard_map/ppermute | solution.py:33
  116.3 1.9 %collective-permute-done.24.refs_3_ = bf16[64,256]{1,0:T(8,128)(2,1)S(1)} collective-permute-done((bf16[64,256]{1,0:T(8,128)(2,1)S(1)}, bf16[64,256]{1,0:T(8,128)(2,1)S(1)}, u32[]{:S(2)}, u32[]{:S(2)}) %collective-permute-start.24) | collective-permute-done | bytes 32800 | tf_op jit(solution)/shard_map/ppermute | solution.py:33
  118.2 1.6 %collective-permute-done.26.refs_5_ = bf16[64,256]{1,0:T(8,128)(2,1)S(1)} collective-permute-done((bf16[64,256]{1,0:T(8,128)(2,1)S(1)}, bf16[64,256]{1,0:T(8,128)(2,1)S(1)}, u32[]{:S(2)}, u32[]{:S(2)}) %collective-permute-start.26) | collective-permute-done | bytes 32800 | tf_op jit(solution)/shard_map/ppermute | solution.py:33
  119.8 1.2 step.14
  121.1 1.0 collective-permute-start.27
  122.1 2.1 %collective-permute-start.28 = (bf16[64,256]{1,0:T(8,128)(2,1)S(1)}, bf16[64,256]{1,0:T(8,128)(2,1)S(1)}, u32[]{:S(2)}, u32[]{:S(2)}) collective-permute-start(bf16[64,256]{1,0:T(8,128)(2,1)S(1)} %get-tuple-element.92), channel_id=1, source_target_pairs={{0,4},{1,5},{2,6},{3,7},{4,0},{5,1},{6,2},{7,3},{8,12},{9,13},{10,... | collective-permute-start | bytes 98312 | tf_op jit(solution)/shard_map/ppermute | solution.py:33
  125.0 1.9 %collective-permute-done.27.refs_1_ = bf16[64,256]{1,0:T(8,128)(2,1)S(1)} collective-permute-done((bf16[64,256]{1,0:T(8,128)(2,1)S(1)}, bf16[64,256]{1,0:T(8,128)(2,1)S(1)}, u32[]{:S(2)}, u32[]{:S(2)}) %collective-permute-start.27) | collective-permute-done | bytes 32800 | tf_op jit(solution)/shard_map/ppermute | solution.py:33
  128.1 1.2 step.15
  (34 shorter events, 7.5 us)
Async XLA Ops:
  1.3 4.5 %copy-start = (s32[2]{0:T(128)S(1)}, s32[2]{0:T(128)}, u32[]{:S(2)}) copy-start(s32[2]{0:T(128)} %param.4) | copy-start | bytes 28
  1.3 4.5 %copy-start.1 = (s32[2]{0:T(128)S(1)}, s32[2]{0:T(128)}, u32[]{:S(2)}) copy-start(s32[2]{0:T(128)} %param.5) | copy-start | bytes 28
  1.3 14.8 %collective-permute-start.1 = (bf16[2,128,2048]{2,1,0:T(8,128)(2,1)S(1)}, bf16[2,128,2048]{2,1,0:T(8,128)(2,1)}, u32[]{:S(2)}, u32[]{:S(2)}) collective-permute-start(bf16[2,128,2048]{2,1,0:T(8,128)(2,1)S(1)} %piece_of.2.rest_0_), channel_id=1, source_target_pairs={{0,24},{8,0},{16,8},{24,16},{1,25},{9,1},{17,9},{25,17},{2,26},{10... | collective-permute-start | bytes 3145736 | tf_op jit(solution)/shard_map/ppermute | solution.py:33
  5.0 22.3 %collective-permute-start = (bf16[2,128,2048]{2,1,0:T(8,128)(2,1)S(1)}, bf16[2,128,2048]{2,1,0:T(8,128)(2,1)S(1)}, u32[]{:S(2)}, u32[]{:S(2)}) collective-permute-start(bf16[2,128,2048]{2,1,0:T(8,128)(2,1)S(1)} %piece_of.3), channel_id=1, source_target_pairs={{0,24},{8,0},{16,8},{24,16},{1,25},{9,1},{17,9},{25,17},{2,26},{10... | collective-permute-start | bytes 3145736 | tf_op jit(solution)/shard_map/ppermute | solution.py:33
  21.8 28.0 %collective-permute-start.4 = (bf16[2,256,2048]{2,1,0:T(8,128)(2,1)S(1)}, bf16[2,256,2048]{2,1,0:T(8,128)(2,1)S(1)}, u32[]{:S(2)}, u32[]{:S(2)}) collective-permute-start(bf16[2,256,2048]{2,1,0:T(8,128)(2,1)S(1)} %get-tuple-element.53), channel_id=1, source_target_pairs={{0,24},{8,0},{16,8},{24,16},{1,25},{9,1},{17,9},{25,17},{2,26},{10... | collective-permute-start | bytes 6291464 | tf_op jit(solution)/shard_map/ppermute | solution.py:33
  23.8 5.0 %collective-permute-start.2 = (bf16[4,64,256]{2,1,0:T(8,128)(2,1)S(1)}, bf16[4,64,256]{2,1,0:T(8,128)(2,1)S(1)}, u32[]{:S(2)}, u32[]{:S(2)}) collective-permute-start(bf16[4,64,256]{2,1,0:T(8,128)(2,1)S(1)} %get-tuple-element.51), channel_id=1, source_target_pairs={{0,1},{1,0},{2,3},{3,2},{4,5},{5,4},{6,7},{7,6},{8,9},{9,8},{10,11... | collective-permute-start | bytes 393224 | tf_op jit(solution)/shard_map/ppermute | solution.py:33
  34.7 37.5 %collective-permute-start.3 = (bf16[2,256,2048]{2,1,0:T(8,128)(2,1)S(1)}, bf16[2,256,2048]{2,1,0:T(8,128)(2,1)S(1)}, u32[]{:S(2)}, u32[]{:S(2)}) collective-permute-start(bf16[2,256,2048]{2,1,0:T(8,128)(2,1)S(1)} %get-tuple-element.52), channel_id=1, source_target_pairs={{0,24},{8,0},{16,8},{24,16},{1,25},{9,1},{17,9},{25,17},{2,26},{10... | collective-permute-start | bytes 6291464 | tf_op jit(solution)/shard_map/ppermute | solution.py:33
  35.4 11.4 %collective-permute-start.5 = (bf16[4,64,256]{2,1,0:T(8,128)(2,1)S(1)}, bf16[4,64,256]{2,1,0:T(8,128)(2,1)S(1)}, u32[]{:S(2)}, u32[]{:S(2)}) collective-permute-start(bf16[4,64,256]{2,1,0:T(8,128)(2,1)S(1)} %get-tuple-element.55), channel_id=1, source_target_pairs={{0,1},{1,0},{2,3},{3,2},{4,5},{5,4},{6,7},{7,6},{8,9},{9,8},{10,11... | collective-permute-start | bytes 393224 | tf_op jit(solution)/shard_map/ppermute | solution.py:33
  36.9 6.0 %collective-permute-start.6 = (bf16[64,256]{1,0:T(8,128)(2,1)S(1)}, bf16[64,256]{1,0:T(8,128)(2,1)S(1)}, u32[]{:S(2)}, u32[]{:S(2)}) collective-permute-start(bf16[64,256]{1,0:T(8,128)(2,1)S(1)} %get-tuple-element.57), channel_id=1, source_target_pairs={{0,2},{1,3},{2,4},{3,5},{4,6},{5,7},{6,0},{7,1},{8,10},{9,11},{10,... | collective-permute-start | bytes 98312 | tf_op jit(solution)/shard_map/ppermute | solution.py:33
  38.5 5.9 %collective-permute-start.7 = (bf16[64,256]{1,0:T(8,128)(2,1)S(1)}, bf16[64,256]{1,0:T(8,128)(2,1)S(1)}, u32[]{:S(2)}, u32[]{:S(2)}) collective-permute-start(bf16[64,256]{1,0:T(8,128)(2,1)S(1)} %get-tuple-element.58), channel_id=1, source_target_pairs={{0,4},{1,5},{2,6},{3,7},{4,0},{5,1},{6,2},{7,3},{8,12},{9,13},{10,... | collective-permute-start | bytes 98312 | tf_op jit(solution)/shard_map/ppermute | solution.py:33
  42.9 3.9 %collective-permute-start.8 = (bf16[64,256]{1,0:T(8,128)(2,1)S(1)}, bf16[64,256]{1,0:T(8,128)(2,1)S(1)}, u32[]{:S(2)}, u32[]{:S(2)}) collective-permute-start(bf16[64,256]{1,0:T(8,128)(2,1)S(1)} %get-tuple-element.59), channel_id=1, source_target_pairs={{0,6},{1,7},{2,0},{3,1},{4,2},{5,3},{6,4},{7,5},{8,14},{9,15},{10,... | collective-permute-start | bytes 98312 | tf_op jit(solution)/shard_map/ppermute | solution.py:33
  56.0 16.3 %collective-permute-start.9 = (bf16[4,64,512]{2,1,0:T(8,128)(2,1)S(1)}, bf16[4,64,512]{2,1,0:T(8,128)(2,1)S(1)}, u32[]{:S(2)}, u32[]{:S(2)}) collective-permute-start(bf16[4,64,512]{2,1,0:T(8,128)(2,1)S(1)} %get-tuple-element.61), channel_id=1, source_target_pairs={{0,1},{1,0},{2,3},{3,2},{4,5},{5,4},{6,7},{7,6},{8,9},{9,8},{10,11... | collective-permute-start | bytes 786440 | tf_op jit(solution)/shard_map/ppermute | solution.py:33
  57.5 34.8 %collective-permute-start.14 = (bf16[2,128,2048]{2,1,0:T(8,128)(2,1)S(1)}, bf16[2,128,2048]{2,1,0:T(8,128)(2,1)S(1)}, u32[]{:S(2)}, u32[]{:S(2)}) collective-permute-start(bf16[2,128,2048]{2,1,0:T(8,128)(2,1)S(1)} %get-tuple-element.68), channel_id=1, source_target_pairs={{0,24},{8,0},{16,8},{24,16},{1,25},{9,1},{17,9},{25,17},{2,26},{10... | collective-permute-start | bytes 3145736 | tf_op jit(solution)/shard_map/ppermute | solution.py:33
  59.2 5.7 %collective-permute-start.10 = (bf16[64,256]{1,0:T(8,128)(2,1)S(1)}, bf16[64,256]{1,0:T(8,128)(2,1)S(1)}, u32[]{:S(2)}, u32[]{:S(2)}) collective-permute-start(bf16[64,256]{1,0:T(8,128)(2,1)S(1)} %get-tuple-element.63), channel_id=1, source_target_pairs={{0,2},{1,3},{2,4},{3,5},{4,6},{5,7},{6,0},{7,1},{8,10},{9,11},{10,... | collective-permute-start | bytes 98312 | tf_op jit(solution)/shard_map/ppermute | solution.py:33
  60.8 5.9 %collective-permute-start.11 = (bf16[64,256]{1,0:T(8,128)(2,1)S(1)}, bf16[64,256]{1,0:T(8,128)(2,1)S(1)}, u32[]{:S(2)}, u32[]{:S(2)}) collective-permute-start(bf16[64,256]{1,0:T(8,128)(2,1)S(1)} %get-tuple-element.64), channel_id=1, source_target_pairs={{0,4},{1,5},{2,6},{3,7},{4,0},{5,1},{6,2},{7,3},{8,12},{9,13},{10,... | collective-permute-start | bytes 98312 | tf_op jit(solution)/shard_map/ppermute | solution.py:33
  64.9 3.9 %collective-permute-start.12 = (bf16[64,256]{1,0:T(8,128)(2,1)S(1)}, bf16[64,256]{1,0:T(8,128)(2,1)S(1)}, u32[]{:S(2)}, u32[]{:S(2)}) collective-permute-start(bf16[64,256]{1,0:T(8,128)(2,1)S(1)} %get-tuple-element.65), channel_id=1, source_target_pairs={{0,6},{1,7},{2,0},{3,1},{4,2},{5,3},{6,4},{7,5},{8,14},{9,15},{10,... | collective-permute-start | bytes 98312 | tf_op jit(solution)/shard_map/ppermute | solution.py:33
  78.5 27.6 %collective-permute-start.13 = (bf16[2,128,2048]{2,1,0:T(8,128)(2,1)S(1)}, bf16[2,128,2048]{2,1,0:T(8,128)(2,1)S(1)}, u32[]{:S(2)}, u32[]{:S(2)}) collective-permute-start(bf16[2,128,2048]{2,1,0:T(8,128)(2,1)S(1)} %get-tuple-element.67), channel_id=1, source_target_pairs={{0,24},{8,0},{16,8},{24,16},{1,25},{9,1},{17,9},{25,17},{2,26},{10... | collective-permute-start | bytes 3145736 | tf_op jit(solution)/shard_map/ppermute | solution.py:33
  80.4 11.9 %collective-permute-start.15 = (bf16[4,64,512]{2,1,0:T(8,128)(2,1)S(1)}, bf16[4,64,512]{2,1,0:T(8,128)(2,1)S(1)}, u32[]{:S(2)}, u32[]{:S(2)}) collective-permute-start(bf16[4,64,512]{2,1,0:T(8,128)(2,1)S(1)} %get-tuple-element.70), channel_id=1, source_target_pairs={{0,1},{1,0},{2,3},{3,2},{4,5},{5,4},{6,7},{7,6},{8,9},{9,8},{10,11... | collective-permute-start | bytes 786440 | tf_op jit(solution)/shard_map/ppermute | solution.py:33
  81.9 6.1 %collective-permute-start.16 = (bf16[64,512]{1,0:T(8,128)(2,1)S(1)}, bf16[64,512]{1,0:T(8,128)(2,1)S(1)}, u32[]{:S(2)}, u32[]{:S(2)}) collective-permute-start(bf16[64,512]{1,0:T(8,128)(2,1)S(1)} %get-tuple-element.72), channel_id=1, source_target_pairs={{0,2},{1,3},{2,4},{3,5},{4,6},{5,7},{6,0},{7,1},{8,10},{9,11},{10,... | collective-permute-start | bytes 196616 | tf_op jit(solution)/shard_map/ppermute | solution.py:33
  83.5 6.6 %collective-permute-start.17 = (bf16[64,512]{1,0:T(8,128)(2,1)S(1)}, bf16[64,512]{1,0:T(8,128)(2,1)S(1)}, u32[]{:S(2)}, u32[]{:S(2)}) collective-permute-start(bf16[64,512]{1,0:T(8,128)(2,1)S(1)} %get-tuple-element.73), channel_id=1, source_target_pairs={{0,4},{1,5},{2,6},{3,7},{4,0},{5,1},{6,2},{7,3},{8,12},{9,13},{10,... | collective-permute-start | bytes 196616 | tf_op jit(solution)/shard_map/ppermute | solution.py:33
  88.0 4.3 %collective-permute-start.18 = (bf16[64,512]{1,0:T(8,128)(2,1)S(1)}, bf16[64,512]{1,0:T(8,128)(2,1)S(1)}, u32[]{:S(2)}, u32[]{:S(2)}) collective-permute-start(bf16[64,512]{1,0:T(8,128)(2,1)S(1)} %get-tuple-element.74), channel_id=1, source_target_pairs={{0,6},{1,7},{2,0},{3,1},{4,2},{5,3},{6,4},{7,5},{8,14},{9,15},{10,... | collective-permute-start | bytes 196616 | tf_op jit(solution)/shard_map/ppermute | solution.py:33
  97.1 9.0 %collective-permute-start.19 = (bf16[4,64,256]{2,1,0:T(8,128)(2,1)S(1)}, bf16[4,64,256]{2,1,0:T(8,128)(2,1)S(1)}, u32[]{:S(2)}, u32[]{:S(2)}) collective-permute-start(bf16[4,64,256]{2,1,0:T(8,128)(2,1)S(1)} %get-tuple-element.77), channel_id=1, source_target_pairs={{0,1},{1,0},{2,3},{3,2},{4,5},{5,4},{6,7},{7,6},{8,9},{9,8},{10,11... | collective-permute-start | bytes 393224 | tf_op jit(solution)/shard_map/ppermute | solution.py:33
  97.7 6.1 %collective-permute-start.20 = (bf16[64,512]{1,0:T(8,128)(2,1)S(1)}, bf16[64,512]{1,0:T(8,128)(2,1)S(1)}, u32[]{:S(2)}, u32[]{:S(2)}) collective-permute-start(bf16[64,512]{1,0:T(8,128)(2,1)S(1)} %get-tuple-element.79), channel_id=1, source_target_pairs={{0,2},{1,3},{2,4},{3,5},{4,6},{5,7},{6,0},{7,1},{8,10},{9,11},{10,... | collective-permute-start | bytes 196616 | tf_op jit(solution)/shard_map/ppermute | solution.py:33
  98.1 7.1 %collective-permute-start.21 = (bf16[64,512]{1,0:T(8,128)(2,1)S(1)}, bf16[64,512]{1,0:T(8,128)(2,1)S(1)}, u32[]{:S(2)}, u32[]{:S(2)}) collective-permute-start(bf16[64,512]{1,0:T(8,128)(2,1)S(1)} %get-tuple-element.80), channel_id=1, source_target_pairs={{0,4},{1,5},{2,6},{3,7},{4,0},{5,1},{6,2},{7,3},{8,12},{9,13},{10,... | collective-permute-start | bytes 196616 | tf_op jit(solution)/shard_map/ppermute | solution.py:33
  101.8 4.3 %collective-permute-start.22 = (bf16[64,512]{1,0:T(8,128)(2,1)S(1)}, bf16[64,512]{1,0:T(8,128)(2,1)S(1)}, u32[]{:S(2)}, u32[]{:S(2)}) collective-permute-start(bf16[64,512]{1,0:T(8,128)(2,1)S(1)} %get-tuple-element.81), channel_id=1, source_target_pairs={{0,6},{1,7},{2,0},{3,1},{4,2},{5,3},{6,4},{7,5},{8,14},{9,15},{10,... | collective-permute-start | bytes 196616 | tf_op jit(solution)/shard_map/ppermute | solution.py:33
  110.9 8.9 %collective-permute-start.23 = (bf16[4,64,256]{2,1,0:T(8,128)(2,1)S(1)}, bf16[4,64,256]{2,1,0:T(8,128)(2,1)S(1)}, u32[]{:S(2)}, u32[]{:S(2)}) collective-permute-start(bf16[4,64,256]{2,1,0:T(8,128)(2,1)S(1)} %get-tuple-element.84), channel_id=1, source_target_pairs={{0,1},{1,0},{2,3},{3,2},{4,5},{5,4},{6,7},{7,6},{8,9},{9,8},{10,11... | collective-permute-start | bytes 393224 | tf_op jit(solution)/shard_map/ppermute | solution.py:33
  112.5 5.7 %collective-permute-start.24 = (bf16[64,256]{1,0:T(8,128)(2,1)S(1)}, bf16[64,256]{1,0:T(8,128)(2,1)S(1)}, u32[]{:S(2)}, u32[]{:S(2)}) collective-permute-start(bf16[64,256]{1,0:T(8,128)(2,1)S(1)} %get-tuple-element.86), channel_id=1, source_target_pairs={{0,2},{1,3},{2,4},{3,5},{4,6},{5,7},{6,0},{7,1},{8,10},{9,11},{10,... | collective-permute-start | bytes 98312 | tf_op jit(solution)/shard_map/ppermute | solution.py:33
  112.8 5.4 %collective-permute-start.25 = (bf16[64,256]{1,0:T(8,128)(2,1)S(1)}, bf16[64,256]{1,0:T(8,128)(2,1)S(1)}, u32[]{:S(2)}, u32[]{:S(2)}) collective-permute-start(bf16[64,256]{1,0:T(8,128)(2,1)S(1)} %get-tuple-element.87), channel_id=1, source_target_pairs={{0,4},{1,5},{2,6},{3,7},{4,0},{5,1},{6,2},{7,3},{8,12},{9,13},{10,... | collective-permute-start | bytes 98312 | tf_op jit(solution)/shard_map/ppermute | solution.py:33
  115.5 4.3 %collective-permute-start.26 = (bf16[64,256]{1,0:T(8,128)(2,1)S(1)}, bf16[64,256]{1,0:T(8,128)(2,1)S(1)}, u32[]{:S(2)}, u32[]{:S(2)}) collective-permute-start(bf16[64,256]{1,0:T(8,128)(2,1)S(1)} %get-tuple-element.88), channel_id=1, source_target_pairs={{0,6},{1,7},{2,0},{3,1},{4,2},{5,3},{6,4},{7,5},{8,14},{9,15},{10,... | collective-permute-start | bytes 98312 | tf_op jit(solution)/shard_map/ppermute | solution.py:33
  121.1 5.8 %collective-permute-start.27 = (bf16[64,256]{1,0:T(8,128)(2,1)S(1)}, bf16[64,256]{1,0:T(8,128)(2,1)S(1)}, u32[]{:S(2)}, u32[]{:S(2)}) collective-permute-start(bf16[64,256]{1,0:T(8,128)(2,1)S(1)} %get-tuple-element.91), channel_id=1, source_target_pairs={{0,2},{1,3},{2,4},{3,5},{4,6},{5,7},{6,0},{7,1},{8,10},{9,11},{10,... | collective-permute-start | bytes 98312 | tf_op jit(solution)/shard_map/ppermute | solution.py:33
  122.1 5.4 %collective-permute-start.28 = (bf16[64,256]{1,0:T(8,128)(2,1)S(1)}, bf16[64,256]{1,0:T(8,128)(2,1)S(1)}, u32[]{:S(2)}, u32[]{:S(2)}) collective-permute-start(bf16[64,256]{1,0:T(8,128)(2,1)S(1)} %get-tuple-element.92), channel_id=1, source_target_pairs={{0,4},{1,5},{2,6},{3,7},{4,0},{5,1},{6,2},{7,3},{8,12},{9,13},{10,... | collective-permute-start | bytes 98312 | tf_op jit(solution)/shard_map/ppermute | solution.py:33
  124.2 3.9 %collective-permute-start.29 = (bf16[64,256]{1,0:T(8,128)(2,1)S(1)}, bf16[64,256]{1,0:T(8,128)(2,1)S(1)}, u32[]{:S(2)}, u32[]{:S(2)}) collective-permute-start(bf16[64,256]{1,0:T(8,128)(2,1)S(1)} %get-tuple-element.93), channel_id=1, source_target_pairs={{0,6},{1,7},{2,0},{3,1},{4,2},{5,3},{6,4},{7,5},{8,14},{9,15},{10,... | collective-permute-start | bytes 98312 | tf_op jit(solution)/shard_map/ppermute | solution.py:33

commit v8 on v7

--- a/solution.py
+++ b/solution.py
@@ -113,10 +113,11 @@
     place, outer = lax.rem(me, fold), lax.div(me, fold)
     if plan.part:
         bands_ref, there_ref = take(2)
-    folded = take(fold) if plan.folding else None
+    folded = [take(fold) for _ in plan.folding]
     arrived = [take(depth) for _ in plan.adding]
     if plan.adding and plan.placed:
         take(1)
+    take(plan.after)
     outs = take(fold) if plan.part else None
     sends = take(depth) if plan.folding else None
     result_ref = take(1)[0] if plan.adding else None
@@ -158,12 +159,15 @@
             copy.start()
     if plan.adding:
         sum_buf, placed_sem = take(2)
-        add_slot, add_start, _ = plan.adding[0]
-        for (_, start, _), arrays in zip(plan.adding, arrived):
+        add_slot, add_start, _ = plan.adding[0][0]
+        for batch, arrays in zip(plan.adding, arrived):
             total = arrays[0][...]
             for array in arrays[1:]:
                 total = total + array[...].astype(jnp.float32)
-            put_sum(sum_buf, start - add_start, total)
+            column = 0
+            for _, start, width in batch:
+                put_sum(sum_buf, start - add_start, total[:, column : column + 2 * width])
+                column += 2 * width
         add_point = table_ref[add_slot * stride].astype(jnp.int32)
         columns = pl.ds(add_start, sum_buf.shape[2])
         placing = pltpu.make_async_copy(
@@ -173,10 +177,14 @@
     if plan.folding:
         for distance, send_ref in enumerate(sends):
             target = lax.rem(outer + distance, depth)
-            total = folded[0][target]
-            for array in folded[1:]:
-                total = total + array[target].astype(jnp.float32)
-            send_ref[...] = total.astype(send_ref.dtype)
+            column = 0
+            for arrays in folded:
+                total = arrays[0][target]
+                for array in arrays[1:]:
+                    total = total + array[target].astype(jnp.float32)
+                columns = slice(column, column + total.shape[1])
+                send_ref[:, columns] = total.astype(send_ref.dtype)
+                column += total.shape[1]
     if plan.part:
         near_into(near_buf, there_ref, table_ref, base, planes)
         dims = (((1,), (1,)), ((), ()))
@@ -225,9 +233,10 @@
     adding: tuple
     placed: bool
     later: tuple
-
-
-def step(plan, table, bands, there, folded, arrived, result):
+    after: int
+
+
+def step(plan, table, bands, there, folded, arrived, result, after):
     rows, _, _, nbands = plan.shape
     fold, depth = plan.fold, plan.depth
     points = bands.shape[3]
@@ -254,11 +263,11 @@
             pltpu.SemaphoreType.DMA((nbands // BLOCK, 2)),
         ]
     if plan.folding:
-        operands += folded
-        in_specs += [vmem] * fold
-        out_shape += [
-            jax.ShapeDtypeStruct((rows, 2 * plan.folding[2]), kind(i)) for i in range(depth)
-        ]
+        for arrays in folded:
+            operands += arrays
+            in_specs += [vmem] * fold
+        wide = sum(2 * width for _, _, width in plan.folding)
+        out_shape += [jax.ShapeDtypeStruct((rows, wide), kind(i)) for i in range(depth)]
         out_specs += [vmem] * depth
     if plan.later:
         scratch += [
@@ -275,8 +284,10 @@
             in_specs.append(hbm)
         out_shape.append(jax.ShapeDtypeStruct(plan.shape, jnp.float32))
         out_specs.append(hbm)
-        lanes = sum(width for _, _, width in plan.adding)
+        lanes = sum(width for batch in plan.adding for _, _, width in batch)
         scratch += [pltpu.VMEM((rows, 2, lanes), jnp.float32), pltpu.SemaphoreType.DMA]
+    operands += after
+    in_specs += [pl.BlockSpec(memory_space=pl.ANY)] * len(after)
     if plan.later:
         out_shape.append(jax.ShapeDtypeStruct((2, plan.later[2], points), bands.dtype))
         out_specs.append(hbm)
@@ -301,21 +312,36 @@
 
 
 def cuts(nbands, first):
-    half, quarter = nbands // 2, nbands // 4
-    widths = [quarter, quarter, half] if first else [half, quarter, quarter]
+    eighth = nbands // 8
+    widths = [4 * eighth, 4 * eighth] if first else [3 * eighth, 3 * eighth, 2 * eighth]
     starts = [sum(widths[:i]) for i in range(len(widths))]
     return list(zip(starts, widths))
 
 
-def adding_jobs(parts):
-    jobs = {}
-    group = ()
-    for index, part in enumerate(parts):
-        group += (part,)
-        if sum(width for _, _, width in group) % LANES == 0:
-            jobs[index] = group
-            group = ()
-    return jobs
+def schedule(parts):
+    kernels = []
+    waiting = []
+    for part in parts[:-2]:
+        kernels.append((part, (), ()))
+        ready = waiting_block(waiting)
+        for batch in ready:
+            waiting.remove(batch)
+        kernels.append((None, (part,), ready))
+        waiting.append((part,))
+    kernels.append((parts[-2], (), ()))
+    kernels.append((parts[-1], (), ()))
+    kernels.append((None, tuple(parts[-2:]), ()))
+    kernels.append((None, (), tuple(waiting) + (tuple(parts[-2:]),)))
+    return kernels
+
+
+def waiting_block(waiting):
+    total = 0
+    for count, batch in enumerate(waiting, 1):
+        total += sum(width for _, _, width in batch)
+        if total % LANES == 0:
+            return tuple(waiting[:count])
+    return ()
 
 
 def body(bands, nbr_slot, gshift):
@@ -347,24 +373,26 @@
     shape = (rows, k_dev, 2, nbands)
     depth = min(OUTER, grid_count)
     fold = grid_count // depth
-    jobs = adding_jobs(parts)
     folded, arrived = {}, {}
     result = None
-    for index in range(len(parts) + 2):
-        part = parts[index] if index < len(parts) else None
-        folding = parts[index - 1] if 0 <= index - 1 < len(parts) else None
-        adding = jobs.get(index - 2, ())
-        later = parts[index + AHEAD] if index + AHEAD < len(parts) else None
-        plan = Plan(shape, fold, depth, part, folding, adding, result is not None, later)
+    after = []
+    for part, folding, adding in schedule(parts):
+        index = parts.index(part) + AHEAD if part else len(parts)
+        later = parts[index] if index < len(parts) else None
+        plan = Plan(
+            shape, fold, depth, part, folding, adding, result is not None, later, len(after)
+        )
         terms, sends, result, piece = step(
             plan,
             table,
             bands,
-            theres[index] if part else None,
-            folded.pop(folding, None),
-            [arrived.pop(done) for done in adding],
+            theres[parts.index(part)] if part else None,
+            [folded.pop(done) for done in folding],
+            [arrived.pop(batch) for batch in adding],
             result,
+            after,
         )
+        after = []
         if later:
             theres.append(shifted(piece, "ka", -1))
         if part:
@@ -375,6 +403,7 @@
             arrived[folding] = [sends[0]] + [
                 shifted(sends[i], "ga", i, fold) for i in range(1, depth)
             ]
+            after = [sends[1]]
     return result
 
 

time: 130 us -> 124 us (0.954)
  starting transfers between devices: 47.2 us -> 25.4 us
  waiting for transfers between devices: 42.8 us -> 59 us
    ppermute x30 -> x22, starting transfers between devices: 47.2 us -> 25.4 us  [shifted(): return lax.ppermute(block, axis, route)]
    ppermute x30 -> x22, waiting for transfers between devices: 42.8 us -> 59 us  [shifted(): return lax.ppermute(block, axis, route)]
    pallas_call x8 -> x10, Pallas kernels: 36.1 us -> 34.3 us  [step(): pl.pallas_call(functools.partial(step_kernel, plan), in_specs=in_specs, o...]
    pallas_call x2, Pallas kernels: 2.54 us -> 4.2 us  [piece_of(): pl.pallas_call(functools.partial(piece_kernel, slot, start), in_specs=[pl...]
  transfers between devices with their start and end apart: 30 -> 22, of which waited for: 20 -> 10; matrix products, arithmetic and copies ran while one was open for 0% -> 0% of each run, Pallas kernels for 23% -> 29%
where the time goes in v8:
time: 124 us
  waiting for transfers between devices  59 us (48%)
  Pallas kernels  38.5 us (31%)
  starting transfers between devices  25.4 us (20%)
    ppermute x22, waiting for transfers between devices, shifted(): return lax.ppermute(block, axis, route)  59 us
    pallas_call x10, Pallas kernels, step(): pl.pallas_call(functools.partial(step_kernel, plan), in_specs=in_specs, o...  34.3 us
    ppermute x22, starting transfers between devices, shifted(): return lax.ppermute(block, axis, route)  25.4 us
    pallas_call x2, Pallas kernels, piece_of(): pl.pallas_call(functools.partial(piece_kernel, slot, start), in_specs=[pl...  4.2 us
  transfers between devices with their start and end apart: 22, of which 10 were waited for; matrix products, arithmetic and copies ran while one was open for 0% of the time, Pallas kernels for 29%

profile of v8, /device:TPU:0, one launch (start us, length us, event | category | flops | bytes accessed | tf_op | source)
XLA Modules:
  0.0 123.8 jit_solution(5597449539320724663)
XLA Ops:
  0.0 1.6 %piece_of.2.rest_0_ = bf16[2,256,2048]{2,1,0:T(8,128)(2,1)S(1)} custom-call(bf16[2,2,512,2048]{3,2,1,0:T(8,128)(2,1)} %refs_0_.9), custom_call_target="tpu_custom_call" | custom-call | flops 1000 | bytes 1000 | tf_op jit(solution)/shard_map/piece_of/pallas_call | solution.py:59
  1.7 2.5 %collective-permute-start = (bf16[2,256,2048]{2,1,0:T(8,128)(2,1)S(1)}, bf16[2,256,2048]{2,1,0:T(8,128)(2,1)}, u32[]{:S(2)}, u32[]{:S(2)}) collective-permute-start(bf16[2,256,2048]{2,1,0:T(8,128)(2,1)S(1)} %piece_of.2.rest_0_), channel_id=1, source_target_pairs={{0,24},{8,0},{16,8},{24,16},{1,25},{9,1},{17,9},{25,17},{2,26},{10... | collective-permute-start | bytes 6291464 | tf_op jit(solution)/shard_map/ppermute | solution.py:33
  4.1 2.6 %piece_of.3 = bf16[2,256,2048]{2,1,0:T(8,128)(2,1)} custom-call(bf16[2,2,512,2048]{3,2,1,0:T(8,128)(2,1)} %refs_0_.9, bf16[2,256,2048]{2,1,0:T(8,128)(2,1)S(1)} %piece_of.2.rest_0_), custom_call_target="tpu_custom_call" | custom-call | flops 1000 | bytes 1000 | tf_op jit(solution)/shard_map/piece_of/pallas_call | solution.py:59
  6.7 0.7 collective-permute-start.2
  7.4 0.1 select_reduce_fusion.1
  7.6 0.1 copy.6
  7.7 0.1 fusion.4
  7.8 0.1 pad_maximum_fusion
  7.9 0.1 reshape.28
  8.0 0.1 pad_maximum_fusion.1.table_ref
  8.1 19.6 %collective-permute-done.refs_1_ = bf16[2,256,2048]{2,1,0:T(8,128)(2,1)} collective-permute-done((bf16[2,256,2048]{2,1,0:T(8,128)(2,1)S(1)}, bf16[2,256,2048]{2,1,0:T(8,128)(2,1)}, u32[]{:S(2)}, u32[]{:S(2)}) %collective-permute-start) | collective-permute-done | bytes 2097184 | tf_op jit(solution)/shard_map/ppermute | solution.py:33
  27.7 7.1 %step.10 = (f32[4,64,512]{2,1,0:T(8,128)S(1)}, bf16[4,64,512]{2,1,0:T(8,128)(2,1)S(1)}, bf16[2,192,2048]{2,1,0:T(8,128)(2,1)S(1)}) custom-call(f32[11]{0:T(128)S(1)} %pad_maximum_fusion.1.table_ref, bf16[2,2,512,2048]{3,2,1,0:T(8,128)(2,1)} %refs_0_.9, bf16[2,256,2048]{2,1,0:T(8,128)(2,1)} %collective-permute-done.refs_1_), custom_call_target="tpu_custom_call" | custom-call | flops 1000 | bytes 1000 | tf_op jit(solution)/shard_map/step/pallas_call | solution.py:295
  34.8 2.1 %collective-permute-start.1 = (bf16[2,192,2048]{2,1,0:T(8,128)(2,1)S(1)}, bf16[2,192,2048]{2,1,0:T(8,128)(2,1)S(1)}, u32[]{:S(2)}, u32[]{:S(2)}) collective-permute-start(bf16[2,192,2048]{2,1,0:T(8,128)(2,1)S(1)} %get-tuple-element.36), channel_id=1, source_target_pairs={{0,24},{8,0},{16,8},{24,16},{1,25},{9,1},{17,9},{25,17},{2,26},{10... | collective-permute-start | bytes 4718600 | tf_op jit(solution)/shard_map/ppermute | solution.py:33
  36.9 1.5 %collective-permute-start.3 = (bf16[4,64,512]{2,1,0:T(8,128)(2,1)S(1)}, bf16[4,64,512]{2,1,0:T(8,128)(2,1)S(1)}, u32[]{:S(2)}, u32[]{:S(2)}) collective-permute-start(bf16[4,64,512]{2,1,0:T(8,128)(2,1)S(1)} %get-tuple-element.38), channel_id=1, source_target_pairs={{0,1},{1,0},{2,3},{3,2},{4,5},{5,4},{6,7},{7,6},{8,9},{9,8},{10,11... | collective-permute-start | bytes 786440 | tf_op jit(solution)/shard_map/ppermute | solution.py:33
  38.4 5.7 %collective-permute-done.3.refs_1_ = bf16[4,64,512]{2,1,0:T(8,128)(2,1)S(1)} collective-permute-done((bf16[4,64,512]{2,1,0:T(8,128)(2,1)S(1)}, bf16[4,64,512]{2,1,0:T(8,128)(2,1)S(1)}, u32[]{:S(2)}, u32[]{:S(2)}) %collective-permute-start.3) | collective-permute-done | bytes 262176 | tf_op jit(solution)/shard_map/ppermute | solution.py:33
  44.1 0.6 step.11
  44.7 5.6 %collective-permute-done.2.refs_1_ = bf16[2,256,2048]{2,1,0:T(8,128)(2,1)} collective-permute-done((bf16[2,256,2048]{2,1,0:T(8,128)(2,1)}, bf16[2,256,2048]{2,1,0:T(8,128)(2,1)}, u32[]{:S(2)}, u32[]{:S(2)}) %collective-permute-start.2) | collective-permute-done | bytes 2097184 | tf_op jit(solution)/shard_map/ppermute | solution.py:33
  50.3 7.1 %step.12 = (f32[4,64,512]{2,1,0:T(8,128)S(1)}, bf16[4,64,512]{2,1,0:T(8,128)(2,1)S(1)}, bf16[2,192,2048]{2,1,0:T(8,128)(2,1)S(1)}) custom-call(f32[11]{0:T(128)S(1)} %pad_maximum_fusion.1.table_ref, bf16[2,2,512,2048]{3,2,1,0:T(8,128)(2,1)} %refs_0_.9, bf16[2,256,2048]{2,1,0:T(8,128)(2,1)} %collective-permute-done.2.refs_1_, ...), custom_call_target="tpu_custom_call" | custom-call | flops 1000 | bytes 1000 | tf_op jit(solution)/shard_map/step/pallas_call | solution.py:295
  57.4 2.0 %collective-permute-start.15 = (bf16[2,192,2048]{2,1,0:T(8,128)(2,1)S(1)}, bf16[2,192,2048]{2,1,0:T(8,128)(2,1)S(1)}, u32[]{:S(2)}, u32[]{:S(2)}) collective-permute-start(bf16[2,192,2048]{2,1,0:T(8,128)(2,1)S(1)} %get-tuple-element.56), channel_id=1, source_target_pairs={{0,24},{8,0},{16,8},{24,16},{1,25},{9,1},{17,9},{25,17},{2,26},{10... | collective-permute-start | bytes 4718600 | tf_op jit(solution)/shard_map/ppermute | solution.py:33
  59.3 1.5 %collective-permute-start.4 = (bf16[4,64,512]{2,1,0:T(8,128)(2,1)S(1)}, bf16[4,64,512]{2,1,0:T(8,128)(2,1)S(1)}, u32[]{:S(2)}, u32[]{:S(2)}) collective-permute-start(bf16[4,64,512]{2,1,0:T(8,128)(2,1)S(1)} %get-tuple-element.41), channel_id=1, source_target_pairs={{0,1},{1,0},{2,3},{3,2},{4,5},{5,4},{6,7},{7,6},{8,9},{9,8},{10,11... | collective-permute-start | bytes 786440 | tf_op jit(solution)/shard_map/ppermute | solution.py:33
  60.8 2.6 %collective-permute-start.6 = (bf16[64,512]{1,0:T(8,128)(2,1)S(1)}, bf16[64,512]{1,0:T(8,128)(2,1)S(1)}, u32[]{:S(2)}, u32[]{:S(2)}) collective-permute-start(bf16[64,512]{1,0:T(8,128)(2,1)S(1)} %get-tuple-element.43), channel_id=1, source_target_pairs={{0,4},{1,5},{2,6},{3,7},{4,0},{5,1},{6,2},{7,3},{8,12},{9,13},{10,... | collective-permute-start | bytes 196616 | tf_op jit(solution)/shard_map/ppermute | solution.py:33
  63.4 1.3 %collective-permute-start.7 = (bf16[64,512]{1,0:T(8,128)(2,1)S(1)}, bf16[64,512]{1,0:T(8,128)(2,1)S(1)}, u32[]{:S(2)}, u32[]{:S(2)}) collective-permute-start(bf16[64,512]{1,0:T(8,128)(2,1)S(1)} %get-tuple-element.44), channel_id=1, source_target_pairs={{0,6},{1,7},{2,0},{3,1},{4,2},{5,3},{6,4},{7,5},{8,14},{9,15},{10,... | collective-permute-start | bytes 196616 | tf_op jit(solution)/shard_map/ppermute | solution.py:33
  64.8 2.4 %collective-permute-done.6.refs_4_ = bf16[64,512]{1,0:T(8,128)(2,1)S(1)} collective-permute-done((bf16[64,512]{1,0:T(8,128)(2,1)S(1)}, bf16[64,512]{1,0:T(8,128)(2,1)S(1)}, u32[]{:S(2)}, u32[]{:S(2)}) %collective-permute-start.6) | collective-permute-done | bytes 65568 | tf_op jit(solution)/shard_map/ppermute | solution.py:33
  67.2 0.9 collective-permute-start.5
  68.1 5.6 %collective-permute-done.5.refs_3_ = bf16[64,512]{1,0:T(8,128)(2,1)S(1)} collective-permute-done((bf16[64,512]{1,0:T(8,128)(2,1)S(1)}, bf16[64,512]{1,0:T(8,128)(2,1)S(1)}, u32[]{:S(2)}, u32[]{:S(2)}) %collective-permute-start.5) | collective-permute-done | bytes 65568 | tf_op jit(solution)/shard_map/ppermute | solution.py:33
  73.6 1.3 %step.13 = (f32[64,512]{1,0:T(8,128)S(1)}, bf16[64,512]{1,0:T(8,128)(2,1)S(1)}, bf16[64,512]{1,0:T(8,128)(2,1)S(1)}, bf16[64,512]{1,0:T(8,128)(2,1)S(1)}, f32[64,2,2,512]{3,2,1,0:T(2,128)}) custom-call(f32[11]{0:T(128)S(1)} %pad_maximum_fusion.1.table_ref, f32[4,64,512]{2,1,0:T(8,128)S(1)} %get-tuple-element.40.refs_0_, ...), custom_call_target="tpu_custom_call" | custom-call | flops 1000 | bytes 1000 | tf_op jit(solution)/shard_map/step/pallas_call | solution.py:295
  74.9 5.1 %step.14 = (f32[4,64,384]{2,1,0:T(8,128)S(1)}, bf16[4,64,384]{2,1,0:T(8,128)(2,1)S(1)}, bf16[2,128,2048]{2,1,0:T(8,128)(2,1)S(1)}) custom-call(f32[11]{0:T(128)S(1)} %pad_maximum_fusion.1.table_ref, bf16[2,2,512,2048]{3,2,1,0:T(8,128)(2,1)} %refs_0_.9, bf16[2,192,2048]{2,1,0:T(8,128)(2,1)S(1)} %collective-permute-done.1.refs_1_, ...), custom_call_target="tpu_custom_call" | custom-call | flops 1000 | bytes 1000 | tf_op jit(solution)/shard_map/step/pallas_call | solution.py:295
  80.0 0.1 collective-permute-start.17
  80.1 0.6 collective-permute-start.8
  80.7 0.2 collective-permute-start.10
  80.9 1.8 %collective-permute-start.11 = (bf16[64,512]{1,0:T(8,128)(2,1)S(1)}, bf16[64,512]{1,0:T(8,128)(2,1)S(1)}, u32[]{:S(2)}, u32[]{:S(2)}) collective-permute-start(bf16[64,512]{1,0:T(8,128)(2,1)S(1)} %get-tuple-element.50), channel_id=1, source_target_pairs={{0,6},{1,7},{2,0},{3,1},{4,2},{5,3},{6,4},{7,5},{8,14},{9,15},{10,... | collective-permute-start | bytes 196616 | tf_op jit(solution)/shard_map/ppermute | solution.py:33
  82.7 3.9 %collective-permute-done.10.refs_4_ = bf16[64,512]{1,0:T(8,128)(2,1)S(1)} collective-permute-done((bf16[64,512]{1,0:T(8,128)(2,1)S(1)}, bf16[64,512]{1,0:T(8,128)(2,1)S(1)}, u32[]{:S(2)}, u32[]{:S(2)}) %collective-permute-start.10) | collective-permute-done | bytes 65568 | tf_op jit(solution)/shard_map/ppermute | solution.py:33
  86.7 0.3 collective-permute-start.9
  87.0 5.7 %collective-permute-done.9.refs_3_ = bf16[64,512]{1,0:T(8,128)(2,1)S(1)} collective-permute-done((bf16[64,512]{1,0:T(8,128)(2,1)S(1)}, bf16[64,512]{1,0:T(8,128)(2,1)S(1)}, u32[]{:S(2)}, u32[]{:S(2)}) %collective-permute-start.9) | collective-permute-done | bytes 65568 | tf_op jit(solution)/shard_map/ppermute | solution.py:33
  92.7 1.3 %step.15 = (f32[64,384]{1,0:T(8,128)S(1)}, bf16[64,384]{1,0:T(8,128)(2,1)S(1)}, bf16[64,384]{1,0:T(8,128)(2,1)S(1)}, bf16[64,384]{1,0:T(8,128)(2,1)S(1)}, f32[64,2,2,512]{3,2,1,0:T(2,128)}) custom-call(f32[11]{0:T(128)S(1)} %pad_maximum_fusion.1.table_ref, f32[4,64,384]{2,1,0:T(8,128)S(1)} %get-tuple-element.46.refs_0_, ...), custom_call_target="tpu_custom_call", output_to_operand_aliasing={{4}: (7, {})} | custom-call | flops 1000 | bytes 1000 | tf_op jit(solution)/shard_map/step/pallas_call | solution.py:295
  94.0 5.0 %step.16 = (f32[4,64,384]{2,1,0:T(8,128)S(1)}, bf16[4,64,384]{2,1,0:T(8,128)(2,1)S(1)}) custom-call(f32[11]{0:T(128)S(1)} %pad_maximum_fusion.1.table_ref, bf16[2,2,512,2048]{3,2,1,0:T(8,128)(2,1)} %refs_0_.9, bf16[2,192,2048]{2,1,0:T(8,128)(2,1)S(1)} %collective-permute-done.15.refs_1_, bf16[64,384]{1,0:T(8,128)(2,1)S(1)} %get-tuple-element.53.refs_2_), custom_call_target="tpu_custom_call" | custom-call | flops 1000 | bytes 1000 | tf_op jit(solution)/shard_map/step/pallas_call | solution.py:295
  99.0 1.5 %collective-permute-start.16 = (bf16[4,64,384]{2,1,0:T(8,128)(2,1)S(1)}, bf16[4,64,384]{2,1,0:T(8,128)(2,1)S(1)}, u32[]{:S(2)}, u32[]{:S(2)}) collective-permute-start(bf16[4,64,384]{2,1,0:T(8,128)(2,1)S(1)} %get-tuple-element.58), channel_id=1, source_target_pairs={{0,1},{1,0},{2,3},{3,2},{4,5},{5,4},{6,7},{7,6},{8,9},{9,8},{10,11... | collective-permute-start | bytes 589832 | tf_op jit(solution)/shard_map/ppermute | solution.py:33
  100.6 4.7 %step.17 = (f32[4,64,256]{2,1,0:T(8,128)S(1)}, bf16[4,64,256]{2,1,0:T(8,128)(2,1)S(1)}) custom-call(f32[11]{0:T(128)S(1)} %pad_maximum_fusion.1.table_ref, bf16[2,2,512,2048]{3,2,1,0:T(8,128)(2,1)} %refs_0_.9, bf16[2,128,2048]{2,1,0:T(8,128)(2,1)S(1)} %collective-permute-done.17.refs_1_), custom_call_target="tpu_custom_call" | custom-call | flops 1000 | bytes 1000 | tf_op jit(solution)/shard_map/step/pallas_call | solution.py:295
  105.3 0.6 collective-permute-start.18
  106.0 4.4 %collective-permute-done.18.refs_3_ = bf16[4,64,256]{2,1,0:T(8,128)(2,1)S(1)} collective-permute-done((bf16[4,64,256]{2,1,0:T(8,128)(2,1)S(1)}, bf16[4,64,256]{2,1,0:T(8,128)(2,1)S(1)}, u32[]{:S(2)}, u32[]{:S(2)}) %collective-permute-start.18) | collective-permute-done | bytes 131104 | tf_op jit(solution)/shard_map/ppermute | solution.py:33
  110.4 0.6 step.18
  111.0 0.1 collective-permute-start.20
  111.1 1.4 %collective-permute-start.21 = (bf16[64,640]{1,0:T(8,128)(2,1)S(1)}, bf16[64,640]{1,0:T(8,128)(2,1)S(1)}, u32[]{:S(2)}, u32[]{:S(2)}) collective-permute-start(bf16[64,640]{1,0:T(8,128)(2,1)S(1)} %get-tuple-element.65), channel_id=1, source_target_pairs={{0,6},{1,7},{2,0},{3,1},{4,2},{5,3},{6,4},{7,5},{8,14},{9,15},{10,... | collective-permute-start | bytes 245768 | tf_op jit(solution)/shard_map/ppermute | solution.py:33
  112.5 0.7 collective-permute-start.19
  113.2 3.1 %collective-permute-start.14 = (bf16[64,384]{1,0:T(8,128)(2,1)S(1)}, bf16[64,384]{1,0:T(8,128)(2,1)S(1)}, u32[]{:S(2)}, u32[]{:S(2)}) collective-permute-start(bf16[64,384]{1,0:T(8,128)(2,1)S(1)} %get-tuple-element.55), channel_id=1, source_target_pairs={{0,6},{1,7},{2,0},{3,1},{4,2},{5,3},{6,4},{7,5},{8,14},{9,15},{10,... | collective-permute-start | bytes 147464 | tf_op jit(solution)/shard_map/ppermute | solution.py:33
  116.3 1.7 %collective-permute-done.14.refs_3_ = bf16[64,384]{1,0:T(8,128)(2,1)S(1)} collective-permute-done((bf16[64,384]{1,0:T(8,128)(2,1)S(1)}, bf16[64,384]{1,0:T(8,128)(2,1)S(1)}, u32[]{:S(2)}, u32[]{:S(2)}) %collective-permute-start.14) | collective-permute-done | bytes 49184 | tf_op jit(solution)/shard_map/ppermute | solution.py:33
  118.0 4.1 %collective-permute-done.12.refs_1_ = bf16[64,384]{1,0:T(8,128)(2,1)S(1)} collective-permute-done((bf16[64,384]{1,0:T(8,128)(2,1)S(1)}, bf16[64,384]{1,0:T(8,128)(2,1)S(1)}, u32[]{:S(2)}, u32[]{:S(2)}) %collective-permute-start.12) | collective-permute-done | bytes 49184 | tf_op jit(solution)/shard_map/ppermute | solution.py:33
  122.2 1.5 %step.19 = f32[64,2,2,512]{3,2,1,0:T(2,128)} custom-call(f32[11]{0:T(128)S(1)} %pad_maximum_fusion.1.table_ref, f32[64,384]{1,0:T(8,128)S(1)} %get-tuple-element.52.refs_0_, bf16[64,384]{1,0:T(8,128)(2,1)S(1)} %collective-permute-done.12.refs_1_, bf16[64,384]{1,0:T(8,128)(2,1)S(1)} %collective-permute-done.13.refs_2_, ...), custom_call_target="tpu_custom_call", output_to_operand_aliasing={{}: (9, {})} | custom-call | flops 1000 | bytes 1000 | tf_op jit(solution)/shard_map/step/pallas_call | solution.py:295
  (20 shorter events, 0.1 us)
Async XLA Ops:
  1.7 5.8 %copy-start = (s32[2]{0:T(128)S(1)}, s32[2]{0:T(128)}, u32[]{:S(2)}) copy-start(s32[2]{0:T(128)} %param.4) | copy-start | bytes 28
  1.7 5.8 %copy-start.1 = (s32[2]{0:T(128)S(1)}, s32[2]{0:T(128)}, u32[]{:S(2)}) copy-start(s32[2]{0:T(128)} %param.5) | copy-start | bytes 28
  1.7 26.0 %collective-permute-start = (bf16[2,256,2048]{2,1,0:T(8,128)(2,1)S(1)}, bf16[2,256,2048]{2,1,0:T(8,128)(2,1)}, u32[]{:S(2)}, u32[]{:S(2)}) collective-permute-start(bf16[2,256,2048]{2,1,0:T(8,128)(2,1)S(1)} %piece_of.2.rest_0_), channel_id=1, source_target_pairs={{0,24},{8,0},{16,8},{24,16},{1,25},{9,1},{17,9},{25,17},{2,26},{10... | collective-permute-start | bytes 6291464 | tf_op jit(solution)/shard_map/ppermute | solution.py:33
  6.7 43.6 %collective-permute-start.2 = (bf16[2,256,2048]{2,1,0:T(8,128)(2,1)}, bf16[2,256,2048]{2,1,0:T(8,128)(2,1)}, u32[]{:S(2)}, u32[]{:S(2)}) collective-permute-start(bf16[2,256,2048]{2,1,0:T(8,128)(2,1)} %piece_of.3), channel_id=1, source_target_pairs={{0,24},{8,0},{16,8},{24,16},{1,25},{9,1},{17,9},{25,17},{2,26},{10... | collective-permute-start | bytes 6291464 | tf_op jit(solution)/shard_map/ppermute | solution.py:33
  34.8 40.1 %collective-permute-start.1 = (bf16[2,192,2048]{2,1,0:T(8,128)(2,1)S(1)}, bf16[2,192,2048]{2,1,0:T(8,128)(2,1)S(1)}, u32[]{:S(2)}, u32[]{:S(2)}) collective-permute-start(bf16[2,192,2048]{2,1,0:T(8,128)(2,1)S(1)} %get-tuple-element.36), channel_id=1, source_target_pairs={{0,24},{8,0},{16,8},{24,16},{1,25},{9,1},{17,9},{25,17},{2,26},{10... | collective-permute-start | bytes 4718600 | tf_op jit(solution)/shard_map/ppermute | solution.py:33
  36.9 7.2 %collective-permute-start.3 = (bf16[4,64,512]{2,1,0:T(8,128)(2,1)S(1)}, bf16[4,64,512]{2,1,0:T(8,128)(2,1)S(1)}, u32[]{:S(2)}, u32[]{:S(2)}) collective-permute-start(bf16[4,64,512]{2,1,0:T(8,128)(2,1)S(1)} %get-tuple-element.38), channel_id=1, source_target_pairs={{0,1},{1,0},{2,3},{3,2},{4,5},{5,4},{6,7},{7,6},{8,9},{9,8},{10,11... | collective-permute-start | bytes 786440 | tf_op jit(solution)/shard_map/ppermute | solution.py:33
  57.4 36.6 %collective-permute-start.15 = (bf16[2,192,2048]{2,1,0:T(8,128)(2,1)S(1)}, bf16[2,192,2048]{2,1,0:T(8,128)(2,1)S(1)}, u32[]{:S(2)}, u32[]{:S(2)}) collective-permute-start(bf16[2,192,2048]{2,1,0:T(8,128)(2,1)S(1)} %get-tuple-element.56), channel_id=1, source_target_pairs={{0,24},{8,0},{16,8},{24,16},{1,25},{9,1},{17,9},{25,17},{2,26},{10... | collective-permute-start | bytes 4718600 | tf_op jit(solution)/shard_map/ppermute | solution.py:33
  59.3 14.3 %collective-permute-start.4 = (bf16[4,64,512]{2,1,0:T(8,128)(2,1)S(1)}, bf16[4,64,512]{2,1,0:T(8,128)(2,1)S(1)}, u32[]{:S(2)}, u32[]{:S(2)}) collective-permute-start(bf16[4,64,512]{2,1,0:T(8,128)(2,1)S(1)} %get-tuple-element.41), channel_id=1, source_target_pairs={{0,1},{1,0},{2,3},{3,2},{4,5},{5,4},{6,7},{7,6},{8,9},{9,8},{10,11... | collective-permute-start | bytes 786440 | tf_op jit(solution)/shard_map/ppermute | solution.py:33
  60.8 6.4 %collective-permute-start.6 = (bf16[64,512]{1,0:T(8,128)(2,1)S(1)}, bf16[64,512]{1,0:T(8,128)(2,1)S(1)}, u32[]{:S(2)}, u32[]{:S(2)}) collective-permute-start(bf16[64,512]{1,0:T(8,128)(2,1)S(1)} %get-tuple-element.43), channel_id=1, source_target_pairs={{0,4},{1,5},{2,6},{3,7},{4,0},{5,1},{6,2},{7,3},{8,12},{9,13},{10,... | collective-permute-start | bytes 196616 | tf_op jit(solution)/shard_map/ppermute | solution.py:33
  63.4 4.6 %collective-permute-start.7 = (bf16[64,512]{1,0:T(8,128)(2,1)S(1)}, bf16[64,512]{1,0:T(8,128)(2,1)S(1)}, u32[]{:S(2)}, u32[]{:S(2)}) collective-permute-start(bf16[64,512]{1,0:T(8,128)(2,1)S(1)} %get-tuple-element.44), channel_id=1, source_target_pairs={{0,6},{1,7},{2,0},{3,1},{4,2},{5,3},{6,4},{7,5},{8,14},{9,15},{10,... | collective-permute-start | bytes 196616 | tf_op jit(solution)/shard_map/ppermute | solution.py:33
  67.2 6.4 %collective-permute-start.5 = (bf16[64,512]{1,0:T(8,128)(2,1)S(1)}, bf16[64,512]{1,0:T(8,128)(2,1)S(1)}, u32[]{:S(2)}, u32[]{:S(2)}) collective-permute-start(bf16[64,512]{1,0:T(8,128)(2,1)S(1)} %get-tuple-element.39.refs_2_), channel_id=1, source_target_pairs={{0,2},{1,3},{2,4},{3,5},{4,6},{5,7},{6,0},{7,1},{8,10},{9,11},{10,... | collective-permute-start | bytes 196616 | tf_op jit(solution)/shard_map/ppermute | solution.py:33
  80.0 20.6 %collective-permute-start.17 = (bf16[2,128,2048]{2,1,0:T(8,128)(2,1)S(1)}, bf16[2,128,2048]{2,1,0:T(8,128)(2,1)S(1)}, u32[]{:S(2)}, u32[]{:S(2)}) collective-permute-start(bf16[2,128,2048]{2,1,0:T(8,128)(2,1)S(1)} %get-tuple-element.59), channel_id=1, source_target_pairs={{0,24},{8,0},{16,8},{24,16},{1,25},{9,1},{17,9},{25,17},{2,26},{10... | collective-permute-start | bytes 3145736 | tf_op jit(solution)/shard_map/ppermute | solution.py:33
  80.1 12.6 %collective-permute-start.8 = (bf16[4,64,384]{2,1,0:T(8,128)(2,1)S(1)}, bf16[4,64,384]{2,1,0:T(8,128)(2,1)S(1)}, u32[]{:S(2)}, u32[]{:S(2)}) collective-permute-start(bf16[4,64,384]{2,1,0:T(8,128)(2,1)S(1)} %get-tuple-element.47), channel_id=1, source_target_pairs={{0,1},{1,0},{2,3},{3,2},{4,5},{5,4},{6,7},{7,6},{8,9},{9,8},{10,11... | collective-permute-start | bytes 589832 | tf_op jit(solution)/shard_map/ppermute | solution.py:33
  80.7 6.0 %collective-permute-start.10 = (bf16[64,512]{1,0:T(8,128)(2,1)S(1)}, bf16[64,512]{1,0:T(8,128)(2,1)S(1)}, u32[]{:S(2)}, u32[]{:S(2)}) collective-permute-start(bf16[64,512]{1,0:T(8,128)(2,1)S(1)} %get-tuple-element.49), channel_id=1, source_target_pairs={{0,4},{1,5},{2,6},{3,7},{4,0},{5,1},{6,2},{7,3},{8,12},{9,13},{10,... | collective-permute-start | bytes 196616 | tf_op jit(solution)/shard_map/ppermute | solution.py:33
  80.9 6.1 %collective-permute-start.11 = (bf16[64,512]{1,0:T(8,128)(2,1)S(1)}, bf16[64,512]{1,0:T(8,128)(2,1)S(1)}, u32[]{:S(2)}, u32[]{:S(2)}) collective-permute-start(bf16[64,512]{1,0:T(8,128)(2,1)S(1)} %get-tuple-element.50), channel_id=1, source_target_pairs={{0,6},{1,7},{2,0},{3,1},{4,2},{5,3},{6,4},{7,5},{8,14},{9,15},{10,... | collective-permute-start | bytes 196616 | tf_op jit(solution)/shard_map/ppermute | solution.py:33
  86.7 6.1 %collective-permute-start.9 = (bf16[64,512]{1,0:T(8,128)(2,1)S(1)}, bf16[64,512]{1,0:T(8,128)(2,1)S(1)}, u32[]{:S(2)}, u32[]{:S(2)}) collective-permute-start(bf16[64,512]{1,0:T(8,128)(2,1)S(1)} %get-tuple-element.45.refs_2_), channel_id=1, source_target_pairs={{0,2},{1,3},{2,4},{3,5},{4,6},{5,7},{6,0},{7,1},{8,10},{9,11},{10,... | collective-permute-start | bytes 196616 | tf_op jit(solution)/shard_map/ppermute | solution.py:33
  99.0 6.9 %collective-permute-start.16 = (bf16[4,64,384]{2,1,0:T(8,128)(2,1)S(1)}, bf16[4,64,384]{2,1,0:T(8,128)(2,1)S(1)}, u32[]{:S(2)}, u32[]{:S(2)}) collective-permute-start(bf16[4,64,384]{2,1,0:T(8,128)(2,1)S(1)} %get-tuple-element.58), channel_id=1, source_target_pairs={{0,1},{1,0},{2,3},{3,2},{4,5},{5,4},{6,7},{7,6},{8,9},{9,8},{10,11... | collective-permute-start | bytes 589832 | tf_op jit(solution)/shard_map/ppermute | solution.py:33
  105.3 5.0 %collective-permute-start.18 = (bf16[4,64,256]{2,1,0:T(8,128)(2,1)S(1)}, bf16[4,64,256]{2,1,0:T(8,128)(2,1)S(1)}, u32[]{:S(2)}, u32[]{:S(2)}) collective-permute-start(bf16[4,64,256]{2,1,0:T(8,128)(2,1)S(1)} %get-tuple-element.61), channel_id=1, source_target_pairs={{0,1},{1,0},{2,3},{3,2},{4,5},{5,4},{6,7},{7,6},{8,9},{9,8},{10,11... | collective-permute-start | bytes 393224 | tf_op jit(solution)/shard_map/ppermute | solution.py:33
  106.0 10.3 %collective-permute-start.13 = (bf16[64,384]{1,0:T(8,128)(2,1)S(1)}, bf16[64,384]{1,0:T(8,128)(2,1)S(1)}, u32[]{:S(2)}, u32[]{:S(2)}) collective-permute-start(bf16[64,384]{1,0:T(8,128)(2,1)S(1)} %get-tuple-element.54), channel_id=1, source_target_pairs={{0,4},{1,5},{2,6},{3,7},{4,0},{5,1},{6,2},{7,3},{8,12},{9,13},{10,... | collective-permute-start | bytes 147464 | tf_op jit(solution)/shard_map/ppermute | solution.py:33
  111.0 11.2 %collective-permute-start.20 = (bf16[64,640]{1,0:T(8,128)(2,1)S(1)}, bf16[64,640]{1,0:T(8,128)(2,1)S(1)}, u32[]{:S(2)}, u32[]{:S(2)}) collective-permute-start(bf16[64,640]{1,0:T(8,128)(2,1)S(1)} %get-tuple-element.64), channel_id=1, source_target_pairs={{0,4},{1,5},{2,6},{3,7},{4,0},{5,1},{6,2},{7,3},{8,12},{9,13},{10,... | collective-permute-start | bytes 245768 | tf_op jit(solution)/shard_map/ppermute | solution.py:33
  111.1 11.1 %collective-permute-start.21 = (bf16[64,640]{1,0:T(8,128)(2,1)S(1)}, bf16[64,640]{1,0:T(8,128)(2,1)S(1)}, u32[]{:S(2)}, u32[]{:S(2)}) collective-permute-start(bf16[64,640]{1,0:T(8,128)(2,1)S(1)} %get-tuple-element.65), channel_id=1, source_target_pairs={{0,6},{1,7},{2,0},{3,1},{4,2},{5,3},{6,4},{7,5},{8,14},{9,15},{10,... | collective-permute-start | bytes 245768 | tf_op jit(solution)/shard_map/ppermute | solution.py:33
  112.5 9.7 %collective-permute-start.19 = (bf16[64,640]{1,0:T(8,128)(2,1)S(1)}, bf16[64,640]{1,0:T(8,128)(2,1)S(1)}, u32[]{:S(2)}, u32[]{:S(2)}) collective-permute-start(bf16[64,640]{1,0:T(8,128)(2,1)S(1)} %get-tuple-element.63.refs_9_), channel_id=1, source_target_pairs={{0,2},{1,3},{2,4},{3,5},{4,6},{5,7},{6,0},{7,1},{8,10},{9,11},{10,... | collective-permute-start | bytes 245768 | tf_op jit(solution)/shard_map/ppermute | solution.py:33
  113.2 4.9 %collective-permute-start.14 = (bf16[64,384]{1,0:T(8,128)(2,1)S(1)}, bf16[64,384]{1,0:T(8,128)(2,1)S(1)}, u32[]{:S(2)}, u32[]{:S(2)}) collective-permute-start(bf16[64,384]{1,0:T(8,128)(2,1)S(1)} %get-tuple-element.55), channel_id=1, source_target_pairs={{0,6},{1,7},{2,0},{3,1},{4,2},{5,3},{6,4},{7,5},{8,14},{9,15},{10,... | collective-permute-start | bytes 147464 | tf_op jit(solution)/shard_map/ppermute | solution.py:33
  116.3 5.9 %collective-permute-start.12 = (bf16[64,384]{1,0:T(8,128)(2,1)S(1)}, bf16[64,384]{1,0:T(8,128)(2,1)S(1)}, u32[]{:S(2)}, u32[]{:S(2)}) collective-permute-start(bf16[64,384]{1,0:T(8,128)(2,1)S(1)} %get-tuple-element.53.refs_2_), channel_id=1, source_target_pairs={{0,2},{1,3},{2,4},{3,5},{4,6},{5,7},{6,0},{7,1},{8,10},{9,11},{10,... | collective-permute-start | bytes 147464 | tf_op jit(solution)/shard_map/ppermute | solution.py:33

commit v9 on v8

--- a/solution.py
+++ b/solution.py
@@ -117,7 +117,6 @@
     arrived = [take(depth) for _ in plan.adding]
     if plan.adding and plan.placed:
         take(1)
-    take(plan.after)
     outs = take(fold) if plan.part else None
     sends = take(depth) if plan.folding else None
     result_ref = take(1)[0] if plan.adding else None
@@ -165,9 +164,9 @@
             for array in arrays[1:]:
                 total = total + array[...].astype(jnp.float32)
             column = 0
-            for _, start, width in batch:
-                put_sum(sum_buf, start - add_start, total[:, column : column + 2 * width])
-                column += 2 * width
+            for _, start, span in batch:
+                put_sum(sum_buf, start - add_start, total[:, column : column + 2 * span])
+                column += 2 * span
         add_point = table_ref[add_slot * stride].astype(jnp.int32)
         columns = pl.ds(add_start, sum_buf.shape[2])
         placing = pltpu.make_async_copy(
@@ -233,10 +232,9 @@
     adding: tuple
     placed: bool
     later: tuple
-    after: int
-
-
-def step(plan, table, bands, there, folded, arrived, result, after):
+
+
+def step(plan, table, bands, there, folded, arrived, result):
     rows, _, _, nbands = plan.shape
     fold, depth = plan.fold, plan.depth
     points = bands.shape[3]
@@ -286,8 +284,6 @@
         out_specs.append(hbm)
         lanes = sum(width for batch in plan.adding for _, _, width in batch)
         scratch += [pltpu.VMEM((rows, 2, lanes), jnp.float32), pltpu.SemaphoreType.DMA]
-    operands += after
-    in_specs += [pl.BlockSpec(memory_space=pl.ANY)] * len(after)
     if plan.later:
         out_shape.append(jax.ShapeDtypeStruct((2, plan.later[2], points), bands.dtype))
         out_specs.append(hbm)
@@ -321,21 +317,21 @@
 def schedule(parts):
     kernels = []
     waiting = []
-    for part in parts[:-2]:
-        kernels.append((part, (), ()))
-        ready = waiting_block(waiting)
-        for batch in ready:
-            waiting.remove(batch)
-        kernels.append((None, (part,), ready))
-        waiting.append((part,))
-    kernels.append((parts[-2], (), ()))
+    for index, part in enumerate(parts[:-1]):
+        folding = (parts[index - 1],) if index else ()
+        ready = ready_batches(waiting)
+        waiting = waiting[len(ready) :]
+        kernels.append((part, folding, ready))
+        if folding:
+            waiting.append(folding)
+    last = tuple(parts[-2:])
     kernels.append((parts[-1], (), ()))
-    kernels.append((None, tuple(parts[-2:]), ()))
-    kernels.append((None, (), tuple(waiting) + (tuple(parts[-2:]),)))
+    kernels.append((None, last, ()))
+    kernels.append((None, (), tuple(waiting) + (last,)))
     return kernels
 
 
-def waiting_block(waiting):
+def ready_batches(waiting):
     total = 0
     for count, batch in enumerate(waiting, 1):
         total += sum(width for _, _, width in batch)
@@ -375,24 +371,19 @@
     fold = grid_count // depth
     folded, arrived = {}, {}
     result = None
-    after = []
     for part, folding, adding in schedule(parts):
-        index = parts.index(part) + AHEAD if part else len(parts)
-        later = parts[index] if index < len(parts) else None
-        plan = Plan(
-            shape, fold, depth, part, folding, adding, result is not None, later, len(after)
-        )
+        place = parts.index(part) if part else len(parts)
+        later = parts[place + AHEAD] if place + AHEAD < len(parts) else None
+        plan = Plan(shape, fold, depth, part, folding, adding, result is not None, later)
         terms, sends, result, piece = step(
             plan,
             table,
             bands,
-            theres[parts.index(part)] if part else None,
+            theres[place] if part else None,
             [folded.pop(done) for done in folding],
             [arrived.pop(batch) for batch in adding],
             result,
-            after,
         )
-        after = []
         if later:
             theres.append(shifted(piece, "ka", -1))
         if part:
@@ -403,7 +394,6 @@
             arrived[folding] = [sends[0]] + [
                 shifted(sends[i], "ga", i, fold) for i in range(1, depth)
             ]
-            after = [sends[1]]
     return result
 
 

time: 124 us -> 122 us (0.984)
  starting transfers between devices: 25.4 us -> 36.1 us
  waiting for transfers between devices: 59 us -> 49.2 us
  Pallas kernels: 38.5 us -> 35.9 us
    ppermute x22, starting transfers between devices: 25.4 us -> 36.1 us  [shifted(): return lax.ppermute(block, axis, route)]
    ppermute x22, waiting for transfers between devices: 59 us -> 49.2 us  [shifted(): return lax.ppermute(block, axis, route)]
    pallas_call x10 -> x7, Pallas kernels: 34.3 us -> 31.7 us  [step(): pl.pallas_call(functools.partial(step_kernel, plan), in_specs=in_specs, o...]
  transfers between devices with their start and end apart: 22 -> 22, of which waited for: 10 -> 10; matrix products, arithmetic and copies ran while one was open for 0% -> 0% of each run, Pallas kernels for 29% -> 27%
where the time goes in v9:
time: 122 us
  waiting for transfers between devices  49.2 us (40%)
  starting transfers between devices  36.1 us (30%)
  Pallas kernels  35.9 us (29%)
    ppermute x22, waiting for transfers between devices, shifted(): return lax.ppermute(block, axis, route)  49.2 us
    ppermute x22, starting transfers between devices, shifted(): return lax.ppermute(block, axis, route)  36.1 us
    pallas_call x7, Pallas kernels, step(): pl.pallas_call(functools.partial(step_kernel, plan), in_specs=in_specs, o...  31.7 us
    pallas_call x2, Pallas kernels, piece_of(): pl.pallas_call(functools.partial(piece_kernel, slot, start), in_specs=[pl...  4.23 us
  transfers between devices with their start and end apart: 22, of which 10 were waited for; matrix products, arithmetic and copies ran while one was open for 0% of the time, Pallas kernels for 27%

profile of v9, /device:TPU:0, one launch (start us, length us, event | category | flops | bytes accessed | tf_op | source)
XLA Modules:
  0.0 122.1 jit_solution(8840986085406389037)
XLA Ops:
  0.0 1.6 %piece_of.2.rest_0_ = bf16[2,256,2048]{2,1,0:T(8,128)(2,1)S(1)} custom-call(bf16[2,2,512,2048]{3,2,1,0:T(8,128)(2,1)} %refs_0_.9), custom_call_target="tpu_custom_call" | custom-call | flops 1000 | bytes 1000 | tf_op jit(solution)/shard_map/piece_of/pallas_call | solution.py:59
  1.7 0.0 copy-start.1
  1.7 2.5 %collective-permute-start.1 = (bf16[2,256,2048]{2,1,0:T(8,128)(2,1)S(1)}, bf16[2,256,2048]{2,1,0:T(8,128)(2,1)}, u32[]{:S(2)}, u32[]{:S(2)}) collective-permute-start(bf16[2,256,2048]{2,1,0:T(8,128)(2,1)S(1)} %piece_of.2.rest_0_), channel_id=1, source_target_pairs={{0,24},{8,0},{16,8},{24,16},{1,25},{9,1},{17,9},{25,17},{2,26},{10... | collective-permute-start | bytes 6291464 | tf_op jit(solution)/shard_map/ppermute | solution.py:33
  4.1 2.6 %piece_of.3 = bf16[2,256,2048]{2,1,0:T(8,128)(2,1)} custom-call(bf16[2,2,512,2048]{3,2,1,0:T(8,128)(2,1)} %refs_0_.9, bf16[2,256,2048]{2,1,0:T(8,128)(2,1)S(1)} %piece_of.2.rest_0_), custom_call_target="tpu_custom_call" | custom-call | flops 1000 | bytes 1000 | tf_op jit(solution)/shard_map/piece_of/pallas_call | solution.py:59
  6.7 0.7 collective-permute-start
  7.5 0.1 select_reduce_fusion.1
  7.6 0.1 copy.6
  7.7 0.1 fusion.4
  7.8 0.1 pad_maximum_fusion
  7.9 0.1 reshape.28
  8.0 0.1 pad_maximum_fusion.1.table_ref
  8.1 19.6 %collective-permute-done.1.refs_1_ = bf16[2,256,2048]{2,1,0:T(8,128)(2,1)} collective-permute-done((bf16[2,256,2048]{2,1,0:T(8,128)(2,1)S(1)}, bf16[2,256,2048]{2,1,0:T(8,128)(2,1)}, u32[]{:S(2)}, u32[]{:S(2)}) %collective-permute-start.1) | collective-permute-done | bytes 2097184 | tf_op jit(solution)/shard_map/ppermute | solution.py:33
  27.7 7.1 %step.7 = (f32[4,64,512]{2,1,0:T(8,128)S(1)}, bf16[4,64,512]{2,1,0:T(8,128)(2,1)S(1)}, bf16[2,192,2048]{2,1,0:T(8,128)(2,1)S(1)}) custom-call(f32[11]{0:T(128)S(1)} %pad_maximum_fusion.1.table_ref, bf16[2,2,512,2048]{3,2,1,0:T(8,128)(2,1)} %refs_0_.9, bf16[2,256,2048]{2,1,0:T(8,128)(2,1)} %collective-permute-done.1.refs_1_), custom_call_target="tpu_custom_call" | custom-call | flops 1000 | bytes 1000 | tf_op jit(solution)/shard_map/step/pallas_call | solution.py:291
  34.8 2.1 %collective-permute-start.4 = (bf16[2,192,2048]{2,1,0:T(8,128)(2,1)S(1)}, bf16[2,192,2048]{2,1,0:T(8,128)(2,1)S(1)}, u32[]{:S(2)}, u32[]{:S(2)}) collective-permute-start(bf16[2,192,2048]{2,1,0:T(8,128)(2,1)S(1)} %get-tuple-element.39), channel_id=1, source_target_pairs={{0,24},{8,0},{16,8},{24,16},{1,25},{9,1},{17,9},{25,17},{2,26},{10... | collective-permute-start | bytes 4718600 | tf_op jit(solution)/shard_map/ppermute | solution.py:33
  36.9 1.5 %collective-permute-start.2 = (bf16[4,64,512]{2,1,0:T(8,128)(2,1)S(1)}, bf16[4,64,512]{2,1,0:T(8,128)(2,1)S(1)}, u32[]{:S(2)}, u32[]{:S(2)}) collective-permute-start(bf16[4,64,512]{2,1,0:T(8,128)(2,1)S(1)} %get-tuple-element.37), channel_id=1, source_target_pairs={{0,1},{1,0},{2,3},{3,2},{4,5},{5,4},{6,7},{7,6},{8,9},{9,8},{10,11... | collective-permute-start | bytes 786440 | tf_op jit(solution)/shard_map/ppermute | solution.py:33
  38.4 11.9 %collective-permute-done.refs_1_ = bf16[2,256,2048]{2,1,0:T(8,128)(2,1)} collective-permute-done((bf16[2,256,2048]{2,1,0:T(8,128)(2,1)}, bf16[2,256,2048]{2,1,0:T(8,128)(2,1)}, u32[]{:S(2)}, u32[]{:S(2)}) %collective-permute-start) | collective-permute-done | bytes 2097184 | tf_op jit(solution)/shard_map/ppermute | solution.py:33
  50.3 7.3 %step.8 = (f32[4,64,512]{2,1,0:T(8,128)S(1)}, bf16[4,64,512]{2,1,0:T(8,128)(2,1)S(1)}, f32[64,512]{1,0:T(8,128)S(1)}, bf16[64,512]{1,0:T(8,128)(2,1)S(1)}, bf16[...) custom-call(f32[11]{0:T(128)S(1)} %pad_maximum_fusion.1.table_ref, ...), custom_call_target="tpu_custom_call" | custom-call | flops 1000 | bytes 1000 | tf_op jit(solution)/shard_map/step/pallas_call | solution.py:291
  57.6 2.0 %collective-permute-start.3 = (bf16[2,192,2048]{2,1,0:T(8,128)(2,1)S(1)}, bf16[2,192,2048]{2,1,0:T(8,128)(2,1)S(1)}, u32[]{:S(2)}, u32[]{:S(2)}) collective-permute-start(bf16[2,192,2048]{2,1,0:T(8,128)(2,1)S(1)} %get-tuple-element.38), channel_id=1, source_target_pairs={{0,24},{8,0},{16,8},{24,16},{1,25},{9,1},{17,9},{25,17},{2,26},{10... | collective-permute-start | bytes 4718600 | tf_op jit(solution)/shard_map/ppermute | solution.py:33
  59.6 1.5 %collective-permute-start.5 = (bf16[4,64,512]{2,1,0:T(8,128)(2,1)S(1)}, bf16[4,64,512]{2,1,0:T(8,128)(2,1)S(1)}, u32[]{:S(2)}, u32[]{:S(2)}) collective-permute-start(bf16[4,64,512]{2,1,0:T(8,128)(2,1)S(1)} %get-tuple-element.41), channel_id=1, source_target_pairs={{0,1},{1,0},{2,3},{3,2},{4,5},{5,4},{6,7},{7,6},{8,9},{9,8},{10,11... | collective-permute-start | bytes 786440 | tf_op jit(solution)/shard_map/ppermute | solution.py:33
  61.1 1.6 %collective-permute-start.6 = (bf16[64,512]{1,0:T(8,128)(2,1)S(1)}, bf16[64,512]{1,0:T(8,128)(2,1)S(1)}, u32[]{:S(2)}, u32[]{:S(2)}) collective-permute-start(bf16[64,512]{1,0:T(8,128)(2,1)S(1)} %get-tuple-element.43), channel_id=1, source_target_pairs={{0,2},{1,3},{2,4},{3,5},{4,6},{5,7},{6,0},{7,1},{8,10},{9,11},{10,... | collective-permute-start | bytes 196616 | tf_op jit(solution)/shard_map/ppermute | solution.py:33
  62.6 2.6 %collective-permute-start.7 = (bf16[64,512]{1,0:T(8,128)(2,1)S(1)}, bf16[64,512]{1,0:T(8,128)(2,1)S(1)}, u32[]{:S(2)}, u32[]{:S(2)}) collective-permute-start(bf16[64,512]{1,0:T(8,128)(2,1)S(1)} %get-tuple-element.44), channel_id=1, source_target_pairs={{0,4},{1,5},{2,6},{3,7},{4,0},{5,1},{6,2},{7,3},{8,12},{9,13},{10,... | collective-permute-start | bytes 196616 | tf_op jit(solution)/shard_map/ppermute | solution.py:33
  65.2 2.0 %collective-permute-done.6.refs_5_ = bf16[64,512]{1,0:T(8,128)(2,1)S(1)} collective-permute-done((bf16[64,512]{1,0:T(8,128)(2,1)S(1)}, bf16[64,512]{1,0:T(8,128)(2,1)S(1)}, u32[]{:S(2)}, u32[]{:S(2)}) %collective-permute-start.6) | collective-permute-done | bytes 65568 | tf_op jit(solution)/shard_map/ppermute | solution.py:33
  67.2 1.7 %collective-permute-start.8 = (bf16[64,512]{1,0:T(8,128)(2,1)S(1)}, bf16[64,512]{1,0:T(8,128)(2,1)S(1)}, u32[]{:S(2)}, u32[]{:S(2)}) collective-permute-start(bf16[64,512]{1,0:T(8,128)(2,1)S(1)} %get-tuple-element.45), channel_id=1, source_target_pairs={{0,6},{1,7},{2,0},{3,1},{4,2},{5,3},{6,4},{7,5},{8,14},{9,15},{10,... | collective-permute-start | bytes 196616 | tf_op jit(solution)/shard_map/ppermute | solution.py:33
  68.9 0.3 collective-permute-done.7.refs_6_
  69.2 2.2 %collective-permute-done.8.refs_7_ = bf16[64,512]{1,0:T(8,128)(2,1)S(1)} collective-permute-done((bf16[64,512]{1,0:T(8,128)(2,1)S(1)}, bf16[64,512]{1,0:T(8,128)(2,1)S(1)}, u32[]{:S(2)}, u32[]{:S(2)}) %collective-permute-start.8) | collective-permute-done | bytes 65568 | tf_op jit(solution)/shard_map/ppermute | solution.py:33
  71.5 5.3 %step.9 = (f32[4,64,384]{2,1,0:T(8,128)S(1)}, bf16[4,64,384]{2,1,0:T(8,128)(2,1)S(1)}, f32[64,512]{1,0:T(8,128)S(1)}, bf16[64,512]{1,0:T(8,128)(2,1)S(1)}, bf16[...) custom-call(f32[11]{0:T(128)S(1)} %pad_maximum_fusion.1.table_ref, ...), custom_call_target="tpu_custom_call" | custom-call | flops 1000 | bytes 1000 | tf_op jit(solution)/shard_map/step/pallas_call | solution.py:291
  76.8 0.1 collective-permute-start.17
  76.9 0.6 collective-permute-start.9
  77.5 0.4 collective-permute-start.10
  77.8 3.8 %collective-permute-start.11 = (bf16[64,512]{1,0:T(8,128)(2,1)S(1)}, bf16[64,512]{1,0:T(8,128)(2,1)S(1)}, u32[]{:S(2)}, u32[]{:S(2)}) collective-permute-start(bf16[64,512]{1,0:T(8,128)(2,1)S(1)} %get-tuple-element.50), channel_id=1, source_target_pairs={{0,4},{1,5},{2,6},{3,7},{4,0},{5,1},{6,2},{7,3},{8,12},{9,13},{10,... | collective-permute-start | bytes 196616 | tf_op jit(solution)/shard_map/ppermute | solution.py:33
  81.6 2.7 %collective-permute-done.10.refs_5_ = bf16[64,512]{1,0:T(8,128)(2,1)S(1)} collective-permute-done((bf16[64,512]{1,0:T(8,128)(2,1)S(1)}, bf16[64,512]{1,0:T(8,128)(2,1)S(1)}, u32[]{:S(2)}, u32[]{:S(2)}) %collective-permute-start.10) | collective-permute-done | bytes 65568 | tf_op jit(solution)/shard_map/ppermute | solution.py:33
  84.2 2.0 %collective-permute-start.12 = (bf16[64,512]{1,0:T(8,128)(2,1)S(1)}, bf16[64,512]{1,0:T(8,128)(2,1)S(1)}, u32[]{:S(2)}, u32[]{:S(2)}) collective-permute-start(bf16[64,512]{1,0:T(8,128)(2,1)S(1)} %get-tuple-element.51), channel_id=1, source_target_pairs={{0,6},{1,7},{2,0},{3,1},{4,2},{5,3},{6,4},{7,5},{8,14},{9,15},{10,... | collective-permute-start | bytes 196616 | tf_op jit(solution)/shard_map/ppermute | solution.py:33
  86.2 0.2 collective-permute-done.11.refs_6_
  86.4 2.2 %collective-permute-done.12.refs_7_ = bf16[64,512]{1,0:T(8,128)(2,1)S(1)} collective-permute-done((bf16[64,512]{1,0:T(8,128)(2,1)S(1)}, bf16[64,512]{1,0:T(8,128)(2,1)S(1)}, u32[]{:S(2)}, u32[]{:S(2)}) %collective-permute-start.12) | collective-permute-done | bytes 65568 | tf_op jit(solution)/shard_map/ppermute | solution.py:33
  88.5 5.1 %step.10 = (f32[4,64,384]{2,1,0:T(8,128)S(1)}, bf16[4,64,384]{2,1,0:T(8,128)(2,1)S(1)}, f32[64,384]{1,0:T(8,128)S(1)}, bf16[64,384]{1,0:T(8,128)(2,1)S(1)}, bf16...) custom-call(f32[11]{0:T(128)S(1)} %pad_maximum_fusion.1.table_ref, ...), custom_call_target="tpu_custom_call", output_to_operand_aliasing={{6}: (9, {})} | custom-call | flops 1000 | bytes 1000 | tf_op jit(solution)/shard_map/step/pallas_call | solution.py:291
  93.6 1.6 %collective-permute-start.16 = (bf16[4,64,384]{2,1,0:T(8,128)(2,1)S(1)}, bf16[4,64,384]{2,1,0:T(8,128)(2,1)S(1)}, u32[]{:S(2)}, u32[]{:S(2)}) collective-permute-start(bf16[4,64,384]{2,1,0:T(8,128)(2,1)S(1)} %get-tuple-element.58), channel_id=1, source_target_pairs={{0,1},{1,0},{2,3},{3,2},{4,5},{5,4},{6,7},{7,6},{8,9},{9,8},{10,11... | collective-permute-start | bytes 589832 | tf_op jit(solution)/shard_map/ppermute | solution.py:33
  95.1 4.7 %step.11 = (f32[4,64,256]{2,1,0:T(8,128)S(1)}, bf16[4,64,256]{2,1,0:T(8,128)(2,1)S(1)}) custom-call(f32[11]{0:T(128)S(1)} %pad_maximum_fusion.1.table_ref, bf16[2,2,512,2048]{3,2,1,0:T(8,128)(2,1)} %refs_0_.9, bf16[2,128,2048]{2,1,0:T(8,128)(2,1)S(1)} %collective-permute-done.17.refs_1_), custom_call_target="tpu_custom_call" | custom-call | flops 1000 | bytes 1000 | tf_op jit(solution)/shard_map/step/pallas_call | solution.py:291
  99.9 1.5 %collective-permute-start.18 = (bf16[4,64,256]{2,1,0:T(8,128)(2,1)S(1)}, bf16[4,64,256]{2,1,0:T(8,128)(2,1)S(1)}, u32[]{:S(2)}, u32[]{:S(2)}) collective-permute-start(bf16[4,64,256]{2,1,0:T(8,128)(2,1)S(1)} %get-tuple-element.61), channel_id=1, source_target_pairs={{0,1},{1,0},{2,3},{3,2},{4,5},{5,4},{6,7},{7,6},{8,9},{9,8},{10,11... | collective-permute-start | bytes 393224 | tf_op jit(solution)/shard_map/ppermute | solution.py:33
  101.4 1.6 %collective-permute-start.13 = (bf16[64,384]{1,0:T(8,128)(2,1)S(1)}, bf16[64,384]{1,0:T(8,128)(2,1)S(1)}, u32[]{:S(2)}, u32[]{:S(2)}) collective-permute-start(bf16[64,384]{1,0:T(8,128)(2,1)S(1)} %get-tuple-element.54), channel_id=1, source_target_pairs={{0,2},{1,3},{2,4},{3,5},{4,6},{5,7},{6,0},{7,1},{8,10},{9,11},{10,... | collective-permute-start | bytes 147464 | tf_op jit(solution)/shard_map/ppermute | solution.py:33
  103.0 3.2 %collective-permute-done.18.refs_3_ = bf16[4,64,256]{2,1,0:T(8,128)(2,1)S(1)} collective-permute-done((bf16[4,64,256]{2,1,0:T(8,128)(2,1)S(1)}, bf16[4,64,256]{2,1,0:T(8,128)(2,1)S(1)}, u32[]{:S(2)}, u32[]{:S(2)}) %collective-permute-start.18) | collective-permute-done | bytes 131104 | tf_op jit(solution)/shard_map/ppermute | solution.py:33
  106.2 0.6 step.12
  106.8 1.6 %collective-permute-start.19 = (bf16[64,640]{1,0:T(8,128)(2,1)S(1)}, bf16[64,640]{1,0:T(8,128)(2,1)S(1)}, u32[]{:S(2)}, u32[]{:S(2)}) collective-permute-start(bf16[64,640]{1,0:T(8,128)(2,1)S(1)} %get-tuple-element.63), channel_id=1, source_target_pairs={{0,2},{1,3},{2,4},{3,5},{4,6},{5,7},{6,0},{7,1},{8,10},{9,11},{10,... | collective-permute-start | bytes 245768 | tf_op jit(solution)/shard_map/ppermute | solution.py:33
  108.4 2.6 %collective-permute-start.20 = (bf16[64,640]{1,0:T(8,128)(2,1)S(1)}, bf16[64,640]{1,0:T(8,128)(2,1)S(1)}, u32[]{:S(2)}, u32[]{:S(2)}) collective-permute-start(bf16[64,640]{1,0:T(8,128)(2,1)S(1)} %get-tuple-element.64), channel_id=1, source_target_pairs={{0,4},{1,5},{2,6},{3,7},{4,0},{5,1},{6,2},{7,3},{8,12},{9,13},{10,... | collective-permute-start | bytes 245768 | tf_op jit(solution)/shard_map/ppermute | solution.py:33
  111.0 1.3 %collective-permute-start.21 = (bf16[64,640]{1,0:T(8,128)(2,1)S(1)}, bf16[64,640]{1,0:T(8,128)(2,1)S(1)}, u32[]{:S(2)}, u32[]{:S(2)}) collective-permute-start(bf16[64,640]{1,0:T(8,128)(2,1)S(1)} %get-tuple-element.65), channel_id=1, source_target_pairs={{0,6},{1,7},{2,0},{3,1},{4,2},{5,3},{6,4},{7,5},{8,14},{9,15},{10,... | collective-permute-start | bytes 245768 | tf_op jit(solution)/shard_map/ppermute | solution.py:33
  112.3 0.4 collective-permute-start.14
  112.7 2.7 %collective-permute-start.15 = (bf16[64,384]{1,0:T(8,128)(2,1)S(1)}, bf16[64,384]{1,0:T(8,128)(2,1)S(1)}, u32[]{:S(2)}, u32[]{:S(2)}) collective-permute-start(bf16[64,384]{1,0:T(8,128)(2,1)S(1)} %get-tuple-element.56), channel_id=1, source_target_pairs={{0,6},{1,7},{2,0},{3,1},{4,2},{5,3},{6,4},{7,5},{8,14},{9,15},{10,... | collective-permute-start | bytes 147464 | tf_op jit(solution)/shard_map/ppermute | solution.py:33
  115.4 5.0 %collective-permute-done.14.refs_2_ = bf16[64,384]{1,0:T(8,128)(2,1)S(1)} collective-permute-done((bf16[64,384]{1,0:T(8,128)(2,1)S(1)}, bf16[64,384]{1,0:T(8,128)(2,1)S(1)}, u32[]{:S(2)}, u32[]{:S(2)}) %collective-permute-start.14) | collective-permute-done | bytes 49184 | tf_op jit(solution)/shard_map/ppermute | solution.py:33
  120.5 1.5 %step.13 = f32[64,2,2,512]{3,2,1,0:T(2,128)} custom-call(f32[11]{0:T(128)S(1)} %pad_maximum_fusion.1.table_ref, f32[64,384]{1,0:T(8,128)S(1)} %get-tuple-element.53.refs_0_, bf16[64,384]{1,0:T(8,128)(2,1)S(1)} %collective-permute-done.13.refs_1_, bf16[64,384]{1,0:T(8,128)(2,1)S(1)} %collective-permute-done.14.refs_2_, ...), custom_call_target="tpu_custom_call", output_to_operand_aliasing={{}: (9, {})} | custom-call | flops 1000 | bytes 1000 | tf_op jit(solution)/shard_map/step/pallas_call | solution.py:291
  (17 shorter events, 0.0 us)
Async XLA Ops:
  1.7 5.8 %copy-start = (s32[2]{0:T(128)S(1)}, s32[2]{0:T(128)}, u32[]{:S(2)}) copy-start(s32[2]{0:T(128)} %param.4) | copy-start | bytes 28
  1.7 5.8 %copy-start.1 = (s32[2]{0:T(128)S(1)}, s32[2]{0:T(128)}, u32[]{:S(2)}) copy-start(s32[2]{0:T(128)} %param.5) | copy-start | bytes 28
  1.7 26.0 %collective-permute-start.1 = (bf16[2,256,2048]{2,1,0:T(8,128)(2,1)S(1)}, bf16[2,256,2048]{2,1,0:T(8,128)(2,1)}, u32[]{:S(2)}, u32[]{:S(2)}) collective-permute-start(bf16[2,256,2048]{2,1,0:T(8,128)(2,1)S(1)} %piece_of.2.rest_0_), channel_id=1, source_target_pairs={{0,24},{8,0},{16,8},{24,16},{1,25},{9,1},{17,9},{25,17},{2,26},{10... | collective-permute-start | bytes 6291464 | tf_op jit(solution)/shard_map/ppermute | solution.py:33
  6.7 43.5 %collective-permute-start = (bf16[2,256,2048]{2,1,0:T(8,128)(2,1)}, bf16[2,256,2048]{2,1,0:T(8,128)(2,1)}, u32[]{:S(2)}, u32[]{:S(2)}) collective-permute-start(bf16[2,256,2048]{2,1,0:T(8,128)(2,1)} %piece_of.3), channel_id=1, source_target_pairs={{0,24},{8,0},{16,8},{24,16},{1,25},{9,1},{17,9},{25,17},{2,26},{10... | collective-permute-start | bytes 6291464 | tf_op jit(solution)/shard_map/ppermute | solution.py:33
  34.8 36.7 %collective-permute-start.4 = (bf16[2,192,2048]{2,1,0:T(8,128)(2,1)S(1)}, bf16[2,192,2048]{2,1,0:T(8,128)(2,1)S(1)}, u32[]{:S(2)}, u32[]{:S(2)}) collective-permute-start(bf16[2,192,2048]{2,1,0:T(8,128)(2,1)S(1)} %get-tuple-element.39), channel_id=1, source_target_pairs={{0,24},{8,0},{16,8},{24,16},{1,25},{9,1},{17,9},{25,17},{2,26},{10... | collective-permute-start | bytes 4718600 | tf_op jit(solution)/shard_map/ppermute | solution.py:33
  36.9 13.4 %collective-permute-start.2 = (bf16[4,64,512]{2,1,0:T(8,128)(2,1)S(1)}, bf16[4,64,512]{2,1,0:T(8,128)(2,1)S(1)}, u32[]{:S(2)}, u32[]{:S(2)}) collective-permute-start(bf16[4,64,512]{2,1,0:T(8,128)(2,1)S(1)} %get-tuple-element.37), channel_id=1, source_target_pairs={{0,1},{1,0},{2,3},{3,2},{4,5},{5,4},{6,7},{7,6},{8,9},{9,8},{10,11... | collective-permute-start | bytes 786440 | tf_op jit(solution)/shard_map/ppermute | solution.py:33
  57.6 30.9 %collective-permute-start.3 = (bf16[2,192,2048]{2,1,0:T(8,128)(2,1)S(1)}, bf16[2,192,2048]{2,1,0:T(8,128)(2,1)S(1)}, u32[]{:S(2)}, u32[]{:S(2)}) collective-permute-start(bf16[2,192,2048]{2,1,0:T(8,128)(2,1)S(1)} %get-tuple-element.38), channel_id=1, source_target_pairs={{0,24},{8,0},{16,8},{24,16},{1,25},{9,1},{17,9},{25,17},{2,26},{10... | collective-permute-start | bytes 4718600 | tf_op jit(solution)/shard_map/ppermute | solution.py:33
  59.6 11.9 %collective-permute-start.5 = (bf16[4,64,512]{2,1,0:T(8,128)(2,1)S(1)}, bf16[4,64,512]{2,1,0:T(8,128)(2,1)S(1)}, u32[]{:S(2)}, u32[]{:S(2)}) collective-permute-start(bf16[4,64,512]{2,1,0:T(8,128)(2,1)S(1)} %get-tuple-element.41), channel_id=1, source_target_pairs={{0,1},{1,0},{2,3},{3,2},{4,5},{5,4},{6,7},{7,6},{8,9},{9,8},{10,11... | collective-permute-start | bytes 786440 | tf_op jit(solution)/shard_map/ppermute | solution.py:33
  61.1 6.1 %collective-permute-start.6 = (bf16[64,512]{1,0:T(8,128)(2,1)S(1)}, bf16[64,512]{1,0:T(8,128)(2,1)S(1)}, u32[]{:S(2)}, u32[]{:S(2)}) collective-permute-start(bf16[64,512]{1,0:T(8,128)(2,1)S(1)} %get-tuple-element.43), channel_id=1, source_target_pairs={{0,2},{1,3},{2,4},{3,5},{4,6},{5,7},{6,0},{7,1},{8,10},{9,11},{10,... | collective-permute-start | bytes 196616 | tf_op jit(solution)/shard_map/ppermute | solution.py:33
  62.6 6.6 %collective-permute-start.7 = (bf16[64,512]{1,0:T(8,128)(2,1)S(1)}, bf16[64,512]{1,0:T(8,128)(2,1)S(1)}, u32[]{:S(2)}, u32[]{:S(2)}) collective-permute-start(bf16[64,512]{1,0:T(8,128)(2,1)S(1)} %get-tuple-element.44), channel_id=1, source_target_pairs={{0,4},{1,5},{2,6},{3,7},{4,0},{5,1},{6,2},{7,3},{8,12},{9,13},{10,... | collective-permute-start | bytes 196616 | tf_op jit(solution)/shard_map/ppermute | solution.py:33
  67.2 4.3 %collective-permute-start.8 = (bf16[64,512]{1,0:T(8,128)(2,1)S(1)}, bf16[64,512]{1,0:T(8,128)(2,1)S(1)}, u32[]{:S(2)}, u32[]{:S(2)}) collective-permute-start(bf16[64,512]{1,0:T(8,128)(2,1)S(1)} %get-tuple-element.45), channel_id=1, source_target_pairs={{0,6},{1,7},{2,0},{3,1},{4,2},{5,3},{6,4},{7,5},{8,14},{9,15},{10,... | collective-permute-start | bytes 196616 | tf_op jit(solution)/shard_map/ppermute | solution.py:33
  76.8 18.3 %collective-permute-start.17 = (bf16[2,128,2048]{2,1,0:T(8,128)(2,1)S(1)}, bf16[2,128,2048]{2,1,0:T(8,128)(2,1)S(1)}, u32[]{:S(2)}, u32[]{:S(2)}) collective-permute-start(bf16[2,128,2048]{2,1,0:T(8,128)(2,1)S(1)} %get-tuple-element.59), channel_id=1, source_target_pairs={{0,24},{8,0},{16,8},{24,16},{1,25},{9,1},{17,9},{25,17},{2,26},{10... | collective-permute-start | bytes 3145736 | tf_op jit(solution)/shard_map/ppermute | solution.py:33
  76.9 11.6 %collective-permute-start.9 = (bf16[4,64,384]{2,1,0:T(8,128)(2,1)S(1)}, bf16[4,64,384]{2,1,0:T(8,128)(2,1)S(1)}, u32[]{:S(2)}, u32[]{:S(2)}) collective-permute-start(bf16[4,64,384]{2,1,0:T(8,128)(2,1)S(1)} %get-tuple-element.47), channel_id=1, source_target_pairs={{0,1},{1,0},{2,3},{3,2},{4,5},{5,4},{6,7},{7,6},{8,9},{9,8},{10,11... | collective-permute-start | bytes 589832 | tf_op jit(solution)/shard_map/ppermute | solution.py:33
  77.5 6.8 %collective-permute-start.10 = (bf16[64,512]{1,0:T(8,128)(2,1)S(1)}, bf16[64,512]{1,0:T(8,128)(2,1)S(1)}, u32[]{:S(2)}, u32[]{:S(2)}) collective-permute-start(bf16[64,512]{1,0:T(8,128)(2,1)S(1)} %get-tuple-element.49), channel_id=1, source_target_pairs={{0,2},{1,3},{2,4},{3,5},{4,6},{5,7},{6,0},{7,1},{8,10},{9,11},{10,... | collective-permute-start | bytes 196616 | tf_op jit(solution)/shard_map/ppermute | solution.py:33
  77.8 8.5 %collective-permute-start.11 = (bf16[64,512]{1,0:T(8,128)(2,1)S(1)}, bf16[64,512]{1,0:T(8,128)(2,1)S(1)}, u32[]{:S(2)}, u32[]{:S(2)}) collective-permute-start(bf16[64,512]{1,0:T(8,128)(2,1)S(1)} %get-tuple-element.50), channel_id=1, source_target_pairs={{0,4},{1,5},{2,6},{3,7},{4,0},{5,1},{6,2},{7,3},{8,12},{9,13},{10,... | collective-permute-start | bytes 196616 | tf_op jit(solution)/shard_map/ppermute | solution.py:33
  84.2 4.3 %collective-permute-start.12 = (bf16[64,512]{1,0:T(8,128)(2,1)S(1)}, bf16[64,512]{1,0:T(8,128)(2,1)S(1)}, u32[]{:S(2)}, u32[]{:S(2)}) collective-permute-start(bf16[64,512]{1,0:T(8,128)(2,1)S(1)} %get-tuple-element.51), channel_id=1, source_target_pairs={{0,6},{1,7},{2,0},{3,1},{4,2},{5,3},{6,4},{7,5},{8,14},{9,15},{10,... | collective-permute-start | bytes 196616 | tf_op jit(solution)/shard_map/ppermute | solution.py:33
  93.6 9.4 %collective-permute-start.16 = (bf16[4,64,384]{2,1,0:T(8,128)(2,1)S(1)}, bf16[4,64,384]{2,1,0:T(8,128)(2,1)S(1)}, u32[]{:S(2)}, u32[]{:S(2)}) collective-permute-start(bf16[4,64,384]{2,1,0:T(8,128)(2,1)S(1)} %get-tuple-element.58), channel_id=1, source_target_pairs={{0,1},{1,0},{2,3},{3,2},{4,5},{5,4},{6,7},{7,6},{8,9},{9,8},{10,11... | collective-permute-start | bytes 589832 | tf_op jit(solution)/shard_map/ppermute | solution.py:33
  99.9 6.3 %collective-permute-start.18 = (bf16[4,64,256]{2,1,0:T(8,128)(2,1)S(1)}, bf16[4,64,256]{2,1,0:T(8,128)(2,1)S(1)}, u32[]{:S(2)}, u32[]{:S(2)}) collective-permute-start(bf16[4,64,256]{2,1,0:T(8,128)(2,1)S(1)} %get-tuple-element.61), channel_id=1, source_target_pairs={{0,1},{1,0},{2,3},{3,2},{4,5},{5,4},{6,7},{7,6},{8,9},{9,8},{10,11... | collective-permute-start | bytes 393224 | tf_op jit(solution)/shard_map/ppermute | solution.py:33
  101.4 11.3 %collective-permute-start.13 = (bf16[64,384]{1,0:T(8,128)(2,1)S(1)}, bf16[64,384]{1,0:T(8,128)(2,1)S(1)}, u32[]{:S(2)}, u32[]{:S(2)}) collective-permute-start(bf16[64,384]{1,0:T(8,128)(2,1)S(1)} %get-tuple-element.54), channel_id=1, source_target_pairs={{0,2},{1,3},{2,4},{3,5},{4,6},{5,7},{6,0},{7,1},{8,10},{9,11},{10,... | collective-permute-start | bytes 147464 | tf_op jit(solution)/shard_map/ppermute | solution.py:33
  106.8 13.7 %collective-permute-start.19 = (bf16[64,640]{1,0:T(8,128)(2,1)S(1)}, bf16[64,640]{1,0:T(8,128)(2,1)S(1)}, u32[]{:S(2)}, u32[]{:S(2)}) collective-permute-start(bf16[64,640]{1,0:T(8,128)(2,1)S(1)} %get-tuple-element.63), channel_id=1, source_target_pairs={{0,2},{1,3},{2,4},{3,5},{4,6},{5,7},{6,0},{7,1},{8,10},{9,11},{10,... | collective-permute-start | bytes 245768 | tf_op jit(solution)/shard_map/ppermute | solution.py:33
  108.4 12.1 %collective-permute-start.20 = (bf16[64,640]{1,0:T(8,128)(2,1)S(1)}, bf16[64,640]{1,0:T(8,128)(2,1)S(1)}, u32[]{:S(2)}, u32[]{:S(2)}) collective-permute-start(bf16[64,640]{1,0:T(8,128)(2,1)S(1)} %get-tuple-element.64), channel_id=1, source_target_pairs={{0,4},{1,5},{2,6},{3,7},{4,0},{5,1},{6,2},{7,3},{8,12},{9,13},{10,... | collective-permute-start | bytes 245768 | tf_op jit(solution)/shard_map/ppermute | solution.py:33
  111.0 9.5 %collective-permute-start.21 = (bf16[64,640]{1,0:T(8,128)(2,1)S(1)}, bf16[64,640]{1,0:T(8,128)(2,1)S(1)}, u32[]{:S(2)}, u32[]{:S(2)}) collective-permute-start(bf16[64,640]{1,0:T(8,128)(2,1)S(1)} %get-tuple-element.65), channel_id=1, source_target_pairs={{0,6},{1,7},{2,0},{3,1},{4,2},{5,3},{6,4},{7,5},{8,14},{9,15},{10,... | collective-permute-start | bytes 245768 | tf_op jit(solution)/shard_map/ppermute | solution.py:33
  112.3 8.1 %collective-permute-start.14 = (bf16[64,384]{1,0:T(8,128)(2,1)S(1)}, bf16[64,384]{1,0:T(8,128)(2,1)S(1)}, u32[]{:S(2)}, u32[]{:S(2)}) collective-permute-start(bf16[64,384]{1,0:T(8,128)(2,1)S(1)} %get-tuple-element.55), channel_id=1, source_target_pairs={{0,4},{1,5},{2,6},{3,7},{4,0},{5,1},{6,2},{7,3},{8,12},{9,13},{10,... | collective-permute-start | bytes 147464 | tf_op jit(solution)/shard_map/ppermute | solution.py:33
  112.7 7.8 %collective-permute-start.15 = (bf16[64,384]{1,0:T(8,128)(2,1)S(1)}, bf16[64,384]{1,0:T(8,128)(2,1)S(1)}, u32[]{:S(2)}, u32[]{:S(2)}) collective-permute-start(bf16[64,384]{1,0:T(8,128)(2,1)S(1)} %get-tuple-element.56), channel_id=1, source_target_pairs={{0,6},{1,7},{2,0},{3,1},{4,2},{5,3},{6,4},{7,5},{8,14},{9,15},{10,... | collective-permute-start | bytes 147464 | tf_op jit(solution)/shard_map/ppermute | solution.py:33

commit v10 on v9

--- a/solution.py
+++ b/solution.py
@@ -31,6 +31,11 @@
         else:
             route.append((i, (outer + distance) % (count // fold) * fold + place))
     return lax.ppermute(block, axis, route)
+
+
+def swapped(block, axis, distance):
+    count = lax.axis_size(axis)
+    return lax.ppermute(block, axis, [(i, i ^ distance) for i in range(count)])
 
 
 def piece_kernel(slot, start, bands_ref, *rest):
@@ -113,12 +118,12 @@
     place, outer = lax.rem(me, fold), lax.div(me, fold)
     if plan.part:
         bands_ref, there_ref = take(2)
-    folded = [take(fold) for _ in plan.folding]
-    arrived = [take(depth) for _ in plan.adding]
+    sources = [take(count) for count in plan.takes]
+    arrived = [take(count) for count in plan.adds]
     if plan.adding and plan.placed:
         take(1)
     outs = take(fold) if plan.part else None
-    sends = take(depth) if plan.folding else None
+    targets = [take(task.count) for task in plan.tasks]
     result_ref = take(1)[0] if plan.adding else None
     piece_ref = take(1)[0] if plan.later else None
     if plan.part:
@@ -160,9 +165,7 @@
         sum_buf, placed_sem = take(2)
         add_slot, add_start, _ = plan.adding[0][0]
         for batch, arrays in zip(plan.adding, arrived):
-            total = arrays[0][...]
-            for array in arrays[1:]:
-                total = total + array[...].astype(jnp.float32)
+            total = summed(arrays, 0)
             column = 0
             for _, start, span in batch:
                 put_sum(sum_buf, start - add_start, total[:, column : column + 2 * span])
@@ -173,17 +176,23 @@
             sum_buf, result_ref.at[:, add_point, :, columns], placed_sem
         )
         placing.start()
-    if plan.folding:
-        for distance, send_ref in enumerate(sends):
-            target = lax.rem(outer + distance, depth)
-            column = 0
-            for arrays in folded:
-                total = arrays[0][target]
-                for array in arrays[1:]:
-                    total = total + array[target].astype(jnp.float32)
-                columns = slice(column, column + total.shape[1])
-                send_ref[:, columns] = total.astype(send_ref.dtype)
-                column += total.shape[1]
+    for task, arrays, outputs in zip(plan.tasks, sources, targets):
+        groups = [arrays[i : i + task.each] for i in range(0, len(arrays), task.each)]
+        bit = lax.rem(lax.div(outer, 1 << task.stage), 2)
+        for index, out_ref in enumerate(outputs):
+            for level in range(out_ref.shape[0]):
+                if task.count == 1:
+                    source = 0
+                elif task.direct:
+                    source = lax.rem(outer + index, depth)
+                else:
+                    source = 2 * level + (1 - bit if index else bit)
+                column = 0
+                for group in groups:
+                    total = summed(group, source)
+                    columns = slice(column, column + total.shape[1])
+                    out_ref[level, :, columns] = total.astype(out_ref.dtype)
+                    column += total.shape[1]
     if plan.part:
         near_into(near_buf, there_ref, table_ref, base, planes)
         dims = (((1,), (1,)), ((), ()))
@@ -223,18 +232,35 @@
             store.wait()
 
 
+def summed(arrays, level):
+    total = arrays[0][level]
+    for array in arrays[1:]:
+        total = total + array[level].astype(jnp.float32)
+    return total
+
+
+class Task(NamedTuple):
+    batch: tuple
+    stage: int
+    direct: bool
+    each: int
+    count: int
+
+
 class Plan(NamedTuple):
     shape: tuple
     fold: int
     depth: int
     part: tuple
-    folding: tuple
+    tasks: tuple
+    takes: tuple
     adding: tuple
+    adds: tuple
     placed: bool
     later: tuple
 
 
-def step(plan, table, bands, there, folded, arrived, result):
+def step(plan, table, bands, there, sources, arrived, result):
     rows, _, _, nbands = plan.shape
     fold, depth = plan.fold, plan.depth
     points = bands.shape[3]
@@ -253,29 +279,28 @@
         out_shape += [
             jax.ShapeDtypeStruct((depth, rows, 2 * width), kind(i)) for i in range(fold)
         ]
-        out_specs += [vmem] * fold
         scratch += [
             pltpu.VMEM((2, nbands, points), jnp.bfloat16),
             pltpu.VMEM((2 * width, points), jnp.bfloat16),
             pltpu.VMEM((nbands, 2 * width), jnp.float32),
             pltpu.SemaphoreType.DMA((nbands // BLOCK, 2)),
         ]
-    if plan.folding:
-        for arrays in folded:
-            operands += arrays
-            in_specs += [vmem] * fold
-        wide = sum(2 * width for _, _, width in plan.folding)
-        out_shape += [jax.ShapeDtypeStruct((rows, wide), kind(i)) for i in range(depth)]
-        out_specs += [vmem] * depth
+    for arrays in sources + arrived:
+        operands += arrays
+        in_specs += [vmem] * len(arrays)
+    for task in plan.tasks:
+        wide = sum(2 * width for _, _, width in task.batch)
+        levels = 1 if task.direct else depth >> (task.stage + 1)
+        out_shape += [
+            jax.ShapeDtypeStruct((levels, rows, wide), kind(i)) for i in range(task.count)
+        ]
+    out_specs += [vmem] * len(out_shape)
     if plan.later:
         scratch += [
             pltpu.VMEM((2, plan.later[2], points), bands.dtype),
             pltpu.SemaphoreType.DMA((2, 2)),
         ]
     if plan.adding:
-        for arrays in arrived:
-            operands += arrays
-            in_specs += [vmem] * depth
         if plan.placed:
             aliases = {len(operands): len(out_shape)}
             operands.append(result)
@@ -303,7 +328,11 @@
     piece = outs.pop() if plan.later else None
     result = outs.pop() if plan.adding else result
     terms = outs[:fold] if plan.part else None
-    sends = outs[-depth:] if plan.folding else None
+    handed = outs[fold if plan.part else 0 :]
+    sends = []
+    for task in plan.tasks:
+        sends.append(handed[: task.count])
+        handed = handed[task.count :]
     return terms, sends, result, piece
 
 
@@ -314,19 +343,24 @@
     return list(zip(starts, widths))
 
 
-def schedule(parts):
+def schedule(parts, fold, depth):
+    stages = depth.bit_length() - 1
     kernels = []
     waiting = []
-    for index, part in enumerate(parts[:-1]):
-        folding = (parts[index - 1],) if index else ()
+    moving = []
+    for index, part in enumerate(parts):
         ready = ready_batches(waiting)
         waiting = waiting[len(ready) :]
-        kernels.append((part, folding, ready))
-        if folding:
-            waiting.append(folding)
+        tasks = [Task(batch, stage, False, 2, 2) for batch, stage in moving]
+        if 0 < index < len(parts) - 1:
+            tasks.append(Task((parts[index - 1],), 0, False, fold, 2))
+        kernels.append((part, tuple(tasks), ready))
+        ended = [task.batch for task in tasks if task.stage + 1 == stages]
+        waiting += ended
+        moving = [(task.batch, task.stage + 1) for task in tasks if task.stage + 1 < stages]
     last = tuple(parts[-2:])
-    kernels.append((parts[-1], (), ()))
-    kernels.append((None, last, ()))
+    tasks = [Task(batch, 0, True, 2, 1) for batch in ended]
+    kernels.append((None, (Task(last, 0, True, fold, depth), *tasks), ()))
     kernels.append((None, (), tuple(waiting) + (last,)))
     return kernels
 
@@ -369,31 +403,45 @@
     shape = (rows, k_dev, 2, nbands)
     depth = min(OUTER, grid_count)
     fold = grid_count // depth
-    folded, arrived = {}, {}
+    held = {}
     result = None
-    for part, folding, adding in schedule(parts):
+    for part, tasks, adding in schedule(parts, fold, depth):
         place = parts.index(part) if part else len(parts)
         later = parts[place + AHEAD] if place + AHEAD < len(parts) else None
-        plan = Plan(shape, fold, depth, part, folding, adding, result is not None, later)
+        sources = []
+        for task in tasks:
+            whole = task.stage or task.count == 1
+            keys = [task.batch] if whole else [(done,) for done in task.batch]
+            sources.append([array for key in keys for array in held.pop(key)])
+        arrived = [held.pop(batch) for batch in adding]
+        plan = Plan(
+            shape,
+            fold,
+            depth,
+            part,
+            tasks,
+            tuple(len(arrays) for arrays in sources),
+            adding,
+            tuple(len(arrays) for arrays in arrived),
+            result is not None,
+            later,
+        )
         terms, sends, result, piece = step(
-            plan,
-            table,
-            bands,
-            theres[place] if part else None,
-            [folded.pop(done) for done in folding],
-            [arrived.pop(batch) for batch in adding],
-            result,
+            plan, table, bands, theres[place] if part else None, sources, arrived, result
         )
         if later:
             theres.append(shifted(piece, "ka", -1))
         if part:
-            folded[part] = [terms[0]] + [
+            held[(part,)] = [terms[0]] + [
                 shifted(terms[i], "ga", i, fold, True) for i in range(1, fold)
             ]
-        if folding:
-            arrived[folding] = [sends[0]] + [
-                shifted(sends[i], "ga", i, fold) for i in range(1, depth)
-            ]
+        for task, arrays in zip(tasks, sends):
+            if task.direct:
+                held[task.batch] = [arrays[0]] + [
+                    shifted(arrays[i], "ga", i, fold) for i in range(1, task.count)
+                ]
+            else:
+                held[task.batch] = [arrays[0], swapped(arrays[1], "ga", fold << task.stage)]
     return result
 
 

time: 122 us -> 120 us (0.984)
  waiting for transfers between devices: 49.2 us -> 47.6 us
    ppermute x22 -> x13, starting transfers between devices: 36.1 us -> 22.6 us  [shifted(): return lax.ppermute(block, axis, route)]
    ppermute x0 -> x6, starting transfers between devices: none -> 12.6 us  [swapped(): return lax.ppermute(block, axis, [(i, i ^ distance) for i in range(count)])]
    ppermute x22 -> x13, waiting for transfers between devices: 49.2 us -> 38 us  [shifted(): return lax.ppermute(block, axis, route)]
    ppermute x0 -> x6, waiting for transfers between devices: none -> 9.65 us  [swapped(): return lax.ppermute(block, axis, [(i, i ^ distance) for i in range(count)])]
  transfers between devices with their start and end apart: 22 -> 19, of which waited for: 10 -> 11; matrix products, arithmetic and copies ran while one was open for 0% -> 1% of each run, Pallas kernels for 27% -> 27%
where the time goes in v10:
time: 120 us
  waiting for transfers between devices  47.6 us (40%)
  Pallas kernels  35.9 us (30%)
  starting transfers between devices  35.2 us (29%)
    ppermute x13, waiting for transfers between devices, shifted(): return lax.ppermute(block, axis, route)  38 us
    pallas_call x7, Pallas kernels, step(): pl.pallas_call(functools.partial(step_kernel, plan), in_specs=in_specs, o...  31.6 us
    ppermute x13, starting transfers between devices, shifted(): return lax.ppermute(block, axis, route)  22.6 us
    ppermute x6, starting transfers between devices, swapped(): return lax.ppermute(block, axis, [(i, i ^ distance) for i in range(count)])  12.6 us
    ppermute x6, waiting for transfers between devices, swapped(): return lax.ppermute(block, axis, [(i, i ^ distance) for i in range(count)])  9.65 us
    pallas_call x2, Pallas kernels, piece_of(): pl.pallas_call(functools.partial(piece_kernel, slot, start), in_specs=[pl...  4.24 us
  transfers between devices with their start and end apart: 19, of which 11 were waited for; matrix products, arithmetic and copies ran while one was open for 1% of the time, Pallas kernels for 27%

profile of v10, /device:TPU:0, one launch (start us, length us, event | category | flops | bytes accessed | tf_op | source)
XLA Modules:
  0.0 119.6 jit_solution(13821143109902785762)
XLA Ops:
  0.0 1.6 %piece_of.2.rest_0_ = bf16[2,256,2048]{2,1,0:T(8,128)(2,1)S(1)} custom-call(bf16[2,2,512,2048]{3,2,1,0:T(8,128)(2,1)} %refs_0_.9), custom_call_target="tpu_custom_call" | custom-call | flops 1000 | bytes 1000 | tf_op jit(solution)/shard_map/piece_of/pallas_call | solution.py:64
  1.7 0.0 copy-start
  1.7 0.0 copy-start.1
  1.7 2.5 %collective-permute-start.1 = (bf16[2,256,2048]{2,1,0:T(8,128)(2,1)S(1)}, bf16[2,256,2048]{2,1,0:T(8,128)(2,1)}, u32[]{:S(2)}, u32[]{:S(2)}) collective-permute-start(bf16[2,256,2048]{2,1,0:T(8,128)(2,1)S(1)} %piece_of.2.rest_0_), channel_id=1, source_target_pairs={{0,24},{8,0},{16,8},{24,16},{1,25},{9,1},{17,9},{25,17},{2,26},{10... | collective-permute-start | bytes 6291464 | tf_op jit(solution)/shard_map/ppermute | solution.py:33
  4.1 2.6 %piece_of.3 = bf16[2,256,2048]{2,1,0:T(8,128)(2,1)} custom-call(bf16[2,2,512,2048]{3,2,1,0:T(8,128)(2,1)} %refs_0_.9, bf16[2,256,2048]{2,1,0:T(8,128)(2,1)S(1)} %piece_of.2.rest_0_), custom_call_target="tpu_custom_call" | custom-call | flops 1000 | bytes 1000 | tf_op jit(solution)/shard_map/piece_of/pallas_call | solution.py:64
  6.7 0.7 collective-permute-start
  7.5 0.1 select_reduce_fusion.1
  7.6 0.1 copy.6
  7.7 0.1 fusion.4
  7.9 0.1 pad_maximum_fusion
  7.9 0.1 reshape.28
  8.0 0.1 pad_maximum_fusion.1.table_ref
  8.1 19.6 %collective-permute-done.1.refs_1_ = bf16[2,256,2048]{2,1,0:T(8,128)(2,1)} collective-permute-done((bf16[2,256,2048]{2,1,0:T(8,128)(2,1)S(1)}, bf16[2,256,2048]{2,1,0:T(8,128)(2,1)}, u32[]{:S(2)}, u32[]{:S(2)}) %collective-permute-start.1) | collective-permute-done | bytes 2097184 | tf_op jit(solution)/shard_map/ppermute | solution.py:33
  27.7 7.1 %step.7 = (f32[4,64,512]{2,1,0:T(8,128)S(1)}, bf16[4,64,512]{2,1,0:T(8,128)(2,1)S(1)}, bf16[2,192,2048]{2,1,0:T(8,128)(2,1)S(1)}) custom-call(f32[11]{0:T(128)S(1)} %pad_maximum_fusion.1.table_ref, bf16[2,2,512,2048]{3,2,1,0:T(8,128)(2,1)} %refs_0_.9, bf16[2,256,2048]{2,1,0:T(8,128)(2,1)} %collective-permute-done.1.refs_1_), custom_call_target="tpu_custom_call" | custom-call | flops 1000 | bytes 1000 | tf_op jit(solution)/shard_map/step/pallas_call | solution.py:316
  34.8 2.1 %collective-permute-start.4 = (bf16[2,192,2048]{2,1,0:T(8,128)(2,1)S(1)}, bf16[2,192,2048]{2,1,0:T(8,128)(2,1)S(1)}, u32[]{:S(2)}, u32[]{:S(2)}) collective-permute-start(bf16[2,192,2048]{2,1,0:T(8,128)(2,1)S(1)} %get-tuple-element.40), channel_id=1, source_target_pairs={{0,24},{8,0},{16,8},{24,16},{1,25},{9,1},{17,9},{25,17},{2,26},{10... | collective-permute-start | bytes 4718600 | tf_op jit(solution)/shard_map/ppermute | solution.py:33
  36.9 1.5 %collective-permute-start.2 = (bf16[4,64,512]{2,1,0:T(8,128)(2,1)S(1)}, bf16[4,64,512]{2,1,0:T(8,128)(2,1)S(1)}, u32[]{:S(2)}, u32[]{:S(2)}) collective-permute-start(bf16[4,64,512]{2,1,0:T(8,128)(2,1)S(1)} %get-tuple-element.38), channel_id=1, source_target_pairs={{0,1},{1,0},{2,3},{3,2},{4,5},{5,4},{6,7},{7,6},{8,9},{9,8},{10,11... | collective-permute-start | bytes 786440 | tf_op jit(solution)/shard_map/ppermute | solution.py:33
  38.4 11.9 %collective-permute-done.refs_1_ = bf16[2,256,2048]{2,1,0:T(8,128)(2,1)} collective-permute-done((bf16[2,256,2048]{2,1,0:T(8,128)(2,1)}, bf16[2,256,2048]{2,1,0:T(8,128)(2,1)}, u32[]{:S(2)}, u32[]{:S(2)}) %collective-permute-start) | collective-permute-done | bytes 2097184 | tf_op jit(solution)/shard_map/ppermute | solution.py:33
  50.3 7.3 %step.8 = (f32[4,64,512]{2,1,0:T(8,128)S(1)}, bf16[4,64,512]{2,1,0:T(8,128)(2,1)S(1)}, f32[2,64,512]{2,1,0:T(8,128)S(1)}, bf16[2,64,512]{2,1,0:T(8,128)(2,1)S(1)}, bf16[2,192,2048]{2,1,0:T(8,128)(2,1)S(1)}) custom-call(f32[11]{0:T(128)S(1)} %pad_maximum_fusion.1.table_ref, bf16[2,2,512,2048]{3,2,1,0:T(8,128)(2,1)} %refs_0_.9, ...), custom_call_target="tpu_custom_call" | custom-call | flops 1000 | bytes 1000 | tf_op jit(solution)/shard_map/step/pallas_call | solution.py:316
  57.6 2.0 %collective-permute-start.3 = (bf16[2,192,2048]{2,1,0:T(8,128)(2,1)S(1)}, bf16[2,192,2048]{2,1,0:T(8,128)(2,1)S(1)}, u32[]{:S(2)}, u32[]{:S(2)}) collective-permute-start(bf16[2,192,2048]{2,1,0:T(8,128)(2,1)S(1)} %get-tuple-element.39), channel_id=1, source_target_pairs={{0,24},{8,0},{16,8},{24,16},{1,25},{9,1},{17,9},{25,17},{2,26},{10... | collective-permute-start | bytes 4718600 | tf_op jit(solution)/shard_map/ppermute | solution.py:33
  59.6 1.5 %collective-permute-start.6 = (bf16[4,64,512]{2,1,0:T(8,128)(2,1)S(1)}, bf16[4,64,512]{2,1,0:T(8,128)(2,1)S(1)}, u32[]{:S(2)}, u32[]{:S(2)}) collective-permute-start(bf16[4,64,512]{2,1,0:T(8,128)(2,1)S(1)} %get-tuple-element.44), channel_id=1, source_target_pairs={{0,1},{1,0},{2,3},{3,2},{4,5},{5,4},{6,7},{7,6},{8,9},{9,8},{10,11... | collective-permute-start | bytes 786440 | tf_op jit(solution)/shard_map/ppermute | solution.py:33
  61.1 1.6 %collective-permute-start.5 = (bf16[2,64,512]{2,1,0:T(8,128)(2,1)S(1)}, bf16[2,64,512]{2,1,0:T(8,128)(2,1)S(1)}, u32[]{:S(2)}, u32[]{:S(2)}) collective-permute-start(bf16[2,64,512]{2,1,0:T(8,128)(2,1)S(1)} %get-tuple-element.42), channel_id=1, source_target_pairs={{0,2},{1,3},{2,0},{3,1},{4,6},{5,7},{6,4},{7,5},{8,10},{9,11},{10,... | collective-permute-start | bytes 393224 | tf_op jit(solution)/shard_map/ppermute | solution.py:38
  62.6 3.4 %collective-permute-done.5.refs_3_ = bf16[2,64,512]{2,1,0:T(8,128)(2,1)S(1)} collective-permute-done((bf16[2,64,512]{2,1,0:T(8,128)(2,1)S(1)}, bf16[2,64,512]{2,1,0:T(8,128)(2,1)S(1)}, u32[]{:S(2)}, u32[]{:S(2)}) %collective-permute-start.5) | collective-permute-done | bytes 131104 | tf_op jit(solution)/shard_map/ppermute | solution.py:38
  66.0 0.8 collective-permute-done.6.refs_5_
  66.8 0.2 collective-permute-done.4.refs_1_
  67.0 5.3 %step.9 = (f32[4,64,384]{2,1,0:T(8,128)S(1)}, bf16[4,64,384]{2,1,0:T(8,128)(2,1)S(1)}, f32[1,64,512]{2,1,0:T(8,128)S(1)}, bf16[1,64,512]{2,1,0:T(8,128)(2,1)S(1)...) custom-call(f32[11]{0:T(128)S(1)} %pad_maximum_fusion.1.table_ref, ...), custom_call_target="tpu_custom_call" | custom-call | flops 1000 | bytes 1000 | tf_op jit(solution)/shard_map/step/pallas_call | solution.py:316
  72.3 2.1 %collective-permute-start.11 = (bf16[2,128,2048]{2,1,0:T(8,128)(2,1)S(1)}, bf16[2,128,2048]{2,1,0:T(8,128)(2,1)S(1)}, u32[]{:S(2)}, u32[]{:S(2)}) collective-permute-start(bf16[2,128,2048]{2,1,0:T(8,128)(2,1)S(1)} %get-tuple-element.53), channel_id=1, source_target_pairs={{0,24},{8,0},{16,8},{24,16},{1,25},{9,1},{17,9},{25,17},{2,26},{10... | collective-permute-start | bytes 3145736 | tf_op jit(solution)/shard_map/ppermute | solution.py:33
  74.4 1.5 %collective-permute-start.8 = (bf16[4,64,384]{2,1,0:T(8,128)(2,1)S(1)}, bf16[4,64,384]{2,1,0:T(8,128)(2,1)S(1)}, u32[]{:S(2)}, u32[]{:S(2)}) collective-permute-start(bf16[4,64,384]{2,1,0:T(8,128)(2,1)S(1)} %get-tuple-element.48), channel_id=1, source_target_pairs={{0,1},{1,0},{2,3},{3,2},{4,5},{5,4},{6,7},{7,6},{8,9},{9,8},{10,11... | collective-permute-start | bytes 589832 | tf_op jit(solution)/shard_map/ppermute | solution.py:33
  75.9 1.6 %collective-permute-start.7 = (bf16[2,64,512]{2,1,0:T(8,128)(2,1)S(1)}, bf16[2,64,512]{2,1,0:T(8,128)(2,1)S(1)}, u32[]{:S(2)}, u32[]{:S(2)}) collective-permute-start(bf16[2,64,512]{2,1,0:T(8,128)(2,1)S(1)} %get-tuple-element.46), channel_id=1, source_target_pairs={{0,2},{1,3},{2,0},{3,1},{4,6},{5,7},{6,4},{7,5},{8,10},{9,11},{10,... | collective-permute-start | bytes 393224 | tf_op jit(solution)/shard_map/ppermute | solution.py:38
  77.5 2.6 %collective-permute-start.9 = (bf16[1,64,512]{2,1,0:T(8,128)(2,1)S(1)}, bf16[1,64,512]{2,1,0:T(8,128)(2,1)S(1)}, u32[]{:S(2)}, u32[]{:S(2)}) collective-permute-start(bf16[1,64,512]{2,1,0:T(8,128)(2,1)S(1)} %get-tuple-element.50), channel_id=1, source_target_pairs={{0,4},{1,5},{2,6},{3,7},{4,0},{5,1},{6,2},{7,3},{8,12},{9,13},{10,... | collective-permute-start | bytes 196616 | tf_op jit(solution)/shard_map/ppermute | solution.py:38
  80.1 2.6 %collective-permute-done.9.refs_7_ = bf16[1,64,512]{2,1,0:T(8,128)(2,1)S(1)} collective-permute-done((bf16[1,64,512]{2,1,0:T(8,128)(2,1)S(1)}, bf16[1,64,512]{2,1,0:T(8,128)(2,1)S(1)}, u32[]{:S(2)}, u32[]{:S(2)}) %collective-permute-start.9) | collective-permute-done | bytes 65568 | tf_op jit(solution)/shard_map/ppermute | solution.py:38
  82.7 1.2 collective-permute-done.3.refs_1_
  83.9 5.1 %step.10 = (f32[4,64,384]{2,1,0:T(8,128)S(1)}, bf16[4,64,384]{2,1,0:T(8,128)(2,1)S(1)}, f32[1,64,512]{2,1,0:T(8,128)S(1)}, bf16[1,64,512]{2,1,0:T(8,128)(2,1)S(1...) custom-call(f32[11]{0:T(128)S(1)} %pad_maximum_fusion.1.table_ref, ...), custom_call_target="tpu_custom_call" | custom-call | flops 1000 | bytes 1000 | tf_op jit(solution)/shard_map/step/pallas_call | solution.py:316
  88.9 1.6 %collective-permute-start.12 = (bf16[2,64,384]{2,1,0:T(8,128)(2,1)S(1)}, bf16[2,64,384]{2,1,0:T(8,128)(2,1)S(1)}, u32[]{:S(2)}, u32[]{:S(2)}) collective-permute-start(bf16[2,64,384]{2,1,0:T(8,128)(2,1)S(1)} %get-tuple-element.55), channel_id=1, source_target_pairs={{0,2},{1,3},{2,0},{3,1},{4,6},{5,7},{6,4},{7,5},{8,10},{9,11},{10,... | collective-permute-start | bytes 294920 | tf_op jit(solution)/shard_map/ppermute | solution.py:38
  90.6 2.6 %collective-permute-start.13 = (bf16[1,64,512]{2,1,0:T(8,128)(2,1)S(1)}, bf16[1,64,512]{2,1,0:T(8,128)(2,1)S(1)}, u32[]{:S(2)}, u32[]{:S(2)}) collective-permute-start(bf16[1,64,512]{2,1,0:T(8,128)(2,1)S(1)} %get-tuple-element.57), channel_id=1, source_target_pairs={{0,4},{1,5},{2,6},{3,7},{4,0},{5,1},{6,2},{7,3},{8,12},{9,13},{10,... | collective-permute-start | bytes 196616 | tf_op jit(solution)/shard_map/ppermute | solution.py:38
  93.2 1.5 %collective-permute-start.10 = (bf16[4,64,384]{2,1,0:T(8,128)(2,1)S(1)}, bf16[4,64,384]{2,1,0:T(8,128)(2,1)S(1)}, u32[]{:S(2)}, u32[]{:S(2)}) collective-permute-start(bf16[4,64,384]{2,1,0:T(8,128)(2,1)S(1)} %get-tuple-element.52), channel_id=1, source_target_pairs={{0,1},{1,0},{2,3},{3,2},{4,5},{5,4},{6,7},{7,6},{8,9},{9,8},{10,11... | collective-permute-start | bytes 589832 | tf_op jit(solution)/shard_map/ppermute | solution.py:33
  94.7 1.4 %collective-permute-done.13.refs_5_ = bf16[1,64,512]{2,1,0:T(8,128)(2,1)S(1)} collective-permute-done((bf16[1,64,512]{2,1,0:T(8,128)(2,1)S(1)}, bf16[1,64,512]{2,1,0:T(8,128)(2,1)S(1)}, u32[]{:S(2)}, u32[]{:S(2)}) %collective-permute-start.13) | collective-permute-done | bytes 65568 | tf_op jit(solution)/shard_map/ppermute | solution.py:38
  96.0 4.8 %step.11 = (f32[4,64,256]{2,1,0:T(8,128)S(1)}, bf16[4,64,256]{2,1,0:T(8,128)(2,1)S(1)}, f32[1,64,384]{2,1,0:T(8,128)S(1)}, bf16[1,64,384]{2,1,0:T(8,128)(2,1)S(1)}, f32[64,2,2,512]{3,2,1,0:T(2,128)}) custom-call(f32[11]{0:T(128)S(1)} %pad_maximum_fusion.1.table_ref, bf16[2,2,512,2048]{3,2,1,0:T(8,128)(2,1)} %refs_0_.9, ...), custom_call_target="tpu_custom_call", output_to_operand_aliasing={{4}: (7, {})} | custom-call | flops 1000 | bytes 1000 | tf_op jit(solution)/shard_map/step/pallas_call | solution.py:316
  100.8 1.6 %collective-permute-start.14 = (bf16[4,64,256]{2,1,0:T(8,128)(2,1)S(1)}, bf16[4,64,256]{2,1,0:T(8,128)(2,1)S(1)}, u32[]{:S(2)}, u32[]{:S(2)}) collective-permute-start(bf16[4,64,256]{2,1,0:T(8,128)(2,1)S(1)} %get-tuple-element.60), channel_id=1, source_target_pairs={{0,1},{1,0},{2,3},{3,2},{4,5},{5,4},{6,7},{7,6},{8,9},{9,8},{10,11... | collective-permute-start | bytes 393224 | tf_op jit(solution)/shard_map/ppermute | solution.py:33
  102.4 2.7 %collective-permute-start.15 = (bf16[1,64,384]{2,1,0:T(8,128)(2,1)S(1)}, bf16[1,64,384]{2,1,0:T(8,128)(2,1)S(1)}, u32[]{:S(2)}, u32[]{:S(2)}) collective-permute-start(bf16[1,64,384]{2,1,0:T(8,128)(2,1)S(1)} %get-tuple-element.62), channel_id=1, source_target_pairs={{0,4},{1,5},{2,6},{3,7},{4,0},{5,1},{6,2},{7,3},{8,12},{9,13},{10,... | collective-permute-start | bytes 147464 | tf_op jit(solution)/shard_map/ppermute | solution.py:38
  105.1 2.3 %collective-permute-done.15.refs_5_ = bf16[1,64,384]{2,1,0:T(8,128)(2,1)S(1)} collective-permute-done((bf16[1,64,384]{2,1,0:T(8,128)(2,1)S(1)}, bf16[1,64,384]{2,1,0:T(8,128)(2,1)S(1)}, u32[]{:S(2)}, u32[]{:S(2)}) %collective-permute-start.15) | collective-permute-done | bytes 49184 | tf_op jit(solution)/shard_map/ppermute | solution.py:38
  107.4 0.6 step.12
  108.0 2.6 %collective-permute-start.16 = (bf16[1,64,640]{2,1,0:T(8,128)(2,1)S(1)}, bf16[1,64,640]{2,1,0:T(8,128)(2,1)S(1)}, u32[]{:S(2)}, u32[]{:S(2)}) collective-permute-start(bf16[1,64,640]{2,1,0:T(8,128)(2,1)S(1)} %get-tuple-element.65), channel_id=1, source_target_pairs={{0,2},{1,3},{2,4},{3,5},{4,6},{5,7},{6,0},{7,1},{8,10},{9,11},{10,... | collective-permute-start | bytes 245768 | tf_op jit(solution)/shard_map/ppermute | solution.py:33
  110.6 2.2 %collective-permute-start.17 = (bf16[1,64,640]{2,1,0:T(8,128)(2,1)S(1)}, bf16[1,64,640]{2,1,0:T(8,128)(2,1)S(1)}, u32[]{:S(2)}, u32[]{:S(2)}) collective-permute-start(bf16[1,64,640]{2,1,0:T(8,128)(2,1)S(1)} %get-tuple-element.66), channel_id=1, source_target_pairs={{0,4},{1,5},{2,6},{3,7},{4,0},{5,1},{6,2},{7,3},{8,12},{9,13},{10,... | collective-permute-start | bytes 245768 | tf_op jit(solution)/shard_map/ppermute | solution.py:33
  112.8 1.0 collective-permute-start.18
  113.7 1.6 %collective-permute-done.16.refs_2_ = bf16[1,64,640]{2,1,0:T(8,128)(2,1)S(1)} collective-permute-done((bf16[1,64,640]{2,1,0:T(8,128)(2,1)S(1)}, bf16[1,64,640]{2,1,0:T(8,128)(2,1)S(1)}, u32[]{:S(2)}, u32[]{:S(2)}) %collective-permute-start.16) | collective-permute-done | bytes 81952 | tf_op jit(solution)/shard_map/ppermute | solution.py:33
  115.3 2.7 %collective-permute-done.17.refs_3_ = bf16[1,64,640]{2,1,0:T(8,128)(2,1)S(1)} collective-permute-done((bf16[1,64,640]{2,1,0:T(8,128)(2,1)S(1)}, bf16[1,64,640]{2,1,0:T(8,128)(2,1)S(1)}, u32[]{:S(2)}, u32[]{:S(2)}) %collective-permute-start.17) | collective-permute-done | bytes 81952 | tf_op jit(solution)/shard_map/ppermute | solution.py:33
  118.0 0.0 collective-permute-done.18.refs_4_
  118.0 1.5 %step.13 = f32[64,2,2,512]{3,2,1,0:T(2,128)} custom-call(f32[11]{0:T(128)S(1)} %pad_maximum_fusion.1.table_ref, f32[1,64,384]{2,1,0:T(8,128)S(1)} %get-tuple-element.63.refs_0_, f32[1,64,640]{2,1,0:T(8,128)S(1)} %get-tuple-element.64.refs_1_, bf16[1,64,640]{2,1,0:T(8,128)(2,1)S(1)} %collective-permute-done.16.refs_2_, ...), custom_call_target="tpu_custom_call", output_to_operand_aliasing={{}: (6, {})} | custom-call | flops 1000 | bytes 1000 | tf_op jit(solution)/shard_map/step/pallas_call | solution.py:316
  (11 shorter events, 0.0 us)
Async XLA Ops:
  1.7 5.8 %copy-start = (s32[2]{0:T(128)S(1)}, s32[2]{0:T(128)}, u32[]{:S(2)}) copy-start(s32[2]{0:T(128)} %param.4) | copy-start | bytes 28
  1.7 5.8 %copy-start.1 = (s32[2]{0:T(128)S(1)}, s32[2]{0:T(128)}, u32[]{:S(2)}) copy-start(s32[2]{0:T(128)} %param.5) | copy-start | bytes 28
  1.7 26.0 %collective-permute-start.1 = (bf16[2,256,2048]{2,1,0:T(8,128)(2,1)S(1)}, bf16[2,256,2048]{2,1,0:T(8,128)(2,1)}, u32[]{:S(2)}, u32[]{:S(2)}) collective-permute-start(bf16[2,256,2048]{2,1,0:T(8,128)(2,1)S(1)} %piece_of.2.rest_0_), channel_id=1, source_target_pairs={{0,24},{8,0},{16,8},{24,16},{1,25},{9,1},{17,9},{25,17},{2,26},{10... | collective-permute-start | bytes 6291464 | tf_op jit(solution)/shard_map/ppermute | solution.py:33
  6.7 43.5 %collective-permute-start = (bf16[2,256,2048]{2,1,0:T(8,128)(2,1)}, bf16[2,256,2048]{2,1,0:T(8,128)(2,1)}, u32[]{:S(2)}, u32[]{:S(2)}) collective-permute-start(bf16[2,256,2048]{2,1,0:T(8,128)(2,1)} %piece_of.3), channel_id=1, source_target_pairs={{0,24},{8,0},{16,8},{24,16},{1,25},{9,1},{17,9},{25,17},{2,26},{10... | collective-permute-start | bytes 6291464 | tf_op jit(solution)/shard_map/ppermute | solution.py:33
  34.8 32.2 %collective-permute-start.4 = (bf16[2,192,2048]{2,1,0:T(8,128)(2,1)S(1)}, bf16[2,192,2048]{2,1,0:T(8,128)(2,1)S(1)}, u32[]{:S(2)}, u32[]{:S(2)}) collective-permute-start(bf16[2,192,2048]{2,1,0:T(8,128)(2,1)S(1)} %get-tuple-element.40), channel_id=1, source_target_pairs={{0,24},{8,0},{16,8},{24,16},{1,25},{9,1},{17,9},{25,17},{2,26},{10... | collective-permute-start | bytes 4718600 | tf_op jit(solution)/shard_map/ppermute | solution.py:33
  36.9 13.4 %collective-permute-start.2 = (bf16[4,64,512]{2,1,0:T(8,128)(2,1)S(1)}, bf16[4,64,512]{2,1,0:T(8,128)(2,1)S(1)}, u32[]{:S(2)}, u32[]{:S(2)}) collective-permute-start(bf16[4,64,512]{2,1,0:T(8,128)(2,1)S(1)} %get-tuple-element.38), channel_id=1, source_target_pairs={{0,1},{1,0},{2,3},{3,2},{4,5},{5,4},{6,7},{7,6},{8,9},{9,8},{10,11... | collective-permute-start | bytes 786440 | tf_op jit(solution)/shard_map/ppermute | solution.py:33
  57.6 26.3 %collective-permute-start.3 = (bf16[2,192,2048]{2,1,0:T(8,128)(2,1)S(1)}, bf16[2,192,2048]{2,1,0:T(8,128)(2,1)S(1)}, u32[]{:S(2)}, u32[]{:S(2)}) collective-permute-start(bf16[2,192,2048]{2,1,0:T(8,128)(2,1)S(1)} %get-tuple-element.39), channel_id=1, source_target_pairs={{0,24},{8,0},{16,8},{24,16},{1,25},{9,1},{17,9},{25,17},{2,26},{10... | collective-permute-start | bytes 4718600 | tf_op jit(solution)/shard_map/ppermute | solution.py:33
  59.6 7.2 %collective-permute-start.6 = (bf16[4,64,512]{2,1,0:T(8,128)(2,1)S(1)}, bf16[4,64,512]{2,1,0:T(8,128)(2,1)S(1)}, u32[]{:S(2)}, u32[]{:S(2)}) collective-permute-start(bf16[4,64,512]{2,1,0:T(8,128)(2,1)S(1)} %get-tuple-element.44), channel_id=1, source_target_pairs={{0,1},{1,0},{2,3},{3,2},{4,5},{5,4},{6,7},{7,6},{8,9},{9,8},{10,11... | collective-permute-start | bytes 786440 | tf_op jit(solution)/shard_map/ppermute | solution.py:33
  61.1 5.0 %collective-permute-start.5 = (bf16[2,64,512]{2,1,0:T(8,128)(2,1)S(1)}, bf16[2,64,512]{2,1,0:T(8,128)(2,1)S(1)}, u32[]{:S(2)}, u32[]{:S(2)}) collective-permute-start(bf16[2,64,512]{2,1,0:T(8,128)(2,1)S(1)} %get-tuple-element.42), channel_id=1, source_target_pairs={{0,2},{1,3},{2,0},{3,1},{4,6},{5,7},{6,4},{7,5},{8,10},{9,11},{10,... | collective-permute-start | bytes 393224 | tf_op jit(solution)/shard_map/ppermute | solution.py:38
  72.3 23.7 %collective-permute-start.11 = (bf16[2,128,2048]{2,1,0:T(8,128)(2,1)S(1)}, bf16[2,128,2048]{2,1,0:T(8,128)(2,1)S(1)}, u32[]{:S(2)}, u32[]{:S(2)}) collective-permute-start(bf16[2,128,2048]{2,1,0:T(8,128)(2,1)S(1)} %get-tuple-element.53), channel_id=1, source_target_pairs={{0,24},{8,0},{16,8},{24,16},{1,25},{9,1},{17,9},{25,17},{2,26},{10... | collective-permute-start | bytes 3145736 | tf_op jit(solution)/shard_map/ppermute | solution.py:33
  74.4 8.3 %collective-permute-start.8 = (bf16[4,64,384]{2,1,0:T(8,128)(2,1)S(1)}, bf16[4,64,384]{2,1,0:T(8,128)(2,1)S(1)}, u32[]{:S(2)}, u32[]{:S(2)}) collective-permute-start(bf16[4,64,384]{2,1,0:T(8,128)(2,1)S(1)} %get-tuple-element.48), channel_id=1, source_target_pairs={{0,1},{1,0},{2,3},{3,2},{4,5},{5,4},{6,7},{7,6},{8,9},{9,8},{10,11... | collective-permute-start | bytes 589832 | tf_op jit(solution)/shard_map/ppermute | solution.py:33
  75.9 6.7 %collective-permute-start.7 = (bf16[2,64,512]{2,1,0:T(8,128)(2,1)S(1)}, bf16[2,64,512]{2,1,0:T(8,128)(2,1)S(1)}, u32[]{:S(2)}, u32[]{:S(2)}) collective-permute-start(bf16[2,64,512]{2,1,0:T(8,128)(2,1)S(1)} %get-tuple-element.46), channel_id=1, source_target_pairs={{0,2},{1,3},{2,0},{3,1},{4,6},{5,7},{6,4},{7,5},{8,10},{9,11},{10,... | collective-permute-start | bytes 393224 | tf_op jit(solution)/shard_map/ppermute | solution.py:38
  77.5 5.2 %collective-permute-start.9 = (bf16[1,64,512]{2,1,0:T(8,128)(2,1)S(1)}, bf16[1,64,512]{2,1,0:T(8,128)(2,1)S(1)}, u32[]{:S(2)}, u32[]{:S(2)}) collective-permute-start(bf16[1,64,512]{2,1,0:T(8,128)(2,1)S(1)} %get-tuple-element.50), channel_id=1, source_target_pairs={{0,4},{1,5},{2,6},{3,7},{4,0},{5,1},{6,2},{7,3},{8,12},{9,13},{10,... | collective-permute-start | bytes 196616 | tf_op jit(solution)/shard_map/ppermute | solution.py:38
  88.9 7.1 %collective-permute-start.12 = (bf16[2,64,384]{2,1,0:T(8,128)(2,1)S(1)}, bf16[2,64,384]{2,1,0:T(8,128)(2,1)S(1)}, u32[]{:S(2)}, u32[]{:S(2)}) collective-permute-start(bf16[2,64,384]{2,1,0:T(8,128)(2,1)S(1)} %get-tuple-element.55), channel_id=1, source_target_pairs={{0,2},{1,3},{2,0},{3,1},{4,6},{5,7},{6,4},{7,5},{8,10},{9,11},{10,... | collective-permute-start | bytes 294920 | tf_op jit(solution)/shard_map/ppermute | solution.py:38
  90.6 5.5 %collective-permute-start.13 = (bf16[1,64,512]{2,1,0:T(8,128)(2,1)S(1)}, bf16[1,64,512]{2,1,0:T(8,128)(2,1)S(1)}, u32[]{:S(2)}, u32[]{:S(2)}) collective-permute-start(bf16[1,64,512]{2,1,0:T(8,128)(2,1)S(1)} %get-tuple-element.57), channel_id=1, source_target_pairs={{0,4},{1,5},{2,6},{3,7},{4,0},{5,1},{6,2},{7,3},{8,12},{9,13},{10,... | collective-permute-start | bytes 196616 | tf_op jit(solution)/shard_map/ppermute | solution.py:38
  93.2 11.9 %collective-permute-start.10 = (bf16[4,64,384]{2,1,0:T(8,128)(2,1)S(1)}, bf16[4,64,384]{2,1,0:T(8,128)(2,1)S(1)}, u32[]{:S(2)}, u32[]{:S(2)}) collective-permute-start(bf16[4,64,384]{2,1,0:T(8,128)(2,1)S(1)} %get-tuple-element.52), channel_id=1, source_target_pairs={{0,1},{1,0},{2,3},{3,2},{4,5},{5,4},{6,7},{7,6},{8,9},{9,8},{10,11... | collective-permute-start | bytes 589832 | tf_op jit(solution)/shard_map/ppermute | solution.py:33
  100.8 6.6 %collective-permute-start.14 = (bf16[4,64,256]{2,1,0:T(8,128)(2,1)S(1)}, bf16[4,64,256]{2,1,0:T(8,128)(2,1)S(1)}, u32[]{:S(2)}, u32[]{:S(2)}) collective-permute-start(bf16[4,64,256]{2,1,0:T(8,128)(2,1)S(1)} %get-tuple-element.60), channel_id=1, source_target_pairs={{0,1},{1,0},{2,3},{3,2},{4,5},{5,4},{6,7},{7,6},{8,9},{9,8},{10,11... | collective-permute-start | bytes 393224 | tf_op jit(solution)/shard_map/ppermute | solution.py:33
  102.4 5.0 %collective-permute-start.15 = (bf16[1,64,384]{2,1,0:T(8,128)(2,1)S(1)}, bf16[1,64,384]{2,1,0:T(8,128)(2,1)S(1)}, u32[]{:S(2)}, u32[]{:S(2)}) collective-permute-start(bf16[1,64,384]{2,1,0:T(8,128)(2,1)S(1)} %get-tuple-element.62), channel_id=1, source_target_pairs={{0,4},{1,5},{2,6},{3,7},{4,0},{5,1},{6,2},{7,3},{8,12},{9,13},{10,... | collective-permute-start | bytes 147464 | tf_op jit(solution)/shard_map/ppermute | solution.py:38
  108.0 7.3 %collective-permute-start.16 = (bf16[1,64,640]{2,1,0:T(8,128)(2,1)S(1)}, bf16[1,64,640]{2,1,0:T(8,128)(2,1)S(1)}, u32[]{:S(2)}, u32[]{:S(2)}) collective-permute-start(bf16[1,64,640]{2,1,0:T(8,128)(2,1)S(1)} %get-tuple-element.65), channel_id=1, source_target_pairs={{0,2},{1,3},{2,4},{3,5},{4,6},{5,7},{6,0},{7,1},{8,10},{9,11},{10,... | collective-permute-start | bytes 245768 | tf_op jit(solution)/shard_map/ppermute | solution.py:33
  110.6 7.4 %collective-permute-start.17 = (bf16[1,64,640]{2,1,0:T(8,128)(2,1)S(1)}, bf16[1,64,640]{2,1,0:T(8,128)(2,1)S(1)}, u32[]{:S(2)}, u32[]{:S(2)}) collective-permute-start(bf16[1,64,640]{2,1,0:T(8,128)(2,1)S(1)} %get-tuple-element.66), channel_id=1, source_target_pairs={{0,4},{1,5},{2,6},{3,7},{4,0},{5,1},{6,2},{7,3},{8,12},{9,13},{10,... | collective-permute-start | bytes 245768 | tf_op jit(solution)/shard_map/ppermute | solution.py:33
  112.8 5.3 %collective-permute-start.18 = (bf16[1,64,640]{2,1,0:T(8,128)(2,1)S(1)}, bf16[1,64,640]{2,1,0:T(8,128)(2,1)S(1)}, u32[]{:S(2)}, u32[]{:S(2)}) collective-permute-start(bf16[1,64,640]{2,1,0:T(8,128)(2,1)S(1)} %get-tuple-element.67), channel_id=1, source_target_pairs={{0,6},{1,7},{2,0},{3,1},{4,2},{5,3},{6,4},{7,5},{8,14},{9,15},{10,... | collective-permute-start | bytes 245768 | tf_op jit(solution)/shard_map/ppermute | solution.py:33

commit v11 on v10

--- a/solution.py
+++ b/solution.py
@@ -117,33 +117,35 @@
     me = table_ref[k_dev * stride].astype(jnp.int32)
     place, outer = lax.rem(me, fold), lax.div(me, fold)
     if plan.part:
-        bands_ref, there_ref = take(2)
+        bands_ref, phased_ref = take(2)
     sources = [take(count) for count in plan.takes]
     arrived = [take(count) for count in plan.adds]
     if plan.adding and plan.placed:
         take(1)
-    outs = take(fold) if plan.part else None
+    given_ref = take(1)[0] if plan.near == "give" else None
+    outs = take(len(plan.ways))
     targets = [take(task.count) for task in plan.tasks]
     result_ref = take(1)[0] if plan.adding else None
     piece_ref = take(1)[0] if plan.later else None
     if plan.part:
-        own_buf, near_buf, terms_buf, own_sems = take(4)
-        slot = plan.part[0]
+        own_buf, own_sems = take(2)
+        slot, _, width = plan.part
         base = slot * stride
         point = table_ref[base].astype(jnp.int32)
-        width = there_ref.shape[1]
-        blocks = nbands // BLOCK
-        own = [
-            pltpu.make_async_copy(
-                bands_ref.at[point, part, pl.ds(block * BLOCK, BLOCK), :],
-                own_buf.at[part, pl.ds(block * BLOCK, BLOCK), :],
-                own_sems.at[block, part],
-            )
-            for block in range(blocks)
-            for part in range(2)
-        ]
-        for copy in own:
-            copy.start()
+        own = []
+        for way, distance in enumerate(plan.ways):
+            target = lax.rem(place + distance, fold)
+            own.append([])
+            for part in range(2):
+                for level in range(depth):
+                    first = pl.multiple_of((level * fold + target) * rows, rows)
+                    copy = pltpu.make_async_copy(
+                        bands_ref.at[point, part, pl.ds(first, rows), :],
+                        own_buf.at[way, part, pl.ds(level * rows, rows), :],
+                        own_sems.at[way, part, level],
+                    )
+                    copy.start()
+                    own[way].append(copy)
     if plan.later:
         piece_buf, piece_sems = take(2)
         later_slot, later_start, later_width = plan.later
@@ -163,13 +165,10 @@
             copy.start()
     if plan.adding:
         sum_buf, placed_sem = take(2)
-        add_slot, add_start, _ = plan.adding[0][0]
-        for batch, arrays in zip(plan.adding, arrived):
-            total = summed(arrays, 0)
-            column = 0
-            for _, start, span in batch:
-                put_sum(sum_buf, start - add_start, total[:, column : column + 2 * span])
-                column += 2 * span
+        add_slot, add_start, pieces = plan.adding
+        for index, column, start, span in pieces:
+            total = summed(arrived[index], 0, slice(column, column + 2 * span))
+            put_sum(sum_buf, start - add_start, total)
         add_point = table_ref[add_slot * stride].astype(jnp.int32)
         columns = pl.ds(add_start, sum_buf.shape[2])
         placing = pltpu.make_async_copy(
@@ -181,10 +180,8 @@
         bit = lax.rem(lax.div(outer, 1 << task.stage), 2)
         for index, out_ref in enumerate(outputs):
             for level in range(out_ref.shape[0]):
-                if task.count == 1:
-                    source = 0
-                elif task.direct:
-                    source = lax.rem(outer + index, depth)
+                if task.direct:
+                    source = partner(outer, index)
                 else:
                     source = 2 * level + (1 - bit if index else bit)
                 column = 0
@@ -194,19 +191,22 @@
                     out_ref[level, :, columns] = total.astype(out_ref.dtype)
                     column += total.shape[1]
     if plan.part:
-        near_into(near_buf, there_ref, table_ref, base, planes)
+        near_ref = phased_ref
+        if plan.near != "use":
+            near_ref = given_ref if plan.near == "give" else take(1)[0]
+            near_into(near_ref, phased_ref, table_ref, base, planes)
         dims = (((1,), (1,)), ((), ()))
-        points = there_ref.shape[2]
+        points = own_buf.shape[3]
         run = points // 2 if width <= SPLIT else points
-        for block in range(blocks):
-            lines = pl.ds(block * BLOCK, BLOCK)
+        for way, out_ref in enumerate(outs):
             of_both = []
             for part in range(2):
-                own[2 * block + part].wait()
+                for copy in own[way][part * depth : (part + 1) * depth]:
+                    copy.wait()
                 products = [
                     lax.dot_general(
-                        own_buf[part, lines, pl.ds(first, run)],
-                        near_buf[:, pl.ds(first, run)],
+                        own_buf[way, part, :, pl.ds(first, run)],
+                        near_ref[:, pl.ds(first, run)],
                         dims,
                         preferred_element_type=jnp.float32,
                     )
@@ -214,17 +214,16 @@
                 ]
                 of_both.append(sum(products[1:], products[0]))
             of_re, of_im = of_both
-            terms_buf[lines, :width] = of_re[:, :width] + of_im[:, width:]
-            terms_buf[lines, width:] = of_re[:, width:] - of_im[:, :width]
-            if plan.later and block == 0:
+            real_part = (of_re[:, :width] + of_im[:, width:]).astype(out_ref.dtype)
+            imag_part = (of_re[:, width:] - of_im[:, :width]).astype(out_ref.dtype)
+            for level in range(depth):
+                lines = slice(level * rows, (level + 1) * rows)
+                out_ref[level, :, :width] = real_part[lines]
+                out_ref[level, :, width:] = imag_part[lines]
+            if plan.later and way == 0:
                 for load, store in zip(loads, stores):
                     load.wait()
                     store.start()
-        for distance, out_ref in enumerate(outs):
-            target = lax.rem(place + distance, fold)
-            for level in range(depth):
-                first = pl.multiple_of((level * fold + target) * rows, rows)
-                out_ref[level] = terms_buf[pl.ds(first, rows), :].astype(out_ref.dtype)
     if plan.adding:
         placing.wait()
     if plan.later:
@@ -232,10 +231,17 @@
             store.wait()
 
 
-def summed(arrays, level):
-    total = arrays[0][level]
+def partner(outer, distance):
+    low, high = lax.rem(outer, 2), lax.rem(lax.div(outer, 2), 2)
+    low = 1 - low if distance % 2 else low
+    high = 1 - high if distance // 2 else high
+    return outer - lax.rem(outer, 4) + 2 * high + low
+
+
+def summed(arrays, level, columns=slice(None)):
+    total = arrays[0][level, :, columns]
     for array in arrays[1:]:
-        total = total + array[level].astype(jnp.float32)
+        total = total + array[level, :, columns].astype(jnp.float32)
     return total
 
 
@@ -252,6 +258,8 @@
     fold: int
     depth: int
     part: tuple
+    ways: tuple
+    near: str
     tasks: tuple
     takes: tuple
     adding: tuple
@@ -260,7 +268,7 @@
     later: tuple
 
 
-def step(plan, table, bands, there, sources, arrived, result):
+def step(plan, table, bands, phased, sources, arrived, result):
     rows, _, _, nbands = plan.shape
     fold, depth = plan.fold, plan.depth
     points = bands.shape[3]
@@ -274,16 +282,16 @@
 
     if plan.part:
         width = plan.part[2]
-        operands += [bands, there]
+        operands += [bands, phased]
         in_specs += [hbm, vmem]
+        if plan.near == "give":
+            out_shape.append(jax.ShapeDtypeStruct((2 * width, points), jnp.bfloat16))
         out_shape += [
-            jax.ShapeDtypeStruct((depth, rows, 2 * width), kind(i)) for i in range(fold)
+            jax.ShapeDtypeStruct((depth, rows, 2 * width), kind(way)) for way in plan.ways
         ]
         scratch += [
-            pltpu.VMEM((2, nbands, points), jnp.bfloat16),
-            pltpu.VMEM((2 * width, points), jnp.bfloat16),
-            pltpu.VMEM((nbands, 2 * width), jnp.float32),
-            pltpu.SemaphoreType.DMA((nbands // BLOCK, 2)),
+            pltpu.VMEM((len(plan.ways), 2, depth * rows, points), jnp.bfloat16),
+            pltpu.SemaphoreType.DMA((len(plan.ways), 2, depth)),
         ]
     for arrays in sources + arrived:
         operands += arrays
@@ -307,11 +315,13 @@
             in_specs.append(hbm)
         out_shape.append(jax.ShapeDtypeStruct(plan.shape, jnp.float32))
         out_specs.append(hbm)
-        lanes = sum(width for batch in plan.adding for _, _, width in batch)
+        lanes = sum(span for _, _, _, span in plan.adding[2])
         scratch += [pltpu.VMEM((rows, 2, lanes), jnp.float32), pltpu.SemaphoreType.DMA]
     if plan.later:
         out_shape.append(jax.ShapeDtypeStruct((2, plan.later[2], points), bands.dtype))
         out_specs.append(hbm)
+    if plan.near == "make":
+        scratch.append(pltpu.VMEM((2 * width, points), jnp.bfloat16))
     outs = list(
         pl.pallas_call(
             functools.partial(step_kernel, plan),
@@ -327,13 +337,14 @@
     )
     piece = outs.pop() if plan.later else None
     result = outs.pop() if plan.adding else result
-    terms = outs[:fold] if plan.part else None
-    handed = outs[fold if plan.part else 0 :]
+    near = outs.pop(0) if plan.near == "give" else None
+    terms = outs[: len(plan.ways)]
+    handed = outs[len(plan.ways) :]
     sends = []
     for task in plan.tasks:
         sends.append(handed[: task.count])
         handed = handed[task.count :]
-    return terms, sends, result, piece
+    return terms, near, sends, result, piece
 
 
 def cuts(nbands, first):
@@ -344,31 +355,40 @@
 
 
 def schedule(parts, fold, depth):
-    stages = depth.bit_length() - 1
+    every, others = tuple(range(fold)), tuple(range(1, fold))
+    count = len(parts)
     kernels = []
-    waiting = []
-    moving = []
+    waiting, halved, crossed = [], [], []
     for index, part in enumerate(parts):
-        ready = ready_batches(waiting)
+        ready = ready_parts(waiting)
         waiting = waiting[len(ready) :]
-        tasks = [Task(batch, stage, False, 2, 2) for batch, stage in moving]
-        if 0 < index < len(parts) - 1:
-            tasks.append(Task((parts[index - 1],), 0, False, fold, 2))
-        kernels.append((part, tuple(tasks), ready))
-        ended = [task.batch for task in tasks if task.stage + 1 == stages]
-        waiting += ended
-        moving = [(task.batch, task.stage + 1) for task in tasks if task.stage + 1 < stages]
+        tasks = []
+        if halved:
+            tasks.append(Task(tuple(halved), 1, False, 2, 2))
+        if crossed:
+            tasks.append(Task(tuple(crossed), 0, False, fold, 2))
+        waiting += halved
+        if index == count - 1:
+            kernels.append((part, others, "give", tuple(tasks), ready))
+            kernels.append((part, every[:1], "use", (), ()))
+        else:
+            kernels.append((part, every, "make", tuple(tasks), ready))
+        halved, crossed = crossed, [part] if index < count - 2 else []
+        if index == count - 3:
+            kernels.append((None, (), "", (Task((part,), 0, False, fold, 2),), ()))
+            halved, crossed = halved + crossed, []
     last = tuple(parts[-2:])
-    tasks = [Task(batch, 0, True, 2, 1) for batch in ended]
-    kernels.append((None, (Task(last, 0, True, fold, depth), *tasks), ()))
-    kernels.append((None, (), tuple(waiting) + (last,)))
+    kernels.append((None, (), "", (Task(last, 0, True, fold, depth),), ()))
+    kernels.append((None, (), "", (), tuple(waiting) + last))
     return kernels
 
 
-def ready_batches(waiting):
+def ready_parts(waiting):
     total = 0
-    for count, batch in enumerate(waiting, 1):
-        total += sum(width for _, _, width in batch)
+    for count, (slot, _, width) in enumerate(waiting, 1):
+        total += width
+        if slot != waiting[0][0]:
+            break
         if total % LANES == 0:
             return tuple(waiting[:count])
     return ()
@@ -404,21 +424,27 @@
     depth = min(OUTER, grid_count)
     fold = grid_count // depth
     held = {}
-    result = None
-    for part, tasks, adding in schedule(parts, fold, depth):
+    near, result = None, None
+    for part, ways, phase, tasks, adds in schedule(parts, fold, depth):
         place = parts.index(part) if part else len(parts)
         later = parts[place + AHEAD] if place + AHEAD < len(parts) else None
-        sources = []
-        for task in tasks:
-            whole = task.stage or task.count == 1
-            keys = [task.batch] if whole else [(done,) for done in task.batch]
-            sources.append([array for key in keys for array in held.pop(key)])
-        arrived = [held.pop(batch) for batch in adding]
+        sources = [[array for done in task.batch for array in held[(done,)]] for task in tasks]
+        batches, pieces = [], []
+        for done in adds:
+            batch = max((key for key in held if done in key), key=len)
+            if batch not in batches:
+                batches.append(batch)
+            column = sum(2 * width for _, _, width in batch[: batch.index(done)])
+            pieces.append((batches.index(batch), column, done[1], done[2]))
+        arrived = [held[batch] for batch in batches]
+        adding = (adds[0][0], adds[0][1], tuple(pieces)) if adds else ()
         plan = Plan(
             shape,
             fold,
             depth,
             part,
+            ways,
+            phase,
             tasks,
             tuple(len(arrays) for arrays in sources),
             adding,
@@ -426,22 +452,20 @@
             result is not None,
             later,
         )
-        terms, sends, result, piece = step(
-            plan, table, bands, theres[place] if part else None, sources, arrived, result
+        phased = near if phase == "use" else theres[place] if part else None
+        terms, near, sends, result, piece = step(
+            plan, table, bands, phased, sources, arrived, result
         )
         if later:
             theres.append(shifted(piece, "ka", -1))
-        if part:
-            held[(part,)] = [terms[0]] + [
-                shifted(terms[i], "ga", i, fold, True) for i in range(1, fold)
+        for way, array in zip(ways, terms):
+            array = shifted(array, "ga", way, fold, True) if way else array
+            held.setdefault((part,), []).insert(0 if way == 0 else fold, array)
+        for task, arrays in zip(tasks, sends):
+            steps = range(1, depth) if task.direct else [1 << task.stage]
+            held[task.batch] = [arrays[0]] + [
+                swapped(array, "ga", fold * i) for array, i in zip(arrays[1:], steps)
             ]
-        for task, arrays in zip(tasks, sends):
-            if task.direct:
-                held[task.batch] = [arrays[0]] + [
-                    shifted(arrays[i], "ga", i, fold) for i in range(1, task.count)
-                ]
-            else:
-                held[task.batch] = [arrays[0], swapped(arrays[1], "ga", fold << task.stage)]
     return result
 
 

time: 120 us -> 120 us (level)
  starting transfers between devices: 35.2 us -> 31.4 us
  Pallas kernels: 35.9 us -> 37.9 us
  waiting for transfers between devices: 47.6 us -> 49.4 us
    ppermute x13 -> x10, starting transfers between devices: 22.6 us -> 16.9 us  [shifted(): return lax.ppermute(block, axis, route)]
    ppermute x6 -> x8, waiting for transfers between devices: 9.65 us -> 13.7 us  [swapped(): return lax.ppermute(block, axis, [(i, i ^ distance) for i in range(count)])]
    ppermute x13 -> x10, waiting for transfers between devices: 38 us -> 35.7 us  [shifted(): return lax.ppermute(block, axis, route)]
    pallas_call x7 -> x9, Pallas kernels: 31.6 us -> 33.7 us  [step(): pl.pallas_call(functools.partial(step_kernel, plan), in_specs=in_specs, o...]
    ppermute x6 -> x8, starting transfers between devices: 12.6 us -> 14.5 us  [swapped(): return lax.ppermute(block, axis, [(i, i ^ distance) for i in range(count)])]
  transfers between devices with their start and end apart: 19 -> 18, of which waited for: 11 -> 11; matrix products, arithmetic and copies ran while one was open for 1% -> 1% of each run, Pallas kernels for 27% -> 29%
where the time goes in v11:
time: 120 us
  waiting for transfers between devices  49.4 us (41%)
  Pallas kernels  37.9 us (32%)
  starting transfers between devices  31.4 us (26%)
    ppermute x10, waiting for transfers between devices, shifted(): return lax.ppermute(block, axis, route)  35.7 us
    pallas_call x9, Pallas kernels, step(): pl.pallas_call(functools.partial(step_kernel, plan), in_specs=in_specs, o...  33.7 us
    ppermute x10, starting transfers between devices, shifted(): return lax.ppermute(block, axis, route)  16.9 us
    ppermute x8, starting transfers between devices, swapped(): return lax.ppermute(block, axis, [(i, i ^ distance) for i in range(count)])  14.5 us
    ppermute x8, waiting for transfers between devices, swapped(): return lax.ppermute(block, axis, [(i, i ^ distance) for i in range(count)])  13.7 us
    pallas_call x2, Pallas kernels, piece_of(): pl.pallas_call(functools.partial(piece_kernel, slot, start), in_specs=[pl...  4.24 us
  transfers between devices with their start and end apart: 18, of which 11 were waited for; matrix products, arithmetic and copies ran while one was open for 1% of the time, Pallas kernels for 29%

profile of v11, /device:TPU:0, one launch (start us, length us, event | category | flops | bytes accessed | tf_op | source)
XLA Modules:
  0.0 119.6 jit_solution(3236231789328667042)
XLA Ops:
  0.0 1.6 %piece_of.2.rest_0_ = bf16[2,256,2048]{2,1,0:T(8,128)(2,1)S(1)} custom-call(bf16[2,2,512,2048]{3,2,1,0:T(8,128)(2,1)} %refs_0_.11), custom_call_target="tpu_custom_call" | custom-call | flops 1000 | bytes 1000 | tf_op jit(solution)/shard_map/piece_of/pallas_call | solution.py:64
  1.7 0.0 copy-start
  1.7 0.0 copy-start.1
  1.7 2.5 %collective-permute-start.1 = (bf16[2,256,2048]{2,1,0:T(8,128)(2,1)S(1)}, bf16[2,256,2048]{2,1,0:T(8,128)(2,1)}, u32[]{:S(2)}, u32[]{:S(2)}) collective-permute-start(bf16[2,256,2048]{2,1,0:T(8,128)(2,1)S(1)} %piece_of.2.rest_0_), channel_id=1, source_target_pairs={{0,24},{8,0},{16,8},{24,16},{1,25},{9,1},{17,9},{25,17},{2,26},{10... | collective-permute-start | bytes 6291464 | tf_op jit(solution)/shard_map/ppermute | solution.py:33
  4.1 2.6 %piece_of.3 = bf16[2,256,2048]{2,1,0:T(8,128)(2,1)} custom-call(bf16[2,2,512,2048]{3,2,1,0:T(8,128)(2,1)} %refs_0_.11, bf16[2,256,2048]{2,1,0:T(8,128)(2,1)S(1)} %piece_of.2.rest_0_), custom_call_target="tpu_custom_call" | custom-call | flops 1000 | bytes 1000 | tf_op jit(solution)/shard_map/piece_of/pallas_call | solution.py:64
  6.7 0.7 collective-permute-start
  7.5 0.1 select_reduce_fusion.1
  7.6 0.1 copy.6
  7.7 0.1 fusion.4
  7.9 0.1 pad_maximum_fusion
  7.9 0.1 reshape.28
  8.0 0.1 pad_maximum_fusion.1.table_ref
  8.1 19.6 %collective-permute-done.1.refs_1_ = bf16[2,256,2048]{2,1,0:T(8,128)(2,1)} collective-permute-done((bf16[2,256,2048]{2,1,0:T(8,128)(2,1)S(1)}, bf16[2,256,2048]{2,1,0:T(8,128)(2,1)}, u32[]{:S(2)}, u32[]{:S(2)}) %collective-permute-start.1) | collective-permute-done | bytes 2097184 | tf_op jit(solution)/shard_map/ppermute | solution.py:33
  27.7 7.1 %step.9 = (f32[4,64,512]{2,1,0:T(8,128)S(1)}, bf16[4,64,512]{2,1,0:T(8,128)(2,1)S(1)}, bf16[2,192,2048]{2,1,0:T(8,128)(2,1)S(1)}) custom-call(f32[11]{0:T(128)S(1)} %pad_maximum_fusion.1.table_ref, bf16[2,2,512,2048]{3,2,1,0:T(8,128)(2,1)} %refs_0_.11, bf16[2,256,2048]{2,1,0:T(8,128)(2,1)} %collective-permute-done.1.refs_1_), custom_call_target="tpu_custom_call" | custom-call | flops 1000 | bytes 1000 | tf_op jit(solution)/shard_map/step/pallas_call | solution.py:326
  34.8 2.1 %collective-permute-start.4 = (bf16[2,192,2048]{2,1,0:T(8,128)(2,1)S(1)}, bf16[2,192,2048]{2,1,0:T(8,128)(2,1)S(1)}, u32[]{:S(2)}, u32[]{:S(2)}) collective-permute-start(bf16[2,192,2048]{2,1,0:T(8,128)(2,1)S(1)} %get-tuple-element.37), channel_id=1, source_target_pairs={{0,24},{8,0},{16,8},{24,16},{1,25},{9,1},{17,9},{25,17},{2,26},{10... | collective-permute-start | bytes 4718600 | tf_op jit(solution)/shard_map/ppermute | solution.py:33
  36.9 1.5 %collective-permute-start.2 = (bf16[4,64,512]{2,1,0:T(8,128)(2,1)S(1)}, bf16[4,64,512]{2,1,0:T(8,128)(2,1)S(1)}, u32[]{:S(2)}, u32[]{:S(2)}) collective-permute-start(bf16[4,64,512]{2,1,0:T(8,128)(2,1)S(1)} %get-tuple-element.35), channel_id=1, source_target_pairs={{0,1},{1,0},{2,3},{3,2},{4,5},{5,4},{6,7},{7,6},{8,9},{9,8},{10,11... | collective-permute-start | bytes 786440 | tf_op jit(solution)/shard_map/ppermute | solution.py:33
  38.4 11.9 %collective-permute-done.refs_1_ = bf16[2,256,2048]{2,1,0:T(8,128)(2,1)} collective-permute-done((bf16[2,256,2048]{2,1,0:T(8,128)(2,1)}, bf16[2,256,2048]{2,1,0:T(8,128)(2,1)}, u32[]{:S(2)}, u32[]{:S(2)}) %collective-permute-start) | collective-permute-done | bytes 2097184 | tf_op jit(solution)/shard_map/ppermute | solution.py:33
  50.3 7.1 %step.10 = (f32[4,64,512]{2,1,0:T(8,128)S(1)}, bf16[4,64,512]{2,1,0:T(8,128)(2,1)S(1)}, f32[2,64,512]{2,1,0:T(8,128)S(1)}, bf16[2,64,512]{2,1,0:T(8,128)(2,1)S(1)}, bf16[2,192,2048]{2,1,0:T(8,128)(2,1)S(1)}) custom-call(f32[11]{0:T(128)S(1)} %pad_maximum_fusion.1.table_ref, bf16[2,2,512,2048]{3,2,1,0:T(8,128)(2,1)} %refs_0_.11, ...), custom_call_target="tpu_custom_call" | custom-call | flops 1000 | bytes 1000 | tf_op jit(solution)/shard_map/step/pallas_call | solution.py:326
  57.4 2.0 %collective-permute-start.3 = (bf16[2,192,2048]{2,1,0:T(8,128)(2,1)S(1)}, bf16[2,192,2048]{2,1,0:T(8,128)(2,1)S(1)}, u32[]{:S(2)}, u32[]{:S(2)}) collective-permute-start(bf16[2,192,2048]{2,1,0:T(8,128)(2,1)S(1)} %get-tuple-element.36), channel_id=1, source_target_pairs={{0,24},{8,0},{16,8},{24,16},{1,25},{9,1},{17,9},{25,17},{2,26},{10... | collective-permute-start | bytes 4718600 | tf_op jit(solution)/shard_map/ppermute | solution.py:33
  59.3 1.5 %collective-permute-start.6 = (bf16[4,64,512]{2,1,0:T(8,128)(2,1)S(1)}, bf16[4,64,512]{2,1,0:T(8,128)(2,1)S(1)}, u32[]{:S(2)}, u32[]{:S(2)}) collective-permute-start(bf16[4,64,512]{2,1,0:T(8,128)(2,1)S(1)} %get-tuple-element.41), channel_id=1, source_target_pairs={{0,1},{1,0},{2,3},{3,2},{4,5},{5,4},{6,7},{7,6},{8,9},{9,8},{10,11... | collective-permute-start | bytes 786440 | tf_op jit(solution)/shard_map/ppermute | solution.py:33
  60.8 1.6 %collective-permute-start.5 = (bf16[2,64,512]{2,1,0:T(8,128)(2,1)S(1)}, bf16[2,64,512]{2,1,0:T(8,128)(2,1)S(1)}, u32[]{:S(2)}, u32[]{:S(2)}) collective-permute-start(bf16[2,64,512]{2,1,0:T(8,128)(2,1)S(1)} %get-tuple-element.39), channel_id=1, source_target_pairs={{0,2},{1,3},{2,0},{3,1},{4,6},{5,7},{6,4},{7,5},{8,10},{9,11},{10,... | collective-permute-start | bytes 393224 | tf_op jit(solution)/shard_map/ppermute | solution.py:38
  62.4 3.4 %collective-permute-done.5.refs_3_ = bf16[2,64,512]{2,1,0:T(8,128)(2,1)S(1)} collective-permute-done((bf16[2,64,512]{2,1,0:T(8,128)(2,1)S(1)}, bf16[2,64,512]{2,1,0:T(8,128)(2,1)S(1)}, u32[]{:S(2)}, u32[]{:S(2)}) %collective-permute-start.5) | collective-permute-done | bytes 131104 | tf_op jit(solution)/shard_map/ppermute | solution.py:38
  65.8 0.8 collective-permute-done.6.refs_5_
  66.6 0.5 collective-permute-done.4.refs_1_
  67.0 5.1 %step.11 = (f32[4,64,384]{2,1,0:T(8,128)S(1)}, bf16[4,64,384]{2,1,0:T(8,128)(2,1)S(1)}, f32[1,64,512]{2,1,0:T(8,128)S(1)}, bf16[1,64,512]{2,1,0:T(8,128)(2,1)S(1...) custom-call(f32[11]{0:T(128)S(1)} %pad_maximum_fusion.1.table_ref, ...), custom_call_target="tpu_custom_call" | custom-call | flops 1000 | bytes 1000 | tf_op jit(solution)/shard_map/step/pallas_call | solution.py:326
  72.2 2.1 %collective-permute-start.13 = (bf16[2,128,2048]{2,1,0:T(8,128)(2,1)S(1)}, bf16[2,128,2048]{2,1,0:T(8,128)(2,1)S(1)}, u32[]{:S(2)}, u32[]{:S(2)}) collective-permute-start(bf16[2,128,2048]{2,1,0:T(8,128)(2,1)S(1)} %get-tuple-element.54), channel_id=1, source_target_pairs={{0,24},{8,0},{16,8},{24,16},{1,25},{9,1},{17,9},{25,17},{2,26},{10... | collective-permute-start | bytes 3145736 | tf_op jit(solution)/shard_map/ppermute | solution.py:33
  74.3 1.5 %collective-permute-start.8 = (bf16[4,64,384]{2,1,0:T(8,128)(2,1)S(1)}, bf16[4,64,384]{2,1,0:T(8,128)(2,1)S(1)}, u32[]{:S(2)}, u32[]{:S(2)}) collective-permute-start(bf16[4,64,384]{2,1,0:T(8,128)(2,1)S(1)} %get-tuple-element.45), channel_id=1, source_target_pairs={{0,1},{1,0},{2,3},{3,2},{4,5},{5,4},{6,7},{7,6},{8,9},{9,8},{10,11... | collective-permute-start | bytes 589832 | tf_op jit(solution)/shard_map/ppermute | solution.py:33
  75.8 1.6 %collective-permute-start.7 = (bf16[2,64,512]{2,1,0:T(8,128)(2,1)S(1)}, bf16[2,64,512]{2,1,0:T(8,128)(2,1)S(1)}, u32[]{:S(2)}, u32[]{:S(2)}) collective-permute-start(bf16[2,64,512]{2,1,0:T(8,128)(2,1)S(1)} %get-tuple-element.43), channel_id=1, source_target_pairs={{0,2},{1,3},{2,0},{3,1},{4,6},{5,7},{6,4},{7,5},{8,10},{9,11},{10,... | collective-permute-start | bytes 393224 | tf_op jit(solution)/shard_map/ppermute | solution.py:38
  77.4 2.8 %collective-permute-done.8.refs_1_ = bf16[4,64,384]{2,1,0:T(8,128)(2,1)S(1)} collective-permute-done((bf16[4,64,384]{2,1,0:T(8,128)(2,1)S(1)}, bf16[4,64,384]{2,1,0:T(8,128)(2,1)S(1)}, u32[]{:S(2)}, u32[]{:S(2)}) %collective-permute-start.8) | collective-permute-done | bytes 196640 | tf_op jit(solution)/shard_map/ppermute | solution.py:33
  80.1 0.6 step.12
  80.7 1.6 %collective-permute-start.9 = (bf16[2,64,384]{2,1,0:T(8,128)(2,1)S(1)}, bf16[2,64,384]{2,1,0:T(8,128)(2,1)S(1)}, u32[]{:S(2)}, u32[]{:S(2)}) collective-permute-start(bf16[2,64,384]{2,1,0:T(8,128)(2,1)S(1)} %get-tuple-element.47), channel_id=1, source_target_pairs={{0,2},{1,3},{2,0},{3,1},{4,6},{5,7},{6,4},{7,5},{8,10},{9,11},{10,... | collective-permute-start | bytes 294920 | tf_op jit(solution)/shard_map/ppermute | solution.py:38
  82.4 2.6 %collective-permute-start.10 = (bf16[1,64,512]{2,1,0:T(8,128)(2,1)S(1)}, bf16[1,64,512]{2,1,0:T(8,128)(2,1)S(1)}, u32[]{:S(2)}, u32[]{:S(2)}) collective-permute-start(bf16[1,64,512]{2,1,0:T(8,128)(2,1)S(1)} %get-tuple-element.49), channel_id=1, source_target_pairs={{0,4},{1,5},{2,6},{3,7},{4,0},{5,1},{6,2},{7,3},{8,12},{9,13},{10,... | collective-permute-start | bytes 196616 | tf_op jit(solution)/shard_map/ppermute | solution.py:38
  85.0 2.6 %collective-permute-done.10.refs_7_ = bf16[1,64,512]{2,1,0:T(8,128)(2,1)S(1)} collective-permute-done((bf16[1,64,512]{2,1,0:T(8,128)(2,1)S(1)}, bf16[1,64,512]{2,1,0:T(8,128)(2,1)S(1)}, u32[]{:S(2)}, u32[]{:S(2)}) %collective-permute-start.10) | collective-permute-done | bytes 65568 | tf_op jit(solution)/shard_map/ppermute | solution.py:38
  87.5 5.1 %step.13 = (f32[4,64,384]{2,1,0:T(8,128)S(1)}, bf16[4,64,384]{2,1,0:T(8,128)(2,1)S(1)}, f32[1,64,896]{2,1,0:T(8,128)S(1)}, bf16[1,64,896]{2,1,0:T(8,128)(2,1)S(1)}, f32[64,2,2,512]{3,2,1,0:T(2,128)}) custom-call(f32[11]{0:T(128)S(1)} %pad_maximum_fusion.1.table_ref, bf16[2,2,512,2048]{3,2,1,0:T(8,128)(2,1)} %refs_0_.11, ...), custom_call_target="tpu_custom_call" | custom-call | flops 1000 | bytes 1000 | tf_op jit(solution)/shard_map/step/pallas_call | solution.py:326
  92.6 2.6 %collective-permute-start.11 = (bf16[1,64,896]{2,1,0:T(8,128)(2,1)S(1)}, bf16[1,64,896]{2,1,0:T(8,128)(2,1)S(1)}, u32[]{:S(2)}, u32[]{:S(2)}) collective-permute-start(bf16[1,64,896]{2,1,0:T(8,128)(2,1)S(1)} %get-tuple-element.51), channel_id=1, source_target_pairs={{0,4},{1,5},{2,6},{3,7},{4,0},{5,1},{6,2},{7,3},{8,12},{9,13},{10,... | collective-permute-start | bytes 344072 | tf_op jit(solution)/shard_map/ppermute | solution.py:38
  95.3 1.5 %collective-permute-start.12 = (bf16[4,64,384]{2,1,0:T(8,128)(2,1)S(1)}, bf16[4,64,384]{2,1,0:T(8,128)(2,1)S(1)}, u32[]{:S(2)}, u32[]{:S(2)}) collective-permute-start(bf16[4,64,384]{2,1,0:T(8,128)(2,1)S(1)} %get-tuple-element.53), channel_id=1, source_target_pairs={{0,1},{1,0},{2,3},{3,2},{4,5},{5,4},{6,7},{7,6},{8,9},{9,8},{10,11... | collective-permute-start | bytes 589832 | tf_op jit(solution)/shard_map/ppermute | solution.py:33
  96.8 2.9 %collective-permute-done.11.refs_3_.refs_1_ = bf16[1,64,896]{2,1,0:T(8,128)(2,1)S(1)} collective-permute-done((bf16[1,64,896]{2,1,0:T(8,128)(2,1)S(1)}, bf16[1,64,896]{2,1,0:T(8,128)(2,1)S(1)}, u32[]{:S(2)}, u32[]{:S(2)}) %collective-permute-start.11) | collective-permute-done | bytes 114720 | tf_op jit(solution)/shard_map/ppermute | solution.py:38
  99.6 3.3 %step.14 = (bf16[256,2048]{1,0:T(8,128)(2,1)S(1)}, bf16[4,64,256]{2,1,0:T(8,128)(2,1)S(1)}, f32[64,2,2,512]{3,2,1,0:T(2,128)}) custom-call(f32[11]{0:T(128)S(1)} %pad_maximum_fusion.1.table_ref, bf16[2,2,512,2048]{3,2,1,0:T(8,128)(2,1)} %refs_0_.11, bf16[2,128,2048]{2,1,0:T(8,128)(2,1)S(1)} %collective-permute-done.13.refs_1_, ...), custom_call_target="tpu_custom_call", output_to_operand_aliasing={{2}: (5, {})} | custom-call | flops 1000 | bytes 1000 | tf_op jit(solution)/shard_map/step/pallas_call | solution.py:326
  103.0 1.6 %collective-permute-start.14 = (bf16[4,64,256]{2,1,0:T(8,128)(2,1)S(1)}, bf16[4,64,256]{2,1,0:T(8,128)(2,1)S(1)}, u32[]{:S(2)}, u32[]{:S(2)}) collective-permute-start(bf16[4,64,256]{2,1,0:T(8,128)(2,1)S(1)} %get-tuple-element.57), channel_id=1, source_target_pairs={{0,1},{1,0},{2,3},{3,2},{4,5},{5,4},{6,7},{7,6},{8,9},{9,8},{10,11... | collective-permute-start | bytes 393224 | tf_op jit(solution)/shard_map/ppermute | solution.py:33
  104.5 3.3 %step.15.refs_2_ = f32[4,64,256]{2,1,0:T(8,128)S(1)} custom-call(f32[11]{0:T(128)S(1)} %pad_maximum_fusion.1.table_ref, bf16[2,2,512,2048]{3,2,1,0:T(8,128)(2,1)} %refs_0_.11, bf16[256,2048]{1,0:T(8,128)(2,1)S(1)} %get-tuple-element.56.refs_1_), custom_call_target="tpu_custom_call" | custom-call | flops 1000 | bytes 1000 | tf_op jit(solution)/shard_map/step/pallas_call | solution.py:326
  107.8 0.2 collective-permute-done.14.refs_3_
  108.0 0.6 step.16
  108.6 0.2 collective-permute-start.15
  108.8 2.9 %collective-permute-start.16 = (bf16[1,64,640]{2,1,0:T(8,128)(2,1)S(1)}, bf16[1,64,640]{2,1,0:T(8,128)(2,1)S(1)}, u32[]{:S(2)}, u32[]{:S(2)}) collective-permute-start(bf16[1,64,640]{2,1,0:T(8,128)(2,1)S(1)} %get-tuple-element.60), channel_id=1, source_target_pairs={{0,4},{1,5},{2,6},{3,7},{4,0},{5,1},{6,2},{7,3},{8,12},{9,13},{10,... | collective-permute-start | bytes 245768 | tf_op jit(solution)/shard_map/ppermute | solution.py:38
  111.7 1.4 %collective-permute-start.17 = (bf16[1,64,640]{2,1,0:T(8,128)(2,1)S(1)}, bf16[1,64,640]{2,1,0:T(8,128)(2,1)S(1)}, u32[]{:S(2)}, u32[]{:S(2)}) collective-permute-start(bf16[1,64,640]{2,1,0:T(8,128)(2,1)S(1)} %get-tuple-element.61), channel_id=1, source_target_pairs={{0,6},{1,7},{2,4},{3,5},{4,2},{5,3},{6,0},{7,1},{8,14},{9,15},{10,... | collective-permute-start | bytes 245768 | tf_op jit(solution)/shard_map/ppermute | solution.py:38
  113.1 1.8 %collective-permute-done.15.refs_3_ = bf16[1,64,640]{2,1,0:T(8,128)(2,1)S(1)} collective-permute-done((bf16[1,64,640]{2,1,0:T(8,128)(2,1)S(1)}, bf16[1,64,640]{2,1,0:T(8,128)(2,1)S(1)}, u32[]{:S(2)}, u32[]{:S(2)}) %collective-permute-start.15) | collective-permute-done | bytes 81952 | tf_op jit(solution)/shard_map/ppermute | solution.py:38
  114.9 3.1 %collective-permute-done.17.refs_5_ = bf16[1,64,640]{2,1,0:T(8,128)(2,1)S(1)} collective-permute-done((bf16[1,64,640]{2,1,0:T(8,128)(2,1)S(1)}, bf16[1,64,640]{2,1,0:T(8,128)(2,1)S(1)}, u32[]{:S(2)}, u32[]{:S(2)}) %collective-permute-start.17) | collective-permute-done | bytes 81952 | tf_op jit(solution)/shard_map/ppermute | solution.py:38
  118.0 1.5 %step.17 = f32[64,2,2,512]{3,2,1,0:T(2,128)} custom-call(f32[11]{0:T(128)S(1)} %pad_maximum_fusion.1.table_ref, f32[1,64,896]{2,1,0:T(8,128)S(1)} %get-tuple-element.50.refs_2_.refs_0_, bf16[1,64,896]{2,1,0:T(8,128)(2,1)S(1)} %collective-permute-done.11.refs_3_.refs_1_, f32[1,64,640]{2,1,0:T(8,128)S(1)} %get-tuple-element.58.refs_2_, ...), custom_call_target="tpu_custom_call", output_to_operand_aliasing={{}: (7, {})} | custom-call | flops 1000 | bytes 1000 | tf_op jit(solution)/shard_map/step/pallas_call | solution.py:326
  (11 shorter events, 0.0 us)
Async XLA Ops:
  1.7 5.8 %copy-start = (s32[2]{0:T(128)S(1)}, s32[2]{0:T(128)}, u32[]{:S(2)}) copy-start(s32[2]{0:T(128)} %param.4) | copy-start | bytes 28
  1.7 5.8 %copy-start.1 = (s32[2]{0:T(128)S(1)}, s32[2]{0:T(128)}, u32[]{:S(2)}) copy-start(s32[2]{0:T(128)} %param.5) | copy-start | bytes 28
  1.7 26.0 %collective-permute-start.1 = (bf16[2,256,2048]{2,1,0:T(8,128)(2,1)S(1)}, bf16[2,256,2048]{2,1,0:T(8,128)(2,1)}, u32[]{:S(2)}, u32[]{:S(2)}) collective-permute-start(bf16[2,256,2048]{2,1,0:T(8,128)(2,1)S(1)} %piece_of.2.rest_0_), channel_id=1, source_target_pairs={{0,24},{8,0},{16,8},{24,16},{1,25},{9,1},{17,9},{25,17},{2,26},{10... | collective-permute-start | bytes 6291464 | tf_op jit(solution)/shard_map/ppermute | solution.py:33
  6.7 43.5 %collective-permute-start = (bf16[2,256,2048]{2,1,0:T(8,128)(2,1)}, bf16[2,256,2048]{2,1,0:T(8,128)(2,1)}, u32[]{:S(2)}, u32[]{:S(2)}) collective-permute-start(bf16[2,256,2048]{2,1,0:T(8,128)(2,1)} %piece_of.3), channel_id=1, source_target_pairs={{0,24},{8,0},{16,8},{24,16},{1,25},{9,1},{17,9},{25,17},{2,26},{10... | collective-permute-start | bytes 6291464 | tf_op jit(solution)/shard_map/ppermute | solution.py:33
  34.8 32.2 %collective-permute-start.4 = (bf16[2,192,2048]{2,1,0:T(8,128)(2,1)S(1)}, bf16[2,192,2048]{2,1,0:T(8,128)(2,1)S(1)}, u32[]{:S(2)}, u32[]{:S(2)}) collective-permute-start(bf16[2,192,2048]{2,1,0:T(8,128)(2,1)S(1)} %get-tuple-element.37), channel_id=1, source_target_pairs={{0,24},{8,0},{16,8},{24,16},{1,25},{9,1},{17,9},{25,17},{2,26},{10... | collective-permute-start | bytes 4718600 | tf_op jit(solution)/shard_map/ppermute | solution.py:33
  36.9 13.4 %collective-permute-start.2 = (bf16[4,64,512]{2,1,0:T(8,128)(2,1)S(1)}, bf16[4,64,512]{2,1,0:T(8,128)(2,1)S(1)}, u32[]{:S(2)}, u32[]{:S(2)}) collective-permute-start(bf16[4,64,512]{2,1,0:T(8,128)(2,1)S(1)} %get-tuple-element.35), channel_id=1, source_target_pairs={{0,1},{1,0},{2,3},{3,2},{4,5},{5,4},{6,7},{7,6},{8,9},{9,8},{10,11... | collective-permute-start | bytes 786440 | tf_op jit(solution)/shard_map/ppermute | solution.py:33
  57.4 30.2 %collective-permute-start.3 = (bf16[2,192,2048]{2,1,0:T(8,128)(2,1)S(1)}, bf16[2,192,2048]{2,1,0:T(8,128)(2,1)S(1)}, u32[]{:S(2)}, u32[]{:S(2)}) collective-permute-start(bf16[2,192,2048]{2,1,0:T(8,128)(2,1)S(1)} %get-tuple-element.36), channel_id=1, source_target_pairs={{0,24},{8,0},{16,8},{24,16},{1,25},{9,1},{17,9},{25,17},{2,26},{10... | collective-permute-start | bytes 4718600 | tf_op jit(solution)/shard_map/ppermute | solution.py:33
  59.3 7.2 %collective-permute-start.6 = (bf16[4,64,512]{2,1,0:T(8,128)(2,1)S(1)}, bf16[4,64,512]{2,1,0:T(8,128)(2,1)S(1)}, u32[]{:S(2)}, u32[]{:S(2)}) collective-permute-start(bf16[4,64,512]{2,1,0:T(8,128)(2,1)S(1)} %get-tuple-element.41), channel_id=1, source_target_pairs={{0,1},{1,0},{2,3},{3,2},{4,5},{5,4},{6,7},{7,6},{8,9},{9,8},{10,11... | collective-permute-start | bytes 786440 | tf_op jit(solution)/shard_map/ppermute | solution.py:33
  60.8 5.0 %collective-permute-start.5 = (bf16[2,64,512]{2,1,0:T(8,128)(2,1)S(1)}, bf16[2,64,512]{2,1,0:T(8,128)(2,1)S(1)}, u32[]{:S(2)}, u32[]{:S(2)}) collective-permute-start(bf16[2,64,512]{2,1,0:T(8,128)(2,1)S(1)} %get-tuple-element.39), channel_id=1, source_target_pairs={{0,2},{1,3},{2,0},{3,1},{4,6},{5,7},{6,4},{7,5},{8,10},{9,11},{10,... | collective-permute-start | bytes 393224 | tf_op jit(solution)/shard_map/ppermute | solution.py:38
  72.2 27.5 %collective-permute-start.13 = (bf16[2,128,2048]{2,1,0:T(8,128)(2,1)S(1)}, bf16[2,128,2048]{2,1,0:T(8,128)(2,1)S(1)}, u32[]{:S(2)}, u32[]{:S(2)}) collective-permute-start(bf16[2,128,2048]{2,1,0:T(8,128)(2,1)S(1)} %get-tuple-element.54), channel_id=1, source_target_pairs={{0,24},{8,0},{16,8},{24,16},{1,25},{9,1},{17,9},{25,17},{2,26},{10... | collective-permute-start | bytes 3145736 | tf_op jit(solution)/shard_map/ppermute | solution.py:33
  74.3 5.8 %collective-permute-start.8 = (bf16[4,64,384]{2,1,0:T(8,128)(2,1)S(1)}, bf16[4,64,384]{2,1,0:T(8,128)(2,1)S(1)}, u32[]{:S(2)}, u32[]{:S(2)}) collective-permute-start(bf16[4,64,384]{2,1,0:T(8,128)(2,1)S(1)} %get-tuple-element.45), channel_id=1, source_target_pairs={{0,1},{1,0},{2,3},{3,2},{4,5},{5,4},{6,7},{7,6},{8,9},{9,8},{10,11... | collective-permute-start | bytes 589832 | tf_op jit(solution)/shard_map/ppermute | solution.py:33
  75.8 11.7 %collective-permute-start.7 = (bf16[2,64,512]{2,1,0:T(8,128)(2,1)S(1)}, bf16[2,64,512]{2,1,0:T(8,128)(2,1)S(1)}, u32[]{:S(2)}, u32[]{:S(2)}) collective-permute-start(bf16[2,64,512]{2,1,0:T(8,128)(2,1)S(1)} %get-tuple-element.43), channel_id=1, source_target_pairs={{0,2},{1,3},{2,0},{3,1},{4,6},{5,7},{6,4},{7,5},{8,10},{9,11},{10,... | collective-permute-start | bytes 393224 | tf_op jit(solution)/shard_map/ppermute | solution.py:38
  80.7 6.8 %collective-permute-start.9 = (bf16[2,64,384]{2,1,0:T(8,128)(2,1)S(1)}, bf16[2,64,384]{2,1,0:T(8,128)(2,1)S(1)}, u32[]{:S(2)}, u32[]{:S(2)}) collective-permute-start(bf16[2,64,384]{2,1,0:T(8,128)(2,1)S(1)} %get-tuple-element.47), channel_id=1, source_target_pairs={{0,2},{1,3},{2,0},{3,1},{4,6},{5,7},{6,4},{7,5},{8,10},{9,11},{10,... | collective-permute-start | bytes 294920 | tf_op jit(solution)/shard_map/ppermute | solution.py:38
  82.4 5.2 %collective-permute-start.10 = (bf16[1,64,512]{2,1,0:T(8,128)(2,1)S(1)}, bf16[1,64,512]{2,1,0:T(8,128)(2,1)S(1)}, u32[]{:S(2)}, u32[]{:S(2)}) collective-permute-start(bf16[1,64,512]{2,1,0:T(8,128)(2,1)S(1)} %get-tuple-element.49), channel_id=1, source_target_pairs={{0,4},{1,5},{2,6},{3,7},{4,0},{5,1},{6,2},{7,3},{8,12},{9,13},{10,... | collective-permute-start | bytes 196616 | tf_op jit(solution)/shard_map/ppermute | solution.py:38
  92.6 7.0 %collective-permute-start.11 = (bf16[1,64,896]{2,1,0:T(8,128)(2,1)S(1)}, bf16[1,64,896]{2,1,0:T(8,128)(2,1)S(1)}, u32[]{:S(2)}, u32[]{:S(2)}) collective-permute-start(bf16[1,64,896]{2,1,0:T(8,128)(2,1)S(1)} %get-tuple-element.51), channel_id=1, source_target_pairs={{0,4},{1,5},{2,6},{3,7},{4,0},{5,1},{6,2},{7,3},{8,12},{9,13},{10,... | collective-permute-start | bytes 344072 | tf_op jit(solution)/shard_map/ppermute | solution.py:38
  95.3 12.5 %collective-permute-start.12 = (bf16[4,64,384]{2,1,0:T(8,128)(2,1)S(1)}, bf16[4,64,384]{2,1,0:T(8,128)(2,1)S(1)}, u32[]{:S(2)}, u32[]{:S(2)}) collective-permute-start(bf16[4,64,384]{2,1,0:T(8,128)(2,1)S(1)} %get-tuple-element.53), channel_id=1, source_target_pairs={{0,1},{1,0},{2,3},{3,2},{4,5},{5,4},{6,7},{7,6},{8,9},{9,8},{10,11... | collective-permute-start | bytes 589832 | tf_op jit(solution)/shard_map/ppermute | solution.py:33
  103.0 5.0 %collective-permute-start.14 = (bf16[4,64,256]{2,1,0:T(8,128)(2,1)S(1)}, bf16[4,64,256]{2,1,0:T(8,128)(2,1)S(1)}, u32[]{:S(2)}, u32[]{:S(2)}) collective-permute-start(bf16[4,64,256]{2,1,0:T(8,128)(2,1)S(1)} %get-tuple-element.57), channel_id=1, source_target_pairs={{0,1},{1,0},{2,3},{3,2},{4,5},{5,4},{6,7},{7,6},{8,9},{9,8},{10,11... | collective-permute-start | bytes 393224 | tf_op jit(solution)/shard_map/ppermute | solution.py:33
  108.6 6.3 %collective-permute-start.15 = (bf16[1,64,640]{2,1,0:T(8,128)(2,1)S(1)}, bf16[1,64,640]{2,1,0:T(8,128)(2,1)S(1)}, u32[]{:S(2)}, u32[]{:S(2)}) collective-permute-start(bf16[1,64,640]{2,1,0:T(8,128)(2,1)S(1)} %get-tuple-element.59), channel_id=1, source_target_pairs={{0,2},{1,3},{2,0},{3,1},{4,6},{5,7},{6,4},{7,5},{8,10},{9,11},{10,... | collective-permute-start | bytes 245768 | tf_op jit(solution)/shard_map/ppermute | solution.py:38
  108.8 6.1 %collective-permute-start.16 = (bf16[1,64,640]{2,1,0:T(8,128)(2,1)S(1)}, bf16[1,64,640]{2,1,0:T(8,128)(2,1)S(1)}, u32[]{:S(2)}, u32[]{:S(2)}) collective-permute-start(bf16[1,64,640]{2,1,0:T(8,128)(2,1)S(1)} %get-tuple-element.60), channel_id=1, source_target_pairs={{0,4},{1,5},{2,6},{3,7},{4,0},{5,1},{6,2},{7,3},{8,12},{9,13},{10,... | collective-permute-start | bytes 245768 | tf_op jit(solution)/shard_map/ppermute | solution.py:38
  111.7 6.2 %collective-permute-start.17 = (bf16[1,64,640]{2,1,0:T(8,128)(2,1)S(1)}, bf16[1,64,640]{2,1,0:T(8,128)(2,1)S(1)}, u32[]{:S(2)}, u32[]{:S(2)}) collective-permute-start(bf16[1,64,640]{2,1,0:T(8,128)(2,1)S(1)} %get-tuple-element.61), channel_id=1, source_target_pairs={{0,6},{1,7},{2,4},{3,5},{4,2},{5,3},{6,0},{7,1},{8,14},{9,15},{10,... | collective-permute-start | bytes 245768 | tf_op jit(solution)/shard_map/ppermute | solution.py:38

commit v12 on v11

--- a/solution.py
+++ b/solution.py
@@ -122,26 +122,29 @@
     arrived = [take(count) for count in plan.adds]
     if plan.adding and plan.placed:
         take(1)
-    given_ref = take(1)[0] if plan.near == "give" else None
+    given_ref, kept_ref = take(2) if plan.near == "give" else (None, None)
     outs = take(len(plan.ways))
     targets = [take(task.count) for task in plan.tasks]
     result_ref = take(1)[0] if plan.adding else None
     piece_ref = take(1)[0] if plan.later else None
     if plan.part:
-        own_buf, own_sems = take(2)
+        if plan.near != "use":
+            own_buf, own_sems = take(2)
         slot, _, width = plan.part
         base = slot * stride
         point = table_ref[base].astype(jnp.int32)
         own = []
-        for way, distance in enumerate(plan.ways):
+        loads_of = plan.ways + (0,) if plan.near == "give" else plan.ways
+        for way, distance in enumerate(loads_of if plan.near != "use" else ()):
             target = lax.rem(place + distance, fold)
+            rows_ref = own_buf.at[way] if way < len(plan.ways) else kept_ref
             own.append([])
             for part in range(2):
                 for level in range(depth):
                     first = pl.multiple_of((level * fold + target) * rows, rows)
                     copy = pltpu.make_async_copy(
                         bands_ref.at[point, part, pl.ds(first, rows), :],
-                        own_buf.at[way, part, pl.ds(level * rows, rows), :],
+                        rows_ref.at[part, pl.ds(level * rows, rows), :],
                         own_sems.at[way, part, level],
                     )
                     copy.start()
@@ -196,16 +199,17 @@
             near_ref = given_ref if plan.near == "give" else take(1)[0]
             near_into(near_ref, phased_ref, table_ref, base, planes)
         dims = (((1,), (1,)), ((), ()))
-        points = own_buf.shape[3]
+        points = near_ref.shape[1]
         run = points // 2 if width <= SPLIT else points
         for way, out_ref in enumerate(outs):
             of_both = []
             for part in range(2):
-                for copy in own[way][part * depth : (part + 1) * depth]:
+                for copy in own[way][part * depth : (part + 1) * depth] if own else ():
                     copy.wait()
+                rows_ref = bands_ref if plan.near == "use" else own_buf.at[way]
                 products = [
                     lax.dot_general(
-                        own_buf[way, part, :, pl.ds(first, run)],
+                        rows_ref[part, :, pl.ds(first, run)],
                         near_ref[:, pl.ds(first, run)],
                         dims,
                         preferred_element_type=jnp.float32,
@@ -220,6 +224,9 @@
                 lines = slice(level * rows, (level + 1) * rows)
                 out_ref[level, :, :width] = real_part[lines]
                 out_ref[level, :, width:] = imag_part[lines]
+            if plan.near == "give" and way + 1 == len(outs):
+                for copy in own[-1]:
+                    copy.wait()
             if plan.later and way == 0:
                 for load, store in zip(loads, stores):
                     load.wait()
@@ -271,7 +278,7 @@
 def step(plan, table, bands, phased, sources, arrived, result):
     rows, _, _, nbands = plan.shape
     fold, depth = plan.fold, plan.depth
-    points = bands.shape[3]
+    points = bands.shape[-1]
     vmem = pl.BlockSpec(memory_space=pltpu.VMEM)
     hbm = pl.BlockSpec(memory_space=pltpu.HBM)
     operands, in_specs = [table], [pl.BlockSpec(memory_space=pltpu.SMEM)]
@@ -283,16 +290,18 @@
     if plan.part:
         width = plan.part[2]
         operands += [bands, phased]
-        in_specs += [hbm, vmem]
+        in_specs += [vmem if plan.near == "use" else hbm, vmem]
         if plan.near == "give":
             out_shape.append(jax.ShapeDtypeStruct((2 * width, points), jnp.bfloat16))
+            out_shape.append(jax.ShapeDtypeStruct((2, depth * rows, points), jnp.bfloat16))
         out_shape += [
             jax.ShapeDtypeStruct((depth, rows, 2 * width), kind(way)) for way in plan.ways
         ]
-        scratch += [
-            pltpu.VMEM((len(plan.ways), 2, depth * rows, points), jnp.bfloat16),
-            pltpu.SemaphoreType.DMA((len(plan.ways), 2, depth)),
-        ]
+        if plan.near != "use":
+            scratch += [
+                pltpu.VMEM((len(plan.ways), 2, depth * rows, points), jnp.bfloat16),
+                pltpu.SemaphoreType.DMA((fold, 2, depth)),
+            ]
     for arrays in sources + arrived:
         operands += arrays
         in_specs += [vmem] * len(arrays)
@@ -337,7 +346,7 @@
     )
     piece = outs.pop() if plan.later else None
     result = outs.pop() if plan.adding else result
-    near = outs.pop(0) if plan.near == "give" else None
+    near = [outs.pop(0), outs.pop(0)] if plan.near == "give" else None
     terms = outs[: len(plan.ways)]
     handed = outs[len(plan.ways) :]
     sends = []
@@ -374,7 +383,7 @@
         else:
             kernels.append((part, every, "make", tuple(tasks), ready))
         halved, crossed = crossed, [part] if index < count - 2 else []
-        if index == count - 3:
+        if index in (0, count - 3):
             kernels.append((None, (), "", (Task((part,), 0, False, fold, 2),), ()))
             halved, crossed = halved + crossed, []
     last = tuple(parts[-2:])
@@ -452,9 +461,11 @@
             result is not None,
             later,
         )
-        phased = near if phase == "use" else theres[place] if part else None
+        phased, own = theres[place] if part else None, bands
+        if phase == "use":
+            phased, own = near
         terms, near, sends, result, piece = step(
-            plan, table, bands, phased, sources, arrived, result
+            plan, table, own, phased, sources, arrived, result
         )
         if later:
             theres.append(shifted(piece, "ka", -1))

time: 120 us -> 120 us (level)
  waiting for transfers between devices: 49.4 us -> 51.1 us
  Pallas kernels: 37.9 us -> 36.6 us
    ppermute x8, waiting for transfers between devices: 13.7 us -> 15.8 us  [swapped(): return lax.ppermute(block, axis, [(i, i ^ distance) for i in range(count)])]
    pallas_call x9 -> x10, Pallas kernels: 33.7 us -> 32.4 us  [step(): pl.pallas_call(functools.partial(step_kernel, plan), in_specs=in_specs, o...]
  transfers between devices with their start and end apart: 18 -> 18, of which waited for: 11 -> 13; matrix products, arithmetic and copies ran while one was open for 1% -> 1% of each run, Pallas kernels for 29% -> 27%
where the time goes in v12:
time: 120 us
  waiting for transfers between devices  51.1 us (43%)
  Pallas kernels  36.6 us (30%)
  starting transfers between devices  31.4 us (26%)
    ppermute x10, waiting for transfers between devices, shifted(): return lax.ppermute(block, axis, route)  35.2 us
    pallas_call x10, Pallas kernels, step(): pl.pallas_call(functools.partial(step_kernel, plan), in_specs=in_specs, o...  32.4 us
    ppermute x10, starting transfers between devices, shifted(): return lax.ppermute(block, axis, route)  16.8 us
    ppermute x8, waiting for transfers between devices, swapped(): return lax.ppermute(block, axis, [(i, i ^ distance) for i in range(count)])  15.8 us
    ppermute x8, starting transfers between devices, swapped(): return lax.ppermute(block, axis, [(i, i ^ distance) for i in range(count)])  14.6 us
    pallas_call x2, Pallas kernels, piece_of(): pl.pallas_call(functools.partial(piece_kernel, slot, start), in_specs=[pl...  4.24 us
  transfers between devices with their start and end apart: 18, of which 13 were waited for; matrix products, arithmetic and copies ran while one was open for 1% of the time, Pallas kernels for 27%

profile of v12, /device:TPU:0, one launch (start us, length us, event | category | flops | bytes accessed | tf_op | source)
XLA Modules:
  0.0 120.0 jit_solution(1671554699723316555)
XLA Ops:
  0.0 1.6 %piece_of.2.rest_0_ = bf16[2,256,2048]{2,1,0:T(8,128)(2,1)S(1)} custom-call(bf16[2,2,512,2048]{3,2,1,0:T(8,128)(2,1)} %refs_0_.9), custom_call_target="tpu_custom_call" | custom-call | flops 1000 | bytes 1000 | tf_op jit(solution)/shard_map/piece_of/pallas_call | solution.py:64
  1.7 2.5 %collective-permute-start.1 = (bf16[2,256,2048]{2,1,0:T(8,128)(2,1)S(1)}, bf16[2,256,2048]{2,1,0:T(8,128)(2,1)}, u32[]{:S(2)}, u32[]{:S(2)}) collective-permute-start(bf16[2,256,2048]{2,1,0:T(8,128)(2,1)S(1)} %piece_of.2.rest_0_), channel_id=1, source_target_pairs={{0,24},{8,0},{16,8},{24,16},{1,25},{9,1},{17,9},{25,17},{2,26},{10... | collective-permute-start | bytes 6291464 | tf_op jit(solution)/shard_map/ppermute | solution.py:33
  4.1 2.6 %piece_of.3 = bf16[2,256,2048]{2,1,0:T(8,128)(2,1)} custom-call(bf16[2,2,512,2048]{3,2,1,0:T(8,128)(2,1)} %refs_0_.9, bf16[2,256,2048]{2,1,0:T(8,128)(2,1)S(1)} %piece_of.2.rest_0_), custom_call_target="tpu_custom_call" | custom-call | flops 1000 | bytes 1000 | tf_op jit(solution)/shard_map/piece_of/pallas_call | solution.py:64
  6.7 0.7 collective-permute-start
  7.5 0.1 select_reduce_fusion.1
  7.6 0.1 copy.6
  7.7 0.1 fusion.4
  7.8 0.1 pad_maximum_fusion
  7.9 0.1 reshape.28
  8.0 0.1 pad_maximum_fusion.1.table_ref
  8.1 19.6 %collective-permute-done.1.refs_1_ = bf16[2,256,2048]{2,1,0:T(8,128)(2,1)} collective-permute-done((bf16[2,256,2048]{2,1,0:T(8,128)(2,1)S(1)}, bf16[2,256,2048]{2,1,0:T(8,128)(2,1)}, u32[]{:S(2)}, u32[]{:S(2)}) %collective-permute-start.1) | collective-permute-done | bytes 2097184 | tf_op jit(solution)/shard_map/ppermute | solution.py:33
  27.7 7.1 %step.10 = (f32[4,64,512]{2,1,0:T(8,128)S(1)}, bf16[4,64,512]{2,1,0:T(8,128)(2,1)S(1)}, bf16[2,192,2048]{2,1,0:T(8,128)(2,1)S(1)}) custom-call(f32[11]{0:T(128)S(1)} %pad_maximum_fusion.1.table_ref, bf16[2,2,512,2048]{3,2,1,0:T(8,128)(2,1)} %refs_0_.9, bf16[2,256,2048]{2,1,0:T(8,128)(2,1)} %collective-permute-done.1.refs_1_), custom_call_target="tpu_custom_call" | custom-call | flops 1000 | bytes 1000 | tf_op jit(solution)/shard_map/step/pallas_call | solution.py:335
  34.8 2.1 %collective-permute-start.5 = (bf16[2,192,2048]{2,1,0:T(8,128)(2,1)S(1)}, bf16[2,192,2048]{2,1,0:T(8,128)(2,1)S(1)}, u32[]{:S(2)}, u32[]{:S(2)}) collective-permute-start(bf16[2,192,2048]{2,1,0:T(8,128)(2,1)S(1)} %get-tuple-element.40), channel_id=1, source_target_pairs={{0,24},{8,0},{16,8},{24,16},{1,25},{9,1},{17,9},{25,17},{2,26},{10... | collective-permute-start | bytes 4718600 | tf_op jit(solution)/shard_map/ppermute | solution.py:33
  36.9 1.5 %collective-permute-start.2 = (bf16[4,64,512]{2,1,0:T(8,128)(2,1)S(1)}, bf16[4,64,512]{2,1,0:T(8,128)(2,1)S(1)}, u32[]{:S(2)}, u32[]{:S(2)}) collective-permute-start(bf16[4,64,512]{2,1,0:T(8,128)(2,1)S(1)} %get-tuple-element.36), channel_id=1, source_target_pairs={{0,1},{1,0},{2,3},{3,2},{4,5},{5,4},{6,7},{7,6},{8,9},{9,8},{10,11... | collective-permute-start | bytes 786440 | tf_op jit(solution)/shard_map/ppermute | solution.py:33
  38.4 5.7 %collective-permute-done.2.refs_1_ = bf16[4,64,512]{2,1,0:T(8,128)(2,1)S(1)} collective-permute-done((bf16[4,64,512]{2,1,0:T(8,128)(2,1)S(1)}, bf16[4,64,512]{2,1,0:T(8,128)(2,1)S(1)}, u32[]{:S(2)}, u32[]{:S(2)}) %collective-permute-start.2) | collective-permute-done | bytes 262176 | tf_op jit(solution)/shard_map/ppermute | solution.py:33
  44.1 0.6 step.11
  44.7 1.6 %collective-permute-start.3 = (bf16[2,64,512]{2,1,0:T(8,128)(2,1)S(1)}, bf16[2,64,512]{2,1,0:T(8,128)(2,1)S(1)}, u32[]{:S(2)}, u32[]{:S(2)}) collective-permute-start(bf16[2,64,512]{2,1,0:T(8,128)(2,1)S(1)} %get-tuple-element.38), channel_id=1, source_target_pairs={{0,2},{1,3},{2,0},{3,1},{4,6},{5,7},{6,4},{7,5},{8,10},{9,11},{10,... | collective-permute-start | bytes 393224 | tf_op jit(solution)/shard_map/ppermute | solution.py:38
  46.3 3.9 %collective-permute-done.refs_1_ = bf16[2,256,2048]{2,1,0:T(8,128)(2,1)} collective-permute-done((bf16[2,256,2048]{2,1,0:T(8,128)(2,1)}, bf16[2,256,2048]{2,1,0:T(8,128)(2,1)}, u32[]{:S(2)}, u32[]{:S(2)}) %collective-permute-start) | collective-permute-done | bytes 2097184 | tf_op jit(solution)/shard_map/ppermute | solution.py:33
  50.3 7.1 %step.12 = (f32[4,64,512]{2,1,0:T(8,128)S(1)}, bf16[4,64,512]{2,1,0:T(8,128)(2,1)S(1)}, f32[1,64,512]{2,1,0:T(8,128)S(1)}, bf16[1,64,512]{2,1,0:T(8,128)(2,1)S(1)}, bf16[2,192,2048]{2,1,0:T(8,128)(2,1)S(1)}) custom-call(f32[11]{0:T(128)S(1)} %pad_maximum_fusion.1.table_ref, bf16[2,2,512,2048]{3,2,1,0:T(8,128)(2,1)} %refs_0_.9, ...), custom_call_target="tpu_custom_call" | custom-call | flops 1000 | bytes 1000 | tf_op jit(solution)/shard_map/step/pallas_call | solution.py:335
  57.4 2.0 %collective-permute-start.4 = (bf16[2,192,2048]{2,1,0:T(8,128)(2,1)S(1)}, bf16[2,192,2048]{2,1,0:T(8,128)(2,1)S(1)}, u32[]{:S(2)}, u32[]{:S(2)}) collective-permute-start(bf16[2,192,2048]{2,1,0:T(8,128)(2,1)S(1)} %get-tuple-element.39), channel_id=1, source_target_pairs={{0,24},{8,0},{16,8},{24,16},{1,25},{9,1},{17,9},{25,17},{2,26},{10... | collective-permute-start | bytes 4718600 | tf_op jit(solution)/shard_map/ppermute | solution.py:33
  59.3 1.5 %collective-permute-start.6 = (bf16[4,64,512]{2,1,0:T(8,128)(2,1)S(1)}, bf16[4,64,512]{2,1,0:T(8,128)(2,1)S(1)}, u32[]{:S(2)}, u32[]{:S(2)}) collective-permute-start(bf16[4,64,512]{2,1,0:T(8,128)(2,1)S(1)} %get-tuple-element.42), channel_id=1, source_target_pairs={{0,1},{1,0},{2,3},{3,2},{4,5},{5,4},{6,7},{7,6},{8,9},{9,8},{10,11... | collective-permute-start | bytes 786440 | tf_op jit(solution)/shard_map/ppermute | solution.py:33
  60.8 2.6 %collective-permute-start.7 = (bf16[1,64,512]{2,1,0:T(8,128)(2,1)S(1)}, bf16[1,64,512]{2,1,0:T(8,128)(2,1)S(1)}, u32[]{:S(2)}, u32[]{:S(2)}) collective-permute-start(bf16[1,64,512]{2,1,0:T(8,128)(2,1)S(1)} %get-tuple-element.44), channel_id=1, source_target_pairs={{0,4},{1,5},{2,6},{3,7},{4,0},{5,1},{6,2},{7,3},{8,12},{9,13},{10,... | collective-permute-start | bytes 196616 | tf_op jit(solution)/shard_map/ppermute | solution.py:38
  63.4 2.6 %collective-permute-done.7.refs_5_ = bf16[1,64,512]{2,1,0:T(8,128)(2,1)S(1)} collective-permute-done((bf16[1,64,512]{2,1,0:T(8,128)(2,1)S(1)}, bf16[1,64,512]{2,1,0:T(8,128)(2,1)S(1)}, u32[]{:S(2)}, u32[]{:S(2)}) %collective-permute-start.7) | collective-permute-done | bytes 65568 | tf_op jit(solution)/shard_map/ppermute | solution.py:38
  66.0 0.6 collective-permute-done.6.refs_3_
  66.6 0.5 collective-permute-done.5.refs_1_
  67.0 5.2 %step.13 = (f32[4,64,384]{2,1,0:T(8,128)S(1)}, bf16[4,64,384]{2,1,0:T(8,128)(2,1)S(1)}, f32[2,64,512]{2,1,0:T(8,128)S(1)}, bf16[2,64,512]{2,1,0:T(8,128)(2,1)S(1...) custom-call(f32[11]{0:T(128)S(1)} %pad_maximum_fusion.1.table_ref, bf16[2,2,512,2048]{3,2,1,0:T(8,128)(2,1)} %refs_0_.9, ...), custom_call_target="tpu_custom_call" | custom-call | flops 1000 | bytes 1000 | tf_op jit(solution)/shard_map/step/pallas_call | solution.py:335
  72.3 2.1 %collective-permute-start.13 = (bf16[2,128,2048]{2,1,0:T(8,128)(2,1)S(1)}, bf16[2,128,2048]{2,1,0:T(8,128)(2,1)S(1)}, u32[]{:S(2)}, u32[]{:S(2)}) collective-permute-start(bf16[2,128,2048]{2,1,0:T(8,128)(2,1)S(1)} %get-tuple-element.55), channel_id=1, source_target_pairs={{0,24},{8,0},{16,8},{24,16},{1,25},{9,1},{17,9},{25,17},{2,26},{10... | collective-permute-start | bytes 3145736 | tf_op jit(solution)/shard_map/ppermute | solution.py:33
  74.4 1.5 %collective-permute-start.9 = (bf16[4,64,384]{2,1,0:T(8,128)(2,1)S(1)}, bf16[4,64,384]{2,1,0:T(8,128)(2,1)S(1)}, u32[]{:S(2)}, u32[]{:S(2)}) collective-permute-start(bf16[4,64,384]{2,1,0:T(8,128)(2,1)S(1)} %get-tuple-element.48), channel_id=1, source_target_pairs={{0,1},{1,0},{2,3},{3,2},{4,5},{5,4},{6,7},{7,6},{8,9},{9,8},{10,11... | collective-permute-start | bytes 589832 | tf_op jit(solution)/shard_map/ppermute | solution.py:33
  75.9 1.6 %collective-permute-start.8 = (bf16[2,64,512]{2,1,0:T(8,128)(2,1)S(1)}, bf16[2,64,512]{2,1,0:T(8,128)(2,1)S(1)}, u32[]{:S(2)}, u32[]{:S(2)}) collective-permute-start(bf16[2,64,512]{2,1,0:T(8,128)(2,1)S(1)} %get-tuple-element.46), channel_id=1, source_target_pairs={{0,2},{1,3},{2,0},{3,1},{4,6},{5,7},{6,4},{7,5},{8,10},{9,11},{10,... | collective-permute-start | bytes 393224 | tf_op jit(solution)/shard_map/ppermute | solution.py:38
  77.4 2.8 %collective-permute-done.9.refs_1_ = bf16[4,64,384]{2,1,0:T(8,128)(2,1)S(1)} collective-permute-done((bf16[4,64,384]{2,1,0:T(8,128)(2,1)S(1)}, bf16[4,64,384]{2,1,0:T(8,128)(2,1)S(1)}, u32[]{:S(2)}, u32[]{:S(2)}) %collective-permute-start.9) | collective-permute-done | bytes 196640 | tf_op jit(solution)/shard_map/ppermute | solution.py:33
  80.2 0.6 step.14
  80.8 1.6 %collective-permute-start.10 = (bf16[2,64,384]{2,1,0:T(8,128)(2,1)S(1)}, bf16[2,64,384]{2,1,0:T(8,128)(2,1)S(1)}, u32[]{:S(2)}, u32[]{:S(2)}) collective-permute-start(bf16[2,64,384]{2,1,0:T(8,128)(2,1)S(1)} %get-tuple-element.50), channel_id=1, source_target_pairs={{0,2},{1,3},{2,0},{3,1},{4,6},{5,7},{6,4},{7,5},{8,10},{9,11},{10,... | collective-permute-start | bytes 294920 | tf_op jit(solution)/shard_map/ppermute | solution.py:38
  82.4 3.0 %collective-permute-done.10.refs_5_ = bf16[2,64,384]{2,1,0:T(8,128)(2,1)S(1)} collective-permute-done((bf16[2,64,384]{2,1,0:T(8,128)(2,1)S(1)}, bf16[2,64,384]{2,1,0:T(8,128)(2,1)S(1)}, u32[]{:S(2)}, u32[]{:S(2)}) %collective-permute-start.10) | collective-permute-done | bytes 98336 | tf_op jit(solution)/shard_map/ppermute | solution.py:38
  85.5 5.0 %step.15 = (f32[4,64,384]{2,1,0:T(8,128)S(1)}, bf16[4,64,384]{2,1,0:T(8,128)(2,1)S(1)}, f32[1,64,896]{2,1,0:T(8,128)S(1)}, bf16[1,64,896]{2,1,0:T(8,128)(2,1)S(1)}) custom-call(f32[11]{0:T(128)S(1)} %pad_maximum_fusion.1.table_ref, bf16[2,2,512,2048]{3,2,1,0:T(8,128)(2,1)} %refs_0_.9, bf16[2,192,2048]{2,1,0:T(8,128)(2,1)S(1)} %collective-permute-done.4.refs_1_, ...), custom_call_target="tpu_custom_call" | custom-call | flops 1000 | bytes 1000 | tf_op jit(solution)/shard_map/step/pallas_call | solution.py:335
  90.5 2.7 %collective-permute-start.11 = (bf16[1,64,896]{2,1,0:T(8,128)(2,1)S(1)}, bf16[1,64,896]{2,1,0:T(8,128)(2,1)S(1)}, u32[]{:S(2)}, u32[]{:S(2)}) collective-permute-start(bf16[1,64,896]{2,1,0:T(8,128)(2,1)S(1)} %get-tuple-element.52), channel_id=1, source_target_pairs={{0,4},{1,5},{2,6},{3,7},{4,0},{5,1},{6,2},{7,3},{8,12},{9,13},{10,... | collective-permute-start | bytes 344072 | tf_op jit(solution)/shard_map/ppermute | solution.py:38
  93.1 1.5 %collective-permute-start.12 = (bf16[4,64,384]{2,1,0:T(8,128)(2,1)S(1)}, bf16[4,64,384]{2,1,0:T(8,128)(2,1)S(1)}, u32[]{:S(2)}, u32[]{:S(2)}) collective-permute-start(bf16[4,64,384]{2,1,0:T(8,128)(2,1)S(1)} %get-tuple-element.54), channel_id=1, source_target_pairs={{0,1},{1,0},{2,3},{3,2},{4,5},{5,4},{6,7},{7,6},{8,9},{9,8},{10,11... | collective-permute-start | bytes 589832 | tf_op jit(solution)/shard_map/ppermute | solution.py:33
  94.6 3.9 %collective-permute-done.11.refs_3_.refs_1_ = bf16[1,64,896]{2,1,0:T(8,128)(2,1)S(1)} collective-permute-done((bf16[1,64,896]{2,1,0:T(8,128)(2,1)S(1)}, bf16[1,64,896]{2,1,0:T(8,128)(2,1)S(1)}, u32[]{:S(2)}, u32[]{:S(2)}) %collective-permute-start.11) | collective-permute-done | bytes 114720 | tf_op jit(solution)/shard_map/ppermute | solution.py:38
  98.5 3.4 %step.16 = (bf16[256,2048]{1,0:T(8,128)(2,1)S(1)}, bf16[2,256,2048]{2,1,0:T(8,128)(2,1)S(1)}, bf16[4,64,256]{2,1,0:T(8,128)(2,1)S(1)}, f32[64,2,2,512]{3,2,1,0:T(2,128)}) custom-call(f32[11]{0:T(128)S(1)} %pad_maximum_fusion.1.table_ref, bf16[2,2,512,2048]{3,2,1,0:T(8,128)(2,1)} %refs_0_.9, ...), custom_call_target="tpu_custom_call", output_to_operand_aliasing={{3}: (5, {})} | custom-call | flops 1000 | bytes 1000 | tf_op jit(solution)/shard_map/step/pallas_call | solution.py:335
  101.9 1.6 %collective-permute-start.14 = (bf16[4,64,256]{2,1,0:T(8,128)(2,1)S(1)}, bf16[4,64,256]{2,1,0:T(8,128)(2,1)S(1)}, u32[]{:S(2)}, u32[]{:S(2)}) collective-permute-start(bf16[4,64,256]{2,1,0:T(8,128)(2,1)S(1)} %get-tuple-element.59), channel_id=1, source_target_pairs={{0,1},{1,0},{2,3},{3,2},{4,5},{5,4},{6,7},{7,6},{8,9},{9,8},{10,11... | collective-permute-start | bytes 393224 | tf_op jit(solution)/shard_map/ppermute | solution.py:33
  103.5 1.3 %step.17.refs_2_ = f32[4,64,256]{2,1,0:T(8,128)S(1)} custom-call(f32[11]{0:T(128)S(1)} %pad_maximum_fusion.1.table_ref, bf16[2,256,2048]{2,1,0:T(8,128)(2,1)S(1)} %get-tuple-element.57.refs_0_, bf16[256,2048]{1,0:T(8,128)(2,1)S(1)} %get-tuple-element.58.refs_1_), custom_call_target="tpu_custom_call" | custom-call | flops 1000 | bytes 1000 | tf_op jit(solution)/shard_map/step/pallas_call | solution.py:335
  104.8 2.2 %collective-permute-done.14.refs_3_ = bf16[4,64,256]{2,1,0:T(8,128)(2,1)S(1)} collective-permute-done((bf16[4,64,256]{2,1,0:T(8,128)(2,1)S(1)}, bf16[4,64,256]{2,1,0:T(8,128)(2,1)S(1)}, u32[]{:S(2)}, u32[]{:S(2)}) %collective-permute-start.14) | collective-permute-done | bytes 131104 | tf_op jit(solution)/shard_map/ppermute | solution.py:33
  107.0 0.6 step.18
  107.6 1.1 collective-permute-start.15
  108.7 3.4 %collective-permute-start.16 = (bf16[1,64,640]{2,1,0:T(8,128)(2,1)S(1)}, bf16[1,64,640]{2,1,0:T(8,128)(2,1)S(1)}, u32[]{:S(2)}, u32[]{:S(2)}) collective-permute-start(bf16[1,64,640]{2,1,0:T(8,128)(2,1)S(1)} %get-tuple-element.62), channel_id=1, source_target_pairs={{0,4},{1,5},{2,6},{3,7},{4,0},{5,1},{6,2},{7,3},{8,12},{9,13},{10,... | collective-permute-start | bytes 245768 | tf_op jit(solution)/shard_map/ppermute | solution.py:38
  112.1 0.7 collective-permute-done.15.refs_3_
  112.8 4.2 %collective-permute-done.16.refs_4_ = bf16[1,64,640]{2,1,0:T(8,128)(2,1)S(1)} collective-permute-done((bf16[1,64,640]{2,1,0:T(8,128)(2,1)S(1)}, bf16[1,64,640]{2,1,0:T(8,128)(2,1)S(1)}, u32[]{:S(2)}, u32[]{:S(2)}) %collective-permute-start.16) | collective-permute-done | bytes 81952 | tf_op jit(solution)/shard_map/ppermute | solution.py:38
  116.9 1.5 %collective-permute-done.17.refs_5_ = bf16[1,64,640]{2,1,0:T(8,128)(2,1)S(1)} collective-permute-done((bf16[1,64,640]{2,1,0:T(8,128)(2,1)S(1)}, bf16[1,64,640]{2,1,0:T(8,128)(2,1)S(1)}, u32[]{:S(2)}, u32[]{:S(2)}) %collective-permute-start.17) | collective-permute-done | bytes 81952 | tf_op jit(solution)/shard_map/ppermute | solution.py:38
  118.4 1.5 %step.19 = f32[64,2,2,512]{3,2,1,0:T(2,128)} custom-call(f32[11]{0:T(128)S(1)} %pad_maximum_fusion.1.table_ref, f32[1,64,896]{2,1,0:T(8,128)S(1)} %get-tuple-element.51.refs_2_.refs_0_, bf16[1,64,896]{2,1,0:T(8,128)(2,1)S(1)} %collective-permute-done.11.refs_3_.refs_1_, f32[1,64,640]{2,1,0:T(8,128)S(1)} %get-tuple-element.60.refs_2_, ...), custom_call_target="tpu_custom_call", output_to_operand_aliasing={{}: (7, {})} | custom-call | flops 1000 | bytes 1000 | tf_op jit(solution)/shard_map/step/pallas_call | solution.py:335
  (12 shorter events, 0.0 us)
Async XLA Ops:
  1.7 5.8 %copy-start = (s32[2]{0:T(128)S(1)}, s32[2]{0:T(128)}, u32[]{:S(2)}) copy-start(s32[2]{0:T(128)} %param.4) | copy-start | bytes 28
  1.7 5.8 %copy-start.1 = (s32[2]{0:T(128)S(1)}, s32[2]{0:T(128)}, u32[]{:S(2)}) copy-start(s32[2]{0:T(128)} %param.5) | copy-start | bytes 28
  1.7 26.0 %collective-permute-start.1 = (bf16[2,256,2048]{2,1,0:T(8,128)(2,1)S(1)}, bf16[2,256,2048]{2,1,0:T(8,128)(2,1)}, u32[]{:S(2)}, u32[]{:S(2)}) collective-permute-start(bf16[2,256,2048]{2,1,0:T(8,128)(2,1)S(1)} %piece_of.2.rest_0_), channel_id=1, source_target_pairs={{0,24},{8,0},{16,8},{24,16},{1,25},{9,1},{17,9},{25,17},{2,26},{10... | collective-permute-start | bytes 6291464 | tf_op jit(solution)/shard_map/ppermute | solution.py:33
  6.7 43.5 %collective-permute-start = (bf16[2,256,2048]{2,1,0:T(8,128)(2,1)}, bf16[2,256,2048]{2,1,0:T(8,128)(2,1)}, u32[]{:S(2)}, u32[]{:S(2)}) collective-permute-start(bf16[2,256,2048]{2,1,0:T(8,128)(2,1)} %piece_of.3), channel_id=1, source_target_pairs={{0,24},{8,0},{16,8},{24,16},{1,25},{9,1},{17,9},{25,17},{2,26},{10... | collective-permute-start | bytes 6291464 | tf_op jit(solution)/shard_map/ppermute | solution.py:33
  34.8 32.2 %collective-permute-start.5 = (bf16[2,192,2048]{2,1,0:T(8,128)(2,1)S(1)}, bf16[2,192,2048]{2,1,0:T(8,128)(2,1)S(1)}, u32[]{:S(2)}, u32[]{:S(2)}) collective-permute-start(bf16[2,192,2048]{2,1,0:T(8,128)(2,1)S(1)} %get-tuple-element.40), channel_id=1, source_target_pairs={{0,24},{8,0},{16,8},{24,16},{1,25},{9,1},{17,9},{25,17},{2,26},{10... | collective-permute-start | bytes 4718600 | tf_op jit(solution)/shard_map/ppermute | solution.py:33
  36.9 7.2 %collective-permute-start.2 = (bf16[4,64,512]{2,1,0:T(8,128)(2,1)S(1)}, bf16[4,64,512]{2,1,0:T(8,128)(2,1)S(1)}, u32[]{:S(2)}, u32[]{:S(2)}) collective-permute-start(bf16[4,64,512]{2,1,0:T(8,128)(2,1)S(1)} %get-tuple-element.36), channel_id=1, source_target_pairs={{0,1},{1,0},{2,3},{3,2},{4,5},{5,4},{6,7},{7,6},{8,9},{9,8},{10,11... | collective-permute-start | bytes 786440 | tf_op jit(solution)/shard_map/ppermute | solution.py:33
  44.7 5.6 %collective-permute-start.3 = (bf16[2,64,512]{2,1,0:T(8,128)(2,1)S(1)}, bf16[2,64,512]{2,1,0:T(8,128)(2,1)S(1)}, u32[]{:S(2)}, u32[]{:S(2)}) collective-permute-start(bf16[2,64,512]{2,1,0:T(8,128)(2,1)S(1)} %get-tuple-element.38), channel_id=1, source_target_pairs={{0,2},{1,3},{2,0},{3,1},{4,6},{5,7},{6,4},{7,5},{8,10},{9,11},{10,... | collective-permute-start | bytes 393224 | tf_op jit(solution)/shard_map/ppermute | solution.py:38
  57.4 28.1 %collective-permute-start.4 = (bf16[2,192,2048]{2,1,0:T(8,128)(2,1)S(1)}, bf16[2,192,2048]{2,1,0:T(8,128)(2,1)S(1)}, u32[]{:S(2)}, u32[]{:S(2)}) collective-permute-start(bf16[2,192,2048]{2,1,0:T(8,128)(2,1)S(1)} %get-tuple-element.39), channel_id=1, source_target_pairs={{0,24},{8,0},{16,8},{24,16},{1,25},{9,1},{17,9},{25,17},{2,26},{10... | collective-permute-start | bytes 4718600 | tf_op jit(solution)/shard_map/ppermute | solution.py:33
  59.3 7.2 %collective-permute-start.6 = (bf16[4,64,512]{2,1,0:T(8,128)(2,1)S(1)}, bf16[4,64,512]{2,1,0:T(8,128)(2,1)S(1)}, u32[]{:S(2)}, u32[]{:S(2)}) collective-permute-start(bf16[4,64,512]{2,1,0:T(8,128)(2,1)S(1)} %get-tuple-element.42), channel_id=1, source_target_pairs={{0,1},{1,0},{2,3},{3,2},{4,5},{5,4},{6,7},{7,6},{8,9},{9,8},{10,11... | collective-permute-start | bytes 786440 | tf_op jit(solution)/shard_map/ppermute | solution.py:33
  60.8 5.2 %collective-permute-start.7 = (bf16[1,64,512]{2,1,0:T(8,128)(2,1)S(1)}, bf16[1,64,512]{2,1,0:T(8,128)(2,1)S(1)}, u32[]{:S(2)}, u32[]{:S(2)}) collective-permute-start(bf16[1,64,512]{2,1,0:T(8,128)(2,1)S(1)} %get-tuple-element.44), channel_id=1, source_target_pairs={{0,4},{1,5},{2,6},{3,7},{4,0},{5,1},{6,2},{7,3},{8,12},{9,13},{10,... | collective-permute-start | bytes 196616 | tf_op jit(solution)/shard_map/ppermute | solution.py:38
  72.3 26.2 %collective-permute-start.13 = (bf16[2,128,2048]{2,1,0:T(8,128)(2,1)S(1)}, bf16[2,128,2048]{2,1,0:T(8,128)(2,1)S(1)}, u32[]{:S(2)}, u32[]{:S(2)}) collective-permute-start(bf16[2,128,2048]{2,1,0:T(8,128)(2,1)S(1)} %get-tuple-element.55), channel_id=1, source_target_pairs={{0,24},{8,0},{16,8},{24,16},{1,25},{9,1},{17,9},{25,17},{2,26},{10... | collective-permute-start | bytes 3145736 | tf_op jit(solution)/shard_map/ppermute | solution.py:33
  74.4 5.8 %collective-permute-start.9 = (bf16[4,64,384]{2,1,0:T(8,128)(2,1)S(1)}, bf16[4,64,384]{2,1,0:T(8,128)(2,1)S(1)}, u32[]{:S(2)}, u32[]{:S(2)}) collective-permute-start(bf16[4,64,384]{2,1,0:T(8,128)(2,1)S(1)} %get-tuple-element.48), channel_id=1, source_target_pairs={{0,1},{1,0},{2,3},{3,2},{4,5},{5,4},{6,7},{7,6},{8,9},{9,8},{10,11... | collective-permute-start | bytes 589832 | tf_op jit(solution)/shard_map/ppermute | solution.py:33
  75.9 6.6 %collective-permute-start.8 = (bf16[2,64,512]{2,1,0:T(8,128)(2,1)S(1)}, bf16[2,64,512]{2,1,0:T(8,128)(2,1)S(1)}, u32[]{:S(2)}, u32[]{:S(2)}) collective-permute-start(bf16[2,64,512]{2,1,0:T(8,128)(2,1)S(1)} %get-tuple-element.46), channel_id=1, source_target_pairs={{0,2},{1,3},{2,0},{3,1},{4,6},{5,7},{6,4},{7,5},{8,10},{9,11},{10,... | collective-permute-start | bytes 393224 | tf_op jit(solution)/shard_map/ppermute | solution.py:38
  80.8 4.7 %collective-permute-start.10 = (bf16[2,64,384]{2,1,0:T(8,128)(2,1)S(1)}, bf16[2,64,384]{2,1,0:T(8,128)(2,1)S(1)}, u32[]{:S(2)}, u32[]{:S(2)}) collective-permute-start(bf16[2,64,384]{2,1,0:T(8,128)(2,1)S(1)} %get-tuple-element.50), channel_id=1, source_target_pairs={{0,2},{1,3},{2,0},{3,1},{4,6},{5,7},{6,4},{7,5},{8,10},{9,11},{10,... | collective-permute-start | bytes 294920 | tf_op jit(solution)/shard_map/ppermute | solution.py:38
  90.5 8.0 %collective-permute-start.11 = (bf16[1,64,896]{2,1,0:T(8,128)(2,1)S(1)}, bf16[1,64,896]{2,1,0:T(8,128)(2,1)S(1)}, u32[]{:S(2)}, u32[]{:S(2)}) collective-permute-start(bf16[1,64,896]{2,1,0:T(8,128)(2,1)S(1)} %get-tuple-element.52), channel_id=1, source_target_pairs={{0,4},{1,5},{2,6},{3,7},{4,0},{5,1},{6,2},{7,3},{8,12},{9,13},{10,... | collective-permute-start | bytes 344072 | tf_op jit(solution)/shard_map/ppermute | solution.py:38
  93.1 11.6 %collective-permute-start.12 = (bf16[4,64,384]{2,1,0:T(8,128)(2,1)S(1)}, bf16[4,64,384]{2,1,0:T(8,128)(2,1)S(1)}, u32[]{:S(2)}, u32[]{:S(2)}) collective-permute-start(bf16[4,64,384]{2,1,0:T(8,128)(2,1)S(1)} %get-tuple-element.54), channel_id=1, source_target_pairs={{0,1},{1,0},{2,3},{3,2},{4,5},{5,4},{6,7},{7,6},{8,9},{9,8},{10,11... | collective-permute-start | bytes 589832 | tf_op jit(solution)/shard_map/ppermute | solution.py:33
  101.9 5.0 %collective-permute-start.14 = (bf16[4,64,256]{2,1,0:T(8,128)(2,1)S(1)}, bf16[4,64,256]{2,1,0:T(8,128)(2,1)S(1)}, u32[]{:S(2)}, u32[]{:S(2)}) collective-permute-start(bf16[4,64,256]{2,1,0:T(8,128)(2,1)S(1)} %get-tuple-element.59), channel_id=1, source_target_pairs={{0,1},{1,0},{2,3},{3,2},{4,5},{5,4},{6,7},{7,6},{8,9},{9,8},{10,11... | collective-permute-start | bytes 393224 | tf_op jit(solution)/shard_map/ppermute | solution.py:33
  107.6 5.2 %collective-permute-start.15 = (bf16[1,64,640]{2,1,0:T(8,128)(2,1)S(1)}, bf16[1,64,640]{2,1,0:T(8,128)(2,1)S(1)}, u32[]{:S(2)}, u32[]{:S(2)}) collective-permute-start(bf16[1,64,640]{2,1,0:T(8,128)(2,1)S(1)} %get-tuple-element.61), channel_id=1, source_target_pairs={{0,2},{1,3},{2,0},{3,1},{4,6},{5,7},{6,4},{7,5},{8,10},{9,11},{10,... | collective-permute-start | bytes 245768 | tf_op jit(solution)/shard_map/ppermute | solution.py:38
  108.7 8.3 %collective-permute-start.16 = (bf16[1,64,640]{2,1,0:T(8,128)(2,1)S(1)}, bf16[1,64,640]{2,1,0:T(8,128)(2,1)S(1)}, u32[]{:S(2)}, u32[]{:S(2)}) collective-permute-start(bf16[1,64,640]{2,1,0:T(8,128)(2,1)S(1)} %get-tuple-element.62), channel_id=1, source_target_pairs={{0,4},{1,5},{2,6},{3,7},{4,0},{5,1},{6,2},{7,3},{8,12},{9,13},{10,... | collective-permute-start | bytes 245768 | tf_op jit(solution)/shard_map/ppermute | solution.py:38
  112.0 6.3 %collective-permute-start.17 = (bf16[1,64,640]{2,1,0:T(8,128)(2,1)S(1)}, bf16[1,64,640]{2,1,0:T(8,128)(2,1)S(1)}, u32[]{:S(2)}, u32[]{:S(2)}) collective-permute-start(bf16[1,64,640]{2,1,0:T(8,128)(2,1)S(1)} %get-tuple-element.63), channel_id=1, source_target_pairs={{0,6},{1,7},{2,4},{3,5},{4,2},{5,3},{6,0},{7,1},{8,14},{9,15},{10,... | collective-permute-start | bytes 245768 | tf_op jit(solution)/shard_map/ppermute | solution.py:38

commit v13 on v12

--- a/solution.py
+++ b/solution.py
@@ -21,21 +21,28 @@
 VMEM_BYTES = 48 * 1024 * 1024
 
 
-def shifted(block, axis, distance, fold=1, inner=False):
-    count = lax.axis_size(axis)
-    route = []
-    for i in range(count):
-        outer, place = divmod(i, fold)
-        if inner:
-            route.append((i, outer * fold + (place + distance) % fold))
-        else:
-            route.append((i, (outer + distance) % (count // fold) * fold + place))
-    return lax.ppermute(block, axis, route)
-
-
-def swapped(block, axis, distance):
-    count = lax.axis_size(axis)
-    return lax.ppermute(block, axis, [(i, i ^ distance) for i in range(count)])
+def sent(block, step, parity):
+    ka, ga = lax.axis_size("ka"), lax.axis_size("ga")
+    route = [(i, step(i)) for i in range(ga)]
+    if parity is None:
+        return lax.ppermute(block, "ga", route)
+    groups = range(parity, ka, 2)
+    pairs = [(j * ga + source, j * ga + target) for j in groups for source, target in route]
+    return lax.ppermute(block, ("ka", "ga"), pairs)
+
+
+def crossed_over(block, distance, fold, parity):
+    return sent(block, lambda i: i // fold * fold + (i + distance) % fold, parity)
+
+
+def swapped(block, distance, parity):
+    return sent(block, lambda i: i ^ distance, parity)
+
+
+def from_next(block, parity):
+    count = lax.axis_size("ka")
+    targets = range(count) if parity is None else range(parity, count, 2)
+    return lax.ppermute(block, "ka", [((i + 1) % count, i) for i in targets])
 
 
 def piece_kernel(slot, start, bands_ref, *rest):
@@ -96,10 +103,13 @@
             near_buf[mirror, columns] = near_im.astype(jnp.bfloat16)
 
 
-def put_sum(sum_buf, lane, total):
+def put_sum(sum_buf, lane, total, again):
     width = total.shape[1] // 2
-    sum_buf[:, 0, lane : lane + width] = total[:, :width]
-    sum_buf[:, 1, lane : lane + width] = total[:, width:]
+    for side in range(2):
+        half = total[:, side * width : (side + 1) * width]
+        if again:
+            half = half + sum_buf[:, side, lane : lane + width]
+        sum_buf[:, side, lane : lane + width] = half
 
 
 def step_kernel(plan, table_ref, *refs):
@@ -122,6 +132,7 @@
     arrived = [take(count) for count in plan.adds]
     if plan.adding and plan.placed:
         take(1)
+    take(plan.after)
     given_ref, kept_ref = take(2) if plan.near == "give" else (None, None)
     outs = take(len(plan.ways))
     targets = [take(task.count) for task in plan.tasks]
@@ -130,9 +141,21 @@
     if plan.part:
         if plan.near != "use":
             own_buf, own_sems = take(2)
-        slot, _, width = plan.part
+        slot, _, width, _ = plan.part
         base = slot * stride
         point = table_ref[base].astype(jnp.int32)
+        if plan.far:
+            far_buf, far_sems = take(2)
+            far = [
+                pltpu.make_async_copy(
+                    phased_ref.at[slot, part, pl.ds(plan.part[1], width), :],
+                    far_buf.at[part],
+                    far_sems.at[part],
+                )
+                for part in range(2)
+            ]
+            for copy in far:
+                copy.start()
         own = []
         loads_of = plan.ways + (0,) if plan.near == "give" else plan.ways
         for way, distance in enumerate(loads_of if plan.near != "use" else ()):
@@ -151,7 +174,7 @@
                     own[way].append(copy)
     if plan.later:
         piece_buf, piece_sems = take(2)
-        later_slot, later_start, later_width = plan.later
+        later_slot, later_start, later_width, _ = plan.later
         loads = [
             pltpu.make_async_copy(
                 bands_ref.at[later_slot, part, pl.ds(later_start, later_width), :],
@@ -169,9 +192,9 @@
     if plan.adding:
         sum_buf, placed_sem = take(2)
         add_slot, add_start, pieces = plan.adding
-        for index, column, start, span in pieces:
+        for index, column, start, span, again in pieces:
             total = summed(arrived[index], 0, slice(column, column + 2 * span))
-            put_sum(sum_buf, start - add_start, total)
+            put_sum(sum_buf, start - add_start, total, again)
         add_point = table_ref[add_slot * stride].astype(jnp.int32)
         columns = pl.ds(add_start, sum_buf.shape[2])
         placing = pltpu.make_async_copy(
@@ -183,7 +206,9 @@
         bit = lax.rem(lax.div(outer, 1 << task.stage), 2)
         for index, out_ref in enumerate(outputs):
             for level in range(out_ref.shape[0]):
-                if task.direct:
+                if task.count == 1:
+                    source = 0
+                elif task.direct:
                     source = partner(outer, index)
                 else:
                     source = 2 * level + (1 - bit if index else bit)
@@ -195,6 +220,10 @@
                     column += total.shape[1]
     if plan.part:
         near_ref = phased_ref
+        if plan.far:
+            for copy in far:
+                copy.wait()
+            phased_ref = far_buf
         if plan.near != "use":
             near_ref = given_ref if plan.near == "give" else take(1)[0]
             near_into(near_ref, phased_ref, table_ref, base, planes)
@@ -253,11 +282,15 @@
 
 
 class Task(NamedTuple):
-    batch: tuple
+    keys: tuple
     stage: int
     direct: bool
     each: int
     count: int
+
+    @property
+    def batch(self):
+        return sum(self.keys, ())
 
 
 class Plan(NamedTuple):
@@ -267,15 +300,17 @@
     part: tuple
     ways: tuple
     near: str
+    far: bool
     tasks: tuple
     takes: tuple
     adding: tuple
     adds: tuple
     placed: bool
     later: tuple
-
-
-def step(plan, table, bands, phased, sources, arrived, result):
+    after: int
+
+
+def step(plan, table, bands, phased, sources, arrived, result, after):
     rows, _, _, nbands = plan.shape
     fold, depth = plan.fold, plan.depth
     points = bands.shape[-1]
@@ -290,7 +325,7 @@
     if plan.part:
         width = plan.part[2]
         operands += [bands, phased]
-        in_specs += [vmem if plan.near == "use" else hbm, vmem]
+        in_specs += [vmem if plan.near == "use" else hbm, hbm if plan.far else vmem]
         if plan.near == "give":
             out_shape.append(jax.ShapeDtypeStruct((2 * width, points), jnp.bfloat16))
             out_shape.append(jax.ShapeDtypeStruct((2, depth * rows, points), jnp.bfloat16))
@@ -302,11 +337,16 @@
                 pltpu.VMEM((len(plan.ways), 2, depth * rows, points), jnp.bfloat16),
                 pltpu.SemaphoreType.DMA((fold, 2, depth)),
             ]
+        if plan.far:
+            scratch += [
+                pltpu.VMEM((2, width, points), jnp.bfloat16),
+                pltpu.SemaphoreType.DMA((2,)),
+            ]
     for arrays in sources + arrived:
         operands += arrays
         in_specs += [vmem] * len(arrays)
     for task in plan.tasks:
-        wide = sum(2 * width for _, _, width in task.batch)
+        wide = sum(2 * part[2] for part in task.batch)
         levels = 1 if task.direct else depth >> (task.stage + 1)
         out_shape += [
             jax.ShapeDtypeStruct((levels, rows, wide), kind(i)) for i in range(task.count)
@@ -324,11 +364,13 @@
             in_specs.append(hbm)
         out_shape.append(jax.ShapeDtypeStruct(plan.shape, jnp.float32))
         out_specs.append(hbm)
-        lanes = sum(span for _, _, _, span in plan.adding[2])
+        lanes = sum(span for _, _, _, span, again in plan.adding[2] if not again)
         scratch += [pltpu.VMEM((rows, 2, lanes), jnp.float32), pltpu.SemaphoreType.DMA]
     if plan.later:
         out_shape.append(jax.ShapeDtypeStruct((2, plan.later[2], points), bands.dtype))
         out_specs.append(hbm)
+    operands += after
+    in_specs += [pl.BlockSpec(memory_space=pl.ANY)] * len(after)
     if plan.near == "make":
         scratch.append(pltpu.VMEM((2 * width, points), jnp.bfloat16))
     outs = list(
@@ -356,51 +398,61 @@
     return terms, near, sends, result, piece
 
 
-def cuts(nbands, first):
-    eighth = nbands // 8
-    widths = [4 * eighth, 4 * eighth] if first else [3 * eighth, 3 * eighth, 2 * eighth]
-    starts = [sum(widths[:i]) for i in range(len(widths))]
-    return list(zip(starts, widths))
-
-
-def schedule(parts, fold, depth):
+def cuts(nbands, k_dev):
+    half, eighth = nbands // 2, nbands // 8
+    last = k_dev - 1
+    wide = [(slot, start, half, None) for slot in range(last) for start in (0, half)]
+    early = [(last, start, half, 0) for start in (0, half)]
+    widths = (3 * eighth, 3 * eighth, 2 * eighth)
+    late = [(last, sum(widths[:i]), width, 1) for i, width in enumerate(widths)]
+    return wide, early, late
+
+
+def schedule(wide, early, late, fold, depth):
     every, others = tuple(range(fold)), tuple(range(1, fold))
+    parts = wide + late
     count = len(parts)
-    kernels = []
+    kernels = [(early[0], every, "make", (), ())]
+
+    def cross(*done):
+        return Task(tuple((part,) for part in done), 0, False, fold, 2)
+
+    def halve(*keys):
+        return Task(keys, 1, False, 2, 2)
+
     waiting, halved, crossed = [], [], []
+    aside = [
+        (),
+        (cross(*early),),
+        (halve(tuple(early)),),
+        (Task((tuple(early),), 2, True, 2, 1),),
+    ]
     for index, part in enumerate(parts):
-        ready = ready_parts(waiting)
-        waiting = waiting[len(ready) :]
+        ready = tuple(waiting[:1])
+        waiting = waiting[1:]
         tasks = []
         if halved:
-            tasks.append(Task(tuple(halved), 1, False, 2, 2))
+            tasks.append(halve(*((done,) for done in halved)))
         if crossed:
-            tasks.append(Task(tuple(crossed), 0, False, fold, 2))
-        waiting += halved
+            tasks.append(cross(*crossed))
+        if index < len(aside):
+            tasks += aside[index]
+        waiting += [done for done in halved if done in wide]
         if index == count - 1:
             kernels.append((part, others, "give", tuple(tasks), ready))
             kernels.append((part, every[:1], "use", (), ()))
         else:
             kernels.append((part, every, "make", tuple(tasks), ready))
         halved, crossed = crossed, [part] if index < count - 2 else []
+        if index == 0:
+            kernels += [(other, every, "make", (), ()) for other in early[1:]]
         if index in (0, count - 3):
-            kernels.append((None, (), "", (Task((part,), 0, False, fold, 2),), ()))
+            kernels.append((None, (), "", (cross(part),), ()))
             halved, crossed = halved + crossed, []
-    last = tuple(parts[-2:])
+    last = tuple((part,) for part in late[-2:])
     kernels.append((None, (), "", (Task(last, 0, True, fold, depth),), ()))
-    kernels.append((None, (), "", (), tuple(waiting) + last))
+    kernels.append((None, (), "", (), tuple(early) + tuple(late)))
     return kernels
-
-
-def ready_parts(waiting):
-    total = 0
-    for count, (slot, _, width) in enumerate(waiting, 1):
-        total += width
-        if slot != waiting[0][0]:
-            break
-        if total % LANES == 0:
-            return tuple(waiting[:count])
-    return ()
 
 
 def body(bands, nbr_slot, gshift):
@@ -420,31 +472,33 @@
     columns = [order[:, None].astype(jnp.float32), jnp.cos(angle), jnp.sin(angle)]
     table = jnp.concatenate(columns, axis=1).reshape(-1)
     table = jnp.append(table, grid_index.astype(jnp.float32))
-    parts = []
-    for slot in range(k_dev):
-        for start, width in cuts(nbands, slot == 0):
-            parts.append((slot, start, width))
-    theres = []
+    wide, early, late = cuts(nbands, k_dev)
+    parts = wide + late
+    theres = {}
     piece = None
-    for slot, start, width in parts[:AHEAD]:
-        piece = piece_of(slot, start, width, bands, [] if piece is None else [piece])
-        theres.append(shifted(piece, "ka", -1))
+    beside = from_next(bands, early[0][3])
+    for part in parts[:AHEAD]:
+        piece = piece_of(*part[:3], bands, [] if piece is None else [piece])
+        theres[part] = from_next(piece, part[3])
     shape = (rows, k_dev, 2, nbands)
     depth = min(OUTER, grid_count)
     fold = grid_count // depth
     held = {}
     near, result = None, None
-    for part, ways, phase, tasks, adds in schedule(parts, fold, depth):
-        place = parts.index(part) if part else len(parts)
-        later = parts[place + AHEAD] if place + AHEAD < len(parts) else None
-        sources = [[array for done in task.batch for array in held[(done,)]] for task in tasks]
+    after = []
+    for part, ways, phase, tasks, adds in schedule(wide, early, late, fold, depth):
+        later = None
+        if part in parts and phase != "use" and parts.index(part) + AHEAD < len(parts):
+            later = parts[parts.index(part) + AHEAD]
+        sources = [[array for key in task.keys for array in held[key]] for task in tasks]
         batches, pieces = [], []
         for done in adds:
             batch = max((key for key in held if done in key), key=len)
             if batch not in batches:
                 batches.append(batch)
-            column = sum(2 * width for _, _, width in batch[: batch.index(done)])
-            pieces.append((batches.index(batch), column, done[1], done[2]))
+            column = sum(2 * other[2] for other in batch[: batch.index(done)])
+            again = done in late
+            pieces.append((batches.index(batch), column, done[1], done[2], again))
         arrived = [held[batch] for batch in batches]
         adding = (adds[0][0], adds[0][1], tuple(pieces)) if adds else ()
         plan = Plan(
@@ -454,28 +508,34 @@
             part,
             ways,
             phase,
+            part in early,
             tasks,
             tuple(len(arrays) for arrays in sources),
             adding,
             tuple(len(arrays) for arrays in arrived),
             result is not None,
             later,
+            len(after),
         )
-        phased, own = theres[place] if part else None, bands
+        phased, own = beside if part in early else theres.get(part), bands
         if phase == "use":
             phased, own = near
         terms, near, sends, result, piece = step(
-            plan, table, own, phased, sources, arrived, result
+            plan, table, own, phased, sources, arrived, result, after
         )
+        after = terms[:1]
         if later:
-            theres.append(shifted(piece, "ka", -1))
+            theres[later] = from_next(piece, later[3])
         for way, array in zip(ways, terms):
-            array = shifted(array, "ga", way, fold, True) if way else array
+            if way:
+                array = crossed_over(array, way, fold, part[3])
             held.setdefault((part,), []).insert(0 if way == 0 else fold, array)
         for task, arrays in zip(tasks, sends):
             steps = range(1, depth) if task.direct else [1 << task.stage]
+            parities = {done[3] for done in task.batch}
+            parity = parities.pop() if len(parities) == 1 else None
             held[task.batch] = [arrays[0]] + [
-                swapped(array, "ga", fold * i) for array, i in zip(arrays[1:], steps)
+                swapped(array, fold * i, parity) for array, i in zip(arrays[1:], steps)
             ]
     return result
 

time: 120 us -> 130 us (1.083)
  the two profiles are of different devices: /device:TPU:0 before, /device:TPU:1 now
where the time goes in v13:
time: 130 us
  Pallas kernels  53.2 us (41%)
  starting transfers between devices  48.5 us (37%)
  waiting for transfers between devices  27 us (21%)
    pallas_call x12, Pallas kernels, step(): pl.pallas_call(functools.partial(step_kernel, plan), in_specs=in_specs, o...  49 us
    ppermute x11, starting transfers between devices, sent(): return lax.ppermute(block, ('ka', 'ga'), pairs)  25.5 us
    ppermute x6, starting transfers between devices, from_next(): return lax.ppermute(block, 'ka', [((i + 1) % count, i) for i in targets])  12.5 us
    ppermute x6, waiting for transfers between devices, from_next(): return lax.ppermute(block, 'ka', [((i + 1) % count, i) for i in targets])  11.8 us
    ppermute x6, starting transfers between devices, sent(): return lax.ppermute(block, 'ga', route)  10.5 us
    ppermute x11, waiting for transfers between devices, sent(): return lax.ppermute(block, ('ka', 'ga'), pairs)  8.48 us
    ppermute x6, waiting for transfers between devices, sent(): return lax.ppermute(block, 'ga', route)  6.75 us
    pallas_call x2, Pallas kernels, piece_of(): pl.pallas_call(functools.partial(piece_kernel, slot, start), in_specs=[pl...  4.28 us
  transfers between devices with their start and end apart: 23, of which 13 were waited for; matrix products, arithmetic and copies ran while one was open for 0% of the time, Pallas kernels for 39%

profile of v13, /device:TPU:1, one launch (start us, length us, event | category | flops | bytes accessed | tf_op | source)
XLA Modules:
  0.0 129.8 jit_solution(17277224478440789451)
XLA Ops:
  0.0 5.2 %collective-permute-start.2 = (bf16[2,2,512,2048]{3,2,1,0:T(8,128)(2,1)}, bf16[2,2,512,2048]{3,2,1,0:T(8,128)(2,1)}, u32[]{:S(2)}, u32[]{:S(2)}) collective-permute-start(bf16[2,2,512,2048]{3,2,1,0:T(8,128)(2,1)} %refs_0_.13), channel_id=1, source_target_pairs={{8,0},{24,16},{9,1},{25,17},{10,2},{26,18},{11,3},{27,19},{12,4},{... | collective-permute-start | bytes 25165832 | tf_op jit(solution)/shard_map/ppermute | solution.py:45
  5.2 1.6 %piece_of.2.rest_0_ = bf16[2,256,2048]{2,1,0:T(8,128)(2,1)S(1)} custom-call(bf16[2,2,512,2048]{3,2,1,0:T(8,128)(2,1)} %refs_0_.13), custom_call_target="tpu_custom_call" | custom-call | flops 1000 | bytes 1000 | tf_op jit(solution)/shard_map/piece_of/pallas_call | solution.py:71
  7.0 2.6 %piece_of.3 = bf16[2,256,2048]{2,1,0:T(8,128)(2,1)} custom-call(bf16[2,2,512,2048]{3,2,1,0:T(8,128)(2,1)} %refs_0_.13, bf16[2,256,2048]{2,1,0:T(8,128)(2,1)S(1)} %piece_of.2.rest_0_), custom_call_target="tpu_custom_call" | custom-call | flops 1000 | bytes 1000 | tf_op jit(solution)/shard_map/piece_of/pallas_call | solution.py:71
  9.6 3.1 %collective-permute-start = (bf16[2,256,2048]{2,1,0:T(8,128)(2,1)}, bf16[2,256,2048]{2,1,0:T(8,128)(2,1)}, u32[]{:S(2)}, u32[]{:S(2)}) collective-permute-start(bf16[2,256,2048]{2,1,0:T(8,128)(2,1)} %piece_of.3), channel_id=1, source_target_pairs={{8,0},{16,8},{24,16},{0,24},{9,1},{17,9},{25,17},{1,25},{10,2},{18... | collective-permute-start | bytes 6291464 | tf_op jit(solution)/shard_map/ppermute | solution.py:45
  13.3 1.7 %collective-permute-done.2.refs_1_ = bf16[2,2,512,2048]{3,2,1,0:T(8,128)(2,1)} collective-permute-done((bf16[2,2,512,2048]{3,2,1,0:T(8,128)(2,1)}, bf16[2,2,512,2048]{3,2,1,0:T(8,128)(2,1)}, u32[]{:S(2)}, u32[]{:S(2)}) %collective-permute-start.2) | collective-permute-done | bytes 8388640 | tf_op jit(solution)/shard_map/ppermute | solution.py:45
  15.1 8.1 %step.12 = (f32[4,64,512]{2,1,0:T(8,128)S(1)}, bf16[4,64,512]{2,1,0:T(8,128)(2,1)S(1)}) custom-call(f32[11]{0:T(128)S(1)} %pad_maximum_fusion.1.table_ref, bf16[2,2,512,2048]{3,2,1,0:T(8,128)(2,1)} %refs_0_.13, bf16[2,2,512,2048]{3,2,1,0:T(8,128)(2,1)} %collective-permute-done.2.refs_1_), custom_call_target="tpu_custom_call" | custom-call | flops 1000 | bytes 1000 | tf_op jit(solution)/shard_map/step/pallas_call | solution.py:377
  23.2 9.3 %collective-permute-done.1.refs_1_ = bf16[2,256,2048]{2,1,0:T(8,128)(2,1)} collective-permute-done((bf16[2,256,2048]{2,1,0:T(8,128)(2,1)S(1)}, bf16[2,256,2048]{2,1,0:T(8,128)(2,1)}, u32[]{:S(2)}, u32[]{:S(2)}) %collective-permute-start.1) | collective-permute-done | bytes 2097184 | tf_op jit(solution)/shard_map/ppermute | solution.py:45
  32.5 7.1 %step.13 = (f32[4,64,512]{2,1,0:T(8,128)S(1)}, bf16[4,64,512]{2,1,0:T(8,128)(2,1)S(1)}, bf16[2,192,2048]{2,1,0:T(8,128)(2,1)S(1)}) custom-call(f32[11]{0:T(128)S(1)} %pad_maximum_fusion.1.table_ref, bf16[2,2,512,2048]{3,2,1,0:T(8,128)(2,1)} %refs_0_.13, bf16[2,256,2048]{2,1,0:T(8,128)(2,1)} %collective-permute-done.1.refs_1_, ...), custom_call_target="tpu_custom_call" | custom-call | flops 1000 | bytes 1000 | tf_op jit(solution)/shard_map/step/pallas_call | solution.py:377
  39.6 1.3 collective-permute-start.8
  40.9 2.7 %collective-permute-start.3 = (bf16[4,64,512]{2,1,0:T(8,128)(2,1)S(1)}, bf16[4,64,512]{2,1,0:T(8,128)(2,1)S(1)}, u32[]{:S(2)}, u32[]{:S(2)}) collective-permute-start(bf16[4,64,512]{2,1,0:T(8,128)(2,1)S(1)} %get-tuple-element.46), channel_id=1, source_target_pairs={{0,1},{1,0},{2,3},{3,2},{4,5},{5,4},{6,7},{7,6},{8,9},{9,8},{10,11... | collective-permute-start | bytes 786440 | tf_op jit(solution)/shard_map/ppermute | solution.py:28
  43.7 8.1 %step.14 = (f32[4,64,512]{2,1,0:T(8,128)S(1)}, bf16[4,64,512]{2,1,0:T(8,128)(2,1)S(1)}) custom-call(f32[11]{0:T(128)S(1)} %pad_maximum_fusion.1.table_ref, bf16[2,2,512,2048]{3,2,1,0:T(8,128)(2,1)} %refs_0_.13, bf16[2,2,512,2048]{3,2,1,0:T(8,128)(2,1)} %collective-permute-done.2.refs_1_, f32[4,64,512]{2,1,0:T(8,128)S(1)} %get-tuple-element.45.refs_2_.refs_0_), custom_call_target="tpu_custom_call" | custom-call | flops 1000 | bytes 1000 | tf_op jit(solution)/shard_map/step/pallas_call | solution.py:377
  51.8 0.7 collective-permute-start.6
  52.5 0.7 collective-permute-start.5
  53.2 0.6 step.15
  53.8 1.4 %collective-permute-start.4 = (bf16[2,64,512]{2,1,0:T(8,128)(2,1)S(1)}, bf16[2,64,512]{2,1,0:T(8,128)(2,1)S(1)}, u32[]{:S(2)}, u32[]{:S(2)}) collective-permute-start(bf16[2,64,512]{2,1,0:T(8,128)(2,1)S(1)} %get-tuple-element.49), channel_id=1, source_target_pairs={{0,2},{1,3},{2,0},{3,1},{4,6},{5,7},{6,4},{7,5},{8,10},{9,11},{10,... | collective-permute-start | bytes 393224 | tf_op jit(solution)/shard_map/ppermute | solution.py:28
  55.1 2.5 %collective-permute-done.4.refs_3_ = bf16[2,64,512]{2,1,0:T(8,128)(2,1)S(1)} collective-permute-done((bf16[2,64,512]{2,1,0:T(8,128)(2,1)S(1)}, bf16[2,64,512]{2,1,0:T(8,128)(2,1)S(1)}, u32[]{:S(2)}, u32[]{:S(2)}) %collective-permute-start.4) | collective-permute-done | bytes 131104 | tf_op jit(solution)/shard_map/ppermute | solution.py:28
  57.7 7.1 %step.16 = (f32[4,64,512]{2,1,0:T(8,128)S(1)}, bf16[4,64,512]{2,1,0:T(8,128)(2,1)S(1)}, f32[1,64,512]{2,1,0:T(8,128)S(1)}, bf16[1,64,512]{2,1,0:T(8,128)(2,1)S(1...) custom-call(f32[11]{0:T(128)S(1)} %pad_maximum_fusion.1.table_ref, ...), custom_call_target="tpu_custom_call" | custom-call | flops 1000 | bytes 1000 | tf_op jit(solution)/shard_map/step/pallas_call | solution.py:377
  64.8 1.5 %collective-permute-start.7 = (bf16[2,192,2048]{2,1,0:T(8,128)(2,1)S(1)}, bf16[2,192,2048]{2,1,0:T(8,128)(2,1)S(1)}, u32[]{:S(2)}, u32[]{:S(2)}) collective-permute-start(bf16[2,192,2048]{2,1,0:T(8,128)(2,1)S(1)} %get-tuple-element.52), channel_id=1, source_target_pairs={{16,8},{0,24},{17,9},{1,25},{18,10},{2,26},{19,11},{3,27},{20,12},... | collective-permute-start | bytes 4718600 | tf_op jit(solution)/shard_map/ppermute | solution.py:45
  66.4 0.7 collective-permute-start.10
  67.1 2.5 %collective-permute-start.11 = (bf16[1,64,512]{2,1,0:T(8,128)(2,1)S(1)}, bf16[1,64,512]{2,1,0:T(8,128)(2,1)S(1)}, u32[]{:S(2)}, u32[]{:S(2)}) collective-permute-start(bf16[1,64,512]{2,1,0:T(8,128)(2,1)S(1)} %get-tuple-element.59), channel_id=1, source_target_pairs={{0,4},{1,5},{2,6},{3,7},{4,0},{5,1},{6,2},{7,3},{8,12},{9,13},{10,... | collective-permute-start | bytes 196616 | tf_op jit(solution)/shard_map/ppermute | solution.py:28
  69.6 1.7 %collective-permute-done.11.refs_7_ = bf16[1,64,512]{2,1,0:T(8,128)(2,1)S(1)} collective-permute-done((bf16[1,64,512]{2,1,0:T(8,128)(2,1)S(1)}, bf16[1,64,512]{2,1,0:T(8,128)(2,1)S(1)}, u32[]{:S(2)}, u32[]{:S(2)}) %collective-permute-start.11) | collective-permute-done | bytes 65568 | tf_op jit(solution)/shard_map/ppermute | solution.py:28
  71.3 0.3 collective-permute-done.9.refs_3_
  71.5 0.2 collective-permute-done.8.refs_1_
  71.7 5.3 %step.17 = (f32[4,64,384]{2,1,0:T(8,128)S(1)}, bf16[4,64,384]{2,1,0:T(8,128)(2,1)S(1)}, f32[2,64,512]{2,1,0:T(8,128)S(1)}, bf16[2,64,512]{2,1,0:T(8,128)(2,1)S(1...) custom-call(f32[11]{0:T(128)S(1)} %pad_maximum_fusion.1.table_ref, ...), custom_call_target="tpu_custom_call" | custom-call | flops 1000 | bytes 1000 | tf_op jit(solution)/shard_map/step/pallas_call | solution.py:377
  77.0 1.3 collective-permute-start.18
  78.3 4.5 %collective-permute-start.13 = (bf16[4,64,384]{2,1,0:T(8,128)(2,1)S(1)}, bf16[4,64,384]{2,1,0:T(8,128)(2,1)S(1)}, u32[]{:S(2)}, u32[]{:S(2)}) collective-permute-start(bf16[4,64,384]{2,1,0:T(8,128)(2,1)S(1)} %get-tuple-element.63), channel_id=1, source_target_pairs={{8,9},{9,8},{10,11},{11,10},{12,13},{13,12},{14,15},{15,14},{24,25... | collective-permute-start | bytes 589832 | tf_op jit(solution)/shard_map/ppermute | solution.py:31
  82.8 1.4 %collective-permute-start.12 = (bf16[2,64,512]{2,1,0:T(8,128)(2,1)S(1)}, bf16[2,64,512]{2,1,0:T(8,128)(2,1)S(1)}, u32[]{:S(2)}, u32[]{:S(2)}) collective-permute-start(bf16[2,64,512]{2,1,0:T(8,128)(2,1)S(1)} %get-tuple-element.61), channel_id=1, source_target_pairs={{0,2},{1,3},{2,0},{3,1},{4,6},{5,7},{6,4},{7,5},{8,10},{9,11},{10,... | collective-permute-start | bytes 393224 | tf_op jit(solution)/shard_map/ppermute | solution.py:28
  84.2 0.7 collective-permute-start.15
  84.8 1.0 collective-permute-done.13.refs_1_
  85.9 0.6 step.18
  86.5 3.5 %collective-permute-start.14 = (bf16[2,64,384]{2,1,0:T(8,128)(2,1)S(1)}, bf16[2,64,384]{2,1,0:T(8,128)(2,1)S(1)}, u32[]{:S(2)}, u32[]{:S(2)}) collective-permute-start(bf16[2,64,384]{2,1,0:T(8,128)(2,1)S(1)} %get-tuple-element.65), channel_id=1, source_target_pairs={{8,10},{9,11},{10,8},{11,9},{12,14},{13,15},{14,12},{15,13},{24,26... | collective-permute-start | bytes 294920 | tf_op jit(solution)/shard_map/ppermute | solution.py:31
  90.0 2.0 %collective-permute-done.14.refs_5_ = bf16[2,64,384]{2,1,0:T(8,128)(2,1)S(1)} collective-permute-done((bf16[2,64,384]{2,1,0:T(8,128)(2,1)S(1)}, bf16[2,64,384]{2,1,0:T(8,128)(2,1)S(1)}, u32[]{:S(2)}, u32[]{:S(2)}) %collective-permute-start.14) | collective-permute-done | bytes 98336 | tf_op jit(solution)/shard_map/ppermute | solution.py:31
  92.0 0.5 collective-permute-done.7.refs_1_
  92.5 5.0 %step.19 = (f32[4,64,384]{2,1,0:T(8,128)S(1)}, bf16[4,64,384]{2,1,0:T(8,128)(2,1)S(1)}, f32[1,64,896]{2,1,0:T(8,128)S(1)}, bf16[1,64,896]{2,1,0:T(8,128)(2,1)S(1)}, f32[1,64,1024]{2,1,0:T(8,128)S(1)}) custom-call(f32[11]{0:T(128)S(1)} %pad_maximum_fusion.1.table_ref, bf16[2,2,512,2048]{3,2,1,0:T(8,128)(2,1)} %refs_0_.13, ...), custom_call_target="tpu_custom_call" | custom-call | flops 1000 | bytes 1000 | tf_op jit(solution)/shard_map/step/pallas_call | solution.py:377
  97.5 2.4 %collective-permute-start.16 = (bf16[1,64,896]{2,1,0:T(8,128)(2,1)S(1)}, bf16[1,64,896]{2,1,0:T(8,128)(2,1)S(1)}, u32[]{:S(2)}, u32[]{:S(2)}) collective-permute-start(bf16[1,64,896]{2,1,0:T(8,128)(2,1)S(1)} %get-tuple-element.70), channel_id=1, source_target_pairs={{0,4},{1,5},{2,6},{3,7},{4,0},{5,1},{6,2},{7,3},{8,12},{9,13},{10,... | collective-permute-start | bytes 344072 | tf_op jit(solution)/shard_map/ppermute | solution.py:28
  99.9 2.7 %collective-permute-start.17 = (bf16[4,64,384]{2,1,0:T(8,128)(2,1)S(1)}, bf16[4,64,384]{2,1,0:T(8,128)(2,1)S(1)}, u32[]{:S(2)}, u32[]{:S(2)}) collective-permute-start(bf16[4,64,384]{2,1,0:T(8,128)(2,1)S(1)} %get-tuple-element.72), channel_id=1, source_target_pairs={{8,9},{9,8},{10,11},{11,10},{12,13},{13,12},{14,15},{15,14},{24,25... | collective-permute-start | bytes 589832 | tf_op jit(solution)/shard_map/ppermute | solution.py:31
  102.6 2.3 %collective-permute-done.16.refs_3_.refs_2_ = bf16[1,64,896]{2,1,0:T(8,128)(2,1)S(1)} collective-permute-done((bf16[1,64,896]{2,1,0:T(8,128)(2,1)S(1)}, bf16[1,64,896]{2,1,0:T(8,128)(2,1)S(1)}, u32[]{:S(2)}, u32[]{:S(2)}) %collective-permute-start.16) | collective-permute-done | bytes 114720 | tf_op jit(solution)/shard_map/ppermute | solution.py:28
  104.9 3.4 %step.20 = (bf16[256,2048]{1,0:T(8,128)(2,1)S(1)}, bf16[2,256,2048]{2,1,0:T(8,128)(2,1)S(1)}, bf16[4,64,256]{2,1,0:T(8,128)(2,1)S(1)}, f32[64,2,2,512]{3,2,1,0:T(2,128)}) custom-call(f32[11]{0:T(128)S(1)} %pad_maximum_fusion.1.table_ref, bf16[2,2,512,2048]{3,2,1,0:T(8,128)(2,1)} %refs_0_.13, ...), custom_call_target="tpu_custom_call", output_to_operand_aliasing={{3}: (5, {})} | custom-call | flops 1000 | bytes 1000 | tf_op jit(solution)/shard_map/step/pallas_call | solution.py:377
  108.3 2.9 %collective-permute-start.19 = (bf16[4,64,256]{2,1,0:T(8,128)(2,1)S(1)}, bf16[4,64,256]{2,1,0:T(8,128)(2,1)S(1)}, u32[]{:S(2)}, u32[]{:S(2)}) collective-permute-start(bf16[4,64,256]{2,1,0:T(8,128)(2,1)S(1)} %get-tuple-element.77.refs_2_), channel_id=1, source_target_pairs={{8,9},{9,8},{10,11},{11,10},{12,13},{13,12},{14,15},{15,14},{24,25... | collective-permute-start | bytes 393224 | tf_op jit(solution)/shard_map/ppermute | solution.py:31
  111.2 1.3 step.21.refs_2_.refs_4_
  112.5 1.5 %collective-permute-done.19.refs_3_ = bf16[4,64,256]{2,1,0:T(8,128)(2,1)S(1)} collective-permute-done((bf16[4,64,256]{2,1,0:T(8,128)(2,1)S(1)}, bf16[4,64,256]{2,1,0:T(8,128)(2,1)S(1)}, u32[]{:S(2)}, u32[]{:S(2)}) %collective-permute-start.19) | collective-permute-done | bytes 131104 | tf_op jit(solution)/shard_map/ppermute | solution.py:31
  114.0 0.6 step.22
  114.7 2.7 %collective-permute-start.20 = (bf16[1,64,640]{2,1,0:T(8,128)(2,1)S(1)}, bf16[1,64,640]{2,1,0:T(8,128)(2,1)S(1)}, u32[]{:S(2)}, u32[]{:S(2)}) collective-permute-start(bf16[1,64,640]{2,1,0:T(8,128)(2,1)S(1)} %get-tuple-element.79), channel_id=1, source_target_pairs={{8,10},{9,11},{10,8},{11,9},{12,14},{13,15},{14,12},{15,13},{24,26... | collective-permute-start | bytes 245768 | tf_op jit(solution)/shard_map/ppermute | solution.py:31
  117.4 3.5 %collective-permute-start.21 = (bf16[1,64,640]{2,1,0:T(8,128)(2,1)S(1)}, bf16[1,64,640]{2,1,0:T(8,128)(2,1)S(1)}, u32[]{:S(2)}, u32[]{:S(2)}) collective-permute-start(bf16[1,64,640]{2,1,0:T(8,128)(2,1)S(1)} %get-tuple-element.80), channel_id=1, source_target_pairs={{8,12},{9,13},{10,14},{11,15},{12,8},{13,9},{14,10},{15,11},{24,28... | collective-permute-start | bytes 245768 | tf_op jit(solution)/shard_map/ppermute | solution.py:31
  120.9 3.0 %collective-permute-start.22 = (bf16[1,64,640]{2,1,0:T(8,128)(2,1)S(1)}, bf16[1,64,640]{2,1,0:T(8,128)(2,1)S(1)}, u32[]{:S(2)}, u32[]{:S(2)}) collective-permute-start(bf16[1,64,640]{2,1,0:T(8,128)(2,1)S(1)} %get-tuple-element.81), channel_id=1, source_target_pairs={{8,14},{9,15},{10,12},{11,13},{12,10},{13,11},{14,8},{15,9},{24,30... | collective-permute-start | bytes 245768 | tf_op jit(solution)/shard_map/ppermute | solution.py:31
  124.0 0.4 collective-permute-done.21.refs_5_
  124.4 3.5 %collective-permute-done.22.refs_6_ = bf16[1,64,640]{2,1,0:T(8,128)(2,1)S(1)} collective-permute-done((bf16[1,64,640]{2,1,0:T(8,128)(2,1)S(1)}, bf16[1,64,640]{2,1,0:T(8,128)(2,1)S(1)}, u32[]{:S(2)}, u32[]{:S(2)}) %collective-permute-start.22) | collective-permute-done | bytes 81952 | tf_op jit(solution)/shard_map/ppermute | solution.py:31
  127.9 1.8 %step.23 = f32[64,2,2,512]{3,2,1,0:T(2,128)} custom-call(f32[11]{0:T(128)S(1)} %pad_maximum_fusion.1.table_ref, f32[1,64,1024]{2,1,0:T(8,128)S(1)} %get-tuple-element.68.refs_0_, f32[1,64,896]{2,1,0:T(8,128)S(1)} %get-tuple-element.69.refs_2_.refs_1_, ...), custom_call_target="tpu_custom_call", output_to_operand_aliasing={{}: (8, {})} | custom-call | flops 1000 | bytes 1000 | tf_op jit(solution)/shard_map/step/pallas_call | solution.py:377
  (24 shorter events, 0.9 us)
Async XLA Ops:
  0.0 15.1 %collective-permute-start.2 = (bf16[2,2,512,2048]{3,2,1,0:T(8,128)(2,1)}, bf16[2,2,512,2048]{3,2,1,0:T(8,128)(2,1)}, u32[]{:S(2)}, u32[]{:S(2)}) collective-permute-start(bf16[2,2,512,2048]{3,2,1,0:T(8,128)(2,1)} %refs_0_.13), channel_id=1, source_target_pairs={{8,0},{24,16},{9,1},{25,17},{10,2},{26,18},{11,3},{27,19},{12,4},{... | collective-permute-start | bytes 25165832 | tf_op jit(solution)/shard_map/ppermute | solution.py:45
  6.9 5.8 %copy-start = (s32[2]{0:T(128)S(1)}, s32[2]{0:T(128)}, u32[]{:S(2)}) copy-start(s32[2]{0:T(128)} %param.4) | copy-start | bytes 28
  6.9 5.8 %copy-start.1 = (s32[2]{0:T(128)S(1)}, s32[2]{0:T(128)}, u32[]{:S(2)}) copy-start(s32[2]{0:T(128)} %param.5) | copy-start | bytes 28
  6.9 25.6 %collective-permute-start.1 = (bf16[2,256,2048]{2,1,0:T(8,128)(2,1)S(1)}, bf16[2,256,2048]{2,1,0:T(8,128)(2,1)}, u32[]{:S(2)}, u32[]{:S(2)}) collective-permute-start(bf16[2,256,2048]{2,1,0:T(8,128)(2,1)S(1)} %piece_of.2.rest_0_), channel_id=1, source_target_pairs={{8,0},{16,8},{24,16},{0,24},{9,1},{17,9},{25,17},{1,25},{10,2},{18... | collective-permute-start | bytes 6291464 | tf_op jit(solution)/shard_map/ppermute | solution.py:45
  9.6 45.5 %collective-permute-start = (bf16[2,256,2048]{2,1,0:T(8,128)(2,1)}, bf16[2,256,2048]{2,1,0:T(8,128)(2,1)}, u32[]{:S(2)}, u32[]{:S(2)}) collective-permute-start(bf16[2,256,2048]{2,1,0:T(8,128)(2,1)} %piece_of.3), channel_id=1, source_target_pairs={{8,0},{16,8},{24,16},{0,24},{9,1},{17,9},{25,17},{1,25},{10,2},{18... | collective-permute-start | bytes 6291464 | tf_op jit(solution)/shard_map/ppermute | solution.py:45
  39.6 32.1 %collective-permute-start.8 = (bf16[2,192,2048]{2,1,0:T(8,128)(2,1)S(1)}, bf16[2,192,2048]{2,1,0:T(8,128)(2,1)S(1)}, u32[]{:S(2)}, u32[]{:S(2)}) collective-permute-start(bf16[2,192,2048]{2,1,0:T(8,128)(2,1)S(1)} %get-tuple-element.53), channel_id=1, source_target_pairs={{16,8},{0,24},{17,9},{1,25},{18,10},{2,26},{19,11},{3,27},{20,12},... | collective-permute-start | bytes 4718600 | tf_op jit(solution)/shard_map/ppermute | solution.py:45
  40.9 12.2 %collective-permute-start.3 = (bf16[4,64,512]{2,1,0:T(8,128)(2,1)S(1)}, bf16[4,64,512]{2,1,0:T(8,128)(2,1)S(1)}, u32[]{:S(2)}, u32[]{:S(2)}) collective-permute-start(bf16[4,64,512]{2,1,0:T(8,128)(2,1)S(1)} %get-tuple-element.46), channel_id=1, source_target_pairs={{0,1},{1,0},{2,3},{3,2},{4,5},{5,4},{6,7},{7,6},{8,9},{9,8},{10,11... | collective-permute-start | bytes 786440 | tf_op jit(solution)/shard_map/ppermute | solution.py:28
  51.8 3.4 %collective-permute-start.6 = (bf16[4,64,512]{2,1,0:T(8,128)(2,1)S(1)}, bf16[4,64,512]{2,1,0:T(8,128)(2,1)S(1)}, u32[]{:S(2)}, u32[]{:S(2)}) collective-permute-start(bf16[4,64,512]{2,1,0:T(8,128)(2,1)S(1)} %get-tuple-element.51), channel_id=1, source_target_pairs={{0,1},{1,0},{2,3},{3,2},{4,5},{5,4},{6,7},{7,6},{16,17},{17,16},{1... | collective-permute-start | bytes 786440 | tf_op jit(solution)/shard_map/ppermute | solution.py:31
  52.5 2.7 %collective-permute-start.5 = (bf16[4,64,512]{2,1,0:T(8,128)(2,1)S(1)}, bf16[4,64,512]{2,1,0:T(8,128)(2,1)S(1)}, u32[]{:S(2)}, u32[]{:S(2)}) collective-permute-start(bf16[4,64,512]{2,1,0:T(8,128)(2,1)S(1)} %get-tuple-element.50), channel_id=1, source_target_pairs={{0,1},{1,0},{2,3},{3,2},{4,5},{5,4},{6,7},{7,6},{16,17},{17,16},{1... | collective-permute-start | bytes 786440 | tf_op jit(solution)/shard_map/ppermute | solution.py:31
  53.8 3.9 %collective-permute-start.4 = (bf16[2,64,512]{2,1,0:T(8,128)(2,1)S(1)}, bf16[2,64,512]{2,1,0:T(8,128)(2,1)S(1)}, u32[]{:S(2)}, u32[]{:S(2)}) collective-permute-start(bf16[2,64,512]{2,1,0:T(8,128)(2,1)S(1)} %get-tuple-element.49), channel_id=1, source_target_pairs={{0,2},{1,3},{2,0},{3,1},{4,6},{5,7},{6,4},{7,5},{8,10},{9,11},{10,... | collective-permute-start | bytes 393224 | tf_op jit(solution)/shard_map/ppermute | solution.py:28
  64.8 27.7 %collective-permute-start.7 = (bf16[2,192,2048]{2,1,0:T(8,128)(2,1)S(1)}, bf16[2,192,2048]{2,1,0:T(8,128)(2,1)S(1)}, u32[]{:S(2)}, u32[]{:S(2)}) collective-permute-start(bf16[2,192,2048]{2,1,0:T(8,128)(2,1)S(1)} %get-tuple-element.52), channel_id=1, source_target_pairs={{16,8},{0,24},{17,9},{1,25},{18,10},{2,26},{19,11},{3,27},{20,12},... | collective-permute-start | bytes 4718600 | tf_op jit(solution)/shard_map/ppermute | solution.py:45
  66.2 5.3 %collective-permute-start.9 = (bf16[4,64,512]{2,1,0:T(8,128)(2,1)S(1)}, bf16[4,64,512]{2,1,0:T(8,128)(2,1)S(1)}, u32[]{:S(2)}, u32[]{:S(2)}) collective-permute-start(bf16[4,64,512]{2,1,0:T(8,128)(2,1)S(1)} %get-tuple-element.55), channel_id=1, source_target_pairs={{0,1},{1,0},{2,3},{3,2},{4,5},{5,4},{6,7},{7,6},{8,9},{9,8},{10,11... | collective-permute-start | bytes 786440 | tf_op jit(solution)/shard_map/ppermute | solution.py:28
  66.4 5.1 %collective-permute-start.10 = (bf16[2,64,1024]{2,1,0:T(8,128)(2,1)S(1)}, bf16[2,64,1024]{2,1,0:T(8,128)(2,1)S(1)}, u32[]{:S(2)}, u32[]{:S(2)}) collective-permute-start(bf16[2,64,1024]{2,1,0:T(8,128)(2,1)S(1)} %get-tuple-element.57), channel_id=1, source_target_pairs={{0,2},{1,3},{2,0},{3,1},{4,6},{5,7},{6,4},{7,5},{16,18},{17,19},{1... | collective-permute-start | bytes 786440 | tf_op jit(solution)/shard_map/ppermute | solution.py:31
  67.1 4.2 %collective-permute-start.11 = (bf16[1,64,512]{2,1,0:T(8,128)(2,1)S(1)}, bf16[1,64,512]{2,1,0:T(8,128)(2,1)S(1)}, u32[]{:S(2)}, u32[]{:S(2)}) collective-permute-start(bf16[1,64,512]{2,1,0:T(8,128)(2,1)S(1)} %get-tuple-element.59), channel_id=1, source_target_pairs={{0,4},{1,5},{2,6},{3,7},{4,0},{5,1},{6,2},{7,3},{8,12},{9,13},{10,... | collective-permute-start | bytes 196616 | tf_op jit(solution)/shard_map/ppermute | solution.py:28
  77.0 27.9 %collective-permute-start.18 = (bf16[2,128,2048]{2,1,0:T(8,128)(2,1)S(1)}, bf16[2,128,2048]{2,1,0:T(8,128)(2,1)S(1)}, u32[]{:S(2)}, u32[]{:S(2)}) collective-permute-start(bf16[2,128,2048]{2,1,0:T(8,128)(2,1)S(1)} %get-tuple-element.73), channel_id=1, source_target_pairs={{16,8},{0,24},{17,9},{1,25},{18,10},{2,26},{19,11},{3,27},{20,12},... | collective-permute-start | bytes 3145736 | tf_op jit(solution)/shard_map/ppermute | solution.py:45
  78.3 7.6 %collective-permute-start.13 = (bf16[4,64,384]{2,1,0:T(8,128)(2,1)S(1)}, bf16[4,64,384]{2,1,0:T(8,128)(2,1)S(1)}, u32[]{:S(2)}, u32[]{:S(2)}) collective-permute-start(bf16[4,64,384]{2,1,0:T(8,128)(2,1)S(1)} %get-tuple-element.63), channel_id=1, source_target_pairs={{8,9},{9,8},{10,11},{11,10},{12,13},{13,12},{14,15},{15,14},{24,25... | collective-permute-start | bytes 589832 | tf_op jit(solution)/shard_map/ppermute | solution.py:31
  82.8 7.2 %collective-permute-start.12 = (bf16[2,64,512]{2,1,0:T(8,128)(2,1)S(1)}, bf16[2,64,512]{2,1,0:T(8,128)(2,1)S(1)}, u32[]{:S(2)}, u32[]{:S(2)}) collective-permute-start(bf16[2,64,512]{2,1,0:T(8,128)(2,1)S(1)} %get-tuple-element.61), channel_id=1, source_target_pairs={{0,2},{1,3},{2,0},{3,1},{4,6},{5,7},{6,4},{7,5},{8,10},{9,11},{10,... | collective-permute-start | bytes 393224 | tf_op jit(solution)/shard_map/ppermute | solution.py:28
  84.2 5.8 %collective-permute-start.15 = (bf16[1,64,1024]{2,1,0:T(8,128)(2,1)S(1)}, bf16[1,64,1024]{2,1,0:T(8,128)(2,1)S(1)}, u32[]{:S(2)}, u32[]{:S(2)}) collective-permute-start(bf16[1,64,1024]{2,1,0:T(8,128)(2,1)S(1)} %get-tuple-element.67), channel_id=1, source_target_pairs={{0,4},{1,5},{2,6},{3,7},{4,0},{5,1},{6,2},{7,3},{16,20},{17,21},{1... | collective-permute-start | bytes 393224 | tf_op jit(solution)/shard_map/ppermute | solution.py:31
  86.5 5.5 %collective-permute-start.14 = (bf16[2,64,384]{2,1,0:T(8,128)(2,1)S(1)}, bf16[2,64,384]{2,1,0:T(8,128)(2,1)S(1)}, u32[]{:S(2)}, u32[]{:S(2)}) collective-permute-start(bf16[2,64,384]{2,1,0:T(8,128)(2,1)S(1)} %get-tuple-element.65), channel_id=1, source_target_pairs={{8,10},{9,11},{10,8},{11,9},{12,14},{13,15},{14,12},{15,13},{24,26... | collective-permute-start | bytes 294920 | tf_op jit(solution)/shard_map/ppermute | solution.py:31
  97.5 7.4 %collective-permute-start.16 = (bf16[1,64,896]{2,1,0:T(8,128)(2,1)S(1)}, bf16[1,64,896]{2,1,0:T(8,128)(2,1)S(1)}, u32[]{:S(2)}, u32[]{:S(2)}) collective-permute-start(bf16[1,64,896]{2,1,0:T(8,128)(2,1)S(1)} %get-tuple-element.70), channel_id=1, source_target_pairs={{0,4},{1,5},{2,6},{3,7},{4,0},{5,1},{6,2},{7,3},{8,12},{9,13},{10,... | collective-permute-start | bytes 344072 | tf_op jit(solution)/shard_map/ppermute | solution.py:28
  99.9 12.6 %collective-permute-start.17 = (bf16[4,64,384]{2,1,0:T(8,128)(2,1)S(1)}, bf16[4,64,384]{2,1,0:T(8,128)(2,1)S(1)}, u32[]{:S(2)}, u32[]{:S(2)}) collective-permute-start(bf16[4,64,384]{2,1,0:T(8,128)(2,1)S(1)} %get-tuple-element.72), channel_id=1, source_target_pairs={{8,9},{9,8},{10,11},{11,10},{12,13},{13,12},{14,15},{15,14},{24,25... | collective-permute-start | bytes 589832 | tf_op jit(solution)/shard_map/ppermute | solution.py:31
  108.3 5.7 %collective-permute-start.19 = (bf16[4,64,256]{2,1,0:T(8,128)(2,1)S(1)}, bf16[4,64,256]{2,1,0:T(8,128)(2,1)S(1)}, u32[]{:S(2)}, u32[]{:S(2)}) collective-permute-start(bf16[4,64,256]{2,1,0:T(8,128)(2,1)S(1)} %get-tuple-element.77.refs_2_), channel_id=1, source_target_pairs={{8,9},{9,8},{10,11},{11,10},{12,13},{13,12},{14,15},{15,14},{24,25... | collective-permute-start | bytes 393224 | tf_op jit(solution)/shard_map/ppermute | solution.py:31
  114.7 9.3 %collective-permute-start.20 = (bf16[1,64,640]{2,1,0:T(8,128)(2,1)S(1)}, bf16[1,64,640]{2,1,0:T(8,128)(2,1)S(1)}, u32[]{:S(2)}, u32[]{:S(2)}) collective-permute-start(bf16[1,64,640]{2,1,0:T(8,128)(2,1)S(1)} %get-tuple-element.79), channel_id=1, source_target_pairs={{8,10},{9,11},{10,8},{11,9},{12,14},{13,15},{14,12},{15,13},{24,26... | collective-permute-start | bytes 245768 | tf_op jit(solution)/shard_map/ppermute | solution.py:31
  117.4 7.0 %collective-permute-start.21 = (bf16[1,64,640]{2,1,0:T(8,128)(2,1)S(1)}, bf16[1,64,640]{2,1,0:T(8,128)(2,1)S(1)}, u32[]{:S(2)}, u32[]{:S(2)}) collective-permute-start(bf16[1,64,640]{2,1,0:T(8,128)(2,1)S(1)} %get-tuple-element.80), channel_id=1, source_target_pairs={{8,12},{9,13},{10,14},{11,15},{12,8},{13,9},{14,10},{15,11},{24,28... | collective-permute-start | bytes 245768 | tf_op jit(solution)/shard_map/ppermute | solution.py:31
  120.9 7.0 %collective-permute-start.22 = (bf16[1,64,640]{2,1,0:T(8,128)(2,1)S(1)}, bf16[1,64,640]{2,1,0:T(8,128)(2,1)S(1)}, u32[]{:S(2)}, u32[]{:S(2)}) collective-permute-start(bf16[1,64,640]{2,1,0:T(8,128)(2,1)S(1)} %get-tuple-element.81), channel_id=1, source_target_pairs={{8,14},{9,15},{10,12},{11,13},{12,10},{13,11},{14,8},{15,9},{24,30... | collective-permute-start | bytes 245768 | tf_op jit(solution)/shard_map/ppermute | solution.py:31

commit v14 on v12

--- a/solution.py
+++ b/solution.py
@@ -13,7 +13,7 @@
 PLANE = 1024
 STRIP = 32
 DEPTH = 512
-AHEAD = 2
+AHEAD = 3
 OUTER = 4
 SPLIT = 128
 LANES = 128

time: 120 us -> 120 us (level)
  Pallas kernels: 36.6 us -> 39.6 us
  starting transfers between devices: 31.4 us -> 29.6 us
  waiting for transfers between devices: 51.1 us -> 49.6 us
    ppermute x8, waiting for transfers between devices: 15.8 us -> 12.5 us  [swapped(): return lax.ppermute(block, axis, [(i, i ^ distance) for i in range(count)])]
    pallas_call x2 -> x3, Pallas kernels: 4.24 us -> 6.53 us  [piece_of(): pl.pallas_call(functools.partial(piece_kernel, slot, start), in_specs=[pl...]
    ppermute x10, waiting for transfers between devices: 35.2 us -> 37.1 us  [shifted(): return lax.ppermute(block, axis, route)]
    ppermute x10, starting transfers between devices: 16.8 us -> 15.1 us  [shifted(): return lax.ppermute(block, axis, route)]
  transfers between devices with their start and end apart: 18 -> 18, of which waited for: 13 -> 11; matrix products, arithmetic and copies ran while one was open for 1% -> 1% of each run, Pallas kernels for 27% -> 30%
where the time goes in v14:
time: 120 us
  waiting for transfers between devices  49.6 us (41%)
  Pallas kernels  39.6 us (33%)
  starting transfers between devices  29.6 us (25%)
    ppermute x10, waiting for transfers between devices, shifted(): return lax.ppermute(block, axis, route)  37.1 us
    pallas_call x10, Pallas kernels, step(): pl.pallas_call(functools.partial(step_kernel, plan), in_specs=in_specs, o...  33.1 us
    ppermute x10, starting transfers between devices, shifted(): return lax.ppermute(block, axis, route)  15.1 us
    ppermute x8, starting transfers between devices, swapped(): return lax.ppermute(block, axis, [(i, i ^ distance) for i in range(count)])  14.6 us
    ppermute x8, waiting for transfers between devices, swapped(): return lax.ppermute(block, axis, [(i, i ^ distance) for i in range(count)])  12.5 us
    pallas_call x3, Pallas kernels, piece_of(): pl.pallas_call(functools.partial(piece_kernel, slot, start), in_specs=[pl...  6.53 us
  transfers between devices with their start and end apart: 18, of which 11 were waited for; matrix products, arithmetic and copies ran while one was open for 1% of the time, Pallas kernels for 30%

profile of v14, /device:TPU:0, one launch (start us, length us, event | category | flops | bytes accessed | tf_op | source)
XLA Modules:
  0.0 119.8 jit_solution(11741222232944745697)
XLA Ops:
  0.0 1.6 %piece_of.3.rest_0_ = bf16[2,256,2048]{2,1,0:T(8,128)(2,1)S(1)} custom-call(bf16[2,2,512,2048]{3,2,1,0:T(8,128)(2,1)} %refs_0_.9), custom_call_target="tpu_custom_call" | custom-call | flops 1000 | bytes 1000 | tf_op jit(solution)/shard_map/piece_of/pallas_call | solution.py:64
  1.7 2.5 %collective-permute-start = (bf16[2,256,2048]{2,1,0:T(8,128)(2,1)S(1)}, bf16[2,256,2048]{2,1,0:T(8,128)(2,1)}, u32[]{:S(2)}, u32[]{:S(2)}) collective-permute-start(bf16[2,256,2048]{2,1,0:T(8,128)(2,1)S(1)} %piece_of.3.rest_0_), channel_id=1, source_target_pairs={{0,24},{8,0},{16,8},{24,16},{1,25},{9,1},{17,9},{25,17},{2,26},{10... | collective-permute-start | bytes 6291464 | tf_op jit(solution)/shard_map/ppermute | solution.py:33
  4.1 2.6 %piece_of.4.rest_0_ = bf16[2,256,2048]{2,1,0:T(8,128)(2,1)} custom-call(bf16[2,2,512,2048]{3,2,1,0:T(8,128)(2,1)} %refs_0_.9, bf16[2,256,2048]{2,1,0:T(8,128)(2,1)S(1)} %piece_of.3.rest_0_), custom_call_target="tpu_custom_call" | custom-call | flops 1000 | bytes 1000 | tf_op jit(solution)/shard_map/piece_of/pallas_call | solution.py:64
  6.7 0.7 collective-permute-start.3
  7.4 2.3 %piece_of.5 = bf16[2,192,2048]{2,1,0:T(8,128)(2,1)} custom-call(bf16[2,2,512,2048]{3,2,1,0:T(8,128)(2,1)} %refs_0_.9, bf16[2,256,2048]{2,1,0:T(8,128)(2,1)} %piece_of.4.rest_0_), custom_call_target="tpu_custom_call" | custom-call | flops 1000 | bytes 1000 | tf_op jit(solution)/shard_map/piece_of/pallas_call | solution.py:64
  9.8 0.1 collective-permute-start.2
  9.9 0.1 select_reduce_fusion.1
  10.0 0.1 fusion.4
  10.1 0.1 copy.6
  10.2 0.1 pad_maximum_fusion
  10.3 0.1 reshape.28
  10.4 0.1 pad_maximum_fusion.1.table_ref
  10.5 17.2 %collective-permute-done.refs_1_ = bf16[2,256,2048]{2,1,0:T(8,128)(2,1)} collective-permute-done((bf16[2,256,2048]{2,1,0:T(8,128)(2,1)S(1)}, bf16[2,256,2048]{2,1,0:T(8,128)(2,1)}, u32[]{:S(2)}, u32[]{:S(2)}) %collective-permute-start) | collective-permute-done | bytes 2097184 | tf_op jit(solution)/shard_map/ppermute | solution.py:33
  27.7 7.1 %step.10 = (f32[4,64,512]{2,1,0:T(8,128)S(1)}, bf16[4,64,512]{2,1,0:T(8,128)(2,1)S(1)}, bf16[2,192,2048]{2,1,0:T(8,128)(2,1)S(1)}) custom-call(f32[11]{0:T(128)S(1)} %pad_maximum_fusion.1.table_ref, bf16[2,2,512,2048]{3,2,1,0:T(8,128)(2,1)} %refs_0_.9, bf16[2,256,2048]{2,1,0:T(8,128)(2,1)} %collective-permute-done.refs_1_), custom_call_target="tpu_custom_call" | custom-call | flops 1000 | bytes 1000 | tf_op jit(solution)/shard_map/step/pallas_call | solution.py:335
  34.8 2.1 %collective-permute-start.1 = (bf16[2,192,2048]{2,1,0:T(8,128)(2,1)S(1)}, bf16[2,192,2048]{2,1,0:T(8,128)(2,1)S(1)}, u32[]{:S(2)}, u32[]{:S(2)}) collective-permute-start(bf16[2,192,2048]{2,1,0:T(8,128)(2,1)S(1)} %get-tuple-element.34), channel_id=1, source_target_pairs={{0,24},{8,0},{16,8},{24,16},{1,25},{9,1},{17,9},{25,17},{2,26},{10... | collective-permute-start | bytes 4718600 | tf_op jit(solution)/shard_map/ppermute | solution.py:33
  36.8 1.5 %collective-permute-start.4 = (bf16[4,64,512]{2,1,0:T(8,128)(2,1)S(1)}, bf16[4,64,512]{2,1,0:T(8,128)(2,1)S(1)}, u32[]{:S(2)}, u32[]{:S(2)}) collective-permute-start(bf16[4,64,512]{2,1,0:T(8,128)(2,1)S(1)} %get-tuple-element.36), channel_id=1, source_target_pairs={{0,1},{1,0},{2,3},{3,2},{4,5},{5,4},{6,7},{7,6},{8,9},{9,8},{10,11... | collective-permute-start | bytes 786440 | tf_op jit(solution)/shard_map/ppermute | solution.py:33
  38.3 5.7 %collective-permute-done.4.refs_1_ = bf16[4,64,512]{2,1,0:T(8,128)(2,1)S(1)} collective-permute-done((bf16[4,64,512]{2,1,0:T(8,128)(2,1)S(1)}, bf16[4,64,512]{2,1,0:T(8,128)(2,1)S(1)}, u32[]{:S(2)}, u32[]{:S(2)}) %collective-permute-start.4) | collective-permute-done | bytes 262176 | tf_op jit(solution)/shard_map/ppermute | solution.py:33
  44.1 0.6 step.11
  44.7 1.6 %collective-permute-start.5 = (bf16[2,64,512]{2,1,0:T(8,128)(2,1)S(1)}, bf16[2,64,512]{2,1,0:T(8,128)(2,1)S(1)}, u32[]{:S(2)}, u32[]{:S(2)}) collective-permute-start(bf16[2,64,512]{2,1,0:T(8,128)(2,1)S(1)} %get-tuple-element.38), channel_id=1, source_target_pairs={{0,2},{1,3},{2,0},{3,1},{4,6},{5,7},{6,4},{7,5},{8,10},{9,11},{10,... | collective-permute-start | bytes 393224 | tf_op jit(solution)/shard_map/ppermute | solution.py:38
  46.3 3.9 %collective-permute-done.3.refs_1_ = bf16[2,256,2048]{2,1,0:T(8,128)(2,1)} collective-permute-done((bf16[2,256,2048]{2,1,0:T(8,128)(2,1)}, bf16[2,256,2048]{2,1,0:T(8,128)(2,1)}, u32[]{:S(2)}, u32[]{:S(2)}) %collective-permute-start.3) | collective-permute-done | bytes 2097184 | tf_op jit(solution)/shard_map/ppermute | solution.py:33
  50.2 7.1 %step.12 = (f32[4,64,512]{2,1,0:T(8,128)S(1)}, bf16[4,64,512]{2,1,0:T(8,128)(2,1)S(1)}, f32[1,64,512]{2,1,0:T(8,128)S(1)}, bf16[1,64,512]{2,1,0:T(8,128)(2,1)S(1)}, bf16[2,128,2048]{2,1,0:T(8,128)(2,1)S(1)}) custom-call(f32[11]{0:T(128)S(1)} %pad_maximum_fusion.1.table_ref, bf16[2,2,512,2048]{3,2,1,0:T(8,128)(2,1)} %refs_0_.9, ...), custom_call_target="tpu_custom_call" | custom-call | flops 1000 | bytes 1000 | tf_op jit(solution)/shard_map/step/pallas_call | solution.py:335
  57.3 2.2 %collective-permute-start.13 = (bf16[2,128,2048]{2,1,0:T(8,128)(2,1)S(1)}, bf16[2,128,2048]{2,1,0:T(8,128)(2,1)S(1)}, u32[]{:S(2)}, u32[]{:S(2)}) collective-permute-start(bf16[2,128,2048]{2,1,0:T(8,128)(2,1)S(1)} %get-tuple-element.53), channel_id=1, source_target_pairs={{0,24},{8,0},{16,8},{24,16},{1,25},{9,1},{17,9},{25,17},{2,26},{10... | collective-permute-start | bytes 3145736 | tf_op jit(solution)/shard_map/ppermute | solution.py:33
  59.5 1.4 %collective-permute-start.6 = (bf16[4,64,512]{2,1,0:T(8,128)(2,1)S(1)}, bf16[4,64,512]{2,1,0:T(8,128)(2,1)S(1)}, u32[]{:S(2)}, u32[]{:S(2)}) collective-permute-start(bf16[4,64,512]{2,1,0:T(8,128)(2,1)S(1)} %get-tuple-element.40), channel_id=1, source_target_pairs={{0,1},{1,0},{2,3},{3,2},{4,5},{5,4},{6,7},{7,6},{8,9},{9,8},{10,11... | collective-permute-start | bytes 786440 | tf_op jit(solution)/shard_map/ppermute | solution.py:33
  61.0 2.6 %collective-permute-start.7 = (bf16[1,64,512]{2,1,0:T(8,128)(2,1)S(1)}, bf16[1,64,512]{2,1,0:T(8,128)(2,1)S(1)}, u32[]{:S(2)}, u32[]{:S(2)}) collective-permute-start(bf16[1,64,512]{2,1,0:T(8,128)(2,1)S(1)} %get-tuple-element.42), channel_id=1, source_target_pairs={{0,4},{1,5},{2,6},{3,7},{4,0},{5,1},{6,2},{7,3},{8,12},{9,13},{10,... | collective-permute-start | bytes 196616 | tf_op jit(solution)/shard_map/ppermute | solution.py:38
  63.5 3.6 %collective-permute-done.2.refs_1_ = bf16[2,192,2048]{2,1,0:T(8,128)(2,1)} collective-permute-done((bf16[2,192,2048]{2,1,0:T(8,128)(2,1)}, bf16[2,192,2048]{2,1,0:T(8,128)(2,1)}, u32[]{:S(2)}, u32[]{:S(2)}) %collective-permute-start.2) | collective-permute-done | bytes 1572896 | tf_op jit(solution)/shard_map/ppermute | solution.py:33
  67.1 6.0 %step.13 = (f32[4,64,384]{2,1,0:T(8,128)S(1)}, bf16[4,64,384]{2,1,0:T(8,128)(2,1)S(1)}, f32[2,64,512]{2,1,0:T(8,128)S(1)}, bf16[2,64,512]{2,1,0:T(8,128)(2,1)S(1)}, f32[64,2,2,512]{3,2,1,0:T(2,128)}) custom-call(f32[11]{0:T(128)S(1)} %pad_maximum_fusion.1.table_ref, bf16[2,2,512,2048]{3,2,1,0:T(8,128)(2,1)} %refs_0_.9, ...), custom_call_target="tpu_custom_call" | custom-call | flops 1000 | bytes 1000 | tf_op jit(solution)/shard_map/step/pallas_call | solution.py:335
  73.1 1.6 %collective-permute-start.9 = (bf16[4,64,384]{2,1,0:T(8,128)(2,1)S(1)}, bf16[4,64,384]{2,1,0:T(8,128)(2,1)S(1)}, u32[]{:S(2)}, u32[]{:S(2)}) collective-permute-start(bf16[4,64,384]{2,1,0:T(8,128)(2,1)S(1)} %get-tuple-element.46), channel_id=1, source_target_pairs={{0,1},{1,0},{2,3},{3,2},{4,5},{5,4},{6,7},{7,6},{8,9},{9,8},{10,11... | collective-permute-start | bytes 589832 | tf_op jit(solution)/shard_map/ppermute | solution.py:33
  74.6 1.6 %collective-permute-start.8 = (bf16[2,64,512]{2,1,0:T(8,128)(2,1)S(1)}, bf16[2,64,512]{2,1,0:T(8,128)(2,1)S(1)}, u32[]{:S(2)}, u32[]{:S(2)}) collective-permute-start(bf16[2,64,512]{2,1,0:T(8,128)(2,1)S(1)} %get-tuple-element.44), channel_id=1, source_target_pairs={{0,2},{1,3},{2,0},{3,1},{4,6},{5,7},{6,4},{7,5},{8,10},{9,11},{10,... | collective-permute-start | bytes 393224 | tf_op jit(solution)/shard_map/ppermute | solution.py:38
  76.2 4.6 %collective-permute-done.9.refs_1_ = bf16[4,64,384]{2,1,0:T(8,128)(2,1)S(1)} collective-permute-done((bf16[4,64,384]{2,1,0:T(8,128)(2,1)S(1)}, bf16[4,64,384]{2,1,0:T(8,128)(2,1)S(1)}, u32[]{:S(2)}, u32[]{:S(2)}) %collective-permute-start.9) | collective-permute-done | bytes 196640 | tf_op jit(solution)/shard_map/ppermute | solution.py:33
  80.8 0.6 step.14
  81.4 1.6 %collective-permute-start.10 = (bf16[2,64,384]{2,1,0:T(8,128)(2,1)S(1)}, bf16[2,64,384]{2,1,0:T(8,128)(2,1)S(1)}, u32[]{:S(2)}, u32[]{:S(2)}) collective-permute-start(bf16[2,64,384]{2,1,0:T(8,128)(2,1)S(1)} %get-tuple-element.48), channel_id=1, source_target_pairs={{0,2},{1,3},{2,0},{3,1},{4,6},{5,7},{6,4},{7,5},{8,10},{9,11},{10,... | collective-permute-start | bytes 294920 | tf_op jit(solution)/shard_map/ppermute | solution.py:38
  83.0 3.1 %collective-permute-done.10.refs_5_ = bf16[2,64,384]{2,1,0:T(8,128)(2,1)S(1)} collective-permute-done((bf16[2,64,384]{2,1,0:T(8,128)(2,1)S(1)}, bf16[2,64,384]{2,1,0:T(8,128)(2,1)S(1)}, u32[]{:S(2)}, u32[]{:S(2)}) %collective-permute-start.10) | collective-permute-done | bytes 98336 | tf_op jit(solution)/shard_map/ppermute | solution.py:38
  86.1 5.0 %step.15 = (f32[4,64,384]{2,1,0:T(8,128)S(1)}, bf16[4,64,384]{2,1,0:T(8,128)(2,1)S(1)}, f32[1,64,896]{2,1,0:T(8,128)S(1)}, bf16[1,64,896]{2,1,0:T(8,128)(2,1)S(1)}) custom-call(f32[11]{0:T(128)S(1)} %pad_maximum_fusion.1.table_ref, bf16[2,2,512,2048]{3,2,1,0:T(8,128)(2,1)} %refs_0_.9, bf16[2,192,2048]{2,1,0:T(8,128)(2,1)S(1)} %collective-permute-done.1.refs_1_, ...), custom_call_target="tpu_custom_call" | custom-call | flops 1000 | bytes 1000 | tf_op jit(solution)/shard_map/step/pallas_call | solution.py:335
  91.2 2.7 %collective-permute-start.11 = (bf16[1,64,896]{2,1,0:T(8,128)(2,1)S(1)}, bf16[1,64,896]{2,1,0:T(8,128)(2,1)S(1)}, u32[]{:S(2)}, u32[]{:S(2)}) collective-permute-start(bf16[1,64,896]{2,1,0:T(8,128)(2,1)S(1)} %get-tuple-element.50), channel_id=1, source_target_pairs={{0,4},{1,5},{2,6},{3,7},{4,0},{5,1},{6,2},{7,3},{8,12},{9,13},{10,... | collective-permute-start | bytes 344072 | tf_op jit(solution)/shard_map/ppermute | solution.py:38
  93.8 1.5 %collective-permute-start.12 = (bf16[4,64,384]{2,1,0:T(8,128)(2,1)S(1)}, bf16[4,64,384]{2,1,0:T(8,128)(2,1)S(1)}, u32[]{:S(2)}, u32[]{:S(2)}) collective-permute-start(bf16[4,64,384]{2,1,0:T(8,128)(2,1)S(1)} %get-tuple-element.52), channel_id=1, source_target_pairs={{0,1},{1,0},{2,3},{3,2},{4,5},{5,4},{6,7},{7,6},{8,9},{9,8},{10,11... | collective-permute-start | bytes 589832 | tf_op jit(solution)/shard_map/ppermute | solution.py:33
  95.3 3.5 %collective-permute-done.11.refs_3_.refs_1_ = bf16[1,64,896]{2,1,0:T(8,128)(2,1)S(1)} collective-permute-done((bf16[1,64,896]{2,1,0:T(8,128)(2,1)S(1)}, bf16[1,64,896]{2,1,0:T(8,128)(2,1)S(1)}, u32[]{:S(2)}, u32[]{:S(2)}) %collective-permute-start.11) | collective-permute-done | bytes 114720 | tf_op jit(solution)/shard_map/ppermute | solution.py:38
  98.8 3.4 %step.16 = (bf16[256,2048]{1,0:T(8,128)(2,1)S(1)}, bf16[2,256,2048]{2,1,0:T(8,128)(2,1)S(1)}, bf16[4,64,256]{2,1,0:T(8,128)(2,1)S(1)}, f32[64,2,2,512]{3,2,1,0:T(2,128)}) custom-call(f32[11]{0:T(128)S(1)} %pad_maximum_fusion.1.table_ref, bf16[2,2,512,2048]{3,2,1,0:T(8,128)(2,1)} %refs_0_.9, ...), custom_call_target="tpu_custom_call", output_to_operand_aliasing={{3}: (5, {})} | custom-call | flops 1000 | bytes 1000 | tf_op jit(solution)/shard_map/step/pallas_call | solution.py:335
  102.2 1.6 %collective-permute-start.14 = (bf16[4,64,256]{2,1,0:T(8,128)(2,1)S(1)}, bf16[4,64,256]{2,1,0:T(8,128)(2,1)S(1)}, u32[]{:S(2)}, u32[]{:S(2)}) collective-permute-start(bf16[4,64,256]{2,1,0:T(8,128)(2,1)S(1)} %get-tuple-element.57), channel_id=1, source_target_pairs={{0,1},{1,0},{2,3},{3,2},{4,5},{5,4},{6,7},{7,6},{8,9},{9,8},{10,11... | collective-permute-start | bytes 393224 | tf_op jit(solution)/shard_map/ppermute | solution.py:33
  103.8 1.3 %step.17.refs_2_ = f32[4,64,256]{2,1,0:T(8,128)S(1)} custom-call(f32[11]{0:T(128)S(1)} %pad_maximum_fusion.1.table_ref, bf16[2,256,2048]{2,1,0:T(8,128)(2,1)S(1)} %get-tuple-element.55.refs_0_, bf16[256,2048]{1,0:T(8,128)(2,1)S(1)} %get-tuple-element.56.refs_1_), custom_call_target="tpu_custom_call" | custom-call | flops 1000 | bytes 1000 | tf_op jit(solution)/shard_map/step/pallas_call | solution.py:335
  105.1 2.2 %collective-permute-done.14.refs_3_ = bf16[4,64,256]{2,1,0:T(8,128)(2,1)S(1)} collective-permute-done((bf16[4,64,256]{2,1,0:T(8,128)(2,1)S(1)}, bf16[4,64,256]{2,1,0:T(8,128)(2,1)S(1)}, u32[]{:S(2)}, u32[]{:S(2)}) %collective-permute-start.14) | collective-permute-done | bytes 131104 | tf_op jit(solution)/shard_map/ppermute | solution.py:33
  107.2 0.6 step.18
  107.8 0.7 collective-permute-start.15
  108.6 3.4 %collective-permute-start.16 = (bf16[1,64,640]{2,1,0:T(8,128)(2,1)S(1)}, bf16[1,64,640]{2,1,0:T(8,128)(2,1)S(1)}, u32[]{:S(2)}, u32[]{:S(2)}) collective-permute-start(bf16[1,64,640]{2,1,0:T(8,128)(2,1)S(1)} %get-tuple-element.60), channel_id=1, source_target_pairs={{0,4},{1,5},{2,6},{3,7},{4,0},{5,1},{6,2},{7,3},{8,12},{9,13},{10,... | collective-permute-start | bytes 245768 | tf_op jit(solution)/shard_map/ppermute | solution.py:38
  112.0 0.3 collective-permute-start.17
  112.3 0.1 collective-permute-done.15.refs_3_
  112.4 3.8 %collective-permute-done.16.refs_4_ = bf16[1,64,640]{2,1,0:T(8,128)(2,1)S(1)} collective-permute-done((bf16[1,64,640]{2,1,0:T(8,128)(2,1)S(1)}, bf16[1,64,640]{2,1,0:T(8,128)(2,1)S(1)}, u32[]{:S(2)}, u32[]{:S(2)}) %collective-permute-start.16) | collective-permute-done | bytes 81952 | tf_op jit(solution)/shard_map/ppermute | solution.py:38
  116.1 2.1 %collective-permute-done.17.refs_5_ = bf16[1,64,640]{2,1,0:T(8,128)(2,1)S(1)} collective-permute-done((bf16[1,64,640]{2,1,0:T(8,128)(2,1)S(1)}, bf16[1,64,640]{2,1,0:T(8,128)(2,1)S(1)}, u32[]{:S(2)}, u32[]{:S(2)}) %collective-permute-start.17) | collective-permute-done | bytes 81952 | tf_op jit(solution)/shard_map/ppermute | solution.py:38
  118.2 1.5 %step.19 = f32[64,2,2,512]{3,2,1,0:T(2,128)} custom-call(f32[11]{0:T(128)S(1)} %pad_maximum_fusion.1.table_ref, f32[1,64,896]{2,1,0:T(8,128)S(1)} %get-tuple-element.49.refs_2_.refs_0_, bf16[1,64,896]{2,1,0:T(8,128)(2,1)S(1)} %collective-permute-done.11.refs_3_.refs_1_, f32[1,64,640]{2,1,0:T(8,128)S(1)} %get-tuple-element.58.refs_2_, ...), custom_call_target="tpu_custom_call", output_to_operand_aliasing={{}: (7, {})} | custom-call | flops 1000 | bytes 1000 | tf_op jit(solution)/shard_map/step/pallas_call | solution.py:335
  (13 shorter events, 0.0 us)
Async XLA Ops:
  1.7 26.0 %collective-permute-start = (bf16[2,256,2048]{2,1,0:T(8,128)(2,1)S(1)}, bf16[2,256,2048]{2,1,0:T(8,128)(2,1)}, u32[]{:S(2)}, u32[]{:S(2)}) collective-permute-start(bf16[2,256,2048]{2,1,0:T(8,128)(2,1)S(1)} %piece_of.3.rest_0_), channel_id=1, source_target_pairs={{0,24},{8,0},{16,8},{24,16},{1,25},{9,1},{17,9},{25,17},{2,26},{10... | collective-permute-start | bytes 6291464 | tf_op jit(solution)/shard_map/ppermute | solution.py:33
  6.7 3.2 %copy-start = (s32[2]{0:T(128)S(1)}, s32[2]{0:T(128)}, u32[]{:S(2)}) copy-start(s32[2]{0:T(128)} %param.4) | copy-start | bytes 28
  6.7 3.1 %copy-start.1 = (s32[2]{0:T(128)S(1)}, s32[2]{0:T(128)}, u32[]{:S(2)}) copy-start(s32[2]{0:T(128)} %param.5) | copy-start | bytes 28
  6.7 43.5 %collective-permute-start.3 = (bf16[2,256,2048]{2,1,0:T(8,128)(2,1)}, bf16[2,256,2048]{2,1,0:T(8,128)(2,1)}, u32[]{:S(2)}, u32[]{:S(2)}) collective-permute-start(bf16[2,256,2048]{2,1,0:T(8,128)(2,1)} %piece_of.4.rest_0_), channel_id=1, source_target_pairs={{0,24},{8,0},{16,8},{24,16},{1,25},{9,1},{17,9},{25,17},{2,26},{10... | collective-permute-start | bytes 6291464 | tf_op jit(solution)/shard_map/ppermute | solution.py:33
  9.8 57.3 %collective-permute-start.2 = (bf16[2,192,2048]{2,1,0:T(8,128)(2,1)}, bf16[2,192,2048]{2,1,0:T(8,128)(2,1)}, u32[]{:S(2)}, u32[]{:S(2)}) collective-permute-start(bf16[2,192,2048]{2,1,0:T(8,128)(2,1)} %piece_of.5), channel_id=1, source_target_pairs={{0,24},{8,0},{16,8},{24,16},{1,25},{9,1},{17,9},{25,17},{2,26},{10... | collective-permute-start | bytes 4718600 | tf_op jit(solution)/shard_map/ppermute | solution.py:33
  34.8 51.4 %collective-permute-start.1 = (bf16[2,192,2048]{2,1,0:T(8,128)(2,1)S(1)}, bf16[2,192,2048]{2,1,0:T(8,128)(2,1)S(1)}, u32[]{:S(2)}, u32[]{:S(2)}) collective-permute-start(bf16[2,192,2048]{2,1,0:T(8,128)(2,1)S(1)} %get-tuple-element.34), channel_id=1, source_target_pairs={{0,24},{8,0},{16,8},{24,16},{1,25},{9,1},{17,9},{25,17},{2,26},{10... | collective-permute-start | bytes 4718600 | tf_op jit(solution)/shard_map/ppermute | solution.py:33
  36.8 7.2 %collective-permute-start.4 = (bf16[4,64,512]{2,1,0:T(8,128)(2,1)S(1)}, bf16[4,64,512]{2,1,0:T(8,128)(2,1)S(1)}, u32[]{:S(2)}, u32[]{:S(2)}) collective-permute-start(bf16[4,64,512]{2,1,0:T(8,128)(2,1)S(1)} %get-tuple-element.36), channel_id=1, source_target_pairs={{0,1},{1,0},{2,3},{3,2},{4,5},{5,4},{6,7},{7,6},{8,9},{9,8},{10,11... | collective-permute-start | bytes 786440 | tf_op jit(solution)/shard_map/ppermute | solution.py:33
  44.7 5.6 %collective-permute-start.5 = (bf16[2,64,512]{2,1,0:T(8,128)(2,1)S(1)}, bf16[2,64,512]{2,1,0:T(8,128)(2,1)S(1)}, u32[]{:S(2)}, u32[]{:S(2)}) collective-permute-start(bf16[2,64,512]{2,1,0:T(8,128)(2,1)S(1)} %get-tuple-element.38), channel_id=1, source_target_pairs={{0,2},{1,3},{2,0},{3,1},{4,6},{5,7},{6,4},{7,5},{8,10},{9,11},{10,... | collective-permute-start | bytes 393224 | tf_op jit(solution)/shard_map/ppermute | solution.py:38
  57.3 38.0 %collective-permute-start.13 = (bf16[2,128,2048]{2,1,0:T(8,128)(2,1)S(1)}, bf16[2,128,2048]{2,1,0:T(8,128)(2,1)S(1)}, u32[]{:S(2)}, u32[]{:S(2)}) collective-permute-start(bf16[2,128,2048]{2,1,0:T(8,128)(2,1)S(1)} %get-tuple-element.53), channel_id=1, source_target_pairs={{0,24},{8,0},{16,8},{24,16},{1,25},{9,1},{17,9},{25,17},{2,26},{10... | collective-permute-start | bytes 3145736 | tf_op jit(solution)/shard_map/ppermute | solution.py:33
  59.5 7.6 %collective-permute-start.6 = (bf16[4,64,512]{2,1,0:T(8,128)(2,1)S(1)}, bf16[4,64,512]{2,1,0:T(8,128)(2,1)S(1)}, u32[]{:S(2)}, u32[]{:S(2)}) collective-permute-start(bf16[4,64,512]{2,1,0:T(8,128)(2,1)S(1)} %get-tuple-element.40), channel_id=1, source_target_pairs={{0,1},{1,0},{2,3},{3,2},{4,5},{5,4},{6,7},{7,6},{8,9},{9,8},{10,11... | collective-permute-start | bytes 786440 | tf_op jit(solution)/shard_map/ppermute | solution.py:33
  61.0 6.1 %collective-permute-start.7 = (bf16[1,64,512]{2,1,0:T(8,128)(2,1)S(1)}, bf16[1,64,512]{2,1,0:T(8,128)(2,1)S(1)}, u32[]{:S(2)}, u32[]{:S(2)}) collective-permute-start(bf16[1,64,512]{2,1,0:T(8,128)(2,1)S(1)} %get-tuple-element.42), channel_id=1, source_target_pairs={{0,4},{1,5},{2,6},{3,7},{4,0},{5,1},{6,2},{7,3},{8,12},{9,13},{10,... | collective-permute-start | bytes 196616 | tf_op jit(solution)/shard_map/ppermute | solution.py:38
  73.1 7.7 %collective-permute-start.9 = (bf16[4,64,384]{2,1,0:T(8,128)(2,1)S(1)}, bf16[4,64,384]{2,1,0:T(8,128)(2,1)S(1)}, u32[]{:S(2)}, u32[]{:S(2)}) collective-permute-start(bf16[4,64,384]{2,1,0:T(8,128)(2,1)S(1)} %get-tuple-element.46), channel_id=1, source_target_pairs={{0,1},{1,0},{2,3},{3,2},{4,5},{5,4},{6,7},{7,6},{8,9},{9,8},{10,11... | collective-permute-start | bytes 589832 | tf_op jit(solution)/shard_map/ppermute | solution.py:33
  74.6 8.4 %collective-permute-start.8 = (bf16[2,64,512]{2,1,0:T(8,128)(2,1)S(1)}, bf16[2,64,512]{2,1,0:T(8,128)(2,1)S(1)}, u32[]{:S(2)}, u32[]{:S(2)}) collective-permute-start(bf16[2,64,512]{2,1,0:T(8,128)(2,1)S(1)} %get-tuple-element.44), channel_id=1, source_target_pairs={{0,2},{1,3},{2,0},{3,1},{4,6},{5,7},{6,4},{7,5},{8,10},{9,11},{10,... | collective-permute-start | bytes 393224 | tf_op jit(solution)/shard_map/ppermute | solution.py:38
  81.4 4.7 %collective-permute-start.10 = (bf16[2,64,384]{2,1,0:T(8,128)(2,1)S(1)}, bf16[2,64,384]{2,1,0:T(8,128)(2,1)S(1)}, u32[]{:S(2)}, u32[]{:S(2)}) collective-permute-start(bf16[2,64,384]{2,1,0:T(8,128)(2,1)S(1)} %get-tuple-element.48), channel_id=1, source_target_pairs={{0,2},{1,3},{2,0},{3,1},{4,6},{5,7},{6,4},{7,5},{8,10},{9,11},{10,... | collective-permute-start | bytes 294920 | tf_op jit(solution)/shard_map/ppermute | solution.py:38
  91.2 7.6 %collective-permute-start.11 = (bf16[1,64,896]{2,1,0:T(8,128)(2,1)S(1)}, bf16[1,64,896]{2,1,0:T(8,128)(2,1)S(1)}, u32[]{:S(2)}, u32[]{:S(2)}) collective-permute-start(bf16[1,64,896]{2,1,0:T(8,128)(2,1)S(1)} %get-tuple-element.50), channel_id=1, source_target_pairs={{0,4},{1,5},{2,6},{3,7},{4,0},{5,1},{6,2},{7,3},{8,12},{9,13},{10,... | collective-permute-start | bytes 344072 | tf_op jit(solution)/shard_map/ppermute | solution.py:38
  93.8 11.2 %collective-permute-start.12 = (bf16[4,64,384]{2,1,0:T(8,128)(2,1)S(1)}, bf16[4,64,384]{2,1,0:T(8,128)(2,1)S(1)}, u32[]{:S(2)}, u32[]{:S(2)}) collective-permute-start(bf16[4,64,384]{2,1,0:T(8,128)(2,1)S(1)} %get-tuple-element.52), channel_id=1, source_target_pairs={{0,1},{1,0},{2,3},{3,2},{4,5},{5,4},{6,7},{7,6},{8,9},{9,8},{10,11... | collective-permute-start | bytes 589832 | tf_op jit(solution)/shard_map/ppermute | solution.py:33
  102.2 5.0 %collective-permute-start.14 = (bf16[4,64,256]{2,1,0:T(8,128)(2,1)S(1)}, bf16[4,64,256]{2,1,0:T(8,128)(2,1)S(1)}, u32[]{:S(2)}, u32[]{:S(2)}) collective-permute-start(bf16[4,64,256]{2,1,0:T(8,128)(2,1)S(1)} %get-tuple-element.57), channel_id=1, source_target_pairs={{0,1},{1,0},{2,3},{3,2},{4,5},{5,4},{6,7},{7,6},{8,9},{9,8},{10,11... | collective-permute-start | bytes 393224 | tf_op jit(solution)/shard_map/ppermute | solution.py:33
  107.8 4.5 %collective-permute-start.15 = (bf16[1,64,640]{2,1,0:T(8,128)(2,1)S(1)}, bf16[1,64,640]{2,1,0:T(8,128)(2,1)S(1)}, u32[]{:S(2)}, u32[]{:S(2)}) collective-permute-start(bf16[1,64,640]{2,1,0:T(8,128)(2,1)S(1)} %get-tuple-element.59), channel_id=1, source_target_pairs={{0,2},{1,3},{2,0},{3,1},{4,6},{5,7},{6,4},{7,5},{8,10},{9,11},{10,... | collective-permute-start | bytes 245768 | tf_op jit(solution)/shard_map/ppermute | solution.py:38
  108.6 7.6 %collective-permute-start.16 = (bf16[1,64,640]{2,1,0:T(8,128)(2,1)S(1)}, bf16[1,64,640]{2,1,0:T(8,128)(2,1)S(1)}, u32[]{:S(2)}, u32[]{:S(2)}) collective-permute-start(bf16[1,64,640]{2,1,0:T(8,128)(2,1)S(1)} %get-tuple-element.60), channel_id=1, source_target_pairs={{0,4},{1,5},{2,6},{3,7},{4,0},{5,1},{6,2},{7,3},{8,12},{9,13},{10,... | collective-permute-start | bytes 245768 | tf_op jit(solution)/shard_map/ppermute | solution.py:38
  112.0 6.2 %collective-permute-start.17 = (bf16[1,64,640]{2,1,0:T(8,128)(2,1)S(1)}, bf16[1,64,640]{2,1,0:T(8,128)(2,1)S(1)}, u32[]{:S(2)}, u32[]{:S(2)}) collective-permute-start(bf16[1,64,640]{2,1,0:T(8,128)(2,1)S(1)} %get-tuple-element.61), channel_id=1, source_target_pairs={{0,6},{1,7},{2,4},{3,5},{4,2},{5,3},{6,0},{7,1},{8,14},{9,15},{10,... | collective-permute-start | bytes 245768 | tf_op jit(solution)/shard_map/ppermute | solution.py:38

commit v15 on v14

--- a/solution.py
+++ b/solution.py
@@ -18,7 +18,7 @@
 SPLIT = 128
 LANES = 128
 BLOCK = 256
-VMEM_BYTES = 48 * 1024 * 1024
+VMEM_BYTES = 46 * 1024 * 1024
 
 
 def shifted(block, axis, distance, fold=1, inner=False):
@@ -377,18 +377,21 @@
         if crossed:
             tasks.append(Task(tuple(crossed), 0, False, fold, 2))
         waiting += halved
-        if index == count - 1:
+        if index >= count - 3:
             kernels.append((part, others, "give", tuple(tasks), ready))
             kernels.append((part, every[:1], "use", (), ()))
         else:
             kernels.append((part, every, "make", tuple(tasks), ready))
-        halved, crossed = crossed, [part] if index < count - 2 else []
+        halved, crossed = crossed, [part] if index < count - 1 else []
         if index in (0, count - 3):
             kernels.append((None, (), "", (Task((part,), 0, False, fold, 2),), ()))
             halved, crossed = halved + crossed, []
-    last = tuple(parts[-2:])
-    kernels.append((None, (), "", (Task(last, 0, True, fold, depth),), ()))
-    kernels.append((None, (), "", (), tuple(waiting) + last))
+    tasks = (
+        Task((parts[-1],), 0, True, fold, depth),
+        Task(tuple(halved), 1, False, 2, 2),
+    )
+    kernels.append((None, (), "", tasks, ()))
+    kernels.append((None, (), "", (), tuple(waiting) + tuple(halved) + (parts[-1],)))
     return kernels
 
 
@@ -436,7 +439,7 @@
     near, result = None, None
     for part, ways, phase, tasks, adds in schedule(parts, fold, depth):
         place = parts.index(part) if part else len(parts)
-        later = parts[place + AHEAD] if place + AHEAD < len(parts) else None
+        later = parts[place + AHEAD] if place + AHEAD < len(parts) and phase != "use" else None
         sources = [[array for done in task.batch for array in held[(done,)]] for task in tasks]
         batches, pieces = [], []
         for done in adds:

time: 120 us -> 119 us (level)
  waiting for transfers between devices: 49.6 us -> 46.1 us
  starting transfers between devices: 29.6 us -> 31.5 us
    ppermute x10, waiting for transfers between devices: 37.1 us -> 34.1 us  [shifted(): return lax.ppermute(block, axis, route)]
    ppermute x8 -> x10, starting transfers between devices: 14.6 us -> 17.5 us  [swapped(): return lax.ppermute(block, axis, [(i, i ^ distance) for i in range(count)])]
    pallas_call x10 -> x12, Pallas kernels: 33.1 us -> 33.8 us  [step(): pl.pallas_call(functools.partial(step_kernel, plan), in_specs=in_specs, o...]
    ppermute x8 -> x10, waiting for transfers between devices: 12.5 us -> 12 us  [swapped(): return lax.ppermute(block, axis, [(i, i ^ distance) for i in range(count)])]
  transfers between devices with their start and end apart: 18 -> 20, of which waited for: 11 -> 11; matrix products, arithmetic and copies ran while one was open for 1% -> 1% of each run, Pallas kernels for 30% -> 28%
where the time goes in v15:
time: 119 us
  waiting for transfers between devices  46.1 us (39%)
  Pallas kernels  40.3 us (34%)
  starting transfers between devices  31.5 us (26%)
    ppermute x10, waiting for transfers between devices, shifted(): return lax.ppermute(block, axis, route)  34.1 us
    pallas_call x12, Pallas kernels, step(): pl.pallas_call(functools.partial(step_kernel, plan), in_specs=in_specs, o...  33.8 us
    ppermute x10, starting transfers between devices, swapped(): return lax.ppermute(block, axis, [(i, i ^ distance) for i in range(count)])  17.5 us
    ppermute x10, starting transfers between devices, shifted(): return lax.ppermute(block, axis, route)  14.1 us
    ppermute x10, waiting for transfers between devices, swapped(): return lax.ppermute(block, axis, [(i, i ^ distance) for i in range(count)])  12 us
    pallas_call x3, Pallas kernels, piece_of(): pl.pallas_call(functools.partial(piece_kernel, slot, start), in_specs=[pl...  6.51 us
  transfers between devices with their start and end apart: 20, of which 11 were waited for; matrix products, arithmetic and copies ran while one was open for 1% of the time, Pallas kernels for 28%

profile of v15, /device:TPU:0, one launch (start us, length us, event | category | flops | bytes accessed | tf_op | source)
XLA Modules:
  0.0 118.9 jit_solution(15289511671866394450)
XLA Ops:
  0.0 1.6 %piece_of.3.rest_0_ = bf16[2,256,2048]{2,1,0:T(8,128)(2,1)S(1)} custom-call(bf16[2,2,512,2048]{3,2,1,0:T(8,128)(2,1)} %refs_0_.9), custom_call_target="tpu_custom_call" | custom-call | flops 1000 | bytes 1000 | tf_op jit(solution)/shard_map/piece_of/pallas_call | solution.py:64
  1.7 2.5 %collective-permute-start = (bf16[2,256,2048]{2,1,0:T(8,128)(2,1)S(1)}, bf16[2,256,2048]{2,1,0:T(8,128)(2,1)}, u32[]{:S(2)}, u32[]{:S(2)}) collective-permute-start(bf16[2,256,2048]{2,1,0:T(8,128)(2,1)S(1)} %piece_of.3.rest_0_), channel_id=1, source_target_pairs={{0,24},{8,0},{16,8},{24,16},{1,25},{9,1},{17,9},{25,17},{2,26},{10... | collective-permute-start | bytes 6291464 | tf_op jit(solution)/shard_map/ppermute | solution.py:33
  4.1 2.6 %piece_of.4.rest_0_ = bf16[2,256,2048]{2,1,0:T(8,128)(2,1)} custom-call(bf16[2,2,512,2048]{3,2,1,0:T(8,128)(2,1)} %refs_0_.9, bf16[2,256,2048]{2,1,0:T(8,128)(2,1)S(1)} %piece_of.3.rest_0_), custom_call_target="tpu_custom_call" | custom-call | flops 1000 | bytes 1000 | tf_op jit(solution)/shard_map/piece_of/pallas_call | solution.py:64
  6.7 0.7 collective-permute-start.3
  7.4 2.3 %piece_of.5 = bf16[2,192,2048]{2,1,0:T(8,128)(2,1)} custom-call(bf16[2,2,512,2048]{3,2,1,0:T(8,128)(2,1)} %refs_0_.9, bf16[2,256,2048]{2,1,0:T(8,128)(2,1)} %piece_of.4.rest_0_), custom_call_target="tpu_custom_call" | custom-call | flops 1000 | bytes 1000 | tf_op jit(solution)/shard_map/piece_of/pallas_call | solution.py:64
  9.8 0.1 select_reduce_fusion.1
  10.0 0.1 fusion.4
  10.1 0.1 copy.6
  10.3 0.1 reshape.28
  10.5 17.2 %collective-permute-done.refs_1_ = bf16[2,256,2048]{2,1,0:T(8,128)(2,1)} collective-permute-done((bf16[2,256,2048]{2,1,0:T(8,128)(2,1)S(1)}, bf16[2,256,2048]{2,1,0:T(8,128)(2,1)}, u32[]{:S(2)}, u32[]{:S(2)}) %collective-permute-start) | collective-permute-done | bytes 2097184 | tf_op jit(solution)/shard_map/ppermute | solution.py:33
  27.7 7.1 %step.12 = (f32[4,64,512]{2,1,0:T(8,128)S(1)}, bf16[4,64,512]{2,1,0:T(8,128)(2,1)S(1)}, bf16[2,192,2048]{2,1,0:T(8,128)(2,1)S(1)}) custom-call(f32[11]{0:T(128)S(1)} %pad_maximum_fusion.1.table_ref, bf16[2,2,512,2048]{3,2,1,0:T(8,128)(2,1)} %refs_0_.9, bf16[2,256,2048]{2,1,0:T(8,128)(2,1)} %collective-permute-done.refs_1_), custom_call_target="tpu_custom_call" | custom-call | flops 1000 | bytes 1000 | tf_op jit(solution)/shard_map/step/pallas_call | solution.py:335
  34.8 2.1 %collective-permute-start.1 = (bf16[2,192,2048]{2,1,0:T(8,128)(2,1)S(1)}, bf16[2,192,2048]{2,1,0:T(8,128)(2,1)S(1)}, u32[]{:S(2)}, u32[]{:S(2)}) collective-permute-start(bf16[2,192,2048]{2,1,0:T(8,128)(2,1)S(1)} %get-tuple-element.40), channel_id=1, source_target_pairs={{0,24},{8,0},{16,8},{24,16},{1,25},{9,1},{17,9},{25,17},{2,26},{10... | collective-permute-start | bytes 4718600 | tf_op jit(solution)/shard_map/ppermute | solution.py:33
  36.8 1.5 %collective-permute-start.4 = (bf16[4,64,512]{2,1,0:T(8,128)(2,1)S(1)}, bf16[4,64,512]{2,1,0:T(8,128)(2,1)S(1)}, u32[]{:S(2)}, u32[]{:S(2)}) collective-permute-start(bf16[4,64,512]{2,1,0:T(8,128)(2,1)S(1)} %get-tuple-element.42), channel_id=1, source_target_pairs={{0,1},{1,0},{2,3},{3,2},{4,5},{5,4},{6,7},{7,6},{8,9},{9,8},{10,11... | collective-permute-start | bytes 786440 | tf_op jit(solution)/shard_map/ppermute | solution.py:33
  38.3 5.7 %collective-permute-done.4.refs_1_ = bf16[4,64,512]{2,1,0:T(8,128)(2,1)S(1)} collective-permute-done((bf16[4,64,512]{2,1,0:T(8,128)(2,1)S(1)}, bf16[4,64,512]{2,1,0:T(8,128)(2,1)S(1)}, u32[]{:S(2)}, u32[]{:S(2)}) %collective-permute-start.4) | collective-permute-done | bytes 262176 | tf_op jit(solution)/shard_map/ppermute | solution.py:33
  44.1 0.6 step.13
  44.7 1.6 %collective-permute-start.5 = (bf16[2,64,512]{2,1,0:T(8,128)(2,1)S(1)}, bf16[2,64,512]{2,1,0:T(8,128)(2,1)S(1)}, u32[]{:S(2)}, u32[]{:S(2)}) collective-permute-start(bf16[2,64,512]{2,1,0:T(8,128)(2,1)S(1)} %get-tuple-element.44), channel_id=1, source_target_pairs={{0,2},{1,3},{2,0},{3,1},{4,6},{5,7},{6,4},{7,5},{8,10},{9,11},{10,... | collective-permute-start | bytes 393224 | tf_op jit(solution)/shard_map/ppermute | solution.py:38
  46.3 3.9 %collective-permute-done.3.refs_1_ = bf16[2,256,2048]{2,1,0:T(8,128)(2,1)} collective-permute-done((bf16[2,256,2048]{2,1,0:T(8,128)(2,1)}, bf16[2,256,2048]{2,1,0:T(8,128)(2,1)}, u32[]{:S(2)}, u32[]{:S(2)}) %collective-permute-start.3) | collective-permute-done | bytes 2097184 | tf_op jit(solution)/shard_map/ppermute | solution.py:33
  50.2 7.1 %step.14 = (f32[4,64,512]{2,1,0:T(8,128)S(1)}, bf16[4,64,512]{2,1,0:T(8,128)(2,1)S(1)}, f32[1,64,512]{2,1,0:T(8,128)S(1)}, bf16[1,64,512]{2,1,0:T(8,128)(2,1)S(1)}, bf16[2,128,2048]{2,1,0:T(8,128)(2,1)S(1)}) custom-call(f32[11]{0:T(128)S(1)} %pad_maximum_fusion.1.table_ref, bf16[2,2,512,2048]{3,2,1,0:T(8,128)(2,1)} %refs_0_.9, ...), custom_call_target="tpu_custom_call" | custom-call | flops 1000 | bytes 1000 | tf_op jit(solution)/shard_map/step/pallas_call | solution.py:335
  57.4 2.1 %collective-permute-start.12 = (bf16[2,128,2048]{2,1,0:T(8,128)(2,1)S(1)}, bf16[2,128,2048]{2,1,0:T(8,128)(2,1)S(1)}, u32[]{:S(2)}, u32[]{:S(2)}) collective-permute-start(bf16[2,128,2048]{2,1,0:T(8,128)(2,1)S(1)} %get-tuple-element.58), channel_id=1, source_target_pairs={{0,24},{8,0},{16,8},{24,16},{1,25},{9,1},{17,9},{25,17},{2,26},{10... | collective-permute-start | bytes 3145736 | tf_op jit(solution)/shard_map/ppermute | solution.py:33
  59.5 1.5 %collective-permute-start.6 = (bf16[4,64,512]{2,1,0:T(8,128)(2,1)S(1)}, bf16[4,64,512]{2,1,0:T(8,128)(2,1)S(1)}, u32[]{:S(2)}, u32[]{:S(2)}) collective-permute-start(bf16[4,64,512]{2,1,0:T(8,128)(2,1)S(1)} %get-tuple-element.46), channel_id=1, source_target_pairs={{0,1},{1,0},{2,3},{3,2},{4,5},{5,4},{6,7},{7,6},{8,9},{9,8},{10,11... | collective-permute-start | bytes 786440 | tf_op jit(solution)/shard_map/ppermute | solution.py:33
  61.0 2.6 %collective-permute-start.7 = (bf16[1,64,512]{2,1,0:T(8,128)(2,1)S(1)}, bf16[1,64,512]{2,1,0:T(8,128)(2,1)S(1)}, u32[]{:S(2)}, u32[]{:S(2)}) collective-permute-start(bf16[1,64,512]{2,1,0:T(8,128)(2,1)S(1)} %get-tuple-element.48), channel_id=1, source_target_pairs={{0,4},{1,5},{2,6},{3,7},{4,0},{5,1},{6,2},{7,3},{8,12},{9,13},{10,... | collective-permute-start | bytes 196616 | tf_op jit(solution)/shard_map/ppermute | solution.py:38
  63.5 3.6 %collective-permute-done.2.refs_1_ = bf16[2,192,2048]{2,1,0:T(8,128)(2,1)} collective-permute-done((bf16[2,192,2048]{2,1,0:T(8,128)(2,1)}, bf16[2,192,2048]{2,1,0:T(8,128)(2,1)}, u32[]{:S(2)}, u32[]{:S(2)}) %collective-permute-start.2) | collective-permute-done | bytes 1572896 | tf_op jit(solution)/shard_map/ppermute | solution.py:33
  67.1 4.4 %step.15 = (bf16[384,2048]{1,0:T(8,128)(2,1)S(1)}, bf16[2,256,2048]{2,1,0:T(8,128)(2,1)S(1)}, bf16[4,64,384]{2,1,0:T(8,128)(2,1)S(1)}, f32[2,64,512]{2,1,0:T(8,1...) custom-call(f32[11]{0:T(128)S(1)} %pad_maximum_fusion.1.table_ref, ...), custom_call_target="tpu_custom_call" | custom-call | flops 1000 | bytes 1000 | tf_op jit(solution)/shard_map/step/pallas_call | solution.py:335
  71.5 1.6 %collective-permute-start.9 = (bf16[4,64,384]{2,1,0:T(8,128)(2,1)S(1)}, bf16[4,64,384]{2,1,0:T(8,128)(2,1)S(1)}, u32[]{:S(2)}, u32[]{:S(2)}) collective-permute-start(bf16[4,64,384]{2,1,0:T(8,128)(2,1)S(1)} %get-tuple-element.53), channel_id=1, source_target_pairs={{0,1},{1,0},{2,3},{3,2},{4,5},{5,4},{6,7},{7,6},{8,9},{9,8},{10,11... | collective-permute-start | bytes 589832 | tf_op jit(solution)/shard_map/ppermute | solution.py:33
  73.1 1.6 %collective-permute-start.8 = (bf16[2,64,512]{2,1,0:T(8,128)(2,1)S(1)}, bf16[2,64,512]{2,1,0:T(8,128)(2,1)S(1)}, u32[]{:S(2)}, u32[]{:S(2)}) collective-permute-start(bf16[2,64,512]{2,1,0:T(8,128)(2,1)S(1)} %get-tuple-element.50), channel_id=1, source_target_pairs={{0,2},{1,3},{2,0},{3,1},{4,6},{5,7},{6,4},{7,5},{8,10},{9,11},{10,... | collective-permute-start | bytes 393224 | tf_op jit(solution)/shard_map/ppermute | solution.py:38
  74.6 1.9 %step.16.refs_0_ = f32[4,64,384]{2,1,0:T(8,128)S(1)} custom-call(f32[11]{0:T(128)S(1)} %pad_maximum_fusion.1.table_ref, bf16[2,256,2048]{2,1,0:T(8,128)(2,1)S(1)} %get-tuple-element.51.refs_0_, bf16[384,2048]{1,0:T(8,128)(2,1)S(1)} %get-tuple-element.52.refs_1_), custom_call_target="tpu_custom_call" | custom-call | flops 1000 | bytes 1000 | tf_op jit(solution)/shard_map/step/pallas_call | solution.py:335
  76.5 2.7 %collective-permute-done.9.refs_1_ = bf16[4,64,384]{2,1,0:T(8,128)(2,1)S(1)} collective-permute-done((bf16[4,64,384]{2,1,0:T(8,128)(2,1)S(1)}, bf16[4,64,384]{2,1,0:T(8,128)(2,1)S(1)}, u32[]{:S(2)}, u32[]{:S(2)}) %collective-permute-start.9) | collective-permute-done | bytes 196640 | tf_op jit(solution)/shard_map/ppermute | solution.py:33
  79.2 0.6 step.17
  79.8 1.6 %collective-permute-start.10 = (bf16[2,64,384]{2,1,0:T(8,128)(2,1)S(1)}, bf16[2,64,384]{2,1,0:T(8,128)(2,1)S(1)}, u32[]{:S(2)}, u32[]{:S(2)}) collective-permute-start(bf16[2,64,384]{2,1,0:T(8,128)(2,1)S(1)} %get-tuple-element.55), channel_id=1, source_target_pairs={{0,2},{1,3},{2,0},{3,1},{4,6},{5,7},{6,4},{7,5},{8,10},{9,11},{10,... | collective-permute-start | bytes 294920 | tf_op jit(solution)/shard_map/ppermute | solution.py:38
  81.5 3.1 %collective-permute-done.10.refs_5_ = bf16[2,64,384]{2,1,0:T(8,128)(2,1)S(1)} collective-permute-done((bf16[2,64,384]{2,1,0:T(8,128)(2,1)S(1)}, bf16[2,64,384]{2,1,0:T(8,128)(2,1)S(1)}, u32[]{:S(2)}, u32[]{:S(2)}) %collective-permute-start.10) | collective-permute-done | bytes 98336 | tf_op jit(solution)/shard_map/ppermute | solution.py:38
  84.6 3.5 %step.18 = (bf16[384,2048]{1,0:T(8,128)(2,1)S(1)}, bf16[2,256,2048]{2,1,0:T(8,128)(2,1)S(1)}, bf16[4,64,384]{2,1,0:T(8,128)(2,1)S(1)}, f32[1,64,896]{2,1,0:T(8,128)S(1)}, bf16[1,64,896]{2,1,0:T(8,128)(2,1)S(1)}) custom-call(f32[11]{0:T(128)S(1)} %pad_maximum_fusion.1.table_ref, bf16[2,2,512,2048]{3,2,1,0:T(8,128)(2,1)} %refs_0_.9, ...), custom_call_target="tpu_custom_call" | custom-call | flops 1000 | bytes 1000 | tf_op jit(solution)/shard_map/step/pallas_call | solution.py:335
  88.1 1.6 %collective-permute-start.13 = (bf16[4,64,384]{2,1,0:T(8,128)(2,1)S(1)}, bf16[4,64,384]{2,1,0:T(8,128)(2,1)S(1)}, u32[]{:S(2)}, u32[]{:S(2)}) collective-permute-start(bf16[4,64,384]{2,1,0:T(8,128)(2,1)S(1)} %get-tuple-element.61), channel_id=1, source_target_pairs={{0,1},{1,0},{2,3},{3,2},{4,5},{5,4},{6,7},{7,6},{8,9},{9,8},{10,11... | collective-permute-start | bytes 589832 | tf_op jit(solution)/shard_map/ppermute | solution.py:33
  89.6 2.6 %collective-permute-start.11 = (bf16[1,64,896]{2,1,0:T(8,128)(2,1)S(1)}, bf16[1,64,896]{2,1,0:T(8,128)(2,1)S(1)}, u32[]{:S(2)}, u32[]{:S(2)}) collective-permute-start(bf16[1,64,896]{2,1,0:T(8,128)(2,1)S(1)} %get-tuple-element.57), channel_id=1, source_target_pairs={{0,4},{1,5},{2,6},{3,7},{4,0},{5,1},{6,2},{7,3},{8,12},{9,13},{10,... | collective-permute-start | bytes 344072 | tf_op jit(solution)/shard_map/ppermute | solution.py:38
  92.2 1.9 %step.19.refs_2_ = f32[4,64,384]{2,1,0:T(8,128)S(1)} custom-call(f32[11]{0:T(128)S(1)} %pad_maximum_fusion.1.table_ref, bf16[2,256,2048]{2,1,0:T(8,128)(2,1)S(1)} %get-tuple-element.59.refs_0_, bf16[384,2048]{1,0:T(8,128)(2,1)S(1)} %get-tuple-element.60.refs_1_), custom_call_target="tpu_custom_call" | custom-call | flops 1000 | bytes 1000 | tf_op jit(solution)/shard_map/step/pallas_call | solution.py:335
  94.1 1.0 collective-permute-done.12.refs_1_
  95.1 2.8 %collective-permute-done.11.refs_5_.refs_1_ = bf16[1,64,896]{2,1,0:T(8,128)(2,1)S(1)} collective-permute-done((bf16[1,64,896]{2,1,0:T(8,128)(2,1)S(1)}, bf16[1,64,896]{2,1,0:T(8,128)(2,1)S(1)}, u32[]{:S(2)}, u32[]{:S(2)}) %collective-permute-start.11) | collective-permute-done | bytes 114720 | tf_op jit(solution)/shard_map/ppermute | solution.py:38
  97.9 3.4 %step.20 = (bf16[256,2048]{1,0:T(8,128)(2,1)S(1)}, bf16[2,256,2048]{2,1,0:T(8,128)(2,1)S(1)}, bf16[4,64,256]{2,1,0:T(8,128)(2,1)S(1)}, f32[2,64,384]{2,1,0:T(8,1...) custom-call(f32[11]{0:T(128)S(1)} %pad_maximum_fusion.1.table_ref, ...), custom_call_target="tpu_custom_call", output_to_operand_aliasing={{5}: (7, {})} | custom-call | flops 1000 | bytes 1000 | tf_op jit(solution)/shard_map/step/pallas_call | solution.py:335
  101.3 0.6 collective-permute-start.14
  101.9 0.7 collective-permute-start.15
  102.5 1.3 %step.21.refs_0_ = f32[4,64,256]{2,1,0:T(8,128)S(1)} custom-call(f32[11]{0:T(128)S(1)} %pad_maximum_fusion.1.table_ref, bf16[2,256,2048]{2,1,0:T(8,128)(2,1)S(1)} %get-tuple-element.63.refs_0_, bf16[256,2048]{1,0:T(8,128)(2,1)S(1)} %get-tuple-element.64.refs_1_), custom_call_target="tpu_custom_call" | custom-call | flops 1000 | bytes 1000 | tf_op jit(solution)/shard_map/step/pallas_call | solution.py:335
  103.8 2.7 %collective-permute-done.15.refs_3_ = bf16[2,64,384]{2,1,0:T(8,128)(2,1)S(1)} collective-permute-done((bf16[2,64,384]{2,1,0:T(8,128)(2,1)S(1)}, bf16[2,64,384]{2,1,0:T(8,128)(2,1)S(1)}, u32[]{:S(2)}, u32[]{:S(2)}) %collective-permute-start.15) | collective-permute-done | bytes 98336 | tf_op jit(solution)/shard_map/ppermute | solution.py:38
  106.5 0.6 step.22
  107.1 2.2 %collective-permute-start.16 = (bf16[1,64,384]{2,1,0:T(8,128)(2,1)S(1)}, bf16[1,64,384]{2,1,0:T(8,128)(2,1)S(1)}, u32[]{:S(2)}, u32[]{:S(2)}) collective-permute-start(bf16[1,64,384]{2,1,0:T(8,128)(2,1)S(1)} %get-tuple-element.69), channel_id=1, source_target_pairs={{0,4},{1,5},{2,6},{3,7},{4,0},{5,1},{6,2},{7,3},{8,12},{9,13},{10,... | collective-permute-start | bytes 147464 | tf_op jit(solution)/shard_map/ppermute | solution.py:38
  109.3 2.2 %collective-permute-start.17 = (bf16[1,64,256]{2,1,0:T(8,128)(2,1)S(1)}, bf16[1,64,256]{2,1,0:T(8,128)(2,1)S(1)}, u32[]{:S(2)}, u32[]{:S(2)}) collective-permute-start(bf16[1,64,256]{2,1,0:T(8,128)(2,1)S(1)} %get-tuple-element.71), channel_id=1, source_target_pairs={{0,2},{1,3},{2,0},{3,1},{4,6},{5,7},{6,4},{7,5},{8,10},{9,11},{10,... | collective-permute-start | bytes 98312 | tf_op jit(solution)/shard_map/ppermute | solution.py:38
  111.6 2.3 %collective-permute-start.19 = (bf16[1,64,256]{2,1,0:T(8,128)(2,1)S(1)}, bf16[1,64,256]{2,1,0:T(8,128)(2,1)S(1)}, u32[]{:S(2)}, u32[]{:S(2)}) collective-permute-start(bf16[1,64,256]{2,1,0:T(8,128)(2,1)S(1)} %get-tuple-element.73), channel_id=1, source_target_pairs={{0,6},{1,7},{2,4},{3,5},{4,2},{5,3},{6,0},{7,1},{8,14},{9,15},{10,... | collective-permute-start | bytes 98312 | tf_op jit(solution)/shard_map/ppermute | solution.py:38
  113.8 2.4 %collective-permute-done.18.refs_6_ = bf16[1,64,256]{2,1,0:T(8,128)(2,1)S(1)} collective-permute-done((bf16[1,64,256]{2,1,0:T(8,128)(2,1)S(1)}, bf16[1,64,256]{2,1,0:T(8,128)(2,1)S(1)}, u32[]{:S(2)}, u32[]{:S(2)}) %collective-permute-start.18) | collective-permute-done | bytes 32800 | tf_op jit(solution)/shard_map/ppermute | solution.py:38
  116.3 1.0 collective-permute-done.19.refs_7_
  117.3 1.5 %step.23 = f32[64,2,2,512]{3,2,1,0:T(2,128)} custom-call(f32[11]{0:T(128)S(1)} %pad_maximum_fusion.1.table_ref, f32[1,64,896]{2,1,0:T(8,128)S(1)} %get-tuple-element.56.refs_4_.refs_0_, bf16[1,64,896]{2,1,0:T(8,128)(2,1)S(1)} %collective-permute-done.11.refs_5_.refs_1_, f32[1,64,384]{2,1,0:T(8,128)S(1)} %get-tuple-element.68.refs_2_, ...), custom_call_target="tpu_custom_call", output_to_operand_aliasing={{}: (9, {})} | custom-call | flops 1000 | bytes 1000 | tf_op jit(solution)/shard_map/step/pallas_call | solution.py:335
  (19 shorter events, 0.4 us)
Async XLA Ops:
  1.7 26.0 %collective-permute-start = (bf16[2,256,2048]{2,1,0:T(8,128)(2,1)S(1)}, bf16[2,256,2048]{2,1,0:T(8,128)(2,1)}, u32[]{:S(2)}, u32[]{:S(2)}) collective-permute-start(bf16[2,256,2048]{2,1,0:T(8,128)(2,1)S(1)} %piece_of.3.rest_0_), channel_id=1, source_target_pairs={{0,24},{8,0},{16,8},{24,16},{1,25},{9,1},{17,9},{25,17},{2,26},{10... | collective-permute-start | bytes 6291464 | tf_op jit(solution)/shard_map/ppermute | solution.py:33
  6.7 3.1 %copy-start = (s32[2]{0:T(128)S(1)}, s32[2]{0:T(128)}, u32[]{:S(2)}) copy-start(s32[2]{0:T(128)} %param.4) | copy-start | bytes 28
  6.7 3.1 %copy-start.1 = (s32[2]{0:T(128)S(1)}, s32[2]{0:T(128)}, u32[]{:S(2)}) copy-start(s32[2]{0:T(128)} %param.5) | copy-start | bytes 28
  6.7 43.5 %collective-permute-start.3 = (bf16[2,256,2048]{2,1,0:T(8,128)(2,1)}, bf16[2,256,2048]{2,1,0:T(8,128)(2,1)}, u32[]{:S(2)}, u32[]{:S(2)}) collective-permute-start(bf16[2,256,2048]{2,1,0:T(8,128)(2,1)} %piece_of.4.rest_0_), channel_id=1, source_target_pairs={{0,24},{8,0},{16,8},{24,16},{1,25},{9,1},{17,9},{25,17},{2,26},{10... | collective-permute-start | bytes 6291464 | tf_op jit(solution)/shard_map/ppermute | solution.py:33
  9.7 57.4 %collective-permute-start.2 = (bf16[2,192,2048]{2,1,0:T(8,128)(2,1)}, bf16[2,192,2048]{2,1,0:T(8,128)(2,1)}, u32[]{:S(2)}, u32[]{:S(2)}) collective-permute-start(bf16[2,192,2048]{2,1,0:T(8,128)(2,1)} %piece_of.5), channel_id=1, source_target_pairs={{0,24},{8,0},{16,8},{24,16},{1,25},{9,1},{17,9},{25,17},{2,26},{10... | collective-permute-start | bytes 4718600 | tf_op jit(solution)/shard_map/ppermute | solution.py:33
  34.8 49.8 %collective-permute-start.1 = (bf16[2,192,2048]{2,1,0:T(8,128)(2,1)S(1)}, bf16[2,192,2048]{2,1,0:T(8,128)(2,1)S(1)}, u32[]{:S(2)}, u32[]{:S(2)}) collective-permute-start(bf16[2,192,2048]{2,1,0:T(8,128)(2,1)S(1)} %get-tuple-element.40), channel_id=1, source_target_pairs={{0,24},{8,0},{16,8},{24,16},{1,25},{9,1},{17,9},{25,17},{2,26},{10... | collective-permute-start | bytes 4718600 | tf_op jit(solution)/shard_map/ppermute | solution.py:33
  36.8 7.2 %collective-permute-start.4 = (bf16[4,64,512]{2,1,0:T(8,128)(2,1)S(1)}, bf16[4,64,512]{2,1,0:T(8,128)(2,1)S(1)}, u32[]{:S(2)}, u32[]{:S(2)}) collective-permute-start(bf16[4,64,512]{2,1,0:T(8,128)(2,1)S(1)} %get-tuple-element.42), channel_id=1, source_target_pairs={{0,1},{1,0},{2,3},{3,2},{4,5},{5,4},{6,7},{7,6},{8,9},{9,8},{10,11... | collective-permute-start | bytes 786440 | tf_op jit(solution)/shard_map/ppermute | solution.py:33
  44.7 5.6 %collective-permute-start.5 = (bf16[2,64,512]{2,1,0:T(8,128)(2,1)S(1)}, bf16[2,64,512]{2,1,0:T(8,128)(2,1)S(1)}, u32[]{:S(2)}, u32[]{:S(2)}) collective-permute-start(bf16[2,64,512]{2,1,0:T(8,128)(2,1)S(1)} %get-tuple-element.44), channel_id=1, source_target_pairs={{0,2},{1,3},{2,0},{3,1},{4,6},{5,7},{6,4},{7,5},{8,10},{9,11},{10,... | collective-permute-start | bytes 393224 | tf_op jit(solution)/shard_map/ppermute | solution.py:38
  57.4 37.7 %collective-permute-start.12 = (bf16[2,128,2048]{2,1,0:T(8,128)(2,1)S(1)}, bf16[2,128,2048]{2,1,0:T(8,128)(2,1)S(1)}, u32[]{:S(2)}, u32[]{:S(2)}) collective-permute-start(bf16[2,128,2048]{2,1,0:T(8,128)(2,1)S(1)} %get-tuple-element.58), channel_id=1, source_target_pairs={{0,24},{8,0},{16,8},{24,16},{1,25},{9,1},{17,9},{25,17},{2,26},{10... | collective-permute-start | bytes 3145736 | tf_op jit(solution)/shard_map/ppermute | solution.py:33
  59.5 7.6 %collective-permute-start.6 = (bf16[4,64,512]{2,1,0:T(8,128)(2,1)S(1)}, bf16[4,64,512]{2,1,0:T(8,128)(2,1)S(1)}, u32[]{:S(2)}, u32[]{:S(2)}) collective-permute-start(bf16[4,64,512]{2,1,0:T(8,128)(2,1)S(1)} %get-tuple-element.46), channel_id=1, source_target_pairs={{0,1},{1,0},{2,3},{3,2},{4,5},{5,4},{6,7},{7,6},{8,9},{9,8},{10,11... | collective-permute-start | bytes 786440 | tf_op jit(solution)/shard_map/ppermute | solution.py:33
  61.0 6.1 %collective-permute-start.7 = (bf16[1,64,512]{2,1,0:T(8,128)(2,1)S(1)}, bf16[1,64,512]{2,1,0:T(8,128)(2,1)S(1)}, u32[]{:S(2)}, u32[]{:S(2)}) collective-permute-start(bf16[1,64,512]{2,1,0:T(8,128)(2,1)S(1)} %get-tuple-element.48), channel_id=1, source_target_pairs={{0,4},{1,5},{2,6},{3,7},{4,0},{5,1},{6,2},{7,3},{8,12},{9,13},{10,... | collective-permute-start | bytes 196616 | tf_op jit(solution)/shard_map/ppermute | solution.py:38
  71.5 7.7 %collective-permute-start.9 = (bf16[4,64,384]{2,1,0:T(8,128)(2,1)S(1)}, bf16[4,64,384]{2,1,0:T(8,128)(2,1)S(1)}, u32[]{:S(2)}, u32[]{:S(2)}) collective-permute-start(bf16[4,64,384]{2,1,0:T(8,128)(2,1)S(1)} %get-tuple-element.53), channel_id=1, source_target_pairs={{0,1},{1,0},{2,3},{3,2},{4,5},{5,4},{6,7},{7,6},{8,9},{9,8},{10,11... | collective-permute-start | bytes 589832 | tf_op jit(solution)/shard_map/ppermute | solution.py:33
  73.1 8.4 %collective-permute-start.8 = (bf16[2,64,512]{2,1,0:T(8,128)(2,1)S(1)}, bf16[2,64,512]{2,1,0:T(8,128)(2,1)S(1)}, u32[]{:S(2)}, u32[]{:S(2)}) collective-permute-start(bf16[2,64,512]{2,1,0:T(8,128)(2,1)S(1)} %get-tuple-element.50), channel_id=1, source_target_pairs={{0,2},{1,3},{2,0},{3,1},{4,6},{5,7},{6,4},{7,5},{8,10},{9,11},{10,... | collective-permute-start | bytes 393224 | tf_op jit(solution)/shard_map/ppermute | solution.py:38
  79.8 4.7 %collective-permute-start.10 = (bf16[2,64,384]{2,1,0:T(8,128)(2,1)S(1)}, bf16[2,64,384]{2,1,0:T(8,128)(2,1)S(1)}, u32[]{:S(2)}, u32[]{:S(2)}) collective-permute-start(bf16[2,64,384]{2,1,0:T(8,128)(2,1)S(1)} %get-tuple-element.55), channel_id=1, source_target_pairs={{0,2},{1,3},{2,0},{3,1},{4,6},{5,7},{6,4},{7,5},{8,10},{9,11},{10,... | collective-permute-start | bytes 294920 | tf_op jit(solution)/shard_map/ppermute | solution.py:38
  88.1 9.8 %collective-permute-start.13 = (bf16[4,64,384]{2,1,0:T(8,128)(2,1)S(1)}, bf16[4,64,384]{2,1,0:T(8,128)(2,1)S(1)}, u32[]{:S(2)}, u32[]{:S(2)}) collective-permute-start(bf16[4,64,384]{2,1,0:T(8,128)(2,1)S(1)} %get-tuple-element.61), channel_id=1, source_target_pairs={{0,1},{1,0},{2,3},{3,2},{4,5},{5,4},{6,7},{7,6},{8,9},{9,8},{10,11... | collective-permute-start | bytes 589832 | tf_op jit(solution)/shard_map/ppermute | solution.py:33
  89.6 8.2 %collective-permute-start.11 = (bf16[1,64,896]{2,1,0:T(8,128)(2,1)S(1)}, bf16[1,64,896]{2,1,0:T(8,128)(2,1)S(1)}, u32[]{:S(2)}, u32[]{:S(2)}) collective-permute-start(bf16[1,64,896]{2,1,0:T(8,128)(2,1)S(1)} %get-tuple-element.57), channel_id=1, source_target_pairs={{0,4},{1,5},{2,6},{3,7},{4,0},{5,1},{6,2},{7,3},{8,12},{9,13},{10,... | collective-permute-start | bytes 344072 | tf_op jit(solution)/shard_map/ppermute | solution.py:38
  101.3 5.2 %collective-permute-start.14 = (bf16[4,64,256]{2,1,0:T(8,128)(2,1)S(1)}, bf16[4,64,256]{2,1,0:T(8,128)(2,1)S(1)}, u32[]{:S(2)}, u32[]{:S(2)}) collective-permute-start(bf16[4,64,256]{2,1,0:T(8,128)(2,1)S(1)} %get-tuple-element.65), channel_id=1, source_target_pairs={{0,1},{1,0},{2,3},{3,2},{4,5},{5,4},{6,7},{7,6},{8,9},{9,8},{10,11... | collective-permute-start | bytes 393224 | tf_op jit(solution)/shard_map/ppermute | solution.py:33
  101.9 4.6 %collective-permute-start.15 = (bf16[2,64,384]{2,1,0:T(8,128)(2,1)S(1)}, bf16[2,64,384]{2,1,0:T(8,128)(2,1)S(1)}, u32[]{:S(2)}, u32[]{:S(2)}) collective-permute-start(bf16[2,64,384]{2,1,0:T(8,128)(2,1)S(1)} %get-tuple-element.67), channel_id=1, source_target_pairs={{0,2},{1,3},{2,0},{3,1},{4,6},{5,7},{6,4},{7,5},{8,10},{9,11},{10,... | collective-permute-start | bytes 294920 | tf_op jit(solution)/shard_map/ppermute | solution.py:38
  107.1 10.2 %collective-permute-start.16 = (bf16[1,64,384]{2,1,0:T(8,128)(2,1)S(1)}, bf16[1,64,384]{2,1,0:T(8,128)(2,1)S(1)}, u32[]{:S(2)}, u32[]{:S(2)}) collective-permute-start(bf16[1,64,384]{2,1,0:T(8,128)(2,1)S(1)} %get-tuple-element.69), channel_id=1, source_target_pairs={{0,4},{1,5},{2,6},{3,7},{4,0},{5,1},{6,2},{7,3},{8,12},{9,13},{10,... | collective-permute-start | bytes 147464 | tf_op jit(solution)/shard_map/ppermute | solution.py:38
  109.3 4.6 %collective-permute-start.17 = (bf16[1,64,256]{2,1,0:T(8,128)(2,1)S(1)}, bf16[1,64,256]{2,1,0:T(8,128)(2,1)S(1)}, u32[]{:S(2)}, u32[]{:S(2)}) collective-permute-start(bf16[1,64,256]{2,1,0:T(8,128)(2,1)S(1)} %get-tuple-element.71), channel_id=1, source_target_pairs={{0,2},{1,3},{2,0},{3,1},{4,6},{5,7},{6,4},{7,5},{8,10},{9,11},{10,... | collective-permute-start | bytes 98312 | tf_op jit(solution)/shard_map/ppermute | solution.py:38
  111.5 4.8 %collective-permute-start.18 = (bf16[1,64,256]{2,1,0:T(8,128)(2,1)S(1)}, bf16[1,64,256]{2,1,0:T(8,128)(2,1)S(1)}, u32[]{:S(2)}, u32[]{:S(2)}) collective-permute-start(bf16[1,64,256]{2,1,0:T(8,128)(2,1)S(1)} %get-tuple-element.72), channel_id=1, source_target_pairs={{0,4},{1,5},{2,6},{3,7},{4,0},{5,1},{6,2},{7,3},{8,12},{9,13},{10,... | collective-permute-start | bytes 98312 | tf_op jit(solution)/shard_map/ppermute | solution.py:38
  111.6 5.7 %collective-permute-start.19 = (bf16[1,64,256]{2,1,0:T(8,128)(2,1)S(1)}, bf16[1,64,256]{2,1,0:T(8,128)(2,1)S(1)}, u32[]{:S(2)}, u32[]{:S(2)}) collective-permute-start(bf16[1,64,256]{2,1,0:T(8,128)(2,1)S(1)} %get-tuple-element.73), channel_id=1, source_target_pairs={{0,6},{1,7},{2,4},{3,5},{4,2},{5,3},{6,0},{7,1},{8,14},{9,15},{10,... | collective-permute-start | bytes 98312 | tf_op jit(solution)/shard_map/ppermute | solution.py:38

commit v16 on v15

--- a/solution.py
+++ b/solution.py
@@ -16,6 +16,7 @@
 AHEAD = 3
 OUTER = 4
 SPLIT = 128
+JOINT = 2
 LANES = 128
 BLOCK = 256
 VMEM_BYTES = 46 * 1024 * 1024
@@ -119,7 +120,7 @@
     if plan.part:
         bands_ref, phased_ref = take(2)
     sources = [take(count) for count in plan.takes]
-    arrived = [take(count) for count in plan.adds]
+    arrived = take(plan.adds)
     if plan.adding and plan.placed:
         take(1)
     given_ref, kept_ref = take(2) if plan.near == "give" else (None, None)
@@ -169,8 +170,10 @@
     if plan.adding:
         sum_buf, placed_sem = take(2)
         add_slot, add_start, pieces = plan.adding
-        for index, column, start, span in pieces:
-            total = summed(arrived[index], 0, slice(column, column + 2 * span))
+        for start, span, terms in pieces:
+            total = 0.0
+            for index, column in terms:
+                total += arrived[index][0, :, column : column + 2 * span].astype(jnp.float32)
             put_sum(sum_buf, start - add_start, total)
         add_point = table_ref[add_slot * stride].astype(jnp.int32)
         columns = pl.ds(add_start, sum_buf.shape[2])
@@ -181,13 +184,16 @@
     for task, arrays, outputs in zip(plan.tasks, sources, targets):
         groups = [arrays[i : i + task.each] for i in range(0, len(arrays), task.each)]
         bit = lax.rem(lax.div(outer, 1 << task.stage), 2)
-        for index, out_ref in enumerate(outputs):
+        filled = [(out_ref, 0) for out_ref in outputs]
+        if plan.joined and not task.direct:
+            filled.append((targets[0][JOINT], 2 * plan.tasks[0].batch[0][2]))
+        for index, (out_ref, shift) in enumerate(filled):
             for level in range(out_ref.shape[0]):
                 if task.direct:
                     source = partner(outer, index)
                 else:
                     source = 2 * level + (1 - bit if index else bit)
-                column = 0
+                column = shift
                 for group in groups:
                     total = summed(group, source)
                     columns = slice(column, column + total.shape[1])
@@ -270,7 +276,8 @@
     tasks: tuple
     takes: tuple
     adding: tuple
-    adds: tuple
+    adds: int
+    joined: bool
     placed: bool
     later: tuple
 
@@ -302,15 +309,16 @@
                 pltpu.VMEM((len(plan.ways), 2, depth * rows, points), jnp.bfloat16),
                 pltpu.SemaphoreType.DMA((fold, 2, depth)),
             ]
-    for arrays in sources + arrived:
+    for arrays in [*sources, arrived]:
         operands += arrays
         in_specs += [vmem] * len(arrays)
     for task in plan.tasks:
         wide = sum(2 * width for _, _, width in task.batch)
         levels = 1 if task.direct else depth >> (task.stage + 1)
-        out_shape += [
-            jax.ShapeDtypeStruct((levels, rows, wide), kind(i)) for i in range(task.count)
-        ]
+        extra = 2 * plan.tasks[1].batch[0][2] if plan.joined and task.direct else 0
+        for i in range(task.count):
+            columns = wide + extra if i == JOINT else wide
+            out_shape.append(jax.ShapeDtypeStruct((levels, rows, columns), kind(i)))
     out_specs += [vmem] * len(out_shape)
     if plan.later:
         scratch += [
@@ -324,7 +332,7 @@
             in_specs.append(hbm)
         out_shape.append(jax.ShapeDtypeStruct(plan.shape, jnp.float32))
         out_specs.append(hbm)
-        lanes = sum(span for _, _, _, span in plan.adding[2])
+        lanes = sum(span for _, span, _ in plan.adding[2])
         scratch += [pltpu.VMEM((rows, 2, lanes), jnp.float32), pltpu.SemaphoreType.DMA]
     if plan.later:
         out_shape.append(jax.ShapeDtypeStruct((2, plan.later[2], points), bands.dtype))
@@ -388,7 +396,7 @@
             halved, crossed = halved + crossed, []
     tasks = (
         Task((parts[-1],), 0, True, fold, depth),
-        Task(tuple(halved), 1, False, 2, 2),
+        Task(tuple(halved), 1, False, 2, 1),
     )
     kernels.append((None, (), "", tasks, ()))
     kernels.append((None, (), "", (), tuple(waiting) + tuple(halved) + (parts[-1],)))
@@ -440,15 +448,16 @@
     for part, ways, phase, tasks, adds in schedule(parts, fold, depth):
         place = parts.index(part) if part else len(parts)
         later = parts[place + AHEAD] if place + AHEAD < len(parts) and phase != "use" else None
-        sources = [[array for done in task.batch for array in held[(done,)]] for task in tasks]
-        batches, pieces = [], []
+        sources = [
+            [array for done in task.batch for array, _ in held[(done,)]] for task in tasks
+        ]
+        arrived, pieces = [], []
         for done in adds:
             batch = max((key for key in held if done in key), key=len)
-            if batch not in batches:
-                batches.append(batch)
             column = sum(2 * width for _, _, width in batch[: batch.index(done)])
-            pieces.append((batches.index(batch), column, done[1], done[2]))
-        arrived = [held[batch] for batch in batches]
+            terms = [(len(arrived) + i, first + column) for i, (_, first) in enumerate(held[batch])]
+            arrived += [array for array, _ in held[batch]]
+            pieces.append((done[1], done[2], tuple(terms)))
         adding = (adds[0][0], adds[0][1], tuple(pieces)) if adds else ()
         plan = Plan(
             shape,
@@ -460,7 +469,8 @@
             tasks,
             tuple(len(arrays) for arrays in sources),
             adding,
-            tuple(len(arrays) for arrays in arrived),
+            len(arrived),
+            len(tasks) > 1 and tasks[0].direct,
             result is not None,
             later,
         )
@@ -474,12 +484,15 @@
             theres.append(shifted(piece, "ka", -1))
         for way, array in zip(ways, terms):
             array = shifted(array, "ga", way, fold, True) if way else array
-            held.setdefault((part,), []).insert(0 if way == 0 else fold, array)
+            held.setdefault((part,), []).insert(0 if way == 0 else fold, (array, 0))
         for task, arrays in zip(tasks, sends):
             steps = range(1, depth) if task.direct else [1 << task.stage]
-            held[task.batch] = [arrays[0]] + [
-                swapped(array, "ga", fold * i) for array, i in zip(arrays[1:], steps)
+            held[task.batch] = [(arrays[0], 0)] + [
+                (swapped(array, "ga", fold * i), 0) for array, i in zip(arrays[1:], steps)
             ]
+        if plan.joined:
+            joint = held[tasks[0].batch][JOINT][0]
+            held[tasks[1].batch].append((joint, 2 * tasks[0].batch[0][2]))
     return result
 
 

time: 119 us -> 119 us (level)
  starting transfers between devices: 31.5 us -> 29.2 us
  waiting for transfers between devices: 46.1 us -> 48.3 us
    ppermute x10 -> x9, starting transfers between devices: 17.5 us -> 15.2 us  [swapped(): return lax.ppermute(block, axis, [(i, i ^ distance) for i in range(count)])]
    ppermute x10 -> x9, waiting for transfers between devices: 12 us -> 14.2 us  [swapped(): return lax.ppermute(block, axis, [(i, i ^ distance) for i in range(count)])]
  transfers between devices with their start and end apart: 20 -> 19, of which waited for: 11 -> 11; matrix products, arithmetic and copies ran while one was open for 1% -> 1% of each run, Pallas kernels for 28% -> 28%
where the time goes in v16:
time: 119 us
  waiting for transfers between devices  48.3 us (41%)
  Pallas kernels  40.3 us (34%)
  starting transfers between devices  29.2 us (25%)
    ppermute x10, waiting for transfers between devices, shifted(): return lax.ppermute(block, axis, route)  34.1 us
    pallas_call x12, Pallas kernels, step(): pl.pallas_call(functools.partial(step_kernel, plan), in_specs=in_specs, o...  33.8 us
    ppermute x9, starting transfers between devices, swapped(): return lax.ppermute(block, axis, [(i, i ^ distance) for i in range(count)])  15.2 us
    ppermute x9, waiting for transfers between devices, swapped(): return lax.ppermute(block, axis, [(i, i ^ distance) for i in range(count)])  14.2 us
    ppermute x10, starting transfers between devices, shifted(): return lax.ppermute(block, axis, route)  14.1 us
    pallas_call x3, Pallas kernels, piece_of(): pl.pallas_call(functools.partial(piece_kernel, slot, start), in_specs=[pl...  6.52 us
  transfers between devices with their start and end apart: 19, of which 11 were waited for; matrix products, arithmetic and copies ran while one was open for 1% of the time, Pallas kernels for 28%

profile of v16, /device:TPU:0, one launch (start us, length us, event | category | flops | bytes accessed | tf_op | source)
XLA Modules:
  0.0 118.8 jit_solution(1427214975834079648)
XLA Ops:
  0.0 1.6 %piece_of.3.rest_0_ = bf16[2,256,2048]{2,1,0:T(8,128)(2,1)S(1)} custom-call(bf16[2,2,512,2048]{3,2,1,0:T(8,128)(2,1)} %refs_0_.9), custom_call_target="tpu_custom_call" | custom-call | flops 1000 | bytes 1000 | tf_op jit(solution)/shard_map/piece_of/pallas_call | solution.py:65
  1.7 2.5 %collective-permute-start = (bf16[2,256,2048]{2,1,0:T(8,128)(2,1)S(1)}, bf16[2,256,2048]{2,1,0:T(8,128)(2,1)}, u32[]{:S(2)}, u32[]{:S(2)}) collective-permute-start(bf16[2,256,2048]{2,1,0:T(8,128)(2,1)S(1)} %piece_of.3.rest_0_), channel_id=1, source_target_pairs={{0,24},{8,0},{16,8},{24,16},{1,25},{9,1},{17,9},{25,17},{2,26},{10... | collective-permute-start | bytes 6291464 | tf_op jit(solution)/shard_map/ppermute | solution.py:34
  4.1 2.6 %piece_of.4.rest_0_ = bf16[2,256,2048]{2,1,0:T(8,128)(2,1)} custom-call(bf16[2,2,512,2048]{3,2,1,0:T(8,128)(2,1)} %refs_0_.9, bf16[2,256,2048]{2,1,0:T(8,128)(2,1)S(1)} %piece_of.3.rest_0_), custom_call_target="tpu_custom_call" | custom-call | flops 1000 | bytes 1000 | tf_op jit(solution)/shard_map/piece_of/pallas_call | solution.py:65
  6.7 0.7 collective-permute-start.3
  7.4 2.3 %piece_of.5 = bf16[2,192,2048]{2,1,0:T(8,128)(2,1)} custom-call(bf16[2,2,512,2048]{3,2,1,0:T(8,128)(2,1)} %refs_0_.9, bf16[2,256,2048]{2,1,0:T(8,128)(2,1)} %piece_of.4.rest_0_), custom_call_target="tpu_custom_call" | custom-call | flops 1000 | bytes 1000 | tf_op jit(solution)/shard_map/piece_of/pallas_call | solution.py:65
  9.8 0.1 select_reduce_fusion.1
  10.0 0.1 fusion.4
  10.1 0.1 copy.6
  10.3 0.1 reshape.28
  10.4 0.1 pad_maximum_fusion.1.table_ref
  10.5 17.2 %collective-permute-done.refs_1_ = bf16[2,256,2048]{2,1,0:T(8,128)(2,1)} collective-permute-done((bf16[2,256,2048]{2,1,0:T(8,128)(2,1)S(1)}, bf16[2,256,2048]{2,1,0:T(8,128)(2,1)}, u32[]{:S(2)}, u32[]{:S(2)}) %collective-permute-start) | collective-permute-done | bytes 2097184 | tf_op jit(solution)/shard_map/ppermute | solution.py:34
  27.7 7.1 %step.12 = (f32[4,64,512]{2,1,0:T(8,128)S(1)}, bf16[4,64,512]{2,1,0:T(8,128)(2,1)S(1)}, bf16[2,192,2048]{2,1,0:T(8,128)(2,1)S(1)}) custom-call(f32[11]{0:T(128)S(1)} %pad_maximum_fusion.1.table_ref, bf16[2,2,512,2048]{3,2,1,0:T(8,128)(2,1)} %refs_0_.9, bf16[2,256,2048]{2,1,0:T(8,128)(2,1)} %collective-permute-done.refs_1_), custom_call_target="tpu_custom_call" | custom-call | flops 1000 | bytes 1000 | tf_op jit(solution)/shard_map/step/pallas_call | solution.py:343
  34.8 2.1 %collective-permute-start.1 = (bf16[2,192,2048]{2,1,0:T(8,128)(2,1)S(1)}, bf16[2,192,2048]{2,1,0:T(8,128)(2,1)S(1)}, u32[]{:S(2)}, u32[]{:S(2)}) collective-permute-start(bf16[2,192,2048]{2,1,0:T(8,128)(2,1)S(1)} %get-tuple-element.39), channel_id=1, source_target_pairs={{0,24},{8,0},{16,8},{24,16},{1,25},{9,1},{17,9},{25,17},{2,26},{10... | collective-permute-start | bytes 4718600 | tf_op jit(solution)/shard_map/ppermute | solution.py:34
  36.8 1.5 %collective-permute-start.4 = (bf16[4,64,512]{2,1,0:T(8,128)(2,1)S(1)}, bf16[4,64,512]{2,1,0:T(8,128)(2,1)S(1)}, u32[]{:S(2)}, u32[]{:S(2)}) collective-permute-start(bf16[4,64,512]{2,1,0:T(8,128)(2,1)S(1)} %get-tuple-element.41), channel_id=1, source_target_pairs={{0,1},{1,0},{2,3},{3,2},{4,5},{5,4},{6,7},{7,6},{8,9},{9,8},{10,11... | collective-permute-start | bytes 786440 | tf_op jit(solution)/shard_map/ppermute | solution.py:34
  38.3 5.7 %collective-permute-done.4.refs_1_ = bf16[4,64,512]{2,1,0:T(8,128)(2,1)S(1)} collective-permute-done((bf16[4,64,512]{2,1,0:T(8,128)(2,1)S(1)}, bf16[4,64,512]{2,1,0:T(8,128)(2,1)S(1)}, u32[]{:S(2)}, u32[]{:S(2)}) %collective-permute-start.4) | collective-permute-done | bytes 262176 | tf_op jit(solution)/shard_map/ppermute | solution.py:34
  44.1 0.6 step.13
  44.7 1.6 %collective-permute-start.5 = (bf16[2,64,512]{2,1,0:T(8,128)(2,1)S(1)}, bf16[2,64,512]{2,1,0:T(8,128)(2,1)S(1)}, u32[]{:S(2)}, u32[]{:S(2)}) collective-permute-start(bf16[2,64,512]{2,1,0:T(8,128)(2,1)S(1)} %get-tuple-element.43), channel_id=1, source_target_pairs={{0,2},{1,3},{2,0},{3,1},{4,6},{5,7},{6,4},{7,5},{8,10},{9,11},{10,... | collective-permute-start | bytes 393224 | tf_op jit(solution)/shard_map/ppermute | solution.py:39
  46.3 3.9 %collective-permute-done.3.refs_1_ = bf16[2,256,2048]{2,1,0:T(8,128)(2,1)} collective-permute-done((bf16[2,256,2048]{2,1,0:T(8,128)(2,1)}, bf16[2,256,2048]{2,1,0:T(8,128)(2,1)}, u32[]{:S(2)}, u32[]{:S(2)}) %collective-permute-start.3) | collective-permute-done | bytes 2097184 | tf_op jit(solution)/shard_map/ppermute | solution.py:34
  50.2 7.1 %step.14 = (f32[4,64,512]{2,1,0:T(8,128)S(1)}, bf16[4,64,512]{2,1,0:T(8,128)(2,1)S(1)}, f32[1,64,512]{2,1,0:T(8,128)S(1)}, bf16[1,64,512]{2,1,0:T(8,128)(2,1)S(1)}, bf16[2,128,2048]{2,1,0:T(8,128)(2,1)S(1)}) custom-call(f32[11]{0:T(128)S(1)} %pad_maximum_fusion.1.table_ref, bf16[2,2,512,2048]{3,2,1,0:T(8,128)(2,1)} %refs_0_.9, ...), custom_call_target="tpu_custom_call" | custom-call | flops 1000 | bytes 1000 | tf_op jit(solution)/shard_map/step/pallas_call | solution.py:343
  57.4 2.1 %collective-permute-start.12 = (bf16[2,128,2048]{2,1,0:T(8,128)(2,1)S(1)}, bf16[2,128,2048]{2,1,0:T(8,128)(2,1)S(1)}, u32[]{:S(2)}, u32[]{:S(2)}) collective-permute-start(bf16[2,128,2048]{2,1,0:T(8,128)(2,1)S(1)} %get-tuple-element.57), channel_id=1, source_target_pairs={{0,24},{8,0},{16,8},{24,16},{1,25},{9,1},{17,9},{25,17},{2,26},{10... | collective-permute-start | bytes 3145736 | tf_op jit(solution)/shard_map/ppermute | solution.py:34
  59.5 1.5 %collective-permute-start.6 = (bf16[4,64,512]{2,1,0:T(8,128)(2,1)S(1)}, bf16[4,64,512]{2,1,0:T(8,128)(2,1)S(1)}, u32[]{:S(2)}, u32[]{:S(2)}) collective-permute-start(bf16[4,64,512]{2,1,0:T(8,128)(2,1)S(1)} %get-tuple-element.45), channel_id=1, source_target_pairs={{0,1},{1,0},{2,3},{3,2},{4,5},{5,4},{6,7},{7,6},{8,9},{9,8},{10,11... | collective-permute-start | bytes 786440 | tf_op jit(solution)/shard_map/ppermute | solution.py:34
  61.0 2.6 %collective-permute-start.7 = (bf16[1,64,512]{2,1,0:T(8,128)(2,1)S(1)}, bf16[1,64,512]{2,1,0:T(8,128)(2,1)S(1)}, u32[]{:S(2)}, u32[]{:S(2)}) collective-permute-start(bf16[1,64,512]{2,1,0:T(8,128)(2,1)S(1)} %get-tuple-element.47), channel_id=1, source_target_pairs={{0,4},{1,5},{2,6},{3,7},{4,0},{5,1},{6,2},{7,3},{8,12},{9,13},{10,... | collective-permute-start | bytes 196616 | tf_op jit(solution)/shard_map/ppermute | solution.py:39
  63.5 3.6 %collective-permute-done.2.refs_1_ = bf16[2,192,2048]{2,1,0:T(8,128)(2,1)} collective-permute-done((bf16[2,192,2048]{2,1,0:T(8,128)(2,1)}, bf16[2,192,2048]{2,1,0:T(8,128)(2,1)}, u32[]{:S(2)}, u32[]{:S(2)}) %collective-permute-start.2) | collective-permute-done | bytes 1572896 | tf_op jit(solution)/shard_map/ppermute | solution.py:34
  67.1 4.4 %step.15 = (bf16[384,2048]{1,0:T(8,128)(2,1)S(1)}, bf16[2,256,2048]{2,1,0:T(8,128)(2,1)S(1)}, bf16[4,64,384]{2,1,0:T(8,128)(2,1)S(1)}, f32[2,64,512]{2,1,0:T(8,1...) custom-call(f32[11]{0:T(128)S(1)} %pad_maximum_fusion.1.table_ref, ...), custom_call_target="tpu_custom_call" | custom-call | flops 1000 | bytes 1000 | tf_op jit(solution)/shard_map/step/pallas_call | solution.py:343
  71.5 1.6 %collective-permute-start.9 = (bf16[4,64,384]{2,1,0:T(8,128)(2,1)S(1)}, bf16[4,64,384]{2,1,0:T(8,128)(2,1)S(1)}, u32[]{:S(2)}, u32[]{:S(2)}) collective-permute-start(bf16[4,64,384]{2,1,0:T(8,128)(2,1)S(1)} %get-tuple-element.52), channel_id=1, source_target_pairs={{0,1},{1,0},{2,3},{3,2},{4,5},{5,4},{6,7},{7,6},{8,9},{9,8},{10,11... | collective-permute-start | bytes 589832 | tf_op jit(solution)/shard_map/ppermute | solution.py:34
  73.1 1.6 %collective-permute-start.8 = (bf16[2,64,512]{2,1,0:T(8,128)(2,1)S(1)}, bf16[2,64,512]{2,1,0:T(8,128)(2,1)S(1)}, u32[]{:S(2)}, u32[]{:S(2)}) collective-permute-start(bf16[2,64,512]{2,1,0:T(8,128)(2,1)S(1)} %get-tuple-element.49), channel_id=1, source_target_pairs={{0,2},{1,3},{2,0},{3,1},{4,6},{5,7},{6,4},{7,5},{8,10},{9,11},{10,... | collective-permute-start | bytes 393224 | tf_op jit(solution)/shard_map/ppermute | solution.py:39
  74.6 1.9 %step.16.refs_0_ = f32[4,64,384]{2,1,0:T(8,128)S(1)} custom-call(f32[11]{0:T(128)S(1)} %pad_maximum_fusion.1.table_ref, bf16[2,256,2048]{2,1,0:T(8,128)(2,1)S(1)} %get-tuple-element.50.refs_0_, bf16[384,2048]{1,0:T(8,128)(2,1)S(1)} %get-tuple-element.51.refs_1_), custom_call_target="tpu_custom_call" | custom-call | flops 1000 | bytes 1000 | tf_op jit(solution)/shard_map/step/pallas_call | solution.py:343
  76.5 2.7 %collective-permute-done.9.refs_1_ = bf16[4,64,384]{2,1,0:T(8,128)(2,1)S(1)} collective-permute-done((bf16[4,64,384]{2,1,0:T(8,128)(2,1)S(1)}, bf16[4,64,384]{2,1,0:T(8,128)(2,1)S(1)}, u32[]{:S(2)}, u32[]{:S(2)}) %collective-permute-start.9) | collective-permute-done | bytes 196640 | tf_op jit(solution)/shard_map/ppermute | solution.py:34
  79.2 0.6 step.17
  79.8 1.6 %collective-permute-start.10 = (bf16[2,64,384]{2,1,0:T(8,128)(2,1)S(1)}, bf16[2,64,384]{2,1,0:T(8,128)(2,1)S(1)}, u32[]{:S(2)}, u32[]{:S(2)}) collective-permute-start(bf16[2,64,384]{2,1,0:T(8,128)(2,1)S(1)} %get-tuple-element.54), channel_id=1, source_target_pairs={{0,2},{1,3},{2,0},{3,1},{4,6},{5,7},{6,4},{7,5},{8,10},{9,11},{10,... | collective-permute-start | bytes 294920 | tf_op jit(solution)/shard_map/ppermute | solution.py:39
  81.5 3.1 %collective-permute-done.10.refs_5_ = bf16[2,64,384]{2,1,0:T(8,128)(2,1)S(1)} collective-permute-done((bf16[2,64,384]{2,1,0:T(8,128)(2,1)S(1)}, bf16[2,64,384]{2,1,0:T(8,128)(2,1)S(1)}, u32[]{:S(2)}, u32[]{:S(2)}) %collective-permute-start.10) | collective-permute-done | bytes 98336 | tf_op jit(solution)/shard_map/ppermute | solution.py:39
  84.6 3.5 %step.18 = (bf16[384,2048]{1,0:T(8,128)(2,1)S(1)}, bf16[2,256,2048]{2,1,0:T(8,128)(2,1)S(1)}, bf16[4,64,384]{2,1,0:T(8,128)(2,1)S(1)}, f32[1,64,896]{2,1,0:T(8,128)S(1)}, bf16[1,64,896]{2,1,0:T(8,128)(2,1)S(1)}) custom-call(f32[11]{0:T(128)S(1)} %pad_maximum_fusion.1.table_ref, bf16[2,2,512,2048]{3,2,1,0:T(8,128)(2,1)} %refs_0_.9, ...), custom_call_target="tpu_custom_call" | custom-call | flops 1000 | bytes 1000 | tf_op jit(solution)/shard_map/step/pallas_call | solution.py:343
  88.1 1.6 %collective-permute-start.13 = (bf16[4,64,384]{2,1,0:T(8,128)(2,1)S(1)}, bf16[4,64,384]{2,1,0:T(8,128)(2,1)S(1)}, u32[]{:S(2)}, u32[]{:S(2)}) collective-permute-start(bf16[4,64,384]{2,1,0:T(8,128)(2,1)S(1)} %get-tuple-element.60), channel_id=1, source_target_pairs={{0,1},{1,0},{2,3},{3,2},{4,5},{5,4},{6,7},{7,6},{8,9},{9,8},{10,11... | collective-permute-start | bytes 589832 | tf_op jit(solution)/shard_map/ppermute | solution.py:34
  89.6 2.6 %collective-permute-start.11 = (bf16[1,64,896]{2,1,0:T(8,128)(2,1)S(1)}, bf16[1,64,896]{2,1,0:T(8,128)(2,1)S(1)}, u32[]{:S(2)}, u32[]{:S(2)}) collective-permute-start(bf16[1,64,896]{2,1,0:T(8,128)(2,1)S(1)} %get-tuple-element.56), channel_id=1, source_target_pairs={{0,4},{1,5},{2,6},{3,7},{4,0},{5,1},{6,2},{7,3},{8,12},{9,13},{10,... | collective-permute-start | bytes 344072 | tf_op jit(solution)/shard_map/ppermute | solution.py:39
  92.2 1.9 %step.19.refs_2_ = f32[4,64,384]{2,1,0:T(8,128)S(1)} custom-call(f32[11]{0:T(128)S(1)} %pad_maximum_fusion.1.table_ref, bf16[2,256,2048]{2,1,0:T(8,128)(2,1)S(1)} %get-tuple-element.58.refs_0_, bf16[384,2048]{1,0:T(8,128)(2,1)S(1)} %get-tuple-element.59.refs_1_), custom_call_target="tpu_custom_call" | custom-call | flops 1000 | bytes 1000 | tf_op jit(solution)/shard_map/step/pallas_call | solution.py:343
  94.1 1.0 collective-permute-done.12.refs_1_
  95.1 2.8 %collective-permute-done.11.refs_5_.refs_1_ = bf16[1,64,896]{2,1,0:T(8,128)(2,1)S(1)} collective-permute-done((bf16[1,64,896]{2,1,0:T(8,128)(2,1)S(1)}, bf16[1,64,896]{2,1,0:T(8,128)(2,1)S(1)}, u32[]{:S(2)}, u32[]{:S(2)}) %collective-permute-start.11) | collective-permute-done | bytes 114720 | tf_op jit(solution)/shard_map/ppermute | solution.py:39
  97.9 3.4 %step.20 = (bf16[256,2048]{1,0:T(8,128)(2,1)S(1)}, bf16[2,256,2048]{2,1,0:T(8,128)(2,1)S(1)}, bf16[4,64,256]{2,1,0:T(8,128)(2,1)S(1)}, f32[2,64,384]{2,1,0:T(8,1...) custom-call(f32[11]{0:T(128)S(1)} %pad_maximum_fusion.1.table_ref, ...), custom_call_target="tpu_custom_call", output_to_operand_aliasing={{5}: (7, {})} | custom-call | flops 1000 | bytes 1000 | tf_op jit(solution)/shard_map/step/pallas_call | solution.py:343
  101.3 0.6 collective-permute-start.14
  101.9 0.7 collective-permute-start.15
  102.5 1.3 %step.21.refs_0_ = f32[4,64,256]{2,1,0:T(8,128)S(1)} custom-call(f32[11]{0:T(128)S(1)} %pad_maximum_fusion.1.table_ref, bf16[2,256,2048]{2,1,0:T(8,128)(2,1)S(1)} %get-tuple-element.62.refs_0_, bf16[256,2048]{1,0:T(8,128)(2,1)S(1)} %get-tuple-element.63.refs_1_), custom_call_target="tpu_custom_call" | custom-call | flops 1000 | bytes 1000 | tf_op jit(solution)/shard_map/step/pallas_call | solution.py:343
  103.8 2.7 %collective-permute-done.15.refs_3_ = bf16[2,64,384]{2,1,0:T(8,128)(2,1)S(1)} collective-permute-done((bf16[2,64,384]{2,1,0:T(8,128)(2,1)S(1)}, bf16[2,64,384]{2,1,0:T(8,128)(2,1)S(1)}, u32[]{:S(2)}, u32[]{:S(2)}) %collective-permute-start.15) | collective-permute-done | bytes 98336 | tf_op jit(solution)/shard_map/ppermute | solution.py:39
  106.5 0.6 step.22
  107.1 2.2 %collective-permute-start.16 = (bf16[1,64,640]{2,1,0:T(8,128)(2,1)S(1)}, bf16[1,64,640]{2,1,0:T(8,128)(2,1)S(1)}, u32[]{:S(2)}, u32[]{:S(2)}) collective-permute-start(bf16[1,64,640]{2,1,0:T(8,128)(2,1)S(1)} %get-tuple-element.68), channel_id=1, source_target_pairs={{0,4},{1,5},{2,6},{3,7},{4,0},{5,1},{6,2},{7,3},{8,12},{9,13},{10,... | collective-permute-start | bytes 245768 | tf_op jit(solution)/shard_map/ppermute | solution.py:39
  109.3 2.2 %collective-permute-start.17 = (bf16[1,64,256]{2,1,0:T(8,128)(2,1)S(1)}, bf16[1,64,256]{2,1,0:T(8,128)(2,1)S(1)}, u32[]{:S(2)}, u32[]{:S(2)}) collective-permute-start(bf16[1,64,256]{2,1,0:T(8,128)(2,1)S(1)} %get-tuple-element.70), channel_id=1, source_target_pairs={{0,2},{1,3},{2,0},{3,1},{4,6},{5,7},{6,4},{7,5},{8,10},{9,11},{10,... | collective-permute-start | bytes 98312 | tf_op jit(solution)/shard_map/ppermute | solution.py:39
  111.5 1.8 %collective-permute-done.17.refs_5_ = bf16[1,64,256]{2,1,0:T(8,128)(2,1)S(1)} collective-permute-done((bf16[1,64,256]{2,1,0:T(8,128)(2,1)S(1)}, bf16[1,64,256]{2,1,0:T(8,128)(2,1)S(1)}, u32[]{:S(2)}, u32[]{:S(2)}) %collective-permute-start.17) | collective-permute-done | bytes 32800 | tf_op jit(solution)/shard_map/ppermute | solution.py:39
  113.4 3.8 %collective-permute-done.18.refs_7_ = bf16[1,64,256]{2,1,0:T(8,128)(2,1)S(1)} collective-permute-done((bf16[1,64,256]{2,1,0:T(8,128)(2,1)S(1)}, bf16[1,64,256]{2,1,0:T(8,128)(2,1)S(1)}, u32[]{:S(2)}, u32[]{:S(2)}) %collective-permute-start.18) | collective-permute-done | bytes 32800 | tf_op jit(solution)/shard_map/ppermute | solution.py:39
  117.2 1.5 %step.23 = f32[64,2,2,512]{3,2,1,0:T(2,128)} custom-call(f32[11]{0:T(128)S(1)} %pad_maximum_fusion.1.table_ref, f32[1,64,896]{2,1,0:T(8,128)S(1)} %get-tuple-element.55.refs_4_.refs_0_, bf16[1,64,896]{2,1,0:T(8,128)(2,1)S(1)} %collective-permute-done.11.refs_5_.refs_1_, f32[1,64,384]{2,1,0:T(8,128)S(1)} %get-tuple-element.67.refs_2_, ...), custom_call_target="tpu_custom_call", output_to_operand_aliasing={{}: (9, {})} | custom-call | flops 1000 | bytes 1000 | tf_op jit(solution)/shard_map/step/pallas_call | solution.py:343
  (17 shorter events, 0.3 us)
Async XLA Ops:
  1.7 26.0 %collective-permute-start = (bf16[2,256,2048]{2,1,0:T(8,128)(2,1)S(1)}, bf16[2,256,2048]{2,1,0:T(8,128)(2,1)}, u32[]{:S(2)}, u32[]{:S(2)}) collective-permute-start(bf16[2,256,2048]{2,1,0:T(8,128)(2,1)S(1)} %piece_of.3.rest_0_), channel_id=1, source_target_pairs={{0,24},{8,0},{16,8},{24,16},{1,25},{9,1},{17,9},{25,17},{2,26},{10... | collective-permute-start | bytes 6291464 | tf_op jit(solution)/shard_map/ppermute | solution.py:34
  6.7 3.1 %copy-start = (s32[2]{0:T(128)S(1)}, s32[2]{0:T(128)}, u32[]{:S(2)}) copy-start(s32[2]{0:T(128)} %param.4) | copy-start | bytes 28
  6.7 3.1 %copy-start.1 = (s32[2]{0:T(128)S(1)}, s32[2]{0:T(128)}, u32[]{:S(2)}) copy-start(s32[2]{0:T(128)} %param.5) | copy-start | bytes 28
  6.7 43.5 %collective-permute-start.3 = (bf16[2,256,2048]{2,1,0:T(8,128)(2,1)}, bf16[2,256,2048]{2,1,0:T(8,128)(2,1)}, u32[]{:S(2)}, u32[]{:S(2)}) collective-permute-start(bf16[2,256,2048]{2,1,0:T(8,128)(2,1)} %piece_of.4.rest_0_), channel_id=1, source_target_pairs={{0,24},{8,0},{16,8},{24,16},{1,25},{9,1},{17,9},{25,17},{2,26},{10... | collective-permute-start | bytes 6291464 | tf_op jit(solution)/shard_map/ppermute | solution.py:34
  9.8 57.3 %collective-permute-start.2 = (bf16[2,192,2048]{2,1,0:T(8,128)(2,1)}, bf16[2,192,2048]{2,1,0:T(8,128)(2,1)}, u32[]{:S(2)}, u32[]{:S(2)}) collective-permute-start(bf16[2,192,2048]{2,1,0:T(8,128)(2,1)} %piece_of.5), channel_id=1, source_target_pairs={{0,24},{8,0},{16,8},{24,16},{1,25},{9,1},{17,9},{25,17},{2,26},{10... | collective-permute-start | bytes 4718600 | tf_op jit(solution)/shard_map/ppermute | solution.py:34
  34.8 49.8 %collective-permute-start.1 = (bf16[2,192,2048]{2,1,0:T(8,128)(2,1)S(1)}, bf16[2,192,2048]{2,1,0:T(8,128)(2,1)S(1)}, u32[]{:S(2)}, u32[]{:S(2)}) collective-permute-start(bf16[2,192,2048]{2,1,0:T(8,128)(2,1)S(1)} %get-tuple-element.39), channel_id=1, source_target_pairs={{0,24},{8,0},{16,8},{24,16},{1,25},{9,1},{17,9},{25,17},{2,26},{10... | collective-permute-start | bytes 4718600 | tf_op jit(solution)/shard_map/ppermute | solution.py:34
  36.8 7.2 %collective-permute-start.4 = (bf16[4,64,512]{2,1,0:T(8,128)(2,1)S(1)}, bf16[4,64,512]{2,1,0:T(8,128)(2,1)S(1)}, u32[]{:S(2)}, u32[]{:S(2)}) collective-permute-start(bf16[4,64,512]{2,1,0:T(8,128)(2,1)S(1)} %get-tuple-element.41), channel_id=1, source_target_pairs={{0,1},{1,0},{2,3},{3,2},{4,5},{5,4},{6,7},{7,6},{8,9},{9,8},{10,11... | collective-permute-start | bytes 786440 | tf_op jit(solution)/shard_map/ppermute | solution.py:34
  44.7 5.6 %collective-permute-start.5 = (bf16[2,64,512]{2,1,0:T(8,128)(2,1)S(1)}, bf16[2,64,512]{2,1,0:T(8,128)(2,1)S(1)}, u32[]{:S(2)}, u32[]{:S(2)}) collective-permute-start(bf16[2,64,512]{2,1,0:T(8,128)(2,1)S(1)} %get-tuple-element.43), channel_id=1, source_target_pairs={{0,2},{1,3},{2,0},{3,1},{4,6},{5,7},{6,4},{7,5},{8,10},{9,11},{10,... | collective-permute-start | bytes 393224 | tf_op jit(solution)/shard_map/ppermute | solution.py:39
  57.4 37.7 %collective-permute-start.12 = (bf16[2,128,2048]{2,1,0:T(8,128)(2,1)S(1)}, bf16[2,128,2048]{2,1,0:T(8,128)(2,1)S(1)}, u32[]{:S(2)}, u32[]{:S(2)}) collective-permute-start(bf16[2,128,2048]{2,1,0:T(8,128)(2,1)S(1)} %get-tuple-element.57), channel_id=1, source_target_pairs={{0,24},{8,0},{16,8},{24,16},{1,25},{9,1},{17,9},{25,17},{2,26},{10... | collective-permute-start | bytes 3145736 | tf_op jit(solution)/shard_map/ppermute | solution.py:34
  59.5 7.6 %collective-permute-start.6 = (bf16[4,64,512]{2,1,0:T(8,128)(2,1)S(1)}, bf16[4,64,512]{2,1,0:T(8,128)(2,1)S(1)}, u32[]{:S(2)}, u32[]{:S(2)}) collective-permute-start(bf16[4,64,512]{2,1,0:T(8,128)(2,1)S(1)} %get-tuple-element.45), channel_id=1, source_target_pairs={{0,1},{1,0},{2,3},{3,2},{4,5},{5,4},{6,7},{7,6},{8,9},{9,8},{10,11... | collective-permute-start | bytes 786440 | tf_op jit(solution)/shard_map/ppermute | solution.py:34
  61.0 6.1 %collective-permute-start.7 = (bf16[1,64,512]{2,1,0:T(8,128)(2,1)S(1)}, bf16[1,64,512]{2,1,0:T(8,128)(2,1)S(1)}, u32[]{:S(2)}, u32[]{:S(2)}) collective-permute-start(bf16[1,64,512]{2,1,0:T(8,128)(2,1)S(1)} %get-tuple-element.47), channel_id=1, source_target_pairs={{0,4},{1,5},{2,6},{3,7},{4,0},{5,1},{6,2},{7,3},{8,12},{9,13},{10,... | collective-permute-start | bytes 196616 | tf_op jit(solution)/shard_map/ppermute | solution.py:39
  71.5 7.7 %collective-permute-start.9 = (bf16[4,64,384]{2,1,0:T(8,128)(2,1)S(1)}, bf16[4,64,384]{2,1,0:T(8,128)(2,1)S(1)}, u32[]{:S(2)}, u32[]{:S(2)}) collective-permute-start(bf16[4,64,384]{2,1,0:T(8,128)(2,1)S(1)} %get-tuple-element.52), channel_id=1, source_target_pairs={{0,1},{1,0},{2,3},{3,2},{4,5},{5,4},{6,7},{7,6},{8,9},{9,8},{10,11... | collective-permute-start | bytes 589832 | tf_op jit(solution)/shard_map/ppermute | solution.py:34
  73.1 8.4 %collective-permute-start.8 = (bf16[2,64,512]{2,1,0:T(8,128)(2,1)S(1)}, bf16[2,64,512]{2,1,0:T(8,128)(2,1)S(1)}, u32[]{:S(2)}, u32[]{:S(2)}) collective-permute-start(bf16[2,64,512]{2,1,0:T(8,128)(2,1)S(1)} %get-tuple-element.49), channel_id=1, source_target_pairs={{0,2},{1,3},{2,0},{3,1},{4,6},{5,7},{6,4},{7,5},{8,10},{9,11},{10,... | collective-permute-start | bytes 393224 | tf_op jit(solution)/shard_map/ppermute | solution.py:39
  79.8 4.7 %collective-permute-start.10 = (bf16[2,64,384]{2,1,0:T(8,128)(2,1)S(1)}, bf16[2,64,384]{2,1,0:T(8,128)(2,1)S(1)}, u32[]{:S(2)}, u32[]{:S(2)}) collective-permute-start(bf16[2,64,384]{2,1,0:T(8,128)(2,1)S(1)} %get-tuple-element.54), channel_id=1, source_target_pairs={{0,2},{1,3},{2,0},{3,1},{4,6},{5,7},{6,4},{7,5},{8,10},{9,11},{10,... | collective-permute-start | bytes 294920 | tf_op jit(solution)/shard_map/ppermute | solution.py:39
  88.1 9.8 %collective-permute-start.13 = (bf16[4,64,384]{2,1,0:T(8,128)(2,1)S(1)}, bf16[4,64,384]{2,1,0:T(8,128)(2,1)S(1)}, u32[]{:S(2)}, u32[]{:S(2)}) collective-permute-start(bf16[4,64,384]{2,1,0:T(8,128)(2,1)S(1)} %get-tuple-element.60), channel_id=1, source_target_pairs={{0,1},{1,0},{2,3},{3,2},{4,5},{5,4},{6,7},{7,6},{8,9},{9,8},{10,11... | collective-permute-start | bytes 589832 | tf_op jit(solution)/shard_map/ppermute | solution.py:34
  89.6 8.2 %collective-permute-start.11 = (bf16[1,64,896]{2,1,0:T(8,128)(2,1)S(1)}, bf16[1,64,896]{2,1,0:T(8,128)(2,1)S(1)}, u32[]{:S(2)}, u32[]{:S(2)}) collective-permute-start(bf16[1,64,896]{2,1,0:T(8,128)(2,1)S(1)} %get-tuple-element.56), channel_id=1, source_target_pairs={{0,4},{1,5},{2,6},{3,7},{4,0},{5,1},{6,2},{7,3},{8,12},{9,13},{10,... | collective-permute-start | bytes 344072 | tf_op jit(solution)/shard_map/ppermute | solution.py:39
  101.3 5.2 %collective-permute-start.14 = (bf16[4,64,256]{2,1,0:T(8,128)(2,1)S(1)}, bf16[4,64,256]{2,1,0:T(8,128)(2,1)S(1)}, u32[]{:S(2)}, u32[]{:S(2)}) collective-permute-start(bf16[4,64,256]{2,1,0:T(8,128)(2,1)S(1)} %get-tuple-element.64), channel_id=1, source_target_pairs={{0,1},{1,0},{2,3},{3,2},{4,5},{5,4},{6,7},{7,6},{8,9},{9,8},{10,11... | collective-permute-start | bytes 393224 | tf_op jit(solution)/shard_map/ppermute | solution.py:34
  101.9 4.6 %collective-permute-start.15 = (bf16[2,64,384]{2,1,0:T(8,128)(2,1)S(1)}, bf16[2,64,384]{2,1,0:T(8,128)(2,1)S(1)}, u32[]{:S(2)}, u32[]{:S(2)}) collective-permute-start(bf16[2,64,384]{2,1,0:T(8,128)(2,1)S(1)} %get-tuple-element.66), channel_id=1, source_target_pairs={{0,2},{1,3},{2,0},{3,1},{4,6},{5,7},{6,4},{7,5},{8,10},{9,11},{10,... | collective-permute-start | bytes 294920 | tf_op jit(solution)/shard_map/ppermute | solution.py:39
  107.1 10.1 %collective-permute-start.16 = (bf16[1,64,640]{2,1,0:T(8,128)(2,1)S(1)}, bf16[1,64,640]{2,1,0:T(8,128)(2,1)S(1)}, u32[]{:S(2)}, u32[]{:S(2)}) collective-permute-start(bf16[1,64,640]{2,1,0:T(8,128)(2,1)S(1)} %get-tuple-element.68), channel_id=1, source_target_pairs={{0,4},{1,5},{2,6},{3,7},{4,0},{5,1},{6,2},{7,3},{8,12},{9,13},{10,... | collective-permute-start | bytes 245768 | tf_op jit(solution)/shard_map/ppermute | solution.py:39
  109.3 4.1 %collective-permute-start.17 = (bf16[1,64,256]{2,1,0:T(8,128)(2,1)S(1)}, bf16[1,64,256]{2,1,0:T(8,128)(2,1)S(1)}, u32[]{:S(2)}, u32[]{:S(2)}) collective-permute-start(bf16[1,64,256]{2,1,0:T(8,128)(2,1)S(1)} %get-tuple-element.70), channel_id=1, source_target_pairs={{0,2},{1,3},{2,0},{3,1},{4,6},{5,7},{6,4},{7,5},{8,10},{9,11},{10,... | collective-permute-start | bytes 98312 | tf_op jit(solution)/shard_map/ppermute | solution.py:39
  111.5 5.7 %collective-permute-start.18 = (bf16[1,64,256]{2,1,0:T(8,128)(2,1)S(1)}, bf16[1,64,256]{2,1,0:T(8,128)(2,1)S(1)}, u32[]{:S(2)}, u32[]{:S(2)}) collective-permute-start(bf16[1,64,256]{2,1,0:T(8,128)(2,1)S(1)} %get-tuple-element.71), channel_id=1, source_target_pairs={{0,6},{1,7},{2,4},{3,5},{4,2},{5,3},{6,0},{7,1},{8,14},{9,15},{10,... | collective-permute-start | bytes 98312 | tf_op jit(solution)/shard_map/ppermute | solution.py:39

commit v17 on v16

--- a/solution.py
+++ b/solution.py
@@ -17,6 +17,7 @@
 OUTER = 4
 SPLIT = 128
 JOINT = 2
+CHUNKS = 4
 LANES = 128
 BLOCK = 256
 VMEM_BYTES = 46 * 1024 * 1024
@@ -41,16 +42,15 @@
 
 def piece_kernel(slot, start, bands_ref, *rest):
     out_ref, piece_buf, sems = rest[-3:]
-    width = piece_buf.shape[1]
-    rows = pl.ds(start, width)
-    loads = [
-        pltpu.make_async_copy(bands_ref.at[slot, part, rows, :], piece_buf.at[part], sems.at[0, part])
-        for part in range(2)
-    ]
-    stores = [
-        pltpu.make_async_copy(piece_buf.at[part], out_ref.at[part], sems.at[1, part])
-        for part in range(2)
-    ]
+    width = piece_buf.shape[1] // CHUNKS
+    loads, stores = [], []
+    for index in range(2 * CHUNKS):
+        part, chunk = divmod(index, CHUNKS)
+        lines = pl.ds(chunk * width, width)
+        source = bands_ref.at[slot, part, pl.ds(start + chunk * width, width), :]
+        buf = piece_buf.at[part, lines, :]
+        loads.append(pltpu.make_async_copy(source, buf, sems.at[0, index]))
+        stores.append(pltpu.make_async_copy(buf, out_ref.at[part, lines, :], sems.at[1, index]))
     for load in loads:
         load.start()
     for load, store in zip(loads, stores):
@@ -68,7 +68,7 @@
         out_specs=pl.BlockSpec(memory_space=pl.ANY),
         scratch_shapes=[
             pltpu.VMEM((2, width, points), bands.dtype),
-            pltpu.SemaphoreType.DMA((2, 2)),
+            pltpu.SemaphoreType.DMA((2, 2 * CHUNKS)),
         ],
         out_shape=jax.ShapeDtypeStruct((2, width, points), bands.dtype),
         compiler_params=pltpu.CompilerParams(vmem_limit_bytes=VMEM_BYTES),
@@ -487,9 +487,8 @@
             held.setdefault((part,), []).insert(0 if way == 0 else fold, (array, 0))
         for task, arrays in zip(tasks, sends):
             steps = range(1, depth) if task.direct else [1 << task.stage]
-            held[task.batch] = [(arrays[0], 0)] + [
-                (swapped(array, "ga", fold * i), 0) for array, i in zip(arrays[1:], steps)
-            ]
+            moved = [swapped(array, "ga", fold * i) for array, i in zip(arrays[1:], steps)]
+            held[task.batch] = [(array, 0) for array in [arrays[0], *reversed(moved)]]
         if plan.joined:
             joint = held[tasks[0].batch][JOINT][0]
             held[tasks[1].batch].append((joint, 2 * tasks[0].batch[0][2]))

time: 119 us -> 117 us (0.983)
  waiting for transfers between devices: 48.3 us -> 46.6 us
    ppermute x9, waiting for transfers between devices: 14.2 us -> 12.3 us  [swapped(): return lax.ppermute(block, axis, [(i, i ^ distance) for i in range(count)])]
where the time goes in v17:
time: 117 us
  waiting for transfers between devices  46.6 us (40%)
  Pallas kernels  40.1 us (34%)
  starting transfers between devices  29.3 us (25%)
    ppermute x10, waiting for transfers between devices, shifted(): return lax.ppermute(block, axis, route)  34.3 us
    pallas_call x12, Pallas kernels, step(): pl.pallas_call(functools.partial(step_kernel, plan), in_specs=in_specs, o...  33.8 us
    ppermute x9, starting transfers between devices, swapped(): return lax.ppermute(block, axis, [(i, i ^ distance) for i in range(count)])  15.1 us
    ppermute x10, starting transfers between devices, shifted(): return lax.ppermute(block, axis, route)  14.2 us
    ppermute x9, waiting for transfers between devices, swapped(): return lax.ppermute(block, axis, [(i, i ^ distance) for i in range(count)])  12.3 us
    pallas_call x3, Pallas kernels, piece_of(): pl.pallas_call(functools.partial(piece_kernel, slot, start), in_specs=[pl...  6.37 us
  transfers between devices with their start and end apart: 19, of which 11 were waited for; matrix products, arithmetic and copies ran while one was open for 1% of the time, Pallas kernels for 28%

profile of v17, /device:TPU:0, one launch (start us, length us, event | category | flops | bytes accessed | tf_op | source)
XLA Modules:
  0.0 116.9 jit_solution(2895793621190390947)
XLA Ops:
  0.0 1.7 %piece_of.3.rest_0_ = bf16[2,256,2048]{2,1,0:T(8,128)(2,1)S(1)} custom-call(bf16[2,2,512,2048]{3,2,1,0:T(8,128)(2,1)} %refs_0_.9), custom_call_target="tpu_custom_call" | custom-call | flops 1000 | bytes 1000 | tf_op jit(solution)/shard_map/piece_of/pallas_call | solution.py:65
  1.7 2.5 %collective-permute-start = (bf16[2,256,2048]{2,1,0:T(8,128)(2,1)S(1)}, bf16[2,256,2048]{2,1,0:T(8,128)(2,1)}, u32[]{:S(2)}, u32[]{:S(2)}) collective-permute-start(bf16[2,256,2048]{2,1,0:T(8,128)(2,1)S(1)} %piece_of.3.rest_0_), channel_id=1, source_target_pairs={{0,24},{8,0},{16,8},{24,16},{1,25},{9,1},{17,9},{25,17},{2,26},{10... | collective-permute-start | bytes 6291464 | tf_op jit(solution)/shard_map/ppermute | solution.py:35
  4.1 2.4 %piece_of.4.rest_0_ = bf16[2,256,2048]{2,1,0:T(8,128)(2,1)} custom-call(bf16[2,2,512,2048]{3,2,1,0:T(8,128)(2,1)} %refs_0_.9, bf16[2,256,2048]{2,1,0:T(8,128)(2,1)S(1)} %piece_of.3.rest_0_), custom_call_target="tpu_custom_call" | custom-call | flops 1000 | bytes 1000 | tf_op jit(solution)/shard_map/piece_of/pallas_call | solution.py:65
  6.6 0.7 collective-permute-start.3
  7.3 2.3 %piece_of.5 = bf16[2,192,2048]{2,1,0:T(8,128)(2,1)} custom-call(bf16[2,2,512,2048]{3,2,1,0:T(8,128)(2,1)} %refs_0_.9, bf16[2,256,2048]{2,1,0:T(8,128)(2,1)} %piece_of.4.rest_0_), custom_call_target="tpu_custom_call" | custom-call | flops 1000 | bytes 1000 | tf_op jit(solution)/shard_map/piece_of/pallas_call | solution.py:65
  9.7 0.1 select_reduce_fusion.1
  9.9 0.1 fusion.4
  10.0 0.1 copy.6
  10.2 0.1 reshape.28
  10.3 17.4 %collective-permute-done.refs_1_ = bf16[2,256,2048]{2,1,0:T(8,128)(2,1)} collective-permute-done((bf16[2,256,2048]{2,1,0:T(8,128)(2,1)S(1)}, bf16[2,256,2048]{2,1,0:T(8,128)(2,1)}, u32[]{:S(2)}, u32[]{:S(2)}) %collective-permute-start) | collective-permute-done | bytes 2097184 | tf_op jit(solution)/shard_map/ppermute | solution.py:35
  27.7 7.1 %step.12 = (f32[4,64,512]{2,1,0:T(8,128)S(1)}, bf16[4,64,512]{2,1,0:T(8,128)(2,1)S(1)}, bf16[2,192,2048]{2,1,0:T(8,128)(2,1)S(1)}) custom-call(f32[11]{0:T(128)S(1)} %pad_maximum_fusion.1.table_ref, bf16[2,2,512,2048]{3,2,1,0:T(8,128)(2,1)} %refs_0_.9, bf16[2,256,2048]{2,1,0:T(8,128)(2,1)} %collective-permute-done.refs_1_), custom_call_target="tpu_custom_call" | custom-call | flops 1000 | bytes 1000 | tf_op jit(solution)/shard_map/step/pallas_call | solution.py:343
  34.8 2.1 %collective-permute-start.1 = (bf16[2,192,2048]{2,1,0:T(8,128)(2,1)S(1)}, bf16[2,192,2048]{2,1,0:T(8,128)(2,1)S(1)}, u32[]{:S(2)}, u32[]{:S(2)}) collective-permute-start(bf16[2,192,2048]{2,1,0:T(8,128)(2,1)S(1)} %get-tuple-element.39), channel_id=1, source_target_pairs={{0,24},{8,0},{16,8},{24,16},{1,25},{9,1},{17,9},{25,17},{2,26},{10... | collective-permute-start | bytes 4718600 | tf_op jit(solution)/shard_map/ppermute | solution.py:35
  36.9 1.5 %collective-permute-start.4 = (bf16[4,64,512]{2,1,0:T(8,128)(2,1)S(1)}, bf16[4,64,512]{2,1,0:T(8,128)(2,1)S(1)}, u32[]{:S(2)}, u32[]{:S(2)}) collective-permute-start(bf16[4,64,512]{2,1,0:T(8,128)(2,1)S(1)} %get-tuple-element.41), channel_id=1, source_target_pairs={{0,1},{1,0},{2,3},{3,2},{4,5},{5,4},{6,7},{7,6},{8,9},{9,8},{10,11... | collective-permute-start | bytes 786440 | tf_op jit(solution)/shard_map/ppermute | solution.py:35
  38.4 5.7 %collective-permute-done.4.refs_1_ = bf16[4,64,512]{2,1,0:T(8,128)(2,1)S(1)} collective-permute-done((bf16[4,64,512]{2,1,0:T(8,128)(2,1)S(1)}, bf16[4,64,512]{2,1,0:T(8,128)(2,1)S(1)}, u32[]{:S(2)}, u32[]{:S(2)}) %collective-permute-start.4) | collective-permute-done | bytes 262176 | tf_op jit(solution)/shard_map/ppermute | solution.py:35
  44.1 0.6 step.13
  44.7 1.6 %collective-permute-start.5 = (bf16[2,64,512]{2,1,0:T(8,128)(2,1)S(1)}, bf16[2,64,512]{2,1,0:T(8,128)(2,1)S(1)}, u32[]{:S(2)}, u32[]{:S(2)}) collective-permute-start(bf16[2,64,512]{2,1,0:T(8,128)(2,1)S(1)} %get-tuple-element.43), channel_id=1, source_target_pairs={{0,2},{1,3},{2,0},{3,1},{4,6},{5,7},{6,4},{7,5},{8,10},{9,11},{10,... | collective-permute-start | bytes 393224 | tf_op jit(solution)/shard_map/ppermute | solution.py:40
  46.3 3.9 %collective-permute-done.3.refs_1_ = bf16[2,256,2048]{2,1,0:T(8,128)(2,1)} collective-permute-done((bf16[2,256,2048]{2,1,0:T(8,128)(2,1)}, bf16[2,256,2048]{2,1,0:T(8,128)(2,1)}, u32[]{:S(2)}, u32[]{:S(2)}) %collective-permute-start.3) | collective-permute-done | bytes 2097184 | tf_op jit(solution)/shard_map/ppermute | solution.py:35
  50.3 7.1 %step.14 = (f32[4,64,512]{2,1,0:T(8,128)S(1)}, bf16[4,64,512]{2,1,0:T(8,128)(2,1)S(1)}, f32[1,64,512]{2,1,0:T(8,128)S(1)}, bf16[1,64,512]{2,1,0:T(8,128)(2,1)S(1)}, bf16[2,128,2048]{2,1,0:T(8,128)(2,1)S(1)}) custom-call(f32[11]{0:T(128)S(1)} %pad_maximum_fusion.1.table_ref, bf16[2,2,512,2048]{3,2,1,0:T(8,128)(2,1)} %refs_0_.9, ...), custom_call_target="tpu_custom_call" | custom-call | flops 1000 | bytes 1000 | tf_op jit(solution)/shard_map/step/pallas_call | solution.py:343
  57.3 2.1 %collective-permute-start.12 = (bf16[2,128,2048]{2,1,0:T(8,128)(2,1)S(1)}, bf16[2,128,2048]{2,1,0:T(8,128)(2,1)S(1)}, u32[]{:S(2)}, u32[]{:S(2)}) collective-permute-start(bf16[2,128,2048]{2,1,0:T(8,128)(2,1)S(1)} %get-tuple-element.57), channel_id=1, source_target_pairs={{0,24},{8,0},{16,8},{24,16},{1,25},{9,1},{17,9},{25,17},{2,26},{10... | collective-permute-start | bytes 3145736 | tf_op jit(solution)/shard_map/ppermute | solution.py:35
  59.5 1.5 %collective-permute-start.6 = (bf16[4,64,512]{2,1,0:T(8,128)(2,1)S(1)}, bf16[4,64,512]{2,1,0:T(8,128)(2,1)S(1)}, u32[]{:S(2)}, u32[]{:S(2)}) collective-permute-start(bf16[4,64,512]{2,1,0:T(8,128)(2,1)S(1)} %get-tuple-element.45), channel_id=1, source_target_pairs={{0,1},{1,0},{2,3},{3,2},{4,5},{5,4},{6,7},{7,6},{8,9},{9,8},{10,11... | collective-permute-start | bytes 786440 | tf_op jit(solution)/shard_map/ppermute | solution.py:35
  61.0 2.6 %collective-permute-start.7 = (bf16[1,64,512]{2,1,0:T(8,128)(2,1)S(1)}, bf16[1,64,512]{2,1,0:T(8,128)(2,1)S(1)}, u32[]{:S(2)}, u32[]{:S(2)}) collective-permute-start(bf16[1,64,512]{2,1,0:T(8,128)(2,1)S(1)} %get-tuple-element.47), channel_id=1, source_target_pairs={{0,4},{1,5},{2,6},{3,7},{4,0},{5,1},{6,2},{7,3},{8,12},{9,13},{10,... | collective-permute-start | bytes 196616 | tf_op jit(solution)/shard_map/ppermute | solution.py:40
  63.6 3.6 %collective-permute-done.2.refs_1_ = bf16[2,192,2048]{2,1,0:T(8,128)(2,1)} collective-permute-done((bf16[2,192,2048]{2,1,0:T(8,128)(2,1)}, bf16[2,192,2048]{2,1,0:T(8,128)(2,1)}, u32[]{:S(2)}, u32[]{:S(2)}) %collective-permute-start.2) | collective-permute-done | bytes 1572896 | tf_op jit(solution)/shard_map/ppermute | solution.py:35
  67.1 4.4 %step.15 = (bf16[384,2048]{1,0:T(8,128)(2,1)S(1)}, bf16[2,256,2048]{2,1,0:T(8,128)(2,1)S(1)}, bf16[4,64,384]{2,1,0:T(8,128)(2,1)S(1)}, f32[2,64,512]{2,1,0:T(8,1...) custom-call(f32[11]{0:T(128)S(1)} %pad_maximum_fusion.1.table_ref, ...), custom_call_target="tpu_custom_call" | custom-call | flops 1000 | bytes 1000 | tf_op jit(solution)/shard_map/step/pallas_call | solution.py:343
  71.5 1.6 %collective-permute-start.9 = (bf16[4,64,384]{2,1,0:T(8,128)(2,1)S(1)}, bf16[4,64,384]{2,1,0:T(8,128)(2,1)S(1)}, u32[]{:S(2)}, u32[]{:S(2)}) collective-permute-start(bf16[4,64,384]{2,1,0:T(8,128)(2,1)S(1)} %get-tuple-element.52), channel_id=1, source_target_pairs={{0,1},{1,0},{2,3},{3,2},{4,5},{5,4},{6,7},{7,6},{8,9},{9,8},{10,11... | collective-permute-start | bytes 589832 | tf_op jit(solution)/shard_map/ppermute | solution.py:35
  73.1 1.6 %collective-permute-start.8 = (bf16[2,64,512]{2,1,0:T(8,128)(2,1)S(1)}, bf16[2,64,512]{2,1,0:T(8,128)(2,1)S(1)}, u32[]{:S(2)}, u32[]{:S(2)}) collective-permute-start(bf16[2,64,512]{2,1,0:T(8,128)(2,1)S(1)} %get-tuple-element.49), channel_id=1, source_target_pairs={{0,2},{1,3},{2,0},{3,1},{4,6},{5,7},{6,4},{7,5},{8,10},{9,11},{10,... | collective-permute-start | bytes 393224 | tf_op jit(solution)/shard_map/ppermute | solution.py:40
  74.7 1.9 %step.16.refs_0_ = f32[4,64,384]{2,1,0:T(8,128)S(1)} custom-call(f32[11]{0:T(128)S(1)} %pad_maximum_fusion.1.table_ref, bf16[2,256,2048]{2,1,0:T(8,128)(2,1)S(1)} %get-tuple-element.50.refs_0_, bf16[384,2048]{1,0:T(8,128)(2,1)S(1)} %get-tuple-element.51.refs_1_), custom_call_target="tpu_custom_call" | custom-call | flops 1000 | bytes 1000 | tf_op jit(solution)/shard_map/step/pallas_call | solution.py:343
  76.6 2.7 %collective-permute-done.9.refs_1_ = bf16[4,64,384]{2,1,0:T(8,128)(2,1)S(1)} collective-permute-done((bf16[4,64,384]{2,1,0:T(8,128)(2,1)S(1)}, bf16[4,64,384]{2,1,0:T(8,128)(2,1)S(1)}, u32[]{:S(2)}, u32[]{:S(2)}) %collective-permute-start.9) | collective-permute-done | bytes 196640 | tf_op jit(solution)/shard_map/ppermute | solution.py:35
  79.3 0.6 step.17
  79.8 1.6 %collective-permute-start.10 = (bf16[2,64,384]{2,1,0:T(8,128)(2,1)S(1)}, bf16[2,64,384]{2,1,0:T(8,128)(2,1)S(1)}, u32[]{:S(2)}, u32[]{:S(2)}) collective-permute-start(bf16[2,64,384]{2,1,0:T(8,128)(2,1)S(1)} %get-tuple-element.54), channel_id=1, source_target_pairs={{0,2},{1,3},{2,0},{3,1},{4,6},{5,7},{6,4},{7,5},{8,10},{9,11},{10,... | collective-permute-start | bytes 294920 | tf_op jit(solution)/shard_map/ppermute | solution.py:40
  81.5 3.1 %collective-permute-done.10.refs_5_ = bf16[2,64,384]{2,1,0:T(8,128)(2,1)S(1)} collective-permute-done((bf16[2,64,384]{2,1,0:T(8,128)(2,1)S(1)}, bf16[2,64,384]{2,1,0:T(8,128)(2,1)S(1)}, u32[]{:S(2)}, u32[]{:S(2)}) %collective-permute-start.10) | collective-permute-done | bytes 98336 | tf_op jit(solution)/shard_map/ppermute | solution.py:40
  84.6 3.5 %step.18 = (bf16[384,2048]{1,0:T(8,128)(2,1)S(1)}, bf16[2,256,2048]{2,1,0:T(8,128)(2,1)S(1)}, bf16[4,64,384]{2,1,0:T(8,128)(2,1)S(1)}, f32[1,64,896]{2,1,0:T(8,128)S(1)}, bf16[1,64,896]{2,1,0:T(8,128)(2,1)S(1)}) custom-call(f32[11]{0:T(128)S(1)} %pad_maximum_fusion.1.table_ref, bf16[2,2,512,2048]{3,2,1,0:T(8,128)(2,1)} %refs_0_.9, ...), custom_call_target="tpu_custom_call" | custom-call | flops 1000 | bytes 1000 | tf_op jit(solution)/shard_map/step/pallas_call | solution.py:343
  88.1 1.6 %collective-permute-start.13 = (bf16[4,64,384]{2,1,0:T(8,128)(2,1)S(1)}, bf16[4,64,384]{2,1,0:T(8,128)(2,1)S(1)}, u32[]{:S(2)}, u32[]{:S(2)}) collective-permute-start(bf16[4,64,384]{2,1,0:T(8,128)(2,1)S(1)} %get-tuple-element.60), channel_id=1, source_target_pairs={{0,1},{1,0},{2,3},{3,2},{4,5},{5,4},{6,7},{7,6},{8,9},{9,8},{10,11... | collective-permute-start | bytes 589832 | tf_op jit(solution)/shard_map/ppermute | solution.py:35
  89.6 2.6 %collective-permute-start.11 = (bf16[1,64,896]{2,1,0:T(8,128)(2,1)S(1)}, bf16[1,64,896]{2,1,0:T(8,128)(2,1)S(1)}, u32[]{:S(2)}, u32[]{:S(2)}) collective-permute-start(bf16[1,64,896]{2,1,0:T(8,128)(2,1)S(1)} %get-tuple-element.56), channel_id=1, source_target_pairs={{0,4},{1,5},{2,6},{3,7},{4,0},{5,1},{6,2},{7,3},{8,12},{9,13},{10,... | collective-permute-start | bytes 344072 | tf_op jit(solution)/shard_map/ppermute | solution.py:40
  92.2 1.9 %step.19.refs_2_ = f32[4,64,384]{2,1,0:T(8,128)S(1)} custom-call(f32[11]{0:T(128)S(1)} %pad_maximum_fusion.1.table_ref, bf16[2,256,2048]{2,1,0:T(8,128)(2,1)S(1)} %get-tuple-element.58.refs_0_, bf16[384,2048]{1,0:T(8,128)(2,1)S(1)} %get-tuple-element.59.refs_1_), custom_call_target="tpu_custom_call" | custom-call | flops 1000 | bytes 1000 | tf_op jit(solution)/shard_map/step/pallas_call | solution.py:343
  94.1 1.0 collective-permute-done.12.refs_1_
  95.1 2.8 %collective-permute-done.11.refs_5_.refs_1_ = bf16[1,64,896]{2,1,0:T(8,128)(2,1)S(1)} collective-permute-done((bf16[1,64,896]{2,1,0:T(8,128)(2,1)S(1)}, bf16[1,64,896]{2,1,0:T(8,128)(2,1)S(1)}, u32[]{:S(2)}, u32[]{:S(2)}) %collective-permute-start.11) | collective-permute-done | bytes 114720 | tf_op jit(solution)/shard_map/ppermute | solution.py:40
  97.9 3.4 %step.20 = (bf16[256,2048]{1,0:T(8,128)(2,1)S(1)}, bf16[2,256,2048]{2,1,0:T(8,128)(2,1)S(1)}, bf16[4,64,256]{2,1,0:T(8,128)(2,1)S(1)}, f32[2,64,384]{2,1,0:T(8,1...) custom-call(f32[11]{0:T(128)S(1)} %pad_maximum_fusion.1.table_ref, ...), custom_call_target="tpu_custom_call", output_to_operand_aliasing={{5}: (7, {})} | custom-call | flops 1000 | bytes 1000 | tf_op jit(solution)/shard_map/step/pallas_call | solution.py:343
  101.3 0.6 collective-permute-start.14
  101.9 0.7 collective-permute-start.15
  102.6 1.3 %step.21.refs_0_ = f32[4,64,256]{2,1,0:T(8,128)S(1)} custom-call(f32[11]{0:T(128)S(1)} %pad_maximum_fusion.1.table_ref, bf16[2,256,2048]{2,1,0:T(8,128)(2,1)S(1)} %get-tuple-element.62.refs_0_, bf16[256,2048]{1,0:T(8,128)(2,1)S(1)} %get-tuple-element.63.refs_1_), custom_call_target="tpu_custom_call" | custom-call | flops 1000 | bytes 1000 | tf_op jit(solution)/shard_map/step/pallas_call | solution.py:343
  103.9 2.6 %collective-permute-done.15.refs_3_ = bf16[2,64,384]{2,1,0:T(8,128)(2,1)S(1)} collective-permute-done((bf16[2,64,384]{2,1,0:T(8,128)(2,1)S(1)}, bf16[2,64,384]{2,1,0:T(8,128)(2,1)S(1)}, u32[]{:S(2)}, u32[]{:S(2)}) %collective-permute-start.15) | collective-permute-done | bytes 98336 | tf_op jit(solution)/shard_map/ppermute | solution.py:40
  106.5 0.6 step.22
  107.1 2.2 %collective-permute-start.16 = (bf16[1,64,640]{2,1,0:T(8,128)(2,1)S(1)}, bf16[1,64,640]{2,1,0:T(8,128)(2,1)S(1)}, u32[]{:S(2)}, u32[]{:S(2)}) collective-permute-start(bf16[1,64,640]{2,1,0:T(8,128)(2,1)S(1)} %get-tuple-element.68), channel_id=1, source_target_pairs={{0,4},{1,5},{2,6},{3,7},{4,0},{5,1},{6,2},{7,3},{8,12},{9,13},{10,... | collective-permute-start | bytes 245768 | tf_op jit(solution)/shard_map/ppermute | solution.py:40
  109.3 1.7 %collective-permute-start.17 = (bf16[1,64,256]{2,1,0:T(8,128)(2,1)S(1)}, bf16[1,64,256]{2,1,0:T(8,128)(2,1)S(1)}, u32[]{:S(2)}, u32[]{:S(2)}) collective-permute-start(bf16[1,64,256]{2,1,0:T(8,128)(2,1)S(1)} %get-tuple-element.70), channel_id=1, source_target_pairs={{0,6},{1,7},{2,4},{3,5},{4,2},{5,3},{6,0},{7,1},{8,14},{9,15},{10,... | collective-permute-start | bytes 98312 | tf_op jit(solution)/shard_map/ppermute | solution.py:40
  111.0 0.5 collective-permute-start.18
  111.5 3.7 %collective-permute-done.17.refs_5_ = bf16[1,64,256]{2,1,0:T(8,128)(2,1)S(1)} collective-permute-done((bf16[1,64,256]{2,1,0:T(8,128)(2,1)S(1)}, bf16[1,64,256]{2,1,0:T(8,128)(2,1)S(1)}, u32[]{:S(2)}, u32[]{:S(2)}) %collective-permute-start.17) | collective-permute-done | bytes 32800 | tf_op jit(solution)/shard_map/ppermute | solution.py:40
  115.2 0.1 collective-permute-done.18.refs_7_
  115.3 1.5 %step.23 = f32[64,2,2,512]{3,2,1,0:T(2,128)} custom-call(f32[11]{0:T(128)S(1)} %pad_maximum_fusion.1.table_ref, f32[1,64,896]{2,1,0:T(8,128)S(1)} %get-tuple-element.55.refs_4_.refs_0_, bf16[1,64,896]{2,1,0:T(8,128)(2,1)S(1)} %collective-permute-done.11.refs_5_.refs_1_, f32[1,64,384]{2,1,0:T(8,128)S(1)} %get-tuple-element.67.refs_2_, ...), custom_call_target="tpu_custom_call", output_to_operand_aliasing={{}: (9, {})} | custom-call | flops 1000 | bytes 1000 | tf_op jit(solution)/shard_map/step/pallas_call | solution.py:343
  (17 shorter events, 0.3 us)
Async XLA Ops:
  1.7 26.0 %collective-permute-start = (bf16[2,256,2048]{2,1,0:T(8,128)(2,1)S(1)}, bf16[2,256,2048]{2,1,0:T(8,128)(2,1)}, u32[]{:S(2)}, u32[]{:S(2)}) collective-permute-start(bf16[2,256,2048]{2,1,0:T(8,128)(2,1)S(1)} %piece_of.3.rest_0_), channel_id=1, source_target_pairs={{0,24},{8,0},{16,8},{24,16},{1,25},{9,1},{17,9},{25,17},{2,26},{10... | collective-permute-start | bytes 6291464 | tf_op jit(solution)/shard_map/ppermute | solution.py:35
  6.5 3.1 %copy-start = (s32[2]{0:T(128)S(1)}, s32[2]{0:T(128)}, u32[]{:S(2)}) copy-start(s32[2]{0:T(128)} %param.4) | copy-start | bytes 28
  6.5 3.1 %copy-start.1 = (s32[2]{0:T(128)S(1)}, s32[2]{0:T(128)}, u32[]{:S(2)}) copy-start(s32[2]{0:T(128)} %param.5) | copy-start | bytes 28
  6.6 43.7 %collective-permute-start.3 = (bf16[2,256,2048]{2,1,0:T(8,128)(2,1)}, bf16[2,256,2048]{2,1,0:T(8,128)(2,1)}, u32[]{:S(2)}, u32[]{:S(2)}) collective-permute-start(bf16[2,256,2048]{2,1,0:T(8,128)(2,1)} %piece_of.4.rest_0_), channel_id=1, source_target_pairs={{0,24},{8,0},{16,8},{24,16},{1,25},{9,1},{17,9},{25,17},{2,26},{10... | collective-permute-start | bytes 6291464 | tf_op jit(solution)/shard_map/ppermute | solution.py:35
  9.6 57.5 %collective-permute-start.2 = (bf16[2,192,2048]{2,1,0:T(8,128)(2,1)}, bf16[2,192,2048]{2,1,0:T(8,128)(2,1)}, u32[]{:S(2)}, u32[]{:S(2)}) collective-permute-start(bf16[2,192,2048]{2,1,0:T(8,128)(2,1)} %piece_of.5), channel_id=1, source_target_pairs={{0,24},{8,0},{16,8},{24,16},{1,25},{9,1},{17,9},{25,17},{2,26},{10... | collective-permute-start | bytes 4718600 | tf_op jit(solution)/shard_map/ppermute | solution.py:35
  34.8 49.8 %collective-permute-start.1 = (bf16[2,192,2048]{2,1,0:T(8,128)(2,1)S(1)}, bf16[2,192,2048]{2,1,0:T(8,128)(2,1)S(1)}, u32[]{:S(2)}, u32[]{:S(2)}) collective-permute-start(bf16[2,192,2048]{2,1,0:T(8,128)(2,1)S(1)} %get-tuple-element.39), channel_id=1, source_target_pairs={{0,24},{8,0},{16,8},{24,16},{1,25},{9,1},{17,9},{25,17},{2,26},{10... | collective-permute-start | bytes 4718600 | tf_op jit(solution)/shard_map/ppermute | solution.py:35
  36.9 7.2 %collective-permute-start.4 = (bf16[4,64,512]{2,1,0:T(8,128)(2,1)S(1)}, bf16[4,64,512]{2,1,0:T(8,128)(2,1)S(1)}, u32[]{:S(2)}, u32[]{:S(2)}) collective-permute-start(bf16[4,64,512]{2,1,0:T(8,128)(2,1)S(1)} %get-tuple-element.41), channel_id=1, source_target_pairs={{0,1},{1,0},{2,3},{3,2},{4,5},{5,4},{6,7},{7,6},{8,9},{9,8},{10,11... | collective-permute-start | bytes 786440 | tf_op jit(solution)/shard_map/ppermute | solution.py:35
  44.7 5.6 %collective-permute-start.5 = (bf16[2,64,512]{2,1,0:T(8,128)(2,1)S(1)}, bf16[2,64,512]{2,1,0:T(8,128)(2,1)S(1)}, u32[]{:S(2)}, u32[]{:S(2)}) collective-permute-start(bf16[2,64,512]{2,1,0:T(8,128)(2,1)S(1)} %get-tuple-element.43), channel_id=1, source_target_pairs={{0,2},{1,3},{2,0},{3,1},{4,6},{5,7},{6,4},{7,5},{8,10},{9,11},{10,... | collective-permute-start | bytes 393224 | tf_op jit(solution)/shard_map/ppermute | solution.py:40
  57.3 37.8 %collective-permute-start.12 = (bf16[2,128,2048]{2,1,0:T(8,128)(2,1)S(1)}, bf16[2,128,2048]{2,1,0:T(8,128)(2,1)S(1)}, u32[]{:S(2)}, u32[]{:S(2)}) collective-permute-start(bf16[2,128,2048]{2,1,0:T(8,128)(2,1)S(1)} %get-tuple-element.57), channel_id=1, source_target_pairs={{0,24},{8,0},{16,8},{24,16},{1,25},{9,1},{17,9},{25,17},{2,26},{10... | collective-permute-start | bytes 3145736 | tf_op jit(solution)/shard_map/ppermute | solution.py:35
  59.5 7.6 %collective-permute-start.6 = (bf16[4,64,512]{2,1,0:T(8,128)(2,1)S(1)}, bf16[4,64,512]{2,1,0:T(8,128)(2,1)S(1)}, u32[]{:S(2)}, u32[]{:S(2)}) collective-permute-start(bf16[4,64,512]{2,1,0:T(8,128)(2,1)S(1)} %get-tuple-element.45), channel_id=1, source_target_pairs={{0,1},{1,0},{2,3},{3,2},{4,5},{5,4},{6,7},{7,6},{8,9},{9,8},{10,11... | collective-permute-start | bytes 786440 | tf_op jit(solution)/shard_map/ppermute | solution.py:35
  61.0 6.1 %collective-permute-start.7 = (bf16[1,64,512]{2,1,0:T(8,128)(2,1)S(1)}, bf16[1,64,512]{2,1,0:T(8,128)(2,1)S(1)}, u32[]{:S(2)}, u32[]{:S(2)}) collective-permute-start(bf16[1,64,512]{2,1,0:T(8,128)(2,1)S(1)} %get-tuple-element.47), channel_id=1, source_target_pairs={{0,4},{1,5},{2,6},{3,7},{4,0},{5,1},{6,2},{7,3},{8,12},{9,13},{10,... | collective-permute-start | bytes 196616 | tf_op jit(solution)/shard_map/ppermute | solution.py:40
  71.5 7.7 %collective-permute-start.9 = (bf16[4,64,384]{2,1,0:T(8,128)(2,1)S(1)}, bf16[4,64,384]{2,1,0:T(8,128)(2,1)S(1)}, u32[]{:S(2)}, u32[]{:S(2)}) collective-permute-start(bf16[4,64,384]{2,1,0:T(8,128)(2,1)S(1)} %get-tuple-element.52), channel_id=1, source_target_pairs={{0,1},{1,0},{2,3},{3,2},{4,5},{5,4},{6,7},{7,6},{8,9},{9,8},{10,11... | collective-permute-start | bytes 589832 | tf_op jit(solution)/shard_map/ppermute | solution.py:35
  73.1 8.4 %collective-permute-start.8 = (bf16[2,64,512]{2,1,0:T(8,128)(2,1)S(1)}, bf16[2,64,512]{2,1,0:T(8,128)(2,1)S(1)}, u32[]{:S(2)}, u32[]{:S(2)}) collective-permute-start(bf16[2,64,512]{2,1,0:T(8,128)(2,1)S(1)} %get-tuple-element.49), channel_id=1, source_target_pairs={{0,2},{1,3},{2,0},{3,1},{4,6},{5,7},{6,4},{7,5},{8,10},{9,11},{10,... | collective-permute-start | bytes 393224 | tf_op jit(solution)/shard_map/ppermute | solution.py:40
  79.8 4.7 %collective-permute-start.10 = (bf16[2,64,384]{2,1,0:T(8,128)(2,1)S(1)}, bf16[2,64,384]{2,1,0:T(8,128)(2,1)S(1)}, u32[]{:S(2)}, u32[]{:S(2)}) collective-permute-start(bf16[2,64,384]{2,1,0:T(8,128)(2,1)S(1)} %get-tuple-element.54), channel_id=1, source_target_pairs={{0,2},{1,3},{2,0},{3,1},{4,6},{5,7},{6,4},{7,5},{8,10},{9,11},{10,... | collective-permute-start | bytes 294920 | tf_op jit(solution)/shard_map/ppermute | solution.py:40
  88.1 9.8 %collective-permute-start.13 = (bf16[4,64,384]{2,1,0:T(8,128)(2,1)S(1)}, bf16[4,64,384]{2,1,0:T(8,128)(2,1)S(1)}, u32[]{:S(2)}, u32[]{:S(2)}) collective-permute-start(bf16[4,64,384]{2,1,0:T(8,128)(2,1)S(1)} %get-tuple-element.60), channel_id=1, source_target_pairs={{0,1},{1,0},{2,3},{3,2},{4,5},{5,4},{6,7},{7,6},{8,9},{9,8},{10,11... | collective-permute-start | bytes 589832 | tf_op jit(solution)/shard_map/ppermute | solution.py:35
  89.6 8.2 %collective-permute-start.11 = (bf16[1,64,896]{2,1,0:T(8,128)(2,1)S(1)}, bf16[1,64,896]{2,1,0:T(8,128)(2,1)S(1)}, u32[]{:S(2)}, u32[]{:S(2)}) collective-permute-start(bf16[1,64,896]{2,1,0:T(8,128)(2,1)S(1)} %get-tuple-element.56), channel_id=1, source_target_pairs={{0,4},{1,5},{2,6},{3,7},{4,0},{5,1},{6,2},{7,3},{8,12},{9,13},{10,... | collective-permute-start | bytes 344072 | tf_op jit(solution)/shard_map/ppermute | solution.py:40
  101.3 5.2 %collective-permute-start.14 = (bf16[4,64,256]{2,1,0:T(8,128)(2,1)S(1)}, bf16[4,64,256]{2,1,0:T(8,128)(2,1)S(1)}, u32[]{:S(2)}, u32[]{:S(2)}) collective-permute-start(bf16[4,64,256]{2,1,0:T(8,128)(2,1)S(1)} %get-tuple-element.64), channel_id=1, source_target_pairs={{0,1},{1,0},{2,3},{3,2},{4,5},{5,4},{6,7},{7,6},{8,9},{9,8},{10,11... | collective-permute-start | bytes 393224 | tf_op jit(solution)/shard_map/ppermute | solution.py:35
  101.9 4.6 %collective-permute-start.15 = (bf16[2,64,384]{2,1,0:T(8,128)(2,1)S(1)}, bf16[2,64,384]{2,1,0:T(8,128)(2,1)S(1)}, u32[]{:S(2)}, u32[]{:S(2)}) collective-permute-start(bf16[2,64,384]{2,1,0:T(8,128)(2,1)S(1)} %get-tuple-element.66), channel_id=1, source_target_pairs={{0,2},{1,3},{2,0},{3,1},{4,6},{5,7},{6,4},{7,5},{8,10},{9,11},{10,... | collective-permute-start | bytes 294920 | tf_op jit(solution)/shard_map/ppermute | solution.py:40
  107.1 8.2 %collective-permute-start.16 = (bf16[1,64,640]{2,1,0:T(8,128)(2,1)S(1)}, bf16[1,64,640]{2,1,0:T(8,128)(2,1)S(1)}, u32[]{:S(2)}, u32[]{:S(2)}) collective-permute-start(bf16[1,64,640]{2,1,0:T(8,128)(2,1)S(1)} %get-tuple-element.68), channel_id=1, source_target_pairs={{0,4},{1,5},{2,6},{3,7},{4,0},{5,1},{6,2},{7,3},{8,12},{9,13},{10,... | collective-permute-start | bytes 245768 | tf_op jit(solution)/shard_map/ppermute | solution.py:40
  109.3 5.8 %collective-permute-start.17 = (bf16[1,64,256]{2,1,0:T(8,128)(2,1)S(1)}, bf16[1,64,256]{2,1,0:T(8,128)(2,1)S(1)}, u32[]{:S(2)}, u32[]{:S(2)}) collective-permute-start(bf16[1,64,256]{2,1,0:T(8,128)(2,1)S(1)} %get-tuple-element.70), channel_id=1, source_target_pairs={{0,6},{1,7},{2,4},{3,5},{4,2},{5,3},{6,0},{7,1},{8,14},{9,15},{10,... | collective-permute-start | bytes 98312 | tf_op jit(solution)/shard_map/ppermute | solution.py:40
  111.0 4.3 %collective-permute-start.18 = (bf16[1,64,256]{2,1,0:T(8,128)(2,1)S(1)}, bf16[1,64,256]{2,1,0:T(8,128)(2,1)S(1)}, u32[]{:S(2)}, u32[]{:S(2)}) collective-permute-start(bf16[1,64,256]{2,1,0:T(8,128)(2,1)S(1)} %get-tuple-element.71), channel_id=1, source_target_pairs={{0,2},{1,3},{2,0},{3,1},{4,6},{5,7},{6,4},{7,5},{8,10},{9,11},{10,... | collective-permute-start | bytes 98312 | tf_op jit(solution)/shard_map/ppermute | solution.py:40

commit v18 on v17

--- a/solution.py
+++ b/solution.py
@@ -20,7 +20,8 @@
 CHUNKS = 4
 LANES = 128
 BLOCK = 256
-VMEM_BYTES = 46 * 1024 * 1024
+VMEM_BYTES = 44 * 1024 * 1024
+LEAN_BYTES = 32 * 1024 * 1024
 
 
 def shifted(block, axis, distance, fold=1, inner=False):
@@ -123,33 +124,34 @@
     arrived = take(plan.adds)
     if plan.adding and plan.placed:
         take(1)
-    given_ref, kept_ref = take(2) if plan.near == "give" else (None, None)
+    given_ref = take(1)[0] if plan.near == "give" else None
+    kept_ref = take(1)[0] if plan.rows == "keep" else None
     outs = take(len(plan.ways))
     targets = [take(task.count) for task in plan.tasks]
     result_ref = take(1)[0] if plan.adding else None
     piece_ref = take(1)[0] if plan.later else None
     if plan.part:
-        if plan.near != "use":
-            own_buf, own_sems = take(2)
         slot, _, width = plan.part
         base = slot * stride
         point = table_ref[base].astype(jnp.int32)
+        own_ref = bands_ref
         own = []
-        loads_of = plan.ways + (0,) if plan.near == "give" else plan.ways
-        for way, distance in enumerate(loads_of if plan.near != "use" else ()):
-            target = lax.rem(place + distance, fold)
-            rows_ref = own_buf.at[way] if way < len(plan.ways) else kept_ref
-            own.append([])
-            for part in range(2):
-                for level in range(depth):
-                    first = pl.multiple_of((level * fold + target) * rows, rows)
-                    copy = pltpu.make_async_copy(
-                        bands_ref.at[point, part, pl.ds(first, rows), :],
-                        rows_ref.at[part, pl.ds(level * rows, rows), :],
-                        own_sems.at[way, part, level],
-                    )
-                    copy.start()
-                    own[way].append(copy)
+        if plan.rows != "held":
+            own_ref = take(1)[0] if plan.rows == "load" else kept_ref
+            own_sems = take(1)[0]
+            for distance in range(1, fold + 1):
+                way = distance % fold
+                target = lax.rem(place + way, fold)
+                for part in range(2):
+                    for level in range(depth):
+                        first = pl.multiple_of((level * fold + target) * rows, rows)
+                        copy = pltpu.make_async_copy(
+                            bands_ref.at[point, part, pl.ds(first, rows), :],
+                            own_ref.at[way, part, pl.ds(level * rows, rows), :],
+                            own_sems.at[way, part, level],
+                        )
+                        copy.start()
+                        own.append((way, part, copy))
     if plan.later:
         piece_buf, piece_sems = take(2)
         later_slot, later_start, later_width = plan.later
@@ -207,15 +209,14 @@
         dims = (((1,), (1,)), ((), ()))
         points = near_ref.shape[1]
         run = points // 2 if width <= SPLIT else points
-        for way, out_ref in enumerate(outs):
+        for way, out_ref in zip(plan.ways, outs):
             of_both = []
             for part in range(2):
-                for copy in own[way][part * depth : (part + 1) * depth] if own else ():
+                for copy in [copy for *which, copy in own if which == [way, part]]:
                     copy.wait()
-                rows_ref = bands_ref if plan.near == "use" else own_buf.at[way]
                 products = [
                     lax.dot_general(
-                        rows_ref[part, :, pl.ds(first, run)],
+                        own_ref[way, part, :, pl.ds(first, run)],
                         near_ref[:, pl.ds(first, run)],
                         dims,
                         preferred_element_type=jnp.float32,
@@ -230,13 +231,13 @@
                 lines = slice(level * rows, (level + 1) * rows)
                 out_ref[level, :, :width] = real_part[lines]
                 out_ref[level, :, width:] = imag_part[lines]
-            if plan.near == "give" and way + 1 == len(outs):
-                for copy in own[-1]:
-                    copy.wait()
-            if plan.later and way == 0:
+            if plan.later and way == plan.ways[0]:
                 for load, store in zip(loads, stores):
                     load.wait()
                     store.start()
+        for way, _, copy in own:
+            if way not in plan.ways:
+                copy.wait()
     if plan.adding:
         placing.wait()
     if plan.later:
@@ -273,6 +274,7 @@
     part: tuple
     ways: tuple
     near: str
+    rows: str
     tasks: tuple
     takes: tuple
     adding: tuple
@@ -297,18 +299,19 @@
     if plan.part:
         width = plan.part[2]
         operands += [bands, phased]
-        in_specs += [vmem if plan.near == "use" else hbm, vmem]
+        in_specs += [vmem if plan.rows == "held" else hbm, vmem]
+        kept = (fold, 2, depth * rows, points)
         if plan.near == "give":
             out_shape.append(jax.ShapeDtypeStruct((2 * width, points), jnp.bfloat16))
-            out_shape.append(jax.ShapeDtypeStruct((2, depth * rows, points), jnp.bfloat16))
+        if plan.rows == "keep":
+            out_shape.append(jax.ShapeDtypeStruct(kept, jnp.bfloat16))
         out_shape += [
             jax.ShapeDtypeStruct((depth, rows, 2 * width), kind(way)) for way in plan.ways
         ]
-        if plan.near != "use":
-            scratch += [
-                pltpu.VMEM((len(plan.ways), 2, depth * rows, points), jnp.bfloat16),
-                pltpu.SemaphoreType.DMA((fold, 2, depth)),
-            ]
+        if plan.rows == "load":
+            scratch.append(pltpu.VMEM(kept, jnp.bfloat16))
+        if plan.rows != "held":
+            scratch.append(pltpu.SemaphoreType.DMA((fold, 2, depth)))
     for arrays in [*sources, arrived]:
         operands += arrays
         in_specs += [vmem] * len(arrays)
@@ -347,21 +350,24 @@
             scratch_shapes=scratch,
             out_shape=out_shape,
             input_output_aliases=aliases,
-            compiler_params=pltpu.CompilerParams(vmem_limit_bytes=VMEM_BYTES),
+            compiler_params=pltpu.CompilerParams(
+                vmem_limit_bytes=VMEM_BYTES if plan.part and plan.rows != "held" else LEAN_BYTES
+            ),
             cost_estimate=pl.CostEstimate(flops=1000, bytes_accessed=1000, transcendentals=0),
             name="step",
         )(*operands)
     )
     piece = outs.pop() if plan.later else None
     result = outs.pop() if plan.adding else result
-    near = [outs.pop(0), outs.pop(0)] if plan.near == "give" else None
+    near = outs.pop(0) if plan.near == "give" else None
+    kept = outs.pop(0) if plan.rows == "keep" else None
     terms = outs[: len(plan.ways)]
     handed = outs[len(plan.ways) :]
     sends = []
     for task in plan.tasks:
         sends.append(handed[: task.count])
         handed = handed[task.count :]
-    return terms, near, sends, result, piece
+    return terms, near, kept, sends, result, piece
 
 
 def cuts(nbands, first):
@@ -444,7 +450,7 @@
     depth = min(OUTER, grid_count)
     fold = grid_count // depth
     held = {}
-    near, result = None, None
+    near, kept, result = None, None, None
     for part, ways, phase, tasks, adds in schedule(parts, fold, depth):
         place = parts.index(part) if part else len(parts)
         later = parts[place + AHEAD] if place + AHEAD < len(parts) and phase != "use" else None
@@ -466,6 +472,7 @@
             part,
             ways,
             phase,
+            "held" if kept is not None else "keep" if phase == "give" else "load",
             tasks,
             tuple(len(arrays) for arrays in sources),
             adding,
@@ -474,12 +481,17 @@
             result is not None,
             later,
         )
-        phased, own = theres[place] if part else None, bands
-        if phase == "use":
-            phased, own = near
-        terms, near, sends, result, piece = step(
-            plan, table, own, phased, sources, arrived, result
+        phased = near if phase == "use" else theres[place] if part else None
+        terms, near, found, sends, result, piece = step(
+            plan,
+            table,
+            bands if kept is None else kept,
+            phased,
+            sources,
+            arrived,
+            result,
         )
+        kept = found if kept is None else kept
         if later:
             theres.append(shifted(piece, "ka", -1))
         for way, array in zip(ways, terms):

time: 117 us -> 115 us (0.983)
  Pallas kernels: 40.1 us -> 38.7 us
  waiting for transfers between devices: 46.6 us -> 45.4 us
    pallas_call x12, Pallas kernels: 33.8 us -> 32.3 us  [step(): pl.pallas_call(functools.partial(step_kernel, plan), in_specs=in_specs, o...]
  transfers between devices with their start and end apart: 19 -> 19, of which waited for: 11 -> 12; matrix products, arithmetic and copies ran while one was open for 1% -> 1% of each run, Pallas kernels for 28% -> 29%
where the time goes in v18:
time: 115 us; the launch traced here: 114 us
  waiting for transfers between devices  45.4 us (39%)
  Pallas kernels  38.7 us (34%)
  starting transfers between devices  29.3 us (25%)
    ppermute x10, waiting for transfers between devices, shifted(): return lax.ppermute(block, axis, route)  34.1 us
    pallas_call x12, Pallas kernels, step(): pl.pallas_call(functools.partial(step_kernel, plan), in_specs=in_specs, o...  32.3 us
    ppermute x9, starting transfers between devices, swapped(): return lax.ppermute(block, axis, [(i, i ^ distance) for i in range(count)])  15.2 us
    ppermute x10, starting transfers between devices, shifted(): return lax.ppermute(block, axis, route)  14.1 us
    ppermute x9, waiting for transfers between devices, swapped(): return lax.ppermute(block, axis, [(i, i ^ distance) for i in range(count)])  11.3 us
    pallas_call x3, Pallas kernels, piece_of(): pl.pallas_call(functools.partial(piece_kernel, slot, start), in_specs=[pl...  6.4 us
  transfers between devices with their start and end apart: 19, of which 12 were waited for; matrix products, arithmetic and copies ran while one was open for 1% of the time, Pallas kernels for 29%

profile of v18, /device:TPU:0, one launch (start us, length us, event | category | flops | bytes accessed | tf_op | source)
XLA Modules:
  0.0 114.3 jit_solution(12974488003151513388)
XLA Ops:
  0.0 1.7 %piece_of.3.rest_0_ = bf16[2,256,2048]{2,1,0:T(8,128)(2,1)S(1)} custom-call(bf16[2,2,512,2048]{3,2,1,0:T(8,128)(2,1)} %refs_0_.5), custom_call_target="tpu_custom_call" | custom-call | flops 1000 | bytes 1000 | tf_op jit(solution)/shard_map/piece_of/pallas_call | solution.py:66
  1.7 2.5 %collective-permute-start.2 = (bf16[2,256,2048]{2,1,0:T(8,128)(2,1)S(1)}, bf16[2,256,2048]{2,1,0:T(8,128)(2,1)}, u32[]{:S(2)}, u32[]{:S(2)}) collective-permute-start(bf16[2,256,2048]{2,1,0:T(8,128)(2,1)S(1)} %piece_of.3.rest_0_), channel_id=1, source_target_pairs={{0,24},{8,0},{16,8},{24,16},{1,25},{9,1},{17,9},{25,17},{2,26},{10... | collective-permute-start | bytes 6291464 | tf_op jit(solution)/shard_map/ppermute | solution.py:36
  4.1 2.4 %piece_of.4.rest_0_ = bf16[2,256,2048]{2,1,0:T(8,128)(2,1)} custom-call(bf16[2,2,512,2048]{3,2,1,0:T(8,128)(2,1)} %refs_0_.5, bf16[2,256,2048]{2,1,0:T(8,128)(2,1)S(1)} %piece_of.3.rest_0_), custom_call_target="tpu_custom_call" | custom-call | flops 1000 | bytes 1000 | tf_op jit(solution)/shard_map/piece_of/pallas_call | solution.py:66
  6.6 0.7 collective-permute-start.1
  7.3 2.3 %piece_of.5 = bf16[2,192,2048]{2,1,0:T(8,128)(2,1)} custom-call(bf16[2,2,512,2048]{3,2,1,0:T(8,128)(2,1)} %refs_0_.5, bf16[2,256,2048]{2,1,0:T(8,128)(2,1)} %piece_of.4.rest_0_), custom_call_target="tpu_custom_call" | custom-call | flops 1000 | bytes 1000 | tf_op jit(solution)/shard_map/piece_of/pallas_call | solution.py:66
  9.7 0.1 select_reduce_fusion.1
  9.9 0.1 fusion.4
  10.0 0.1 copy.6
  10.4 17.3 %collective-permute-done.2.refs_1_ = bf16[2,256,2048]{2,1,0:T(8,128)(2,1)} collective-permute-done((bf16[2,256,2048]{2,1,0:T(8,128)(2,1)S(1)}, bf16[2,256,2048]{2,1,0:T(8,128)(2,1)}, u32[]{:S(2)}, u32[]{:S(2)}) %collective-permute-start.2) | collective-permute-done | bytes 2097184 | tf_op jit(solution)/shard_map/ppermute | solution.py:36
  27.7 7.7 %step.12 = (f32[4,64,512]{2,1,0:T(8,128)S(1)}, bf16[4,64,512]{2,1,0:T(8,128)(2,1)S(1)}, bf16[2,192,2048]{2,1,0:T(8,128)(2,1)S(1)}) custom-call(f32[11]{0:T(128)S(1)} %pad_maximum_fusion.1.table_ref, bf16[2,2,512,2048]{3,2,1,0:T(8,128)(2,1)} %refs_0_.5, bf16[2,256,2048]{2,1,0:T(8,128)(2,1)} %collective-permute-done.2.refs_1_), custom_call_target="tpu_custom_call" | custom-call | flops 1000 | bytes 1000 | tf_op jit(solution)/shard_map/step/pallas_call | solution.py:346
  35.4 2.1 %collective-permute-start.7 = (bf16[2,192,2048]{2,1,0:T(8,128)(2,1)S(1)}, bf16[2,192,2048]{2,1,0:T(8,128)(2,1)S(1)}, u32[]{:S(2)}, u32[]{:S(2)}) collective-permute-start(bf16[2,192,2048]{2,1,0:T(8,128)(2,1)S(1)} %get-tuple-element.46), channel_id=1, source_target_pairs={{0,24},{8,0},{16,8},{24,16},{1,25},{9,1},{17,9},{25,17},{2,26},{10... | collective-permute-start | bytes 4718600 | tf_op jit(solution)/shard_map/ppermute | solution.py:36
  37.5 1.5 %collective-permute-start.3 = (bf16[4,64,512]{2,1,0:T(8,128)(2,1)S(1)}, bf16[4,64,512]{2,1,0:T(8,128)(2,1)S(1)}, u32[]{:S(2)}, u32[]{:S(2)}) collective-permute-start(bf16[4,64,512]{2,1,0:T(8,128)(2,1)S(1)} %get-tuple-element.38), channel_id=1, source_target_pairs={{0,1},{1,0},{2,3},{3,2},{4,5},{5,4},{6,7},{7,6},{8,9},{9,8},{10,11... | collective-permute-start | bytes 786440 | tf_op jit(solution)/shard_map/ppermute | solution.py:36
  39.0 5.7 %collective-permute-done.3.refs_1_ = bf16[4,64,512]{2,1,0:T(8,128)(2,1)S(1)} collective-permute-done((bf16[4,64,512]{2,1,0:T(8,128)(2,1)S(1)}, bf16[4,64,512]{2,1,0:T(8,128)(2,1)S(1)}, u32[]{:S(2)}, u32[]{:S(2)}) %collective-permute-start.3) | collective-permute-done | bytes 262176 | tf_op jit(solution)/shard_map/ppermute | solution.py:36
  44.7 0.6 step.13
  45.3 1.6 %collective-permute-start.4 = (bf16[2,64,512]{2,1,0:T(8,128)(2,1)S(1)}, bf16[2,64,512]{2,1,0:T(8,128)(2,1)S(1)}, u32[]{:S(2)}, u32[]{:S(2)}) collective-permute-start(bf16[2,64,512]{2,1,0:T(8,128)(2,1)S(1)} %get-tuple-element.40), channel_id=1, source_target_pairs={{0,2},{1,3},{2,0},{3,1},{4,6},{5,7},{6,4},{7,5},{8,10},{9,11},{10,... | collective-permute-start | bytes 393224 | tf_op jit(solution)/shard_map/ppermute | solution.py:41
  47.0 3.3 %collective-permute-done.1.refs_1_ = bf16[2,256,2048]{2,1,0:T(8,128)(2,1)} collective-permute-done((bf16[2,256,2048]{2,1,0:T(8,128)(2,1)}, bf16[2,256,2048]{2,1,0:T(8,128)(2,1)}, u32[]{:S(2)}, u32[]{:S(2)}) %collective-permute-start.1) | collective-permute-done | bytes 2097184 | tf_op jit(solution)/shard_map/ppermute | solution.py:36
  50.3 0.1 collective-permute-done.4.refs_3_
  50.4 7.7 %step.14 = (f32[4,64,512]{2,1,0:T(8,128)S(1)}, bf16[4,64,512]{2,1,0:T(8,128)(2,1)S(1)}, f32[1,64,512]{2,1,0:T(8,128)S(1)}, bf16[1,64,512]{2,1,0:T(8,128)(2,1)S(1)}, bf16[2,128,2048]{2,1,0:T(8,128)(2,1)S(1)}) custom-call(f32[11]{0:T(128)S(1)} %pad_maximum_fusion.1.table_ref, bf16[2,2,512,2048]{3,2,1,0:T(8,128)(2,1)} %refs_0_.5, ...), custom_call_target="tpu_custom_call" | custom-call | flops 1000 | bytes 1000 | tf_op jit(solution)/shard_map/step/pallas_call | solution.py:346
  58.1 2.1 %collective-permute-start.12 = (bf16[2,128,2048]{2,1,0:T(8,128)(2,1)S(1)}, bf16[2,128,2048]{2,1,0:T(8,128)(2,1)S(1)}, u32[]{:S(2)}, u32[]{:S(2)}) collective-permute-start(bf16[2,128,2048]{2,1,0:T(8,128)(2,1)S(1)} %get-tuple-element.55), channel_id=1, source_target_pairs={{0,24},{8,0},{16,8},{24,16},{1,25},{9,1},{17,9},{25,17},{2,26},{10... | collective-permute-start | bytes 3145736 | tf_op jit(solution)/shard_map/ppermute | solution.py:36
  60.1 1.5 %collective-permute-start.5 = (bf16[4,64,512]{2,1,0:T(8,128)(2,1)S(1)}, bf16[4,64,512]{2,1,0:T(8,128)(2,1)S(1)}, u32[]{:S(2)}, u32[]{:S(2)}) collective-permute-start(bf16[4,64,512]{2,1,0:T(8,128)(2,1)S(1)} %get-tuple-element.42), channel_id=1, source_target_pairs={{0,1},{1,0},{2,3},{3,2},{4,5},{5,4},{6,7},{7,6},{8,9},{9,8},{10,11... | collective-permute-start | bytes 786440 | tf_op jit(solution)/shard_map/ppermute | solution.py:36
  61.6 2.6 %collective-permute-start.6 = (bf16[1,64,512]{2,1,0:T(8,128)(2,1)S(1)}, bf16[1,64,512]{2,1,0:T(8,128)(2,1)S(1)}, u32[]{:S(2)}, u32[]{:S(2)}) collective-permute-start(bf16[1,64,512]{2,1,0:T(8,128)(2,1)S(1)} %get-tuple-element.44), channel_id=1, source_target_pairs={{0,4},{1,5},{2,6},{3,7},{4,0},{5,1},{6,2},{7,3},{8,12},{9,13},{10,... | collective-permute-start | bytes 196616 | tf_op jit(solution)/shard_map/ppermute | solution.py:41
  64.2 2.9 %collective-permute-done.refs_1_ = bf16[2,192,2048]{2,1,0:T(8,128)(2,1)} collective-permute-done((bf16[2,192,2048]{2,1,0:T(8,128)(2,1)}, bf16[2,192,2048]{2,1,0:T(8,128)(2,1)}, u32[]{:S(2)}, u32[]{:S(2)}) %collective-permute-start) | collective-permute-done | bytes 1572896 | tf_op jit(solution)/shard_map/ppermute | solution.py:36
  67.1 0.2 collective-permute-done.5.refs_3_
  67.3 4.4 %step.15 = (bf16[384,2048]{1,0:T(8,128)(2,1)S(1)}, bf16[2,2,256,2048]{3,2,1,0:T(8,128)(2,1)S(1)}, bf16[4,64,384]{2,1,0:T(8,128)(2,1)S(1)}, f32[2,64,512]{2,1,0:T...) custom-call(f32[11]{0:T(128)S(1)} %pad_maximum_fusion.1.table_ref, ...), custom_call_target="tpu_custom_call" | custom-call | flops 1000 | bytes 1000 | tf_op jit(solution)/shard_map/step/pallas_call | solution.py:346
  71.8 1.6 %collective-permute-start.9 = (bf16[4,64,384]{2,1,0:T(8,128)(2,1)S(1)}, bf16[4,64,384]{2,1,0:T(8,128)(2,1)S(1)}, u32[]{:S(2)}, u32[]{:S(2)}) collective-permute-start(bf16[4,64,384]{2,1,0:T(8,128)(2,1)S(1)} %get-tuple-element.50), channel_id=1, source_target_pairs={{0,1},{1,0},{2,3},{3,2},{4,5},{5,4},{6,7},{7,6},{8,9},{9,8},{10,11... | collective-permute-start | bytes 589832 | tf_op jit(solution)/shard_map/ppermute | solution.py:36
  73.3 1.6 %collective-permute-start.8 = (bf16[2,64,512]{2,1,0:T(8,128)(2,1)S(1)}, bf16[2,64,512]{2,1,0:T(8,128)(2,1)S(1)}, u32[]{:S(2)}, u32[]{:S(2)}) collective-permute-start(bf16[2,64,512]{2,1,0:T(8,128)(2,1)S(1)} %get-tuple-element.48), channel_id=1, source_target_pairs={{0,2},{1,3},{2,0},{3,1},{4,6},{5,7},{6,4},{7,5},{8,10},{9,11},{10,... | collective-permute-start | bytes 393224 | tf_op jit(solution)/shard_map/ppermute | solution.py:41
  74.9 1.9 %step.16.refs_0_ = f32[4,64,384]{2,1,0:T(8,128)S(1)} custom-call(f32[11]{0:T(128)S(1)} %pad_maximum_fusion.1.table_ref, bf16[2,2,256,2048]{3,2,1,0:T(8,128)(2,1)S(1)} %get-tuple-element.45.refs_0_, bf16[384,2048]{1,0:T(8,128)(2,1)S(1)} %get-tuple-element.49.refs_1_), custom_call_target="tpu_custom_call" | custom-call | flops 1000 | bytes 1000 | tf_op jit(solution)/shard_map/step/pallas_call | solution.py:346
  76.8 2.5 %collective-permute-done.9.refs_1_ = bf16[4,64,384]{2,1,0:T(8,128)(2,1)S(1)} collective-permute-done((bf16[4,64,384]{2,1,0:T(8,128)(2,1)S(1)}, bf16[4,64,384]{2,1,0:T(8,128)(2,1)S(1)}, u32[]{:S(2)}, u32[]{:S(2)}) %collective-permute-start.9) | collective-permute-done | bytes 196640 | tf_op jit(solution)/shard_map/ppermute | solution.py:36
  79.3 0.6 step.17
  79.8 1.6 %collective-permute-start.10 = (bf16[2,64,384]{2,1,0:T(8,128)(2,1)S(1)}, bf16[2,64,384]{2,1,0:T(8,128)(2,1)S(1)}, u32[]{:S(2)}, u32[]{:S(2)}) collective-permute-start(bf16[2,64,384]{2,1,0:T(8,128)(2,1)S(1)} %get-tuple-element.52), channel_id=1, source_target_pairs={{0,2},{1,3},{2,0},{3,1},{4,6},{5,7},{6,4},{7,5},{8,10},{9,11},{10,... | collective-permute-start | bytes 294920 | tf_op jit(solution)/shard_map/ppermute | solution.py:41
  81.5 3.0 %collective-permute-done.10.refs_5_ = bf16[2,64,384]{2,1,0:T(8,128)(2,1)S(1)} collective-permute-done((bf16[2,64,384]{2,1,0:T(8,128)(2,1)S(1)}, bf16[2,64,384]{2,1,0:T(8,128)(2,1)S(1)}, u32[]{:S(2)}, u32[]{:S(2)}) %collective-permute-start.10) | collective-permute-done | bytes 98336 | tf_op jit(solution)/shard_map/ppermute | solution.py:41
  84.5 2.4 %step.18 = (bf16[384,2048]{1,0:T(8,128)(2,1)S(1)}, bf16[4,64,384]{2,1,0:T(8,128)(2,1)S(1)}, f32[1,64,896]{2,1,0:T(8,128)S(1)}, bf16[1,64,896]{2,1,0:T(8,128)(2,1)S(1)}) custom-call(f32[11]{0:T(128)S(1)} %pad_maximum_fusion.1.table_ref, bf16[2,2,256,2048]{3,2,1,0:T(8,128)(2,1)S(1)} %get-tuple-element.45.refs_0_, ...), custom_call_target="tpu_custom_call" | custom-call | flops 1000 | bytes 1000 | tf_op jit(solution)/shard_map/step/pallas_call | solution.py:346
  87.0 1.6 %collective-permute-start.13 = (bf16[4,64,384]{2,1,0:T(8,128)(2,1)S(1)}, bf16[4,64,384]{2,1,0:T(8,128)(2,1)S(1)}, u32[]{:S(2)}, u32[]{:S(2)}) collective-permute-start(bf16[4,64,384]{2,1,0:T(8,128)(2,1)S(1)} %get-tuple-element.57), channel_id=1, source_target_pairs={{0,1},{1,0},{2,3},{3,2},{4,5},{5,4},{6,7},{7,6},{8,9},{9,8},{10,11... | collective-permute-start | bytes 589832 | tf_op jit(solution)/shard_map/ppermute | solution.py:36
  88.5 2.6 %collective-permute-start.11 = (bf16[1,64,896]{2,1,0:T(8,128)(2,1)S(1)}, bf16[1,64,896]{2,1,0:T(8,128)(2,1)S(1)}, u32[]{:S(2)}, u32[]{:S(2)}) collective-permute-start(bf16[1,64,896]{2,1,0:T(8,128)(2,1)S(1)} %get-tuple-element.54), channel_id=1, source_target_pairs={{0,4},{1,5},{2,6},{3,7},{4,0},{5,1},{6,2},{7,3},{8,12},{9,13},{10,... | collective-permute-start | bytes 344072 | tf_op jit(solution)/shard_map/ppermute | solution.py:41
  91.1 1.9 %step.19.refs_2_ = f32[4,64,384]{2,1,0:T(8,128)S(1)} custom-call(f32[11]{0:T(128)S(1)} %pad_maximum_fusion.1.table_ref, bf16[2,2,256,2048]{3,2,1,0:T(8,128)(2,1)S(1)} %get-tuple-element.45.refs_0_, bf16[384,2048]{1,0:T(8,128)(2,1)S(1)} %get-tuple-element.56.refs_1_), custom_call_target="tpu_custom_call" | custom-call | flops 1000 | bytes 1000 | tf_op jit(solution)/shard_map/step/pallas_call | solution.py:346
  93.0 2.1 %collective-permute-done.12.refs_1_ = bf16[2,128,2048]{2,1,0:T(8,128)(2,1)S(1)} collective-permute-done((bf16[2,128,2048]{2,1,0:T(8,128)(2,1)S(1)}, bf16[2,128,2048]{2,1,0:T(8,128)(2,1)S(1)}, u32[]{:S(2)}, u32[]{:S(2)}) %collective-permute-start.12) | collective-permute-done | bytes 1048608 | tf_op jit(solution)/shard_map/ppermute | solution.py:36
  95.1 1.7 %collective-permute-done.11.refs_5_.refs_1_ = bf16[1,64,896]{2,1,0:T(8,128)(2,1)S(1)} collective-permute-done((bf16[1,64,896]{2,1,0:T(8,128)(2,1)S(1)}, bf16[1,64,896]{2,1,0:T(8,128)(2,1)S(1)}, u32[]{:S(2)}, u32[]{:S(2)}) %collective-permute-start.11) | collective-permute-done | bytes 114720 | tf_op jit(solution)/shard_map/ppermute | solution.py:41
  96.9 1.7 %step.20 = (bf16[256,2048]{1,0:T(8,128)(2,1)S(1)}, bf16[4,64,256]{2,1,0:T(8,128)(2,1)S(1)}, f32[2,64,384]{2,1,0:T(8,128)S(1)}, bf16[2,64,384]{2,1,0:T(8,128)(2,1)S(1)}, f32[64,2,2,512]{3,2,1,0:T(2,128)}) custom-call(f32[11]{0:T(128)S(1)} %pad_maximum_fusion.1.table_ref, ...), custom_call_target="tpu_custom_call", output_to_operand_aliasing={{4}: (7, {})} | custom-call | flops 1000 | bytes 1000 | tf_op jit(solution)/shard_map/step/pallas_call | solution.py:346
  98.6 0.6 collective-permute-start.14
  99.2 0.8 collective-permute-start.15
  100.0 1.3 %step.21.refs_0_ = f32[4,64,256]{2,1,0:T(8,128)S(1)} custom-call(f32[11]{0:T(128)S(1)} %pad_maximum_fusion.1.table_ref, bf16[2,2,256,2048]{3,2,1,0:T(8,128)(2,1)S(1)} %get-tuple-element.45.refs_0_, bf16[256,2048]{1,0:T(8,128)(2,1)S(1)} %get-tuple-element.59.refs_1_), custom_call_target="tpu_custom_call" | custom-call | flops 1000 | bytes 1000 | tf_op jit(solution)/shard_map/step/pallas_call | solution.py:346
  101.3 2.5 %collective-permute-done.15.refs_3_ = bf16[2,64,384]{2,1,0:T(8,128)(2,1)S(1)} collective-permute-done((bf16[2,64,384]{2,1,0:T(8,128)(2,1)S(1)}, bf16[2,64,384]{2,1,0:T(8,128)(2,1)S(1)}, u32[]{:S(2)}, u32[]{:S(2)}) %collective-permute-start.15) | collective-permute-done | bytes 98336 | tf_op jit(solution)/shard_map/ppermute | solution.py:41
  103.8 0.6 step.22
  104.4 2.5 %collective-permute-start.16 = (bf16[1,64,640]{2,1,0:T(8,128)(2,1)S(1)}, bf16[1,64,640]{2,1,0:T(8,128)(2,1)S(1)}, u32[]{:S(2)}, u32[]{:S(2)}) collective-permute-start(bf16[1,64,640]{2,1,0:T(8,128)(2,1)S(1)} %get-tuple-element.64), channel_id=1, source_target_pairs={{0,4},{1,5},{2,6},{3,7},{4,0},{5,1},{6,2},{7,3},{8,12},{9,13},{10,... | collective-permute-start | bytes 245768 | tf_op jit(solution)/shard_map/ppermute | solution.py:41
  106.9 1.4 %collective-permute-start.17 = (bf16[1,64,256]{2,1,0:T(8,128)(2,1)S(1)}, bf16[1,64,256]{2,1,0:T(8,128)(2,1)S(1)}, u32[]{:S(2)}, u32[]{:S(2)}) collective-permute-start(bf16[1,64,256]{2,1,0:T(8,128)(2,1)S(1)} %get-tuple-element.66), channel_id=1, source_target_pairs={{0,6},{1,7},{2,4},{3,5},{4,2},{5,3},{6,0},{7,1},{8,14},{9,15},{10,... | collective-permute-start | bytes 98312 | tf_op jit(solution)/shard_map/ppermute | solution.py:41
  108.3 0.5 collective-permute-start.18
  108.8 3.9 %collective-permute-done.17.refs_5_ = bf16[1,64,256]{2,1,0:T(8,128)(2,1)S(1)} collective-permute-done((bf16[1,64,256]{2,1,0:T(8,128)(2,1)S(1)}, bf16[1,64,256]{2,1,0:T(8,128)(2,1)S(1)}, u32[]{:S(2)}, u32[]{:S(2)}) %collective-permute-start.17) | collective-permute-done | bytes 32800 | tf_op jit(solution)/shard_map/ppermute | solution.py:41
  112.7 1.5 %step.23 = f32[64,2,2,512]{3,2,1,0:T(2,128)} custom-call(f32[11]{0:T(128)S(1)} %pad_maximum_fusion.1.table_ref, f32[1,64,896]{2,1,0:T(8,128)S(1)} %get-tuple-element.53.refs_4_.refs_0_, bf16[1,64,896]{2,1,0:T(8,128)(2,1)S(1)} %collective-permute-done.11.refs_5_.refs_1_, f32[1,64,384]{2,1,0:T(8,128)S(1)} %get-tuple-element.63.refs_2_, ...), custom_call_target="tpu_custom_call", output_to_operand_aliasing={{}: (9, {})} | custom-call | flops 1000 | bytes 1000 | tf_op jit(solution)/shard_map/step/pallas_call | solution.py:346
  (17 shorter events, 0.4 us)
Async XLA Ops:
  1.7 26.0 %collective-permute-start.2 = (bf16[2,256,2048]{2,1,0:T(8,128)(2,1)S(1)}, bf16[2,256,2048]{2,1,0:T(8,128)(2,1)}, u32[]{:S(2)}, u32[]{:S(2)}) collective-permute-start(bf16[2,256,2048]{2,1,0:T(8,128)(2,1)S(1)} %piece_of.3.rest_0_), channel_id=1, source_target_pairs={{0,24},{8,0},{16,8},{24,16},{1,25},{9,1},{17,9},{25,17},{2,26},{10... | collective-permute-start | bytes 6291464 | tf_op jit(solution)/shard_map/ppermute | solution.py:36
  6.6 3.1 %copy-start = (s32[2]{0:T(128)S(1)}, s32[2]{0:T(128)}, u32[]{:S(2)}) copy-start(s32[2]{0:T(128)} %param.4) | copy-start | bytes 28
  6.6 3.1 %copy-start.1 = (s32[2]{0:T(128)S(1)}, s32[2]{0:T(128)}, u32[]{:S(2)}) copy-start(s32[2]{0:T(128)} %param.5) | copy-start | bytes 28
  6.6 43.7 %collective-permute-start.1 = (bf16[2,256,2048]{2,1,0:T(8,128)(2,1)}, bf16[2,256,2048]{2,1,0:T(8,128)(2,1)}, u32[]{:S(2)}, u32[]{:S(2)}) collective-permute-start(bf16[2,256,2048]{2,1,0:T(8,128)(2,1)} %piece_of.4.rest_0_), channel_id=1, source_target_pairs={{0,24},{8,0},{16,8},{24,16},{1,25},{9,1},{17,9},{25,17},{2,26},{10... | collective-permute-start | bytes 6291464 | tf_op jit(solution)/shard_map/ppermute | solution.py:36
  9.6 57.5 %collective-permute-start = (bf16[2,192,2048]{2,1,0:T(8,128)(2,1)}, bf16[2,192,2048]{2,1,0:T(8,128)(2,1)}, u32[]{:S(2)}, u32[]{:S(2)}) collective-permute-start(bf16[2,192,2048]{2,1,0:T(8,128)(2,1)} %piece_of.5), channel_id=1, source_target_pairs={{0,24},{8,0},{16,8},{24,16},{1,25},{9,1},{17,9},{25,17},{2,26},{10... | collective-permute-start | bytes 4718600 | tf_op jit(solution)/shard_map/ppermute | solution.py:36
  35.4 49.1 %collective-permute-start.7 = (bf16[2,192,2048]{2,1,0:T(8,128)(2,1)S(1)}, bf16[2,192,2048]{2,1,0:T(8,128)(2,1)S(1)}, u32[]{:S(2)}, u32[]{:S(2)}) collective-permute-start(bf16[2,192,2048]{2,1,0:T(8,128)(2,1)S(1)} %get-tuple-element.46), channel_id=1, source_target_pairs={{0,24},{8,0},{16,8},{24,16},{1,25},{9,1},{17,9},{25,17},{2,26},{10... | collective-permute-start | bytes 4718600 | tf_op jit(solution)/shard_map/ppermute | solution.py:36
  37.5 7.2 %collective-permute-start.3 = (bf16[4,64,512]{2,1,0:T(8,128)(2,1)S(1)}, bf16[4,64,512]{2,1,0:T(8,128)(2,1)S(1)}, u32[]{:S(2)}, u32[]{:S(2)}) collective-permute-start(bf16[4,64,512]{2,1,0:T(8,128)(2,1)S(1)} %get-tuple-element.38), channel_id=1, source_target_pairs={{0,1},{1,0},{2,3},{3,2},{4,5},{5,4},{6,7},{7,6},{8,9},{9,8},{10,11... | collective-permute-start | bytes 786440 | tf_op jit(solution)/shard_map/ppermute | solution.py:36
  45.3 5.0 %collective-permute-start.4 = (bf16[2,64,512]{2,1,0:T(8,128)(2,1)S(1)}, bf16[2,64,512]{2,1,0:T(8,128)(2,1)S(1)}, u32[]{:S(2)}, u32[]{:S(2)}) collective-permute-start(bf16[2,64,512]{2,1,0:T(8,128)(2,1)S(1)} %get-tuple-element.40), channel_id=1, source_target_pairs={{0,2},{1,3},{2,0},{3,1},{4,6},{5,7},{6,4},{7,5},{8,10},{9,11},{10,... | collective-permute-start | bytes 393224 | tf_op jit(solution)/shard_map/ppermute | solution.py:41
  58.1 37.0 %collective-permute-start.12 = (bf16[2,128,2048]{2,1,0:T(8,128)(2,1)S(1)}, bf16[2,128,2048]{2,1,0:T(8,128)(2,1)S(1)}, u32[]{:S(2)}, u32[]{:S(2)}) collective-permute-start(bf16[2,128,2048]{2,1,0:T(8,128)(2,1)S(1)} %get-tuple-element.55), channel_id=1, source_target_pairs={{0,24},{8,0},{16,8},{24,16},{1,25},{9,1},{17,9},{25,17},{2,26},{10... | collective-permute-start | bytes 3145736 | tf_op jit(solution)/shard_map/ppermute | solution.py:36
  60.1 7.2 %collective-permute-start.5 = (bf16[4,64,512]{2,1,0:T(8,128)(2,1)S(1)}, bf16[4,64,512]{2,1,0:T(8,128)(2,1)S(1)}, u32[]{:S(2)}, u32[]{:S(2)}) collective-permute-start(bf16[4,64,512]{2,1,0:T(8,128)(2,1)S(1)} %get-tuple-element.42), channel_id=1, source_target_pairs={{0,1},{1,0},{2,3},{3,2},{4,5},{5,4},{6,7},{7,6},{8,9},{9,8},{10,11... | collective-permute-start | bytes 786440 | tf_op jit(solution)/shard_map/ppermute | solution.py:36
  61.6 5.5 %collective-permute-start.6 = (bf16[1,64,512]{2,1,0:T(8,128)(2,1)S(1)}, bf16[1,64,512]{2,1,0:T(8,128)(2,1)S(1)}, u32[]{:S(2)}, u32[]{:S(2)}) collective-permute-start(bf16[1,64,512]{2,1,0:T(8,128)(2,1)S(1)} %get-tuple-element.44), channel_id=1, source_target_pairs={{0,4},{1,5},{2,6},{3,7},{4,0},{5,1},{6,2},{7,3},{8,12},{9,13},{10,... | collective-permute-start | bytes 196616 | tf_op jit(solution)/shard_map/ppermute | solution.py:41
  71.8 7.5 %collective-permute-start.9 = (bf16[4,64,384]{2,1,0:T(8,128)(2,1)S(1)}, bf16[4,64,384]{2,1,0:T(8,128)(2,1)S(1)}, u32[]{:S(2)}, u32[]{:S(2)}) collective-permute-start(bf16[4,64,384]{2,1,0:T(8,128)(2,1)S(1)} %get-tuple-element.50), channel_id=1, source_target_pairs={{0,1},{1,0},{2,3},{3,2},{4,5},{5,4},{6,7},{7,6},{8,9},{9,8},{10,11... | collective-permute-start | bytes 589832 | tf_op jit(solution)/shard_map/ppermute | solution.py:36
  73.3 8.2 %collective-permute-start.8 = (bf16[2,64,512]{2,1,0:T(8,128)(2,1)S(1)}, bf16[2,64,512]{2,1,0:T(8,128)(2,1)S(1)}, u32[]{:S(2)}, u32[]{:S(2)}) collective-permute-start(bf16[2,64,512]{2,1,0:T(8,128)(2,1)S(1)} %get-tuple-element.48), channel_id=1, source_target_pairs={{0,2},{1,3},{2,0},{3,1},{4,6},{5,7},{6,4},{7,5},{8,10},{9,11},{10,... | collective-permute-start | bytes 393224 | tf_op jit(solution)/shard_map/ppermute | solution.py:41
  79.8 4.7 %collective-permute-start.10 = (bf16[2,64,384]{2,1,0:T(8,128)(2,1)S(1)}, bf16[2,64,384]{2,1,0:T(8,128)(2,1)S(1)}, u32[]{:S(2)}, u32[]{:S(2)}) collective-permute-start(bf16[2,64,384]{2,1,0:T(8,128)(2,1)S(1)} %get-tuple-element.52), channel_id=1, source_target_pairs={{0,2},{1,3},{2,0},{3,1},{4,6},{5,7},{6,4},{7,5},{8,10},{9,11},{10,... | collective-permute-start | bytes 294920 | tf_op jit(solution)/shard_map/ppermute | solution.py:41
  87.0 9.9 %collective-permute-start.13 = (bf16[4,64,384]{2,1,0:T(8,128)(2,1)S(1)}, bf16[4,64,384]{2,1,0:T(8,128)(2,1)S(1)}, u32[]{:S(2)}, u32[]{:S(2)}) collective-permute-start(bf16[4,64,384]{2,1,0:T(8,128)(2,1)S(1)} %get-tuple-element.57), channel_id=1, source_target_pairs={{0,1},{1,0},{2,3},{3,2},{4,5},{5,4},{6,7},{7,6},{8,9},{9,8},{10,11... | collective-permute-start | bytes 589832 | tf_op jit(solution)/shard_map/ppermute | solution.py:36
  88.5 8.3 %collective-permute-start.11 = (bf16[1,64,896]{2,1,0:T(8,128)(2,1)S(1)}, bf16[1,64,896]{2,1,0:T(8,128)(2,1)S(1)}, u32[]{:S(2)}, u32[]{:S(2)}) collective-permute-start(bf16[1,64,896]{2,1,0:T(8,128)(2,1)S(1)} %get-tuple-element.54), channel_id=1, source_target_pairs={{0,4},{1,5},{2,6},{3,7},{4,0},{5,1},{6,2},{7,3},{8,12},{9,13},{10,... | collective-permute-start | bytes 344072 | tf_op jit(solution)/shard_map/ppermute | solution.py:41
  98.6 5.2 %collective-permute-start.14 = (bf16[4,64,256]{2,1,0:T(8,128)(2,1)S(1)}, bf16[4,64,256]{2,1,0:T(8,128)(2,1)S(1)}, u32[]{:S(2)}, u32[]{:S(2)}) collective-permute-start(bf16[4,64,256]{2,1,0:T(8,128)(2,1)S(1)} %get-tuple-element.60), channel_id=1, source_target_pairs={{0,1},{1,0},{2,3},{3,2},{4,5},{5,4},{6,7},{7,6},{8,9},{9,8},{10,11... | collective-permute-start | bytes 393224 | tf_op jit(solution)/shard_map/ppermute | solution.py:36
  99.2 4.6 %collective-permute-start.15 = (bf16[2,64,384]{2,1,0:T(8,128)(2,1)S(1)}, bf16[2,64,384]{2,1,0:T(8,128)(2,1)S(1)}, u32[]{:S(2)}, u32[]{:S(2)}) collective-permute-start(bf16[2,64,384]{2,1,0:T(8,128)(2,1)S(1)} %get-tuple-element.62), channel_id=1, source_target_pairs={{0,2},{1,3},{2,0},{3,1},{4,6},{5,7},{6,4},{7,5},{8,10},{9,11},{10,... | collective-permute-start | bytes 294920 | tf_op jit(solution)/shard_map/ppermute | solution.py:41
  104.4 8.3 %collective-permute-start.16 = (bf16[1,64,640]{2,1,0:T(8,128)(2,1)S(1)}, bf16[1,64,640]{2,1,0:T(8,128)(2,1)S(1)}, u32[]{:S(2)}, u32[]{:S(2)}) collective-permute-start(bf16[1,64,640]{2,1,0:T(8,128)(2,1)S(1)} %get-tuple-element.64), channel_id=1, source_target_pairs={{0,4},{1,5},{2,6},{3,7},{4,0},{5,1},{6,2},{7,3},{8,12},{9,13},{10,... | collective-permute-start | bytes 245768 | tf_op jit(solution)/shard_map/ppermute | solution.py:41
  106.9 5.7 %collective-permute-start.17 = (bf16[1,64,256]{2,1,0:T(8,128)(2,1)S(1)}, bf16[1,64,256]{2,1,0:T(8,128)(2,1)S(1)}, u32[]{:S(2)}, u32[]{:S(2)}) collective-permute-start(bf16[1,64,256]{2,1,0:T(8,128)(2,1)S(1)} %get-tuple-element.66), channel_id=1, source_target_pairs={{0,6},{1,7},{2,4},{3,5},{4,2},{5,3},{6,0},{7,1},{8,14},{9,15},{10,... | collective-permute-start | bytes 98312 | tf_op jit(solution)/shard_map/ppermute | solution.py:41
  108.3 4.4 %collective-permute-start.18 = (bf16[1,64,256]{2,1,0:T(8,128)(2,1)S(1)}, bf16[1,64,256]{2,1,0:T(8,128)(2,1)S(1)}, u32[]{:S(2)}, u32[]{:S(2)}) collective-permute-start(bf16[1,64,256]{2,1,0:T(8,128)(2,1)S(1)} %get-tuple-element.67), channel_id=1, source_target_pairs={{0,2},{1,3},{2,0},{3,1},{4,6},{5,7},{6,4},{7,5},{8,10},{9,11},{10,... | collective-permute-start | bytes 98312 | tf_op jit(solution)/shard_map/ppermute | solution.py:41

commit v19 on v18

--- a/solution.py
+++ b/solution.py
@@ -17,7 +17,6 @@
 OUTER = 4
 SPLIT = 128
 JOINT = 2
-CHUNKS = 4
 LANES = 128
 BLOCK = 256
 VMEM_BYTES = 44 * 1024 * 1024
@@ -41,17 +40,32 @@
     return lax.ppermute(block, axis, [(i, i ^ distance) for i in range(count)])
 
 
+def first_kernel(slot, start, bands_ref, out_ref, sems):
+    width = out_ref.shape[1]
+    loads = [
+        pltpu.make_async_copy(
+            bands_ref.at[slot, part, pl.ds(start, width), :], out_ref.at[part], sems.at[part]
+        )
+        for part in range(2)
+    ]
+    for load in loads:
+        load.start()
+    for load in loads:
+        load.wait()
+
+
 def piece_kernel(slot, start, bands_ref, *rest):
     out_ref, piece_buf, sems = rest[-3:]
-    width = piece_buf.shape[1] // CHUNKS
-    loads, stores = [], []
-    for index in range(2 * CHUNKS):
-        part, chunk = divmod(index, CHUNKS)
-        lines = pl.ds(chunk * width, width)
-        source = bands_ref.at[slot, part, pl.ds(start + chunk * width, width), :]
-        buf = piece_buf.at[part, lines, :]
-        loads.append(pltpu.make_async_copy(source, buf, sems.at[0, index]))
-        stores.append(pltpu.make_async_copy(buf, out_ref.at[part, lines, :], sems.at[1, index]))
+    width = piece_buf.shape[1]
+    rows = pl.ds(start, width)
+    loads = [
+        pltpu.make_async_copy(bands_ref.at[slot, part, rows, :], piece_buf.at[part], sems.at[0, part])
+        for part in range(2)
+    ]
+    stores = [
+        pltpu.make_async_copy(piece_buf.at[part], out_ref.at[part], sems.at[1, part])
+        for part in range(2)
+    ]
     for load in loads:
         load.start()
     for load, store in zip(loads, stores):
@@ -63,14 +77,13 @@
 
 def piece_of(slot, start, width, bands, after):
     points = bands.shape[3]
+    hbm = pl.BlockSpec(memory_space=pltpu.HBM)
+    scratch = [pltpu.VMEM((2, width, points), bands.dtype), pltpu.SemaphoreType.DMA((2, 2))]
     return pl.pallas_call(
-        functools.partial(piece_kernel, slot, start),
-        in_specs=[pl.BlockSpec(memory_space=pl.ANY)] * (1 + len(after)),
-        out_specs=pl.BlockSpec(memory_space=pl.ANY),
-        scratch_shapes=[
-            pltpu.VMEM((2, width, points), bands.dtype),
-            pltpu.SemaphoreType.DMA((2, 2 * CHUNKS)),
-        ],
+        functools.partial(piece_kernel if after else first_kernel, slot, start),
+        in_specs=[hbm] * (1 + len(after)),
+        out_specs=hbm if after else pl.BlockSpec(memory_space=pltpu.VMEM),
+        scratch_shapes=scratch if after else [pltpu.SemaphoreType.DMA((2,))],
         out_shape=jax.ShapeDtypeStruct((2, width, points), bands.dtype),
         compiler_params=pltpu.CompilerParams(vmem_limit_bytes=VMEM_BYTES),
         cost_estimate=pl.CostEstimate(flops=1000, bytes_accessed=1000, transcendentals=0),

time: 115 us -> 114 us (level)
  no operation moved by 1% of the time
where the time goes in v19:
time: 114 us
  waiting for transfers between devices  45.1 us (40%)
  Pallas kernels  38.7 us (34%)
  starting transfers between devices  29.3 us (26%)
    ppermute x10, waiting for transfers between devices, shifted(): return lax.ppermute(block, axis, route)  33.9 us
    pallas_call x12, Pallas kernels, step(): pl.pallas_call(functools.partial(step_kernel, plan), in_specs=in_specs, o...  32.3 us
    ppermute x9, starting transfers between devices, swapped(): return lax.ppermute(block, axis, [(i, i ^ distance) for i in range(count)])  15.2 us
    ppermute x10, starting transfers between devices, shifted(): return lax.ppermute(block, axis, route)  14.1 us
    ppermute x9, waiting for transfers between devices, swapped(): return lax.ppermute(block, axis, [(i, i ^ distance) for i in range(count)])  11.3 us
    pallas_call x3, Pallas kernels, piece_of(): pl.pallas_call(functools.partial(piece_kernel if after else first_kernel,...  6.46 us
  transfers between devices with their start and end apart: 19, of which 12 were waited for; matrix products, arithmetic and copies ran while one was open for 1% of the time, Pallas kernels for 29%

profile of v19, /device:TPU:0, one launch (start us, length us, event | category | flops | bytes accessed | tf_op | source)
XLA Modules:
  0.0 114.2 jit_solution(3780388226498336137)
XLA Ops:
  0.0 1.6 %piece_of.3.rest_0_ = bf16[2,256,2048]{2,1,0:T(8,128)(2,1)S(1)} custom-call(bf16[2,2,512,2048]{3,2,1,0:T(8,128)(2,1)} %refs_0_.5), custom_call_target="tpu_custom_call" | custom-call | flops 1000 | bytes 1000 | tf_op jit(solution)/shard_map/piece_of/pallas_call | solution.py:82
  1.6 2.5 %collective-permute-start.2 = (bf16[2,256,2048]{2,1,0:T(8,128)(2,1)S(1)}, bf16[2,256,2048]{2,1,0:T(8,128)(2,1)}, u32[]{:S(2)}, u32[]{:S(2)}) collective-permute-start(bf16[2,256,2048]{2,1,0:T(8,128)(2,1)S(1)} %piece_of.3.rest_0_), channel_id=1, source_target_pairs={{0,24},{8,0},{16,8},{24,16},{1,25},{9,1},{17,9},{25,17},{2,26},{10... | collective-permute-start | bytes 6291464 | tf_op jit(solution)/shard_map/ppermute | solution.py:35
  4.0 2.6 %piece_of.4.rest_0_ = bf16[2,256,2048]{2,1,0:T(8,128)(2,1)} custom-call(bf16[2,2,512,2048]{3,2,1,0:T(8,128)(2,1)} %refs_0_.5, bf16[2,256,2048]{2,1,0:T(8,128)(2,1)S(1)} %piece_of.3.rest_0_), custom_call_target="tpu_custom_call" | custom-call | flops 1000 | bytes 1000 | tf_op jit(solution)/shard_map/piece_of/pallas_call | solution.py:82
  6.6 0.7 collective-permute-start.1
  7.4 2.3 %piece_of.5 = bf16[2,192,2048]{2,1,0:T(8,128)(2,1)} custom-call(bf16[2,2,512,2048]{3,2,1,0:T(8,128)(2,1)} %refs_0_.5, bf16[2,256,2048]{2,1,0:T(8,128)(2,1)} %piece_of.4.rest_0_), custom_call_target="tpu_custom_call" | custom-call | flops 1000 | bytes 1000 | tf_op jit(solution)/shard_map/piece_of/pallas_call | solution.py:82
  9.8 0.1 select_reduce_fusion.1
  9.9 0.1 fusion.4
  10.1 0.1 copy.6
  10.4 17.2 %collective-permute-done.2.refs_1_ = bf16[2,256,2048]{2,1,0:T(8,128)(2,1)} collective-permute-done((bf16[2,256,2048]{2,1,0:T(8,128)(2,1)S(1)}, bf16[2,256,2048]{2,1,0:T(8,128)(2,1)}, u32[]{:S(2)}, u32[]{:S(2)}) %collective-permute-start.2) | collective-permute-done | bytes 2097184 | tf_op jit(solution)/shard_map/ppermute | solution.py:35
  27.6 7.7 %step.12 = (f32[4,64,512]{2,1,0:T(8,128)S(1)}, bf16[4,64,512]{2,1,0:T(8,128)(2,1)S(1)}, bf16[2,192,2048]{2,1,0:T(8,128)(2,1)S(1)}) custom-call(f32[11]{0:T(128)S(1)} %pad_maximum_fusion.1.table_ref, bf16[2,2,512,2048]{3,2,1,0:T(8,128)(2,1)} %refs_0_.5, bf16[2,256,2048]{2,1,0:T(8,128)(2,1)} %collective-permute-done.2.refs_1_), custom_call_target="tpu_custom_call" | custom-call | flops 1000 | bytes 1000 | tf_op jit(solution)/shard_map/step/pallas_call | solution.py:359
  35.3 2.1 %collective-permute-start.7 = (bf16[2,192,2048]{2,1,0:T(8,128)(2,1)S(1)}, bf16[2,192,2048]{2,1,0:T(8,128)(2,1)S(1)}, u32[]{:S(2)}, u32[]{:S(2)}) collective-permute-start(bf16[2,192,2048]{2,1,0:T(8,128)(2,1)S(1)} %get-tuple-element.46), channel_id=1, source_target_pairs={{0,24},{8,0},{16,8},{24,16},{1,25},{9,1},{17,9},{25,17},{2,26},{10... | collective-permute-start | bytes 4718600 | tf_op jit(solution)/shard_map/ppermute | solution.py:35
  37.4 1.5 %collective-permute-start.3 = (bf16[4,64,512]{2,1,0:T(8,128)(2,1)S(1)}, bf16[4,64,512]{2,1,0:T(8,128)(2,1)S(1)}, u32[]{:S(2)}, u32[]{:S(2)}) collective-permute-start(bf16[4,64,512]{2,1,0:T(8,128)(2,1)S(1)} %get-tuple-element.38), channel_id=1, source_target_pairs={{0,1},{1,0},{2,3},{3,2},{4,5},{5,4},{6,7},{7,6},{8,9},{9,8},{10,11... | collective-permute-start | bytes 786440 | tf_op jit(solution)/shard_map/ppermute | solution.py:35
  38.9 5.7 %collective-permute-done.3.refs_1_ = bf16[4,64,512]{2,1,0:T(8,128)(2,1)S(1)} collective-permute-done((bf16[4,64,512]{2,1,0:T(8,128)(2,1)S(1)}, bf16[4,64,512]{2,1,0:T(8,128)(2,1)S(1)}, u32[]{:S(2)}, u32[]{:S(2)}) %collective-permute-start.3) | collective-permute-done | bytes 262176 | tf_op jit(solution)/shard_map/ppermute | solution.py:35
  44.6 0.6 step.13
  45.2 1.6 %collective-permute-start.4 = (bf16[2,64,512]{2,1,0:T(8,128)(2,1)S(1)}, bf16[2,64,512]{2,1,0:T(8,128)(2,1)S(1)}, u32[]{:S(2)}, u32[]{:S(2)}) collective-permute-start(bf16[2,64,512]{2,1,0:T(8,128)(2,1)S(1)} %get-tuple-element.40), channel_id=1, source_target_pairs={{0,2},{1,3},{2,0},{3,1},{4,6},{5,7},{6,4},{7,5},{8,10},{9,11},{10,... | collective-permute-start | bytes 393224 | tf_op jit(solution)/shard_map/ppermute | solution.py:40
  46.9 3.3 %collective-permute-done.1.refs_1_ = bf16[2,256,2048]{2,1,0:T(8,128)(2,1)} collective-permute-done((bf16[2,256,2048]{2,1,0:T(8,128)(2,1)}, bf16[2,256,2048]{2,1,0:T(8,128)(2,1)}, u32[]{:S(2)}, u32[]{:S(2)}) %collective-permute-start.1) | collective-permute-done | bytes 2097184 | tf_op jit(solution)/shard_map/ppermute | solution.py:35
  50.2 0.1 collective-permute-done.4.refs_3_
  50.2 7.7 %step.14 = (f32[4,64,512]{2,1,0:T(8,128)S(1)}, bf16[4,64,512]{2,1,0:T(8,128)(2,1)S(1)}, f32[1,64,512]{2,1,0:T(8,128)S(1)}, bf16[1,64,512]{2,1,0:T(8,128)(2,1)S(1)}, bf16[2,128,2048]{2,1,0:T(8,128)(2,1)S(1)}) custom-call(f32[11]{0:T(128)S(1)} %pad_maximum_fusion.1.table_ref, bf16[2,2,512,2048]{3,2,1,0:T(8,128)(2,1)} %refs_0_.5, ...), custom_call_target="tpu_custom_call" | custom-call | flops 1000 | bytes 1000 | tf_op jit(solution)/shard_map/step/pallas_call | solution.py:359
  57.9 2.1 %collective-permute-start.12 = (bf16[2,128,2048]{2,1,0:T(8,128)(2,1)S(1)}, bf16[2,128,2048]{2,1,0:T(8,128)(2,1)S(1)}, u32[]{:S(2)}, u32[]{:S(2)}) collective-permute-start(bf16[2,128,2048]{2,1,0:T(8,128)(2,1)S(1)} %get-tuple-element.55), channel_id=1, source_target_pairs={{0,24},{8,0},{16,8},{24,16},{1,25},{9,1},{17,9},{25,17},{2,26},{10... | collective-permute-start | bytes 3145736 | tf_op jit(solution)/shard_map/ppermute | solution.py:35
  60.0 1.5 %collective-permute-start.5 = (bf16[4,64,512]{2,1,0:T(8,128)(2,1)S(1)}, bf16[4,64,512]{2,1,0:T(8,128)(2,1)S(1)}, u32[]{:S(2)}, u32[]{:S(2)}) collective-permute-start(bf16[4,64,512]{2,1,0:T(8,128)(2,1)S(1)} %get-tuple-element.42), channel_id=1, source_target_pairs={{0,1},{1,0},{2,3},{3,2},{4,5},{5,4},{6,7},{7,6},{8,9},{9,8},{10,11... | collective-permute-start | bytes 786440 | tf_op jit(solution)/shard_map/ppermute | solution.py:35
  61.5 2.6 %collective-permute-start.6 = (bf16[1,64,512]{2,1,0:T(8,128)(2,1)S(1)}, bf16[1,64,512]{2,1,0:T(8,128)(2,1)S(1)}, u32[]{:S(2)}, u32[]{:S(2)}) collective-permute-start(bf16[1,64,512]{2,1,0:T(8,128)(2,1)S(1)} %get-tuple-element.44), channel_id=1, source_target_pairs={{0,4},{1,5},{2,6},{3,7},{4,0},{5,1},{6,2},{7,3},{8,12},{9,13},{10,... | collective-permute-start | bytes 196616 | tf_op jit(solution)/shard_map/ppermute | solution.py:40
  64.1 2.9 %collective-permute-done.refs_1_ = bf16[2,192,2048]{2,1,0:T(8,128)(2,1)} collective-permute-done((bf16[2,192,2048]{2,1,0:T(8,128)(2,1)}, bf16[2,192,2048]{2,1,0:T(8,128)(2,1)}, u32[]{:S(2)}, u32[]{:S(2)}) %collective-permute-start) | collective-permute-done | bytes 1572896 | tf_op jit(solution)/shard_map/ppermute | solution.py:35
  67.0 0.2 collective-permute-done.5.refs_3_
  67.3 4.4 %step.15 = (bf16[384,2048]{1,0:T(8,128)(2,1)S(1)}, bf16[2,2,256,2048]{3,2,1,0:T(8,128)(2,1)S(1)}, bf16[4,64,384]{2,1,0:T(8,128)(2,1)S(1)}, f32[2,64,512]{2,1,0:T...) custom-call(f32[11]{0:T(128)S(1)} %pad_maximum_fusion.1.table_ref, ...), custom_call_target="tpu_custom_call" | custom-call | flops 1000 | bytes 1000 | tf_op jit(solution)/shard_map/step/pallas_call | solution.py:359
  71.7 1.5 %collective-permute-start.9 = (bf16[4,64,384]{2,1,0:T(8,128)(2,1)S(1)}, bf16[4,64,384]{2,1,0:T(8,128)(2,1)S(1)}, u32[]{:S(2)}, u32[]{:S(2)}) collective-permute-start(bf16[4,64,384]{2,1,0:T(8,128)(2,1)S(1)} %get-tuple-element.50), channel_id=1, source_target_pairs={{0,1},{1,0},{2,3},{3,2},{4,5},{5,4},{6,7},{7,6},{8,9},{9,8},{10,11... | collective-permute-start | bytes 589832 | tf_op jit(solution)/shard_map/ppermute | solution.py:35
  73.2 1.6 %collective-permute-start.8 = (bf16[2,64,512]{2,1,0:T(8,128)(2,1)S(1)}, bf16[2,64,512]{2,1,0:T(8,128)(2,1)S(1)}, u32[]{:S(2)}, u32[]{:S(2)}) collective-permute-start(bf16[2,64,512]{2,1,0:T(8,128)(2,1)S(1)} %get-tuple-element.48), channel_id=1, source_target_pairs={{0,2},{1,3},{2,0},{3,1},{4,6},{5,7},{6,4},{7,5},{8,10},{9,11},{10,... | collective-permute-start | bytes 393224 | tf_op jit(solution)/shard_map/ppermute | solution.py:40
  74.8 1.9 %step.16.refs_0_ = f32[4,64,384]{2,1,0:T(8,128)S(1)} custom-call(f32[11]{0:T(128)S(1)} %pad_maximum_fusion.1.table_ref, bf16[2,2,256,2048]{3,2,1,0:T(8,128)(2,1)S(1)} %get-tuple-element.45.refs_0_, bf16[384,2048]{1,0:T(8,128)(2,1)S(1)} %get-tuple-element.49.refs_1_), custom_call_target="tpu_custom_call" | custom-call | flops 1000 | bytes 1000 | tf_op jit(solution)/shard_map/step/pallas_call | solution.py:359
  76.7 2.5 %collective-permute-done.9.refs_1_ = bf16[4,64,384]{2,1,0:T(8,128)(2,1)S(1)} collective-permute-done((bf16[4,64,384]{2,1,0:T(8,128)(2,1)S(1)}, bf16[4,64,384]{2,1,0:T(8,128)(2,1)S(1)}, u32[]{:S(2)}, u32[]{:S(2)}) %collective-permute-start.9) | collective-permute-done | bytes 196640 | tf_op jit(solution)/shard_map/ppermute | solution.py:35
  79.1 0.6 step.17
  79.7 1.6 %collective-permute-start.10 = (bf16[2,64,384]{2,1,0:T(8,128)(2,1)S(1)}, bf16[2,64,384]{2,1,0:T(8,128)(2,1)S(1)}, u32[]{:S(2)}, u32[]{:S(2)}) collective-permute-start(bf16[2,64,384]{2,1,0:T(8,128)(2,1)S(1)} %get-tuple-element.52), channel_id=1, source_target_pairs={{0,2},{1,3},{2,0},{3,1},{4,6},{5,7},{6,4},{7,5},{8,10},{9,11},{10,... | collective-permute-start | bytes 294920 | tf_op jit(solution)/shard_map/ppermute | solution.py:40
  81.4 3.0 %collective-permute-done.10.refs_5_ = bf16[2,64,384]{2,1,0:T(8,128)(2,1)S(1)} collective-permute-done((bf16[2,64,384]{2,1,0:T(8,128)(2,1)S(1)}, bf16[2,64,384]{2,1,0:T(8,128)(2,1)S(1)}, u32[]{:S(2)}, u32[]{:S(2)}) %collective-permute-start.10) | collective-permute-done | bytes 98336 | tf_op jit(solution)/shard_map/ppermute | solution.py:40
  84.4 2.4 %step.18 = (bf16[384,2048]{1,0:T(8,128)(2,1)S(1)}, bf16[4,64,384]{2,1,0:T(8,128)(2,1)S(1)}, f32[1,64,896]{2,1,0:T(8,128)S(1)}, bf16[1,64,896]{2,1,0:T(8,128)(2,1)S(1)}) custom-call(f32[11]{0:T(128)S(1)} %pad_maximum_fusion.1.table_ref, bf16[2,2,256,2048]{3,2,1,0:T(8,128)(2,1)S(1)} %get-tuple-element.45.refs_0_, ...), custom_call_target="tpu_custom_call" | custom-call | flops 1000 | bytes 1000 | tf_op jit(solution)/shard_map/step/pallas_call | solution.py:359
  86.9 1.6 %collective-permute-start.13 = (bf16[4,64,384]{2,1,0:T(8,128)(2,1)S(1)}, bf16[4,64,384]{2,1,0:T(8,128)(2,1)S(1)}, u32[]{:S(2)}, u32[]{:S(2)}) collective-permute-start(bf16[4,64,384]{2,1,0:T(8,128)(2,1)S(1)} %get-tuple-element.57), channel_id=1, source_target_pairs={{0,1},{1,0},{2,3},{3,2},{4,5},{5,4},{6,7},{7,6},{8,9},{9,8},{10,11... | collective-permute-start | bytes 589832 | tf_op jit(solution)/shard_map/ppermute | solution.py:35
  88.4 2.6 %collective-permute-start.11 = (bf16[1,64,896]{2,1,0:T(8,128)(2,1)S(1)}, bf16[1,64,896]{2,1,0:T(8,128)(2,1)S(1)}, u32[]{:S(2)}, u32[]{:S(2)}) collective-permute-start(bf16[1,64,896]{2,1,0:T(8,128)(2,1)S(1)} %get-tuple-element.54), channel_id=1, source_target_pairs={{0,4},{1,5},{2,6},{3,7},{4,0},{5,1},{6,2},{7,3},{8,12},{9,13},{10,... | collective-permute-start | bytes 344072 | tf_op jit(solution)/shard_map/ppermute | solution.py:40
  91.0 1.9 %step.19.refs_2_ = f32[4,64,384]{2,1,0:T(8,128)S(1)} custom-call(f32[11]{0:T(128)S(1)} %pad_maximum_fusion.1.table_ref, bf16[2,2,256,2048]{3,2,1,0:T(8,128)(2,1)S(1)} %get-tuple-element.45.refs_0_, bf16[384,2048]{1,0:T(8,128)(2,1)S(1)} %get-tuple-element.56.refs_1_), custom_call_target="tpu_custom_call" | custom-call | flops 1000 | bytes 1000 | tf_op jit(solution)/shard_map/step/pallas_call | solution.py:359
  92.9 2.1 %collective-permute-done.12.refs_1_ = bf16[2,128,2048]{2,1,0:T(8,128)(2,1)S(1)} collective-permute-done((bf16[2,128,2048]{2,1,0:T(8,128)(2,1)S(1)}, bf16[2,128,2048]{2,1,0:T(8,128)(2,1)S(1)}, u32[]{:S(2)}, u32[]{:S(2)}) %collective-permute-start.12) | collective-permute-done | bytes 1048608 | tf_op jit(solution)/shard_map/ppermute | solution.py:35
  95.0 1.7 %collective-permute-done.11.refs_5_.refs_1_ = bf16[1,64,896]{2,1,0:T(8,128)(2,1)S(1)} collective-permute-done((bf16[1,64,896]{2,1,0:T(8,128)(2,1)S(1)}, bf16[1,64,896]{2,1,0:T(8,128)(2,1)S(1)}, u32[]{:S(2)}, u32[]{:S(2)}) %collective-permute-start.11) | collective-permute-done | bytes 114720 | tf_op jit(solution)/shard_map/ppermute | solution.py:40
  96.7 1.7 %step.20 = (bf16[256,2048]{1,0:T(8,128)(2,1)S(1)}, bf16[4,64,256]{2,1,0:T(8,128)(2,1)S(1)}, f32[2,64,384]{2,1,0:T(8,128)S(1)}, bf16[2,64,384]{2,1,0:T(8,128)(2,1)S(1)}, f32[64,2,2,512]{3,2,1,0:T(2,128)}) custom-call(f32[11]{0:T(128)S(1)} %pad_maximum_fusion.1.table_ref, ...), custom_call_target="tpu_custom_call", output_to_operand_aliasing={{4}: (7, {})} | custom-call | flops 1000 | bytes 1000 | tf_op jit(solution)/shard_map/step/pallas_call | solution.py:359
  98.5 0.6 collective-permute-start.14
  99.1 0.8 collective-permute-start.15
  99.9 1.3 %step.21.refs_0_ = f32[4,64,256]{2,1,0:T(8,128)S(1)} custom-call(f32[11]{0:T(128)S(1)} %pad_maximum_fusion.1.table_ref, bf16[2,2,256,2048]{3,2,1,0:T(8,128)(2,1)S(1)} %get-tuple-element.45.refs_0_, bf16[256,2048]{1,0:T(8,128)(2,1)S(1)} %get-tuple-element.59.refs_1_), custom_call_target="tpu_custom_call" | custom-call | flops 1000 | bytes 1000 | tf_op jit(solution)/shard_map/step/pallas_call | solution.py:359
  101.2 2.5 %collective-permute-done.15.refs_3_ = bf16[2,64,384]{2,1,0:T(8,128)(2,1)S(1)} collective-permute-done((bf16[2,64,384]{2,1,0:T(8,128)(2,1)S(1)}, bf16[2,64,384]{2,1,0:T(8,128)(2,1)S(1)}, u32[]{:S(2)}, u32[]{:S(2)}) %collective-permute-start.15) | collective-permute-done | bytes 98336 | tf_op jit(solution)/shard_map/ppermute | solution.py:40
  103.7 0.6 step.22
  104.3 2.5 %collective-permute-start.16 = (bf16[1,64,640]{2,1,0:T(8,128)(2,1)S(1)}, bf16[1,64,640]{2,1,0:T(8,128)(2,1)S(1)}, u32[]{:S(2)}, u32[]{:S(2)}) collective-permute-start(bf16[1,64,640]{2,1,0:T(8,128)(2,1)S(1)} %get-tuple-element.64), channel_id=1, source_target_pairs={{0,4},{1,5},{2,6},{3,7},{4,0},{5,1},{6,2},{7,3},{8,12},{9,13},{10,... | collective-permute-start | bytes 245768 | tf_op jit(solution)/shard_map/ppermute | solution.py:40
  106.8 1.4 %collective-permute-start.17 = (bf16[1,64,256]{2,1,0:T(8,128)(2,1)S(1)}, bf16[1,64,256]{2,1,0:T(8,128)(2,1)S(1)}, u32[]{:S(2)}, u32[]{:S(2)}) collective-permute-start(bf16[1,64,256]{2,1,0:T(8,128)(2,1)S(1)} %get-tuple-element.66), channel_id=1, source_target_pairs={{0,6},{1,7},{2,4},{3,5},{4,2},{5,3},{6,0},{7,1},{8,14},{9,15},{10,... | collective-permute-start | bytes 98312 | tf_op jit(solution)/shard_map/ppermute | solution.py:40
  108.2 0.5 collective-permute-start.18
  108.7 3.9 %collective-permute-done.17.refs_5_ = bf16[1,64,256]{2,1,0:T(8,128)(2,1)S(1)} collective-permute-done((bf16[1,64,256]{2,1,0:T(8,128)(2,1)S(1)}, bf16[1,64,256]{2,1,0:T(8,128)(2,1)S(1)}, u32[]{:S(2)}, u32[]{:S(2)}) %collective-permute-start.17) | collective-permute-done | bytes 32800 | tf_op jit(solution)/shard_map/ppermute | solution.py:40
  112.5 1.5 %step.23 = f32[64,2,2,512]{3,2,1,0:T(2,128)} custom-call(f32[11]{0:T(128)S(1)} %pad_maximum_fusion.1.table_ref, f32[1,64,896]{2,1,0:T(8,128)S(1)} %get-tuple-element.53.refs_4_.refs_0_, bf16[1,64,896]{2,1,0:T(8,128)(2,1)S(1)} %collective-permute-done.11.refs_5_.refs_1_, f32[1,64,384]{2,1,0:T(8,128)S(1)} %get-tuple-element.63.refs_2_, ...), custom_call_target="tpu_custom_call", output_to_operand_aliasing={{}: (9, {})} | custom-call | flops 1000 | bytes 1000 | tf_op jit(solution)/shard_map/step/pallas_call | solution.py:359
  (17 shorter events, 0.4 us)
Async XLA Ops:
  1.6 26.0 %collective-permute-start.2 = (bf16[2,256,2048]{2,1,0:T(8,128)(2,1)S(1)}, bf16[2,256,2048]{2,1,0:T(8,128)(2,1)}, u32[]{:S(2)}, u32[]{:S(2)}) collective-permute-start(bf16[2,256,2048]{2,1,0:T(8,128)(2,1)S(1)} %piece_of.3.rest_0_), channel_id=1, source_target_pairs={{0,24},{8,0},{16,8},{24,16},{1,25},{9,1},{17,9},{25,17},{2,26},{10... | collective-permute-start | bytes 6291464 | tf_op jit(solution)/shard_map/ppermute | solution.py:35
  6.6 3.1 %copy-start = (s32[2]{0:T(128)S(1)}, s32[2]{0:T(128)}, u32[]{:S(2)}) copy-start(s32[2]{0:T(128)} %param.4) | copy-start | bytes 28
  6.6 3.1 %copy-start.1 = (s32[2]{0:T(128)S(1)}, s32[2]{0:T(128)}, u32[]{:S(2)}) copy-start(s32[2]{0:T(128)} %param.5) | copy-start | bytes 28
  6.6 43.5 %collective-permute-start.1 = (bf16[2,256,2048]{2,1,0:T(8,128)(2,1)}, bf16[2,256,2048]{2,1,0:T(8,128)(2,1)}, u32[]{:S(2)}, u32[]{:S(2)}) collective-permute-start(bf16[2,256,2048]{2,1,0:T(8,128)(2,1)} %piece_of.4.rest_0_), channel_id=1, source_target_pairs={{0,24},{8,0},{16,8},{24,16},{1,25},{9,1},{17,9},{25,17},{2,26},{10... | collective-permute-start | bytes 6291464 | tf_op jit(solution)/shard_map/ppermute | solution.py:35
  9.7 57.3 %collective-permute-start = (bf16[2,192,2048]{2,1,0:T(8,128)(2,1)}, bf16[2,192,2048]{2,1,0:T(8,128)(2,1)}, u32[]{:S(2)}, u32[]{:S(2)}) collective-permute-start(bf16[2,192,2048]{2,1,0:T(8,128)(2,1)} %piece_of.5), channel_id=1, source_target_pairs={{0,24},{8,0},{16,8},{24,16},{1,25},{9,1},{17,9},{25,17},{2,26},{10... | collective-permute-start | bytes 4718600 | tf_op jit(solution)/shard_map/ppermute | solution.py:35
  35.3 49.1 %collective-permute-start.7 = (bf16[2,192,2048]{2,1,0:T(8,128)(2,1)S(1)}, bf16[2,192,2048]{2,1,0:T(8,128)(2,1)S(1)}, u32[]{:S(2)}, u32[]{:S(2)}) collective-permute-start(bf16[2,192,2048]{2,1,0:T(8,128)(2,1)S(1)} %get-tuple-element.46), channel_id=1, source_target_pairs={{0,24},{8,0},{16,8},{24,16},{1,25},{9,1},{17,9},{25,17},{2,26},{10... | collective-permute-start | bytes 4718600 | tf_op jit(solution)/shard_map/ppermute | solution.py:35
  37.4 7.2 %collective-permute-start.3 = (bf16[4,64,512]{2,1,0:T(8,128)(2,1)S(1)}, bf16[4,64,512]{2,1,0:T(8,128)(2,1)S(1)}, u32[]{:S(2)}, u32[]{:S(2)}) collective-permute-start(bf16[4,64,512]{2,1,0:T(8,128)(2,1)S(1)} %get-tuple-element.38), channel_id=1, source_target_pairs={{0,1},{1,0},{2,3},{3,2},{4,5},{5,4},{6,7},{7,6},{8,9},{9,8},{10,11... | collective-permute-start | bytes 786440 | tf_op jit(solution)/shard_map/ppermute | solution.py:35
  45.2 5.0 %collective-permute-start.4 = (bf16[2,64,512]{2,1,0:T(8,128)(2,1)S(1)}, bf16[2,64,512]{2,1,0:T(8,128)(2,1)S(1)}, u32[]{:S(2)}, u32[]{:S(2)}) collective-permute-start(bf16[2,64,512]{2,1,0:T(8,128)(2,1)S(1)} %get-tuple-element.40), channel_id=1, source_target_pairs={{0,2},{1,3},{2,0},{3,1},{4,6},{5,7},{6,4},{7,5},{8,10},{9,11},{10,... | collective-permute-start | bytes 393224 | tf_op jit(solution)/shard_map/ppermute | solution.py:40
  57.9 37.0 %collective-permute-start.12 = (bf16[2,128,2048]{2,1,0:T(8,128)(2,1)S(1)}, bf16[2,128,2048]{2,1,0:T(8,128)(2,1)S(1)}, u32[]{:S(2)}, u32[]{:S(2)}) collective-permute-start(bf16[2,128,2048]{2,1,0:T(8,128)(2,1)S(1)} %get-tuple-element.55), channel_id=1, source_target_pairs={{0,24},{8,0},{16,8},{24,16},{1,25},{9,1},{17,9},{25,17},{2,26},{10... | collective-permute-start | bytes 3145736 | tf_op jit(solution)/shard_map/ppermute | solution.py:35
  60.0 7.2 %collective-permute-start.5 = (bf16[4,64,512]{2,1,0:T(8,128)(2,1)S(1)}, bf16[4,64,512]{2,1,0:T(8,128)(2,1)S(1)}, u32[]{:S(2)}, u32[]{:S(2)}) collective-permute-start(bf16[4,64,512]{2,1,0:T(8,128)(2,1)S(1)} %get-tuple-element.42), channel_id=1, source_target_pairs={{0,1},{1,0},{2,3},{3,2},{4,5},{5,4},{6,7},{7,6},{8,9},{9,8},{10,11... | collective-permute-start | bytes 786440 | tf_op jit(solution)/shard_map/ppermute | solution.py:35
  61.5 5.5 %collective-permute-start.6 = (bf16[1,64,512]{2,1,0:T(8,128)(2,1)S(1)}, bf16[1,64,512]{2,1,0:T(8,128)(2,1)S(1)}, u32[]{:S(2)}, u32[]{:S(2)}) collective-permute-start(bf16[1,64,512]{2,1,0:T(8,128)(2,1)S(1)} %get-tuple-element.44), channel_id=1, source_target_pairs={{0,4},{1,5},{2,6},{3,7},{4,0},{5,1},{6,2},{7,3},{8,12},{9,13},{10,... | collective-permute-start | bytes 196616 | tf_op jit(solution)/shard_map/ppermute | solution.py:40
  71.7 7.5 %collective-permute-start.9 = (bf16[4,64,384]{2,1,0:T(8,128)(2,1)S(1)}, bf16[4,64,384]{2,1,0:T(8,128)(2,1)S(1)}, u32[]{:S(2)}, u32[]{:S(2)}) collective-permute-start(bf16[4,64,384]{2,1,0:T(8,128)(2,1)S(1)} %get-tuple-element.50), channel_id=1, source_target_pairs={{0,1},{1,0},{2,3},{3,2},{4,5},{5,4},{6,7},{7,6},{8,9},{9,8},{10,11... | collective-permute-start | bytes 589832 | tf_op jit(solution)/shard_map/ppermute | solution.py:35
  73.2 8.2 %collective-permute-start.8 = (bf16[2,64,512]{2,1,0:T(8,128)(2,1)S(1)}, bf16[2,64,512]{2,1,0:T(8,128)(2,1)S(1)}, u32[]{:S(2)}, u32[]{:S(2)}) collective-permute-start(bf16[2,64,512]{2,1,0:T(8,128)(2,1)S(1)} %get-tuple-element.48), channel_id=1, source_target_pairs={{0,2},{1,3},{2,0},{3,1},{4,6},{5,7},{6,4},{7,5},{8,10},{9,11},{10,... | collective-permute-start | bytes 393224 | tf_op jit(solution)/shard_map/ppermute | solution.py:40
  79.7 4.7 %collective-permute-start.10 = (bf16[2,64,384]{2,1,0:T(8,128)(2,1)S(1)}, bf16[2,64,384]{2,1,0:T(8,128)(2,1)S(1)}, u32[]{:S(2)}, u32[]{:S(2)}) collective-permute-start(bf16[2,64,384]{2,1,0:T(8,128)(2,1)S(1)} %get-tuple-element.52), channel_id=1, source_target_pairs={{0,2},{1,3},{2,0},{3,1},{4,6},{5,7},{6,4},{7,5},{8,10},{9,11},{10,... | collective-permute-start | bytes 294920 | tf_op jit(solution)/shard_map/ppermute | solution.py:40
  86.9 9.9 %collective-permute-start.13 = (bf16[4,64,384]{2,1,0:T(8,128)(2,1)S(1)}, bf16[4,64,384]{2,1,0:T(8,128)(2,1)S(1)}, u32[]{:S(2)}, u32[]{:S(2)}) collective-permute-start(bf16[4,64,384]{2,1,0:T(8,128)(2,1)S(1)} %get-tuple-element.57), channel_id=1, source_target_pairs={{0,1},{1,0},{2,3},{3,2},{4,5},{5,4},{6,7},{7,6},{8,9},{9,8},{10,11... | collective-permute-start | bytes 589832 | tf_op jit(solution)/shard_map/ppermute | solution.py:35
  88.4 8.3 %collective-permute-start.11 = (bf16[1,64,896]{2,1,0:T(8,128)(2,1)S(1)}, bf16[1,64,896]{2,1,0:T(8,128)(2,1)S(1)}, u32[]{:S(2)}, u32[]{:S(2)}) collective-permute-start(bf16[1,64,896]{2,1,0:T(8,128)(2,1)S(1)} %get-tuple-element.54), channel_id=1, source_target_pairs={{0,4},{1,5},{2,6},{3,7},{4,0},{5,1},{6,2},{7,3},{8,12},{9,13},{10,... | collective-permute-start | bytes 344072 | tf_op jit(solution)/shard_map/ppermute | solution.py:40
  98.5 5.2 %collective-permute-start.14 = (bf16[4,64,256]{2,1,0:T(8,128)(2,1)S(1)}, bf16[4,64,256]{2,1,0:T(8,128)(2,1)S(1)}, u32[]{:S(2)}, u32[]{:S(2)}) collective-permute-start(bf16[4,64,256]{2,1,0:T(8,128)(2,1)S(1)} %get-tuple-element.60), channel_id=1, source_target_pairs={{0,1},{1,0},{2,3},{3,2},{4,5},{5,4},{6,7},{7,6},{8,9},{9,8},{10,11... | collective-permute-start | bytes 393224 | tf_op jit(solution)/shard_map/ppermute | solution.py:35
  99.1 4.6 %collective-permute-start.15 = (bf16[2,64,384]{2,1,0:T(8,128)(2,1)S(1)}, bf16[2,64,384]{2,1,0:T(8,128)(2,1)S(1)}, u32[]{:S(2)}, u32[]{:S(2)}) collective-permute-start(bf16[2,64,384]{2,1,0:T(8,128)(2,1)S(1)} %get-tuple-element.62), channel_id=1, source_target_pairs={{0,2},{1,3},{2,0},{3,1},{4,6},{5,7},{6,4},{7,5},{8,10},{9,11},{10,... | collective-permute-start | bytes 294920 | tf_op jit(solution)/shard_map/ppermute | solution.py:40
  104.3 8.3 %collective-permute-start.16 = (bf16[1,64,640]{2,1,0:T(8,128)(2,1)S(1)}, bf16[1,64,640]{2,1,0:T(8,128)(2,1)S(1)}, u32[]{:S(2)}, u32[]{:S(2)}) collective-permute-start(bf16[1,64,640]{2,1,0:T(8,128)(2,1)S(1)} %get-tuple-element.64), channel_id=1, source_target_pairs={{0,4},{1,5},{2,6},{3,7},{4,0},{5,1},{6,2},{7,3},{8,12},{9,13},{10,... | collective-permute-start | bytes 245768 | tf_op jit(solution)/shard_map/ppermute | solution.py:40
  106.8 5.7 %collective-permute-start.17 = (bf16[1,64,256]{2,1,0:T(8,128)(2,1)S(1)}, bf16[1,64,256]{2,1,0:T(8,128)(2,1)S(1)}, u32[]{:S(2)}, u32[]{:S(2)}) collective-permute-start(bf16[1,64,256]{2,1,0:T(8,128)(2,1)S(1)} %get-tuple-element.66), channel_id=1, source_target_pairs={{0,6},{1,7},{2,4},{3,5},{4,2},{5,3},{6,0},{7,1},{8,14},{9,15},{10,... | collective-permute-start | bytes 98312 | tf_op jit(solution)/shard_map/ppermute | solution.py:40
  108.2 4.4 %collective-permute-start.18 = (bf16[1,64,256]{2,1,0:T(8,128)(2,1)S(1)}, bf16[1,64,256]{2,1,0:T(8,128)(2,1)S(1)}, u32[]{:S(2)}, u32[]{:S(2)}) collective-permute-start(bf16[1,64,256]{2,1,0:T(8,128)(2,1)S(1)} %get-tuple-element.67), channel_id=1, source_target_pairs={{0,2},{1,3},{2,0},{3,1},{4,6},{5,7},{6,4},{7,5},{8,10},{9,11},{10,... | collective-permute-start | bytes 98312 | tf_op jit(solution)/shard_map/ppermute | solution.py:40

commit v20 on v19

--- a/solution.py
+++ b/solution.py
@@ -138,7 +138,7 @@
     if plan.adding and plan.placed:
         take(1)
     given_ref = take(1)[0] if plan.near == "give" else None
-    kept_ref = take(1)[0] if plan.rows == "keep" else None
+    kept_ref = take(1)[0] if plan.ahead else None
     outs = take(len(plan.ways))
     targets = [take(task.count) for task in plan.tasks]
     result_ref = take(1)[0] if plan.adding else None
@@ -147,11 +147,9 @@
         slot, _, width = plan.part
         base = slot * stride
         point = table_ref[base].astype(jnp.int32)
-        own_ref = bands_ref
-        own = []
-        if plan.rows != "held":
-            own_ref = take(1)[0] if plan.rows == "load" else kept_ref
-            own_sems = take(1)[0]
+
+        def load_rows(point, into_ref, load_sems):
+            copies = []
             for distance in range(1, fold + 1):
                 way = distance % fold
                 target = lax.rem(place + way, fold)
@@ -160,11 +158,21 @@
                         first = pl.multiple_of((level * fold + target) * rows, rows)
                         copy = pltpu.make_async_copy(
                             bands_ref.at[point, part, pl.ds(first, rows), :],
-                            own_ref.at[way, part, pl.ds(level * rows, rows), :],
-                            own_sems.at[way, part, level],
+                            into_ref.at[way, part, pl.ds(level * rows, rows), :],
+                            load_sems.at[way, part, level],
                         )
                         copy.start()
-                        own.append((way, part, copy))
+                        copies.append((way, part, copy))
+            return copies
+
+        own_ref = bands_ref
+        own, ahead = [], []
+        if plan.rows != "held":
+            own_ref, own_sems = take(2)
+            own = load_rows(point, own_ref, own_sems)
+        if plan.ahead:
+            next_point = table_ref[base + stride].astype(jnp.int32)
+            ahead = load_rows(next_point, kept_ref, take(1)[0])
     if plan.later:
         piece_buf, piece_sems = take(2)
         later_slot, later_start, later_width = plan.later
@@ -248,9 +256,8 @@
                 for load, store in zip(loads, stores):
                     load.wait()
                     store.start()
-        for way, _, copy in own:
-            if way not in plan.ways:
-                copy.wait()
+        for _, _, copy in ahead:
+            copy.wait()
     if plan.adding:
         placing.wait()
     if plan.later:
@@ -288,6 +295,7 @@
     ways: tuple
     near: str
     rows: str
+    ahead: bool
     tasks: tuple
     takes: tuple
     adding: tuple
@@ -316,14 +324,15 @@
         kept = (fold, 2, depth * rows, points)
         if plan.near == "give":
             out_shape.append(jax.ShapeDtypeStruct((2 * width, points), jnp.bfloat16))
-        if plan.rows == "keep":
+        if plan.ahead:
             out_shape.append(jax.ShapeDtypeStruct(kept, jnp.bfloat16))
         out_shape += [
             jax.ShapeDtypeStruct((depth, rows, 2 * width), kind(way)) for way in plan.ways
         ]
-        if plan.rows == "load":
+        if plan.rows != "held":
             scratch.append(pltpu.VMEM(kept, jnp.bfloat16))
-        if plan.rows != "held":
+            scratch.append(pltpu.SemaphoreType.DMA((fold, 2, depth)))
+        if plan.ahead:
             scratch.append(pltpu.SemaphoreType.DMA((fold, 2, depth)))
     for arrays in [*sources, arrived]:
         operands += arrays
@@ -373,7 +382,7 @@
     piece = outs.pop() if plan.later else None
     result = outs.pop() if plan.adding else result
     near = outs.pop(0) if plan.near == "give" else None
-    kept = outs.pop(0) if plan.rows == "keep" else None
+    kept = outs.pop(0) if plan.ahead else None
     terms = outs[: len(plan.ways)]
     handed = outs[len(plan.ways) :]
     sends = []
@@ -485,7 +494,8 @@
             part,
             ways,
             phase,
-            "held" if kept is not None else "keep" if phase == "give" else "load",
+            "load" if kept is None else "held",
+            place == len(parts) - 4,
             tasks,
             tuple(len(arrays) for arrays in sources),
             adding,

time: 114 us -> 114 us (level)
  transfers between devices with their start and end apart: 19 -> 19, of which waited for: 12 -> 14; matrix products, arithmetic and copies ran while one was open for 1% -> 1% of each run, Pallas kernels for 29% -> 29%
where the time goes in v20:
time: 114 us
  waiting for transfers between devices  45.1 us (40%)
  Pallas kernels  38.8 us (34%)
  starting transfers between devices  29.4 us (26%)
    ppermute x10, waiting for transfers between devices, shifted(): return lax.ppermute(block, axis, route)  33.2 us
    pallas_call x12, Pallas kernels, step(): pl.pallas_call(functools.partial(step_kernel, plan), in_specs=in_specs, o...  32.3 us
    ppermute x9, starting transfers between devices, swapped(): return lax.ppermute(block, axis, [(i, i ^ distance) for i in range(count)])  15.2 us
    ppermute x10, starting transfers between devices, shifted(): return lax.ppermute(block, axis, route)  14.1 us
    ppermute x9, waiting for transfers between devices, swapped(): return lax.ppermute(block, axis, [(i, i ^ distance) for i in range(count)])  11.9 us
    pallas_call x3, Pallas kernels, piece_of(): pl.pallas_call(functools.partial(piece_kernel if after else first_kernel,...  6.46 us
  transfers between devices with their start and end apart: 19, of which 14 were waited for; matrix products, arithmetic and copies ran while one was open for 1% of the time, Pallas kernels for 29%

profile of v20, /device:TPU:0, one launch (start us, length us, event | category | flops | bytes accessed | tf_op | source)
XLA Modules:
  0.0 114.2 jit_solution(18272445994352074238)
XLA Ops:
  0.0 1.6 %piece_of.3.rest_0_ = bf16[2,256,2048]{2,1,0:T(8,128)(2,1)S(1)} custom-call(bf16[2,2,512,2048]{3,2,1,0:T(8,128)(2,1)} %bands_ref.5), custom_call_target="tpu_custom_call" | custom-call | flops 1000 | bytes 1000 | tf_op jit(solution)/shard_map/piece_of/pallas_call | solution.py:82
  1.6 2.5 %collective-permute-start.1 = (bf16[2,256,2048]{2,1,0:T(8,128)(2,1)S(1)}, bf16[2,256,2048]{2,1,0:T(8,128)(2,1)}, u32[]{:S(2)}, u32[]{:S(2)}) collective-permute-start(bf16[2,256,2048]{2,1,0:T(8,128)(2,1)S(1)} %piece_of.3.rest_0_), channel_id=1, source_target_pairs={{0,24},{8,0},{16,8},{24,16},{1,25},{9,1},{17,9},{25,17},{2,26},{10... | collective-permute-start | bytes 6291464 | tf_op jit(solution)/shard_map/ppermute | solution.py:35
  4.0 2.6 %piece_of.4.rest_0_ = bf16[2,256,2048]{2,1,0:T(8,128)(2,1)} custom-call(bf16[2,2,512,2048]{3,2,1,0:T(8,128)(2,1)} %bands_ref.5, bf16[2,256,2048]{2,1,0:T(8,128)(2,1)S(1)} %piece_of.3.rest_0_), custom_call_target="tpu_custom_call" | custom-call | flops 1000 | bytes 1000 | tf_op jit(solution)/shard_map/piece_of/pallas_call | solution.py:82
  6.6 0.7 collective-permute-start
  7.4 2.3 %piece_of.5 = bf16[2,192,2048]{2,1,0:T(8,128)(2,1)} custom-call(bf16[2,2,512,2048]{3,2,1,0:T(8,128)(2,1)} %bands_ref.5, bf16[2,256,2048]{2,1,0:T(8,128)(2,1)} %piece_of.4.rest_0_), custom_call_target="tpu_custom_call" | custom-call | flops 1000 | bytes 1000 | tf_op jit(solution)/shard_map/piece_of/pallas_call | solution.py:82
  9.8 0.1 select_reduce_fusion.1
  9.9 0.1 fusion.4
  10.4 17.2 %collective-permute-done.1.refs_1_ = bf16[2,256,2048]{2,1,0:T(8,128)(2,1)} collective-permute-done((bf16[2,256,2048]{2,1,0:T(8,128)(2,1)S(1)}, bf16[2,256,2048]{2,1,0:T(8,128)(2,1)}, u32[]{:S(2)}, u32[]{:S(2)}) %collective-permute-start.1) | collective-permute-done | bytes 2097184 | tf_op jit(solution)/shard_map/ppermute | solution.py:35
  27.6 7.7 %step.12 = (f32[4,64,512]{2,1,0:T(8,128)S(1)}, bf16[4,64,512]{2,1,0:T(8,128)(2,1)S(1)}, bf16[2,192,2048]{2,1,0:T(8,128)(2,1)S(1)}) custom-call(f32[11]{0:T(128)S(1)} %pad_maximum_fusion.1.table_ref, bf16[2,2,512,2048]{3,2,1,0:T(8,128)(2,1)} %bands_ref.5, bf16[2,256,2048]{2,1,0:T(8,128)(2,1)} %collective-permute-done.1.refs_1_), custom_call_target="tpu_custom_call" | custom-call | flops 1000 | bytes 1000 | tf_op jit(solution)/shard_map/step/pallas_call | solution.py:368
  35.3 2.1 %collective-permute-start.4 = (bf16[2,192,2048]{2,1,0:T(8,128)(2,1)S(1)}, bf16[2,192,2048]{2,1,0:T(8,128)(2,1)S(1)}, u32[]{:S(2)}, u32[]{:S(2)}) collective-permute-start(bf16[2,192,2048]{2,1,0:T(8,128)(2,1)S(1)} %get-tuple-element.42), channel_id=1, source_target_pairs={{0,24},{8,0},{16,8},{24,16},{1,25},{9,1},{17,9},{25,17},{2,26},{10... | collective-permute-start | bytes 4718600 | tf_op jit(solution)/shard_map/ppermute | solution.py:35
  37.4 1.5 %collective-permute-start.2 = (bf16[4,64,512]{2,1,0:T(8,128)(2,1)S(1)}, bf16[4,64,512]{2,1,0:T(8,128)(2,1)S(1)}, u32[]{:S(2)}, u32[]{:S(2)}) collective-permute-start(bf16[4,64,512]{2,1,0:T(8,128)(2,1)S(1)} %get-tuple-element.38), channel_id=1, source_target_pairs={{0,1},{1,0},{2,3},{3,2},{4,5},{5,4},{6,7},{7,6},{8,9},{9,8},{10,11... | collective-permute-start | bytes 786440 | tf_op jit(solution)/shard_map/ppermute | solution.py:35
  38.9 5.7 %collective-permute-done.2.refs_1_ = bf16[4,64,512]{2,1,0:T(8,128)(2,1)S(1)} collective-permute-done((bf16[4,64,512]{2,1,0:T(8,128)(2,1)S(1)}, bf16[4,64,512]{2,1,0:T(8,128)(2,1)S(1)}, u32[]{:S(2)}, u32[]{:S(2)}) %collective-permute-start.2) | collective-permute-done | bytes 262176 | tf_op jit(solution)/shard_map/ppermute | solution.py:35
  44.6 0.6 step.13
  45.2 1.6 %collective-permute-start.3 = (bf16[2,64,512]{2,1,0:T(8,128)(2,1)S(1)}, bf16[2,64,512]{2,1,0:T(8,128)(2,1)S(1)}, u32[]{:S(2)}, u32[]{:S(2)}) collective-permute-start(bf16[2,64,512]{2,1,0:T(8,128)(2,1)S(1)} %get-tuple-element.40), channel_id=1, source_target_pairs={{0,2},{1,3},{2,0},{3,1},{4,6},{5,7},{6,4},{7,5},{8,10},{9,11},{10,... | collective-permute-start | bytes 393224 | tf_op jit(solution)/shard_map/ppermute | solution.py:40
  46.9 3.3 %collective-permute-done.refs_1_ = bf16[2,256,2048]{2,1,0:T(8,128)(2,1)} collective-permute-done((bf16[2,256,2048]{2,1,0:T(8,128)(2,1)}, bf16[2,256,2048]{2,1,0:T(8,128)(2,1)}, u32[]{:S(2)}, u32[]{:S(2)}) %collective-permute-start) | collective-permute-done | bytes 2097184 | tf_op jit(solution)/shard_map/ppermute | solution.py:35
  50.2 8.7 %step.14 = (bf16[2,2,256,2048]{3,2,1,0:T(8,128)(2,1)S(1)}, f32[4,64,512]{2,1,0:T(8,128)S(1)}, bf16[4,64,512]{2,1,0:T(8,128)(2,1)S(1)}, f32[1,64,512]{2,1,0:T(8,1...) custom-call(f32[11]{0:T(128)S(1)} %pad_maximum_fusion.1.table_ref, ...), custom_call_target="tpu_custom_call" | custom-call | flops 1000 | bytes 1000 | tf_op jit(solution)/shard_map/step/pallas_call | solution.py:368
  59.0 2.1 %collective-permute-start.12 = (bf16[2,128,2048]{2,1,0:T(8,128)(2,1)S(1)}, bf16[2,128,2048]{2,1,0:T(8,128)(2,1)S(1)}, u32[]{:S(2)}, u32[]{:S(2)}) collective-permute-start(bf16[2,128,2048]{2,1,0:T(8,128)(2,1)S(1)} %get-tuple-element.55), channel_id=1, source_target_pairs={{0,24},{8,0},{16,8},{24,16},{1,25},{9,1},{17,9},{25,17},{2,26},{10... | collective-permute-start | bytes 3145736 | tf_op jit(solution)/shard_map/ppermute | solution.py:35
  61.1 1.5 %collective-permute-start.6 = (bf16[4,64,512]{2,1,0:T(8,128)(2,1)S(1)}, bf16[4,64,512]{2,1,0:T(8,128)(2,1)S(1)}, u32[]{:S(2)}, u32[]{:S(2)}) collective-permute-start(bf16[4,64,512]{2,1,0:T(8,128)(2,1)S(1)} %get-tuple-element.44), channel_id=1, source_target_pairs={{0,1},{1,0},{2,3},{3,2},{4,5},{5,4},{6,7},{7,6},{8,9},{9,8},{10,11... | collective-permute-start | bytes 786440 | tf_op jit(solution)/shard_map/ppermute | solution.py:35
  62.5 2.6 %collective-permute-start.7 = (bf16[1,64,512]{2,1,0:T(8,128)(2,1)S(1)}, bf16[1,64,512]{2,1,0:T(8,128)(2,1)S(1)}, u32[]{:S(2)}, u32[]{:S(2)}) collective-permute-start(bf16[1,64,512]{2,1,0:T(8,128)(2,1)S(1)} %get-tuple-element.46), channel_id=1, source_target_pairs={{0,4},{1,5},{2,6},{3,7},{4,0},{5,1},{6,2},{7,3},{8,12},{9,13},{10,... | collective-permute-start | bytes 196616 | tf_op jit(solution)/shard_map/ppermute | solution.py:40
  65.1 1.9 %collective-permute-done.5.refs_1_ = bf16[2,192,2048]{2,1,0:T(8,128)(2,1)} collective-permute-done((bf16[2,192,2048]{2,1,0:T(8,128)(2,1)}, bf16[2,192,2048]{2,1,0:T(8,128)(2,1)}, u32[]{:S(2)}, u32[]{:S(2)}) %collective-permute-start.5) | collective-permute-done | bytes 1572896 | tf_op jit(solution)/shard_map/ppermute | solution.py:35
  67.0 0.7 collective-permute-done.7.refs_5_
  67.7 0.6 collective-permute-done.6.refs_3_
  68.3 3.4 %step.15 = (bf16[384,2048]{1,0:T(8,128)(2,1)S(1)}, bf16[4,64,384]{2,1,0:T(8,128)(2,1)S(1)}, f32[2,64,512]{2,1,0:T(8,128)S(1)}, bf16[2,64,512]{2,1,0:T(8,128)(2,1)S(1)}, f32[64,2,2,512]{3,2,1,0:T(2,128)}) custom-call(f32[11]{0:T(128)S(1)} %pad_maximum_fusion.1.table_ref, bf16[2,2,256,2048]{3,2,1,0:T(8,128)(2,1)S(1)} %get-tuple-element.41.refs_0_, ...), custom_call_target="tpu_custom_call" | custom-call | flops 1000 | bytes 1000 | tf_op jit(solution)/shard_map/step/pallas_call | solution.py:368
  71.7 1.6 %collective-permute-start.9 = (bf16[4,64,384]{2,1,0:T(8,128)(2,1)S(1)}, bf16[4,64,384]{2,1,0:T(8,128)(2,1)S(1)}, u32[]{:S(2)}, u32[]{:S(2)}) collective-permute-start(bf16[4,64,384]{2,1,0:T(8,128)(2,1)S(1)} %get-tuple-element.50), channel_id=1, source_target_pairs={{0,1},{1,0},{2,3},{3,2},{4,5},{5,4},{6,7},{7,6},{8,9},{9,8},{10,11... | collective-permute-start | bytes 589832 | tf_op jit(solution)/shard_map/ppermute | solution.py:35
  73.2 1.6 %collective-permute-start.8 = (bf16[2,64,512]{2,1,0:T(8,128)(2,1)S(1)}, bf16[2,64,512]{2,1,0:T(8,128)(2,1)S(1)}, u32[]{:S(2)}, u32[]{:S(2)}) collective-permute-start(bf16[2,64,512]{2,1,0:T(8,128)(2,1)S(1)} %get-tuple-element.48), channel_id=1, source_target_pairs={{0,2},{1,3},{2,0},{3,1},{4,6},{5,7},{6,4},{7,5},{8,10},{9,11},{10,... | collective-permute-start | bytes 393224 | tf_op jit(solution)/shard_map/ppermute | solution.py:40
  74.8 1.9 %step.16.refs_0_ = f32[4,64,384]{2,1,0:T(8,128)S(1)} custom-call(f32[11]{0:T(128)S(1)} %pad_maximum_fusion.1.table_ref, bf16[2,2,256,2048]{3,2,1,0:T(8,128)(2,1)S(1)} %get-tuple-element.41.refs_0_, bf16[384,2048]{1,0:T(8,128)(2,1)S(1)} %get-tuple-element.49.refs_1_), custom_call_target="tpu_custom_call" | custom-call | flops 1000 | bytes 1000 | tf_op jit(solution)/shard_map/step/pallas_call | solution.py:368
  76.7 1.6 %collective-permute-done.9.refs_1_ = bf16[4,64,384]{2,1,0:T(8,128)(2,1)S(1)} collective-permute-done((bf16[4,64,384]{2,1,0:T(8,128)(2,1)S(1)}, bf16[4,64,384]{2,1,0:T(8,128)(2,1)S(1)}, u32[]{:S(2)}, u32[]{:S(2)}) %collective-permute-start.9) | collective-permute-done | bytes 196640 | tf_op jit(solution)/shard_map/ppermute | solution.py:35
  78.3 0.6 step.17
  78.9 1.6 %collective-permute-start.10 = (bf16[2,64,384]{2,1,0:T(8,128)(2,1)S(1)}, bf16[2,64,384]{2,1,0:T(8,128)(2,1)S(1)}, u32[]{:S(2)}, u32[]{:S(2)}) collective-permute-start(bf16[2,64,384]{2,1,0:T(8,128)(2,1)S(1)} %get-tuple-element.52), channel_id=1, source_target_pairs={{0,2},{1,3},{2,0},{3,1},{4,6},{5,7},{6,4},{7,5},{8,10},{9,11},{10,... | collective-permute-start | bytes 294920 | tf_op jit(solution)/shard_map/ppermute | solution.py:40
  80.5 3.0 %collective-permute-done.10.refs_5_ = bf16[2,64,384]{2,1,0:T(8,128)(2,1)S(1)} collective-permute-done((bf16[2,64,384]{2,1,0:T(8,128)(2,1)S(1)}, bf16[2,64,384]{2,1,0:T(8,128)(2,1)S(1)}, u32[]{:S(2)}, u32[]{:S(2)}) %collective-permute-start.10) | collective-permute-done | bytes 98336 | tf_op jit(solution)/shard_map/ppermute | solution.py:40
  83.6 0.2 collective-permute-done.4.refs_1_
  83.8 2.4 %step.18 = (bf16[384,2048]{1,0:T(8,128)(2,1)S(1)}, bf16[4,64,384]{2,1,0:T(8,128)(2,1)S(1)}, f32[1,64,896]{2,1,0:T(8,128)S(1)}, bf16[1,64,896]{2,1,0:T(8,128)(2,1)S(1)}) custom-call(f32[11]{0:T(128)S(1)} %pad_maximum_fusion.1.table_ref, bf16[2,2,256,2048]{3,2,1,0:T(8,128)(2,1)S(1)} %get-tuple-element.41.refs_0_, ...), custom_call_target="tpu_custom_call" | custom-call | flops 1000 | bytes 1000 | tf_op jit(solution)/shard_map/step/pallas_call | solution.py:368
  86.2 1.6 %collective-permute-start.13 = (bf16[4,64,384]{2,1,0:T(8,128)(2,1)S(1)}, bf16[4,64,384]{2,1,0:T(8,128)(2,1)S(1)}, u32[]{:S(2)}, u32[]{:S(2)}) collective-permute-start(bf16[4,64,384]{2,1,0:T(8,128)(2,1)S(1)} %get-tuple-element.57), channel_id=1, source_target_pairs={{0,1},{1,0},{2,3},{3,2},{4,5},{5,4},{6,7},{7,6},{8,9},{9,8},{10,11... | collective-permute-start | bytes 589832 | tf_op jit(solution)/shard_map/ppermute | solution.py:35
  87.8 2.6 %collective-permute-start.11 = (bf16[1,64,896]{2,1,0:T(8,128)(2,1)S(1)}, bf16[1,64,896]{2,1,0:T(8,128)(2,1)S(1)}, u32[]{:S(2)}, u32[]{:S(2)}) collective-permute-start(bf16[1,64,896]{2,1,0:T(8,128)(2,1)S(1)} %get-tuple-element.54), channel_id=1, source_target_pairs={{0,4},{1,5},{2,6},{3,7},{4,0},{5,1},{6,2},{7,3},{8,12},{9,13},{10,... | collective-permute-start | bytes 344072 | tf_op jit(solution)/shard_map/ppermute | solution.py:40
  90.3 1.9 %step.19.refs_2_ = f32[4,64,384]{2,1,0:T(8,128)S(1)} custom-call(f32[11]{0:T(128)S(1)} %pad_maximum_fusion.1.table_ref, bf16[2,2,256,2048]{3,2,1,0:T(8,128)(2,1)S(1)} %get-tuple-element.41.refs_0_, bf16[384,2048]{1,0:T(8,128)(2,1)S(1)} %get-tuple-element.56.refs_1_), custom_call_target="tpu_custom_call" | custom-call | flops 1000 | bytes 1000 | tf_op jit(solution)/shard_map/step/pallas_call | solution.py:368
  92.2 2.7 %collective-permute-done.12.refs_1_ = bf16[2,128,2048]{2,1,0:T(8,128)(2,1)S(1)} collective-permute-done((bf16[2,128,2048]{2,1,0:T(8,128)(2,1)S(1)}, bf16[2,128,2048]{2,1,0:T(8,128)(2,1)S(1)}, u32[]{:S(2)}, u32[]{:S(2)}) %collective-permute-start.12) | collective-permute-done | bytes 1048608 | tf_op jit(solution)/shard_map/ppermute | solution.py:35
  95.0 1.7 %collective-permute-done.11.refs_5_.refs_1_ = bf16[1,64,896]{2,1,0:T(8,128)(2,1)S(1)} collective-permute-done((bf16[1,64,896]{2,1,0:T(8,128)(2,1)S(1)}, bf16[1,64,896]{2,1,0:T(8,128)(2,1)S(1)}, u32[]{:S(2)}, u32[]{:S(2)}) %collective-permute-start.11) | collective-permute-done | bytes 114720 | tf_op jit(solution)/shard_map/ppermute | solution.py:40
  96.7 1.7 %step.20 = (bf16[256,2048]{1,0:T(8,128)(2,1)S(1)}, bf16[4,64,256]{2,1,0:T(8,128)(2,1)S(1)}, f32[2,64,384]{2,1,0:T(8,128)S(1)}, bf16[2,64,384]{2,1,0:T(8,128)(2,1)S(1)}, f32[64,2,2,512]{3,2,1,0:T(2,128)}) custom-call(f32[11]{0:T(128)S(1)} %pad_maximum_fusion.1.table_ref, ...), custom_call_target="tpu_custom_call", output_to_operand_aliasing={{4}: (7, {})} | custom-call | flops 1000 | bytes 1000 | tf_op jit(solution)/shard_map/step/pallas_call | solution.py:368
  98.5 0.6 collective-permute-start.14
  99.1 0.8 collective-permute-start.15
  99.9 1.3 %step.21.refs_0_ = f32[4,64,256]{2,1,0:T(8,128)S(1)} custom-call(f32[11]{0:T(128)S(1)} %pad_maximum_fusion.1.table_ref, bf16[2,2,256,2048]{3,2,1,0:T(8,128)(2,1)S(1)} %get-tuple-element.41.refs_0_, bf16[256,2048]{1,0:T(8,128)(2,1)S(1)} %get-tuple-element.59.refs_1_), custom_call_target="tpu_custom_call" | custom-call | flops 1000 | bytes 1000 | tf_op jit(solution)/shard_map/step/pallas_call | solution.py:368
  101.2 2.5 %collective-permute-done.15.refs_3_ = bf16[2,64,384]{2,1,0:T(8,128)(2,1)S(1)} collective-permute-done((bf16[2,64,384]{2,1,0:T(8,128)(2,1)S(1)}, bf16[2,64,384]{2,1,0:T(8,128)(2,1)S(1)}, u32[]{:S(2)}, u32[]{:S(2)}) %collective-permute-start.15) | collective-permute-done | bytes 98336 | tf_op jit(solution)/shard_map/ppermute | solution.py:40
  103.7 0.6 step.22
  104.3 2.5 %collective-permute-start.16 = (bf16[1,64,640]{2,1,0:T(8,128)(2,1)S(1)}, bf16[1,64,640]{2,1,0:T(8,128)(2,1)S(1)}, u32[]{:S(2)}, u32[]{:S(2)}) collective-permute-start(bf16[1,64,640]{2,1,0:T(8,128)(2,1)S(1)} %get-tuple-element.64), channel_id=1, source_target_pairs={{0,4},{1,5},{2,6},{3,7},{4,0},{5,1},{6,2},{7,3},{8,12},{9,13},{10,... | collective-permute-start | bytes 245768 | tf_op jit(solution)/shard_map/ppermute | solution.py:40
  106.8 1.4 %collective-permute-start.17 = (bf16[1,64,256]{2,1,0:T(8,128)(2,1)S(1)}, bf16[1,64,256]{2,1,0:T(8,128)(2,1)S(1)}, u32[]{:S(2)}, u32[]{:S(2)}) collective-permute-start(bf16[1,64,256]{2,1,0:T(8,128)(2,1)S(1)} %get-tuple-element.66), channel_id=1, source_target_pairs={{0,6},{1,7},{2,4},{3,5},{4,2},{5,3},{6,0},{7,1},{8,14},{9,15},{10,... | collective-permute-start | bytes 98312 | tf_op jit(solution)/shard_map/ppermute | solution.py:40
  108.2 0.5 collective-permute-start.18
  108.7 3.8 %collective-permute-done.17.refs_5_ = bf16[1,64,256]{2,1,0:T(8,128)(2,1)S(1)} collective-permute-done((bf16[1,64,256]{2,1,0:T(8,128)(2,1)S(1)}, bf16[1,64,256]{2,1,0:T(8,128)(2,1)S(1)}, u32[]{:S(2)}, u32[]{:S(2)}) %collective-permute-start.17) | collective-permute-done | bytes 32800 | tf_op jit(solution)/shard_map/ppermute | solution.py:40
  112.5 1.5 %step.23 = f32[64,2,2,512]{3,2,1,0:T(2,128)} custom-call(f32[11]{0:T(128)S(1)} %pad_maximum_fusion.1.table_ref, f32[1,64,896]{2,1,0:T(8,128)S(1)} %get-tuple-element.53.refs_4_.refs_0_, bf16[1,64,896]{2,1,0:T(8,128)(2,1)S(1)} %collective-permute-done.11.refs_5_.refs_1_, f32[1,64,384]{2,1,0:T(8,128)S(1)} %get-tuple-element.63.refs_2_, ...), custom_call_target="tpu_custom_call", output_to_operand_aliasing={{}: (9, {})} | custom-call | flops 1000 | bytes 1000 | tf_op jit(solution)/shard_map/step/pallas_call | solution.py:368
  (17 shorter events, 0.6 us)
Async XLA Ops:
  1.6 26.0 %collective-permute-start.1 = (bf16[2,256,2048]{2,1,0:T(8,128)(2,1)S(1)}, bf16[2,256,2048]{2,1,0:T(8,128)(2,1)}, u32[]{:S(2)}, u32[]{:S(2)}) collective-permute-start(bf16[2,256,2048]{2,1,0:T(8,128)(2,1)S(1)} %piece_of.3.rest_0_), channel_id=1, source_target_pairs={{0,24},{8,0},{16,8},{24,16},{1,25},{9,1},{17,9},{25,17},{2,26},{10... | collective-permute-start | bytes 6291464 | tf_op jit(solution)/shard_map/ppermute | solution.py:35
  6.6 3.1 %copy-start = (s32[2]{0:T(128)S(1)}, s32[2]{0:T(128)}, u32[]{:S(2)}) copy-start(s32[2]{0:T(128)} %param.4) | copy-start | bytes 28
  6.6 3.1 %copy-start.1 = (s32[2]{0:T(128)S(1)}, s32[2]{0:T(128)}, u32[]{:S(2)}) copy-start(s32[2]{0:T(128)} %param.5) | copy-start | bytes 28
  6.6 43.5 %collective-permute-start = (bf16[2,256,2048]{2,1,0:T(8,128)(2,1)}, bf16[2,256,2048]{2,1,0:T(8,128)(2,1)}, u32[]{:S(2)}, u32[]{:S(2)}) collective-permute-start(bf16[2,256,2048]{2,1,0:T(8,128)(2,1)} %piece_of.4.rest_0_), channel_id=1, source_target_pairs={{0,24},{8,0},{16,8},{24,16},{1,25},{9,1},{17,9},{25,17},{2,26},{10... | collective-permute-start | bytes 6291464 | tf_op jit(solution)/shard_map/ppermute | solution.py:35
  9.7 57.3 %collective-permute-start.5 = (bf16[2,192,2048]{2,1,0:T(8,128)(2,1)}, bf16[2,192,2048]{2,1,0:T(8,128)(2,1)}, u32[]{:S(2)}, u32[]{:S(2)}) collective-permute-start(bf16[2,192,2048]{2,1,0:T(8,128)(2,1)} %piece_of.5), channel_id=1, source_target_pairs={{0,24},{8,0},{16,8},{24,16},{1,25},{9,1},{17,9},{25,17},{2,26},{10... | collective-permute-start | bytes 4718600 | tf_op jit(solution)/shard_map/ppermute | solution.py:35
  35.3 48.4 %collective-permute-start.4 = (bf16[2,192,2048]{2,1,0:T(8,128)(2,1)S(1)}, bf16[2,192,2048]{2,1,0:T(8,128)(2,1)S(1)}, u32[]{:S(2)}, u32[]{:S(2)}) collective-permute-start(bf16[2,192,2048]{2,1,0:T(8,128)(2,1)S(1)} %get-tuple-element.42), channel_id=1, source_target_pairs={{0,24},{8,0},{16,8},{24,16},{1,25},{9,1},{17,9},{25,17},{2,26},{10... | collective-permute-start | bytes 4718600 | tf_op jit(solution)/shard_map/ppermute | solution.py:35
  37.4 7.2 %collective-permute-start.2 = (bf16[4,64,512]{2,1,0:T(8,128)(2,1)S(1)}, bf16[4,64,512]{2,1,0:T(8,128)(2,1)S(1)}, u32[]{:S(2)}, u32[]{:S(2)}) collective-permute-start(bf16[4,64,512]{2,1,0:T(8,128)(2,1)S(1)} %get-tuple-element.38), channel_id=1, source_target_pairs={{0,1},{1,0},{2,3},{3,2},{4,5},{5,4},{6,7},{7,6},{8,9},{9,8},{10,11... | collective-permute-start | bytes 786440 | tf_op jit(solution)/shard_map/ppermute | solution.py:35
  45.2 5.0 %collective-permute-start.3 = (bf16[2,64,512]{2,1,0:T(8,128)(2,1)S(1)}, bf16[2,64,512]{2,1,0:T(8,128)(2,1)S(1)}, u32[]{:S(2)}, u32[]{:S(2)}) collective-permute-start(bf16[2,64,512]{2,1,0:T(8,128)(2,1)S(1)} %get-tuple-element.40), channel_id=1, source_target_pairs={{0,2},{1,3},{2,0},{3,1},{4,6},{5,7},{6,4},{7,5},{8,10},{9,11},{10,... | collective-permute-start | bytes 393224 | tf_op jit(solution)/shard_map/ppermute | solution.py:40
  59.0 36.0 %collective-permute-start.12 = (bf16[2,128,2048]{2,1,0:T(8,128)(2,1)S(1)}, bf16[2,128,2048]{2,1,0:T(8,128)(2,1)S(1)}, u32[]{:S(2)}, u32[]{:S(2)}) collective-permute-start(bf16[2,128,2048]{2,1,0:T(8,128)(2,1)S(1)} %get-tuple-element.55), channel_id=1, source_target_pairs={{0,24},{8,0},{16,8},{24,16},{1,25},{9,1},{17,9},{25,17},{2,26},{10... | collective-permute-start | bytes 3145736 | tf_op jit(solution)/shard_map/ppermute | solution.py:35
  61.1 7.2 %collective-permute-start.6 = (bf16[4,64,512]{2,1,0:T(8,128)(2,1)S(1)}, bf16[4,64,512]{2,1,0:T(8,128)(2,1)S(1)}, u32[]{:S(2)}, u32[]{:S(2)}) collective-permute-start(bf16[4,64,512]{2,1,0:T(8,128)(2,1)S(1)} %get-tuple-element.44), channel_id=1, source_target_pairs={{0,1},{1,0},{2,3},{3,2},{4,5},{5,4},{6,7},{7,6},{8,9},{9,8},{10,11... | collective-permute-start | bytes 786440 | tf_op jit(solution)/shard_map/ppermute | solution.py:35
  62.5 5.2 %collective-permute-start.7 = (bf16[1,64,512]{2,1,0:T(8,128)(2,1)S(1)}, bf16[1,64,512]{2,1,0:T(8,128)(2,1)S(1)}, u32[]{:S(2)}, u32[]{:S(2)}) collective-permute-start(bf16[1,64,512]{2,1,0:T(8,128)(2,1)S(1)} %get-tuple-element.46), channel_id=1, source_target_pairs={{0,4},{1,5},{2,6},{3,7},{4,0},{5,1},{6,2},{7,3},{8,12},{9,13},{10,... | collective-permute-start | bytes 196616 | tf_op jit(solution)/shard_map/ppermute | solution.py:40
  71.7 6.6 %collective-permute-start.9 = (bf16[4,64,384]{2,1,0:T(8,128)(2,1)S(1)}, bf16[4,64,384]{2,1,0:T(8,128)(2,1)S(1)}, u32[]{:S(2)}, u32[]{:S(2)}) collective-permute-start(bf16[4,64,384]{2,1,0:T(8,128)(2,1)S(1)} %get-tuple-element.50), channel_id=1, source_target_pairs={{0,1},{1,0},{2,3},{3,2},{4,5},{5,4},{6,7},{7,6},{8,9},{9,8},{10,11... | collective-permute-start | bytes 589832 | tf_op jit(solution)/shard_map/ppermute | solution.py:35
  73.2 7.3 %collective-permute-start.8 = (bf16[2,64,512]{2,1,0:T(8,128)(2,1)S(1)}, bf16[2,64,512]{2,1,0:T(8,128)(2,1)S(1)}, u32[]{:S(2)}, u32[]{:S(2)}) collective-permute-start(bf16[2,64,512]{2,1,0:T(8,128)(2,1)S(1)} %get-tuple-element.48), channel_id=1, source_target_pairs={{0,2},{1,3},{2,0},{3,1},{4,6},{5,7},{6,4},{7,5},{8,10},{9,11},{10,... | collective-permute-start | bytes 393224 | tf_op jit(solution)/shard_map/ppermute | solution.py:40
  78.9 4.7 %collective-permute-start.10 = (bf16[2,64,384]{2,1,0:T(8,128)(2,1)S(1)}, bf16[2,64,384]{2,1,0:T(8,128)(2,1)S(1)}, u32[]{:S(2)}, u32[]{:S(2)}) collective-permute-start(bf16[2,64,384]{2,1,0:T(8,128)(2,1)S(1)} %get-tuple-element.52), channel_id=1, source_target_pairs={{0,2},{1,3},{2,0},{3,1},{4,6},{5,7},{6,4},{7,5},{8,10},{9,11},{10,... | collective-permute-start | bytes 294920 | tf_op jit(solution)/shard_map/ppermute | solution.py:40
  86.2 10.5 %collective-permute-start.13 = (bf16[4,64,384]{2,1,0:T(8,128)(2,1)S(1)}, bf16[4,64,384]{2,1,0:T(8,128)(2,1)S(1)}, u32[]{:S(2)}, u32[]{:S(2)}) collective-permute-start(bf16[4,64,384]{2,1,0:T(8,128)(2,1)S(1)} %get-tuple-element.57), channel_id=1, source_target_pairs={{0,1},{1,0},{2,3},{3,2},{4,5},{5,4},{6,7},{7,6},{8,9},{9,8},{10,11... | collective-permute-start | bytes 589832 | tf_op jit(solution)/shard_map/ppermute | solution.py:35
  87.8 9.0 %collective-permute-start.11 = (bf16[1,64,896]{2,1,0:T(8,128)(2,1)S(1)}, bf16[1,64,896]{2,1,0:T(8,128)(2,1)S(1)}, u32[]{:S(2)}, u32[]{:S(2)}) collective-permute-start(bf16[1,64,896]{2,1,0:T(8,128)(2,1)S(1)} %get-tuple-element.54), channel_id=1, source_target_pairs={{0,4},{1,5},{2,6},{3,7},{4,0},{5,1},{6,2},{7,3},{8,12},{9,13},{10,... | collective-permute-start | bytes 344072 | tf_op jit(solution)/shard_map/ppermute | solution.py:40
  98.5 5.3 %collective-permute-start.14 = (bf16[4,64,256]{2,1,0:T(8,128)(2,1)S(1)}, bf16[4,64,256]{2,1,0:T(8,128)(2,1)S(1)}, u32[]{:S(2)}, u32[]{:S(2)}) collective-permute-start(bf16[4,64,256]{2,1,0:T(8,128)(2,1)S(1)} %get-tuple-element.60), channel_id=1, source_target_pairs={{0,1},{1,0},{2,3},{3,2},{4,5},{5,4},{6,7},{7,6},{8,9},{9,8},{10,11... | collective-permute-start | bytes 393224 | tf_op jit(solution)/shard_map/ppermute | solution.py:35
  99.1 4.6 %collective-permute-start.15 = (bf16[2,64,384]{2,1,0:T(8,128)(2,1)S(1)}, bf16[2,64,384]{2,1,0:T(8,128)(2,1)S(1)}, u32[]{:S(2)}, u32[]{:S(2)}) collective-permute-start(bf16[2,64,384]{2,1,0:T(8,128)(2,1)S(1)} %get-tuple-element.62), channel_id=1, source_target_pairs={{0,2},{1,3},{2,0},{3,1},{4,6},{5,7},{6,4},{7,5},{8,10},{9,11},{10,... | collective-permute-start | bytes 294920 | tf_op jit(solution)/shard_map/ppermute | solution.py:40
  104.3 8.2 %collective-permute-start.16 = (bf16[1,64,640]{2,1,0:T(8,128)(2,1)S(1)}, bf16[1,64,640]{2,1,0:T(8,128)(2,1)S(1)}, u32[]{:S(2)}, u32[]{:S(2)}) collective-permute-start(bf16[1,64,640]{2,1,0:T(8,128)(2,1)S(1)} %get-tuple-element.64), channel_id=1, source_target_pairs={{0,4},{1,5},{2,6},{3,7},{4,0},{5,1},{6,2},{7,3},{8,12},{9,13},{10,... | collective-permute-start | bytes 245768 | tf_op jit(solution)/shard_map/ppermute | solution.py:40
  106.8 5.7 %collective-permute-start.17 = (bf16[1,64,256]{2,1,0:T(8,128)(2,1)S(1)}, bf16[1,64,256]{2,1,0:T(8,128)(2,1)S(1)}, u32[]{:S(2)}, u32[]{:S(2)}) collective-permute-start(bf16[1,64,256]{2,1,0:T(8,128)(2,1)S(1)} %get-tuple-element.66), channel_id=1, source_target_pairs={{0,6},{1,7},{2,4},{3,5},{4,2},{5,3},{6,0},{7,1},{8,14},{9,15},{10,... | collective-permute-start | bytes 98312 | tf_op jit(solution)/shard_map/ppermute | solution.py:40
  108.2 4.3 %collective-permute-start.18 = (bf16[1,64,256]{2,1,0:T(8,128)(2,1)S(1)}, bf16[1,64,256]{2,1,0:T(8,128)(2,1)S(1)}, u32[]{:S(2)}, u32[]{:S(2)}) collective-permute-start(bf16[1,64,256]{2,1,0:T(8,128)(2,1)S(1)} %get-tuple-element.67), channel_id=1, source_target_pairs={{0,2},{1,3},{2,0},{3,1},{4,6},{5,7},{6,4},{7,5},{8,10},{9,11},{10,... | collective-permute-start | bytes 98312 | tf_op jit(solution)/shard_map/ppermute | solution.py:40

commit v21 on v20

--- a/solution.py
+++ b/solution.py
@@ -137,9 +137,10 @@
     arrived = take(plan.adds)
     if plan.adding and plan.placed:
         take(1)
+    take(plan.after)
     given_ref = take(1)[0] if plan.near == "give" else None
     kept_ref = take(1)[0] if plan.ahead else None
-    outs = take(len(plan.ways))
+    outs = [take(2 if plan.split else 1) for _ in plan.ways]
     targets = [take(task.count) for task in plan.tasks]
     result_ref = take(1)[0] if plan.adding else None
     piece_ref = take(1)[0] if plan.later else None
@@ -230,7 +231,8 @@
         dims = (((1,), (1,)), ((), ()))
         points = near_ref.shape[1]
         run = points // 2 if width <= SPLIT else points
-        for way, out_ref in zip(plan.ways, outs):
+        for way, out_refs in zip(plan.ways, outs):
+            kind = out_refs[0].dtype
             of_both = []
             for part in range(2):
                 for copy in [copy for *which, copy in own if which == [way, part]]:
@@ -246,12 +248,18 @@
                 ]
                 of_both.append(sum(products[1:], products[0]))
             of_re, of_im = of_both
-            real_part = (of_re[:, :width] + of_im[:, width:]).astype(out_ref.dtype)
-            imag_part = (of_re[:, width:] - of_im[:, :width]).astype(out_ref.dtype)
+            sides = (
+                (of_re[:, :width] + of_im[:, width:]).astype(kind),
+                (of_re[:, width:] - of_im[:, :width]).astype(kind),
+            )
             for level in range(depth):
                 lines = slice(level * rows, (level + 1) * rows)
-                out_ref[level, :, :width] = real_part[lines]
-                out_ref[level, :, width:] = imag_part[lines]
+                for side, values in enumerate(sides):
+                    if plan.split:
+                        out_refs[side][level] = values[lines]
+                    else:
+                        columns = slice(side * width, (side + 1) * width)
+                        out_refs[0][level, :, columns] = values[lines]
             if plan.later and way == plan.ways[0]:
                 for load, store in zip(loads, stores):
                     load.wait()
@@ -272,10 +280,14 @@
     return outer - lax.rem(outer, 4) + 2 * high + low
 
 
-def summed(arrays, level, columns=slice(None)):
-    total = arrays[0][level, :, columns]
-    for array in arrays[1:]:
-        total = total + array[level, :, columns].astype(jnp.float32)
+def summed(arrays, level):
+    total = arrays[0][level].astype(jnp.float32)
+    rest = [array[level].astype(jnp.float32) for array in arrays[1:]]
+    while rest:
+        more = rest.pop(0)
+        if more.shape != total.shape:
+            more = jnp.concatenate([more, rest.pop(0)], axis=1)
+        total = total + more
     return total
 
 
@@ -303,9 +315,11 @@
     joined: bool
     placed: bool
     later: tuple
-
-
-def step(plan, table, bands, phased, sources, arrived, result):
+    split: bool
+    after: int
+
+
+def step(plan, table, bands, phased, sources, arrived, result, after):
     rows, _, _, nbands = plan.shape
     fold, depth = plan.fold, plan.depth
     points = bands.shape[-1]
@@ -327,7 +341,9 @@
         if plan.ahead:
             out_shape.append(jax.ShapeDtypeStruct(kept, jnp.bfloat16))
         out_shape += [
-            jax.ShapeDtypeStruct((depth, rows, 2 * width), kind(way)) for way in plan.ways
+            jax.ShapeDtypeStruct((depth, rows, width if plan.split else 2 * width), kind(way))
+            for way in plan.ways
+            for _ in range(2 if plan.split else 1)
         ]
         if plan.rows != "held":
             scratch.append(pltpu.VMEM(kept, jnp.bfloat16))
@@ -359,6 +375,8 @@
         out_specs.append(hbm)
         lanes = sum(span for _, span, _ in plan.adding[2])
         scratch += [pltpu.VMEM((rows, 2, lanes), jnp.float32), pltpu.SemaphoreType.DMA]
+    operands += after
+    in_specs += [pl.BlockSpec(memory_space=pl.ANY)] * len(after)
     if plan.later:
         out_shape.append(jax.ShapeDtypeStruct((2, plan.later[2], points), bands.dtype))
         out_specs.append(hbm)
@@ -383,8 +401,8 @@
     result = outs.pop() if plan.adding else result
     near = outs.pop(0) if plan.near == "give" else None
     kept = outs.pop(0) if plan.ahead else None
-    terms = outs[: len(plan.ways)]
-    handed = outs[len(plan.ways) :]
+    count = len(plan.ways) * (2 if plan.split else 1)
+    terms, handed = outs[:count], outs[count:]
     sends = []
     for task in plan.tasks:
         sends.append(handed[: task.count])
@@ -407,23 +425,26 @@
     for index, part in enumerate(parts):
         ready = ready_parts(waiting)
         waiting = waiting[len(ready) :]
+        final = index == count - 1
         tasks = []
-        if halved:
+        if halved and not final:
             tasks.append(Task(tuple(halved), 1, False, 2, 2))
+            waiting += halved
         if crossed:
             tasks.append(Task(tuple(crossed), 0, False, fold, 2))
-        waiting += halved
         if index >= count - 3:
             kernels.append((part, others, "give", tuple(tasks), ready))
             kernels.append((part, every[:1], "use", (), ()))
         else:
             kernels.append((part, every, "make", tuple(tasks), ready))
-        halved, crossed = crossed, [part] if index < count - 1 else []
-        if index in (0, count - 3):
+        if final:
+            break
+        halved, crossed = crossed, [part]
+        if index in (0, count - 3, count - 2):
             kernels.append((None, (), "", (Task((part,), 0, False, fold, 2),), ()))
             halved, crossed = halved + crossed, []
     tasks = (
-        Task((parts[-1],), 0, True, fold, depth),
+        Task((parts[-1],), 0, True, 2 * fold - 1, depth),
         Task(tuple(halved), 1, False, 2, 1),
     )
     kernels.append((None, (), "", tasks, ()))
@@ -487,6 +508,8 @@
             arrived += [array for array, _ in held[batch]]
             pieces.append((done[1], done[2], tuple(terms)))
         adding = (adds[0][0], adds[0][1], tuple(pieces)) if adds else ()
+        split = place == len(parts) - 1 and phase == "give"
+        after = order_by if split else []
         plan = Plan(
             shape,
             fold,
@@ -503,6 +526,8 @@
             len(tasks) > 1 and tasks[0].direct,
             result is not None,
             later,
+            split,
+            len(after),
         )
         phased = near if phase == "use" else theres[place] if part else None
         terms, near, found, sends, result, piece = step(
@@ -513,13 +538,16 @@
             sources,
             arrived,
             result,
+            after,
         )
+        order_by = sends[0][:1] if sends else []
         kept = found if kept is None else kept
         if later:
             theres.append(shifted(piece, "ka", -1))
-        for way, array in zip(ways, terms):
+        for way, array in zip([way for way in ways for _ in range(1 + split)], terms):
             array = shifted(array, "ga", way, fold, True) if way else array
-            held.setdefault((part,), []).insert(0 if way == 0 else fold, (array, 0))
+            entries = held.setdefault((part,), [])
+            entries.insert(len(entries) if way else 0, (array, 0))
         for task, arrays in zip(tasks, sends):
             steps = range(1, depth) if task.direct else [1 << task.stage]
             moved = [swapped(array, "ga", fold * i) for array, i in zip(arrays[1:], steps)]

time: 114 us -> 115 us (level)
  waiting for transfers between devices: 45.1 us -> 42.3 us
  starting transfers between devices: 29.4 us -> 31.7 us
    ppermute x9, waiting for transfers between devices: 11.9 us -> 8.38 us  [swapped(): return lax.ppermute(block, axis, [(i, i ^ distance) for i in range(count)])]
    ppermute x10 -> x11, starting transfers between devices: 14.1 us -> 15.6 us  [shifted(): return lax.ppermute(block, axis, route)]
    ppermute x10 -> x11, waiting for transfers between devices: 33.2 us -> 33.9 us  [shifted(): return lax.ppermute(block, axis, route)]
    pallas_call x12 -> x13, Pallas kernels: 32.3 us -> 32.9 us  [step(): pl.pallas_call(functools.partial(step_kernel, plan), in_specs=in_specs, o...]
  transfers between devices with their start and end apart: 19 -> 20, of which waited for: 14 -> 15; matrix products, arithmetic and copies ran while one was open for 1% -> 1% of each run, Pallas kernels for 29% -> 31%
where the time goes in v21:
time: 115 us; the launch traced here: 114 us
  waiting for transfers between devices  42.3 us (37%)
  Pallas kernels  39.3 us (34%)
  starting transfers between devices  31.7 us (28%)
    ppermute x11, waiting for transfers between devices, shifted(): return lax.ppermute(block, axis, route)  33.9 us
    pallas_call x13, Pallas kernels, step(): pl.pallas_call(functools.partial(step_kernel, plan), in_specs=in_specs, o...  32.9 us
    ppermute x9, starting transfers between devices, swapped(): return lax.ppermute(block, axis, [(i, i ^ distance) for i in range(count)])  16.1 us
    ppermute x11, starting transfers between devices, shifted(): return lax.ppermute(block, axis, route)  15.6 us
    ppermute x9, waiting for transfers between devices, swapped(): return lax.ppermute(block, axis, [(i, i ^ distance) for i in range(count)])  8.38 us
    pallas_call x3, Pallas kernels, piece_of(): pl.pallas_call(functools.partial(piece_kernel if after else first_kernel,...  6.48 us
  transfers between devices with their start and end apart: 20, of which 15 were waited for; matrix products, arithmetic and copies ran while one was open for 1% of the time, Pallas kernels for 31%

profile of v21, /device:TPU:0, one launch (start us, length us, event | category | flops | bytes accessed | tf_op | source)
XLA Modules:
  0.0 114.3 jit_solution(8996960422821093562)
XLA Ops:
  0.0 1.6 %piece_of.3.rest_0_ = bf16[2,256,2048]{2,1,0:T(8,128)(2,1)S(1)} custom-call(bf16[2,2,512,2048]{3,2,1,0:T(8,128)(2,1)} %bands_ref.5), custom_call_target="tpu_custom_call" | custom-call | flops 1000 | bytes 1000 | tf_op jit(solution)/shard_map/piece_of/pallas_call | solution.py:82
  1.6 2.5 %collective-permute-start.1 = (bf16[2,256,2048]{2,1,0:T(8,128)(2,1)S(1)}, bf16[2,256,2048]{2,1,0:T(8,128)(2,1)}, u32[]{:S(2)}, u32[]{:S(2)}) collective-permute-start(bf16[2,256,2048]{2,1,0:T(8,128)(2,1)S(1)} %piece_of.3.rest_0_), channel_id=1, source_target_pairs={{0,24},{8,0},{16,8},{24,16},{1,25},{9,1},{17,9},{25,17},{2,26},{10... | collective-permute-start | bytes 6291464 | tf_op jit(solution)/shard_map/ppermute | solution.py:35
  4.0 2.6 %piece_of.4.rest_0_ = bf16[2,256,2048]{2,1,0:T(8,128)(2,1)} custom-call(bf16[2,2,512,2048]{3,2,1,0:T(8,128)(2,1)} %bands_ref.5, bf16[2,256,2048]{2,1,0:T(8,128)(2,1)S(1)} %piece_of.3.rest_0_), custom_call_target="tpu_custom_call" | custom-call | flops 1000 | bytes 1000 | tf_op jit(solution)/shard_map/piece_of/pallas_call | solution.py:82
  6.7 0.7 collective-permute-start
  7.4 2.3 %piece_of.5 = bf16[2,192,2048]{2,1,0:T(8,128)(2,1)} custom-call(bf16[2,2,512,2048]{3,2,1,0:T(8,128)(2,1)} %bands_ref.5, bf16[2,256,2048]{2,1,0:T(8,128)(2,1)} %piece_of.4.rest_0_), custom_call_target="tpu_custom_call" | custom-call | flops 1000 | bytes 1000 | tf_op jit(solution)/shard_map/piece_of/pallas_call | solution.py:82
  10.4 17.1 %collective-permute-done.1.refs_1_ = bf16[2,256,2048]{2,1,0:T(8,128)(2,1)} collective-permute-done((bf16[2,256,2048]{2,1,0:T(8,128)(2,1)S(1)}, bf16[2,256,2048]{2,1,0:T(8,128)(2,1)}, u32[]{:S(2)}, u32[]{:S(2)}) %collective-permute-start.1) | collective-permute-done | bytes 2097184 | tf_op jit(solution)/shard_map/ppermute | solution.py:35
  27.6 7.7 %step.13 = (f32[4,64,512]{2,1,0:T(8,128)S(1)}, bf16[4,64,512]{2,1,0:T(8,128)(2,1)S(1)}, bf16[2,192,2048]{2,1,0:T(8,128)(2,1)S(1)}) custom-call(f32[11]{0:T(128)S(1)} %pad_maximum_fusion.1.table_ref, bf16[2,2,512,2048]{3,2,1,0:T(8,128)(2,1)} %bands_ref.5, bf16[2,256,2048]{2,1,0:T(8,128)(2,1)} %collective-permute-done.1.refs_1_), custom_call_target="tpu_custom_call" | custom-call | flops 1000 | bytes 1000 | tf_op jit(solution)/shard_map/step/pallas_call | solution.py:386
  35.3 2.1 %collective-permute-start.4 = (bf16[2,192,2048]{2,1,0:T(8,128)(2,1)S(1)}, bf16[2,192,2048]{2,1,0:T(8,128)(2,1)S(1)}, u32[]{:S(2)}, u32[]{:S(2)}) collective-permute-start(bf16[2,192,2048]{2,1,0:T(8,128)(2,1)S(1)} %get-tuple-element.43), channel_id=1, source_target_pairs={{0,24},{8,0},{16,8},{24,16},{1,25},{9,1},{17,9},{25,17},{2,26},{10... | collective-permute-start | bytes 4718600 | tf_op jit(solution)/shard_map/ppermute | solution.py:35
  37.4 1.5 %collective-permute-start.2 = (bf16[4,64,512]{2,1,0:T(8,128)(2,1)S(1)}, bf16[4,64,512]{2,1,0:T(8,128)(2,1)S(1)}, u32[]{:S(2)}, u32[]{:S(2)}) collective-permute-start(bf16[4,64,512]{2,1,0:T(8,128)(2,1)S(1)} %get-tuple-element.39), channel_id=1, source_target_pairs={{0,1},{1,0},{2,3},{3,2},{4,5},{5,4},{6,7},{7,6},{8,9},{9,8},{10,11... | collective-permute-start | bytes 786440 | tf_op jit(solution)/shard_map/ppermute | solution.py:35
  38.9 5.7 %collective-permute-done.2.refs_1_ = bf16[4,64,512]{2,1,0:T(8,128)(2,1)S(1)} collective-permute-done((bf16[4,64,512]{2,1,0:T(8,128)(2,1)S(1)}, bf16[4,64,512]{2,1,0:T(8,128)(2,1)S(1)}, u32[]{:S(2)}, u32[]{:S(2)}) %collective-permute-start.2) | collective-permute-done | bytes 262176 | tf_op jit(solution)/shard_map/ppermute | solution.py:35
  44.6 0.6 step.14
  45.2 1.6 %collective-permute-start.3 = (bf16[2,64,512]{2,1,0:T(8,128)(2,1)S(1)}, bf16[2,64,512]{2,1,0:T(8,128)(2,1)S(1)}, u32[]{:S(2)}, u32[]{:S(2)}) collective-permute-start(bf16[2,64,512]{2,1,0:T(8,128)(2,1)S(1)} %get-tuple-element.41), channel_id=1, source_target_pairs={{0,2},{1,3},{2,0},{3,1},{4,6},{5,7},{6,4},{7,5},{8,10},{9,11},{10,... | collective-permute-start | bytes 393224 | tf_op jit(solution)/shard_map/ppermute | solution.py:40
  46.9 3.3 %collective-permute-done.refs_1_ = bf16[2,256,2048]{2,1,0:T(8,128)(2,1)} collective-permute-done((bf16[2,256,2048]{2,1,0:T(8,128)(2,1)}, bf16[2,256,2048]{2,1,0:T(8,128)(2,1)}, u32[]{:S(2)}, u32[]{:S(2)}) %collective-permute-start) | collective-permute-done | bytes 2097184 | tf_op jit(solution)/shard_map/ppermute | solution.py:35
  50.2 8.7 %step.15 = (bf16[2,2,256,2048]{3,2,1,0:T(8,128)(2,1)S(1)}, f32[4,64,512]{2,1,0:T(8,128)S(1)}, bf16[4,64,512]{2,1,0:T(8,128)(2,1)S(1)}, f32[1,64,512]{2,1,0:T(8,1...) custom-call(f32[11]{0:T(128)S(1)} %pad_maximum_fusion.1.table_ref, ...), custom_call_target="tpu_custom_call" | custom-call | flops 1000 | bytes 1000 | tf_op jit(solution)/shard_map/step/pallas_call | solution.py:386
  59.0 2.1 %collective-permute-start.12 = (bf16[2,128,2048]{2,1,0:T(8,128)(2,1)S(1)}, bf16[2,128,2048]{2,1,0:T(8,128)(2,1)S(1)}, u32[]{:S(2)}, u32[]{:S(2)}) collective-permute-start(bf16[2,128,2048]{2,1,0:T(8,128)(2,1)S(1)} %get-tuple-element.56), channel_id=1, source_target_pairs={{0,24},{8,0},{16,8},{24,16},{1,25},{9,1},{17,9},{25,17},{2,26},{10... | collective-permute-start | bytes 3145736 | tf_op jit(solution)/shard_map/ppermute | solution.py:35
  61.1 1.5 %collective-permute-start.6 = (bf16[4,64,512]{2,1,0:T(8,128)(2,1)S(1)}, bf16[4,64,512]{2,1,0:T(8,128)(2,1)S(1)}, u32[]{:S(2)}, u32[]{:S(2)}) collective-permute-start(bf16[4,64,512]{2,1,0:T(8,128)(2,1)S(1)} %get-tuple-element.45), channel_id=1, source_target_pairs={{0,1},{1,0},{2,3},{3,2},{4,5},{5,4},{6,7},{7,6},{8,9},{9,8},{10,11... | collective-permute-start | bytes 786440 | tf_op jit(solution)/shard_map/ppermute | solution.py:35
  62.5 2.6 %collective-permute-start.7 = (bf16[1,64,512]{2,1,0:T(8,128)(2,1)S(1)}, bf16[1,64,512]{2,1,0:T(8,128)(2,1)S(1)}, u32[]{:S(2)}, u32[]{:S(2)}) collective-permute-start(bf16[1,64,512]{2,1,0:T(8,128)(2,1)S(1)} %get-tuple-element.47), channel_id=1, source_target_pairs={{0,4},{1,5},{2,6},{3,7},{4,0},{5,1},{6,2},{7,3},{8,12},{9,13},{10,... | collective-permute-start | bytes 196616 | tf_op jit(solution)/shard_map/ppermute | solution.py:40
  65.1 1.9 %collective-permute-done.5.refs_1_ = bf16[2,192,2048]{2,1,0:T(8,128)(2,1)} collective-permute-done((bf16[2,192,2048]{2,1,0:T(8,128)(2,1)}, bf16[2,192,2048]{2,1,0:T(8,128)(2,1)}, u32[]{:S(2)}, u32[]{:S(2)}) %collective-permute-start.5) | collective-permute-done | bytes 1572896 | tf_op jit(solution)/shard_map/ppermute | solution.py:35
  67.0 0.7 collective-permute-done.7.refs_5_
  67.7 0.6 collective-permute-done.6.refs_3_
  68.3 3.4 %step.16 = (bf16[384,2048]{1,0:T(8,128)(2,1)S(1)}, bf16[4,64,384]{2,1,0:T(8,128)(2,1)S(1)}, f32[2,64,512]{2,1,0:T(8,128)S(1)}, bf16[2,64,512]{2,1,0:T(8,128)(2,1)S(1)}, f32[64,2,2,512]{3,2,1,0:T(2,128)}) custom-call(f32[11]{0:T(128)S(1)} %pad_maximum_fusion.1.table_ref, bf16[2,2,256,2048]{3,2,1,0:T(8,128)(2,1)S(1)} %get-tuple-element.42.refs_0_, ...), custom_call_target="tpu_custom_call" | custom-call | flops 1000 | bytes 1000 | tf_op jit(solution)/shard_map/step/pallas_call | solution.py:386
  71.7 1.6 %collective-permute-start.9 = (bf16[4,64,384]{2,1,0:T(8,128)(2,1)S(1)}, bf16[4,64,384]{2,1,0:T(8,128)(2,1)S(1)}, u32[]{:S(2)}, u32[]{:S(2)}) collective-permute-start(bf16[4,64,384]{2,1,0:T(8,128)(2,1)S(1)} %get-tuple-element.51), channel_id=1, source_target_pairs={{0,1},{1,0},{2,3},{3,2},{4,5},{5,4},{6,7},{7,6},{8,9},{9,8},{10,11... | collective-permute-start | bytes 589832 | tf_op jit(solution)/shard_map/ppermute | solution.py:35
  73.2 1.6 %collective-permute-start.8 = (bf16[2,64,512]{2,1,0:T(8,128)(2,1)S(1)}, bf16[2,64,512]{2,1,0:T(8,128)(2,1)S(1)}, u32[]{:S(2)}, u32[]{:S(2)}) collective-permute-start(bf16[2,64,512]{2,1,0:T(8,128)(2,1)S(1)} %get-tuple-element.49), channel_id=1, source_target_pairs={{0,2},{1,3},{2,0},{3,1},{4,6},{5,7},{6,4},{7,5},{8,10},{9,11},{10,... | collective-permute-start | bytes 393224 | tf_op jit(solution)/shard_map/ppermute | solution.py:40
  74.8 1.9 %step.17.refs_0_ = f32[4,64,384]{2,1,0:T(8,128)S(1)} custom-call(f32[11]{0:T(128)S(1)} %pad_maximum_fusion.1.table_ref, bf16[2,2,256,2048]{3,2,1,0:T(8,128)(2,1)S(1)} %get-tuple-element.42.refs_0_, bf16[384,2048]{1,0:T(8,128)(2,1)S(1)} %get-tuple-element.50.refs_1_), custom_call_target="tpu_custom_call" | custom-call | flops 1000 | bytes 1000 | tf_op jit(solution)/shard_map/step/pallas_call | solution.py:386
  76.7 1.6 %collective-permute-done.9.refs_1_ = bf16[4,64,384]{2,1,0:T(8,128)(2,1)S(1)} collective-permute-done((bf16[4,64,384]{2,1,0:T(8,128)(2,1)S(1)}, bf16[4,64,384]{2,1,0:T(8,128)(2,1)S(1)}, u32[]{:S(2)}, u32[]{:S(2)}) %collective-permute-start.9) | collective-permute-done | bytes 196640 | tf_op jit(solution)/shard_map/ppermute | solution.py:35
  78.3 0.6 step.18
  78.9 1.6 %collective-permute-start.10 = (bf16[2,64,384]{2,1,0:T(8,128)(2,1)S(1)}, bf16[2,64,384]{2,1,0:T(8,128)(2,1)S(1)}, u32[]{:S(2)}, u32[]{:S(2)}) collective-permute-start(bf16[2,64,384]{2,1,0:T(8,128)(2,1)S(1)} %get-tuple-element.53), channel_id=1, source_target_pairs={{0,2},{1,3},{2,0},{3,1},{4,6},{5,7},{6,4},{7,5},{8,10},{9,11},{10,... | collective-permute-start | bytes 294920 | tf_op jit(solution)/shard_map/ppermute | solution.py:40
  80.5 3.0 %collective-permute-done.10.refs_5_ = bf16[2,64,384]{2,1,0:T(8,128)(2,1)S(1)} collective-permute-done((bf16[2,64,384]{2,1,0:T(8,128)(2,1)S(1)}, bf16[2,64,384]{2,1,0:T(8,128)(2,1)S(1)}, u32[]{:S(2)}, u32[]{:S(2)}) %collective-permute-start.10) | collective-permute-done | bytes 98336 | tf_op jit(solution)/shard_map/ppermute | solution.py:40
  83.8 2.4 %step.19 = (bf16[384,2048]{1,0:T(8,128)(2,1)S(1)}, bf16[4,64,384]{2,1,0:T(8,128)(2,1)S(1)}, f32[1,64,896]{2,1,0:T(8,128)S(1)}, bf16[1,64,896]{2,1,0:T(8,128)(2,1)S(1)}) custom-call(f32[11]{0:T(128)S(1)} %pad_maximum_fusion.1.table_ref, bf16[2,2,256,2048]{3,2,1,0:T(8,128)(2,1)S(1)} %get-tuple-element.42.refs_0_, ...), custom_call_target="tpu_custom_call" | custom-call | flops 1000 | bytes 1000 | tf_op jit(solution)/shard_map/step/pallas_call | solution.py:386
  86.2 1.6 %collective-permute-start.13 = (bf16[4,64,384]{2,1,0:T(8,128)(2,1)S(1)}, bf16[4,64,384]{2,1,0:T(8,128)(2,1)S(1)}, u32[]{:S(2)}, u32[]{:S(2)}) collective-permute-start(bf16[4,64,384]{2,1,0:T(8,128)(2,1)S(1)} %get-tuple-element.59), channel_id=1, source_target_pairs={{0,1},{1,0},{2,3},{3,2},{4,5},{5,4},{6,7},{7,6},{8,9},{9,8},{10,11... | collective-permute-start | bytes 589832 | tf_op jit(solution)/shard_map/ppermute | solution.py:35
  87.8 2.6 %collective-permute-start.11 = (bf16[1,64,896]{2,1,0:T(8,128)(2,1)S(1)}, bf16[1,64,896]{2,1,0:T(8,128)(2,1)S(1)}, u32[]{:S(2)}, u32[]{:S(2)}) collective-permute-start(bf16[1,64,896]{2,1,0:T(8,128)(2,1)S(1)} %get-tuple-element.55), channel_id=1, source_target_pairs={{0,4},{1,5},{2,6},{3,7},{4,0},{5,1},{6,2},{7,3},{8,12},{9,13},{10,... | collective-permute-start | bytes 344072 | tf_op jit(solution)/shard_map/ppermute | solution.py:40
  90.3 1.9 %step.20.refs_0_ = f32[4,64,384]{2,1,0:T(8,128)S(1)} custom-call(f32[11]{0:T(128)S(1)} %pad_maximum_fusion.1.table_ref, bf16[2,2,256,2048]{3,2,1,0:T(8,128)(2,1)S(1)} %get-tuple-element.42.refs_0_, bf16[384,2048]{1,0:T(8,128)(2,1)S(1)} %get-tuple-element.58.refs_1_), custom_call_target="tpu_custom_call" | custom-call | flops 1000 | bytes 1000 | tf_op jit(solution)/shard_map/step/pallas_call | solution.py:386
  92.2 1.7 %collective-permute-done.13.refs_1_ = bf16[4,64,384]{2,1,0:T(8,128)(2,1)S(1)} collective-permute-done((bf16[4,64,384]{2,1,0:T(8,128)(2,1)S(1)}, bf16[4,64,384]{2,1,0:T(8,128)(2,1)S(1)}, u32[]{:S(2)}, u32[]{:S(2)}) %collective-permute-start.13) | collective-permute-done | bytes 196640 | tf_op jit(solution)/shard_map/ppermute | solution.py:35
  93.9 0.6 step.21
  94.5 1.6 %collective-permute-start.16 = (bf16[2,64,384]{2,1,0:T(8,128)(2,1)S(1)}, bf16[2,64,384]{2,1,0:T(8,128)(2,1)S(1)}, u32[]{:S(2)}, u32[]{:S(2)}) collective-permute-start(bf16[2,64,384]{2,1,0:T(8,128)(2,1)S(1)} %get-tuple-element.64), channel_id=1, source_target_pairs={{0,2},{1,3},{2,0},{3,1},{4,6},{5,7},{6,4},{7,5},{8,10},{9,11},{10,... | collective-permute-start | bytes 294920 | tf_op jit(solution)/shard_map/ppermute | solution.py:40
  96.2 0.6 collective-permute-done.11.refs_3_.refs_1_
  96.7 1.7 %step.22 = (bf16[256,2048]{1,0:T(8,128)(2,1)S(1)}, bf16[4,64,128]{2,1,0:T(8,128)(2,1)S(1)}, bf16[4,64,128]{2,1,0:T(8,128)(2,1)S(1)}, f32[64,2,2,512]{3,2,1,0:T(2,128)}) custom-call(f32[11]{0:T(128)S(1)} %pad_maximum_fusion.1.table_ref, bf16[2,2,256,2048]{3,2,1,0:T(8,128)(2,1)S(1)} %get-tuple-element.42.refs_0_, ...), custom_call_target="tpu_custom_call", output_to_operand_aliasing={{3}: (5, {})} | custom-call | flops 1000 | bytes 1000 | tf_op jit(solution)/shard_map/step/pallas_call | solution.py:386
  98.4 1.0 collective-permute-start.14
  99.4 1.1 collective-permute-start.15
  100.5 1.3 %step.23.refs_0_ = f32[4,64,256]{2,1,0:T(8,128)S(1)} custom-call(f32[11]{0:T(128)S(1)} %pad_maximum_fusion.1.table_ref, bf16[2,2,256,2048]{3,2,1,0:T(8,128)(2,1)S(1)} %get-tuple-element.42.refs_0_, bf16[256,2048]{1,0:T(8,128)(2,1)S(1)} %get-tuple-element.61.refs_1_), custom_call_target="tpu_custom_call" | custom-call | flops 1000 | bytes 1000 | tf_op jit(solution)/shard_map/step/pallas_call | solution.py:386
  101.8 1.2 %collective-permute-done.14.refs_1_ = bf16[4,64,128]{2,1,0:T(8,128)(2,1)S(1)} collective-permute-done((bf16[4,64,128]{2,1,0:T(8,128)(2,1)S(1)}, bf16[4,64,128]{2,1,0:T(8,128)(2,1)S(1)}, u32[]{:S(2)}, u32[]{:S(2)}) %collective-permute-start.14) | collective-permute-done | bytes 65568 | tf_op jit(solution)/shard_map/ppermute | solution.py:35
  103.0 0.7 collective-permute-done.15.refs_2_
  103.7 0.6 step.24
  104.3 2.7 %collective-permute-start.17 = (bf16[1,64,640]{2,1,0:T(8,128)(2,1)S(1)}, bf16[1,64,640]{2,1,0:T(8,128)(2,1)S(1)}, u32[]{:S(2)}, u32[]{:S(2)}) collective-permute-start(bf16[1,64,640]{2,1,0:T(8,128)(2,1)S(1)} %get-tuple-element.66), channel_id=1, source_target_pairs={{0,4},{1,5},{2,6},{3,7},{4,0},{5,1},{6,2},{7,3},{8,12},{9,13},{10,... | collective-permute-start | bytes 245768 | tf_op jit(solution)/shard_map/ppermute | solution.py:40
  107.0 1.3 %collective-permute-start.18 = (bf16[1,64,256]{2,1,0:T(8,128)(2,1)S(1)}, bf16[1,64,256]{2,1,0:T(8,128)(2,1)S(1)}, u32[]{:S(2)}, u32[]{:S(2)}) collective-permute-start(bf16[1,64,256]{2,1,0:T(8,128)(2,1)S(1)} %get-tuple-element.68), channel_id=1, source_target_pairs={{0,6},{1,7},{2,4},{3,5},{4,2},{5,3},{6,0},{7,1},{8,14},{9,15},{10,... | collective-permute-start | bytes 98312 | tf_op jit(solution)/shard_map/ppermute | solution.py:40
  108.2 0.5 collective-permute-start.19
  108.7 4.0 %collective-permute-done.18.refs_5_ = bf16[1,64,256]{2,1,0:T(8,128)(2,1)S(1)} collective-permute-done((bf16[1,64,256]{2,1,0:T(8,128)(2,1)S(1)}, bf16[1,64,256]{2,1,0:T(8,128)(2,1)S(1)}, u32[]{:S(2)}, u32[]{:S(2)}) %collective-permute-start.18) | collective-permute-done | bytes 32800 | tf_op jit(solution)/shard_map/ppermute | solution.py:40
  112.7 1.5 %step.25 = f32[64,2,2,512]{3,2,1,0:T(2,128)} custom-call(f32[11]{0:T(128)S(1)} %pad_maximum_fusion.1.table_ref, f32[1,64,896]{2,1,0:T(8,128)S(1)} %get-tuple-element.54.refs_2_.refs_0_, bf16[1,64,896]{2,1,0:T(8,128)(2,1)S(1)} %collective-permute-done.11.refs_3_.refs_1_, f32[1,64,384]{2,1,0:T(8,128)S(1)} %get-tuple-element.65.refs_2_, ...), custom_call_target="tpu_custom_call", output_to_operand_aliasing={{}: (9, {})} | custom-call | flops 1000 | bytes 1000 | tf_op jit(solution)/shard_map/step/pallas_call | solution.py:386
  (20 shorter events, 1.0 us)
Async XLA Ops:
  1.6 26.0 %collective-permute-start.1 = (bf16[2,256,2048]{2,1,0:T(8,128)(2,1)S(1)}, bf16[2,256,2048]{2,1,0:T(8,128)(2,1)}, u32[]{:S(2)}, u32[]{:S(2)}) collective-permute-start(bf16[2,256,2048]{2,1,0:T(8,128)(2,1)S(1)} %piece_of.3.rest_0_), channel_id=1, source_target_pairs={{0,24},{8,0},{16,8},{24,16},{1,25},{9,1},{17,9},{25,17},{2,26},{10... | collective-permute-start | bytes 6291464 | tf_op jit(solution)/shard_map/ppermute | solution.py:35
  6.6 3.2 %copy-start = (s32[2]{0:T(128)S(1)}, s32[2]{0:T(128)}, u32[]{:S(2)}) copy-start(s32[2]{0:T(128)} %param.4) | copy-start | bytes 28
  6.6 3.2 %copy-start.1 = (s32[2]{0:T(128)S(1)}, s32[2]{0:T(128)}, u32[]{:S(2)}) copy-start(s32[2]{0:T(128)} %param.5) | copy-start | bytes 28
  6.7 43.5 %collective-permute-start = (bf16[2,256,2048]{2,1,0:T(8,128)(2,1)}, bf16[2,256,2048]{2,1,0:T(8,128)(2,1)}, u32[]{:S(2)}, u32[]{:S(2)}) collective-permute-start(bf16[2,256,2048]{2,1,0:T(8,128)(2,1)} %piece_of.4.rest_0_), channel_id=1, source_target_pairs={{0,24},{8,0},{16,8},{24,16},{1,25},{9,1},{17,9},{25,17},{2,26},{10... | collective-permute-start | bytes 6291464 | tf_op jit(solution)/shard_map/ppermute | solution.py:35
  9.7 57.3 %collective-permute-start.5 = (bf16[2,192,2048]{2,1,0:T(8,128)(2,1)}, bf16[2,192,2048]{2,1,0:T(8,128)(2,1)}, u32[]{:S(2)}, u32[]{:S(2)}) collective-permute-start(bf16[2,192,2048]{2,1,0:T(8,128)(2,1)} %piece_of.5), channel_id=1, source_target_pairs={{0,24},{8,0},{16,8},{24,16},{1,25},{9,1},{17,9},{25,17},{2,26},{10... | collective-permute-start | bytes 4718600 | tf_op jit(solution)/shard_map/ppermute | solution.py:35
  35.3 48.4 %collective-permute-start.4 = (bf16[2,192,2048]{2,1,0:T(8,128)(2,1)S(1)}, bf16[2,192,2048]{2,1,0:T(8,128)(2,1)S(1)}, u32[]{:S(2)}, u32[]{:S(2)}) collective-permute-start(bf16[2,192,2048]{2,1,0:T(8,128)(2,1)S(1)} %get-tuple-element.43), channel_id=1, source_target_pairs={{0,24},{8,0},{16,8},{24,16},{1,25},{9,1},{17,9},{25,17},{2,26},{10... | collective-permute-start | bytes 4718600 | tf_op jit(solution)/shard_map/ppermute | solution.py:35
  37.4 7.2 %collective-permute-start.2 = (bf16[4,64,512]{2,1,0:T(8,128)(2,1)S(1)}, bf16[4,64,512]{2,1,0:T(8,128)(2,1)S(1)}, u32[]{:S(2)}, u32[]{:S(2)}) collective-permute-start(bf16[4,64,512]{2,1,0:T(8,128)(2,1)S(1)} %get-tuple-element.39), channel_id=1, source_target_pairs={{0,1},{1,0},{2,3},{3,2},{4,5},{5,4},{6,7},{7,6},{8,9},{9,8},{10,11... | collective-permute-start | bytes 786440 | tf_op jit(solution)/shard_map/ppermute | solution.py:35
  45.2 5.0 %collective-permute-start.3 = (bf16[2,64,512]{2,1,0:T(8,128)(2,1)S(1)}, bf16[2,64,512]{2,1,0:T(8,128)(2,1)S(1)}, u32[]{:S(2)}, u32[]{:S(2)}) collective-permute-start(bf16[2,64,512]{2,1,0:T(8,128)(2,1)S(1)} %get-tuple-element.41), channel_id=1, source_target_pairs={{0,2},{1,3},{2,0},{3,1},{4,6},{5,7},{6,4},{7,5},{8,10},{9,11},{10,... | collective-permute-start | bytes 393224 | tf_op jit(solution)/shard_map/ppermute | solution.py:40
  59.0 37.2 %collective-permute-start.12 = (bf16[2,128,2048]{2,1,0:T(8,128)(2,1)S(1)}, bf16[2,128,2048]{2,1,0:T(8,128)(2,1)S(1)}, u32[]{:S(2)}, u32[]{:S(2)}) collective-permute-start(bf16[2,128,2048]{2,1,0:T(8,128)(2,1)S(1)} %get-tuple-element.56), channel_id=1, source_target_pairs={{0,24},{8,0},{16,8},{24,16},{1,25},{9,1},{17,9},{25,17},{2,26},{10... | collective-permute-start | bytes 3145736 | tf_op jit(solution)/shard_map/ppermute | solution.py:35
  61.1 7.2 %collective-permute-start.6 = (bf16[4,64,512]{2,1,0:T(8,128)(2,1)S(1)}, bf16[4,64,512]{2,1,0:T(8,128)(2,1)S(1)}, u32[]{:S(2)}, u32[]{:S(2)}) collective-permute-start(bf16[4,64,512]{2,1,0:T(8,128)(2,1)S(1)} %get-tuple-element.45), channel_id=1, source_target_pairs={{0,1},{1,0},{2,3},{3,2},{4,5},{5,4},{6,7},{7,6},{8,9},{9,8},{10,11... | collective-permute-start | bytes 786440 | tf_op jit(solution)/shard_map/ppermute | solution.py:35
  62.5 5.2 %collective-permute-start.7 = (bf16[1,64,512]{2,1,0:T(8,128)(2,1)S(1)}, bf16[1,64,512]{2,1,0:T(8,128)(2,1)S(1)}, u32[]{:S(2)}, u32[]{:S(2)}) collective-permute-start(bf16[1,64,512]{2,1,0:T(8,128)(2,1)S(1)} %get-tuple-element.47), channel_id=1, source_target_pairs={{0,4},{1,5},{2,6},{3,7},{4,0},{5,1},{6,2},{7,3},{8,12},{9,13},{10,... | collective-permute-start | bytes 196616 | tf_op jit(solution)/shard_map/ppermute | solution.py:40
  71.7 6.6 %collective-permute-start.9 = (bf16[4,64,384]{2,1,0:T(8,128)(2,1)S(1)}, bf16[4,64,384]{2,1,0:T(8,128)(2,1)S(1)}, u32[]{:S(2)}, u32[]{:S(2)}) collective-permute-start(bf16[4,64,384]{2,1,0:T(8,128)(2,1)S(1)} %get-tuple-element.51), channel_id=1, source_target_pairs={{0,1},{1,0},{2,3},{3,2},{4,5},{5,4},{6,7},{7,6},{8,9},{9,8},{10,11... | collective-permute-start | bytes 589832 | tf_op jit(solution)/shard_map/ppermute | solution.py:35
  73.2 7.3 %collective-permute-start.8 = (bf16[2,64,512]{2,1,0:T(8,128)(2,1)S(1)}, bf16[2,64,512]{2,1,0:T(8,128)(2,1)S(1)}, u32[]{:S(2)}, u32[]{:S(2)}) collective-permute-start(bf16[2,64,512]{2,1,0:T(8,128)(2,1)S(1)} %get-tuple-element.49), channel_id=1, source_target_pairs={{0,2},{1,3},{2,0},{3,1},{4,6},{5,7},{6,4},{7,5},{8,10},{9,11},{10,... | collective-permute-start | bytes 393224 | tf_op jit(solution)/shard_map/ppermute | solution.py:40
  78.9 4.7 %collective-permute-start.10 = (bf16[2,64,384]{2,1,0:T(8,128)(2,1)S(1)}, bf16[2,64,384]{2,1,0:T(8,128)(2,1)S(1)}, u32[]{:S(2)}, u32[]{:S(2)}) collective-permute-start(bf16[2,64,384]{2,1,0:T(8,128)(2,1)S(1)} %get-tuple-element.53), channel_id=1, source_target_pairs={{0,2},{1,3},{2,0},{3,1},{4,6},{5,7},{6,4},{7,5},{8,10},{9,11},{10,... | collective-permute-start | bytes 294920 | tf_op jit(solution)/shard_map/ppermute | solution.py:40
  86.2 7.7 %collective-permute-start.13 = (bf16[4,64,384]{2,1,0:T(8,128)(2,1)S(1)}, bf16[4,64,384]{2,1,0:T(8,128)(2,1)S(1)}, u32[]{:S(2)}, u32[]{:S(2)}) collective-permute-start(bf16[4,64,384]{2,1,0:T(8,128)(2,1)S(1)} %get-tuple-element.59), channel_id=1, source_target_pairs={{0,1},{1,0},{2,3},{3,2},{4,5},{5,4},{6,7},{7,6},{8,9},{9,8},{10,11... | collective-permute-start | bytes 589832 | tf_op jit(solution)/shard_map/ppermute | solution.py:35
  87.8 9.0 %collective-permute-start.11 = (bf16[1,64,896]{2,1,0:T(8,128)(2,1)S(1)}, bf16[1,64,896]{2,1,0:T(8,128)(2,1)S(1)}, u32[]{:S(2)}, u32[]{:S(2)}) collective-permute-start(bf16[1,64,896]{2,1,0:T(8,128)(2,1)S(1)} %get-tuple-element.55), channel_id=1, source_target_pairs={{0,4},{1,5},{2,6},{3,7},{4,0},{5,1},{6,2},{7,3},{8,12},{9,13},{10,... | collective-permute-start | bytes 344072 | tf_op jit(solution)/shard_map/ppermute | solution.py:40
  94.5 9.2 %collective-permute-start.16 = (bf16[2,64,384]{2,1,0:T(8,128)(2,1)S(1)}, bf16[2,64,384]{2,1,0:T(8,128)(2,1)S(1)}, u32[]{:S(2)}, u32[]{:S(2)}) collective-permute-start(bf16[2,64,384]{2,1,0:T(8,128)(2,1)S(1)} %get-tuple-element.64), channel_id=1, source_target_pairs={{0,2},{1,3},{2,0},{3,1},{4,6},{5,7},{6,4},{7,5},{8,10},{9,11},{10,... | collective-permute-start | bytes 294920 | tf_op jit(solution)/shard_map/ppermute | solution.py:40
  98.4 4.5 %collective-permute-start.14 = (bf16[4,64,128]{2,1,0:T(8,128)(2,1)S(1)}, bf16[4,64,128]{2,1,0:T(8,128)(2,1)S(1)}, u32[]{:S(2)}, u32[]{:S(2)}) collective-permute-start(bf16[4,64,128]{2,1,0:T(8,128)(2,1)S(1)} %get-tuple-element.62), channel_id=1, source_target_pairs={{0,1},{1,0},{2,3},{3,2},{4,5},{5,4},{6,7},{7,6},{8,9},{9,8},{10,11... | collective-permute-start | bytes 196616 | tf_op jit(solution)/shard_map/ppermute | solution.py:35
  99.4 4.3 %collective-permute-start.15 = (bf16[4,64,128]{2,1,0:T(8,128)(2,1)S(1)}, bf16[4,64,128]{2,1,0:T(8,128)(2,1)S(1)}, u32[]{:S(2)}, u32[]{:S(2)}) collective-permute-start(bf16[4,64,128]{2,1,0:T(8,128)(2,1)S(1)} %get-tuple-element.63), channel_id=1, source_target_pairs={{0,1},{1,0},{2,3},{3,2},{4,5},{5,4},{6,7},{7,6},{8,9},{9,8},{10,11... | collective-permute-start | bytes 196616 | tf_op jit(solution)/shard_map/ppermute | solution.py:35
  104.3 8.4 %collective-permute-start.17 = (bf16[1,64,640]{2,1,0:T(8,128)(2,1)S(1)}, bf16[1,64,640]{2,1,0:T(8,128)(2,1)S(1)}, u32[]{:S(2)}, u32[]{:S(2)}) collective-permute-start(bf16[1,64,640]{2,1,0:T(8,128)(2,1)S(1)} %get-tuple-element.66), channel_id=1, source_target_pairs={{0,4},{1,5},{2,6},{3,7},{4,0},{5,1},{6,2},{7,3},{8,12},{9,13},{10,... | collective-permute-start | bytes 245768 | tf_op jit(solution)/shard_map/ppermute | solution.py:40
  107.0 5.7 %collective-permute-start.18 = (bf16[1,64,256]{2,1,0:T(8,128)(2,1)S(1)}, bf16[1,64,256]{2,1,0:T(8,128)(2,1)S(1)}, u32[]{:S(2)}, u32[]{:S(2)}) collective-permute-start(bf16[1,64,256]{2,1,0:T(8,128)(2,1)S(1)} %get-tuple-element.68), channel_id=1, source_target_pairs={{0,6},{1,7},{2,4},{3,5},{4,2},{5,3},{6,0},{7,1},{8,14},{9,15},{10,... | collective-permute-start | bytes 98312 | tf_op jit(solution)/shard_map/ppermute | solution.py:40
  108.2 4.5 %collective-permute-start.19 = (bf16[1,64,256]{2,1,0:T(8,128)(2,1)S(1)}, bf16[1,64,256]{2,1,0:T(8,128)(2,1)S(1)}, u32[]{:S(2)}, u32[]{:S(2)}) collective-permute-start(bf16[1,64,256]{2,1,0:T(8,128)(2,1)S(1)} %get-tuple-element.69), channel_id=1, source_target_pairs={{0,2},{1,3},{2,0},{3,1},{4,6},{5,7},{6,4},{7,5},{8,10},{9,11},{10,... | collective-permute-start | bytes 98312 | tf_op jit(solution)/shard_map/ppermute | solution.py:40

commit v22 on v21

--- a/solution.py
+++ b/solution.py
@@ -16,7 +16,7 @@
 AHEAD = 3
 OUTER = 4
 SPLIT = 128
-JOINT = 2
+JOINT = 1
 LANES = 128
 BLOCK = 256
 VMEM_BYTES = 44 * 1024 * 1024
@@ -207,7 +207,7 @@
         placing.start()
     for task, arrays, outputs in zip(plan.tasks, sources, targets):
         groups = [arrays[i : i + task.each] for i in range(0, len(arrays), task.each)]
-        bit = lax.rem(lax.div(outer, 1 << task.stage), 2)
+        bit = lax.rem(lax.div(outer, 1 << task.bit(depth)), 2)
         filled = [(out_ref, 0) for out_ref in outputs]
         if plan.joined and not task.direct:
             filled.append((targets[0][JOINT], 2 * plan.tasks[0].batch[0][2]))
@@ -215,6 +215,8 @@
             for level in range(out_ref.shape[0]):
                 if task.direct:
                     source = partner(outer, index)
+                elif task.far_first:
+                    source = (1 - bit if index else bit) * out_ref.shape[0] + level
                 else:
                     source = 2 * level + (1 - bit if index else bit)
                 column = shift
@@ -297,6 +299,11 @@
     direct: bool
     each: int
     count: int
+    far_first: bool = False
+
+    def bit(self, depth):
+        last = depth.bit_length() - 2
+        return last - self.stage if self.far_first else self.stage
 
 
 class Plan(NamedTuple):
@@ -441,11 +448,12 @@
             break
         halved, crossed = crossed, [part]
         if index in (0, count - 3, count - 2):
-            kernels.append((None, (), "", (Task((part,), 0, False, fold, 2),), ()))
+            task = Task((part,), 0, False, fold, 2, index == count - 2)
+            kernels.append((None, (), "", (task,), ()))
             halved, crossed = halved + crossed, []
     tasks = (
         Task((parts[-1],), 0, True, 2 * fold - 1, depth),
-        Task(tuple(halved), 1, False, 2, 1),
+        Task(tuple(halved), 1, False, 2, 1, True),
     )
     kernels.append((None, (), "", tasks, ()))
     kernels.append((None, (), "", (), tuple(waiting) + tuple(halved) + (parts[-1],)))
@@ -549,11 +557,11 @@
             entries = held.setdefault((part,), [])
             entries.insert(len(entries) if way else 0, (array, 0))
         for task, arrays in zip(tasks, sends):
-            steps = range(1, depth) if task.direct else [1 << task.stage]
+            steps = range(1, depth) if task.direct else [1 << task.bit(depth)]
             moved = [swapped(array, "ga", fold * i) for array, i in zip(arrays[1:], steps)]
             held[task.batch] = [(array, 0) for array in [arrays[0], *reversed(moved)]]
         if plan.joined:
-            joint = held[tasks[0].batch][JOINT][0]
+            joint = held[tasks[0].batch][depth - JOINT][0]
             held[tasks[1].batch].append((joint, 2 * tasks[0].batch[0][2]))
     return result
 

time: 115 us -> 115 us (level)
  no operation moved by 1% of the time
where the time goes in v22:
time: 115 us
  waiting for transfers between devices  42.5 us (37%)
  Pallas kernels  39.3 us (34%)
  starting transfers between devices  31.9 us (28%)
    ppermute x11, waiting for transfers between devices, shifted(): return lax.ppermute(block, axis, route)  34.5 us
    pallas_call x13, Pallas kernels, step(): pl.pallas_call(functools.partial(step_kernel, plan), in_specs=in_specs, o...  32.9 us
    ppermute x9, starting transfers between devices, swapped(): return lax.ppermute(block, axis, [(i, i ^ distance) for i in range(count)])  16.2 us
    ppermute x11, starting transfers between devices, shifted(): return lax.ppermute(block, axis, route)  15.6 us
    ppermute x9, waiting for transfers between devices, swapped(): return lax.ppermute(block, axis, [(i, i ^ distance) for i in range(count)])  8 us
    pallas_call x3, Pallas kernels, piece_of(): pl.pallas_call(functools.partial(piece_kernel if after else first_kernel,...  6.48 us
  transfers between devices with their start and end apart: 20, of which 15 were waited for; matrix products, arithmetic and copies ran while one was open for 1% of the time, Pallas kernels for 31%

profile of v22, /device:TPU:0, one launch (start us, length us, event | category | flops | bytes accessed | tf_op | source)
XLA Modules:
  0.0 114.7 jit_solution(9812961152109061758)
XLA Ops:
  0.0 1.6 %piece_of.3.rest_0_ = bf16[2,256,2048]{2,1,0:T(8,128)(2,1)S(1)} custom-call(bf16[2,2,512,2048]{3,2,1,0:T(8,128)(2,1)} %bands_ref.5), custom_call_target="tpu_custom_call" | custom-call | flops 1000 | bytes 1000 | tf_op jit(solution)/shard_map/piece_of/pallas_call | solution.py:82
  1.6 2.5 %collective-permute-start.1 = (bf16[2,256,2048]{2,1,0:T(8,128)(2,1)S(1)}, bf16[2,256,2048]{2,1,0:T(8,128)(2,1)}, u32[]{:S(2)}, u32[]{:S(2)}) collective-permute-start(bf16[2,256,2048]{2,1,0:T(8,128)(2,1)S(1)} %piece_of.3.rest_0_), channel_id=1, source_target_pairs={{0,24},{8,0},{16,8},{24,16},{1,25},{9,1},{17,9},{25,17},{2,26},{10... | collective-permute-start | bytes 6291464 | tf_op jit(solution)/shard_map/ppermute | solution.py:35
  4.0 2.6 %piece_of.4.rest_0_ = bf16[2,256,2048]{2,1,0:T(8,128)(2,1)} custom-call(bf16[2,2,512,2048]{3,2,1,0:T(8,128)(2,1)} %bands_ref.5, bf16[2,256,2048]{2,1,0:T(8,128)(2,1)S(1)} %piece_of.3.rest_0_), custom_call_target="tpu_custom_call" | custom-call | flops 1000 | bytes 1000 | tf_op jit(solution)/shard_map/piece_of/pallas_call | solution.py:82
  6.7 0.7 collective-permute-start
  7.4 2.3 %piece_of.5 = bf16[2,192,2048]{2,1,0:T(8,128)(2,1)} custom-call(bf16[2,2,512,2048]{3,2,1,0:T(8,128)(2,1)} %bands_ref.5, bf16[2,256,2048]{2,1,0:T(8,128)(2,1)} %piece_of.4.rest_0_), custom_call_target="tpu_custom_call" | custom-call | flops 1000 | bytes 1000 | tf_op jit(solution)/shard_map/piece_of/pallas_call | solution.py:82
  10.4 17.1 %collective-permute-done.1.refs_1_ = bf16[2,256,2048]{2,1,0:T(8,128)(2,1)} collective-permute-done((bf16[2,256,2048]{2,1,0:T(8,128)(2,1)S(1)}, bf16[2,256,2048]{2,1,0:T(8,128)(2,1)}, u32[]{:S(2)}, u32[]{:S(2)}) %collective-permute-start.1) | collective-permute-done | bytes 2097184 | tf_op jit(solution)/shard_map/ppermute | solution.py:35
  27.6 7.7 %step.13 = (f32[4,64,512]{2,1,0:T(8,128)S(1)}, bf16[4,64,512]{2,1,0:T(8,128)(2,1)S(1)}, bf16[2,192,2048]{2,1,0:T(8,128)(2,1)S(1)}) custom-call(f32[11]{0:T(128)S(1)} %pad_maximum_fusion.1.table_ref, bf16[2,2,512,2048]{3,2,1,0:T(8,128)(2,1)} %bands_ref.5, bf16[2,256,2048]{2,1,0:T(8,128)(2,1)} %collective-permute-done.1.refs_1_), custom_call_target="tpu_custom_call" | custom-call | flops 1000 | bytes 1000 | tf_op jit(solution)/shard_map/step/pallas_call | solution.py:393
  35.3 2.1 %collective-permute-start.4 = (bf16[2,192,2048]{2,1,0:T(8,128)(2,1)S(1)}, bf16[2,192,2048]{2,1,0:T(8,128)(2,1)S(1)}, u32[]{:S(2)}, u32[]{:S(2)}) collective-permute-start(bf16[2,192,2048]{2,1,0:T(8,128)(2,1)S(1)} %get-tuple-element.43), channel_id=1, source_target_pairs={{0,24},{8,0},{16,8},{24,16},{1,25},{9,1},{17,9},{25,17},{2,26},{10... | collective-permute-start | bytes 4718600 | tf_op jit(solution)/shard_map/ppermute | solution.py:35
  37.4 1.5 %collective-permute-start.2 = (bf16[4,64,512]{2,1,0:T(8,128)(2,1)S(1)}, bf16[4,64,512]{2,1,0:T(8,128)(2,1)S(1)}, u32[]{:S(2)}, u32[]{:S(2)}) collective-permute-start(bf16[4,64,512]{2,1,0:T(8,128)(2,1)S(1)} %get-tuple-element.39), channel_id=1, source_target_pairs={{0,1},{1,0},{2,3},{3,2},{4,5},{5,4},{6,7},{7,6},{8,9},{9,8},{10,11... | collective-permute-start | bytes 786440 | tf_op jit(solution)/shard_map/ppermute | solution.py:35
  38.9 5.7 %collective-permute-done.2.refs_1_ = bf16[4,64,512]{2,1,0:T(8,128)(2,1)S(1)} collective-permute-done((bf16[4,64,512]{2,1,0:T(8,128)(2,1)S(1)}, bf16[4,64,512]{2,1,0:T(8,128)(2,1)S(1)}, u32[]{:S(2)}, u32[]{:S(2)}) %collective-permute-start.2) | collective-permute-done | bytes 262176 | tf_op jit(solution)/shard_map/ppermute | solution.py:35
  44.6 0.6 step.14
  45.2 1.6 %collective-permute-start.3 = (bf16[2,64,512]{2,1,0:T(8,128)(2,1)S(1)}, bf16[2,64,512]{2,1,0:T(8,128)(2,1)S(1)}, u32[]{:S(2)}, u32[]{:S(2)}) collective-permute-start(bf16[2,64,512]{2,1,0:T(8,128)(2,1)S(1)} %get-tuple-element.41), channel_id=1, source_target_pairs={{0,2},{1,3},{2,0},{3,1},{4,6},{5,7},{6,4},{7,5},{8,10},{9,11},{10,... | collective-permute-start | bytes 393224 | tf_op jit(solution)/shard_map/ppermute | solution.py:40
  46.9 3.3 %collective-permute-done.refs_1_ = bf16[2,256,2048]{2,1,0:T(8,128)(2,1)} collective-permute-done((bf16[2,256,2048]{2,1,0:T(8,128)(2,1)}, bf16[2,256,2048]{2,1,0:T(8,128)(2,1)}, u32[]{:S(2)}, u32[]{:S(2)}) %collective-permute-start) | collective-permute-done | bytes 2097184 | tf_op jit(solution)/shard_map/ppermute | solution.py:35
  50.2 8.7 %step.15 = (bf16[2,2,256,2048]{3,2,1,0:T(8,128)(2,1)S(1)}, f32[4,64,512]{2,1,0:T(8,128)S(1)}, bf16[4,64,512]{2,1,0:T(8,128)(2,1)S(1)}, f32[1,64,512]{2,1,0:T(8,1...) custom-call(f32[11]{0:T(128)S(1)} %pad_maximum_fusion.1.table_ref, ...), custom_call_target="tpu_custom_call" | custom-call | flops 1000 | bytes 1000 | tf_op jit(solution)/shard_map/step/pallas_call | solution.py:393
  59.0 2.1 %collective-permute-start.12 = (bf16[2,128,2048]{2,1,0:T(8,128)(2,1)S(1)}, bf16[2,128,2048]{2,1,0:T(8,128)(2,1)S(1)}, u32[]{:S(2)}, u32[]{:S(2)}) collective-permute-start(bf16[2,128,2048]{2,1,0:T(8,128)(2,1)S(1)} %get-tuple-element.56), channel_id=1, source_target_pairs={{0,24},{8,0},{16,8},{24,16},{1,25},{9,1},{17,9},{25,17},{2,26},{10... | collective-permute-start | bytes 3145736 | tf_op jit(solution)/shard_map/ppermute | solution.py:35
  61.1 1.5 %collective-permute-start.6 = (bf16[4,64,512]{2,1,0:T(8,128)(2,1)S(1)}, bf16[4,64,512]{2,1,0:T(8,128)(2,1)S(1)}, u32[]{:S(2)}, u32[]{:S(2)}) collective-permute-start(bf16[4,64,512]{2,1,0:T(8,128)(2,1)S(1)} %get-tuple-element.45), channel_id=1, source_target_pairs={{0,1},{1,0},{2,3},{3,2},{4,5},{5,4},{6,7},{7,6},{8,9},{9,8},{10,11... | collective-permute-start | bytes 786440 | tf_op jit(solution)/shard_map/ppermute | solution.py:35
  62.5 2.6 %collective-permute-start.7 = (bf16[1,64,512]{2,1,0:T(8,128)(2,1)S(1)}, bf16[1,64,512]{2,1,0:T(8,128)(2,1)S(1)}, u32[]{:S(2)}, u32[]{:S(2)}) collective-permute-start(bf16[1,64,512]{2,1,0:T(8,128)(2,1)S(1)} %get-tuple-element.47), channel_id=1, source_target_pairs={{0,4},{1,5},{2,6},{3,7},{4,0},{5,1},{6,2},{7,3},{8,12},{9,13},{10,... | collective-permute-start | bytes 196616 | tf_op jit(solution)/shard_map/ppermute | solution.py:40
  65.1 1.9 %collective-permute-done.5.refs_1_ = bf16[2,192,2048]{2,1,0:T(8,128)(2,1)} collective-permute-done((bf16[2,192,2048]{2,1,0:T(8,128)(2,1)}, bf16[2,192,2048]{2,1,0:T(8,128)(2,1)}, u32[]{:S(2)}, u32[]{:S(2)}) %collective-permute-start.5) | collective-permute-done | bytes 1572896 | tf_op jit(solution)/shard_map/ppermute | solution.py:35
  67.0 0.7 collective-permute-done.7.refs_5_
  67.7 0.6 collective-permute-done.6.refs_3_
  68.3 3.4 %step.16 = (bf16[384,2048]{1,0:T(8,128)(2,1)S(1)}, bf16[4,64,384]{2,1,0:T(8,128)(2,1)S(1)}, f32[2,64,512]{2,1,0:T(8,128)S(1)}, bf16[2,64,512]{2,1,0:T(8,128)(2,1)S(1)}, f32[64,2,2,512]{3,2,1,0:T(2,128)}) custom-call(f32[11]{0:T(128)S(1)} %pad_maximum_fusion.1.table_ref, bf16[2,2,256,2048]{3,2,1,0:T(8,128)(2,1)S(1)} %get-tuple-element.42.refs_0_, ...), custom_call_target="tpu_custom_call" | custom-call | flops 1000 | bytes 1000 | tf_op jit(solution)/shard_map/step/pallas_call | solution.py:393
  71.7 1.6 %collective-permute-start.9 = (bf16[4,64,384]{2,1,0:T(8,128)(2,1)S(1)}, bf16[4,64,384]{2,1,0:T(8,128)(2,1)S(1)}, u32[]{:S(2)}, u32[]{:S(2)}) collective-permute-start(bf16[4,64,384]{2,1,0:T(8,128)(2,1)S(1)} %get-tuple-element.51), channel_id=1, source_target_pairs={{0,1},{1,0},{2,3},{3,2},{4,5},{5,4},{6,7},{7,6},{8,9},{9,8},{10,11... | collective-permute-start | bytes 589832 | tf_op jit(solution)/shard_map/ppermute | solution.py:35
  73.2 1.6 %collective-permute-start.8 = (bf16[2,64,512]{2,1,0:T(8,128)(2,1)S(1)}, bf16[2,64,512]{2,1,0:T(8,128)(2,1)S(1)}, u32[]{:S(2)}, u32[]{:S(2)}) collective-permute-start(bf16[2,64,512]{2,1,0:T(8,128)(2,1)S(1)} %get-tuple-element.49), channel_id=1, source_target_pairs={{0,2},{1,3},{2,0},{3,1},{4,6},{5,7},{6,4},{7,5},{8,10},{9,11},{10,... | collective-permute-start | bytes 393224 | tf_op jit(solution)/shard_map/ppermute | solution.py:40
  74.8 1.9 %step.17.refs_0_ = f32[4,64,384]{2,1,0:T(8,128)S(1)} custom-call(f32[11]{0:T(128)S(1)} %pad_maximum_fusion.1.table_ref, bf16[2,2,256,2048]{3,2,1,0:T(8,128)(2,1)S(1)} %get-tuple-element.42.refs_0_, bf16[384,2048]{1,0:T(8,128)(2,1)S(1)} %get-tuple-element.50.refs_1_), custom_call_target="tpu_custom_call" | custom-call | flops 1000 | bytes 1000 | tf_op jit(solution)/shard_map/step/pallas_call | solution.py:393
  76.7 1.6 %collective-permute-done.9.refs_1_ = bf16[4,64,384]{2,1,0:T(8,128)(2,1)S(1)} collective-permute-done((bf16[4,64,384]{2,1,0:T(8,128)(2,1)S(1)}, bf16[4,64,384]{2,1,0:T(8,128)(2,1)S(1)}, u32[]{:S(2)}, u32[]{:S(2)}) %collective-permute-start.9) | collective-permute-done | bytes 196640 | tf_op jit(solution)/shard_map/ppermute | solution.py:35
  78.3 0.6 step.18
  78.9 1.6 %collective-permute-start.10 = (bf16[2,64,384]{2,1,0:T(8,128)(2,1)S(1)}, bf16[2,64,384]{2,1,0:T(8,128)(2,1)S(1)}, u32[]{:S(2)}, u32[]{:S(2)}) collective-permute-start(bf16[2,64,384]{2,1,0:T(8,128)(2,1)S(1)} %get-tuple-element.53), channel_id=1, source_target_pairs={{0,2},{1,3},{2,0},{3,1},{4,6},{5,7},{6,4},{7,5},{8,10},{9,11},{10,... | collective-permute-start | bytes 294920 | tf_op jit(solution)/shard_map/ppermute | solution.py:40
  80.5 3.0 %collective-permute-done.10.refs_5_ = bf16[2,64,384]{2,1,0:T(8,128)(2,1)S(1)} collective-permute-done((bf16[2,64,384]{2,1,0:T(8,128)(2,1)S(1)}, bf16[2,64,384]{2,1,0:T(8,128)(2,1)S(1)}, u32[]{:S(2)}, u32[]{:S(2)}) %collective-permute-start.10) | collective-permute-done | bytes 98336 | tf_op jit(solution)/shard_map/ppermute | solution.py:40
  83.8 2.4 %step.19 = (bf16[384,2048]{1,0:T(8,128)(2,1)S(1)}, bf16[4,64,384]{2,1,0:T(8,128)(2,1)S(1)}, f32[1,64,896]{2,1,0:T(8,128)S(1)}, bf16[1,64,896]{2,1,0:T(8,128)(2,1)S(1)}) custom-call(f32[11]{0:T(128)S(1)} %pad_maximum_fusion.1.table_ref, bf16[2,2,256,2048]{3,2,1,0:T(8,128)(2,1)S(1)} %get-tuple-element.42.refs_0_, ...), custom_call_target="tpu_custom_call" | custom-call | flops 1000 | bytes 1000 | tf_op jit(solution)/shard_map/step/pallas_call | solution.py:393
  86.2 1.6 %collective-permute-start.13 = (bf16[4,64,384]{2,1,0:T(8,128)(2,1)S(1)}, bf16[4,64,384]{2,1,0:T(8,128)(2,1)S(1)}, u32[]{:S(2)}, u32[]{:S(2)}) collective-permute-start(bf16[4,64,384]{2,1,0:T(8,128)(2,1)S(1)} %get-tuple-element.59), channel_id=1, source_target_pairs={{0,1},{1,0},{2,3},{3,2},{4,5},{5,4},{6,7},{7,6},{8,9},{9,8},{10,11... | collective-permute-start | bytes 589832 | tf_op jit(solution)/shard_map/ppermute | solution.py:35
  87.8 2.6 %collective-permute-start.11 = (bf16[1,64,896]{2,1,0:T(8,128)(2,1)S(1)}, bf16[1,64,896]{2,1,0:T(8,128)(2,1)S(1)}, u32[]{:S(2)}, u32[]{:S(2)}) collective-permute-start(bf16[1,64,896]{2,1,0:T(8,128)(2,1)S(1)} %get-tuple-element.55), channel_id=1, source_target_pairs={{0,4},{1,5},{2,6},{3,7},{4,0},{5,1},{6,2},{7,3},{8,12},{9,13},{10,... | collective-permute-start | bytes 344072 | tf_op jit(solution)/shard_map/ppermute | solution.py:40
  90.3 1.9 %step.20.refs_0_ = f32[4,64,384]{2,1,0:T(8,128)S(1)} custom-call(f32[11]{0:T(128)S(1)} %pad_maximum_fusion.1.table_ref, bf16[2,2,256,2048]{3,2,1,0:T(8,128)(2,1)S(1)} %get-tuple-element.42.refs_0_, bf16[384,2048]{1,0:T(8,128)(2,1)S(1)} %get-tuple-element.58.refs_1_), custom_call_target="tpu_custom_call" | custom-call | flops 1000 | bytes 1000 | tf_op jit(solution)/shard_map/step/pallas_call | solution.py:393
  92.2 1.7 %collective-permute-done.13.refs_1_ = bf16[4,64,384]{2,1,0:T(8,128)(2,1)S(1)} collective-permute-done((bf16[4,64,384]{2,1,0:T(8,128)(2,1)S(1)}, bf16[4,64,384]{2,1,0:T(8,128)(2,1)S(1)}, u32[]{:S(2)}, u32[]{:S(2)}) %collective-permute-start.13) | collective-permute-done | bytes 196640 | tf_op jit(solution)/shard_map/ppermute | solution.py:35
  93.9 0.6 step.21
  94.5 2.7 %collective-permute-start.16 = (bf16[2,64,384]{2,1,0:T(8,128)(2,1)S(1)}, bf16[2,64,384]{2,1,0:T(8,128)(2,1)S(1)}, u32[]{:S(2)}, u32[]{:S(2)}) collective-permute-start(bf16[2,64,384]{2,1,0:T(8,128)(2,1)S(1)} %get-tuple-element.64), channel_id=1, source_target_pairs={{0,4},{1,5},{2,6},{3,7},{4,0},{5,1},{6,2},{7,3},{8,12},{9,13},{10,... | collective-permute-start | bytes 294920 | tf_op jit(solution)/shard_map/ppermute | solution.py:40
  97.2 1.7 %step.22 = (bf16[256,2048]{1,0:T(8,128)(2,1)S(1)}, bf16[4,64,128]{2,1,0:T(8,128)(2,1)S(1)}, bf16[4,64,128]{2,1,0:T(8,128)(2,1)S(1)}, f32[64,2,2,512]{3,2,1,0:T(2,128)}) custom-call(f32[11]{0:T(128)S(1)} %pad_maximum_fusion.1.table_ref, bf16[2,2,256,2048]{3,2,1,0:T(8,128)(2,1)S(1)} %get-tuple-element.42.refs_0_, ...), custom_call_target="tpu_custom_call", output_to_operand_aliasing={{3}: (5, {})} | custom-call | flops 1000 | bytes 1000 | tf_op jit(solution)/shard_map/step/pallas_call | solution.py:393
  98.9 1.6 %collective-permute-start.14 = (bf16[4,64,128]{2,1,0:T(8,128)(2,1)S(1)}, bf16[4,64,128]{2,1,0:T(8,128)(2,1)S(1)}, u32[]{:S(2)}, u32[]{:S(2)}) collective-permute-start(bf16[4,64,128]{2,1,0:T(8,128)(2,1)S(1)} %get-tuple-element.62), channel_id=1, source_target_pairs={{0,1},{1,0},{2,3},{3,2},{4,5},{5,4},{6,7},{7,6},{8,9},{9,8},{10,11... | collective-permute-start | bytes 196616 | tf_op jit(solution)/shard_map/ppermute | solution.py:35
  100.4 0.5 collective-permute-start.15
  101.0 1.3 %step.23.refs_0_ = f32[4,64,256]{2,1,0:T(8,128)S(1)} custom-call(f32[11]{0:T(128)S(1)} %pad_maximum_fusion.1.table_ref, bf16[2,2,256,2048]{3,2,1,0:T(8,128)(2,1)S(1)} %get-tuple-element.42.refs_0_, bf16[256,2048]{1,0:T(8,128)(2,1)S(1)} %get-tuple-element.61.refs_1_), custom_call_target="tpu_custom_call" | custom-call | flops 1000 | bytes 1000 | tf_op jit(solution)/shard_map/step/pallas_call | solution.py:393
  102.3 1.6 %collective-permute-done.14.refs_1_ = bf16[4,64,128]{2,1,0:T(8,128)(2,1)S(1)} collective-permute-done((bf16[4,64,128]{2,1,0:T(8,128)(2,1)S(1)}, bf16[4,64,128]{2,1,0:T(8,128)(2,1)S(1)}, u32[]{:S(2)}, u32[]{:S(2)}) %collective-permute-start.14) | collective-permute-done | bytes 65568 | tf_op jit(solution)/shard_map/ppermute | solution.py:35
  103.9 0.8 collective-permute-done.15.refs_2_
  104.7 0.6 step.24
  105.3 1.6 %collective-permute-start.17 = (bf16[1,64,640]{2,1,0:T(8,128)(2,1)S(1)}, bf16[1,64,640]{2,1,0:T(8,128)(2,1)S(1)}, u32[]{:S(2)}, u32[]{:S(2)}) collective-permute-start(bf16[1,64,640]{2,1,0:T(8,128)(2,1)S(1)} %get-tuple-element.66), channel_id=1, source_target_pairs={{0,2},{1,3},{2,0},{3,1},{4,6},{5,7},{6,4},{7,5},{8,10},{9,11},{10,... | collective-permute-start | bytes 245768 | tf_op jit(solution)/shard_map/ppermute | solution.py:40
  106.9 1.3 %collective-permute-start.18 = (bf16[1,64,256]{2,1,0:T(8,128)(2,1)S(1)}, bf16[1,64,256]{2,1,0:T(8,128)(2,1)S(1)}, u32[]{:S(2)}, u32[]{:S(2)}) collective-permute-start(bf16[1,64,256]{2,1,0:T(8,128)(2,1)S(1)} %get-tuple-element.68), channel_id=1, source_target_pairs={{0,6},{1,7},{2,4},{3,5},{4,2},{5,3},{6,0},{7,1},{8,14},{9,15},{10,... | collective-permute-start | bytes 98312 | tf_op jit(solution)/shard_map/ppermute | solution.py:40
  108.2 0.6 collective-permute-start.19
  108.9 3.8 %collective-permute-done.18.refs_5_ = bf16[1,64,256]{2,1,0:T(8,128)(2,1)S(1)} collective-permute-done((bf16[1,64,256]{2,1,0:T(8,128)(2,1)S(1)}, bf16[1,64,256]{2,1,0:T(8,128)(2,1)S(1)}, u32[]{:S(2)}, u32[]{:S(2)}) %collective-permute-start.18) | collective-permute-done | bytes 32800 | tf_op jit(solution)/shard_map/ppermute | solution.py:40
  112.7 0.4 collective-permute-done.19.refs_6_
  113.0 1.5 %step.25 = f32[64,2,2,512]{3,2,1,0:T(2,128)} custom-call(f32[11]{0:T(128)S(1)} %pad_maximum_fusion.1.table_ref, f32[1,64,896]{2,1,0:T(8,128)S(1)} %get-tuple-element.54.refs_2_.refs_0_, bf16[1,64,896]{2,1,0:T(8,128)(2,1)S(1)} %collective-permute-done.11.refs_3_.refs_1_, f32[1,64,384]{2,1,0:T(8,128)S(1)} %get-tuple-element.65.refs_2_, ...), custom_call_target="tpu_custom_call", output_to_operand_aliasing={{}: (9, {})} | custom-call | flops 1000 | bytes 1000 | tf_op jit(solution)/shard_map/step/pallas_call | solution.py:393
  (20 shorter events, 1.0 us)
Async XLA Ops:
  1.6 26.0 %collective-permute-start.1 = (bf16[2,256,2048]{2,1,0:T(8,128)(2,1)S(1)}, bf16[2,256,2048]{2,1,0:T(8,128)(2,1)}, u32[]{:S(2)}, u32[]{:S(2)}) collective-permute-start(bf16[2,256,2048]{2,1,0:T(8,128)(2,1)S(1)} %piece_of.3.rest_0_), channel_id=1, source_target_pairs={{0,24},{8,0},{16,8},{24,16},{1,25},{9,1},{17,9},{25,17},{2,26},{10... | collective-permute-start | bytes 6291464 | tf_op jit(solution)/shard_map/ppermute | solution.py:35
  6.6 3.2 %copy-start = (s32[2]{0:T(128)S(1)}, s32[2]{0:T(128)}, u32[]{:S(2)}) copy-start(s32[2]{0:T(128)} %param.4) | copy-start | bytes 28
  6.6 3.2 %copy-start.1 = (s32[2]{0:T(128)S(1)}, s32[2]{0:T(128)}, u32[]{:S(2)}) copy-start(s32[2]{0:T(128)} %param.5) | copy-start | bytes 28
  6.7 43.5 %collective-permute-start = (bf16[2,256,2048]{2,1,0:T(8,128)(2,1)}, bf16[2,256,2048]{2,1,0:T(8,128)(2,1)}, u32[]{:S(2)}, u32[]{:S(2)}) collective-permute-start(bf16[2,256,2048]{2,1,0:T(8,128)(2,1)} %piece_of.4.rest_0_), channel_id=1, source_target_pairs={{0,24},{8,0},{16,8},{24,16},{1,25},{9,1},{17,9},{25,17},{2,26},{10... | collective-permute-start | bytes 6291464 | tf_op jit(solution)/shard_map/ppermute | solution.py:35
  9.7 57.3 %collective-permute-start.5 = (bf16[2,192,2048]{2,1,0:T(8,128)(2,1)}, bf16[2,192,2048]{2,1,0:T(8,128)(2,1)}, u32[]{:S(2)}, u32[]{:S(2)}) collective-permute-start(bf16[2,192,2048]{2,1,0:T(8,128)(2,1)} %piece_of.5), channel_id=1, source_target_pairs={{0,24},{8,0},{16,8},{24,16},{1,25},{9,1},{17,9},{25,17},{2,26},{10... | collective-permute-start | bytes 4718600 | tf_op jit(solution)/shard_map/ppermute | solution.py:35
  35.3 48.4 %collective-permute-start.4 = (bf16[2,192,2048]{2,1,0:T(8,128)(2,1)S(1)}, bf16[2,192,2048]{2,1,0:T(8,128)(2,1)S(1)}, u32[]{:S(2)}, u32[]{:S(2)}) collective-permute-start(bf16[2,192,2048]{2,1,0:T(8,128)(2,1)S(1)} %get-tuple-element.43), channel_id=1, source_target_pairs={{0,24},{8,0},{16,8},{24,16},{1,25},{9,1},{17,9},{25,17},{2,26},{10... | collective-permute-start | bytes 4718600 | tf_op jit(solution)/shard_map/ppermute | solution.py:35
  37.4 7.2 %collective-permute-start.2 = (bf16[4,64,512]{2,1,0:T(8,128)(2,1)S(1)}, bf16[4,64,512]{2,1,0:T(8,128)(2,1)S(1)}, u32[]{:S(2)}, u32[]{:S(2)}) collective-permute-start(bf16[4,64,512]{2,1,0:T(8,128)(2,1)S(1)} %get-tuple-element.39), channel_id=1, source_target_pairs={{0,1},{1,0},{2,3},{3,2},{4,5},{5,4},{6,7},{7,6},{8,9},{9,8},{10,11... | collective-permute-start | bytes 786440 | tf_op jit(solution)/shard_map/ppermute | solution.py:35
  45.2 5.0 %collective-permute-start.3 = (bf16[2,64,512]{2,1,0:T(8,128)(2,1)S(1)}, bf16[2,64,512]{2,1,0:T(8,128)(2,1)S(1)}, u32[]{:S(2)}, u32[]{:S(2)}) collective-permute-start(bf16[2,64,512]{2,1,0:T(8,128)(2,1)S(1)} %get-tuple-element.41), channel_id=1, source_target_pairs={{0,2},{1,3},{2,0},{3,1},{4,6},{5,7},{6,4},{7,5},{8,10},{9,11},{10,... | collective-permute-start | bytes 393224 | tf_op jit(solution)/shard_map/ppermute | solution.py:40
  59.0 38.2 %collective-permute-start.12 = (bf16[2,128,2048]{2,1,0:T(8,128)(2,1)S(1)}, bf16[2,128,2048]{2,1,0:T(8,128)(2,1)S(1)}, u32[]{:S(2)}, u32[]{:S(2)}) collective-permute-start(bf16[2,128,2048]{2,1,0:T(8,128)(2,1)S(1)} %get-tuple-element.56), channel_id=1, source_target_pairs={{0,24},{8,0},{16,8},{24,16},{1,25},{9,1},{17,9},{25,17},{2,26},{10... | collective-permute-start | bytes 3145736 | tf_op jit(solution)/shard_map/ppermute | solution.py:35
  61.1 7.2 %collective-permute-start.6 = (bf16[4,64,512]{2,1,0:T(8,128)(2,1)S(1)}, bf16[4,64,512]{2,1,0:T(8,128)(2,1)S(1)}, u32[]{:S(2)}, u32[]{:S(2)}) collective-permute-start(bf16[4,64,512]{2,1,0:T(8,128)(2,1)S(1)} %get-tuple-element.45), channel_id=1, source_target_pairs={{0,1},{1,0},{2,3},{3,2},{4,5},{5,4},{6,7},{7,6},{8,9},{9,8},{10,11... | collective-permute-start | bytes 786440 | tf_op jit(solution)/shard_map/ppermute | solution.py:35
  62.5 5.2 %collective-permute-start.7 = (bf16[1,64,512]{2,1,0:T(8,128)(2,1)S(1)}, bf16[1,64,512]{2,1,0:T(8,128)(2,1)S(1)}, u32[]{:S(2)}, u32[]{:S(2)}) collective-permute-start(bf16[1,64,512]{2,1,0:T(8,128)(2,1)S(1)} %get-tuple-element.47), channel_id=1, source_target_pairs={{0,4},{1,5},{2,6},{3,7},{4,0},{5,1},{6,2},{7,3},{8,12},{9,13},{10,... | collective-permute-start | bytes 196616 | tf_op jit(solution)/shard_map/ppermute | solution.py:40
  71.7 6.6 %collective-permute-start.9 = (bf16[4,64,384]{2,1,0:T(8,128)(2,1)S(1)}, bf16[4,64,384]{2,1,0:T(8,128)(2,1)S(1)}, u32[]{:S(2)}, u32[]{:S(2)}) collective-permute-start(bf16[4,64,384]{2,1,0:T(8,128)(2,1)S(1)} %get-tuple-element.51), channel_id=1, source_target_pairs={{0,1},{1,0},{2,3},{3,2},{4,5},{5,4},{6,7},{7,6},{8,9},{9,8},{10,11... | collective-permute-start | bytes 589832 | tf_op jit(solution)/shard_map/ppermute | solution.py:35
  73.2 7.3 %collective-permute-start.8 = (bf16[2,64,512]{2,1,0:T(8,128)(2,1)S(1)}, bf16[2,64,512]{2,1,0:T(8,128)(2,1)S(1)}, u32[]{:S(2)}, u32[]{:S(2)}) collective-permute-start(bf16[2,64,512]{2,1,0:T(8,128)(2,1)S(1)} %get-tuple-element.49), channel_id=1, source_target_pairs={{0,2},{1,3},{2,0},{3,1},{4,6},{5,7},{6,4},{7,5},{8,10},{9,11},{10,... | collective-permute-start | bytes 393224 | tf_op jit(solution)/shard_map/ppermute | solution.py:40
  78.9 4.7 %collective-permute-start.10 = (bf16[2,64,384]{2,1,0:T(8,128)(2,1)S(1)}, bf16[2,64,384]{2,1,0:T(8,128)(2,1)S(1)}, u32[]{:S(2)}, u32[]{:S(2)}) collective-permute-start(bf16[2,64,384]{2,1,0:T(8,128)(2,1)S(1)} %get-tuple-element.53), channel_id=1, source_target_pairs={{0,2},{1,3},{2,0},{3,1},{4,6},{5,7},{6,4},{7,5},{8,10},{9,11},{10,... | collective-permute-start | bytes 294920 | tf_op jit(solution)/shard_map/ppermute | solution.py:40
  86.2 7.7 %collective-permute-start.13 = (bf16[4,64,384]{2,1,0:T(8,128)(2,1)S(1)}, bf16[4,64,384]{2,1,0:T(8,128)(2,1)S(1)}, u32[]{:S(2)}, u32[]{:S(2)}) collective-permute-start(bf16[4,64,384]{2,1,0:T(8,128)(2,1)S(1)} %get-tuple-element.59), channel_id=1, source_target_pairs={{0,1},{1,0},{2,3},{3,2},{4,5},{5,4},{6,7},{7,6},{8,9},{9,8},{10,11... | collective-permute-start | bytes 589832 | tf_op jit(solution)/shard_map/ppermute | solution.py:35
  87.8 9.4 %collective-permute-start.11 = (bf16[1,64,896]{2,1,0:T(8,128)(2,1)S(1)}, bf16[1,64,896]{2,1,0:T(8,128)(2,1)S(1)}, u32[]{:S(2)}, u32[]{:S(2)}) collective-permute-start(bf16[1,64,896]{2,1,0:T(8,128)(2,1)S(1)} %get-tuple-element.55), channel_id=1, source_target_pairs={{0,4},{1,5},{2,6},{3,7},{4,0},{5,1},{6,2},{7,3},{8,12},{9,13},{10,... | collective-permute-start | bytes 344072 | tf_op jit(solution)/shard_map/ppermute | solution.py:40
  94.5 10.2 %collective-permute-start.16 = (bf16[2,64,384]{2,1,0:T(8,128)(2,1)S(1)}, bf16[2,64,384]{2,1,0:T(8,128)(2,1)S(1)}, u32[]{:S(2)}, u32[]{:S(2)}) collective-permute-start(bf16[2,64,384]{2,1,0:T(8,128)(2,1)S(1)} %get-tuple-element.64), channel_id=1, source_target_pairs={{0,4},{1,5},{2,6},{3,7},{4,0},{5,1},{6,2},{7,3},{8,12},{9,13},{10,... | collective-permute-start | bytes 294920 | tf_op jit(solution)/shard_map/ppermute | solution.py:40
  98.9 5.0 %collective-permute-start.14 = (bf16[4,64,128]{2,1,0:T(8,128)(2,1)S(1)}, bf16[4,64,128]{2,1,0:T(8,128)(2,1)S(1)}, u32[]{:S(2)}, u32[]{:S(2)}) collective-permute-start(bf16[4,64,128]{2,1,0:T(8,128)(2,1)S(1)} %get-tuple-element.62), channel_id=1, source_target_pairs={{0,1},{1,0},{2,3},{3,2},{4,5},{5,4},{6,7},{7,6},{8,9},{9,8},{10,11... | collective-permute-start | bytes 196616 | tf_op jit(solution)/shard_map/ppermute | solution.py:35
  100.4 4.3 %collective-permute-start.15 = (bf16[4,64,128]{2,1,0:T(8,128)(2,1)S(1)}, bf16[4,64,128]{2,1,0:T(8,128)(2,1)S(1)}, u32[]{:S(2)}, u32[]{:S(2)}) collective-permute-start(bf16[4,64,128]{2,1,0:T(8,128)(2,1)S(1)} %get-tuple-element.63), channel_id=1, source_target_pairs={{0,1},{1,0},{2,3},{3,2},{4,5},{5,4},{6,7},{7,6},{8,9},{9,8},{10,11... | collective-permute-start | bytes 196616 | tf_op jit(solution)/shard_map/ppermute | solution.py:35
  105.3 7.7 %collective-permute-start.17 = (bf16[1,64,640]{2,1,0:T(8,128)(2,1)S(1)}, bf16[1,64,640]{2,1,0:T(8,128)(2,1)S(1)}, u32[]{:S(2)}, u32[]{:S(2)}) collective-permute-start(bf16[1,64,640]{2,1,0:T(8,128)(2,1)S(1)} %get-tuple-element.66), channel_id=1, source_target_pairs={{0,2},{1,3},{2,0},{3,1},{4,6},{5,7},{6,4},{7,5},{8,10},{9,11},{10,... | collective-permute-start | bytes 245768 | tf_op jit(solution)/shard_map/ppermute | solution.py:40
  106.9 5.7 %collective-permute-start.18 = (bf16[1,64,256]{2,1,0:T(8,128)(2,1)S(1)}, bf16[1,64,256]{2,1,0:T(8,128)(2,1)S(1)}, u32[]{:S(2)}, u32[]{:S(2)}) collective-permute-start(bf16[1,64,256]{2,1,0:T(8,128)(2,1)S(1)} %get-tuple-element.68), channel_id=1, source_target_pairs={{0,6},{1,7},{2,4},{3,5},{4,2},{5,3},{6,0},{7,1},{8,14},{9,15},{10,... | collective-permute-start | bytes 98312 | tf_op jit(solution)/shard_map/ppermute | solution.py:40
  108.2 4.8 %collective-permute-start.19 = (bf16[1,64,256]{2,1,0:T(8,128)(2,1)S(1)}, bf16[1,64,256]{2,1,0:T(8,128)(2,1)S(1)}, u32[]{:S(2)}, u32[]{:S(2)}) collective-permute-start(bf16[1,64,256]{2,1,0:T(8,128)(2,1)S(1)} %get-tuple-element.69), channel_id=1, source_target_pairs={{0,4},{1,5},{2,6},{3,7},{4,0},{5,1},{6,2},{7,3},{8,12},{9,13},{10,... | collective-permute-start | bytes 98312 | tf_op jit(solution)/shard_map/ppermute | solution.py:40

commit v23 on v21

--- a/solution.py
+++ b/solution.py
@@ -13,7 +13,7 @@
 PLANE = 1024
 STRIP = 32
 DEPTH = 512
-AHEAD = 3
+AHEAD = 4
 OUTER = 4
 SPLIT = 128
 JOINT = 2

time: 115 us -> 116 us (level)
  Pallas kernels: 39.3 us -> 42.5 us
  starting transfers between devices: 31.7 us -> 29.4 us
    ppermute x11, waiting for transfers between devices: 33.9 us -> 36.9 us  [shifted(): return lax.ppermute(block, axis, route)]
    ppermute x9, waiting for transfers between devices: 8.38 us -> 5.51 us  [swapped(): return lax.ppermute(block, axis, [(i, i ^ distance) for i in range(count)])]
    pallas_call x3 -> x4, Pallas kernels: 6.48 us -> 8.9 us  [piece_of(): pl.pallas_call(functools.partial(piece_kernel if after else first_kernel,...]
    ppermute x11, starting transfers between devices: 15.6 us -> 13.3 us  [shifted(): return lax.ppermute(block, axis, route)]
  transfers between devices with their start and end apart: 20 -> 20, of which waited for: 15 -> 14; matrix products, arithmetic and copies ran while one was open for 1% -> 1% of each run, Pallas kernels for 31% -> 34%
where the time goes in v23:
time: 116 us; the launch traced here: 115 us
  Pallas kernels  42.5 us (37%)
  waiting for transfers between devices  42.4 us (37%)
  starting transfers between devices  29.4 us (25%)
    ppermute x11, waiting for transfers between devices, shifted(): return lax.ppermute(block, axis, route)  36.9 us
    pallas_call x13, Pallas kernels, step(): pl.pallas_call(functools.partial(step_kernel, plan), in_specs=in_specs, o...  33.6 us
    ppermute x9, starting transfers between devices, swapped(): return lax.ppermute(block, axis, [(i, i ^ distance) for i in range(count)])  16.1 us
    ppermute x11, starting transfers between devices, shifted(): return lax.ppermute(block, axis, route)  13.3 us
    pallas_call x4, Pallas kernels, piece_of(): pl.pallas_call(functools.partial(piece_kernel if after else first_kernel,...  8.9 us
    ppermute x9, waiting for transfers between devices, swapped(): return lax.ppermute(block, axis, [(i, i ^ distance) for i in range(count)])  5.51 us
  transfers between devices with their start and end apart: 20, of which 14 were waited for; matrix products, arithmetic and copies ran while one was open for 1% of the time, Pallas kernels for 34%

profile of v23, /device:TPU:0, one launch (start us, length us, event | category | flops | bytes accessed | tf_op | source)
XLA Modules:
  0.0 115.3 jit_solution(11535073627782437629)
XLA Ops:
  0.0 1.6 %piece_of.4.rest_0_ = bf16[2,256,2048]{2,1,0:T(8,128)(2,1)S(1)} custom-call(bf16[2,2,512,2048]{3,2,1,0:T(8,128)(2,1)} %bands_ref.7), custom_call_target="tpu_custom_call" | custom-call | flops 1000 | bytes 1000 | tf_op jit(solution)/shard_map/piece_of/pallas_call | solution.py:82
  1.6 2.5 %collective-permute-start.1 = (bf16[2,256,2048]{2,1,0:T(8,128)(2,1)S(1)}, bf16[2,256,2048]{2,1,0:T(8,128)(2,1)}, u32[]{:S(2)}, u32[]{:S(2)}) collective-permute-start(bf16[2,256,2048]{2,1,0:T(8,128)(2,1)S(1)} %piece_of.4.rest_0_), channel_id=1, source_target_pairs={{0,24},{8,0},{16,8},{24,16},{1,25},{9,1},{17,9},{25,17},{2,26},{10... | collective-permute-start | bytes 6291464 | tf_op jit(solution)/shard_map/ppermute | solution.py:35
  4.0 2.6 %piece_of.5.rest_0_ = bf16[2,256,2048]{2,1,0:T(8,128)(2,1)} custom-call(bf16[2,2,512,2048]{3,2,1,0:T(8,128)(2,1)} %bands_ref.7, bf16[2,256,2048]{2,1,0:T(8,128)(2,1)S(1)} %piece_of.4.rest_0_), custom_call_target="tpu_custom_call" | custom-call | flops 1000 | bytes 1000 | tf_op jit(solution)/shard_map/piece_of/pallas_call | solution.py:82
  6.6 0.7 collective-permute-start
  7.4 2.3 %piece_of.6.rest_0_ = bf16[2,192,2048]{2,1,0:T(8,128)(2,1)} custom-call(bf16[2,2,512,2048]{3,2,1,0:T(8,128)(2,1)} %bands_ref.7, bf16[2,256,2048]{2,1,0:T(8,128)(2,1)} %piece_of.5.rest_0_), custom_call_target="tpu_custom_call" | custom-call | flops 1000 | bytes 1000 | tf_op jit(solution)/shard_map/piece_of/pallas_call | solution.py:82
  9.8 2.4 %piece_of.7 = bf16[2,192,2048]{2,1,0:T(8,128)(2,1)} custom-call(bf16[2,2,512,2048]{3,2,1,0:T(8,128)(2,1)} %bands_ref.7, bf16[2,192,2048]{2,1,0:T(8,128)(2,1)} %piece_of.6.rest_0_), custom_call_target="tpu_custom_call" | custom-call | flops 1000 | bytes 1000 | tf_op jit(solution)/shard_map/piece_of/pallas_call | solution.py:82
  12.9 14.7 %collective-permute-done.1.refs_1_ = bf16[2,256,2048]{2,1,0:T(8,128)(2,1)} collective-permute-done((bf16[2,256,2048]{2,1,0:T(8,128)(2,1)S(1)}, bf16[2,256,2048]{2,1,0:T(8,128)(2,1)}, u32[]{:S(2)}, u32[]{:S(2)}) %collective-permute-start.1) | collective-permute-done | bytes 2097184 | tf_op jit(solution)/shard_map/ppermute | solution.py:35
  27.6 7.7 %step.13 = (f32[4,64,512]{2,1,0:T(8,128)S(1)}, bf16[4,64,512]{2,1,0:T(8,128)(2,1)S(1)}, bf16[2,128,2048]{2,1,0:T(8,128)(2,1)S(1)}) custom-call(f32[11]{0:T(128)S(1)} %pad_maximum_fusion.1.table_ref, bf16[2,2,512,2048]{3,2,1,0:T(8,128)(2,1)} %bands_ref.7, bf16[2,256,2048]{2,1,0:T(8,128)(2,1)} %collective-permute-done.1.refs_1_), custom_call_target="tpu_custom_call" | custom-call | flops 1000 | bytes 1000 | tf_op jit(solution)/shard_map/step/pallas_call | solution.py:386
  35.3 1.6 %collective-permute-start.2 = (bf16[4,64,512]{2,1,0:T(8,128)(2,1)S(1)}, bf16[4,64,512]{2,1,0:T(8,128)(2,1)S(1)}, u32[]{:S(2)}, u32[]{:S(2)}) collective-permute-start(bf16[4,64,512]{2,1,0:T(8,128)(2,1)S(1)} %get-tuple-element.38), channel_id=1, source_target_pairs={{0,1},{1,0},{2,3},{3,2},{4,5},{5,4},{6,7},{7,6},{8,9},{9,8},{10,11... | collective-permute-start | bytes 786440 | tf_op jit(solution)/shard_map/ppermute | solution.py:35
  36.8 1.7 %collective-permute-start.12 = (bf16[2,128,2048]{2,1,0:T(8,128)(2,1)S(1)}, bf16[2,128,2048]{2,1,0:T(8,128)(2,1)S(1)}, u32[]{:S(2)}, u32[]{:S(2)}) collective-permute-start(bf16[2,128,2048]{2,1,0:T(8,128)(2,1)S(1)} %get-tuple-element.54), channel_id=1, source_target_pairs={{0,24},{8,0},{16,8},{24,16},{1,25},{9,1},{17,9},{25,17},{2,26},{10... | collective-permute-start | bytes 3145736 | tf_op jit(solution)/shard_map/ppermute | solution.py:35
  38.6 6.0 %collective-permute-done.2.refs_1_ = bf16[4,64,512]{2,1,0:T(8,128)(2,1)S(1)} collective-permute-done((bf16[4,64,512]{2,1,0:T(8,128)(2,1)S(1)}, bf16[4,64,512]{2,1,0:T(8,128)(2,1)S(1)}, u32[]{:S(2)}, u32[]{:S(2)}) %collective-permute-start.2) | collective-permute-done | bytes 262176 | tf_op jit(solution)/shard_map/ppermute | solution.py:35
  44.5 0.6 step.14
  45.1 1.6 %collective-permute-start.3 = (bf16[2,64,512]{2,1,0:T(8,128)(2,1)S(1)}, bf16[2,64,512]{2,1,0:T(8,128)(2,1)S(1)}, u32[]{:S(2)}, u32[]{:S(2)}) collective-permute-start(bf16[2,64,512]{2,1,0:T(8,128)(2,1)S(1)} %get-tuple-element.40), channel_id=1, source_target_pairs={{0,2},{1,3},{2,0},{3,1},{4,6},{5,7},{6,4},{7,5},{8,10},{9,11},{10,... | collective-permute-start | bytes 393224 | tf_op jit(solution)/shard_map/ppermute | solution.py:40
  46.8 3.4 %collective-permute-done.refs_1_ = bf16[2,256,2048]{2,1,0:T(8,128)(2,1)} collective-permute-done((bf16[2,256,2048]{2,1,0:T(8,128)(2,1)}, bf16[2,256,2048]{2,1,0:T(8,128)(2,1)}, u32[]{:S(2)}, u32[]{:S(2)}) %collective-permute-start) | collective-permute-done | bytes 2097184 | tf_op jit(solution)/shard_map/ppermute | solution.py:35
  50.2 0.6 collective-permute-done.3.refs_3_
  50.7 8.6 %step.15 = (bf16[2,2,256,2048]{3,2,1,0:T(8,128)(2,1)S(1)}, f32[4,64,512]{2,1,0:T(8,128)S(1)}, bf16[4,64,512]{2,1,0:T(8,128)(2,1)S(1)}, f32[1,64,512]{2,1,0:T(8,128)S(1)}, bf16[1,64,512]{2,1,0:T(8,128)(2,1)S(1)}) custom-call(f32[11]{0:T(128)S(1)} %pad_maximum_fusion.1.table_ref, bf16[2,2,512,2048]{3,2,1,0:T(8,128)(2,1)} %bands_ref.7, ...), custom_call_target="tpu_custom_call" | custom-call | flops 1000 | bytes 1000 | tf_op jit(solution)/shard_map/step/pallas_call | solution.py:386
  59.3 1.5 %collective-permute-start.6 = (bf16[4,64,512]{2,1,0:T(8,128)(2,1)S(1)}, bf16[4,64,512]{2,1,0:T(8,128)(2,1)S(1)}, u32[]{:S(2)}, u32[]{:S(2)}) collective-permute-start(bf16[4,64,512]{2,1,0:T(8,128)(2,1)S(1)} %get-tuple-element.43), channel_id=1, source_target_pairs={{0,1},{1,0},{2,3},{3,2},{4,5},{5,4},{6,7},{7,6},{8,9},{9,8},{10,11... | collective-permute-start | bytes 786440 | tf_op jit(solution)/shard_map/ppermute | solution.py:35
  60.8 2.6 %collective-permute-start.7 = (bf16[1,64,512]{2,1,0:T(8,128)(2,1)S(1)}, bf16[1,64,512]{2,1,0:T(8,128)(2,1)S(1)}, u32[]{:S(2)}, u32[]{:S(2)}) collective-permute-start(bf16[1,64,512]{2,1,0:T(8,128)(2,1)S(1)} %get-tuple-element.45), channel_id=1, source_target_pairs={{0,4},{1,5},{2,6},{3,7},{4,0},{5,1},{6,2},{7,3},{8,12},{9,13},{10,... | collective-permute-start | bytes 196616 | tf_op jit(solution)/shard_map/ppermute | solution.py:40
  63.4 3.6 %collective-permute-done.5.refs_1_ = bf16[2,192,2048]{2,1,0:T(8,128)(2,1)} collective-permute-done((bf16[2,192,2048]{2,1,0:T(8,128)(2,1)}, bf16[2,192,2048]{2,1,0:T(8,128)(2,1)}, u32[]{:S(2)}, u32[]{:S(2)}) %collective-permute-start.5) | collective-permute-done | bytes 1572896 | tf_op jit(solution)/shard_map/ppermute | solution.py:35
  67.4 0.5 collective-permute-done.6.refs_3_
  67.9 3.4 %step.16 = (bf16[384,2048]{1,0:T(8,128)(2,1)S(1)}, bf16[4,64,384]{2,1,0:T(8,128)(2,1)S(1)}, f32[2,64,512]{2,1,0:T(8,128)S(1)}, bf16[2,64,512]{2,1,0:T(8,128)(2,1)S(1)}, f32[64,2,2,512]{3,2,1,0:T(2,128)}) custom-call(f32[11]{0:T(128)S(1)} %pad_maximum_fusion.1.table_ref, bf16[2,2,256,2048]{3,2,1,0:T(8,128)(2,1)S(1)} %get-tuple-element.41.refs_0_, ...), custom_call_target="tpu_custom_call" | custom-call | flops 1000 | bytes 1000 | tf_op jit(solution)/shard_map/step/pallas_call | solution.py:386
  71.3 1.6 %collective-permute-start.9 = (bf16[4,64,384]{2,1,0:T(8,128)(2,1)S(1)}, bf16[4,64,384]{2,1,0:T(8,128)(2,1)S(1)}, u32[]{:S(2)}, u32[]{:S(2)}) collective-permute-start(bf16[4,64,384]{2,1,0:T(8,128)(2,1)S(1)} %get-tuple-element.49), channel_id=1, source_target_pairs={{0,1},{1,0},{2,3},{3,2},{4,5},{5,4},{6,7},{7,6},{8,9},{9,8},{10,11... | collective-permute-start | bytes 589832 | tf_op jit(solution)/shard_map/ppermute | solution.py:35
  72.8 1.6 %collective-permute-start.8 = (bf16[2,64,512]{2,1,0:T(8,128)(2,1)S(1)}, bf16[2,64,512]{2,1,0:T(8,128)(2,1)S(1)}, u32[]{:S(2)}, u32[]{:S(2)}) collective-permute-start(bf16[2,64,512]{2,1,0:T(8,128)(2,1)S(1)} %get-tuple-element.47), channel_id=1, source_target_pairs={{0,2},{1,3},{2,0},{3,1},{4,6},{5,7},{6,4},{7,5},{8,10},{9,11},{10,... | collective-permute-start | bytes 393224 | tf_op jit(solution)/shard_map/ppermute | solution.py:40
  74.4 1.9 %step.17.refs_0_ = f32[4,64,384]{2,1,0:T(8,128)S(1)} custom-call(f32[11]{0:T(128)S(1)} %pad_maximum_fusion.1.table_ref, bf16[2,2,256,2048]{3,2,1,0:T(8,128)(2,1)S(1)} %get-tuple-element.41.refs_0_, bf16[384,2048]{1,0:T(8,128)(2,1)S(1)} %get-tuple-element.48.refs_1_), custom_call_target="tpu_custom_call" | custom-call | flops 1000 | bytes 1000 | tf_op jit(solution)/shard_map/step/pallas_call | solution.py:386
  76.3 2.0 %collective-permute-done.9.refs_1_ = bf16[4,64,384]{2,1,0:T(8,128)(2,1)S(1)} collective-permute-done((bf16[4,64,384]{2,1,0:T(8,128)(2,1)S(1)}, bf16[4,64,384]{2,1,0:T(8,128)(2,1)S(1)}, u32[]{:S(2)}, u32[]{:S(2)}) %collective-permute-start.9) | collective-permute-done | bytes 196640 | tf_op jit(solution)/shard_map/ppermute | solution.py:35
  78.3 0.6 step.18
  78.9 1.6 %collective-permute-start.10 = (bf16[2,64,384]{2,1,0:T(8,128)(2,1)S(1)}, bf16[2,64,384]{2,1,0:T(8,128)(2,1)S(1)}, u32[]{:S(2)}, u32[]{:S(2)}) collective-permute-start(bf16[2,64,384]{2,1,0:T(8,128)(2,1)S(1)} %get-tuple-element.51), channel_id=1, source_target_pairs={{0,2},{1,3},{2,0},{3,1},{4,6},{5,7},{6,4},{7,5},{8,10},{9,11},{10,... | collective-permute-start | bytes 294920 | tf_op jit(solution)/shard_map/ppermute | solution.py:40
  80.5 3.4 %collective-permute-done.4.refs_1_ = bf16[2,192,2048]{2,1,0:T(8,128)(2,1)} collective-permute-done((bf16[2,192,2048]{2,1,0:T(8,128)(2,1)}, bf16[2,192,2048]{2,1,0:T(8,128)(2,1)}, u32[]{:S(2)}, u32[]{:S(2)}) %collective-permute-start.4) | collective-permute-done | bytes 1572896 | tf_op jit(solution)/shard_map/ppermute | solution.py:35
  83.9 3.3 %step.19 = (bf16[384,2048]{1,0:T(8,128)(2,1)S(1)}, bf16[4,64,384]{2,1,0:T(8,128)(2,1)S(1)}, f32[1,64,896]{2,1,0:T(8,128)S(1)}, bf16[1,64,896]{2,1,0:T(8,128)(2,1)S(1)}) custom-call(f32[11]{0:T(128)S(1)} %pad_maximum_fusion.1.table_ref, bf16[2,2,256,2048]{3,2,1,0:T(8,128)(2,1)S(1)} %get-tuple-element.41.refs_0_, ...), custom_call_target="tpu_custom_call" | custom-call | flops 1000 | bytes 1000 | tf_op jit(solution)/shard_map/step/pallas_call | solution.py:386
  87.2 1.6 %collective-permute-start.13 = (bf16[4,64,384]{2,1,0:T(8,128)(2,1)S(1)}, bf16[4,64,384]{2,1,0:T(8,128)(2,1)S(1)}, u32[]{:S(2)}, u32[]{:S(2)}) collective-permute-start(bf16[4,64,384]{2,1,0:T(8,128)(2,1)S(1)} %get-tuple-element.57), channel_id=1, source_target_pairs={{0,1},{1,0},{2,3},{3,2},{4,5},{5,4},{6,7},{7,6},{8,9},{9,8},{10,11... | collective-permute-start | bytes 589832 | tf_op jit(solution)/shard_map/ppermute | solution.py:35
  88.8 2.6 %collective-permute-start.11 = (bf16[1,64,896]{2,1,0:T(8,128)(2,1)S(1)}, bf16[1,64,896]{2,1,0:T(8,128)(2,1)S(1)}, u32[]{:S(2)}, u32[]{:S(2)}) collective-permute-start(bf16[1,64,896]{2,1,0:T(8,128)(2,1)S(1)} %get-tuple-element.53), channel_id=1, source_target_pairs={{0,4},{1,5},{2,6},{3,7},{4,0},{5,1},{6,2},{7,3},{8,12},{9,13},{10,... | collective-permute-start | bytes 344072 | tf_op jit(solution)/shard_map/ppermute | solution.py:40
  91.3 1.9 %step.20.refs_0_ = f32[4,64,384]{2,1,0:T(8,128)S(1)} custom-call(f32[11]{0:T(128)S(1)} %pad_maximum_fusion.1.table_ref, bf16[2,2,256,2048]{3,2,1,0:T(8,128)(2,1)S(1)} %get-tuple-element.41.refs_0_, bf16[384,2048]{1,0:T(8,128)(2,1)S(1)} %get-tuple-element.56.refs_1_), custom_call_target="tpu_custom_call" | custom-call | flops 1000 | bytes 1000 | tf_op jit(solution)/shard_map/step/pallas_call | solution.py:386
  93.2 1.7 %collective-permute-done.13.refs_1_ = bf16[4,64,384]{2,1,0:T(8,128)(2,1)S(1)} collective-permute-done((bf16[4,64,384]{2,1,0:T(8,128)(2,1)S(1)}, bf16[4,64,384]{2,1,0:T(8,128)(2,1)S(1)}, u32[]{:S(2)}, u32[]{:S(2)}) %collective-permute-start.13) | collective-permute-done | bytes 196640 | tf_op jit(solution)/shard_map/ppermute | solution.py:35
  94.9 0.6 step.21
  95.5 1.6 %collective-permute-start.16 = (bf16[2,64,384]{2,1,0:T(8,128)(2,1)S(1)}, bf16[2,64,384]{2,1,0:T(8,128)(2,1)S(1)}, u32[]{:S(2)}, u32[]{:S(2)}) collective-permute-start(bf16[2,64,384]{2,1,0:T(8,128)(2,1)S(1)} %get-tuple-element.62), channel_id=1, source_target_pairs={{0,2},{1,3},{2,0},{3,1},{4,6},{5,7},{6,4},{7,5},{8,10},{9,11},{10,... | collective-permute-start | bytes 294920 | tf_op jit(solution)/shard_map/ppermute | solution.py:40
  97.2 0.6 collective-permute-done.11.refs_3_.refs_1_
  97.7 1.7 %step.22 = (bf16[256,2048]{1,0:T(8,128)(2,1)S(1)}, bf16[4,64,128]{2,1,0:T(8,128)(2,1)S(1)}, bf16[4,64,128]{2,1,0:T(8,128)(2,1)S(1)}, f32[64,2,2,512]{3,2,1,0:T(2,128)}) custom-call(f32[11]{0:T(128)S(1)} %pad_maximum_fusion.1.table_ref, bf16[2,2,256,2048]{3,2,1,0:T(8,128)(2,1)S(1)} %get-tuple-element.41.refs_0_, ...), custom_call_target="tpu_custom_call", output_to_operand_aliasing={{3}: (5, {})} | custom-call | flops 1000 | bytes 1000 | tf_op jit(solution)/shard_map/step/pallas_call | solution.py:386
  99.4 1.0 collective-permute-start.14
  100.4 1.1 collective-permute-start.15
  101.5 1.3 %step.23.refs_0_ = f32[4,64,256]{2,1,0:T(8,128)S(1)} custom-call(f32[11]{0:T(128)S(1)} %pad_maximum_fusion.1.table_ref, bf16[2,2,256,2048]{3,2,1,0:T(8,128)(2,1)S(1)} %get-tuple-element.41.refs_0_, bf16[256,2048]{1,0:T(8,128)(2,1)S(1)} %get-tuple-element.59.refs_1_), custom_call_target="tpu_custom_call" | custom-call | flops 1000 | bytes 1000 | tf_op jit(solution)/shard_map/step/pallas_call | solution.py:386
  102.8 1.2 %collective-permute-done.14.refs_1_ = bf16[4,64,128]{2,1,0:T(8,128)(2,1)S(1)} collective-permute-done((bf16[4,64,128]{2,1,0:T(8,128)(2,1)S(1)}, bf16[4,64,128]{2,1,0:T(8,128)(2,1)S(1)}, u32[]{:S(2)}, u32[]{:S(2)}) %collective-permute-start.14) | collective-permute-done | bytes 65568 | tf_op jit(solution)/shard_map/ppermute | solution.py:35
  104.0 0.7 collective-permute-done.15.refs_2_
  104.7 0.6 step.24
  105.3 2.7 %collective-permute-start.17 = (bf16[1,64,640]{2,1,0:T(8,128)(2,1)S(1)}, bf16[1,64,640]{2,1,0:T(8,128)(2,1)S(1)}, u32[]{:S(2)}, u32[]{:S(2)}) collective-permute-start(bf16[1,64,640]{2,1,0:T(8,128)(2,1)S(1)} %get-tuple-element.64), channel_id=1, source_target_pairs={{0,4},{1,5},{2,6},{3,7},{4,0},{5,1},{6,2},{7,3},{8,12},{9,13},{10,... | collective-permute-start | bytes 245768 | tf_op jit(solution)/shard_map/ppermute | solution.py:40
  107.9 1.3 %collective-permute-start.18 = (bf16[1,64,256]{2,1,0:T(8,128)(2,1)S(1)}, bf16[1,64,256]{2,1,0:T(8,128)(2,1)S(1)}, u32[]{:S(2)}, u32[]{:S(2)}) collective-permute-start(bf16[1,64,256]{2,1,0:T(8,128)(2,1)S(1)} %get-tuple-element.66), channel_id=1, source_target_pairs={{0,6},{1,7},{2,4},{3,5},{4,2},{5,3},{6,0},{7,1},{8,14},{9,15},{10,... | collective-permute-start | bytes 98312 | tf_op jit(solution)/shard_map/ppermute | solution.py:40
  109.2 0.5 collective-permute-start.19
  109.7 4.0 %collective-permute-done.18.refs_5_ = bf16[1,64,256]{2,1,0:T(8,128)(2,1)S(1)} collective-permute-done((bf16[1,64,256]{2,1,0:T(8,128)(2,1)S(1)}, bf16[1,64,256]{2,1,0:T(8,128)(2,1)S(1)}, u32[]{:S(2)}, u32[]{:S(2)}) %collective-permute-start.18) | collective-permute-done | bytes 32800 | tf_op jit(solution)/shard_map/ppermute | solution.py:40
  113.6 1.5 %step.25 = f32[64,2,2,512]{3,2,1,0:T(2,128)} custom-call(f32[11]{0:T(128)S(1)} %pad_maximum_fusion.1.table_ref, f32[1,64,896]{2,1,0:T(8,128)S(1)} %get-tuple-element.52.refs_2_.refs_0_, bf16[1,64,896]{2,1,0:T(8,128)(2,1)S(1)} %collective-permute-done.11.refs_3_.refs_1_, f32[1,64,384]{2,1,0:T(8,128)S(1)} %get-tuple-element.63.refs_2_, ...), custom_call_target="tpu_custom_call", output_to_operand_aliasing={{}: (9, {})} | custom-call | flops 1000 | bytes 1000 | tf_op jit(solution)/shard_map/step/pallas_call | solution.py:386
  (21 shorter events, 1.2 us)
Async XLA Ops:
  1.6 26.0 %collective-permute-start.1 = (bf16[2,256,2048]{2,1,0:T(8,128)(2,1)S(1)}, bf16[2,256,2048]{2,1,0:T(8,128)(2,1)}, u32[]{:S(2)}, u32[]{:S(2)}) collective-permute-start(bf16[2,256,2048]{2,1,0:T(8,128)(2,1)S(1)} %piece_of.4.rest_0_), channel_id=1, source_target_pairs={{0,24},{8,0},{16,8},{24,16},{1,25},{9,1},{17,9},{25,17},{2,26},{10... | collective-permute-start | bytes 6291464 | tf_op jit(solution)/shard_map/ppermute | solution.py:35
  6.6 43.5 %collective-permute-start = (bf16[2,256,2048]{2,1,0:T(8,128)(2,1)}, bf16[2,256,2048]{2,1,0:T(8,128)(2,1)}, u32[]{:S(2)}, u32[]{:S(2)}) collective-permute-start(bf16[2,256,2048]{2,1,0:T(8,128)(2,1)} %piece_of.5.rest_0_), channel_id=1, source_target_pairs={{0,24},{8,0},{16,8},{24,16},{1,25},{9,1},{17,9},{25,17},{2,26},{10... | collective-permute-start | bytes 6291464 | tf_op jit(solution)/shard_map/ppermute | solution.py:35
  9.7 2.6 %copy-start = (s32[2]{0:T(128)S(1)}, s32[2]{0:T(128)}, u32[]{:S(2)}) copy-start(s32[2]{0:T(128)} %param.4) | copy-start | bytes 28
  9.7 2.6 %copy-start.1 = (s32[2]{0:T(128)S(1)}, s32[2]{0:T(128)}, u32[]{:S(2)}) copy-start(s32[2]{0:T(128)} %param.5) | copy-start | bytes 28
  9.7 57.3 %collective-permute-start.5 = (bf16[2,192,2048]{2,1,0:T(8,128)(2,1)}, bf16[2,192,2048]{2,1,0:T(8,128)(2,1)}, u32[]{:S(2)}, u32[]{:S(2)}) collective-permute-start(bf16[2,192,2048]{2,1,0:T(8,128)(2,1)} %piece_of.6.rest_0_), channel_id=1, source_target_pairs={{0,24},{8,0},{16,8},{24,16},{1,25},{9,1},{17,9},{25,17},{2,26},{10... | collective-permute-start | bytes 4718600 | tf_op jit(solution)/shard_map/ppermute | solution.py:35
  12.2 71.6 %collective-permute-start.4 = (bf16[2,192,2048]{2,1,0:T(8,128)(2,1)}, bf16[2,192,2048]{2,1,0:T(8,128)(2,1)}, u32[]{:S(2)}, u32[]{:S(2)}) collective-permute-start(bf16[2,192,2048]{2,1,0:T(8,128)(2,1)} %piece_of.7), channel_id=1, source_target_pairs={{0,24},{8,0},{16,8},{24,16},{1,25},{9,1},{17,9},{25,17},{2,26},{10... | collective-permute-start | bytes 4718600 | tf_op jit(solution)/shard_map/ppermute | solution.py:35
  35.3 9.2 %collective-permute-start.2 = (bf16[4,64,512]{2,1,0:T(8,128)(2,1)S(1)}, bf16[4,64,512]{2,1,0:T(8,128)(2,1)S(1)}, u32[]{:S(2)}, u32[]{:S(2)}) collective-permute-start(bf16[4,64,512]{2,1,0:T(8,128)(2,1)S(1)} %get-tuple-element.38), channel_id=1, source_target_pairs={{0,1},{1,0},{2,3},{3,2},{4,5},{5,4},{6,7},{7,6},{8,9},{9,8},{10,11... | collective-permute-start | bytes 786440 | tf_op jit(solution)/shard_map/ppermute | solution.py:35
  36.8 60.3 %collective-permute-start.12 = (bf16[2,128,2048]{2,1,0:T(8,128)(2,1)S(1)}, bf16[2,128,2048]{2,1,0:T(8,128)(2,1)S(1)}, u32[]{:S(2)}, u32[]{:S(2)}) collective-permute-start(bf16[2,128,2048]{2,1,0:T(8,128)(2,1)S(1)} %get-tuple-element.54), channel_id=1, source_target_pairs={{0,24},{8,0},{16,8},{24,16},{1,25},{9,1},{17,9},{25,17},{2,26},{10... | collective-permute-start | bytes 3145736 | tf_op jit(solution)/shard_map/ppermute | solution.py:35
  45.1 5.6 %collective-permute-start.3 = (bf16[2,64,512]{2,1,0:T(8,128)(2,1)S(1)}, bf16[2,64,512]{2,1,0:T(8,128)(2,1)S(1)}, u32[]{:S(2)}, u32[]{:S(2)}) collective-permute-start(bf16[2,64,512]{2,1,0:T(8,128)(2,1)S(1)} %get-tuple-element.40), channel_id=1, source_target_pairs={{0,2},{1,3},{2,0},{3,1},{4,6},{5,7},{6,4},{7,5},{8,10},{9,11},{10,... | collective-permute-start | bytes 393224 | tf_op jit(solution)/shard_map/ppermute | solution.py:40
  59.3 8.6 %collective-permute-start.6 = (bf16[4,64,512]{2,1,0:T(8,128)(2,1)S(1)}, bf16[4,64,512]{2,1,0:T(8,128)(2,1)S(1)}, u32[]{:S(2)}, u32[]{:S(2)}) collective-permute-start(bf16[4,64,512]{2,1,0:T(8,128)(2,1)S(1)} %get-tuple-element.43), channel_id=1, source_target_pairs={{0,1},{1,0},{2,3},{3,2},{4,5},{5,4},{6,7},{7,6},{8,9},{9,8},{10,11... | collective-permute-start | bytes 786440 | tf_op jit(solution)/shard_map/ppermute | solution.py:35
  60.8 6.6 %collective-permute-start.7 = (bf16[1,64,512]{2,1,0:T(8,128)(2,1)S(1)}, bf16[1,64,512]{2,1,0:T(8,128)(2,1)S(1)}, u32[]{:S(2)}, u32[]{:S(2)}) collective-permute-start(bf16[1,64,512]{2,1,0:T(8,128)(2,1)S(1)} %get-tuple-element.45), channel_id=1, source_target_pairs={{0,4},{1,5},{2,6},{3,7},{4,0},{5,1},{6,2},{7,3},{8,12},{9,13},{10,... | collective-permute-start | bytes 196616 | tf_op jit(solution)/shard_map/ppermute | solution.py:40
  71.3 7.0 %collective-permute-start.9 = (bf16[4,64,384]{2,1,0:T(8,128)(2,1)S(1)}, bf16[4,64,384]{2,1,0:T(8,128)(2,1)S(1)}, u32[]{:S(2)}, u32[]{:S(2)}) collective-permute-start(bf16[4,64,384]{2,1,0:T(8,128)(2,1)S(1)} %get-tuple-element.49), channel_id=1, source_target_pairs={{0,1},{1,0},{2,3},{3,2},{4,5},{5,4},{6,7},{7,6},{8,9},{9,8},{10,11... | collective-permute-start | bytes 589832 | tf_op jit(solution)/shard_map/ppermute | solution.py:35
  72.8 11.0 %collective-permute-start.8 = (bf16[2,64,512]{2,1,0:T(8,128)(2,1)S(1)}, bf16[2,64,512]{2,1,0:T(8,128)(2,1)S(1)}, u32[]{:S(2)}, u32[]{:S(2)}) collective-permute-start(bf16[2,64,512]{2,1,0:T(8,128)(2,1)S(1)} %get-tuple-element.47), channel_id=1, source_target_pairs={{0,2},{1,3},{2,0},{3,1},{4,6},{5,7},{6,4},{7,5},{8,10},{9,11},{10,... | collective-permute-start | bytes 393224 | tf_op jit(solution)/shard_map/ppermute | solution.py:40
  78.9 5.0 %collective-permute-start.10 = (bf16[2,64,384]{2,1,0:T(8,128)(2,1)S(1)}, bf16[2,64,384]{2,1,0:T(8,128)(2,1)S(1)}, u32[]{:S(2)}, u32[]{:S(2)}) collective-permute-start(bf16[2,64,384]{2,1,0:T(8,128)(2,1)S(1)} %get-tuple-element.51), channel_id=1, source_target_pairs={{0,2},{1,3},{2,0},{3,1},{4,6},{5,7},{6,4},{7,5},{8,10},{9,11},{10,... | collective-permute-start | bytes 294920 | tf_op jit(solution)/shard_map/ppermute | solution.py:40
  87.2 7.7 %collective-permute-start.13 = (bf16[4,64,384]{2,1,0:T(8,128)(2,1)S(1)}, bf16[4,64,384]{2,1,0:T(8,128)(2,1)S(1)}, u32[]{:S(2)}, u32[]{:S(2)}) collective-permute-start(bf16[4,64,384]{2,1,0:T(8,128)(2,1)S(1)} %get-tuple-element.57), channel_id=1, source_target_pairs={{0,1},{1,0},{2,3},{3,2},{4,5},{5,4},{6,7},{7,6},{8,9},{9,8},{10,11... | collective-permute-start | bytes 589832 | tf_op jit(solution)/shard_map/ppermute | solution.py:35
  88.8 9.0 %collective-permute-start.11 = (bf16[1,64,896]{2,1,0:T(8,128)(2,1)S(1)}, bf16[1,64,896]{2,1,0:T(8,128)(2,1)S(1)}, u32[]{:S(2)}, u32[]{:S(2)}) collective-permute-start(bf16[1,64,896]{2,1,0:T(8,128)(2,1)S(1)} %get-tuple-element.53), channel_id=1, source_target_pairs={{0,4},{1,5},{2,6},{3,7},{4,0},{5,1},{6,2},{7,3},{8,12},{9,13},{10,... | collective-permute-start | bytes 344072 | tf_op jit(solution)/shard_map/ppermute | solution.py:40
  95.5 9.2 %collective-permute-start.16 = (bf16[2,64,384]{2,1,0:T(8,128)(2,1)S(1)}, bf16[2,64,384]{2,1,0:T(8,128)(2,1)S(1)}, u32[]{:S(2)}, u32[]{:S(2)}) collective-permute-start(bf16[2,64,384]{2,1,0:T(8,128)(2,1)S(1)} %get-tuple-element.62), channel_id=1, source_target_pairs={{0,2},{1,3},{2,0},{3,1},{4,6},{5,7},{6,4},{7,5},{8,10},{9,11},{10,... | collective-permute-start | bytes 294920 | tf_op jit(solution)/shard_map/ppermute | solution.py:40
  99.4 4.6 %collective-permute-start.14 = (bf16[4,64,128]{2,1,0:T(8,128)(2,1)S(1)}, bf16[4,64,128]{2,1,0:T(8,128)(2,1)S(1)}, u32[]{:S(2)}, u32[]{:S(2)}) collective-permute-start(bf16[4,64,128]{2,1,0:T(8,128)(2,1)S(1)} %get-tuple-element.60), channel_id=1, source_target_pairs={{0,1},{1,0},{2,3},{3,2},{4,5},{5,4},{6,7},{7,6},{8,9},{9,8},{10,11... | collective-permute-start | bytes 196616 | tf_op jit(solution)/shard_map/ppermute | solution.py:35
  100.4 4.3 %collective-permute-start.15 = (bf16[4,64,128]{2,1,0:T(8,128)(2,1)S(1)}, bf16[4,64,128]{2,1,0:T(8,128)(2,1)S(1)}, u32[]{:S(2)}, u32[]{:S(2)}) collective-permute-start(bf16[4,64,128]{2,1,0:T(8,128)(2,1)S(1)} %get-tuple-element.61), channel_id=1, source_target_pairs={{0,1},{1,0},{2,3},{3,2},{4,5},{5,4},{6,7},{7,6},{8,9},{9,8},{10,11... | collective-permute-start | bytes 196616 | tf_op jit(solution)/shard_map/ppermute | solution.py:35
  105.3 8.4 %collective-permute-start.17 = (bf16[1,64,640]{2,1,0:T(8,128)(2,1)S(1)}, bf16[1,64,640]{2,1,0:T(8,128)(2,1)S(1)}, u32[]{:S(2)}, u32[]{:S(2)}) collective-permute-start(bf16[1,64,640]{2,1,0:T(8,128)(2,1)S(1)} %get-tuple-element.64), channel_id=1, source_target_pairs={{0,4},{1,5},{2,6},{3,7},{4,0},{5,1},{6,2},{7,3},{8,12},{9,13},{10,... | collective-permute-start | bytes 245768 | tf_op jit(solution)/shard_map/ppermute | solution.py:40
  107.9 5.7 %collective-permute-start.18 = (bf16[1,64,256]{2,1,0:T(8,128)(2,1)S(1)}, bf16[1,64,256]{2,1,0:T(8,128)(2,1)S(1)}, u32[]{:S(2)}, u32[]{:S(2)}) collective-permute-start(bf16[1,64,256]{2,1,0:T(8,128)(2,1)S(1)} %get-tuple-element.66), channel_id=1, source_target_pairs={{0,6},{1,7},{2,4},{3,5},{4,2},{5,3},{6,0},{7,1},{8,14},{9,15},{10,... | collective-permute-start | bytes 98312 | tf_op jit(solution)/shard_map/ppermute | solution.py:40
  109.2 4.5 %collective-permute-start.19 = (bf16[1,64,256]{2,1,0:T(8,128)(2,1)S(1)}, bf16[1,64,256]{2,1,0:T(8,128)(2,1)S(1)}, u32[]{:S(2)}, u32[]{:S(2)}) collective-permute-start(bf16[1,64,256]{2,1,0:T(8,128)(2,1)S(1)} %get-tuple-element.67), channel_id=1, source_target_pairs={{0,2},{1,3},{2,0},{3,1},{4,6},{5,7},{6,4},{7,5},{8,10},{9,11},{10,... | collective-permute-start | bytes 98312 | tf_op jit(solution)/shard_map/ppermute | solution.py:40

commit v24 on v21

--- a/solution.py
+++ b/solution.py
@@ -19,7 +19,7 @@
 JOINT = 2
 LANES = 128
 BLOCK = 256
-VMEM_BYTES = 44 * 1024 * 1024
+VMEM_BYTES = 45 * 1024 * 1024
 LEAN_BYTES = 32 * 1024 * 1024
 
 
@@ -517,8 +517,8 @@
             part,
             ways,
             phase,
-            "load" if kept is None else "held",
-            place == len(parts) - 4,
+            "held" if part and part[0] == k_dev - 1 else "load",
+            place == len(parts) - 5,
             tasks,
             tuple(len(arrays) for arrays in sources),
             adding,
@@ -533,7 +533,7 @@
         terms, near, found, sends, result, piece = step(
             plan,
             table,
-            bands if kept is None else kept,
+            kept if part and part[0] == k_dev - 1 else bands,
             phased,
             sources,
             arrived,

time: 115 us -> 115 us (level)
  transfers between devices with their start and end apart: 20 -> 20, of which waited for: 15 -> 14; matrix products, arithmetic and copies ran while one was open for 1% -> 1% of each run, Pallas kernels for 31% -> 31%
where the time goes in v24:
time: 115 us; the launch traced here: 114 us
  waiting for transfers between devices  43.2 us (38%)
  Pallas kernels  39.4 us (34%)
  starting transfers between devices  30.7 us (27%)
    ppermute x11, waiting for transfers between devices, shifted(): return lax.ppermute(block, axis, route)  34.4 us
    pallas_call x13, Pallas kernels, step(): pl.pallas_call(functools.partial(step_kernel, plan), in_specs=in_specs, o...  32.9 us
    ppermute x9, starting transfers between devices, swapped(): return lax.ppermute(block, axis, [(i, i ^ distance) for i in range(count)])  16.1 us
    ppermute x11, starting transfers between devices, shifted(): return lax.ppermute(block, axis, route)  14.7 us
    ppermute x9, waiting for transfers between devices, swapped(): return lax.ppermute(block, axis, [(i, i ^ distance) for i in range(count)])  8.8 us
    pallas_call x3, Pallas kernels, piece_of(): pl.pallas_call(functools.partial(piece_kernel if after else first_kernel,...  6.45 us
  transfers between devices with their start and end apart: 20, of which 14 were waited for; matrix products, arithmetic and copies ran while one was open for 1% of the time, Pallas kernels for 31%

profile of v24, /device:TPU:0, one launch (start us, length us, event | category | flops | bytes accessed | tf_op | source)
XLA Modules:
  0.0 114.3 jit_solution(13105261210861521121)
XLA Ops:
  0.0 1.6 %piece_of.3.rest_0_ = bf16[2,256,2048]{2,1,0:T(8,128)(2,1)S(1)} custom-call(bf16[2,2,512,2048]{3,2,1,0:T(8,128)(2,1)} %refs_0_.3), custom_call_target="tpu_custom_call" | custom-call | flops 1000 | bytes 1000 | tf_op jit(solution)/shard_map/piece_of/pallas_call | solution.py:82
  1.6 2.5 %collective-permute-start = (bf16[2,256,2048]{2,1,0:T(8,128)(2,1)S(1)}, bf16[2,256,2048]{2,1,0:T(8,128)(2,1)}, u32[]{:S(2)}, u32[]{:S(2)}) collective-permute-start(bf16[2,256,2048]{2,1,0:T(8,128)(2,1)S(1)} %piece_of.3.rest_0_), channel_id=1, source_target_pairs={{0,24},{8,0},{16,8},{24,16},{1,25},{9,1},{17,9},{25,17},{2,26},{10... | collective-permute-start | bytes 6291464 | tf_op jit(solution)/shard_map/ppermute | solution.py:35
  4.0 2.6 %piece_of.4.rest_0_ = bf16[2,256,2048]{2,1,0:T(8,128)(2,1)} custom-call(bf16[2,2,512,2048]{3,2,1,0:T(8,128)(2,1)} %refs_0_.3, bf16[2,256,2048]{2,1,0:T(8,128)(2,1)S(1)} %piece_of.3.rest_0_), custom_call_target="tpu_custom_call" | custom-call | flops 1000 | bytes 1000 | tf_op jit(solution)/shard_map/piece_of/pallas_call | solution.py:82
  6.6 0.7 collective-permute-start.3
  7.3 2.3 %piece_of.5 = bf16[2,192,2048]{2,1,0:T(8,128)(2,1)} custom-call(bf16[2,2,512,2048]{3,2,1,0:T(8,128)(2,1)} %refs_0_.3, bf16[2,256,2048]{2,1,0:T(8,128)(2,1)} %piece_of.4.rest_0_), custom_call_target="tpu_custom_call" | custom-call | flops 1000 | bytes 1000 | tf_op jit(solution)/shard_map/piece_of/pallas_call | solution.py:82
  10.4 17.2 %collective-permute-done.refs_1_ = bf16[2,256,2048]{2,1,0:T(8,128)(2,1)} collective-permute-done((bf16[2,256,2048]{2,1,0:T(8,128)(2,1)S(1)}, bf16[2,256,2048]{2,1,0:T(8,128)(2,1)}, u32[]{:S(2)}, u32[]{:S(2)}) %collective-permute-start) | collective-permute-done | bytes 2097184 | tf_op jit(solution)/shard_map/ppermute | solution.py:35
  27.6 8.8 %step.13 = (bf16[2,2,256,2048]{3,2,1,0:T(8,128)(2,1)S(1)}, f32[4,64,512]{2,1,0:T(8,128)S(1)}, bf16[4,64,512]{2,1,0:T(8,128)(2,1)S(1)}, bf16[2,192,2048]{2,1,0:T(8,128)(2,1)S(1)}) custom-call(f32[11]{0:T(128)S(1)} %pad_maximum_fusion.1.table_ref, bf16[2,2,512,2048]{3,2,1,0:T(8,128)(2,1)} %refs_0_.3, bf16[2,256,2048]{2,1,0:T(8,128)(2,1)} %collective-permute-done.refs_1_), custom_call_target="tpu_custom_call" | custom-call | flops 1000 | bytes 1000 | tf_op jit(solution)/shard_map/step/pallas_call | solution.py:386
  36.4 2.1 %collective-permute-start.1 = (bf16[2,192,2048]{2,1,0:T(8,128)(2,1)S(1)}, bf16[2,192,2048]{2,1,0:T(8,128)(2,1)S(1)}, u32[]{:S(2)}, u32[]{:S(2)}) collective-permute-start(bf16[2,192,2048]{2,1,0:T(8,128)(2,1)S(1)} %get-tuple-element.39), channel_id=1, source_target_pairs={{0,24},{8,0},{16,8},{24,16},{1,25},{9,1},{17,9},{25,17},{2,26},{10... | collective-permute-start | bytes 4718600 | tf_op jit(solution)/shard_map/ppermute | solution.py:35
  38.5 1.5 %collective-permute-start.4 = (bf16[4,64,512]{2,1,0:T(8,128)(2,1)S(1)}, bf16[4,64,512]{2,1,0:T(8,128)(2,1)S(1)}, u32[]{:S(2)}, u32[]{:S(2)}) collective-permute-start(bf16[4,64,512]{2,1,0:T(8,128)(2,1)S(1)} %get-tuple-element.41), channel_id=1, source_target_pairs={{0,1},{1,0},{2,3},{3,2},{4,5},{5,4},{6,7},{7,6},{8,9},{9,8},{10,11... | collective-permute-start | bytes 786440 | tf_op jit(solution)/shard_map/ppermute | solution.py:35
  40.0 5.7 %collective-permute-done.4.refs_1_ = bf16[4,64,512]{2,1,0:T(8,128)(2,1)S(1)} collective-permute-done((bf16[4,64,512]{2,1,0:T(8,128)(2,1)S(1)}, bf16[4,64,512]{2,1,0:T(8,128)(2,1)S(1)}, u32[]{:S(2)}, u32[]{:S(2)}) %collective-permute-start.4) | collective-permute-done | bytes 262176 | tf_op jit(solution)/shard_map/ppermute | solution.py:35
  45.7 0.6 step.14
  46.3 1.6 %collective-permute-start.5 = (bf16[2,64,512]{2,1,0:T(8,128)(2,1)S(1)}, bf16[2,64,512]{2,1,0:T(8,128)(2,1)S(1)}, u32[]{:S(2)}, u32[]{:S(2)}) collective-permute-start(bf16[2,64,512]{2,1,0:T(8,128)(2,1)S(1)} %get-tuple-element.43), channel_id=1, source_target_pairs={{0,2},{1,3},{2,0},{3,1},{4,6},{5,7},{6,4},{7,5},{8,10},{9,11},{10,... | collective-permute-start | bytes 393224 | tf_op jit(solution)/shard_map/ppermute | solution.py:40
  48.0 2.2 %collective-permute-done.3.refs_1_ = bf16[2,256,2048]{2,1,0:T(8,128)(2,1)} collective-permute-done((bf16[2,256,2048]{2,1,0:T(8,128)(2,1)}, bf16[2,256,2048]{2,1,0:T(8,128)(2,1)}, u32[]{:S(2)}, u32[]{:S(2)}) %collective-permute-start.3) | collective-permute-done | bytes 2097184 | tf_op jit(solution)/shard_map/ppermute | solution.py:35
  50.2 1.2 %collective-permute-done.5.refs_3_ = bf16[2,64,512]{2,1,0:T(8,128)(2,1)S(1)} collective-permute-done((bf16[2,64,512]{2,1,0:T(8,128)(2,1)S(1)}, bf16[2,64,512]{2,1,0:T(8,128)(2,1)S(1)}, u32[]{:S(2)}, u32[]{:S(2)}) %collective-permute-start.5) | collective-permute-done | bytes 131104 | tf_op jit(solution)/shard_map/ppermute | solution.py:40
  51.4 7.7 %step.15 = (f32[4,64,512]{2,1,0:T(8,128)S(1)}, bf16[4,64,512]{2,1,0:T(8,128)(2,1)S(1)}, f32[1,64,512]{2,1,0:T(8,128)S(1)}, bf16[1,64,512]{2,1,0:T(8,128)(2,1)S(1)}, bf16[2,128,2048]{2,1,0:T(8,128)(2,1)S(1)}) custom-call(f32[11]{0:T(128)S(1)} %pad_maximum_fusion.1.table_ref, bf16[2,2,512,2048]{3,2,1,0:T(8,128)(2,1)} %refs_0_.3, ...), custom_call_target="tpu_custom_call" | custom-call | flops 1000 | bytes 1000 | tf_op jit(solution)/shard_map/step/pallas_call | solution.py:386
  59.1 1.1 %collective-permute-start.12 = (bf16[2,128,2048]{2,1,0:T(8,128)(2,1)S(1)}, bf16[2,128,2048]{2,1,0:T(8,128)(2,1)S(1)}, u32[]{:S(2)}, u32[]{:S(2)}) collective-permute-start(bf16[2,128,2048]{2,1,0:T(8,128)(2,1)S(1)} %get-tuple-element.56), channel_id=1, source_target_pairs={{0,24},{8,0},{16,8},{24,16},{1,25},{9,1},{17,9},{25,17},{2,26},{10... | collective-permute-start | bytes 3145736 | tf_op jit(solution)/shard_map/ppermute | solution.py:35
  60.2 1.5 %collective-permute-start.6 = (bf16[4,64,512]{2,1,0:T(8,128)(2,1)S(1)}, bf16[4,64,512]{2,1,0:T(8,128)(2,1)S(1)}, u32[]{:S(2)}, u32[]{:S(2)}) collective-permute-start(bf16[4,64,512]{2,1,0:T(8,128)(2,1)S(1)} %get-tuple-element.45), channel_id=1, source_target_pairs={{0,1},{1,0},{2,3},{3,2},{4,5},{5,4},{6,7},{7,6},{8,9},{9,8},{10,11... | collective-permute-start | bytes 786440 | tf_op jit(solution)/shard_map/ppermute | solution.py:35
  61.7 2.6 %collective-permute-start.7 = (bf16[1,64,512]{2,1,0:T(8,128)(2,1)S(1)}, bf16[1,64,512]{2,1,0:T(8,128)(2,1)S(1)}, u32[]{:S(2)}, u32[]{:S(2)}) collective-permute-start(bf16[1,64,512]{2,1,0:T(8,128)(2,1)S(1)} %get-tuple-element.47), channel_id=1, source_target_pairs={{0,4},{1,5},{2,6},{3,7},{4,0},{5,1},{6,2},{7,3},{8,12},{9,13},{10,... | collective-permute-start | bytes 196616 | tf_op jit(solution)/shard_map/ppermute | solution.py:40
  64.3 2.7 %collective-permute-done.2.refs_1_ = bf16[2,192,2048]{2,1,0:T(8,128)(2,1)} collective-permute-done((bf16[2,192,2048]{2,1,0:T(8,128)(2,1)}, bf16[2,192,2048]{2,1,0:T(8,128)(2,1)}, u32[]{:S(2)}, u32[]{:S(2)}) %collective-permute-start.2) | collective-permute-done | bytes 1572896 | tf_op jit(solution)/shard_map/ppermute | solution.py:35
  67.0 1.0 collective-permute-done.6.refs_3_
  68.0 3.4 %step.16 = (bf16[384,2048]{1,0:T(8,128)(2,1)S(1)}, bf16[4,64,384]{2,1,0:T(8,128)(2,1)S(1)}, f32[2,64,512]{2,1,0:T(8,128)S(1)}, bf16[2,64,512]{2,1,0:T(8,128)(2,1)S(1)}, f32[64,2,2,512]{3,2,1,0:T(2,128)}) custom-call(f32[11]{0:T(128)S(1)} %pad_maximum_fusion.1.table_ref, bf16[2,2,256,2048]{3,2,1,0:T(8,128)(2,1)S(1)} %get-tuple-element.38.refs_0_, ...), custom_call_target="tpu_custom_call" | custom-call | flops 1000 | bytes 1000 | tf_op jit(solution)/shard_map/step/pallas_call | solution.py:386
  71.4 1.6 %collective-permute-start.9 = (bf16[4,64,384]{2,1,0:T(8,128)(2,1)S(1)}, bf16[4,64,384]{2,1,0:T(8,128)(2,1)S(1)}, u32[]{:S(2)}, u32[]{:S(2)}) collective-permute-start(bf16[4,64,384]{2,1,0:T(8,128)(2,1)S(1)} %get-tuple-element.51), channel_id=1, source_target_pairs={{0,1},{1,0},{2,3},{3,2},{4,5},{5,4},{6,7},{7,6},{8,9},{9,8},{10,11... | collective-permute-start | bytes 589832 | tf_op jit(solution)/shard_map/ppermute | solution.py:35
  73.0 1.6 %collective-permute-start.8 = (bf16[2,64,512]{2,1,0:T(8,128)(2,1)S(1)}, bf16[2,64,512]{2,1,0:T(8,128)(2,1)S(1)}, u32[]{:S(2)}, u32[]{:S(2)}) collective-permute-start(bf16[2,64,512]{2,1,0:T(8,128)(2,1)S(1)} %get-tuple-element.49), channel_id=1, source_target_pairs={{0,2},{1,3},{2,0},{3,1},{4,6},{5,7},{6,4},{7,5},{8,10},{9,11},{10,... | collective-permute-start | bytes 393224 | tf_op jit(solution)/shard_map/ppermute | solution.py:40
  74.5 1.9 %step.17.refs_0_ = f32[4,64,384]{2,1,0:T(8,128)S(1)} custom-call(f32[11]{0:T(128)S(1)} %pad_maximum_fusion.1.table_ref, bf16[2,2,256,2048]{3,2,1,0:T(8,128)(2,1)S(1)} %get-tuple-element.38.refs_0_, bf16[384,2048]{1,0:T(8,128)(2,1)S(1)} %get-tuple-element.50.refs_1_), custom_call_target="tpu_custom_call" | custom-call | flops 1000 | bytes 1000 | tf_op jit(solution)/shard_map/step/pallas_call | solution.py:386
  76.4 1.9 %collective-permute-done.9.refs_1_ = bf16[4,64,384]{2,1,0:T(8,128)(2,1)S(1)} collective-permute-done((bf16[4,64,384]{2,1,0:T(8,128)(2,1)S(1)}, bf16[4,64,384]{2,1,0:T(8,128)(2,1)S(1)}, u32[]{:S(2)}, u32[]{:S(2)}) %collective-permute-start.9) | collective-permute-done | bytes 196640 | tf_op jit(solution)/shard_map/ppermute | solution.py:35
  78.3 0.6 step.18
  78.9 1.6 %collective-permute-start.10 = (bf16[2,64,384]{2,1,0:T(8,128)(2,1)S(1)}, bf16[2,64,384]{2,1,0:T(8,128)(2,1)S(1)}, u32[]{:S(2)}, u32[]{:S(2)}) collective-permute-start(bf16[2,64,384]{2,1,0:T(8,128)(2,1)S(1)} %get-tuple-element.53), channel_id=1, source_target_pairs={{0,2},{1,3},{2,0},{3,1},{4,6},{5,7},{6,4},{7,5},{8,10},{9,11},{10,... | collective-permute-start | bytes 294920 | tf_op jit(solution)/shard_map/ppermute | solution.py:40
  80.5 3.0 %collective-permute-done.10.refs_5_ = bf16[2,64,384]{2,1,0:T(8,128)(2,1)S(1)} collective-permute-done((bf16[2,64,384]{2,1,0:T(8,128)(2,1)S(1)}, bf16[2,64,384]{2,1,0:T(8,128)(2,1)S(1)}, u32[]{:S(2)}, u32[]{:S(2)}) %collective-permute-start.10) | collective-permute-done | bytes 98336 | tf_op jit(solution)/shard_map/ppermute | solution.py:40
  83.8 2.4 %step.19 = (bf16[384,2048]{1,0:T(8,128)(2,1)S(1)}, bf16[4,64,384]{2,1,0:T(8,128)(2,1)S(1)}, f32[1,64,896]{2,1,0:T(8,128)S(1)}, bf16[1,64,896]{2,1,0:T(8,128)(2,1)S(1)}) custom-call(f32[11]{0:T(128)S(1)} %pad_maximum_fusion.1.table_ref, bf16[2,2,256,2048]{3,2,1,0:T(8,128)(2,1)S(1)} %get-tuple-element.38.refs_0_, ...), custom_call_target="tpu_custom_call" | custom-call | flops 1000 | bytes 1000 | tf_op jit(solution)/shard_map/step/pallas_call | solution.py:386
  86.2 1.6 %collective-permute-start.13 = (bf16[4,64,384]{2,1,0:T(8,128)(2,1)S(1)}, bf16[4,64,384]{2,1,0:T(8,128)(2,1)S(1)}, u32[]{:S(2)}, u32[]{:S(2)}) collective-permute-start(bf16[4,64,384]{2,1,0:T(8,128)(2,1)S(1)} %get-tuple-element.59), channel_id=1, source_target_pairs={{0,1},{1,0},{2,3},{3,2},{4,5},{5,4},{6,7},{7,6},{8,9},{9,8},{10,11... | collective-permute-start | bytes 589832 | tf_op jit(solution)/shard_map/ppermute | solution.py:35
  87.8 2.6 %collective-permute-start.11 = (bf16[1,64,896]{2,1,0:T(8,128)(2,1)S(1)}, bf16[1,64,896]{2,1,0:T(8,128)(2,1)S(1)}, u32[]{:S(2)}, u32[]{:S(2)}) collective-permute-start(bf16[1,64,896]{2,1,0:T(8,128)(2,1)S(1)} %get-tuple-element.55), channel_id=1, source_target_pairs={{0,4},{1,5},{2,6},{3,7},{4,0},{5,1},{6,2},{7,3},{8,12},{9,13},{10,... | collective-permute-start | bytes 344072 | tf_op jit(solution)/shard_map/ppermute | solution.py:40
  90.3 1.9 %step.20.refs_0_ = f32[4,64,384]{2,1,0:T(8,128)S(1)} custom-call(f32[11]{0:T(128)S(1)} %pad_maximum_fusion.1.table_ref, bf16[2,2,256,2048]{3,2,1,0:T(8,128)(2,1)S(1)} %get-tuple-element.38.refs_0_, bf16[384,2048]{1,0:T(8,128)(2,1)S(1)} %get-tuple-element.58.refs_1_), custom_call_target="tpu_custom_call" | custom-call | flops 1000 | bytes 1000 | tf_op jit(solution)/shard_map/step/pallas_call | solution.py:386
  92.2 1.7 %collective-permute-done.13.refs_1_ = bf16[4,64,384]{2,1,0:T(8,128)(2,1)S(1)} collective-permute-done((bf16[4,64,384]{2,1,0:T(8,128)(2,1)S(1)}, bf16[4,64,384]{2,1,0:T(8,128)(2,1)S(1)}, u32[]{:S(2)}, u32[]{:S(2)}) %collective-permute-start.13) | collective-permute-done | bytes 196640 | tf_op jit(solution)/shard_map/ppermute | solution.py:35
  93.9 0.6 step.21
  94.5 1.6 %collective-permute-start.16 = (bf16[2,64,384]{2,1,0:T(8,128)(2,1)S(1)}, bf16[2,64,384]{2,1,0:T(8,128)(2,1)S(1)}, u32[]{:S(2)}, u32[]{:S(2)}) collective-permute-start(bf16[2,64,384]{2,1,0:T(8,128)(2,1)S(1)} %get-tuple-element.64), channel_id=1, source_target_pairs={{0,2},{1,3},{2,0},{3,1},{4,6},{5,7},{6,4},{7,5},{8,10},{9,11},{10,... | collective-permute-start | bytes 294920 | tf_op jit(solution)/shard_map/ppermute | solution.py:40
  96.2 0.6 collective-permute-done.11.refs_3_.refs_1_
  96.7 1.7 %step.22 = (bf16[256,2048]{1,0:T(8,128)(2,1)S(1)}, bf16[4,64,128]{2,1,0:T(8,128)(2,1)S(1)}, bf16[4,64,128]{2,1,0:T(8,128)(2,1)S(1)}, f32[64,2,2,512]{3,2,1,0:T(2,128)}) custom-call(f32[11]{0:T(128)S(1)} %pad_maximum_fusion.1.table_ref, bf16[2,2,256,2048]{3,2,1,0:T(8,128)(2,1)S(1)} %get-tuple-element.38.refs_0_, ...), custom_call_target="tpu_custom_call", output_to_operand_aliasing={{3}: (5, {})} | custom-call | flops 1000 | bytes 1000 | tf_op jit(solution)/shard_map/step/pallas_call | solution.py:386
  98.4 1.0 collective-permute-start.14
  99.4 1.1 collective-permute-start.15
  100.5 1.3 %step.23.refs_0_ = f32[4,64,256]{2,1,0:T(8,128)S(1)} custom-call(f32[11]{0:T(128)S(1)} %pad_maximum_fusion.1.table_ref, bf16[2,2,256,2048]{3,2,1,0:T(8,128)(2,1)S(1)} %get-tuple-element.38.refs_0_, bf16[256,2048]{1,0:T(8,128)(2,1)S(1)} %get-tuple-element.61.refs_1_), custom_call_target="tpu_custom_call" | custom-call | flops 1000 | bytes 1000 | tf_op jit(solution)/shard_map/step/pallas_call | solution.py:386
  101.8 1.2 %collective-permute-done.14.refs_1_ = bf16[4,64,128]{2,1,0:T(8,128)(2,1)S(1)} collective-permute-done((bf16[4,64,128]{2,1,0:T(8,128)(2,1)S(1)}, bf16[4,64,128]{2,1,0:T(8,128)(2,1)S(1)}, u32[]{:S(2)}, u32[]{:S(2)}) %collective-permute-start.14) | collective-permute-done | bytes 65568 | tf_op jit(solution)/shard_map/ppermute | solution.py:35
  103.0 0.7 collective-permute-done.15.refs_2_
  103.7 0.6 step.24
  104.3 2.7 %collective-permute-start.17 = (bf16[1,64,640]{2,1,0:T(8,128)(2,1)S(1)}, bf16[1,64,640]{2,1,0:T(8,128)(2,1)S(1)}, u32[]{:S(2)}, u32[]{:S(2)}) collective-permute-start(bf16[1,64,640]{2,1,0:T(8,128)(2,1)S(1)} %get-tuple-element.66), channel_id=1, source_target_pairs={{0,4},{1,5},{2,6},{3,7},{4,0},{5,1},{6,2},{7,3},{8,12},{9,13},{10,... | collective-permute-start | bytes 245768 | tf_op jit(solution)/shard_map/ppermute | solution.py:40
  107.0 1.3 %collective-permute-start.18 = (bf16[1,64,256]{2,1,0:T(8,128)(2,1)S(1)}, bf16[1,64,256]{2,1,0:T(8,128)(2,1)S(1)}, u32[]{:S(2)}, u32[]{:S(2)}) collective-permute-start(bf16[1,64,256]{2,1,0:T(8,128)(2,1)S(1)} %get-tuple-element.68), channel_id=1, source_target_pairs={{0,6},{1,7},{2,4},{3,5},{4,2},{5,3},{6,0},{7,1},{8,14},{9,15},{10,... | collective-permute-start | bytes 98312 | tf_op jit(solution)/shard_map/ppermute | solution.py:40
  108.2 0.5 collective-permute-start.19
  108.7 4.0 %collective-permute-done.18.refs_5_ = bf16[1,64,256]{2,1,0:T(8,128)(2,1)S(1)} collective-permute-done((bf16[1,64,256]{2,1,0:T(8,128)(2,1)S(1)}, bf16[1,64,256]{2,1,0:T(8,128)(2,1)S(1)}, u32[]{:S(2)}, u32[]{:S(2)}) %collective-permute-start.18) | collective-permute-done | bytes 32800 | tf_op jit(solution)/shard_map/ppermute | solution.py:40
  112.7 1.5 %step.25 = f32[64,2,2,512]{3,2,1,0:T(2,128)} custom-call(f32[11]{0:T(128)S(1)} %pad_maximum_fusion.1.table_ref, f32[1,64,896]{2,1,0:T(8,128)S(1)} %get-tuple-element.54.refs_2_.refs_0_, bf16[1,64,896]{2,1,0:T(8,128)(2,1)S(1)} %collective-permute-done.11.refs_3_.refs_1_, f32[1,64,384]{2,1,0:T(8,128)S(1)} %get-tuple-element.65.refs_2_, ...), custom_call_target="tpu_custom_call", output_to_operand_aliasing={{}: (9, {})} | custom-call | flops 1000 | bytes 1000 | tf_op jit(solution)/shard_map/step/pallas_call | solution.py:386
  (20 shorter events, 0.9 us)
Async XLA Ops:
  1.6 26.0 %collective-permute-start = (bf16[2,256,2048]{2,1,0:T(8,128)(2,1)S(1)}, bf16[2,256,2048]{2,1,0:T(8,128)(2,1)}, u32[]{:S(2)}, u32[]{:S(2)}) collective-permute-start(bf16[2,256,2048]{2,1,0:T(8,128)(2,1)S(1)} %piece_of.3.rest_0_), channel_id=1, source_target_pairs={{0,24},{8,0},{16,8},{24,16},{1,25},{9,1},{17,9},{25,17},{2,26},{10... | collective-permute-start | bytes 6291464 | tf_op jit(solution)/shard_map/ppermute | solution.py:35
  6.6 3.2 %copy-start = (s32[2]{0:T(128)S(1)}, s32[2]{0:T(128)}, u32[]{:S(2)}) copy-start(s32[2]{0:T(128)} %param.4) | copy-start | bytes 28
  6.6 3.2 %copy-start.1 = (s32[2]{0:T(128)S(1)}, s32[2]{0:T(128)}, u32[]{:S(2)}) copy-start(s32[2]{0:T(128)} %param.5) | copy-start | bytes 28
  6.6 43.5 %collective-permute-start.3 = (bf16[2,256,2048]{2,1,0:T(8,128)(2,1)}, bf16[2,256,2048]{2,1,0:T(8,128)(2,1)}, u32[]{:S(2)}, u32[]{:S(2)}) collective-permute-start(bf16[2,256,2048]{2,1,0:T(8,128)(2,1)} %piece_of.4.rest_0_), channel_id=1, source_target_pairs={{0,24},{8,0},{16,8},{24,16},{1,25},{9,1},{17,9},{25,17},{2,26},{10... | collective-permute-start | bytes 6291464 | tf_op jit(solution)/shard_map/ppermute | solution.py:35
  9.7 57.3 %collective-permute-start.2 = (bf16[2,192,2048]{2,1,0:T(8,128)(2,1)}, bf16[2,192,2048]{2,1,0:T(8,128)(2,1)}, u32[]{:S(2)}, u32[]{:S(2)}) collective-permute-start(bf16[2,192,2048]{2,1,0:T(8,128)(2,1)} %piece_of.5), channel_id=1, source_target_pairs={{0,24},{8,0},{16,8},{24,16},{1,25},{9,1},{17,9},{25,17},{2,26},{10... | collective-permute-start | bytes 4718600 | tf_op jit(solution)/shard_map/ppermute | solution.py:35
  36.4 47.3 %collective-permute-start.1 = (bf16[2,192,2048]{2,1,0:T(8,128)(2,1)S(1)}, bf16[2,192,2048]{2,1,0:T(8,128)(2,1)S(1)}, u32[]{:S(2)}, u32[]{:S(2)}) collective-permute-start(bf16[2,192,2048]{2,1,0:T(8,128)(2,1)S(1)} %get-tuple-element.39), channel_id=1, source_target_pairs={{0,24},{8,0},{16,8},{24,16},{1,25},{9,1},{17,9},{25,17},{2,26},{10... | collective-permute-start | bytes 4718600 | tf_op jit(solution)/shard_map/ppermute | solution.py:35
  38.5 7.2 %collective-permute-start.4 = (bf16[4,64,512]{2,1,0:T(8,128)(2,1)S(1)}, bf16[4,64,512]{2,1,0:T(8,128)(2,1)S(1)}, u32[]{:S(2)}, u32[]{:S(2)}) collective-permute-start(bf16[4,64,512]{2,1,0:T(8,128)(2,1)S(1)} %get-tuple-element.41), channel_id=1, source_target_pairs={{0,1},{1,0},{2,3},{3,2},{4,5},{5,4},{6,7},{7,6},{8,9},{9,8},{10,11... | collective-permute-start | bytes 786440 | tf_op jit(solution)/shard_map/ppermute | solution.py:35
  46.3 5.0 %collective-permute-start.5 = (bf16[2,64,512]{2,1,0:T(8,128)(2,1)S(1)}, bf16[2,64,512]{2,1,0:T(8,128)(2,1)S(1)}, u32[]{:S(2)}, u32[]{:S(2)}) collective-permute-start(bf16[2,64,512]{2,1,0:T(8,128)(2,1)S(1)} %get-tuple-element.43), channel_id=1, source_target_pairs={{0,2},{1,3},{2,0},{3,1},{4,6},{5,7},{6,4},{7,5},{8,10},{9,11},{10,... | collective-permute-start | bytes 393224 | tf_op jit(solution)/shard_map/ppermute | solution.py:40
  59.1 37.1 %collective-permute-start.12 = (bf16[2,128,2048]{2,1,0:T(8,128)(2,1)S(1)}, bf16[2,128,2048]{2,1,0:T(8,128)(2,1)S(1)}, u32[]{:S(2)}, u32[]{:S(2)}) collective-permute-start(bf16[2,128,2048]{2,1,0:T(8,128)(2,1)S(1)} %get-tuple-element.56), channel_id=1, source_target_pairs={{0,24},{8,0},{16,8},{24,16},{1,25},{9,1},{17,9},{25,17},{2,26},{10... | collective-permute-start | bytes 3145736 | tf_op jit(solution)/shard_map/ppermute | solution.py:35
  60.2 7.8 %collective-permute-start.6 = (bf16[4,64,512]{2,1,0:T(8,128)(2,1)S(1)}, bf16[4,64,512]{2,1,0:T(8,128)(2,1)S(1)}, u32[]{:S(2)}, u32[]{:S(2)}) collective-permute-start(bf16[4,64,512]{2,1,0:T(8,128)(2,1)S(1)} %get-tuple-element.45), channel_id=1, source_target_pairs={{0,1},{1,0},{2,3},{3,2},{4,5},{5,4},{6,7},{7,6},{8,9},{9,8},{10,11... | collective-permute-start | bytes 786440 | tf_op jit(solution)/shard_map/ppermute | solution.py:35
  61.7 5.3 %collective-permute-start.7 = (bf16[1,64,512]{2,1,0:T(8,128)(2,1)S(1)}, bf16[1,64,512]{2,1,0:T(8,128)(2,1)S(1)}, u32[]{:S(2)}, u32[]{:S(2)}) collective-permute-start(bf16[1,64,512]{2,1,0:T(8,128)(2,1)S(1)} %get-tuple-element.47), channel_id=1, source_target_pairs={{0,4},{1,5},{2,6},{3,7},{4,0},{5,1},{6,2},{7,3},{8,12},{9,13},{10,... | collective-permute-start | bytes 196616 | tf_op jit(solution)/shard_map/ppermute | solution.py:40
  71.4 6.9 %collective-permute-start.9 = (bf16[4,64,384]{2,1,0:T(8,128)(2,1)S(1)}, bf16[4,64,384]{2,1,0:T(8,128)(2,1)S(1)}, u32[]{:S(2)}, u32[]{:S(2)}) collective-permute-start(bf16[4,64,384]{2,1,0:T(8,128)(2,1)S(1)} %get-tuple-element.51), channel_id=1, source_target_pairs={{0,1},{1,0},{2,3},{3,2},{4,5},{5,4},{6,7},{7,6},{8,9},{9,8},{10,11... | collective-permute-start | bytes 589832 | tf_op jit(solution)/shard_map/ppermute | solution.py:35
  73.0 7.6 %collective-permute-start.8 = (bf16[2,64,512]{2,1,0:T(8,128)(2,1)S(1)}, bf16[2,64,512]{2,1,0:T(8,128)(2,1)S(1)}, u32[]{:S(2)}, u32[]{:S(2)}) collective-permute-start(bf16[2,64,512]{2,1,0:T(8,128)(2,1)S(1)} %get-tuple-element.49), channel_id=1, source_target_pairs={{0,2},{1,3},{2,0},{3,1},{4,6},{5,7},{6,4},{7,5},{8,10},{9,11},{10,... | collective-permute-start | bytes 393224 | tf_op jit(solution)/shard_map/ppermute | solution.py:40
  78.9 4.7 %collective-permute-start.10 = (bf16[2,64,384]{2,1,0:T(8,128)(2,1)S(1)}, bf16[2,64,384]{2,1,0:T(8,128)(2,1)S(1)}, u32[]{:S(2)}, u32[]{:S(2)}) collective-permute-start(bf16[2,64,384]{2,1,0:T(8,128)(2,1)S(1)} %get-tuple-element.53), channel_id=1, source_target_pairs={{0,2},{1,3},{2,0},{3,1},{4,6},{5,7},{6,4},{7,5},{8,10},{9,11},{10,... | collective-permute-start | bytes 294920 | tf_op jit(solution)/shard_map/ppermute | solution.py:40
  86.2 7.7 %collective-permute-start.13 = (bf16[4,64,384]{2,1,0:T(8,128)(2,1)S(1)}, bf16[4,64,384]{2,1,0:T(8,128)(2,1)S(1)}, u32[]{:S(2)}, u32[]{:S(2)}) collective-permute-start(bf16[4,64,384]{2,1,0:T(8,128)(2,1)S(1)} %get-tuple-element.59), channel_id=1, source_target_pairs={{0,1},{1,0},{2,3},{3,2},{4,5},{5,4},{6,7},{7,6},{8,9},{9,8},{10,11... | collective-permute-start | bytes 589832 | tf_op jit(solution)/shard_map/ppermute | solution.py:35
  87.8 9.0 %collective-permute-start.11 = (bf16[1,64,896]{2,1,0:T(8,128)(2,1)S(1)}, bf16[1,64,896]{2,1,0:T(8,128)(2,1)S(1)}, u32[]{:S(2)}, u32[]{:S(2)}) collective-permute-start(bf16[1,64,896]{2,1,0:T(8,128)(2,1)S(1)} %get-tuple-element.55), channel_id=1, source_target_pairs={{0,4},{1,5},{2,6},{3,7},{4,0},{5,1},{6,2},{7,3},{8,12},{9,13},{10,... | collective-permute-start | bytes 344072 | tf_op jit(solution)/shard_map/ppermute | solution.py:40
  94.5 9.2 %collective-permute-start.16 = (bf16[2,64,384]{2,1,0:T(8,128)(2,1)S(1)}, bf16[2,64,384]{2,1,0:T(8,128)(2,1)S(1)}, u32[]{:S(2)}, u32[]{:S(2)}) collective-permute-start(bf16[2,64,384]{2,1,0:T(8,128)(2,1)S(1)} %get-tuple-element.64), channel_id=1, source_target_pairs={{0,2},{1,3},{2,0},{3,1},{4,6},{5,7},{6,4},{7,5},{8,10},{9,11},{10,... | collective-permute-start | bytes 294920 | tf_op jit(solution)/shard_map/ppermute | solution.py:40
  98.4 4.5 %collective-permute-start.14 = (bf16[4,64,128]{2,1,0:T(8,128)(2,1)S(1)}, bf16[4,64,128]{2,1,0:T(8,128)(2,1)S(1)}, u32[]{:S(2)}, u32[]{:S(2)}) collective-permute-start(bf16[4,64,128]{2,1,0:T(8,128)(2,1)S(1)} %get-tuple-element.62), channel_id=1, source_target_pairs={{0,1},{1,0},{2,3},{3,2},{4,5},{5,4},{6,7},{7,6},{8,9},{9,8},{10,11... | collective-permute-start | bytes 196616 | tf_op jit(solution)/shard_map/ppermute | solution.py:35
  99.4 4.3 %collective-permute-start.15 = (bf16[4,64,128]{2,1,0:T(8,128)(2,1)S(1)}, bf16[4,64,128]{2,1,0:T(8,128)(2,1)S(1)}, u32[]{:S(2)}, u32[]{:S(2)}) collective-permute-start(bf16[4,64,128]{2,1,0:T(8,128)(2,1)S(1)} %get-tuple-element.63), channel_id=1, source_target_pairs={{0,1},{1,0},{2,3},{3,2},{4,5},{5,4},{6,7},{7,6},{8,9},{9,8},{10,11... | collective-permute-start | bytes 196616 | tf_op jit(solution)/shard_map/ppermute | solution.py:35
  104.3 8.4 %collective-permute-start.17 = (bf16[1,64,640]{2,1,0:T(8,128)(2,1)S(1)}, bf16[1,64,640]{2,1,0:T(8,128)(2,1)S(1)}, u32[]{:S(2)}, u32[]{:S(2)}) collective-permute-start(bf16[1,64,640]{2,1,0:T(8,128)(2,1)S(1)} %get-tuple-element.66), channel_id=1, source_target_pairs={{0,4},{1,5},{2,6},{3,7},{4,0},{5,1},{6,2},{7,3},{8,12},{9,13},{10,... | collective-permute-start | bytes 245768 | tf_op jit(solution)/shard_map/ppermute | solution.py:40
  107.0 5.7 %collective-permute-start.18 = (bf16[1,64,256]{2,1,0:T(8,128)(2,1)S(1)}, bf16[1,64,256]{2,1,0:T(8,128)(2,1)S(1)}, u32[]{:S(2)}, u32[]{:S(2)}) collective-permute-start(bf16[1,64,256]{2,1,0:T(8,128)(2,1)S(1)} %get-tuple-element.68), channel_id=1, source_target_pairs={{0,6},{1,7},{2,4},{3,5},{4,2},{5,3},{6,0},{7,1},{8,14},{9,15},{10,... | collective-permute-start | bytes 98312 | tf_op jit(solution)/shard_map/ppermute | solution.py:40
  108.2 4.5 %collective-permute-start.19 = (bf16[1,64,256]{2,1,0:T(8,128)(2,1)S(1)}, bf16[1,64,256]{2,1,0:T(8,128)(2,1)S(1)}, u32[]{:S(2)}, u32[]{:S(2)}) collective-permute-start(bf16[1,64,256]{2,1,0:T(8,128)(2,1)S(1)} %get-tuple-element.69), channel_id=1, source_target_pairs={{0,2},{1,3},{2,0},{3,1},{4,6},{5,7},{6,4},{7,5},{8,10},{9,11},{10,... | collective-permute-start | bytes 98312 | tf_op jit(solution)/shard_map/ppermute | solution.py:40

commit v25 on v19

--- a/solution.py
+++ b/solution.py
@@ -15,7 +15,7 @@
 DEPTH = 512
 AHEAD = 3
 OUTER = 4
-SPLIT = 128
+SPLIT = 0
 JOINT = 2
 LANES = 128
 BLOCK = 256

time: 114 us -> 114 us (level)
  no operation moved by 1% of the time
where the time goes in v25:
time: 114 us
  waiting for transfers between devices  45.1 us (40%)
  Pallas kernels  38.8 us (34%)
  starting transfers between devices  29.3 us (26%)
    ppermute x10, waiting for transfers between devices, shifted(): return lax.ppermute(block, axis, route)  33.9 us
    pallas_call x12, Pallas kernels, step(): pl.pallas_call(functools.partial(step_kernel, plan), in_specs=in_specs, o...  32.3 us
    ppermute x9, starting transfers between devices, swapped(): return lax.ppermute(block, axis, [(i, i ^ distance) for i in range(count)])  15.2 us
    ppermute x10, starting transfers between devices, shifted(): return lax.ppermute(block, axis, route)  14.1 us
    ppermute x9, waiting for transfers between devices, swapped(): return lax.ppermute(block, axis, [(i, i ^ distance) for i in range(count)])  11.3 us
    pallas_call x3, Pallas kernels, piece_of(): pl.pallas_call(functools.partial(piece_kernel if after else first_kernel,...  6.46 us
  transfers between devices with their start and end apart: 19, of which 12 were waited for; matrix products, arithmetic and copies ran while one was open for 1% of the time, Pallas kernels for 29%

profile of v25, /device:TPU:0, one launch (start us, length us, event | category | flops | bytes accessed | tf_op | source)
XLA Modules:
  0.0 114.2 jit_solution(10403759980801284991)
XLA Ops:
  0.0 1.6 %piece_of.3.rest_0_ = bf16[2,256,2048]{2,1,0:T(8,128)(2,1)S(1)} custom-call(bf16[2,2,512,2048]{3,2,1,0:T(8,128)(2,1)} %refs_0_.5), custom_call_target="tpu_custom_call" | custom-call | flops 1000 | bytes 1000 | tf_op jit(solution)/shard_map/piece_of/pallas_call | solution.py:82
  1.6 2.5 %collective-permute-start.2 = (bf16[2,256,2048]{2,1,0:T(8,128)(2,1)S(1)}, bf16[2,256,2048]{2,1,0:T(8,128)(2,1)}, u32[]{:S(2)}, u32[]{:S(2)}) collective-permute-start(bf16[2,256,2048]{2,1,0:T(8,128)(2,1)S(1)} %piece_of.3.rest_0_), channel_id=1, source_target_pairs={{0,24},{8,0},{16,8},{24,16},{1,25},{9,1},{17,9},{25,17},{2,26},{10... | collective-permute-start | bytes 6291464 | tf_op jit(solution)/shard_map/ppermute | solution.py:35
  4.0 2.6 %piece_of.4.rest_0_ = bf16[2,256,2048]{2,1,0:T(8,128)(2,1)} custom-call(bf16[2,2,512,2048]{3,2,1,0:T(8,128)(2,1)} %refs_0_.5, bf16[2,256,2048]{2,1,0:T(8,128)(2,1)S(1)} %piece_of.3.rest_0_), custom_call_target="tpu_custom_call" | custom-call | flops 1000 | bytes 1000 | tf_op jit(solution)/shard_map/piece_of/pallas_call | solution.py:82
  6.6 0.7 collective-permute-start.1
  7.4 2.3 %piece_of.5 = bf16[2,192,2048]{2,1,0:T(8,128)(2,1)} custom-call(bf16[2,2,512,2048]{3,2,1,0:T(8,128)(2,1)} %refs_0_.5, bf16[2,256,2048]{2,1,0:T(8,128)(2,1)} %piece_of.4.rest_0_), custom_call_target="tpu_custom_call" | custom-call | flops 1000 | bytes 1000 | tf_op jit(solution)/shard_map/piece_of/pallas_call | solution.py:82
  9.8 0.1 select_reduce_fusion.1
  9.9 0.1 fusion.4
  10.1 0.1 copy.6
  10.4 17.2 %collective-permute-done.2.refs_1_ = bf16[2,256,2048]{2,1,0:T(8,128)(2,1)} collective-permute-done((bf16[2,256,2048]{2,1,0:T(8,128)(2,1)S(1)}, bf16[2,256,2048]{2,1,0:T(8,128)(2,1)}, u32[]{:S(2)}, u32[]{:S(2)}) %collective-permute-start.2) | collective-permute-done | bytes 2097184 | tf_op jit(solution)/shard_map/ppermute | solution.py:35
  27.6 7.7 %step.12 = (f32[4,64,512]{2,1,0:T(8,128)S(1)}, bf16[4,64,512]{2,1,0:T(8,128)(2,1)S(1)}, bf16[2,192,2048]{2,1,0:T(8,128)(2,1)S(1)}) custom-call(f32[11]{0:T(128)S(1)} %pad_maximum_fusion.1.table_ref, bf16[2,2,512,2048]{3,2,1,0:T(8,128)(2,1)} %refs_0_.5, bf16[2,256,2048]{2,1,0:T(8,128)(2,1)} %collective-permute-done.2.refs_1_), custom_call_target="tpu_custom_call" | custom-call | flops 1000 | bytes 1000 | tf_op jit(solution)/shard_map/step/pallas_call | solution.py:359
  35.3 2.1 %collective-permute-start.7 = (bf16[2,192,2048]{2,1,0:T(8,128)(2,1)S(1)}, bf16[2,192,2048]{2,1,0:T(8,128)(2,1)S(1)}, u32[]{:S(2)}, u32[]{:S(2)}) collective-permute-start(bf16[2,192,2048]{2,1,0:T(8,128)(2,1)S(1)} %get-tuple-element.46), channel_id=1, source_target_pairs={{0,24},{8,0},{16,8},{24,16},{1,25},{9,1},{17,9},{25,17},{2,26},{10... | collective-permute-start | bytes 4718600 | tf_op jit(solution)/shard_map/ppermute | solution.py:35
  37.4 1.5 %collective-permute-start.3 = (bf16[4,64,512]{2,1,0:T(8,128)(2,1)S(1)}, bf16[4,64,512]{2,1,0:T(8,128)(2,1)S(1)}, u32[]{:S(2)}, u32[]{:S(2)}) collective-permute-start(bf16[4,64,512]{2,1,0:T(8,128)(2,1)S(1)} %get-tuple-element.38), channel_id=1, source_target_pairs={{0,1},{1,0},{2,3},{3,2},{4,5},{5,4},{6,7},{7,6},{8,9},{9,8},{10,11... | collective-permute-start | bytes 786440 | tf_op jit(solution)/shard_map/ppermute | solution.py:35
  38.9 5.7 %collective-permute-done.3.refs_1_ = bf16[4,64,512]{2,1,0:T(8,128)(2,1)S(1)} collective-permute-done((bf16[4,64,512]{2,1,0:T(8,128)(2,1)S(1)}, bf16[4,64,512]{2,1,0:T(8,128)(2,1)S(1)}, u32[]{:S(2)}, u32[]{:S(2)}) %collective-permute-start.3) | collective-permute-done | bytes 262176 | tf_op jit(solution)/shard_map/ppermute | solution.py:35
  44.6 0.6 step.13
  45.2 1.6 %collective-permute-start.4 = (bf16[2,64,512]{2,1,0:T(8,128)(2,1)S(1)}, bf16[2,64,512]{2,1,0:T(8,128)(2,1)S(1)}, u32[]{:S(2)}, u32[]{:S(2)}) collective-permute-start(bf16[2,64,512]{2,1,0:T(8,128)(2,1)S(1)} %get-tuple-element.40), channel_id=1, source_target_pairs={{0,2},{1,3},{2,0},{3,1},{4,6},{5,7},{6,4},{7,5},{8,10},{9,11},{10,... | collective-permute-start | bytes 393224 | tf_op jit(solution)/shard_map/ppermute | solution.py:40
  46.9 3.3 %collective-permute-done.1.refs_1_ = bf16[2,256,2048]{2,1,0:T(8,128)(2,1)} collective-permute-done((bf16[2,256,2048]{2,1,0:T(8,128)(2,1)}, bf16[2,256,2048]{2,1,0:T(8,128)(2,1)}, u32[]{:S(2)}, u32[]{:S(2)}) %collective-permute-start.1) | collective-permute-done | bytes 2097184 | tf_op jit(solution)/shard_map/ppermute | solution.py:35
  50.2 0.1 collective-permute-done.4.refs_3_
  50.2 7.7 %step.14 = (f32[4,64,512]{2,1,0:T(8,128)S(1)}, bf16[4,64,512]{2,1,0:T(8,128)(2,1)S(1)}, f32[1,64,512]{2,1,0:T(8,128)S(1)}, bf16[1,64,512]{2,1,0:T(8,128)(2,1)S(1)}, bf16[2,128,2048]{2,1,0:T(8,128)(2,1)S(1)}) custom-call(f32[11]{0:T(128)S(1)} %pad_maximum_fusion.1.table_ref, bf16[2,2,512,2048]{3,2,1,0:T(8,128)(2,1)} %refs_0_.5, ...), custom_call_target="tpu_custom_call" | custom-call | flops 1000 | bytes 1000 | tf_op jit(solution)/shard_map/step/pallas_call | solution.py:359
  58.0 2.0 %collective-permute-start.12 = (bf16[2,128,2048]{2,1,0:T(8,128)(2,1)S(1)}, bf16[2,128,2048]{2,1,0:T(8,128)(2,1)S(1)}, u32[]{:S(2)}, u32[]{:S(2)}) collective-permute-start(bf16[2,128,2048]{2,1,0:T(8,128)(2,1)S(1)} %get-tuple-element.55), channel_id=1, source_target_pairs={{0,24},{8,0},{16,8},{24,16},{1,25},{9,1},{17,9},{25,17},{2,26},{10... | collective-permute-start | bytes 3145736 | tf_op jit(solution)/shard_map/ppermute | solution.py:35
  60.0 1.5 %collective-permute-start.5 = (bf16[4,64,512]{2,1,0:T(8,128)(2,1)S(1)}, bf16[4,64,512]{2,1,0:T(8,128)(2,1)S(1)}, u32[]{:S(2)}, u32[]{:S(2)}) collective-permute-start(bf16[4,64,512]{2,1,0:T(8,128)(2,1)S(1)} %get-tuple-element.42), channel_id=1, source_target_pairs={{0,1},{1,0},{2,3},{3,2},{4,5},{5,4},{6,7},{7,6},{8,9},{9,8},{10,11... | collective-permute-start | bytes 786440 | tf_op jit(solution)/shard_map/ppermute | solution.py:35
  61.5 2.6 %collective-permute-start.6 = (bf16[1,64,512]{2,1,0:T(8,128)(2,1)S(1)}, bf16[1,64,512]{2,1,0:T(8,128)(2,1)S(1)}, u32[]{:S(2)}, u32[]{:S(2)}) collective-permute-start(bf16[1,64,512]{2,1,0:T(8,128)(2,1)S(1)} %get-tuple-element.44), channel_id=1, source_target_pairs={{0,4},{1,5},{2,6},{3,7},{4,0},{5,1},{6,2},{7,3},{8,12},{9,13},{10,... | collective-permute-start | bytes 196616 | tf_op jit(solution)/shard_map/ppermute | solution.py:40
  64.1 2.9 %collective-permute-done.refs_1_ = bf16[2,192,2048]{2,1,0:T(8,128)(2,1)} collective-permute-done((bf16[2,192,2048]{2,1,0:T(8,128)(2,1)}, bf16[2,192,2048]{2,1,0:T(8,128)(2,1)}, u32[]{:S(2)}, u32[]{:S(2)}) %collective-permute-start) | collective-permute-done | bytes 1572896 | tf_op jit(solution)/shard_map/ppermute | solution.py:35
  67.0 0.2 collective-permute-done.5.refs_3_
  67.2 4.4 %step.15 = (bf16[384,2048]{1,0:T(8,128)(2,1)S(1)}, bf16[2,2,256,2048]{3,2,1,0:T(8,128)(2,1)S(1)}, bf16[4,64,384]{2,1,0:T(8,128)(2,1)S(1)}, f32[2,64,512]{2,1,0:T...) custom-call(f32[11]{0:T(128)S(1)} %pad_maximum_fusion.1.table_ref, ...), custom_call_target="tpu_custom_call" | custom-call | flops 1000 | bytes 1000 | tf_op jit(solution)/shard_map/step/pallas_call | solution.py:359
  71.6 1.6 %collective-permute-start.9 = (bf16[4,64,384]{2,1,0:T(8,128)(2,1)S(1)}, bf16[4,64,384]{2,1,0:T(8,128)(2,1)S(1)}, u32[]{:S(2)}, u32[]{:S(2)}) collective-permute-start(bf16[4,64,384]{2,1,0:T(8,128)(2,1)S(1)} %get-tuple-element.50), channel_id=1, source_target_pairs={{0,1},{1,0},{2,3},{3,2},{4,5},{5,4},{6,7},{7,6},{8,9},{9,8},{10,11... | collective-permute-start | bytes 589832 | tf_op jit(solution)/shard_map/ppermute | solution.py:35
  73.2 1.6 %collective-permute-start.8 = (bf16[2,64,512]{2,1,0:T(8,128)(2,1)S(1)}, bf16[2,64,512]{2,1,0:T(8,128)(2,1)S(1)}, u32[]{:S(2)}, u32[]{:S(2)}) collective-permute-start(bf16[2,64,512]{2,1,0:T(8,128)(2,1)S(1)} %get-tuple-element.48), channel_id=1, source_target_pairs={{0,2},{1,3},{2,0},{3,1},{4,6},{5,7},{6,4},{7,5},{8,10},{9,11},{10,... | collective-permute-start | bytes 393224 | tf_op jit(solution)/shard_map/ppermute | solution.py:40
  74.8 1.9 %step.16.refs_0_ = f32[4,64,384]{2,1,0:T(8,128)S(1)} custom-call(f32[11]{0:T(128)S(1)} %pad_maximum_fusion.1.table_ref, bf16[2,2,256,2048]{3,2,1,0:T(8,128)(2,1)S(1)} %get-tuple-element.45.refs_0_, bf16[384,2048]{1,0:T(8,128)(2,1)S(1)} %get-tuple-element.49.refs_1_), custom_call_target="tpu_custom_call" | custom-call | flops 1000 | bytes 1000 | tf_op jit(solution)/shard_map/step/pallas_call | solution.py:359
  76.7 2.5 %collective-permute-done.9.refs_1_ = bf16[4,64,384]{2,1,0:T(8,128)(2,1)S(1)} collective-permute-done((bf16[4,64,384]{2,1,0:T(8,128)(2,1)S(1)}, bf16[4,64,384]{2,1,0:T(8,128)(2,1)S(1)}, u32[]{:S(2)}, u32[]{:S(2)}) %collective-permute-start.9) | collective-permute-done | bytes 196640 | tf_op jit(solution)/shard_map/ppermute | solution.py:35
  79.1 0.6 step.17
  79.7 1.6 %collective-permute-start.10 = (bf16[2,64,384]{2,1,0:T(8,128)(2,1)S(1)}, bf16[2,64,384]{2,1,0:T(8,128)(2,1)S(1)}, u32[]{:S(2)}, u32[]{:S(2)}) collective-permute-start(bf16[2,64,384]{2,1,0:T(8,128)(2,1)S(1)} %get-tuple-element.52), channel_id=1, source_target_pairs={{0,2},{1,3},{2,0},{3,1},{4,6},{5,7},{6,4},{7,5},{8,10},{9,11},{10,... | collective-permute-start | bytes 294920 | tf_op jit(solution)/shard_map/ppermute | solution.py:40
  81.4 3.0 %collective-permute-done.10.refs_5_ = bf16[2,64,384]{2,1,0:T(8,128)(2,1)S(1)} collective-permute-done((bf16[2,64,384]{2,1,0:T(8,128)(2,1)S(1)}, bf16[2,64,384]{2,1,0:T(8,128)(2,1)S(1)}, u32[]{:S(2)}, u32[]{:S(2)}) %collective-permute-start.10) | collective-permute-done | bytes 98336 | tf_op jit(solution)/shard_map/ppermute | solution.py:40
  84.4 2.4 %step.18 = (bf16[384,2048]{1,0:T(8,128)(2,1)S(1)}, bf16[4,64,384]{2,1,0:T(8,128)(2,1)S(1)}, f32[1,64,896]{2,1,0:T(8,128)S(1)}, bf16[1,64,896]{2,1,0:T(8,128)(2,1)S(1)}) custom-call(f32[11]{0:T(128)S(1)} %pad_maximum_fusion.1.table_ref, bf16[2,2,256,2048]{3,2,1,0:T(8,128)(2,1)S(1)} %get-tuple-element.45.refs_0_, ...), custom_call_target="tpu_custom_call" | custom-call | flops 1000 | bytes 1000 | tf_op jit(solution)/shard_map/step/pallas_call | solution.py:359
  86.9 1.6 %collective-permute-start.13 = (bf16[4,64,384]{2,1,0:T(8,128)(2,1)S(1)}, bf16[4,64,384]{2,1,0:T(8,128)(2,1)S(1)}, u32[]{:S(2)}, u32[]{:S(2)}) collective-permute-start(bf16[4,64,384]{2,1,0:T(8,128)(2,1)S(1)} %get-tuple-element.57), channel_id=1, source_target_pairs={{0,1},{1,0},{2,3},{3,2},{4,5},{5,4},{6,7},{7,6},{8,9},{9,8},{10,11... | collective-permute-start | bytes 589832 | tf_op jit(solution)/shard_map/ppermute | solution.py:35
  88.4 2.6 %collective-permute-start.11 = (bf16[1,64,896]{2,1,0:T(8,128)(2,1)S(1)}, bf16[1,64,896]{2,1,0:T(8,128)(2,1)S(1)}, u32[]{:S(2)}, u32[]{:S(2)}) collective-permute-start(bf16[1,64,896]{2,1,0:T(8,128)(2,1)S(1)} %get-tuple-element.54), channel_id=1, source_target_pairs={{0,4},{1,5},{2,6},{3,7},{4,0},{5,1},{6,2},{7,3},{8,12},{9,13},{10,... | collective-permute-start | bytes 344072 | tf_op jit(solution)/shard_map/ppermute | solution.py:40
  91.0 1.9 %step.19.refs_2_ = f32[4,64,384]{2,1,0:T(8,128)S(1)} custom-call(f32[11]{0:T(128)S(1)} %pad_maximum_fusion.1.table_ref, bf16[2,2,256,2048]{3,2,1,0:T(8,128)(2,1)S(1)} %get-tuple-element.45.refs_0_, bf16[384,2048]{1,0:T(8,128)(2,1)S(1)} %get-tuple-element.56.refs_1_), custom_call_target="tpu_custom_call" | custom-call | flops 1000 | bytes 1000 | tf_op jit(solution)/shard_map/step/pallas_call | solution.py:359
  92.9 2.1 %collective-permute-done.12.refs_1_ = bf16[2,128,2048]{2,1,0:T(8,128)(2,1)S(1)} collective-permute-done((bf16[2,128,2048]{2,1,0:T(8,128)(2,1)S(1)}, bf16[2,128,2048]{2,1,0:T(8,128)(2,1)S(1)}, u32[]{:S(2)}, u32[]{:S(2)}) %collective-permute-start.12) | collective-permute-done | bytes 1048608 | tf_op jit(solution)/shard_map/ppermute | solution.py:35
  95.0 1.7 %collective-permute-done.11.refs_5_.refs_1_ = bf16[1,64,896]{2,1,0:T(8,128)(2,1)S(1)} collective-permute-done((bf16[1,64,896]{2,1,0:T(8,128)(2,1)S(1)}, bf16[1,64,896]{2,1,0:T(8,128)(2,1)S(1)}, u32[]{:S(2)}, u32[]{:S(2)}) %collective-permute-start.11) | collective-permute-done | bytes 114720 | tf_op jit(solution)/shard_map/ppermute | solution.py:40
  96.7 1.7 %step.20 = (bf16[256,2048]{1,0:T(8,128)(2,1)S(1)}, bf16[4,64,256]{2,1,0:T(8,128)(2,1)S(1)}, f32[2,64,384]{2,1,0:T(8,128)S(1)}, bf16[2,64,384]{2,1,0:T(8,128)(2,1)S(1)}, f32[64,2,2,512]{3,2,1,0:T(2,128)}) custom-call(f32[11]{0:T(128)S(1)} %pad_maximum_fusion.1.table_ref, ...), custom_call_target="tpu_custom_call", output_to_operand_aliasing={{4}: (7, {})} | custom-call | flops 1000 | bytes 1000 | tf_op jit(solution)/shard_map/step/pallas_call | solution.py:359
  98.5 0.6 collective-permute-start.14
  99.1 0.8 collective-permute-start.15
  99.9 1.3 %step.21.refs_0_ = f32[4,64,256]{2,1,0:T(8,128)S(1)} custom-call(f32[11]{0:T(128)S(1)} %pad_maximum_fusion.1.table_ref, bf16[2,2,256,2048]{3,2,1,0:T(8,128)(2,1)S(1)} %get-tuple-element.45.refs_0_, bf16[256,2048]{1,0:T(8,128)(2,1)S(1)} %get-tuple-element.59.refs_1_), custom_call_target="tpu_custom_call" | custom-call | flops 1000 | bytes 1000 | tf_op jit(solution)/shard_map/step/pallas_call | solution.py:359
  101.2 2.5 %collective-permute-done.15.refs_3_ = bf16[2,64,384]{2,1,0:T(8,128)(2,1)S(1)} collective-permute-done((bf16[2,64,384]{2,1,0:T(8,128)(2,1)S(1)}, bf16[2,64,384]{2,1,0:T(8,128)(2,1)S(1)}, u32[]{:S(2)}, u32[]{:S(2)}) %collective-permute-start.15) | collective-permute-done | bytes 98336 | tf_op jit(solution)/shard_map/ppermute | solution.py:40
  103.7 0.6 step.22
  104.3 2.5 %collective-permute-start.16 = (bf16[1,64,640]{2,1,0:T(8,128)(2,1)S(1)}, bf16[1,64,640]{2,1,0:T(8,128)(2,1)S(1)}, u32[]{:S(2)}, u32[]{:S(2)}) collective-permute-start(bf16[1,64,640]{2,1,0:T(8,128)(2,1)S(1)} %get-tuple-element.64), channel_id=1, source_target_pairs={{0,4},{1,5},{2,6},{3,7},{4,0},{5,1},{6,2},{7,3},{8,12},{9,13},{10,... | collective-permute-start | bytes 245768 | tf_op jit(solution)/shard_map/ppermute | solution.py:40
  106.8 1.4 %collective-permute-start.17 = (bf16[1,64,256]{2,1,0:T(8,128)(2,1)S(1)}, bf16[1,64,256]{2,1,0:T(8,128)(2,1)S(1)}, u32[]{:S(2)}, u32[]{:S(2)}) collective-permute-start(bf16[1,64,256]{2,1,0:T(8,128)(2,1)S(1)} %get-tuple-element.66), channel_id=1, source_target_pairs={{0,6},{1,7},{2,4},{3,5},{4,2},{5,3},{6,0},{7,1},{8,14},{9,15},{10,... | collective-permute-start | bytes 98312 | tf_op jit(solution)/shard_map/ppermute | solution.py:40
  108.2 0.5 collective-permute-start.18
  108.7 3.9 %collective-permute-done.17.refs_5_ = bf16[1,64,256]{2,1,0:T(8,128)(2,1)S(1)} collective-permute-done((bf16[1,64,256]{2,1,0:T(8,128)(2,1)S(1)}, bf16[1,64,256]{2,1,0:T(8,128)(2,1)S(1)}, u32[]{:S(2)}, u32[]{:S(2)}) %collective-permute-start.17) | collective-permute-done | bytes 32800 | tf_op jit(solution)/shard_map/ppermute | solution.py:40
  112.5 1.5 %step.23 = f32[64,2,2,512]{3,2,1,0:T(2,128)} custom-call(f32[11]{0:T(128)S(1)} %pad_maximum_fusion.1.table_ref, f32[1,64,896]{2,1,0:T(8,128)S(1)} %get-tuple-element.53.refs_4_.refs_0_, bf16[1,64,896]{2,1,0:T(8,128)(2,1)S(1)} %collective-permute-done.11.refs_5_.refs_1_, f32[1,64,384]{2,1,0:T(8,128)S(1)} %get-tuple-element.63.refs_2_, ...), custom_call_target="tpu_custom_call", output_to_operand_aliasing={{}: (9, {})} | custom-call | flops 1000 | bytes 1000 | tf_op jit(solution)/shard_map/step/pallas_call | solution.py:359
  (17 shorter events, 0.4 us)
Async XLA Ops:
  1.6 26.0 %collective-permute-start.2 = (bf16[2,256,2048]{2,1,0:T(8,128)(2,1)S(1)}, bf16[2,256,2048]{2,1,0:T(8,128)(2,1)}, u32[]{:S(2)}, u32[]{:S(2)}) collective-permute-start(bf16[2,256,2048]{2,1,0:T(8,128)(2,1)S(1)} %piece_of.3.rest_0_), channel_id=1, source_target_pairs={{0,24},{8,0},{16,8},{24,16},{1,25},{9,1},{17,9},{25,17},{2,26},{10... | collective-permute-start | bytes 6291464 | tf_op jit(solution)/shard_map/ppermute | solution.py:35
  6.6 3.1 %copy-start = (s32[2]{0:T(128)S(1)}, s32[2]{0:T(128)}, u32[]{:S(2)}) copy-start(s32[2]{0:T(128)} %param.4) | copy-start | bytes 28
  6.6 3.1 %copy-start.1 = (s32[2]{0:T(128)S(1)}, s32[2]{0:T(128)}, u32[]{:S(2)}) copy-start(s32[2]{0:T(128)} %param.5) | copy-start | bytes 28
  6.6 43.5 %collective-permute-start.1 = (bf16[2,256,2048]{2,1,0:T(8,128)(2,1)}, bf16[2,256,2048]{2,1,0:T(8,128)(2,1)}, u32[]{:S(2)}, u32[]{:S(2)}) collective-permute-start(bf16[2,256,2048]{2,1,0:T(8,128)(2,1)} %piece_of.4.rest_0_), channel_id=1, source_target_pairs={{0,24},{8,0},{16,8},{24,16},{1,25},{9,1},{17,9},{25,17},{2,26},{10... | collective-permute-start | bytes 6291464 | tf_op jit(solution)/shard_map/ppermute | solution.py:35
  9.7 57.3 %collective-permute-start = (bf16[2,192,2048]{2,1,0:T(8,128)(2,1)}, bf16[2,192,2048]{2,1,0:T(8,128)(2,1)}, u32[]{:S(2)}, u32[]{:S(2)}) collective-permute-start(bf16[2,192,2048]{2,1,0:T(8,128)(2,1)} %piece_of.5), channel_id=1, source_target_pairs={{0,24},{8,0},{16,8},{24,16},{1,25},{9,1},{17,9},{25,17},{2,26},{10... | collective-permute-start | bytes 4718600 | tf_op jit(solution)/shard_map/ppermute | solution.py:35
  35.3 49.1 %collective-permute-start.7 = (bf16[2,192,2048]{2,1,0:T(8,128)(2,1)S(1)}, bf16[2,192,2048]{2,1,0:T(8,128)(2,1)S(1)}, u32[]{:S(2)}, u32[]{:S(2)}) collective-permute-start(bf16[2,192,2048]{2,1,0:T(8,128)(2,1)S(1)} %get-tuple-element.46), channel_id=1, source_target_pairs={{0,24},{8,0},{16,8},{24,16},{1,25},{9,1},{17,9},{25,17},{2,26},{10... | collective-permute-start | bytes 4718600 | tf_op jit(solution)/shard_map/ppermute | solution.py:35
  37.4 7.2 %collective-permute-start.3 = (bf16[4,64,512]{2,1,0:T(8,128)(2,1)S(1)}, bf16[4,64,512]{2,1,0:T(8,128)(2,1)S(1)}, u32[]{:S(2)}, u32[]{:S(2)}) collective-permute-start(bf16[4,64,512]{2,1,0:T(8,128)(2,1)S(1)} %get-tuple-element.38), channel_id=1, source_target_pairs={{0,1},{1,0},{2,3},{3,2},{4,5},{5,4},{6,7},{7,6},{8,9},{9,8},{10,11... | collective-permute-start | bytes 786440 | tf_op jit(solution)/shard_map/ppermute | solution.py:35
  45.2 5.0 %collective-permute-start.4 = (bf16[2,64,512]{2,1,0:T(8,128)(2,1)S(1)}, bf16[2,64,512]{2,1,0:T(8,128)(2,1)S(1)}, u32[]{:S(2)}, u32[]{:S(2)}) collective-permute-start(bf16[2,64,512]{2,1,0:T(8,128)(2,1)S(1)} %get-tuple-element.40), channel_id=1, source_target_pairs={{0,2},{1,3},{2,0},{3,1},{4,6},{5,7},{6,4},{7,5},{8,10},{9,11},{10,... | collective-permute-start | bytes 393224 | tf_op jit(solution)/shard_map/ppermute | solution.py:40
  58.0 37.0 %collective-permute-start.12 = (bf16[2,128,2048]{2,1,0:T(8,128)(2,1)S(1)}, bf16[2,128,2048]{2,1,0:T(8,128)(2,1)S(1)}, u32[]{:S(2)}, u32[]{:S(2)}) collective-permute-start(bf16[2,128,2048]{2,1,0:T(8,128)(2,1)S(1)} %get-tuple-element.55), channel_id=1, source_target_pairs={{0,24},{8,0},{16,8},{24,16},{1,25},{9,1},{17,9},{25,17},{2,26},{10... | collective-permute-start | bytes 3145736 | tf_op jit(solution)/shard_map/ppermute | solution.py:35
  60.0 7.2 %collective-permute-start.5 = (bf16[4,64,512]{2,1,0:T(8,128)(2,1)S(1)}, bf16[4,64,512]{2,1,0:T(8,128)(2,1)S(1)}, u32[]{:S(2)}, u32[]{:S(2)}) collective-permute-start(bf16[4,64,512]{2,1,0:T(8,128)(2,1)S(1)} %get-tuple-element.42), channel_id=1, source_target_pairs={{0,1},{1,0},{2,3},{3,2},{4,5},{5,4},{6,7},{7,6},{8,9},{9,8},{10,11... | collective-permute-start | bytes 786440 | tf_op jit(solution)/shard_map/ppermute | solution.py:35
  61.5 5.5 %collective-permute-start.6 = (bf16[1,64,512]{2,1,0:T(8,128)(2,1)S(1)}, bf16[1,64,512]{2,1,0:T(8,128)(2,1)S(1)}, u32[]{:S(2)}, u32[]{:S(2)}) collective-permute-start(bf16[1,64,512]{2,1,0:T(8,128)(2,1)S(1)} %get-tuple-element.44), channel_id=1, source_target_pairs={{0,4},{1,5},{2,6},{3,7},{4,0},{5,1},{6,2},{7,3},{8,12},{9,13},{10,... | collective-permute-start | bytes 196616 | tf_op jit(solution)/shard_map/ppermute | solution.py:40
  71.6 7.5 %collective-permute-start.9 = (bf16[4,64,384]{2,1,0:T(8,128)(2,1)S(1)}, bf16[4,64,384]{2,1,0:T(8,128)(2,1)S(1)}, u32[]{:S(2)}, u32[]{:S(2)}) collective-permute-start(bf16[4,64,384]{2,1,0:T(8,128)(2,1)S(1)} %get-tuple-element.50), channel_id=1, source_target_pairs={{0,1},{1,0},{2,3},{3,2},{4,5},{5,4},{6,7},{7,6},{8,9},{9,8},{10,11... | collective-permute-start | bytes 589832 | tf_op jit(solution)/shard_map/ppermute | solution.py:35
  73.2 8.2 %collective-permute-start.8 = (bf16[2,64,512]{2,1,0:T(8,128)(2,1)S(1)}, bf16[2,64,512]{2,1,0:T(8,128)(2,1)S(1)}, u32[]{:S(2)}, u32[]{:S(2)}) collective-permute-start(bf16[2,64,512]{2,1,0:T(8,128)(2,1)S(1)} %get-tuple-element.48), channel_id=1, source_target_pairs={{0,2},{1,3},{2,0},{3,1},{4,6},{5,7},{6,4},{7,5},{8,10},{9,11},{10,... | collective-permute-start | bytes 393224 | tf_op jit(solution)/shard_map/ppermute | solution.py:40
  79.7 4.7 %collective-permute-start.10 = (bf16[2,64,384]{2,1,0:T(8,128)(2,1)S(1)}, bf16[2,64,384]{2,1,0:T(8,128)(2,1)S(1)}, u32[]{:S(2)}, u32[]{:S(2)}) collective-permute-start(bf16[2,64,384]{2,1,0:T(8,128)(2,1)S(1)} %get-tuple-element.52), channel_id=1, source_target_pairs={{0,2},{1,3},{2,0},{3,1},{4,6},{5,7},{6,4},{7,5},{8,10},{9,11},{10,... | collective-permute-start | bytes 294920 | tf_op jit(solution)/shard_map/ppermute | solution.py:40
  86.9 9.9 %collective-permute-start.13 = (bf16[4,64,384]{2,1,0:T(8,128)(2,1)S(1)}, bf16[4,64,384]{2,1,0:T(8,128)(2,1)S(1)}, u32[]{:S(2)}, u32[]{:S(2)}) collective-permute-start(bf16[4,64,384]{2,1,0:T(8,128)(2,1)S(1)} %get-tuple-element.57), channel_id=1, source_target_pairs={{0,1},{1,0},{2,3},{3,2},{4,5},{5,4},{6,7},{7,6},{8,9},{9,8},{10,11... | collective-permute-start | bytes 589832 | tf_op jit(solution)/shard_map/ppermute | solution.py:35
  88.4 8.3 %collective-permute-start.11 = (bf16[1,64,896]{2,1,0:T(8,128)(2,1)S(1)}, bf16[1,64,896]{2,1,0:T(8,128)(2,1)S(1)}, u32[]{:S(2)}, u32[]{:S(2)}) collective-permute-start(bf16[1,64,896]{2,1,0:T(8,128)(2,1)S(1)} %get-tuple-element.54), channel_id=1, source_target_pairs={{0,4},{1,5},{2,6},{3,7},{4,0},{5,1},{6,2},{7,3},{8,12},{9,13},{10,... | collective-permute-start | bytes 344072 | tf_op jit(solution)/shard_map/ppermute | solution.py:40
  98.5 5.2 %collective-permute-start.14 = (bf16[4,64,256]{2,1,0:T(8,128)(2,1)S(1)}, bf16[4,64,256]{2,1,0:T(8,128)(2,1)S(1)}, u32[]{:S(2)}, u32[]{:S(2)}) collective-permute-start(bf16[4,64,256]{2,1,0:T(8,128)(2,1)S(1)} %get-tuple-element.60), channel_id=1, source_target_pairs={{0,1},{1,0},{2,3},{3,2},{4,5},{5,4},{6,7},{7,6},{8,9},{9,8},{10,11... | collective-permute-start | bytes 393224 | tf_op jit(solution)/shard_map/ppermute | solution.py:35
  99.1 4.6 %collective-permute-start.15 = (bf16[2,64,384]{2,1,0:T(8,128)(2,1)S(1)}, bf16[2,64,384]{2,1,0:T(8,128)(2,1)S(1)}, u32[]{:S(2)}, u32[]{:S(2)}) collective-permute-start(bf16[2,64,384]{2,1,0:T(8,128)(2,1)S(1)} %get-tuple-element.62), channel_id=1, source_target_pairs={{0,2},{1,3},{2,0},{3,1},{4,6},{5,7},{6,4},{7,5},{8,10},{9,11},{10,... | collective-permute-start | bytes 294920 | tf_op jit(solution)/shard_map/ppermute | solution.py:40
  104.3 8.3 %collective-permute-start.16 = (bf16[1,64,640]{2,1,0:T(8,128)(2,1)S(1)}, bf16[1,64,640]{2,1,0:T(8,128)(2,1)S(1)}, u32[]{:S(2)}, u32[]{:S(2)}) collective-permute-start(bf16[1,64,640]{2,1,0:T(8,128)(2,1)S(1)} %get-tuple-element.64), channel_id=1, source_target_pairs={{0,4},{1,5},{2,6},{3,7},{4,0},{5,1},{6,2},{7,3},{8,12},{9,13},{10,... | collective-permute-start | bytes 245768 | tf_op jit(solution)/shard_map/ppermute | solution.py:40
  106.8 5.7 %collective-permute-start.17 = (bf16[1,64,256]{2,1,0:T(8,128)(2,1)S(1)}, bf16[1,64,256]{2,1,0:T(8,128)(2,1)S(1)}, u32[]{:S(2)}, u32[]{:S(2)}) collective-permute-start(bf16[1,64,256]{2,1,0:T(8,128)(2,1)S(1)} %get-tuple-element.66), channel_id=1, source_target_pairs={{0,6},{1,7},{2,4},{3,5},{4,2},{5,3},{6,0},{7,1},{8,14},{9,15},{10,... | collective-permute-start | bytes 98312 | tf_op jit(solution)/shard_map/ppermute | solution.py:40
  108.2 4.4 %collective-permute-start.18 = (bf16[1,64,256]{2,1,0:T(8,128)(2,1)S(1)}, bf16[1,64,256]{2,1,0:T(8,128)(2,1)S(1)}, u32[]{:S(2)}, u32[]{:S(2)}) collective-permute-start(bf16[1,64,256]{2,1,0:T(8,128)(2,1)S(1)} %get-tuple-element.67), channel_id=1, source_target_pairs={{0,2},{1,3},{2,0},{3,1},{4,6},{5,7},{6,4},{7,5},{8,10},{9,11},{10,... | collective-permute-start | bytes 98312 | tf_op jit(solution)/shard_map/ppermute | solution.py:40

commit v26 on v25

--- a/solution.py
+++ b/solution.py
@@ -185,17 +185,25 @@
     if plan.adding:
         sum_buf, placed_sem = take(2)
         add_slot, add_start, pieces = plan.adding
+        add_point = table_ref[add_slot * stride].astype(jnp.int32)
+        placing = []
+        placed = 0
         for start, span, terms in pieces:
             total = 0.0
             for index, column in terms:
                 total += arrived[index][0, :, column : column + 2 * span].astype(jnp.float32)
             put_sum(sum_buf, start - add_start, total)
-        add_point = table_ref[add_slot * stride].astype(jnp.int32)
-        columns = pl.ds(add_start, sum_buf.shape[2])
-        placing = pltpu.make_async_copy(
-            sum_buf, result_ref.at[:, add_point, :, columns], placed_sem
-        )
-        placing.start()
+            filled_to = start - add_start + span
+            if filled_to % LANES == 0:
+                columns = pl.ds(add_start + placed, filled_to - placed)
+                copy = pltpu.make_async_copy(
+                    sum_buf.at[:, :, pl.ds(placed, filled_to - placed)],
+                    result_ref.at[:, add_point, :, columns],
+                    placed_sem.at[len(placing)],
+                )
+                copy.start()
+                placing.append(copy)
+                placed = filled_to
     for task, arrays, outputs in zip(plan.tasks, sources, targets):
         groups = [arrays[i : i + task.each] for i in range(0, len(arrays), task.each)]
         bit = lax.rem(lax.div(outer, 1 << task.stage), 2)
@@ -252,7 +260,8 @@
             if way not in plan.ways:
                 copy.wait()
     if plan.adding:
-        placing.wait()
+        for copy in placing:
+            copy.wait()
     if plan.later:
         for store in stores:
             store.wait()
@@ -349,7 +358,8 @@
         out_shape.append(jax.ShapeDtypeStruct(plan.shape, jnp.float32))
         out_specs.append(hbm)
         lanes = sum(span for _, span, _ in plan.adding[2])
-        scratch += [pltpu.VMEM((rows, 2, lanes), jnp.float32), pltpu.SemaphoreType.DMA]
+        stores = pltpu.SemaphoreType.DMA((len(plan.adding[2]),))
+        scratch += [pltpu.VMEM((rows, 2, lanes), jnp.float32), stores]
     if plan.later:
         out_shape.append(jax.ShapeDtypeStruct((2, plan.later[2], points), bands.dtype))
         out_specs.append(hbm)

time: 114 us -> 114 us (level)
  no operation moved by 1% of the time
where the time goes in v26:
time: 114 us
  waiting for transfers between devices  45.2 us (40%)
  Pallas kernels  38.8 us (34%)
  starting transfers between devices  29.3 us (26%)
    ppermute x10, waiting for transfers between devices, shifted(): return lax.ppermute(block, axis, route)  33.9 us
    pallas_call x12, Pallas kernels, step(): pl.pallas_call(functools.partial(step_kernel, plan), in_specs=in_specs, o...  32.3 us
    ppermute x9, starting transfers between devices, swapped(): return lax.ppermute(block, axis, [(i, i ^ distance) for i in range(count)])  15.2 us
    ppermute x10, starting transfers between devices, shifted(): return lax.ppermute(block, axis, route)  14 us
    ppermute x9, waiting for transfers between devices, swapped(): return lax.ppermute(block, axis, [(i, i ^ distance) for i in range(count)])  11.3 us
    pallas_call x3, Pallas kernels, piece_of(): pl.pallas_call(functools.partial(piece_kernel if after else first_kernel,...  6.46 us
  transfers between devices with their start and end apart: 19, of which 12 were waited for; matrix products, arithmetic and copies ran while one was open for 1% of the time, Pallas kernels for 29%

profile of v26, /device:TPU:0, one launch (start us, length us, event | category | flops | bytes accessed | tf_op | source)
XLA Modules:
  0.0 114.2 jit_solution(5552558918341974422)
XLA Ops:
  0.0 1.6 %piece_of.3.rest_0_ = bf16[2,256,2048]{2,1,0:T(8,128)(2,1)S(1)} custom-call(bf16[2,2,512,2048]{3,2,1,0:T(8,128)(2,1)} %refs_0_.5), custom_call_target="tpu_custom_call" | custom-call | flops 1000 | bytes 1000 | tf_op jit(solution)/shard_map/piece_of/pallas_call | solution.py:82
  1.6 2.5 %collective-permute-start.2 = (bf16[2,256,2048]{2,1,0:T(8,128)(2,1)S(1)}, bf16[2,256,2048]{2,1,0:T(8,128)(2,1)}, u32[]{:S(2)}, u32[]{:S(2)}) collective-permute-start(bf16[2,256,2048]{2,1,0:T(8,128)(2,1)S(1)} %piece_of.3.rest_0_), channel_id=1, source_target_pairs={{0,24},{8,0},{16,8},{24,16},{1,25},{9,1},{17,9},{25,17},{2,26},{10... | collective-permute-start | bytes 6291464 | tf_op jit(solution)/shard_map/ppermute | solution.py:35
  4.0 2.6 %piece_of.4.rest_0_ = bf16[2,256,2048]{2,1,0:T(8,128)(2,1)} custom-call(bf16[2,2,512,2048]{3,2,1,0:T(8,128)(2,1)} %refs_0_.5, bf16[2,256,2048]{2,1,0:T(8,128)(2,1)S(1)} %piece_of.3.rest_0_), custom_call_target="tpu_custom_call" | custom-call | flops 1000 | bytes 1000 | tf_op jit(solution)/shard_map/piece_of/pallas_call | solution.py:82
  6.6 0.7 collective-permute-start.1
  7.4 2.3 %piece_of.5 = bf16[2,192,2048]{2,1,0:T(8,128)(2,1)} custom-call(bf16[2,2,512,2048]{3,2,1,0:T(8,128)(2,1)} %refs_0_.5, bf16[2,256,2048]{2,1,0:T(8,128)(2,1)} %piece_of.4.rest_0_), custom_call_target="tpu_custom_call" | custom-call | flops 1000 | bytes 1000 | tf_op jit(solution)/shard_map/piece_of/pallas_call | solution.py:82
  9.8 0.1 select_reduce_fusion.1
  9.9 0.1 fusion.4
  10.1 0.1 copy.6
  10.4 17.2 %collective-permute-done.2.refs_1_ = bf16[2,256,2048]{2,1,0:T(8,128)(2,1)} collective-permute-done((bf16[2,256,2048]{2,1,0:T(8,128)(2,1)S(1)}, bf16[2,256,2048]{2,1,0:T(8,128)(2,1)}, u32[]{:S(2)}, u32[]{:S(2)}) %collective-permute-start.2) | collective-permute-done | bytes 2097184 | tf_op jit(solution)/shard_map/ppermute | solution.py:35
  27.6 7.7 %step.12 = (f32[4,64,512]{2,1,0:T(8,128)S(1)}, bf16[4,64,512]{2,1,0:T(8,128)(2,1)S(1)}, bf16[2,192,2048]{2,1,0:T(8,128)(2,1)S(1)}) custom-call(f32[11]{0:T(128)S(1)} %pad_maximum_fusion.1.table_ref, bf16[2,2,512,2048]{3,2,1,0:T(8,128)(2,1)} %refs_0_.5, bf16[2,256,2048]{2,1,0:T(8,128)(2,1)} %collective-permute-done.2.refs_1_), custom_call_target="tpu_custom_call" | custom-call | flops 1000 | bytes 1000 | tf_op jit(solution)/shard_map/step/pallas_call | solution.py:369
  35.3 2.1 %collective-permute-start.7 = (bf16[2,192,2048]{2,1,0:T(8,128)(2,1)S(1)}, bf16[2,192,2048]{2,1,0:T(8,128)(2,1)S(1)}, u32[]{:S(2)}, u32[]{:S(2)}) collective-permute-start(bf16[2,192,2048]{2,1,0:T(8,128)(2,1)S(1)} %get-tuple-element.46), channel_id=1, source_target_pairs={{0,24},{8,0},{16,8},{24,16},{1,25},{9,1},{17,9},{25,17},{2,26},{10... | collective-permute-start | bytes 4718600 | tf_op jit(solution)/shard_map/ppermute | solution.py:35
  37.4 1.5 %collective-permute-start.3 = (bf16[4,64,512]{2,1,0:T(8,128)(2,1)S(1)}, bf16[4,64,512]{2,1,0:T(8,128)(2,1)S(1)}, u32[]{:S(2)}, u32[]{:S(2)}) collective-permute-start(bf16[4,64,512]{2,1,0:T(8,128)(2,1)S(1)} %get-tuple-element.38), channel_id=1, source_target_pairs={{0,1},{1,0},{2,3},{3,2},{4,5},{5,4},{6,7},{7,6},{8,9},{9,8},{10,11... | collective-permute-start | bytes 786440 | tf_op jit(solution)/shard_map/ppermute | solution.py:35
  38.9 5.7 %collective-permute-done.3.refs_1_ = bf16[4,64,512]{2,1,0:T(8,128)(2,1)S(1)} collective-permute-done((bf16[4,64,512]{2,1,0:T(8,128)(2,1)S(1)}, bf16[4,64,512]{2,1,0:T(8,128)(2,1)S(1)}, u32[]{:S(2)}, u32[]{:S(2)}) %collective-permute-start.3) | collective-permute-done | bytes 262176 | tf_op jit(solution)/shard_map/ppermute | solution.py:35
  44.6 0.6 step.13
  45.2 1.6 %collective-permute-start.4 = (bf16[2,64,512]{2,1,0:T(8,128)(2,1)S(1)}, bf16[2,64,512]{2,1,0:T(8,128)(2,1)S(1)}, u32[]{:S(2)}, u32[]{:S(2)}) collective-permute-start(bf16[2,64,512]{2,1,0:T(8,128)(2,1)S(1)} %get-tuple-element.40), channel_id=1, source_target_pairs={{0,2},{1,3},{2,0},{3,1},{4,6},{5,7},{6,4},{7,5},{8,10},{9,11},{10,... | collective-permute-start | bytes 393224 | tf_op jit(solution)/shard_map/ppermute | solution.py:40
  46.9 3.3 %collective-permute-done.1.refs_1_ = bf16[2,256,2048]{2,1,0:T(8,128)(2,1)} collective-permute-done((bf16[2,256,2048]{2,1,0:T(8,128)(2,1)}, bf16[2,256,2048]{2,1,0:T(8,128)(2,1)}, u32[]{:S(2)}, u32[]{:S(2)}) %collective-permute-start.1) | collective-permute-done | bytes 2097184 | tf_op jit(solution)/shard_map/ppermute | solution.py:35
  50.2 0.1 collective-permute-done.4.refs_3_
  50.2 7.7 %step.14 = (f32[4,64,512]{2,1,0:T(8,128)S(1)}, bf16[4,64,512]{2,1,0:T(8,128)(2,1)S(1)}, f32[1,64,512]{2,1,0:T(8,128)S(1)}, bf16[1,64,512]{2,1,0:T(8,128)(2,1)S(1)}, bf16[2,128,2048]{2,1,0:T(8,128)(2,1)S(1)}) custom-call(f32[11]{0:T(128)S(1)} %pad_maximum_fusion.1.table_ref, bf16[2,2,512,2048]{3,2,1,0:T(8,128)(2,1)} %refs_0_.5, ...), custom_call_target="tpu_custom_call" | custom-call | flops 1000 | bytes 1000 | tf_op jit(solution)/shard_map/step/pallas_call | solution.py:369
  58.0 2.0 %collective-permute-start.12 = (bf16[2,128,2048]{2,1,0:T(8,128)(2,1)S(1)}, bf16[2,128,2048]{2,1,0:T(8,128)(2,1)S(1)}, u32[]{:S(2)}, u32[]{:S(2)}) collective-permute-start(bf16[2,128,2048]{2,1,0:T(8,128)(2,1)S(1)} %get-tuple-element.55), channel_id=1, source_target_pairs={{0,24},{8,0},{16,8},{24,16},{1,25},{9,1},{17,9},{25,17},{2,26},{10... | collective-permute-start | bytes 3145736 | tf_op jit(solution)/shard_map/ppermute | solution.py:35
  60.0 1.5 %collective-permute-start.5 = (bf16[4,64,512]{2,1,0:T(8,128)(2,1)S(1)}, bf16[4,64,512]{2,1,0:T(8,128)(2,1)S(1)}, u32[]{:S(2)}, u32[]{:S(2)}) collective-permute-start(bf16[4,64,512]{2,1,0:T(8,128)(2,1)S(1)} %get-tuple-element.42), channel_id=1, source_target_pairs={{0,1},{1,0},{2,3},{3,2},{4,5},{5,4},{6,7},{7,6},{8,9},{9,8},{10,11... | collective-permute-start | bytes 786440 | tf_op jit(solution)/shard_map/ppermute | solution.py:35
  61.5 2.6 %collective-permute-start.6 = (bf16[1,64,512]{2,1,0:T(8,128)(2,1)S(1)}, bf16[1,64,512]{2,1,0:T(8,128)(2,1)S(1)}, u32[]{:S(2)}, u32[]{:S(2)}) collective-permute-start(bf16[1,64,512]{2,1,0:T(8,128)(2,1)S(1)} %get-tuple-element.44), channel_id=1, source_target_pairs={{0,4},{1,5},{2,6},{3,7},{4,0},{5,1},{6,2},{7,3},{8,12},{9,13},{10,... | collective-permute-start | bytes 196616 | tf_op jit(solution)/shard_map/ppermute | solution.py:40
  64.1 2.9 %collective-permute-done.refs_1_ = bf16[2,192,2048]{2,1,0:T(8,128)(2,1)} collective-permute-done((bf16[2,192,2048]{2,1,0:T(8,128)(2,1)}, bf16[2,192,2048]{2,1,0:T(8,128)(2,1)}, u32[]{:S(2)}, u32[]{:S(2)}) %collective-permute-start) | collective-permute-done | bytes 1572896 | tf_op jit(solution)/shard_map/ppermute | solution.py:35
  67.0 0.2 collective-permute-done.5.refs_3_
  67.2 4.4 %step.15 = (bf16[384,2048]{1,0:T(8,128)(2,1)S(1)}, bf16[2,2,256,2048]{3,2,1,0:T(8,128)(2,1)S(1)}, bf16[4,64,384]{2,1,0:T(8,128)(2,1)S(1)}, f32[2,64,512]{2,1,0:T...) custom-call(f32[11]{0:T(128)S(1)} %pad_maximum_fusion.1.table_ref, ...), custom_call_target="tpu_custom_call" | custom-call | flops 1000 | bytes 1000 | tf_op jit(solution)/shard_map/step/pallas_call | solution.py:369
  71.6 1.6 %collective-permute-start.9 = (bf16[4,64,384]{2,1,0:T(8,128)(2,1)S(1)}, bf16[4,64,384]{2,1,0:T(8,128)(2,1)S(1)}, u32[]{:S(2)}, u32[]{:S(2)}) collective-permute-start(bf16[4,64,384]{2,1,0:T(8,128)(2,1)S(1)} %get-tuple-element.50), channel_id=1, source_target_pairs={{0,1},{1,0},{2,3},{3,2},{4,5},{5,4},{6,7},{7,6},{8,9},{9,8},{10,11... | collective-permute-start | bytes 589832 | tf_op jit(solution)/shard_map/ppermute | solution.py:35
  73.2 1.6 %collective-permute-start.8 = (bf16[2,64,512]{2,1,0:T(8,128)(2,1)S(1)}, bf16[2,64,512]{2,1,0:T(8,128)(2,1)S(1)}, u32[]{:S(2)}, u32[]{:S(2)}) collective-permute-start(bf16[2,64,512]{2,1,0:T(8,128)(2,1)S(1)} %get-tuple-element.48), channel_id=1, source_target_pairs={{0,2},{1,3},{2,0},{3,1},{4,6},{5,7},{6,4},{7,5},{8,10},{9,11},{10,... | collective-permute-start | bytes 393224 | tf_op jit(solution)/shard_map/ppermute | solution.py:40
  74.8 1.9 %step.16.refs_0_ = f32[4,64,384]{2,1,0:T(8,128)S(1)} custom-call(f32[11]{0:T(128)S(1)} %pad_maximum_fusion.1.table_ref, bf16[2,2,256,2048]{3,2,1,0:T(8,128)(2,1)S(1)} %get-tuple-element.45.refs_0_, bf16[384,2048]{1,0:T(8,128)(2,1)S(1)} %get-tuple-element.49.refs_1_), custom_call_target="tpu_custom_call" | custom-call | flops 1000 | bytes 1000 | tf_op jit(solution)/shard_map/step/pallas_call | solution.py:369
  76.7 2.5 %collective-permute-done.9.refs_1_ = bf16[4,64,384]{2,1,0:T(8,128)(2,1)S(1)} collective-permute-done((bf16[4,64,384]{2,1,0:T(8,128)(2,1)S(1)}, bf16[4,64,384]{2,1,0:T(8,128)(2,1)S(1)}, u32[]{:S(2)}, u32[]{:S(2)}) %collective-permute-start.9) | collective-permute-done | bytes 196640 | tf_op jit(solution)/shard_map/ppermute | solution.py:35
  79.1 0.6 step.17
  79.7 1.6 %collective-permute-start.10 = (bf16[2,64,384]{2,1,0:T(8,128)(2,1)S(1)}, bf16[2,64,384]{2,1,0:T(8,128)(2,1)S(1)}, u32[]{:S(2)}, u32[]{:S(2)}) collective-permute-start(bf16[2,64,384]{2,1,0:T(8,128)(2,1)S(1)} %get-tuple-element.52), channel_id=1, source_target_pairs={{0,2},{1,3},{2,0},{3,1},{4,6},{5,7},{6,4},{7,5},{8,10},{9,11},{10,... | collective-permute-start | bytes 294920 | tf_op jit(solution)/shard_map/ppermute | solution.py:40
  81.4 3.0 %collective-permute-done.10.refs_5_ = bf16[2,64,384]{2,1,0:T(8,128)(2,1)S(1)} collective-permute-done((bf16[2,64,384]{2,1,0:T(8,128)(2,1)S(1)}, bf16[2,64,384]{2,1,0:T(8,128)(2,1)S(1)}, u32[]{:S(2)}, u32[]{:S(2)}) %collective-permute-start.10) | collective-permute-done | bytes 98336 | tf_op jit(solution)/shard_map/ppermute | solution.py:40
  84.4 2.4 %step.18 = (bf16[384,2048]{1,0:T(8,128)(2,1)S(1)}, bf16[4,64,384]{2,1,0:T(8,128)(2,1)S(1)}, f32[1,64,896]{2,1,0:T(8,128)S(1)}, bf16[1,64,896]{2,1,0:T(8,128)(2,1)S(1)}) custom-call(f32[11]{0:T(128)S(1)} %pad_maximum_fusion.1.table_ref, bf16[2,2,256,2048]{3,2,1,0:T(8,128)(2,1)S(1)} %get-tuple-element.45.refs_0_, ...), custom_call_target="tpu_custom_call" | custom-call | flops 1000 | bytes 1000 | tf_op jit(solution)/shard_map/step/pallas_call | solution.py:369
  86.9 1.6 %collective-permute-start.13 = (bf16[4,64,384]{2,1,0:T(8,128)(2,1)S(1)}, bf16[4,64,384]{2,1,0:T(8,128)(2,1)S(1)}, u32[]{:S(2)}, u32[]{:S(2)}) collective-permute-start(bf16[4,64,384]{2,1,0:T(8,128)(2,1)S(1)} %get-tuple-element.57), channel_id=1, source_target_pairs={{0,1},{1,0},{2,3},{3,2},{4,5},{5,4},{6,7},{7,6},{8,9},{9,8},{10,11... | collective-permute-start | bytes 589832 | tf_op jit(solution)/shard_map/ppermute | solution.py:35
  88.4 2.6 %collective-permute-start.11 = (bf16[1,64,896]{2,1,0:T(8,128)(2,1)S(1)}, bf16[1,64,896]{2,1,0:T(8,128)(2,1)S(1)}, u32[]{:S(2)}, u32[]{:S(2)}) collective-permute-start(bf16[1,64,896]{2,1,0:T(8,128)(2,1)S(1)} %get-tuple-element.54), channel_id=1, source_target_pairs={{0,4},{1,5},{2,6},{3,7},{4,0},{5,1},{6,2},{7,3},{8,12},{9,13},{10,... | collective-permute-start | bytes 344072 | tf_op jit(solution)/shard_map/ppermute | solution.py:40
  91.0 1.9 %step.19.refs_2_ = f32[4,64,384]{2,1,0:T(8,128)S(1)} custom-call(f32[11]{0:T(128)S(1)} %pad_maximum_fusion.1.table_ref, bf16[2,2,256,2048]{3,2,1,0:T(8,128)(2,1)S(1)} %get-tuple-element.45.refs_0_, bf16[384,2048]{1,0:T(8,128)(2,1)S(1)} %get-tuple-element.56.refs_1_), custom_call_target="tpu_custom_call" | custom-call | flops 1000 | bytes 1000 | tf_op jit(solution)/shard_map/step/pallas_call | solution.py:369
  92.9 2.1 %collective-permute-done.12.refs_1_ = bf16[2,128,2048]{2,1,0:T(8,128)(2,1)S(1)} collective-permute-done((bf16[2,128,2048]{2,1,0:T(8,128)(2,1)S(1)}, bf16[2,128,2048]{2,1,0:T(8,128)(2,1)S(1)}, u32[]{:S(2)}, u32[]{:S(2)}) %collective-permute-start.12) | collective-permute-done | bytes 1048608 | tf_op jit(solution)/shard_map/ppermute | solution.py:35
  95.0 1.7 %collective-permute-done.11.refs_5_.refs_1_ = bf16[1,64,896]{2,1,0:T(8,128)(2,1)S(1)} collective-permute-done((bf16[1,64,896]{2,1,0:T(8,128)(2,1)S(1)}, bf16[1,64,896]{2,1,0:T(8,128)(2,1)S(1)}, u32[]{:S(2)}, u32[]{:S(2)}) %collective-permute-start.11) | collective-permute-done | bytes 114720 | tf_op jit(solution)/shard_map/ppermute | solution.py:40
  96.7 1.7 %step.20 = (bf16[256,2048]{1,0:T(8,128)(2,1)S(1)}, bf16[4,64,256]{2,1,0:T(8,128)(2,1)S(1)}, f32[2,64,384]{2,1,0:T(8,128)S(1)}, bf16[2,64,384]{2,1,0:T(8,128)(2,1)S(1)}, f32[64,2,2,512]{3,2,1,0:T(2,128)}) custom-call(f32[11]{0:T(128)S(1)} %pad_maximum_fusion.1.table_ref, ...), custom_call_target="tpu_custom_call", output_to_operand_aliasing={{4}: (7, {})} | custom-call | flops 1000 | bytes 1000 | tf_op jit(solution)/shard_map/step/pallas_call | solution.py:369
  98.5 0.6 collective-permute-start.14
  99.1 0.8 collective-permute-start.15
  99.9 1.3 %step.21.refs_0_ = f32[4,64,256]{2,1,0:T(8,128)S(1)} custom-call(f32[11]{0:T(128)S(1)} %pad_maximum_fusion.1.table_ref, bf16[2,2,256,2048]{3,2,1,0:T(8,128)(2,1)S(1)} %get-tuple-element.45.refs_0_, bf16[256,2048]{1,0:T(8,128)(2,1)S(1)} %get-tuple-element.59.refs_1_), custom_call_target="tpu_custom_call" | custom-call | flops 1000 | bytes 1000 | tf_op jit(solution)/shard_map/step/pallas_call | solution.py:369
  101.2 2.5 %collective-permute-done.15.refs_3_ = bf16[2,64,384]{2,1,0:T(8,128)(2,1)S(1)} collective-permute-done((bf16[2,64,384]{2,1,0:T(8,128)(2,1)S(1)}, bf16[2,64,384]{2,1,0:T(8,128)(2,1)S(1)}, u32[]{:S(2)}, u32[]{:S(2)}) %collective-permute-start.15) | collective-permute-done | bytes 98336 | tf_op jit(solution)/shard_map/ppermute | solution.py:40
  103.7 0.6 step.22
  104.3 2.5 %collective-permute-start.16 = (bf16[1,64,640]{2,1,0:T(8,128)(2,1)S(1)}, bf16[1,64,640]{2,1,0:T(8,128)(2,1)S(1)}, u32[]{:S(2)}, u32[]{:S(2)}) collective-permute-start(bf16[1,64,640]{2,1,0:T(8,128)(2,1)S(1)} %get-tuple-element.64), channel_id=1, source_target_pairs={{0,4},{1,5},{2,6},{3,7},{4,0},{5,1},{6,2},{7,3},{8,12},{9,13},{10,... | collective-permute-start | bytes 245768 | tf_op jit(solution)/shard_map/ppermute | solution.py:40
  106.8 1.4 %collective-permute-start.17 = (bf16[1,64,256]{2,1,0:T(8,128)(2,1)S(1)}, bf16[1,64,256]{2,1,0:T(8,128)(2,1)S(1)}, u32[]{:S(2)}, u32[]{:S(2)}) collective-permute-start(bf16[1,64,256]{2,1,0:T(8,128)(2,1)S(1)} %get-tuple-element.66), channel_id=1, source_target_pairs={{0,6},{1,7},{2,4},{3,5},{4,2},{5,3},{6,0},{7,1},{8,14},{9,15},{10,... | collective-permute-start | bytes 98312 | tf_op jit(solution)/shard_map/ppermute | solution.py:40
  108.2 0.5 collective-permute-start.18
  108.7 3.9 %collective-permute-done.17.refs_5_ = bf16[1,64,256]{2,1,0:T(8,128)(2,1)S(1)} collective-permute-done((bf16[1,64,256]{2,1,0:T(8,128)(2,1)S(1)}, bf16[1,64,256]{2,1,0:T(8,128)(2,1)S(1)}, u32[]{:S(2)}, u32[]{:S(2)}) %collective-permute-start.17) | collective-permute-done | bytes 32800 | tf_op jit(solution)/shard_map/ppermute | solution.py:40
  112.5 1.5 %step.23 = f32[64,2,2,512]{3,2,1,0:T(2,128)} custom-call(f32[11]{0:T(128)S(1)} %pad_maximum_fusion.1.table_ref, f32[1,64,896]{2,1,0:T(8,128)S(1)} %get-tuple-element.53.refs_4_.refs_0_, bf16[1,64,896]{2,1,0:T(8,128)(2,1)S(1)} %collective-permute-done.11.refs_5_.refs_1_, f32[1,64,384]{2,1,0:T(8,128)S(1)} %get-tuple-element.63.refs_2_, ...), custom_call_target="tpu_custom_call", output_to_operand_aliasing={{}: (9, {})} | custom-call | flops 1000 | bytes 1000 | tf_op jit(solution)/shard_map/step/pallas_call | solution.py:369
  (17 shorter events, 0.4 us)
Async XLA Ops:
  1.6 26.0 %collective-permute-start.2 = (bf16[2,256,2048]{2,1,0:T(8,128)(2,1)S(1)}, bf16[2,256,2048]{2,1,0:T(8,128)(2,1)}, u32[]{:S(2)}, u32[]{:S(2)}) collective-permute-start(bf16[2,256,2048]{2,1,0:T(8,128)(2,1)S(1)} %piece_of.3.rest_0_), channel_id=1, source_target_pairs={{0,24},{8,0},{16,8},{24,16},{1,25},{9,1},{17,9},{25,17},{2,26},{10... | collective-permute-start | bytes 6291464 | tf_op jit(solution)/shard_map/ppermute | solution.py:35
  6.6 3.1 %copy-start = (s32[2]{0:T(128)S(1)}, s32[2]{0:T(128)}, u32[]{:S(2)}) copy-start(s32[2]{0:T(128)} %param.4) | copy-start | bytes 28
  6.6 3.1 %copy-start.1 = (s32[2]{0:T(128)S(1)}, s32[2]{0:T(128)}, u32[]{:S(2)}) copy-start(s32[2]{0:T(128)} %param.5) | copy-start | bytes 28
  6.6 43.5 %collective-permute-start.1 = (bf16[2,256,2048]{2,1,0:T(8,128)(2,1)}, bf16[2,256,2048]{2,1,0:T(8,128)(2,1)}, u32[]{:S(2)}, u32[]{:S(2)}) collective-permute-start(bf16[2,256,2048]{2,1,0:T(8,128)(2,1)} %piece_of.4.rest_0_), channel_id=1, source_target_pairs={{0,24},{8,0},{16,8},{24,16},{1,25},{9,1},{17,9},{25,17},{2,26},{10... | collective-permute-start | bytes 6291464 | tf_op jit(solution)/shard_map/ppermute | solution.py:35
  9.7 57.3 %collective-permute-start = (bf16[2,192,2048]{2,1,0:T(8,128)(2,1)}, bf16[2,192,2048]{2,1,0:T(8,128)(2,1)}, u32[]{:S(2)}, u32[]{:S(2)}) collective-permute-start(bf16[2,192,2048]{2,1,0:T(8,128)(2,1)} %piece_of.5), channel_id=1, source_target_pairs={{0,24},{8,0},{16,8},{24,16},{1,25},{9,1},{17,9},{25,17},{2,26},{10... | collective-permute-start | bytes 4718600 | tf_op jit(solution)/shard_map/ppermute | solution.py:35
  35.3 49.1 %collective-permute-start.7 = (bf16[2,192,2048]{2,1,0:T(8,128)(2,1)S(1)}, bf16[2,192,2048]{2,1,0:T(8,128)(2,1)S(1)}, u32[]{:S(2)}, u32[]{:S(2)}) collective-permute-start(bf16[2,192,2048]{2,1,0:T(8,128)(2,1)S(1)} %get-tuple-element.46), channel_id=1, source_target_pairs={{0,24},{8,0},{16,8},{24,16},{1,25},{9,1},{17,9},{25,17},{2,26},{10... | collective-permute-start | bytes 4718600 | tf_op jit(solution)/shard_map/ppermute | solution.py:35
  37.4 7.2 %collective-permute-start.3 = (bf16[4,64,512]{2,1,0:T(8,128)(2,1)S(1)}, bf16[4,64,512]{2,1,0:T(8,128)(2,1)S(1)}, u32[]{:S(2)}, u32[]{:S(2)}) collective-permute-start(bf16[4,64,512]{2,1,0:T(8,128)(2,1)S(1)} %get-tuple-element.38), channel_id=1, source_target_pairs={{0,1},{1,0},{2,3},{3,2},{4,5},{5,4},{6,7},{7,6},{8,9},{9,8},{10,11... | collective-permute-start | bytes 786440 | tf_op jit(solution)/shard_map/ppermute | solution.py:35
  45.2 5.0 %collective-permute-start.4 = (bf16[2,64,512]{2,1,0:T(8,128)(2,1)S(1)}, bf16[2,64,512]{2,1,0:T(8,128)(2,1)S(1)}, u32[]{:S(2)}, u32[]{:S(2)}) collective-permute-start(bf16[2,64,512]{2,1,0:T(8,128)(2,1)S(1)} %get-tuple-element.40), channel_id=1, source_target_pairs={{0,2},{1,3},{2,0},{3,1},{4,6},{5,7},{6,4},{7,5},{8,10},{9,11},{10,... | collective-permute-start | bytes 393224 | tf_op jit(solution)/shard_map/ppermute | solution.py:40
  58.0 37.0 %collective-permute-start.12 = (bf16[2,128,2048]{2,1,0:T(8,128)(2,1)S(1)}, bf16[2,128,2048]{2,1,0:T(8,128)(2,1)S(1)}, u32[]{:S(2)}, u32[]{:S(2)}) collective-permute-start(bf16[2,128,2048]{2,1,0:T(8,128)(2,1)S(1)} %get-tuple-element.55), channel_id=1, source_target_pairs={{0,24},{8,0},{16,8},{24,16},{1,25},{9,1},{17,9},{25,17},{2,26},{10... | collective-permute-start | bytes 3145736 | tf_op jit(solution)/shard_map/ppermute | solution.py:35
  60.0 7.2 %collective-permute-start.5 = (bf16[4,64,512]{2,1,0:T(8,128)(2,1)S(1)}, bf16[4,64,512]{2,1,0:T(8,128)(2,1)S(1)}, u32[]{:S(2)}, u32[]{:S(2)}) collective-permute-start(bf16[4,64,512]{2,1,0:T(8,128)(2,1)S(1)} %get-tuple-element.42), channel_id=1, source_target_pairs={{0,1},{1,0},{2,3},{3,2},{4,5},{5,4},{6,7},{7,6},{8,9},{9,8},{10,11... | collective-permute-start | bytes 786440 | tf_op jit(solution)/shard_map/ppermute | solution.py:35
  61.5 5.5 %collective-permute-start.6 = (bf16[1,64,512]{2,1,0:T(8,128)(2,1)S(1)}, bf16[1,64,512]{2,1,0:T(8,128)(2,1)S(1)}, u32[]{:S(2)}, u32[]{:S(2)}) collective-permute-start(bf16[1,64,512]{2,1,0:T(8,128)(2,1)S(1)} %get-tuple-element.44), channel_id=1, source_target_pairs={{0,4},{1,5},{2,6},{3,7},{4,0},{5,1},{6,2},{7,3},{8,12},{9,13},{10,... | collective-permute-start | bytes 196616 | tf_op jit(solution)/shard_map/ppermute | solution.py:40
  71.6 7.5 %collective-permute-start.9 = (bf16[4,64,384]{2,1,0:T(8,128)(2,1)S(1)}, bf16[4,64,384]{2,1,0:T(8,128)(2,1)S(1)}, u32[]{:S(2)}, u32[]{:S(2)}) collective-permute-start(bf16[4,64,384]{2,1,0:T(8,128)(2,1)S(1)} %get-tuple-element.50), channel_id=1, source_target_pairs={{0,1},{1,0},{2,3},{3,2},{4,5},{5,4},{6,7},{7,6},{8,9},{9,8},{10,11... | collective-permute-start | bytes 589832 | tf_op jit(solution)/shard_map/ppermute | solution.py:35
  73.2 8.2 %collective-permute-start.8 = (bf16[2,64,512]{2,1,0:T(8,128)(2,1)S(1)}, bf16[2,64,512]{2,1,0:T(8,128)(2,1)S(1)}, u32[]{:S(2)}, u32[]{:S(2)}) collective-permute-start(bf16[2,64,512]{2,1,0:T(8,128)(2,1)S(1)} %get-tuple-element.48), channel_id=1, source_target_pairs={{0,2},{1,3},{2,0},{3,1},{4,6},{5,7},{6,4},{7,5},{8,10},{9,11},{10,... | collective-permute-start | bytes 393224 | tf_op jit(solution)/shard_map/ppermute | solution.py:40
  79.7 4.7 %collective-permute-start.10 = (bf16[2,64,384]{2,1,0:T(8,128)(2,1)S(1)}, bf16[2,64,384]{2,1,0:T(8,128)(2,1)S(1)}, u32[]{:S(2)}, u32[]{:S(2)}) collective-permute-start(bf16[2,64,384]{2,1,0:T(8,128)(2,1)S(1)} %get-tuple-element.52), channel_id=1, source_target_pairs={{0,2},{1,3},{2,0},{3,1},{4,6},{5,7},{6,4},{7,5},{8,10},{9,11},{10,... | collective-permute-start | bytes 294920 | tf_op jit(solution)/shard_map/ppermute | solution.py:40
  86.9 9.9 %collective-permute-start.13 = (bf16[4,64,384]{2,1,0:T(8,128)(2,1)S(1)}, bf16[4,64,384]{2,1,0:T(8,128)(2,1)S(1)}, u32[]{:S(2)}, u32[]{:S(2)}) collective-permute-start(bf16[4,64,384]{2,1,0:T(8,128)(2,1)S(1)} %get-tuple-element.57), channel_id=1, source_target_pairs={{0,1},{1,0},{2,3},{3,2},{4,5},{5,4},{6,7},{7,6},{8,9},{9,8},{10,11... | collective-permute-start | bytes 589832 | tf_op jit(solution)/shard_map/ppermute | solution.py:35
  88.4 8.3 %collective-permute-start.11 = (bf16[1,64,896]{2,1,0:T(8,128)(2,1)S(1)}, bf16[1,64,896]{2,1,0:T(8,128)(2,1)S(1)}, u32[]{:S(2)}, u32[]{:S(2)}) collective-permute-start(bf16[1,64,896]{2,1,0:T(8,128)(2,1)S(1)} %get-tuple-element.54), channel_id=1, source_target_pairs={{0,4},{1,5},{2,6},{3,7},{4,0},{5,1},{6,2},{7,3},{8,12},{9,13},{10,... | collective-permute-start | bytes 344072 | tf_op jit(solution)/shard_map/ppermute | solution.py:40
  98.5 5.2 %collective-permute-start.14 = (bf16[4,64,256]{2,1,0:T(8,128)(2,1)S(1)}, bf16[4,64,256]{2,1,0:T(8,128)(2,1)S(1)}, u32[]{:S(2)}, u32[]{:S(2)}) collective-permute-start(bf16[4,64,256]{2,1,0:T(8,128)(2,1)S(1)} %get-tuple-element.60), channel_id=1, source_target_pairs={{0,1},{1,0},{2,3},{3,2},{4,5},{5,4},{6,7},{7,6},{8,9},{9,8},{10,11... | collective-permute-start | bytes 393224 | tf_op jit(solution)/shard_map/ppermute | solution.py:35
  99.1 4.6 %collective-permute-start.15 = (bf16[2,64,384]{2,1,0:T(8,128)(2,1)S(1)}, bf16[2,64,384]{2,1,0:T(8,128)(2,1)S(1)}, u32[]{:S(2)}, u32[]{:S(2)}) collective-permute-start(bf16[2,64,384]{2,1,0:T(8,128)(2,1)S(1)} %get-tuple-element.62), channel_id=1, source_target_pairs={{0,2},{1,3},{2,0},{3,1},{4,6},{5,7},{6,4},{7,5},{8,10},{9,11},{10,... | collective-permute-start | bytes 294920 | tf_op jit(solution)/shard_map/ppermute | solution.py:40
  104.3 8.3 %collective-permute-start.16 = (bf16[1,64,640]{2,1,0:T(8,128)(2,1)S(1)}, bf16[1,64,640]{2,1,0:T(8,128)(2,1)S(1)}, u32[]{:S(2)}, u32[]{:S(2)}) collective-permute-start(bf16[1,64,640]{2,1,0:T(8,128)(2,1)S(1)} %get-tuple-element.64), channel_id=1, source_target_pairs={{0,4},{1,5},{2,6},{3,7},{4,0},{5,1},{6,2},{7,3},{8,12},{9,13},{10,... | collective-permute-start | bytes 245768 | tf_op jit(solution)/shard_map/ppermute | solution.py:40
  106.8 5.7 %collective-permute-start.17 = (bf16[1,64,256]{2,1,0:T(8,128)(2,1)S(1)}, bf16[1,64,256]{2,1,0:T(8,128)(2,1)S(1)}, u32[]{:S(2)}, u32[]{:S(2)}) collective-permute-start(bf16[1,64,256]{2,1,0:T(8,128)(2,1)S(1)} %get-tuple-element.66), channel_id=1, source_target_pairs={{0,6},{1,7},{2,4},{3,5},{4,2},{5,3},{6,0},{7,1},{8,14},{9,15},{10,... | collective-permute-start | bytes 98312 | tf_op jit(solution)/shard_map/ppermute | solution.py:40
  108.2 4.4 %collective-permute-start.18 = (bf16[1,64,256]{2,1,0:T(8,128)(2,1)S(1)}, bf16[1,64,256]{2,1,0:T(8,128)(2,1)S(1)}, u32[]{:S(2)}, u32[]{:S(2)}) collective-permute-start(bf16[1,64,256]{2,1,0:T(8,128)(2,1)S(1)} %get-tuple-element.67), channel_id=1, source_target_pairs={{0,2},{1,3},{2,0},{3,1},{4,6},{5,7},{6,4},{7,5},{8,10},{9,11},{10,... | collective-permute-start | bytes 98312 | tf_op jit(solution)/shard_map/ppermute | solution.py:40

commit v27 on v21

--- a/solution.py
+++ b/solution.py
@@ -15,7 +15,7 @@
 DEPTH = 512
 AHEAD = 3
 OUTER = 4
-SPLIT = 128
+SPLIT = 0
 JOINT = 2
 LANES = 128
 BLOCK = 256

time: 115 us -> 115 us (level)
  no operation moved by 1% of the time
where the time goes in v27:
time: 115 us; the launch traced here: 114 us
  waiting for transfers between devices  42.3 us (37%)
  Pallas kernels  39.3 us (34%)
  starting transfers between devices  31.7 us (28%)
    ppermute x11, waiting for transfers between devices, shifted(): return lax.ppermute(block, axis, route)  34 us
    pallas_call x13, Pallas kernels, step(): pl.pallas_call(functools.partial(step_kernel, plan), in_specs=in_specs, o...  32.9 us
    ppermute x9, starting transfers between devices, swapped(): return lax.ppermute(block, axis, [(i, i ^ distance) for i in range(count)])  16.1 us
    ppermute x11, starting transfers between devices, shifted(): return lax.ppermute(block, axis, route)  15.6 us
    ppermute x9, waiting for transfers between devices, swapped(): return lax.ppermute(block, axis, [(i, i ^ distance) for i in range(count)])  8.38 us
    pallas_call x3, Pallas kernels, piece_of(): pl.pallas_call(functools.partial(piece_kernel if after else first_kernel,...  6.48 us
  transfers between devices with their start and end apart: 20, of which 15 were waited for; matrix products, arithmetic and copies ran while one was open for 1% of the time, Pallas kernels for 31%

profile of v27, /device:TPU:0, one launch (start us, length us, event | category | flops | bytes accessed | tf_op | source)
XLA Modules:
  0.0 114.3 jit_solution(5218443623144611082)
XLA Ops:
  0.0 1.6 %piece_of.3.rest_0_ = bf16[2,256,2048]{2,1,0:T(8,128)(2,1)S(1)} custom-call(bf16[2,2,512,2048]{3,2,1,0:T(8,128)(2,1)} %bands_ref.5), custom_call_target="tpu_custom_call" | custom-call | flops 1000 | bytes 1000 | tf_op jit(solution)/shard_map/piece_of/pallas_call | solution.py:82
  1.6 2.5 %collective-permute-start.1 = (bf16[2,256,2048]{2,1,0:T(8,128)(2,1)S(1)}, bf16[2,256,2048]{2,1,0:T(8,128)(2,1)}, u32[]{:S(2)}, u32[]{:S(2)}) collective-permute-start(bf16[2,256,2048]{2,1,0:T(8,128)(2,1)S(1)} %piece_of.3.rest_0_), channel_id=1, source_target_pairs={{0,24},{8,0},{16,8},{24,16},{1,25},{9,1},{17,9},{25,17},{2,26},{10... | collective-permute-start | bytes 6291464 | tf_op jit(solution)/shard_map/ppermute | solution.py:35
  4.0 2.6 %piece_of.4.rest_0_ = bf16[2,256,2048]{2,1,0:T(8,128)(2,1)} custom-call(bf16[2,2,512,2048]{3,2,1,0:T(8,128)(2,1)} %bands_ref.5, bf16[2,256,2048]{2,1,0:T(8,128)(2,1)S(1)} %piece_of.3.rest_0_), custom_call_target="tpu_custom_call" | custom-call | flops 1000 | bytes 1000 | tf_op jit(solution)/shard_map/piece_of/pallas_call | solution.py:82
  6.7 0.7 collective-permute-start
  7.4 2.3 %piece_of.5 = bf16[2,192,2048]{2,1,0:T(8,128)(2,1)} custom-call(bf16[2,2,512,2048]{3,2,1,0:T(8,128)(2,1)} %bands_ref.5, bf16[2,256,2048]{2,1,0:T(8,128)(2,1)} %piece_of.4.rest_0_), custom_call_target="tpu_custom_call" | custom-call | flops 1000 | bytes 1000 | tf_op jit(solution)/shard_map/piece_of/pallas_call | solution.py:82
  10.4 17.1 %collective-permute-done.1.refs_1_ = bf16[2,256,2048]{2,1,0:T(8,128)(2,1)} collective-permute-done((bf16[2,256,2048]{2,1,0:T(8,128)(2,1)S(1)}, bf16[2,256,2048]{2,1,0:T(8,128)(2,1)}, u32[]{:S(2)}, u32[]{:S(2)}) %collective-permute-start.1) | collective-permute-done | bytes 2097184 | tf_op jit(solution)/shard_map/ppermute | solution.py:35
  27.6 7.7 %step.13 = (f32[4,64,512]{2,1,0:T(8,128)S(1)}, bf16[4,64,512]{2,1,0:T(8,128)(2,1)S(1)}, bf16[2,192,2048]{2,1,0:T(8,128)(2,1)S(1)}) custom-call(f32[11]{0:T(128)S(1)} %pad_maximum_fusion.1.table_ref, bf16[2,2,512,2048]{3,2,1,0:T(8,128)(2,1)} %bands_ref.5, bf16[2,256,2048]{2,1,0:T(8,128)(2,1)} %collective-permute-done.1.refs_1_), custom_call_target="tpu_custom_call" | custom-call | flops 1000 | bytes 1000 | tf_op jit(solution)/shard_map/step/pallas_call | solution.py:386
  35.3 2.1 %collective-permute-start.4 = (bf16[2,192,2048]{2,1,0:T(8,128)(2,1)S(1)}, bf16[2,192,2048]{2,1,0:T(8,128)(2,1)S(1)}, u32[]{:S(2)}, u32[]{:S(2)}) collective-permute-start(bf16[2,192,2048]{2,1,0:T(8,128)(2,1)S(1)} %get-tuple-element.43), channel_id=1, source_target_pairs={{0,24},{8,0},{16,8},{24,16},{1,25},{9,1},{17,9},{25,17},{2,26},{10... | collective-permute-start | bytes 4718600 | tf_op jit(solution)/shard_map/ppermute | solution.py:35
  37.4 1.5 %collective-permute-start.2 = (bf16[4,64,512]{2,1,0:T(8,128)(2,1)S(1)}, bf16[4,64,512]{2,1,0:T(8,128)(2,1)S(1)}, u32[]{:S(2)}, u32[]{:S(2)}) collective-permute-start(bf16[4,64,512]{2,1,0:T(8,128)(2,1)S(1)} %get-tuple-element.39), channel_id=1, source_target_pairs={{0,1},{1,0},{2,3},{3,2},{4,5},{5,4},{6,7},{7,6},{8,9},{9,8},{10,11... | collective-permute-start | bytes 786440 | tf_op jit(solution)/shard_map/ppermute | solution.py:35
  38.9 5.7 %collective-permute-done.2.refs_1_ = bf16[4,64,512]{2,1,0:T(8,128)(2,1)S(1)} collective-permute-done((bf16[4,64,512]{2,1,0:T(8,128)(2,1)S(1)}, bf16[4,64,512]{2,1,0:T(8,128)(2,1)S(1)}, u32[]{:S(2)}, u32[]{:S(2)}) %collective-permute-start.2) | collective-permute-done | bytes 262176 | tf_op jit(solution)/shard_map/ppermute | solution.py:35
  44.6 0.6 step.14
  45.2 1.6 %collective-permute-start.3 = (bf16[2,64,512]{2,1,0:T(8,128)(2,1)S(1)}, bf16[2,64,512]{2,1,0:T(8,128)(2,1)S(1)}, u32[]{:S(2)}, u32[]{:S(2)}) collective-permute-start(bf16[2,64,512]{2,1,0:T(8,128)(2,1)S(1)} %get-tuple-element.41), channel_id=1, source_target_pairs={{0,2},{1,3},{2,0},{3,1},{4,6},{5,7},{6,4},{7,5},{8,10},{9,11},{10,... | collective-permute-start | bytes 393224 | tf_op jit(solution)/shard_map/ppermute | solution.py:40
  46.9 3.3 %collective-permute-done.refs_1_ = bf16[2,256,2048]{2,1,0:T(8,128)(2,1)} collective-permute-done((bf16[2,256,2048]{2,1,0:T(8,128)(2,1)}, bf16[2,256,2048]{2,1,0:T(8,128)(2,1)}, u32[]{:S(2)}, u32[]{:S(2)}) %collective-permute-start) | collective-permute-done | bytes 2097184 | tf_op jit(solution)/shard_map/ppermute | solution.py:35
  50.2 8.7 %step.15 = (bf16[2,2,256,2048]{3,2,1,0:T(8,128)(2,1)S(1)}, f32[4,64,512]{2,1,0:T(8,128)S(1)}, bf16[4,64,512]{2,1,0:T(8,128)(2,1)S(1)}, f32[1,64,512]{2,1,0:T(8,1...) custom-call(f32[11]{0:T(128)S(1)} %pad_maximum_fusion.1.table_ref, ...), custom_call_target="tpu_custom_call" | custom-call | flops 1000 | bytes 1000 | tf_op jit(solution)/shard_map/step/pallas_call | solution.py:386
  59.0 2.1 %collective-permute-start.12 = (bf16[2,128,2048]{2,1,0:T(8,128)(2,1)S(1)}, bf16[2,128,2048]{2,1,0:T(8,128)(2,1)S(1)}, u32[]{:S(2)}, u32[]{:S(2)}) collective-permute-start(bf16[2,128,2048]{2,1,0:T(8,128)(2,1)S(1)} %get-tuple-element.56), channel_id=1, source_target_pairs={{0,24},{8,0},{16,8},{24,16},{1,25},{9,1},{17,9},{25,17},{2,26},{10... | collective-permute-start | bytes 3145736 | tf_op jit(solution)/shard_map/ppermute | solution.py:35
  61.1 1.5 %collective-permute-start.6 = (bf16[4,64,512]{2,1,0:T(8,128)(2,1)S(1)}, bf16[4,64,512]{2,1,0:T(8,128)(2,1)S(1)}, u32[]{:S(2)}, u32[]{:S(2)}) collective-permute-start(bf16[4,64,512]{2,1,0:T(8,128)(2,1)S(1)} %get-tuple-element.45), channel_id=1, source_target_pairs={{0,1},{1,0},{2,3},{3,2},{4,5},{5,4},{6,7},{7,6},{8,9},{9,8},{10,11... | collective-permute-start | bytes 786440 | tf_op jit(solution)/shard_map/ppermute | solution.py:35
  62.5 2.6 %collective-permute-start.7 = (bf16[1,64,512]{2,1,0:T(8,128)(2,1)S(1)}, bf16[1,64,512]{2,1,0:T(8,128)(2,1)S(1)}, u32[]{:S(2)}, u32[]{:S(2)}) collective-permute-start(bf16[1,64,512]{2,1,0:T(8,128)(2,1)S(1)} %get-tuple-element.47), channel_id=1, source_target_pairs={{0,4},{1,5},{2,6},{3,7},{4,0},{5,1},{6,2},{7,3},{8,12},{9,13},{10,... | collective-permute-start | bytes 196616 | tf_op jit(solution)/shard_map/ppermute | solution.py:40
  65.1 1.9 %collective-permute-done.5.refs_1_ = bf16[2,192,2048]{2,1,0:T(8,128)(2,1)} collective-permute-done((bf16[2,192,2048]{2,1,0:T(8,128)(2,1)}, bf16[2,192,2048]{2,1,0:T(8,128)(2,1)}, u32[]{:S(2)}, u32[]{:S(2)}) %collective-permute-start.5) | collective-permute-done | bytes 1572896 | tf_op jit(solution)/shard_map/ppermute | solution.py:35
  67.0 0.7 collective-permute-done.7.refs_5_
  67.7 0.6 collective-permute-done.6.refs_3_
  68.3 3.4 %step.16 = (bf16[384,2048]{1,0:T(8,128)(2,1)S(1)}, bf16[4,64,384]{2,1,0:T(8,128)(2,1)S(1)}, f32[2,64,512]{2,1,0:T(8,128)S(1)}, bf16[2,64,512]{2,1,0:T(8,128)(2,1)S(1)}, f32[64,2,2,512]{3,2,1,0:T(2,128)}) custom-call(f32[11]{0:T(128)S(1)} %pad_maximum_fusion.1.table_ref, bf16[2,2,256,2048]{3,2,1,0:T(8,128)(2,1)S(1)} %get-tuple-element.42.refs_0_, ...), custom_call_target="tpu_custom_call" | custom-call | flops 1000 | bytes 1000 | tf_op jit(solution)/shard_map/step/pallas_call | solution.py:386
  71.7 1.6 %collective-permute-start.9 = (bf16[4,64,384]{2,1,0:T(8,128)(2,1)S(1)}, bf16[4,64,384]{2,1,0:T(8,128)(2,1)S(1)}, u32[]{:S(2)}, u32[]{:S(2)}) collective-permute-start(bf16[4,64,384]{2,1,0:T(8,128)(2,1)S(1)} %get-tuple-element.51), channel_id=1, source_target_pairs={{0,1},{1,0},{2,3},{3,2},{4,5},{5,4},{6,7},{7,6},{8,9},{9,8},{10,11... | collective-permute-start | bytes 589832 | tf_op jit(solution)/shard_map/ppermute | solution.py:35
  73.2 1.6 %collective-permute-start.8 = (bf16[2,64,512]{2,1,0:T(8,128)(2,1)S(1)}, bf16[2,64,512]{2,1,0:T(8,128)(2,1)S(1)}, u32[]{:S(2)}, u32[]{:S(2)}) collective-permute-start(bf16[2,64,512]{2,1,0:T(8,128)(2,1)S(1)} %get-tuple-element.49), channel_id=1, source_target_pairs={{0,2},{1,3},{2,0},{3,1},{4,6},{5,7},{6,4},{7,5},{8,10},{9,11},{10,... | collective-permute-start | bytes 393224 | tf_op jit(solution)/shard_map/ppermute | solution.py:40
  74.8 1.9 %step.17.refs_0_ = f32[4,64,384]{2,1,0:T(8,128)S(1)} custom-call(f32[11]{0:T(128)S(1)} %pad_maximum_fusion.1.table_ref, bf16[2,2,256,2048]{3,2,1,0:T(8,128)(2,1)S(1)} %get-tuple-element.42.refs_0_, bf16[384,2048]{1,0:T(8,128)(2,1)S(1)} %get-tuple-element.50.refs_1_), custom_call_target="tpu_custom_call" | custom-call | flops 1000 | bytes 1000 | tf_op jit(solution)/shard_map/step/pallas_call | solution.py:386
  76.7 1.6 %collective-permute-done.9.refs_1_ = bf16[4,64,384]{2,1,0:T(8,128)(2,1)S(1)} collective-permute-done((bf16[4,64,384]{2,1,0:T(8,128)(2,1)S(1)}, bf16[4,64,384]{2,1,0:T(8,128)(2,1)S(1)}, u32[]{:S(2)}, u32[]{:S(2)}) %collective-permute-start.9) | collective-permute-done | bytes 196640 | tf_op jit(solution)/shard_map/ppermute | solution.py:35
  78.3 0.6 step.18
  78.9 1.6 %collective-permute-start.10 = (bf16[2,64,384]{2,1,0:T(8,128)(2,1)S(1)}, bf16[2,64,384]{2,1,0:T(8,128)(2,1)S(1)}, u32[]{:S(2)}, u32[]{:S(2)}) collective-permute-start(bf16[2,64,384]{2,1,0:T(8,128)(2,1)S(1)} %get-tuple-element.53), channel_id=1, source_target_pairs={{0,2},{1,3},{2,0},{3,1},{4,6},{5,7},{6,4},{7,5},{8,10},{9,11},{10,... | collective-permute-start | bytes 294920 | tf_op jit(solution)/shard_map/ppermute | solution.py:40
  80.5 3.0 %collective-permute-done.10.refs_5_ = bf16[2,64,384]{2,1,0:T(8,128)(2,1)S(1)} collective-permute-done((bf16[2,64,384]{2,1,0:T(8,128)(2,1)S(1)}, bf16[2,64,384]{2,1,0:T(8,128)(2,1)S(1)}, u32[]{:S(2)}, u32[]{:S(2)}) %collective-permute-start.10) | collective-permute-done | bytes 98336 | tf_op jit(solution)/shard_map/ppermute | solution.py:40
  83.8 2.4 %step.19 = (bf16[384,2048]{1,0:T(8,128)(2,1)S(1)}, bf16[4,64,384]{2,1,0:T(8,128)(2,1)S(1)}, f32[1,64,896]{2,1,0:T(8,128)S(1)}, bf16[1,64,896]{2,1,0:T(8,128)(2,1)S(1)}) custom-call(f32[11]{0:T(128)S(1)} %pad_maximum_fusion.1.table_ref, bf16[2,2,256,2048]{3,2,1,0:T(8,128)(2,1)S(1)} %get-tuple-element.42.refs_0_, ...), custom_call_target="tpu_custom_call" | custom-call | flops 1000 | bytes 1000 | tf_op jit(solution)/shard_map/step/pallas_call | solution.py:386
  86.2 1.6 %collective-permute-start.13 = (bf16[4,64,384]{2,1,0:T(8,128)(2,1)S(1)}, bf16[4,64,384]{2,1,0:T(8,128)(2,1)S(1)}, u32[]{:S(2)}, u32[]{:S(2)}) collective-permute-start(bf16[4,64,384]{2,1,0:T(8,128)(2,1)S(1)} %get-tuple-element.59), channel_id=1, source_target_pairs={{0,1},{1,0},{2,3},{3,2},{4,5},{5,4},{6,7},{7,6},{8,9},{9,8},{10,11... | collective-permute-start | bytes 589832 | tf_op jit(solution)/shard_map/ppermute | solution.py:35
  87.8 2.6 %collective-permute-start.11 = (bf16[1,64,896]{2,1,0:T(8,128)(2,1)S(1)}, bf16[1,64,896]{2,1,0:T(8,128)(2,1)S(1)}, u32[]{:S(2)}, u32[]{:S(2)}) collective-permute-start(bf16[1,64,896]{2,1,0:T(8,128)(2,1)S(1)} %get-tuple-element.55), channel_id=1, source_target_pairs={{0,4},{1,5},{2,6},{3,7},{4,0},{5,1},{6,2},{7,3},{8,12},{9,13},{10,... | collective-permute-start | bytes 344072 | tf_op jit(solution)/shard_map/ppermute | solution.py:40
  90.3 1.9 %step.20.refs_0_ = f32[4,64,384]{2,1,0:T(8,128)S(1)} custom-call(f32[11]{0:T(128)S(1)} %pad_maximum_fusion.1.table_ref, bf16[2,2,256,2048]{3,2,1,0:T(8,128)(2,1)S(1)} %get-tuple-element.42.refs_0_, bf16[384,2048]{1,0:T(8,128)(2,1)S(1)} %get-tuple-element.58.refs_1_), custom_call_target="tpu_custom_call" | custom-call | flops 1000 | bytes 1000 | tf_op jit(solution)/shard_map/step/pallas_call | solution.py:386
  92.2 1.7 %collective-permute-done.13.refs_1_ = bf16[4,64,384]{2,1,0:T(8,128)(2,1)S(1)} collective-permute-done((bf16[4,64,384]{2,1,0:T(8,128)(2,1)S(1)}, bf16[4,64,384]{2,1,0:T(8,128)(2,1)S(1)}, u32[]{:S(2)}, u32[]{:S(2)}) %collective-permute-start.13) | collective-permute-done | bytes 196640 | tf_op jit(solution)/shard_map/ppermute | solution.py:35
  93.9 0.6 step.21
  94.5 1.6 %collective-permute-start.16 = (bf16[2,64,384]{2,1,0:T(8,128)(2,1)S(1)}, bf16[2,64,384]{2,1,0:T(8,128)(2,1)S(1)}, u32[]{:S(2)}, u32[]{:S(2)}) collective-permute-start(bf16[2,64,384]{2,1,0:T(8,128)(2,1)S(1)} %get-tuple-element.64), channel_id=1, source_target_pairs={{0,2},{1,3},{2,0},{3,1},{4,6},{5,7},{6,4},{7,5},{8,10},{9,11},{10,... | collective-permute-start | bytes 294920 | tf_op jit(solution)/shard_map/ppermute | solution.py:40
  96.2 0.6 collective-permute-done.11.refs_3_.refs_1_
  96.7 1.7 %step.22 = (bf16[256,2048]{1,0:T(8,128)(2,1)S(1)}, bf16[4,64,128]{2,1,0:T(8,128)(2,1)S(1)}, bf16[4,64,128]{2,1,0:T(8,128)(2,1)S(1)}, f32[64,2,2,512]{3,2,1,0:T(2,128)}) custom-call(f32[11]{0:T(128)S(1)} %pad_maximum_fusion.1.table_ref, bf16[2,2,256,2048]{3,2,1,0:T(8,128)(2,1)S(1)} %get-tuple-element.42.refs_0_, ...), custom_call_target="tpu_custom_call", output_to_operand_aliasing={{3}: (5, {})} | custom-call | flops 1000 | bytes 1000 | tf_op jit(solution)/shard_map/step/pallas_call | solution.py:386
  98.4 1.0 collective-permute-start.14
  99.4 1.1 collective-permute-start.15
  100.5 1.3 %step.23.refs_0_ = f32[4,64,256]{2,1,0:T(8,128)S(1)} custom-call(f32[11]{0:T(128)S(1)} %pad_maximum_fusion.1.table_ref, bf16[2,2,256,2048]{3,2,1,0:T(8,128)(2,1)S(1)} %get-tuple-element.42.refs_0_, bf16[256,2048]{1,0:T(8,128)(2,1)S(1)} %get-tuple-element.61.refs_1_), custom_call_target="tpu_custom_call" | custom-call | flops 1000 | bytes 1000 | tf_op jit(solution)/shard_map/step/pallas_call | solution.py:386
  101.8 1.2 %collective-permute-done.14.refs_1_ = bf16[4,64,128]{2,1,0:T(8,128)(2,1)S(1)} collective-permute-done((bf16[4,64,128]{2,1,0:T(8,128)(2,1)S(1)}, bf16[4,64,128]{2,1,0:T(8,128)(2,1)S(1)}, u32[]{:S(2)}, u32[]{:S(2)}) %collective-permute-start.14) | collective-permute-done | bytes 65568 | tf_op jit(solution)/shard_map/ppermute | solution.py:35
  103.0 0.7 collective-permute-done.15.refs_2_
  103.7 0.6 step.24
  104.3 2.7 %collective-permute-start.17 = (bf16[1,64,640]{2,1,0:T(8,128)(2,1)S(1)}, bf16[1,64,640]{2,1,0:T(8,128)(2,1)S(1)}, u32[]{:S(2)}, u32[]{:S(2)}) collective-permute-start(bf16[1,64,640]{2,1,0:T(8,128)(2,1)S(1)} %get-tuple-element.66), channel_id=1, source_target_pairs={{0,4},{1,5},{2,6},{3,7},{4,0},{5,1},{6,2},{7,3},{8,12},{9,13},{10,... | collective-permute-start | bytes 245768 | tf_op jit(solution)/shard_map/ppermute | solution.py:40
  107.0 1.3 %collective-permute-start.18 = (bf16[1,64,256]{2,1,0:T(8,128)(2,1)S(1)}, bf16[1,64,256]{2,1,0:T(8,128)(2,1)S(1)}, u32[]{:S(2)}, u32[]{:S(2)}) collective-permute-start(bf16[1,64,256]{2,1,0:T(8,128)(2,1)S(1)} %get-tuple-element.68), channel_id=1, source_target_pairs={{0,6},{1,7},{2,4},{3,5},{4,2},{5,3},{6,0},{7,1},{8,14},{9,15},{10,... | collective-permute-start | bytes 98312 | tf_op jit(solution)/shard_map/ppermute | solution.py:40
  108.2 0.5 collective-permute-start.19
  108.7 4.0 %collective-permute-done.18.refs_5_ = bf16[1,64,256]{2,1,0:T(8,128)(2,1)S(1)} collective-permute-done((bf16[1,64,256]{2,1,0:T(8,128)(2,1)S(1)}, bf16[1,64,256]{2,1,0:T(8,128)(2,1)S(1)}, u32[]{:S(2)}, u32[]{:S(2)}) %collective-permute-start.18) | collective-permute-done | bytes 32800 | tf_op jit(solution)/shard_map/ppermute | solution.py:40
  112.7 1.5 %step.25 = f32[64,2,2,512]{3,2,1,0:T(2,128)} custom-call(f32[11]{0:T(128)S(1)} %pad_maximum_fusion.1.table_ref, f32[1,64,896]{2,1,0:T(8,128)S(1)} %get-tuple-element.54.refs_2_.refs_0_, bf16[1,64,896]{2,1,0:T(8,128)(2,1)S(1)} %collective-permute-done.11.refs_3_.refs_1_, f32[1,64,384]{2,1,0:T(8,128)S(1)} %get-tuple-element.65.refs_2_, ...), custom_call_target="tpu_custom_call", output_to_operand_aliasing={{}: (9, {})} | custom-call | flops 1000 | bytes 1000 | tf_op jit(solution)/shard_map/step/pallas_call | solution.py:386
  (20 shorter events, 1.0 us)
Async XLA Ops:
  1.6 26.0 %collective-permute-start.1 = (bf16[2,256,2048]{2,1,0:T(8,128)(2,1)S(1)}, bf16[2,256,2048]{2,1,0:T(8,128)(2,1)}, u32[]{:S(2)}, u32[]{:S(2)}) collective-permute-start(bf16[2,256,2048]{2,1,0:T(8,128)(2,1)S(1)} %piece_of.3.rest_0_), channel_id=1, source_target_pairs={{0,24},{8,0},{16,8},{24,16},{1,25},{9,1},{17,9},{25,17},{2,26},{10... | collective-permute-start | bytes 6291464 | tf_op jit(solution)/shard_map/ppermute | solution.py:35
  6.6 3.2 %copy-start = (s32[2]{0:T(128)S(1)}, s32[2]{0:T(128)}, u32[]{:S(2)}) copy-start(s32[2]{0:T(128)} %param.4) | copy-start | bytes 28
  6.6 3.2 %copy-start.1 = (s32[2]{0:T(128)S(1)}, s32[2]{0:T(128)}, u32[]{:S(2)}) copy-start(s32[2]{0:T(128)} %param.5) | copy-start | bytes 28
  6.7 43.5 %collective-permute-start = (bf16[2,256,2048]{2,1,0:T(8,128)(2,1)}, bf16[2,256,2048]{2,1,0:T(8,128)(2,1)}, u32[]{:S(2)}, u32[]{:S(2)}) collective-permute-start(bf16[2,256,2048]{2,1,0:T(8,128)(2,1)} %piece_of.4.rest_0_), channel_id=1, source_target_pairs={{0,24},{8,0},{16,8},{24,16},{1,25},{9,1},{17,9},{25,17},{2,26},{10... | collective-permute-start | bytes 6291464 | tf_op jit(solution)/shard_map/ppermute | solution.py:35
  9.7 57.3 %collective-permute-start.5 = (bf16[2,192,2048]{2,1,0:T(8,128)(2,1)}, bf16[2,192,2048]{2,1,0:T(8,128)(2,1)}, u32[]{:S(2)}, u32[]{:S(2)}) collective-permute-start(bf16[2,192,2048]{2,1,0:T(8,128)(2,1)} %piece_of.5), channel_id=1, source_target_pairs={{0,24},{8,0},{16,8},{24,16},{1,25},{9,1},{17,9},{25,17},{2,26},{10... | collective-permute-start | bytes 4718600 | tf_op jit(solution)/shard_map/ppermute | solution.py:35
  35.3 48.4 %collective-permute-start.4 = (bf16[2,192,2048]{2,1,0:T(8,128)(2,1)S(1)}, bf16[2,192,2048]{2,1,0:T(8,128)(2,1)S(1)}, u32[]{:S(2)}, u32[]{:S(2)}) collective-permute-start(bf16[2,192,2048]{2,1,0:T(8,128)(2,1)S(1)} %get-tuple-element.43), channel_id=1, source_target_pairs={{0,24},{8,0},{16,8},{24,16},{1,25},{9,1},{17,9},{25,17},{2,26},{10... | collective-permute-start | bytes 4718600 | tf_op jit(solution)/shard_map/ppermute | solution.py:35
  37.4 7.2 %collective-permute-start.2 = (bf16[4,64,512]{2,1,0:T(8,128)(2,1)S(1)}, bf16[4,64,512]{2,1,0:T(8,128)(2,1)S(1)}, u32[]{:S(2)}, u32[]{:S(2)}) collective-permute-start(bf16[4,64,512]{2,1,0:T(8,128)(2,1)S(1)} %get-tuple-element.39), channel_id=1, source_target_pairs={{0,1},{1,0},{2,3},{3,2},{4,5},{5,4},{6,7},{7,6},{8,9},{9,8},{10,11... | collective-permute-start | bytes 786440 | tf_op jit(solution)/shard_map/ppermute | solution.py:35
  45.2 5.0 %collective-permute-start.3 = (bf16[2,64,512]{2,1,0:T(8,128)(2,1)S(1)}, bf16[2,64,512]{2,1,0:T(8,128)(2,1)S(1)}, u32[]{:S(2)}, u32[]{:S(2)}) collective-permute-start(bf16[2,64,512]{2,1,0:T(8,128)(2,1)S(1)} %get-tuple-element.41), channel_id=1, source_target_pairs={{0,2},{1,3},{2,0},{3,1},{4,6},{5,7},{6,4},{7,5},{8,10},{9,11},{10,... | collective-permute-start | bytes 393224 | tf_op jit(solution)/shard_map/ppermute | solution.py:40
  59.0 37.2 %collective-permute-start.12 = (bf16[2,128,2048]{2,1,0:T(8,128)(2,1)S(1)}, bf16[2,128,2048]{2,1,0:T(8,128)(2,1)S(1)}, u32[]{:S(2)}, u32[]{:S(2)}) collective-permute-start(bf16[2,128,2048]{2,1,0:T(8,128)(2,1)S(1)} %get-tuple-element.56), channel_id=1, source_target_pairs={{0,24},{8,0},{16,8},{24,16},{1,25},{9,1},{17,9},{25,17},{2,26},{10... | collective-permute-start | bytes 3145736 | tf_op jit(solution)/shard_map/ppermute | solution.py:35
  61.1 7.2 %collective-permute-start.6 = (bf16[4,64,512]{2,1,0:T(8,128)(2,1)S(1)}, bf16[4,64,512]{2,1,0:T(8,128)(2,1)S(1)}, u32[]{:S(2)}, u32[]{:S(2)}) collective-permute-start(bf16[4,64,512]{2,1,0:T(8,128)(2,1)S(1)} %get-tuple-element.45), channel_id=1, source_target_pairs={{0,1},{1,0},{2,3},{3,2},{4,5},{5,4},{6,7},{7,6},{8,9},{9,8},{10,11... | collective-permute-start | bytes 786440 | tf_op jit(solution)/shard_map/ppermute | solution.py:35
  62.5 5.2 %collective-permute-start.7 = (bf16[1,64,512]{2,1,0:T(8,128)(2,1)S(1)}, bf16[1,64,512]{2,1,0:T(8,128)(2,1)S(1)}, u32[]{:S(2)}, u32[]{:S(2)}) collective-permute-start(bf16[1,64,512]{2,1,0:T(8,128)(2,1)S(1)} %get-tuple-element.47), channel_id=1, source_target_pairs={{0,4},{1,5},{2,6},{3,7},{4,0},{5,1},{6,2},{7,3},{8,12},{9,13},{10,... | collective-permute-start | bytes 196616 | tf_op jit(solution)/shard_map/ppermute | solution.py:40
  71.7 6.6 %collective-permute-start.9 = (bf16[4,64,384]{2,1,0:T(8,128)(2,1)S(1)}, bf16[4,64,384]{2,1,0:T(8,128)(2,1)S(1)}, u32[]{:S(2)}, u32[]{:S(2)}) collective-permute-start(bf16[4,64,384]{2,1,0:T(8,128)(2,1)S(1)} %get-tuple-element.51), channel_id=1, source_target_pairs={{0,1},{1,0},{2,3},{3,2},{4,5},{5,4},{6,7},{7,6},{8,9},{9,8},{10,11... | collective-permute-start | bytes 589832 | tf_op jit(solution)/shard_map/ppermute | solution.py:35
  73.2 7.3 %collective-permute-start.8 = (bf16[2,64,512]{2,1,0:T(8,128)(2,1)S(1)}, bf16[2,64,512]{2,1,0:T(8,128)(2,1)S(1)}, u32[]{:S(2)}, u32[]{:S(2)}) collective-permute-start(bf16[2,64,512]{2,1,0:T(8,128)(2,1)S(1)} %get-tuple-element.49), channel_id=1, source_target_pairs={{0,2},{1,3},{2,0},{3,1},{4,6},{5,7},{6,4},{7,5},{8,10},{9,11},{10,... | collective-permute-start | bytes 393224 | tf_op jit(solution)/shard_map/ppermute | solution.py:40
  78.9 4.7 %collective-permute-start.10 = (bf16[2,64,384]{2,1,0:T(8,128)(2,1)S(1)}, bf16[2,64,384]{2,1,0:T(8,128)(2,1)S(1)}, u32[]{:S(2)}, u32[]{:S(2)}) collective-permute-start(bf16[2,64,384]{2,1,0:T(8,128)(2,1)S(1)} %get-tuple-element.53), channel_id=1, source_target_pairs={{0,2},{1,3},{2,0},{3,1},{4,6},{5,7},{6,4},{7,5},{8,10},{9,11},{10,... | collective-permute-start | bytes 294920 | tf_op jit(solution)/shard_map/ppermute | solution.py:40
  86.2 7.7 %collective-permute-start.13 = (bf16[4,64,384]{2,1,0:T(8,128)(2,1)S(1)}, bf16[4,64,384]{2,1,0:T(8,128)(2,1)S(1)}, u32[]{:S(2)}, u32[]{:S(2)}) collective-permute-start(bf16[4,64,384]{2,1,0:T(8,128)(2,1)S(1)} %get-tuple-element.59), channel_id=1, source_target_pairs={{0,1},{1,0},{2,3},{3,2},{4,5},{5,4},{6,7},{7,6},{8,9},{9,8},{10,11... | collective-permute-start | bytes 589832 | tf_op jit(solution)/shard_map/ppermute | solution.py:35
  87.8 9.0 %collective-permute-start.11 = (bf16[1,64,896]{2,1,0:T(8,128)(2,1)S(1)}, bf16[1,64,896]{2,1,0:T(8,128)(2,1)S(1)}, u32[]{:S(2)}, u32[]{:S(2)}) collective-permute-start(bf16[1,64,896]{2,1,0:T(8,128)(2,1)S(1)} %get-tuple-element.55), channel_id=1, source_target_pairs={{0,4},{1,5},{2,6},{3,7},{4,0},{5,1},{6,2},{7,3},{8,12},{9,13},{10,... | collective-permute-start | bytes 344072 | tf_op jit(solution)/shard_map/ppermute | solution.py:40
  94.5 9.2 %collective-permute-start.16 = (bf16[2,64,384]{2,1,0:T(8,128)(2,1)S(1)}, bf16[2,64,384]{2,1,0:T(8,128)(2,1)S(1)}, u32[]{:S(2)}, u32[]{:S(2)}) collective-permute-start(bf16[2,64,384]{2,1,0:T(8,128)(2,1)S(1)} %get-tuple-element.64), channel_id=1, source_target_pairs={{0,2},{1,3},{2,0},{3,1},{4,6},{5,7},{6,4},{7,5},{8,10},{9,11},{10,... | collective-permute-start | bytes 294920 | tf_op jit(solution)/shard_map/ppermute | solution.py:40
  98.4 4.5 %collective-permute-start.14 = (bf16[4,64,128]{2,1,0:T(8,128)(2,1)S(1)}, bf16[4,64,128]{2,1,0:T(8,128)(2,1)S(1)}, u32[]{:S(2)}, u32[]{:S(2)}) collective-permute-start(bf16[4,64,128]{2,1,0:T(8,128)(2,1)S(1)} %get-tuple-element.62), channel_id=1, source_target_pairs={{0,1},{1,0},{2,3},{3,2},{4,5},{5,4},{6,7},{7,6},{8,9},{9,8},{10,11... | collective-permute-start | bytes 196616 | tf_op jit(solution)/shard_map/ppermute | solution.py:35
  99.4 4.3 %collective-permute-start.15 = (bf16[4,64,128]{2,1,0:T(8,128)(2,1)S(1)}, bf16[4,64,128]{2,1,0:T(8,128)(2,1)S(1)}, u32[]{:S(2)}, u32[]{:S(2)}) collective-permute-start(bf16[4,64,128]{2,1,0:T(8,128)(2,1)S(1)} %get-tuple-element.63), channel_id=1, source_target_pairs={{0,1},{1,0},{2,3},{3,2},{4,5},{5,4},{6,7},{7,6},{8,9},{9,8},{10,11... | collective-permute-start | bytes 196616 | tf_op jit(solution)/shard_map/ppermute | solution.py:35
  104.3 8.4 %collective-permute-start.17 = (bf16[1,64,640]{2,1,0:T(8,128)(2,1)S(1)}, bf16[1,64,640]{2,1,0:T(8,128)(2,1)S(1)}, u32[]{:S(2)}, u32[]{:S(2)}) collective-permute-start(bf16[1,64,640]{2,1,0:T(8,128)(2,1)S(1)} %get-tuple-element.66), channel_id=1, source_target_pairs={{0,4},{1,5},{2,6},{3,7},{4,0},{5,1},{6,2},{7,3},{8,12},{9,13},{10,... | collective-permute-start | bytes 245768 | tf_op jit(solution)/shard_map/ppermute | solution.py:40
  107.0 5.7 %collective-permute-start.18 = (bf16[1,64,256]{2,1,0:T(8,128)(2,1)S(1)}, bf16[1,64,256]{2,1,0:T(8,128)(2,1)S(1)}, u32[]{:S(2)}, u32[]{:S(2)}) collective-permute-start(bf16[1,64,256]{2,1,0:T(8,128)(2,1)S(1)} %get-tuple-element.68), channel_id=1, source_target_pairs={{0,6},{1,7},{2,4},{3,5},{4,2},{5,3},{6,0},{7,1},{8,14},{9,15},{10,... | collective-permute-start | bytes 98312 | tf_op jit(solution)/shard_map/ppermute | solution.py:40
  108.2 4.5 %collective-permute-start.19 = (bf16[1,64,256]{2,1,0:T(8,128)(2,1)S(1)}, bf16[1,64,256]{2,1,0:T(8,128)(2,1)S(1)}, u32[]{:S(2)}, u32[]{:S(2)}) collective-permute-start(bf16[1,64,256]{2,1,0:T(8,128)(2,1)S(1)} %get-tuple-element.69), channel_id=1, source_target_pairs={{0,2},{1,3},{2,0},{3,1},{4,6},{5,7},{6,4},{7,5},{8,10},{9,11},{10,... | collective-permute-start | bytes 98312 | tf_op jit(solution)/shard_map/ppermute | solution.py:40
